TPU v7x, 32 devices: a whole 2x2x4 slice. The times are simulated.
32 devices in a mesh: group: 2 (over x), dp: 16 (over z, y, core).
Axes of the slice: x: 2, y: 2, z: 4, core: 2. Of those that a mesh axis runs over, the one named last changes fastest.
Arguments:
- attn_out: bfloat16 [4608, 12288], P('group', 'dp'), parts along dimension 0, may hold values from -6 to 6
- out_grad: bfloat16 [4608, 4096], P(('group', 'dp')), parts along dimension 0, may hold values from -6 to 6
- o_weight: bfloat16 [12288, 4096], P('dp'), may hold values from -0.09375 to 0.09375
- head_counts: int32 [16], P('dp'), may hold values from 2 to 6, as said below
- seq_counts: int32 [32], P(('group', 'dp')), parts along dimension 0, may hold values from 7 to 9, as said below
Outputs:
- attn_grad: bfloat16 [4608, 12288], P('group', 'dp'), parts along dimension 0
- weight_grad: bfloat16 [24576, 4096], P(('group', 'dp')), parts along dimension 0
There are 2 independent parts, one for each index of `group`. A program takes and returns all parts, laid end to end along the dimension named above; an argument that names none is the same for every part. Nothing has to cross between parts.
Inputs may be any that keep to these rules, and one draw needn't show every extreme that they name: `head_counts`: entry b is the number of 128-feature heads at the start of device b's block of 6 heads; the entries sum to 64, never fall from one device to the next, and both the least and the most are reached. `seq_counts`: entry b is the number of 16-token sequences at the start of device b's 144 token slots; the entries sum to 128, and the most is reached.
All inputs are finite; a program needn't handle non-finite values.
Results may differ from a plain program's by a relative error of at most 0.0004.
Values may be sent and summed in bfloat16 or wider, within the bound.
No kernel may reach another device: no remote copies, remote signals or barrier semaphores. Data moves between devices by JAX's collectives and lax.ppermute only.
A program may use at most 128 MiB of HBM per device.

v0:
```python
import jax
import jax.numpy as jnp
from jax import lax
from jax.sharding import PartitionSpec as P

D = 4096
HEADS = 64
HEAD_DIM = 128
SEQ = 16


def on_device(attn_out, out_grad, o_weight, head_counts, seq_counts):
    row_count = out_grad.shape[0]
    row_index = lax.broadcasted_iota(jnp.int32, (row_count, 1), 0)
    grad_live = jnp.where(row_index < seq_counts[0] * SEQ, out_grad, jnp.zeros_like(out_grad))
    capacity = o_weight.shape[0]
    live_width = head_counts[0] * HEAD_DIM
    column_live = lax.broadcasted_iota(jnp.int32, (1, capacity), 1) < live_width
    gathered = lax.all_gather(grad_live, "dp", axis=0, tiled=True)
    back_grad = lax.dot_general(
        gathered, o_weight, (((1,), (1,)), ((), ())), preferred_element_type=jnp.float32
    )
    back_grad = jnp.where(column_live, back_grad, 0.0).astype(jnp.bfloat16)
    grad_total = back_grad
    weight_total = lax.dot_general(
        attn_out, gathered, (((0,), (0,)), ((), ())), preferred_element_type=jnp.float32
    )
    grad_total, weight_total = (grad_total, weight_total)
    row_live = lax.broadcasted_iota(jnp.int32, (capacity, 1), 0) < live_width
    weight_total = jnp.where(row_live, weight_total, 0.0)
    square_sum = lax.psum(jnp.sum(weight_total * weight_total), "dp")
    factor = jnp.minimum(1.0, 1.0 / jnp.sqrt(square_sum / (HEADS * HEAD_DIM * D) + 1e-06))
    return (grad_total, (weight_total * factor).astype(jnp.bfloat16))


def solution(mesh):
    placed = (
        P("group", "dp"),
        P(("group", "dp"), None),
        P("dp", None),
        P("dp"),
        P(("group", "dp")),
    )
    return jax.shard_map(
        on_device,
        mesh=mesh,
        in_specs=placed,
        out_specs=(P("group", "dp"), P(("group", "dp"), None)),
        check_vma=False,
    )
```

profile of v0, /device:TPU:0, one launch (start us, length us, event | category | flops | bytes accessed | tf_op | source)
XLA Modules:
  0.0 213.6 jit_solution(3249094822744982825)
XLA Ops:
  7.2 0.0 copy-start
  7.2 0.0 all-gather.2.cloned.1.call-start
  8.0 2.6 %broadcast_select_fusion = bf16[144,4096]{1,0:T(8,128)(2,1)} fusion(bf16[144,4096]{1,0:T(8,128)(2,1)} %param.6, pred[144]{0:T(512)(128)(4,1)S(1)} %iota_compare_fusion.1), kind=kLoop, calls=%fused_computation.4 | loop fusion | flops 589824 | bytes 2359440 | tf_op jit(solution)/shard_map/jit(_where)/select_n | solution.py:15
  10.7 0.0 all-gather.2.cloned.1.call-update
  11.3 101.2 %all-gather.2.cloned.1.call-done = bf16[2304,4096]{1,0:T(8,128)(2,1)} async-done(((bf16[144,4096]{1,0:T(8,128)(2,1)}), bf16[2304,4096]{1,0:T(8,128)(2,1)}) %all-gather.2.cloned.1.call-update) | async-done | bytes 18874384 | tf_op jit(solution)/shard_map/all_gather | solution.py:19
  112.5 0.0 copy-done
  112.5 22.5 %multiply_reduce_fusion = (f32[]{:T(128)}, f32[4096,768]{1,0:T(8,128)}) fusion(pred[768]{0:T(1024)(128)(4,1)S(1)} %iota_compare_fusion, bf16[2304,4096]{1,0:T(8,128)(2,1)} %all-gather.2.cloned.1.call-done, bf16[2304,768]{1,0:T(8,128)(2,1)S(1)} %copy-done), kind=kOutput, calls=%fused_computation.1 | convolution fusion | flops 14504951808 | bytes 34996996 | tf_op jit(solution)/shard_map/dot_general | solution.py:25
  135.0 33.2 %psum.7 = f32[]{:T(128)} all-reduce(f32[]{:T(128)} %get-tuple-element.4), channel_id=1, replica_groups=mesh['group'=2,'dp'=16] {'dp'}, use_global_device_ids=true, to_apply=%region_1.2 | all-reduce | flops 1 | bytes 8 | tf_op jit(solution)/shard_map/psum | solution.py:31
  168.9 8.3 %fusion = bf16[768,4096]{0,1:T(8,128)(2,1)} fusion(f32[4096,768]{1,0:T(8,128)} %get-tuple-element.5, f32[]{:T(128)S(6)} %min.3, pred[768]{0:T(1024)(128)(4,1)S(1)} %iota_compare_fusion), kind=kLoop, calls=%fused_computation.3 | loop fusion | flops 9437184 | bytes 18875140 | tf_op jit(solution)/shard_map/convert_element_type | solution.py:33
  177.2 8.6 %copy.7 = bf16[768,4096]{1,0:T(8,128)(2,1)} copy(bf16[768,4096]{0,1:T(8,128)(2,1)} %fusion) | data formatting | bytes 12582912
  185.9 20.8 %select_convert_fusion = bf16[2304,768]{1,0:T(8,128)(2,1)} fusion(bf16[2304,4096]{1,0:T(8,128)(2,1)} %all-gather.2.cloned.1.call-done, bf16[768,4096]{1,0:T(8,128)(2,1)} %param.7, pred[768]{0:T(1024)(128)(4,1)S(1)} %iota_compare_fusion), kind=kOutput, calls=%fused_computation.2 | convolution fusion | flops 14499053568 | bytes 28705536 | tf_op jit(solution)/shard_map/dot_general | solution.py:20
  (2 shorter events, 0.0 us)
Async XLA Ops:
  7.2 105.3 %copy-start = (bf16[2304,768]{1,0:T(8,128)(2,1)S(1)}, bf16[2304,768]{1,0:T(8,128)(2,1)}, u32[]{:S(2)}) copy-start(bf16[2304,768]{1,0:T(8,128)(2,1)} %param.5) | copy-start | bytes 10616836
  7.2 105.3 %all-gather.2.cloned.1.call-start = ((), (), s32[]{:S(2)}) async-start(), calls=%async_computation | async-start | bytes 20054016 | tf_op jit(solution)/shard_map/all_gather | solution.py:19
Sparse Core Ops, SparseCore 0:
  10.8 101.6 all-gather.1
where the time goes:
time: 214 us
  waiting for transfers between devices  101 us (47%)
  matrix products  43.3 us (20%)
  blocking collectives  33.2 us (16%)
  between operations  16.2 us (8%)
  other arithmetic  10.9 us (5%)
  local copies, waits for them, and re-layouts  8.62 us (4%)
    all_gather x1, waiting for transfers between devices, on_device(): gathered = lax.all_gather(grad_live, 'dp', axis=0, tiled=True)  101 us
    psum x1, blocking collectives, on_device(): square_sum = lax.psum(jnp.sum(weight_total * weight_total), 'dp')  33.2 us
    dot_general x1, matrix products, on_device(): lax.dot_general(attn_out, gathered, (((0,), (0,)), ((), ())), preferred_e...  22.5 us
    dot_general x1, matrix products, on_device(): lax.dot_general(gathered, o_weight, (((1,), (1,)), ((), ())), preferred_e...  20.8 us
    unnamed x3, local copies, waits for them, and re-layouts  8.62 us
    convert_element_type x1, other arithmetic, on_device(): return (grad_total, (weight_total * factor).astype(jnp.bfloat16))  8.3 us
  transfers between devices with their start and end apart: 1, of which 1 were waited for; matrix products, arithmetic and copies ran while one was open for 0% of the time, Pallas kernels for 0%

commit v1 on v0

v1 whole, which is shorter than its diff:
```python
import functools

import jax
import jax.numpy as jnp
from jax import lax
from jax.experimental import pallas as pl
from jax.experimental.pallas import tpu as pltpu
from jax.sharding import PartitionSpec as P

HEADS = 64
HEAD_DIM = 128
SEQ = 16
CHUNKS = 4
VMEM_LIMIT = 56 * 1024 * 1024


def params():
    return pltpu.CompilerParams(
        dimension_semantics=("arbitrary",), vmem_limit_bytes=VMEM_LIMIT
    )


def weight_kernel(at_ref, g_ref, before_ref, w_ref, squares_ref):
    @pl.when(pl.program_id(0) == 0)
    def _():
        squares_ref[...] = before_ref[...]

    w = jnp.dot(at_ref[...], g_ref[...], preferred_element_type=jnp.float32)
    w_ref[...] = w
    rows, columns = w.shape
    folded = jnp.sum((w * w).reshape(rows // 8, 8, columns), axis=0)
    total = squares_ref[...]
    for lane in range(0, columns, 128):
        total = total + folded[:, lane : lane + 128]
    squares_ref[...] = total


def weight_chunk(at, g, before):
    capacity, slots = at.shape
    width = g.shape[1]
    tile = min(256, width)
    return pl.pallas_call(
        weight_kernel,
        grid=(width // tile,),
        in_specs=[
            pl.BlockSpec((capacity, slots), lambda j: (0, 0)),
            pl.BlockSpec((slots, tile), lambda j: (0, j)),
            pl.BlockSpec((8, 128), lambda j: (0, 0)),
        ],
        out_specs=[
            pl.BlockSpec((capacity, tile), lambda j: (0, j)),
            pl.BlockSpec((8, 128), lambda j: (0, 0)),
        ],
        out_shape=[
            jax.ShapeDtypeStruct((capacity, width), jnp.float32),
            jax.ShapeDtypeStruct((8, 128), jnp.float32),
        ],
        compiler_params=params(),
        cost_estimate=pl.CostEstimate(
            flops=2 * capacity * slots * width,
            bytes_accessed=2 * slots * (capacity + width) + 4 * capacity * width,
            transcendentals=0,
        ),
        name="weight_chunk",
    )(at, g, before)


def attn_kernel(chunks, width_ref, wt_ref, *refs):
    g_refs, out_ref = refs[:chunks], refs[chunks]
    width = g_refs[0].shape[1]
    total = None
    for i, g_ref in enumerate(g_refs):
        part = lax.dot_general(
            g_ref[...],
            wt_ref[:, i * width : (i + 1) * width],
            (((1,), (1,)), ((), ())),
            preferred_element_type=jnp.float32,
        )
        total = part if total is None else total + part
    column = lax.broadcasted_iota(jnp.int32, total.shape, 1)
    out_ref[...] = jnp.where(column < width_ref[0], total, 0.0).astype(jnp.bfloat16)


def attn_grad_of(gs, o_weight, live_width):
    capacity, features = o_weight.shape
    slots, width = gs[0].shape
    tile = 256
    return pl.pallas_call(
        functools.partial(attn_kernel, len(gs)),
        grid=(slots // tile,),
        in_specs=[
            pl.BlockSpec(memory_space=pltpu.SMEM),
            pl.BlockSpec((capacity, features), lambda j: (0, 0)),
        ]
        + [pl.BlockSpec((tile, width), lambda j: (j, 0)) for _ in gs],
        out_specs=pl.BlockSpec((tile, capacity), lambda j: (j, 0)),
        out_shape=jax.ShapeDtypeStruct((slots, capacity), jnp.bfloat16),
        compiler_params=params(),
        cost_estimate=pl.CostEstimate(
            flops=2 * capacity * slots * features,
            bytes_accessed=2 * (slots * features + capacity * features + capacity * slots),
            transcendentals=0,
        ),
        name="attn_grad",
    )(live_width, o_weight, *gs)


def scale_kernel(chunks, features, *refs):
    w_refs, squares_ref, out_ref = refs[:chunks], refs[chunks], refs[chunks + 1]
    square_sum = jnp.sum(
        jnp.sum(squares_ref[...], axis=0, keepdims=True), axis=1, keepdims=True
    )
    factor = jnp.minimum(
        1.0, 1.0 / jnp.sqrt(square_sum / (HEADS * HEAD_DIM * features) + 1e-06)
    )
    width = w_refs[0].shape[1]
    for i, ref in enumerate(w_refs):
        out_ref[:, i * width : (i + 1) * width] = (ref[...] * factor).astype(jnp.bfloat16)


def scaled(ws, squares):
    capacity, width = ws[0].shape
    features = width * len(ws)
    tile = 64
    return pl.pallas_call(
        functools.partial(scale_kernel, len(ws), features),
        grid=(capacity // tile,),
        in_specs=[pl.BlockSpec((tile, width), lambda j: (j, 0)) for _ in ws]
        + [pl.BlockSpec(squares.shape, lambda j: (0, 0))],
        out_specs=pl.BlockSpec((tile, features), lambda j: (j, 0)),
        out_shape=jax.ShapeDtypeStruct((capacity, features), jnp.bfloat16),
        compiler_params=params(),
        cost_estimate=pl.CostEstimate(
            flops=capacity * features,
            bytes_accessed=6 * capacity * features,
            transcendentals=0,
        ),
        name="scale",
    )(*ws, squares)


def on_device(attn_out, out_grad, o_weight, head_counts, seq_counts):
    row_count, features = out_grad.shape
    capacity = o_weight.shape[0]
    live_width = head_counts * HEAD_DIM
    row_live = lax.broadcasted_iota(jnp.int32, (row_count, 1), 0) < seq_counts[0] * SEQ
    head_live = lax.broadcasted_iota(jnp.int32, (1, capacity), 1) < live_width[0]
    width = features // CHUNKS
    at = jnp.where(head_live, attn_out, jnp.zeros_like(attn_out)).T
    squares = jnp.zeros((8, 128), jnp.float32)
    gs, ws = [], []
    for i in range(CHUNKS):
        piece = out_grad[:, i * width : (i + 1) * width]
        piece = jnp.where(row_live, piece, jnp.zeros_like(piece))
        g = lax.all_gather(piece, "dp", axis=0, tiled=True)
        w, squares = weight_chunk(at, g, squares)
        gs.append(g)
        ws.append(w)
    parts = lax.all_gather(squares, "dp", axis=0, tiled=True)
    attn_grad = attn_grad_of(gs, o_weight, live_width)
    return attn_grad, scaled(ws, parts)


def solution(mesh):
    placed = (
        P("group", "dp"),
        P(("group", "dp"), None),
        P("dp", None),
        P("dp"),
        P(("group", "dp")),
    )
    return jax.shard_map(
        on_device,
        mesh=mesh,
        in_specs=placed,
        out_specs=(P("group", "dp"), P(("group", "dp"), None)),
        check_vma=False,
    )
```

time: 214 us -> 299 us (1.40)
  waiting for transfers between devices: 101 us -> 187 us
  Pallas kernels: 0 us -> 65.6 us
  matrix products: 43.3 us -> 0 us
  blocking collectives: 33.2 us -> 20.7 us
  other arithmetic: 10.9 us -> 4.51 us
  local copies, waits for them, and re-layouts: 8.62 us -> 4.92 us
    all_gather x1 -> x4, waiting for transfers between devices: 101 us -> 185 us  [on_device(): g = lax.all_gather(piece, 'dp', axis=0, tiled=True)]
    pallas_call x0 -> x6, Pallas kernels: none -> 65.6 us  [the longest x4 33.1 us: weight_chunk(): pl.pallas_call(weight_kernel, grid=(width // tile,), in_specs=[pl.BlockSp...]
    dot_general x2 -> x0, matrix products: 43.3 us -> none  [the longest x1 22.5 us: on_device(): lax.dot_general(attn_out, gathered, (((0,), (0,)), ((), ())), preferred_e...]
    psum x1 -> x0, blocking collectives: 33.2 us -> none  [on_device(): square_sum = lax.psum(jnp.sum(weight_total * weight_total), 'dp')]
    all_gather x0 -> x1, blocking collectives: none -> 20.7 us  [on_device(): parts = lax.all_gather(squares, 'dp', axis=0, tiled=True)]
    convert_element_type x1 -> x0, other arithmetic: 8.3 us -> none  [on_device(): return (grad_total, (weight_total * factor).astype(jnp.bfloat16))]
    unnamed x3 -> x1, local copies, waits for them, and re-layouts: 8.62 us -> 4.32 us
  transfers between devices with their start and end apart: 1 -> 4, of which waited for: 1 -> 4; matrix products, arithmetic and copies ran while one was open for 0% -> 2% of each run, Pallas kernels for 0% -> 8%
where the time goes in v1:
time: 299 us; the launch traced here: 298 us
  waiting for transfers between devices  187 us (63%)
  Pallas kernels  65.6 us (22%)
  blocking collectives  20.7 us (7%)
  between operations  15.1 us (5%)
  local copies, waits for them, and re-layouts  4.92 us (2%)
  other arithmetic  4.51 us (2%)
    all_gather x4, waiting for transfers between devices, on_device(): g = lax.all_gather(piece, 'dp', axis=0, tiled=True)  185 us
    pallas_call x4, Pallas kernels, weight_chunk(): pl.pallas_call(weight_kernel, grid=(width // tile,), in_specs=[pl.BlockSp...  33.1 us
    pallas_call x1, Pallas kernels, attn_grad_of(): pl.pallas_call(functools.partial(attn_kernel, len(gs)), grid=(slots // ti...  21.2 us
    all_gather x1, blocking collectives, on_device(): parts = lax.all_gather(squares, 'dp', axis=0, tiled=True)  20.7 us
    pallas_call x1, Pallas kernels, scaled(): pl.pallas_call(functools.partial(scale_kernel, len(ws), features), grid=(...  11.3 us
  transfers between devices with their start and end apart: 4, of which 4 were waited for; matrix products, arithmetic and copies ran while one was open for 2% of the time, Pallas kernels for 8%

profile of v1, /device:TPU:0, one launch (start us, length us, event | category | flops | bytes accessed | tf_op | source)
XLA Modules:
  0.0 297.8 jit_solution(7480654968984102992)
XLA Ops:
  7.2 0.0 all-gather.5.cloned.1.call-start
  7.9 2.4 slice_select_fusion
  10.3 0.0 all-gather.5.cloned.1.call-update
  10.3 0.0 all-gather.7.cloned.1.call-start
  10.3 0.7 all-gather.7.cloned.1.call-update
  11.0 0.0 all-gather.9.cloned.1.call-start
  11.1 0.7 all-gather.9.cloned.1.call-update
  11.8 0.0 all-gather.11.cloned.1.call-start
  11.8 0.5 all-gather.11.cloned.1.call-update
  13.0 4.3 %copy.7 = bf16[2304,768]{0,1:T(8,128)(2,1)S(1)} copy(bf16[2304,768]{1,0:T(8,128)(2,1)} %param.5) | data formatting | bytes 7077888 | tf_op args[0]
  17.3 2.1 select_bitcast_fusion.at_ref
  19.4 47.1 %all-gather.5.cloned.1.call-done.refs_0_.g_ref = bf16[2304,1024]{1,0:T(8,128)(2,1)} async-done(((bf16[144,1024]{1,0:T(8,128)(2,1)}), bf16[2304,1024]{1,0:T(8,128)(2,1)}) %all-gather.5.cloned.1.call-update) | async-done | bytes 4718608 | tf_op jit(solution)/shard_map/all_gather | solution.py:155
  66.5 0.6 broadcast_in_dim.34.before_ref
  67.1 8.3 %weight_chunk.4 = (f32[768,1024]{1,0:T(8,128)}, f32[8,128]{1,0:T(8,128)}) custom-call(bf16[768,2304]{1,0:T(8,128)(2,1)} %select_bitcast_fusion.at_ref, bf16[2304,1024]{1,0:T(8,128)(2,1)} %all-gather.5.cloned.1.call-done.refs_0_.g_ref, f32[8,128]{1,0:T(8,128)} %broadcast_in_dim.34.before_ref), custom_call_target="tpu_custom_call" | custom-call | flops 3623878656 | bytes 11403264 | tf_op jit(solution)/shard_map/weight_chunk/pallas_call | solution.py:42
  75.4 45.4 %all-gather.7.cloned.1.call-done.refs_1_.g_ref = bf16[2304,1024]{1,0:T(8,128)(2,1)} async-done(((bf16[144,1024]{1,0:T(8,128)(2,1)}), bf16[2304,1024]{1,0:T(8,128)(2,1)}) %all-gather.7.cloned.1.call-update) | async-done | bytes 4718608 | tf_op jit(solution)/shard_map/all_gather | solution.py:155
  120.8 8.3 %weight_chunk.5 = (f32[768,1024]{1,0:T(8,128)}, f32[8,128]{1,0:T(8,128)}) custom-call(bf16[768,2304]{1,0:T(8,128)(2,1)} %select_bitcast_fusion.at_ref, bf16[2304,1024]{1,0:T(8,128)(2,1)} %all-gather.7.cloned.1.call-done.refs_1_.g_ref, f32[8,128]{1,0:T(8,128)} %get-tuple-element.11.before_ref), custom_call_target="tpu_custom_call" | custom-call | flops 3623878656 | bytes 11403264 | tf_op jit(solution)/shard_map/weight_chunk/pallas_call | solution.py:42
  129.1 46.0 %all-gather.9.cloned.1.call-done.refs_2_.g_ref = bf16[2304,1024]{1,0:T(8,128)(2,1)} async-done(((bf16[144,1024]{1,0:T(8,128)(2,1)}), bf16[2304,1024]{1,0:T(8,128)(2,1)}) %all-gather.9.cloned.1.call-update) | async-done | bytes 4718608 | tf_op jit(solution)/shard_map/all_gather | solution.py:155
  175.0 8.3 %weight_chunk.6 = (f32[768,1024]{1,0:T(8,128)}, f32[8,128]{1,0:T(8,128)}) custom-call(bf16[768,2304]{1,0:T(8,128)(2,1)} %select_bitcast_fusion.at_ref, bf16[2304,1024]{1,0:T(8,128)(2,1)} %all-gather.9.cloned.1.call-done.refs_2_.g_ref, f32[8,128]{1,0:T(8,128)} %get-tuple-element.13.before_ref), custom_call_target="tpu_custom_call" | custom-call | flops 3623878656 | bytes 11403264 | tf_op jit(solution)/shard_map/weight_chunk/pallas_call | solution.py:42
  183.3 46.4 %all-gather.11.cloned.1.call-done.refs_3_.g_ref = bf16[2304,1024]{1,0:T(8,128)(2,1)} async-done(((bf16[144,1024]{1,0:T(8,128)(2,1)}), bf16[2304,1024]{1,0:T(8,128)(2,1)}) %all-gather.11.cloned.1.call-update) | async-done | bytes 4718608 | tf_op jit(solution)/shard_map/all_gather | solution.py:155
  229.7 8.3 %weight_chunk.7 = (f32[768,1024]{1,0:T(8,128)}, f32[8,128]{1,0:T(8,128)}) custom-call(bf16[768,2304]{1,0:T(8,128)(2,1)} %select_bitcast_fusion.at_ref, bf16[2304,1024]{1,0:T(8,128)(2,1)} %all-gather.11.cloned.1.call-done.refs_3_.g_ref, f32[8,128]{1,0:T(8,128)} %get-tuple-element.15.before_ref), custom_call_target="tpu_custom_call" | custom-call | flops 3623878656 | bytes 11403264 | tf_op jit(solution)/shard_map/weight_chunk/pallas_call | solution.py:42
  238.0 20.7 %all_gather.19.refs_4_ = f32[128,128]{1,0:T(8,128)} all-gather(f32[8,128]{1,0:T(8,128)} %get-tuple-element.17), channel_id=1, replica_groups=mesh['group'=2,'dp'=16] {'dp'}, dimensions={0}, use_global_device_ids=true | all-gather | bytes 69632 | tf_op jit(solution)/shard_map/all_gather | solution.py:159
  258.7 11.3 %scale.1 = bf16[768,4096]{1,0:T(8,128)(2,1)} custom-call(f32[768,1024]{1,0:T(8,128)} %get-tuple-element.10.refs_0_, f32[768,1024]{1,0:T(8,128)} %get-tuple-element.12.refs_1_, f32[768,1024]{1,0:T(8,128)} %get-tuple-element.14.refs_2_, f32[768,1024]{1,0:T(8,128)} %get-tuple-element.16.refs_3_, f32[128,128]{1,0:T(8,128)} %all_gather.19.refs_4_), custom_call_target="tpu_custom_call" | custom-call | flops 3145728 | bytes 18874368 | tf_op jit(solution)/shard_map/scale/pallas_call | solution.py:125
  270.1 21.2 %attn_grad.1 = bf16[2304,768]{1,0:T(8,128)(2,1)} custom-call(s32[1]{0:T(128)} %mul.9.width_ref, bf16[768,4096]{1,0:T(8,128)(2,1)} %wt_ref.1, bf16[2304,1024]{1,0:T(8,128)(2,1)} %all-gather.5.cloned.1.call-done.refs_0_.g_ref, bf16[2304,1024]{1,0:T(8,128)(2,1)} %all-gather.7.cloned.1.call-done.refs_1_.g_ref, ...), custom_call_target="tpu_custom_call" | custom-call | flops 14495514624 | bytes 28704768 | tf_op jit(solution)/shard_map/attn_grad/pallas_call | solution.py:88
  (2 shorter events, 0.0 us)
Async XLA Ops:
  7.2 59.4 %all-gather.5.cloned.1.call-start = ((), (), s32[]{:S(2)}) async-start(), calls=%async_computation | async-start | bytes 5013504 | tf_op jit(solution)/shard_map/all_gather | solution.py:155
  10.3 110.5 %all-gather.7.cloned.1.call-start = ((), (), s32[]{:S(2)}) async-start(), calls=%async_computation.1 | async-start | bytes 5013504 | tf_op jit(solution)/shard_map/all_gather | solution.py:155
  11.0 164.0 %all-gather.9.cloned.1.call-start = ((), (), s32[]{:S(2)}) async-start(), calls=%async_computation.2 | async-start | bytes 5013504 | tf_op jit(solution)/shard_map/all_gather | solution.py:155
  11.8 218.0 %all-gather.11.cloned.1.call-start = ((), (), s32[]{:S(2)}) async-start(), calls=%async_computation.3 | async-start | bytes 5013504 | tf_op jit(solution)/shard_map/all_gather | solution.py:155
Sparse Core Ops, SparseCore 0:
  10.4 56.0 all-gather.4
  68.8 51.9 all-gather.6
  123.1 51.9 all-gather.8
  177.8 51.9 all-gather.10

commit v2 on v0

v2 whole, which is shorter than its diff:
```python
import functools

import jax
import jax.numpy as jnp
from jax import lax
from jax.experimental import pallas as pl
from jax.experimental.pallas import tpu as pltpu
from jax.sharding import PartitionSpec as P

HEADS = 64
HEAD_DIM = 128
SEQ = 16
MIB = 1024 * 1024


def params(mib):
    return pltpu.CompilerParams(vmem_limit_bytes=mib * MIB)


def weight_kernel(at_ref, g_ref, w_ref, squares_ref):
    slots, features = g_ref.shape
    tile = 512
    squares_ref[...] = jnp.zeros_like(squares_ref)

    def body(g_tile):
        start = pl.multiple_of(pl.program_id(0) * tile, tile)
        w = jnp.dot(at_ref[...], g_tile[...], preferred_element_type=jnp.float32)
        w_ref[:, pl.ds(start, tile)] = w
        folded = jnp.sum((w * w).reshape(w.shape[0] // 8, 8, tile), axis=0)
        total = squares_ref[...]
        for lane in range(0, tile, 128):
            total = total + folded[:, lane : lane + 128]
        squares_ref[...] = total

    pltpu.emit_pipeline(
        body,
        grid=(features // tile,),
        in_specs=[pl.BlockSpec((slots, tile), lambda j: (0, j))],
    )(g_ref)


def weight_full(at, g):
    capacity, slots = at.shape
    features = g.shape[1]
    return pl.pallas_call(
        weight_kernel,
        in_specs=[
            pl.BlockSpec(memory_space=pltpu.VMEM),
            pl.BlockSpec(memory_space=pl.ANY),
        ],
        out_specs=[
            pl.BlockSpec(memory_space=pltpu.VMEM),
            pl.BlockSpec(memory_space=pltpu.VMEM),
        ],
        out_shape=[
            pltpu.VMEM((capacity, features), jnp.float32),
            pltpu.VMEM((8, 128), jnp.float32),
        ],
        compiler_params=params(24),
        cost_estimate=pl.CostEstimate(
            flops=2 * capacity * slots * features,
            bytes_accessed=2 * slots * (capacity + features),
            transcendentals=0,
        ),
        name="weight_full",
    )(pltpu.with_memory_space_constraint(at, pltpu.VMEM), g)


def attn_kernel(width_ref, w_ref, g_ref, *refs):
    out_ref = refs[-1]
    total = lax.dot_general(
        g_ref[...], w_ref[...], (((1,), (1,)), ((), ())), preferred_element_type=jnp.float32
    )
    column = lax.broadcasted_iota(jnp.int32, total.shape, 1)
    out_ref[...] = jnp.where(column < width_ref[0], total, 0.0).astype(jnp.bfloat16)


def attn_rows(g, weight, live_width, half, before):
    capacity, features = weight.shape
    slots = g.shape[0]
    tile = slots // 6
    steps = slots // 2 // tile
    first = half * steps
    extra = [] if before is None else [before]
    return pl.pallas_call(
        attn_kernel,
        grid=(steps,),
        in_specs=[
            pl.BlockSpec(memory_space=pltpu.SMEM),
            pl.BlockSpec(memory_space=pltpu.VMEM),
            pl.BlockSpec((tile, features), lambda j: (first + j, 0)),
        ]
        + [pl.BlockSpec(memory_space=pl.ANY) for _ in extra],
        out_specs=pl.BlockSpec((tile, capacity), lambda j: (first + j, 0)),
        out_shape=jax.ShapeDtypeStruct((slots, capacity), jnp.bfloat16),
        input_output_aliases={3: 0} if extra else {},
        compiler_params=params(24),
        cost_estimate=pl.CostEstimate(
            flops=capacity * slots * features,
            bytes_accessed=slots * features + capacity * slots,
            transcendentals=0,
        ),
        name="attn_rows",
    )(live_width, weight, g, *extra)


def scale_kernel(w_ref, squares_ref, out_ref):
    capacity, features = w_ref.shape
    tile = 64
    square_sum = jnp.sum(
        jnp.sum(squares_ref[...], axis=0, keepdims=True), axis=1, keepdims=True
    )
    factor = jnp.minimum(
        1.0, 1.0 / jnp.sqrt(square_sum / (HEADS * HEAD_DIM * features) + 1e-06)
    )

    def body(out_tile):
        start = pl.multiple_of(pl.program_id(0) * tile, tile)
        out_tile[...] = (w_ref[pl.ds(start, tile), :] * factor).astype(jnp.bfloat16)

    pltpu.emit_pipeline(
        body,
        grid=(capacity // tile,),
        out_specs=[pl.BlockSpec((tile, features), lambda j: (j, 0))],
    )(out_ref)


def scaled(w, squares):
    capacity, features = w.shape
    return pl.pallas_call(
        scale_kernel,
        in_specs=[
            pl.BlockSpec(memory_space=pltpu.VMEM),
            pl.BlockSpec(memory_space=pltpu.VMEM),
        ],
        out_specs=pl.BlockSpec(memory_space=pl.ANY),
        out_shape=jax.ShapeDtypeStruct((capacity, features), jnp.bfloat16),
        compiler_params=params(24),
        cost_estimate=pl.CostEstimate(
            flops=capacity * features,
            bytes_accessed=2 * capacity * features,
            transcendentals=0,
        ),
        name="scale",
    )(pltpu.with_memory_space_constraint(w, pltpu.VMEM), squares)


def exchange(x, devices, stride, radix):
    total = x
    for shift in range(1, radix):
        pairs = []
        for d in range(devices):
            digit = d // stride % radix
            pairs.append((d, d + ((digit + shift) % radix - digit) * stride))
        total = total + lax.ppermute(x, "dp", pairs)
    return total


def on_device(devices, attn_out, out_grad, o_weight, head_counts, seq_counts):
    row_count = out_grad.shape[0]
    capacity = o_weight.shape[0]
    live_width = head_counts * HEAD_DIM
    row_live = lax.broadcasted_iota(jnp.int32, (row_count, 1), 0) < seq_counts[0] * SEQ
    head_live = lax.broadcasted_iota(jnp.int32, (1, capacity), 1) < live_width[0]
    grad_live = jnp.where(row_live, out_grad, jnp.zeros_like(out_grad))
    g = lax.all_gather(grad_live, "dp", axis=0, tiled=True)
    g = pltpu.with_memory_space_constraint(g, pltpu.HBM)
    at = jnp.where(head_live, attn_out, jnp.zeros_like(attn_out)).T
    w, squares = weight_full(at, g)
    weight = pltpu.with_memory_space_constraint(o_weight, pltpu.VMEM)
    attn_grad, stride, half = None, 1, 0
    while stride < devices:
        radix = min(4, devices // stride)
        squares = exchange(squares, devices, stride, radix)
        if half < 2:
            attn_grad = attn_rows(g, weight, live_width, half, attn_grad)
        stride, half = stride * radix, half + 1
    return attn_grad, scaled(w, squares)


def solution(mesh):
    placed = (
        P("group", "dp"),
        P(("group", "dp"), None),
        P("dp", None),
        P("dp"),
        P(("group", "dp")),
    )
    return jax.shard_map(
        functools.partial(on_device, mesh.shape["dp"]),
        mesh=mesh,
        in_specs=placed,
        out_specs=(P("group", "dp"), P(("group", "dp"), None)),
        check_vma=False,
    )
```

time: 214 us -> 175 us (0.82)
  Pallas kernels: 0 us -> 44.4 us
  matrix products: 43.3 us -> 0 us
  blocking collectives: 33.2 us -> 0 us
  starting transfers between devices: 0.04 us -> 8.22 us
  waiting for transfers between devices: 101 us -> 95 us
  other arithmetic: 10.9 us -> 4.96 us
    pallas_call x0 -> x4, Pallas kernels: none -> 44.4 us  [the longest x2 21.3 us: attn_rows(): pl.pallas_call(attn_kernel, grid=(steps,), in_specs=[pl.BlockSpec(memory_...]
    dot_general x2 -> x0, matrix products: 43.3 us -> none  [the longest x1 22.5 us: on_device(): lax.dot_general(attn_out, gathered, (((0,), (0,)), ((), ())), preferred_e...]
    psum x1 -> x0, blocking collectives: 33.2 us -> none  [on_device(): square_sum = lax.psum(jnp.sum(weight_total * weight_total), 'dp')]
    convert_element_type x1 -> x0, other arithmetic: 8.3 us -> none  [on_device(): return (grad_total, (weight_total * factor).astype(jnp.bfloat16))]
    ppermute x0 -> x6, starting transfers between devices: none -> 8.18 us  [exchange(): total = total + lax.ppermute(x, 'dp', pairs)]
    all_gather x1, waiting for transfers between devices: 101 us -> 95 us  [on_device(): g = lax.all_gather(grad_live, 'dp', axis=0, tiled=True)]
    transpose x0 -> x1, other arithmetic: none -> 2.31 us  [on_device(): at = jnp.where(head_live, attn_out, jnp.zeros_like(attn_out)).T]
    unnamed x3 -> x5, local copies, waits for them, and re-layouts: 8.62 us -> 6.62 us
  transfers between devices with their start and end apart: 1 -> 7, of which waited for: 1 -> 1; matrix products, arithmetic and copies ran while one was open for 0% -> 4% of each run, Pallas kernels for 0% -> 12%
where the time goes in v2:
time: 175 us
  waiting for transfers between devices  95 us (54%)
  Pallas kernels  44.4 us (25%)
  between operations  15.5 us (9%)
  starting transfers between devices  8.22 us (5%)
  local copies, waits for them, and re-layouts  6.62 us (4%)
  other arithmetic  4.96 us (3%)
    all_gather x1, waiting for transfers between devices, on_device(): g = lax.all_gather(grad_live, 'dp', axis=0, tiled=True)  95 us
    pallas_call x2, Pallas kernels, attn_rows(): pl.pallas_call(attn_kernel, grid=(steps,), in_specs=[pl.BlockSpec(memory_...  21.3 us
    pallas_call x1, Pallas kernels, weight_full(): pl.pallas_call(weight_kernel, in_specs=[pl.BlockSpec(memory_space=pltpu.V...  17.7 us
    ppermute x6, starting transfers between devices, exchange(): total = total + lax.ppermute(x, 'dp', pairs)  8.18 us
    unnamed x5, local copies, waits for them, and re-layouts  6.62 us
    pallas_call x1, Pallas kernels, scaled(): pl.pallas_call(scale_kernel, in_specs=[pl.BlockSpec(memory_space=pltpu.VM...  5.37 us
  transfers between devices with their start and end apart: 7, of which 1 were waited for; matrix products, arithmetic and copies ran while one was open for 4% of the time, Pallas kernels for 12%

profile of v2, /device:TPU:0, one launch (start us, length us, event | category | flops | bytes accessed | tf_op | source)
XLA Modules:
  0.0 174.8 jit_solution(11702468912318730351)
XLA Ops:
  7.2 0.0 copy-start.1
  7.2 0.0 all-gather.2.cloned.1.call-start
  8.0 2.6 %broadcast_select_fusion = bf16[144,4096]{1,0:T(8,128)(2,1)} fusion(bf16[144,4096]{1,0:T(8,128)(2,1)} %param.6, pred[144]{0:T(512)(128)(4,1)S(1)} %iota_compare_fusion.1), kind=kLoop, calls=%fused_computation.1 | loop fusion | flops 589824 | bytes 2359440 | tf_op jit(solution)/shard_map/jit(_where)/select_n | solution.py:165
  10.7 0.0 all-gather.2.cloned.1.call-update
  11.3 0.0 copy-done.1
  11.3 3.8 %copy.8 = bf16[2304,768]{0,1:T(8,128)(2,1)} copy(bf16[2304,768]{1,0:T(8,128)(2,1)S(1)} %copy-done.1) | data formatting | bytes 7077888 | tf_op args[0]
  15.2 2.3 %select_bitcast_fusion.at_ref = bf16[768,2304]{1,0:T(8,128)(2,1)S(1)} fusion(bf16[2304,768]{0,1:T(8,128)(2,1)} %copy.8, pred[768]{0:T(1024)(128)(4,1)S(1)} %iota_compare_fusion), kind=kLoop, calls=%fused_computation | loop fusion | flops 1769472 | bytes 7078656 | tf_op jit(solution)/shard_map/transpose | solution.py:168
  17.5 95.0 %all-gather.2.cloned.1.call-done.g_ref = bf16[2304,4096]{1,0:T(8,128)(2,1)} async-done(((bf16[144,4096]{1,0:T(8,128)(2,1)}), bf16[2304,4096]{1,0:T(8,128)(2,1)}) %all-gather.2.cloned.1.call-update) | async-done | bytes 18874384 | tf_op jit(solution)/shard_map/all_gather | solution.py:166
  112.5 17.7 %weight_full.1 = (f32[768,4096]{1,0:T(8,128)S(1)}, f32[8,128]{1,0:T(8,128)S(1)}) custom-call(bf16[768,2304]{1,0:T(8,128)(2,1)S(1)} %select_bitcast_fusion.at_ref, bf16[2304,4096]{1,0:T(8,128)(2,1)} %all-gather.2.cloned.1.call-done.g_ref), custom_call_target="tpu_custom_call" | custom-call | flops 14495514624 | bytes 22413312 | tf_op jit(solution)/shard_map/weight_full/pallas_call | solution.py:45
  130.2 0.3 collective-permute-start
  130.5 1.3 collective-permute-start.1
  131.8 1.2 collective-permute-start.2
  133.0 0.0 copy-start
  133.0 2.8 %copy-done = bf16[768,4096]{1,0:T(8,128)(2,1)S(1)} copy-done((bf16[768,4096]{1,0:T(8,128)(2,1)S(1)}, bf16[768,4096]{1,0:T(8,128)(2,1)}, u32[]{:S(2)}) %copy-start) | copy-done | bytes 6291480
  135.8 10.7 %attn_rows.2.refs_0_ = bf16[2304,768]{1,0:T(8,128)(2,1)} custom-call(s32[1]{0:T(128)} %mul.9.width_ref, bf16[768,4096]{1,0:T(8,128)(2,1)S(1)} %copy-done, bf16[2304,4096]{1,0:T(8,128)(2,1)} %all-gather.2.cloned.1.call-done.g_ref), custom_call_target="tpu_custom_call" | custom-call | flops 7247757312 | bytes 11206656 | tf_op jit(solution)/shard_map/attn_rows/pallas_call | solution.py:85
  146.5 0.0 collective-permute-done
  146.5 0.0 collective-permute-done.1
  146.5 0.0 collective-permute-done.2
  146.5 1.5 collective-permute-start.3
  148.0 1.7 collective-permute-start.4
  149.7 2.2 %collective-permute-start.5 = (f32[8,128]{1,0:T(8,128)S(1)}, f32[8,128]{1,0:T(8,128)S(1)}, u32[]{:S(2)}, u32[]{:S(2)}) collective-permute-start(f32[8,128]{1,0:T(8,128)S(1)} %add_add_fusion.1), channel_id=1, source_target_pairs={{0,12},{1,13},{2,14},{3,15},{4,0},{5,1},{6,2},{7,3},{8,4},{9,5},{1... | collective-permute-start | bytes 12296 | tf_op jit(solution)/shard_map/ppermute | solution.py:155
  151.9 10.7 %attn_rows.3 = bf16[2304,768]{1,0:T(8,128)(2,1)} custom-call(s32[1]{0:T(128)} %mul.9.width_ref, bf16[768,4096]{1,0:T(8,128)(2,1)S(1)} %copy-done, bf16[2304,4096]{1,0:T(8,128)(2,1)} %all-gather.2.cloned.1.call-done.g_ref, bf16[2304,768]{1,0:T(8,128)(2,1)} %attn_rows.2.refs_0_), custom_call_target="tpu_custom_call", output_to_operand_aliasing={{}: (3, {})} | custom-call | flops 7247757312 | bytes 11206656 | tf_op jit(solution)/shard_map/attn_rows/pallas_call | solution.py:85
  162.5 0.0 collective-permute-done.3
  162.6 0.0 collective-permute-done.4
  162.6 0.0 collective-permute-done.5
  162.6 5.4 %scale.1 = bf16[768,4096]{1,0:T(8,128)(2,1)} custom-call(f32[768,4096]{1,0:T(8,128)S(1)} %get-tuple-element.4.w_ref, f32[8,128]{1,0:T(8,128)S(1)} %add_add_fusion.squares_ref), custom_call_target="tpu_custom_call" | custom-call | flops 3145728 | bytes 6291456 | tf_op jit(solution)/shard_map/scale/pallas_call | solution.py:130
  (4 shorter events, 0.0 us)
Async XLA Ops:
  7.2 4.2 %copy-start.1 = (bf16[2304,768]{1,0:T(8,128)(2,1)S(1)}, bf16[2304,768]{1,0:T(8,128)(2,1)}, u32[]{:S(2)}) copy-start(bf16[2304,768]{1,0:T(8,128)(2,1)} %param.5) | copy-start | bytes 10616836
  7.2 105.3 %all-gather.2.cloned.1.call-start = ((), (), s32[]{:S(2)}) async-start(), calls=%async_computation | async-start | bytes 20054016 | tf_op jit(solution)/shard_map/all_gather | solution.py:166
  130.2 16.3 %collective-permute-start = (f32[8,128]{1,0:T(8,128)S(1)}, f32[8,128]{1,0:T(8,128)S(1)}, u32[]{:S(2)}, u32[]{:S(2)}) collective-permute-start(f32[8,128]{1,0:T(8,128)S(1)} %get-tuple-element.5), channel_id=1, source_target_pairs={{0,1},{1,2},{2,3},{3,0},{4,5},{5,6},{6,7},{7,4},{8,9},{9,10},{10,1... | collective-permute-start | bytes 12296 | tf_op jit(solution)/shard_map/ppermute | solution.py:155
  130.5 15.9 %collective-permute-start.1 = (f32[8,128]{1,0:T(8,128)S(1)}, f32[8,128]{1,0:T(8,128)S(1)}, u32[]{:S(2)}, u32[]{:S(2)}) collective-permute-start(f32[8,128]{1,0:T(8,128)S(1)} %get-tuple-element.5), channel_id=1, source_target_pairs={{0,2},{1,3},{2,0},{3,1},{4,6},{5,7},{6,4},{7,5},{8,10},{9,11},{10,... | collective-permute-start | bytes 12296 | tf_op jit(solution)/shard_map/ppermute | solution.py:155
  131.8 14.7 %collective-permute-start.2 = (f32[8,128]{1,0:T(8,128)S(1)}, f32[8,128]{1,0:T(8,128)S(1)}, u32[]{:S(2)}, u32[]{:S(2)}) collective-permute-start(f32[8,128]{1,0:T(8,128)S(1)} %get-tuple-element.5), channel_id=1, source_target_pairs={{0,3},{1,0},{2,1},{3,2},{4,7},{5,4},{6,5},{7,6},{8,11},{9,8},{10,9... | collective-permute-start | bytes 12296 | tf_op jit(solution)/shard_map/ppermute | solution.py:155
  133.0 2.8 %copy-start = (bf16[768,4096]{1,0:T(8,128)(2,1)S(1)}, bf16[768,4096]{1,0:T(8,128)(2,1)}, u32[]{:S(2)}) copy-start(bf16[768,4096]{1,0:T(8,128)(2,1)} %w_ref.3) | copy-start | bytes 18874372
  146.5 16.1 %collective-permute-start.3 = (f32[8,128]{1,0:T(8,128)S(1)}, f32[8,128]{1,0:T(8,128)S(1)}, u32[]{:S(2)}, u32[]{:S(2)}) collective-permute-start(f32[8,128]{1,0:T(8,128)S(1)} %add_add_fusion.1), channel_id=1, source_target_pairs={{0,4},{1,5},{2,6},{3,7},{4,8},{5,9},{6,10},{7,11},{8,12},{9,13},{1... | collective-permute-start | bytes 12296 | tf_op jit(solution)/shard_map/ppermute | solution.py:155
  148.0 14.5 %collective-permute-start.4 = (f32[8,128]{1,0:T(8,128)S(1)}, f32[8,128]{1,0:T(8,128)S(1)}, u32[]{:S(2)}, u32[]{:S(2)}) collective-permute-start(f32[8,128]{1,0:T(8,128)S(1)} %add_add_fusion.1), channel_id=1, source_target_pairs={{0,8},{1,9},{2,10},{3,11},{4,12},{5,13},{6,14},{7,15},{8,0},{9,1},... | collective-permute-start | bytes 12296 | tf_op jit(solution)/shard_map/ppermute | solution.py:155
  149.7 12.8 %collective-permute-start.5 = (f32[8,128]{1,0:T(8,128)S(1)}, f32[8,128]{1,0:T(8,128)S(1)}, u32[]{:S(2)}, u32[]{:S(2)}) collective-permute-start(f32[8,128]{1,0:T(8,128)S(1)} %add_add_fusion.1), channel_id=1, source_target_pairs={{0,12},{1,13},{2,14},{3,15},{4,0},{5,1},{6,2},{7,3},{8,4},{9,5},{1... | collective-permute-start | bytes 12296 | tf_op jit(solution)/shard_map/ppermute | solution.py:155
Sparse Core Ops, SparseCore 0:
  10.8 101.6 all-gather.1

commit v3 on v0

v3 whole, which is shorter than its diff:
```python
import functools

import jax
import jax.numpy as jnp
import numpy as np
from jax import lax
from jax.experimental import pallas as pl
from jax.experimental.pallas import tpu as pltpu
from jax.sharding import PartitionSpec as P

HEADS = 64
HEAD_DIM = 128
SEQ = 16
TILE = 512
MIB = 1024 * 1024


class Ring:
    def __init__(self, devices, columns):
        self.devices = devices
        self.length = devices // 2
        rows = self.length // columns
        if columns == 1:
            self.chips = list(range(rows))
        else:
            self.chips = [2 * z for z in range(rows)]
            self.chips += [2 * z + 1 for z in reversed(range(rows))]
        self.position = {chip: p for p, chip in enumerate(self.chips)}

    def device(self, position, core):
        return 2 * self.chips[position % self.length] + core

    def shift(self, step):
        return [
            (self.device(p, core), self.device(p + step, core))
            for p in range(self.length)
            for core in range(2)
        ]

    def swap(self):
        return [(d, d ^ 1) for d in range(self.devices)]

    def owners(self, offsets):
        table = []
        for d in range(self.devices):
            p, core = self.position[d // 2], d % 2
            row = []
            for offset in offsets:
                row += [self.device(p + offset, core), self.device(p + offset, 1 - core)]
            table.append(row)
        return np.array(table, np.int32)


def pick_kernel(owners_ref, width_ref, a_ref, out_ref):
    column = lax.broadcasted_iota(jnp.int32, a_ref.shape, 1)
    out_ref[...] = jnp.where(column < width_ref[0], a_ref[...], jnp.zeros_like(a_ref))


def picked(attn_out, owners, live_width, rows):
    slots, capacity = attn_out.shape
    return pl.pallas_call(
        pick_kernel,
        grid_spec=pltpu.PrefetchScalarGridSpec(
            num_scalar_prefetch=2,
            grid=(slots // rows,),
            in_specs=[pl.BlockSpec((rows, capacity), lambda i, owners, w: (owners[i], 0))],
            out_specs=pl.BlockSpec((rows, capacity), lambda i, owners, w: (i, 0)),
        ),
        out_shape=jax.ShapeDtypeStruct((slots, capacity), attn_out.dtype),
        cost_estimate=pl.CostEstimate(
            flops=0, bytes_accessed=4 * slots * capacity, transcendentals=0
        ),
        name="picked",
    )(owners, live_width, attn_out)


def phase_kernel(spec, *refs):
    do_weight, do_attn, fresh, squares, pieces, halves, rows = spec
    refs = list(refs)
    owners_ref, width_ref = refs.pop(0), refs.pop(0)
    at_ref = refs.pop(0) if do_weight else None
    weight_ref = refs.pop(0) if do_attn else None
    g_refs = [[refs.pop(0) for _ in range(pieces)] for _ in range(halves)]
    if do_weight and not fresh:
        refs.pop(0)
    if do_attn and not fresh:
        refs.pop(0)
    w_ref = refs.pop(0) if do_weight else None
    out_ref = refs.pop(0) if do_attn else None
    squares_ref = refs.pop(0)
    if do_attn:
        total_ref, block_ref, sems = refs
        total_ref[...] = jnp.zeros_like(total_ref)
    squares_ref[...] = jnp.zeros_like(squares_ref)
    span = g_refs[0][0].shape[1]

    def body(half, *tiles):
        start = pl.multiple_of(half * span + pl.program_id(0) * TILE, TILE)
        g = jnp.concatenate([t[...] for t in tiles], axis=0)
        if do_weight:
            w = jnp.dot(at_ref[...], g, preferred_element_type=jnp.float32)
            if not fresh:
                w = w + w_ref[:, pl.ds(start, TILE)]
            w_ref[:, pl.ds(start, TILE)] = w
        if squares:
            folded = jnp.sum((w * w).reshape(w.shape[0] // 8, 8, TILE), axis=0)
            total = squares_ref[...]
            for lane in range(0, TILE, 128):
                total = total + folded[:, lane : lane + 128]
            squares_ref[...] = total
        if do_attn:
            total_ref[...] += lax.dot_general(
                g,
                weight_ref[:, pl.ds(start, TILE)],
                (((1,), (1,)), ((), ())),
                preferred_element_type=jnp.float32,
            )

    for half in range(halves):
        pltpu.emit_pipeline(
            functools.partial(body, half),
            grid=(span // TILE,),
            in_specs=[pl.BlockSpec((rows, TILE), lambda j: (0, j))] * pieces,
        )(*g_refs[half])
    if do_attn:
        total = total_ref[...]
        column = lax.broadcasted_iota(jnp.int32, total.shape, 1)
        block_ref[...] = jnp.where(column < width_ref[0], total, 0.0).astype(jnp.bfloat16)
        copies = [
            pltpu.make_async_copy(
                block_ref.at[pl.ds(i * rows, rows)],
                out_ref.at[pl.ds(pl.multiple_of(owners_ref[i] * rows, rows), rows)],
                sems.at[i],
            )
            for i in range(pieces)
        ]
        for copy in copies:
            copy.start()
        for copy in copies:
            copy.wait()


def phase(owners, live_width, at, weight, gs, w, out, slots, squares=False):
    halves, pieces = len(gs), len(gs[0])
    rows = gs[0][0].shape[0]
    features = gs[0][0].shape[1] * halves
    do_weight, do_attn = at is not None, weight is not None
    capacity = at.shape[0] if do_weight else weight.shape[0]
    fresh = (w is None) if do_weight else (out is None)
    vmem = pl.BlockSpec(memory_space=pltpu.VMEM)
    smem = pl.BlockSpec(memory_space=pltpu.SMEM)
    hbm = pl.BlockSpec(memory_space=pl.ANY)

    args, specs, outs, out_specs, aliases, scratch = [], [], [], [], {}, []

    def add(arg, spec):
        args.append(arg)
        specs.append(spec)

    add(owners, smem)
    add(live_width, smem)
    if do_weight:
        add(pltpu.with_memory_space_constraint(at, pltpu.VMEM), vmem)
    if do_attn:
        add(weight, vmem)
    for group in gs:
        for g in group:
            add(g, hbm)
    if do_weight:
        if not fresh:
            aliases[len(args)] = len(outs)
            add(pltpu.with_memory_space_constraint(w, pltpu.VMEM), vmem)
        outs.append(pltpu.VMEM((capacity, features), jnp.float32))
        out_specs.append(vmem)
    if do_attn:
        if not fresh:
            aliases[len(args)] = len(outs)
            add(out, hbm)
        outs.append(jax.ShapeDtypeStruct((slots, capacity), jnp.bfloat16))
        out_specs.append(hbm)
        scratch = [
            pltpu.VMEM((rows * pieces, capacity), jnp.float32),
            pltpu.VMEM((rows * pieces, capacity), jnp.bfloat16),
            pltpu.SemaphoreType.DMA((pieces,)),
        ]
    outs.append(pltpu.VMEM((8, 128), jnp.float32))
    out_specs.append(vmem)
    dots = do_weight + do_attn
    return pl.pallas_call(
        functools.partial(
            phase_kernel, (do_weight, do_attn, fresh, squares, pieces, halves, rows)
        ),
        in_specs=specs,
        out_specs=out_specs,
        out_shape=outs,
        scratch_shapes=scratch,
        input_output_aliases=aliases,
        compiler_params=pltpu.CompilerParams(vmem_limit_bytes=16 * MIB),
        cost_estimate=pl.CostEstimate(
            flops=dots * capacity * rows * pieces * features // 4,
            bytes_accessed=2 * rows * pieces * features,
            transcendentals=0,
        ),
        name="phase_" + "w" * do_weight + "a" * do_attn,
    )(*args)


def scale_kernel(w_ref, squares_ref, out_ref):
    capacity, features = w_ref.shape
    tile = 64
    square_sum = jnp.sum(
        jnp.sum(squares_ref[...], axis=0, keepdims=True), axis=1, keepdims=True
    )
    factor = jnp.minimum(
        1.0, 1.0 / jnp.sqrt(square_sum / (HEADS * HEAD_DIM * features) + 1e-06)
    )

    def body(out_tile):
        start = pl.multiple_of(pl.program_id(0) * tile, tile)
        out_tile[...] = (w_ref[pl.ds(start, tile), :] * factor).astype(jnp.bfloat16)

    pltpu.emit_pipeline(
        body,
        grid=(capacity // tile,),
        out_specs=[pl.BlockSpec((tile, features), lambda j: (j, 0))],
    )(out_ref)


def scaled(w, squares):
    capacity, features = w.shape
    vmem = pl.BlockSpec(memory_space=pltpu.VMEM)
    return pl.pallas_call(
        scale_kernel,
        in_specs=[vmem, vmem],
        out_specs=pl.BlockSpec(memory_space=pl.ANY),
        out_shape=jax.ShapeDtypeStruct((capacity, features), jnp.bfloat16),
        compiler_params=pltpu.CompilerParams(vmem_limit_bytes=16 * MIB),
        cost_estimate=pl.CostEstimate(
            flops=capacity * features,
            bytes_accessed=2 * capacity * features,
            transcendentals=0,
        ),
        name="scale",
    )(pltpu.with_memory_space_constraint(w, pltpu.VMEM), squares)


def after(done, *arrays):
    hbm = pl.BlockSpec(memory_space=pl.ANY)
    return pl.pallas_call(
        lambda *refs: None,
        in_specs=[hbm] * (len(arrays) + 1),
        out_specs=[hbm] * len(arrays),
        out_shape=[jax.ShapeDtypeStruct(x.shape, x.dtype) for x in arrays],
        input_output_aliases={i: i for i in range(len(arrays))},
        name="after",
    )(*arrays, done)


def exchange(x, devices, stride, radix):
    total = x
    for shift in range(1, radix):
        pairs = []
        for d in range(devices):
            digit = d // stride % radix
            pairs.append((d, d + ((digit + shift) % radix - digit) * stride))
        total = total + lax.ppermute(x, "dp", pairs)
    return total


def on_device(ring, attn_out, out_grad, o_weight, head_counts, seq_counts):
    rows, features = out_grad.shape
    slots = attn_out.shape[0]
    devices, last = ring.devices, ring.length // 2
    live_width = head_counts * HEAD_DIM
    row_live = lax.broadcasted_iota(jnp.int32, (rows, 1), 0) < seq_counts[0] * SEQ
    own = jnp.where(row_live, out_grad, jnp.zeros_like(out_grad))

    offsets = [0] + [s * k for k in range(1, last) for s in (-1, 1)] + [last]
    owners = jnp.asarray(ring.owners(offsets))[lax.axis_index("dp")]
    a = picked(attn_out, owners, live_width, rows)
    weight = pltpu.with_memory_space_constraint(o_weight, pltpu.VMEM)

    def swap(x):
        return lax.ppermute(x, "dp", ring.swap())

    def forward(x):
        return lax.ppermute(x, "dp", ring.shift(1))

    def backward(x):
        return lax.ppermute(x, "dp", ring.shift(-1))

    arrived = [[[own, swap(own)]]]
    ahead, behind = forward(own), backward(own)
    w, out, begin, late = None, None, 0, []
    for k in range(last + 1):
        (gs,) = arrived
        count = len(gs[0])
        ids = owners[begin : begin + count]
        at = a[begin * rows : (begin + count) * rows].T
        begin += count
        if k < last - 1:
            w, out, done = phase(ids, live_width, at, weight, gs, w, out, slots)
        else:
            w, done = phase(ids, live_width, at, None, gs, w, None, slots, k == last)
            late.append((ids, gs))
        if k < last - 1:
            ahead, behind = after(done, ahead, behind)
            arrived = [[[ahead, swap(ahead), behind, swap(behind)]]]
            if k + 2 < last:
                ahead, behind = forward(ahead), backward(behind)
            else:
                ahead = forward(ahead[:, : features // 2])
                behind = backward(behind[:, features // 2 :])
        elif k == last - 1:
            ahead, behind = after(done, ahead, behind)
            arrived = [[[ahead, swap(ahead)], [behind, swap(behind)]]]
    squares = done

    stride = 1
    while stride < devices:
        radix = min(4, devices // stride)
        squares = exchange(squares, devices, stride, radix)
        if late:
            ids, gs = late.pop(0)
            out, done = phase(ids, live_width, None, weight, gs, None, out, slots)
        stride *= radix
    return out, scaled(w, squares)


def solution(mesh):
    placed = (
        P("group", "dp"),
        P(("group", "dp"), None),
        P("dp", None),
        P("dp"),
        P(("group", "dp")),
    )
    ring = Ring(mesh.shape["dp"], 2 if mesh.shape["group"] == 2 else 1)
    return jax.shard_map(
        functools.partial(on_device, ring),
        mesh=mesh,
        in_specs=placed,
        out_specs=(P("group", "dp"), P(("group", "dp"), None)),
        check_vma=False,
    )
```

time: 214 us -> 199 us (0.930)
  waiting for transfers between devices: 101 us -> 0.76 us
  Pallas kernels: 0 us -> 85.5 us
  local copies, waits for them, and re-layouts: 8.62 us -> 87 us
  matrix products: 43.3 us -> 0 us
  blocking collectives: 33.2 us -> 0 us
  starting transfers between devices: 0.04 us -> 20.3 us
  between operations: 16.2 us -> 2.26 us
  other arithmetic: 10.9 us -> 1.44 us
    all_gather x1 -> x0, waiting for transfers between devices: 101 us -> none  [on_device(): gathered = lax.all_gather(grad_live, 'dp', axis=0, tiled=True)]
    pallas_call x0 -> x13, Pallas kernels: none -> 85.5 us  [the longest x7 69.5 us: phase(): pl.pallas_call(functools.partial(phase_kernel, (do_weight, do_attn, fresh...]
    unnamed x3 -> x85, local copies, waits for them, and re-layouts: 8.62 us -> 77.3 us
    dot_general x2 -> x0, matrix products: 43.3 us -> none  [the longest x1 22.5 us: on_device(): lax.dot_general(attn_out, gathered, (((0,), (0,)), ((), ())), preferred_e...]
    psum x1 -> x0, blocking collectives: 33.2 us -> none  [on_device(): square_sum = lax.psum(jnp.sum(weight_total * weight_total), 'dp')]
    ppermute x0 -> x23, starting transfers between devices: none -> 20.3 us  [the longest x6 8.97 us: exchange(): total = total + lax.ppermute(x, 'dp', pairs)]
    slice x0 -> x6, local copies, waits for them, and re-layouts: none -> 8.45 us  [the longest x2 5.53 us: on_device(): at = a[begin * rows:(begin + count) * rows].T]
    convert_element_type x1 -> x0, other arithmetic: 8.3 us -> none  [on_device(): return (grad_total, (weight_total * factor).astype(jnp.bfloat16))]
  transfers between devices with their start and end apart: 1 -> 23, of which waited for: 1 -> 3; matrix products, arithmetic and copies ran while one was open for 0% -> 10% of each run, Pallas kernels for 0% -> 37%
where the time goes in v3:
time: 199 us; the launch traced here: 197 us
  local copies, waits for them, and re-layouts  87 us (44%)
  Pallas kernels  85.5 us (43%)
  starting transfers between devices  20.3 us (10%)
  between operations  2.26 us (1%)
    unnamed x85, local copies, waits for them, and re-layouts  77.3 us
    pallas_call x7, Pallas kernels, phase(): pl.pallas_call(functools.partial(phase_kernel, (do_weight, do_attn, fresh...  69.5 us
    pallas_call x1, Pallas kernels, picked(): pl.pallas_call(pick_kernel, grid_spec=pltpu.PrefetchScalarGridSpec(num_sc...  10.6 us
    ppermute x6, starting transfers between devices, exchange(): total = total + lax.ppermute(x, 'dp', pairs)  8.97 us
    ppermute x4, starting transfers between devices, forward(): return lax.ppermute(x, 'dp', ring.shift(1))  8.65 us
    slice x2, local copies, waits for them, and re-layouts, on_device(): at = a[begin * rows:(begin + count) * rows].T  5.53 us
    pallas_call x1, Pallas kernels, scaled(): pl.pallas_call(scale_kernel, in_specs=[vmem, vmem], out_specs=pl.BlockSpe...  5.37 us
  transfers between devices with their start and end apart: 23, of which 3 were waited for; matrix products, arithmetic and copies ran while one was open for 10% of the time, Pallas kernels for 37%

profile of v3, /device:TPU:0, one launch (start us, length us, event | category | flops | bytes accessed | tf_op | source)
XLA Modules:
  0.0 197.2 jit_solution(11371920897601762017)
XLA Ops:
  1.3 1.4 broadcast_select_fusion.refs_4_
  2.7 0.5 collective-permute-start.2
  3.2 2.6 %collective-permute-start = (bf16[144,4096]{1,0:T(8,128)(2,1)S(1)}, bf16[144,4096]{1,0:T(8,128)(2,1)S(1)}, u32[]{:S(2)}, u32[]{:S(2)}) collective-permute-start(bf16[144,4096]{1,0:T(8,128)(2,1)S(1)} %broadcast_select_fusion.refs_4_), channel_id=1, source_target_pairs={{0,4},{1,5},{4,8},{5,9},{8,12},{9,13},{12,14},{13,15},{14,10},{15,... | collective-permute-start | bytes 3538952 | tf_op jit(solution)/shard_map/ppermute | solution.py:287
  6.6 1.2 fusion
  7.8 10.6 %picked.1 = bf16[2304,768]{1,0:T(8,128)(2,1)} custom-call(s32[16]{0:T(128)} %get-tuple-element.53.owners_ref, s32[1]{0:T(128)S(6)} %mul.9.width_ref.refs_1_, bf16[2304,768]{1,0:T(8,128)(2,1)} %a_ref.1), custom_call_target="tpu_custom_call" | custom-call | bytes 7077888 | tf_op jit(solution)/shard_map/picked/pallas_call | solution.py:61
  18.4 2.1 %fusion.1 = (bf16[288,768]{1,0:T(8,128)(2,1)}, bf16[288,768]{1,0:T(8,128)(2,1)}) fusion(bf16[2304,768]{1,0:T(8,128)(2,1)} %picked.1), kind=kLoop, calls=%fused_computation.11 | loop fusion | bytes 1769472 | tf_op jit(solution)/shard_map/slice | solution.py:299
  20.5 2.1 %copy.29 = bf16[288,768]{0,1:T(8,128)(2,1)} copy(bf16[288,768]{1,0:T(8,128)(2,1)} %get-tuple-element.49) | data formatting | bytes 884736
  22.7 2.8 %copy-done.9 = bf16[768,4096]{1,0:T(8,128)(2,1)S(1)} copy-done((bf16[768,4096]{1,0:T(8,128)(2,1)S(1)}, bf16[768,4096]{1,0:T(8,128)(2,1)}, u32[]{:S(2)}) %copy-start.9) | copy-done | bytes 6291480
  25.4 1.1 copy-done.31
  26.5 9.2 %phase_wa.3 = (f32[768,4096]{1,0:T(8,128)S(1)}, bf16[2304,768]{1,0:T(8,128)(2,1)}, f32[8,128]{1,0:T(8,128)S(1)}) custom-call(s32[2]{0:T(128)S(1)} %get-tuple-element.58.refs_0_, s32[1]{0:T(128)S(6)} %mul.9.width_ref.refs_1_, bf16[768,288]{1,0:T(8,128)(2,1)S(1)} %bitcast.23, bf16[768,4096]{1,0:T(8,128)(2,1)S(1)} %copy-done.9, ...), custom_call_target="tpu_custom_call" | custom-call | flops 452984832 | bytes 2359296 | tf_op jit(solution)/shard_map/phase_wa/pallas_call | solution.py:189
  35.8 4.6 %copy-done = f32[768,4096]{1,0:T(8,128)} copy-done((f32[768,4096]{1,0:T(8,128)}, f32[768,4096]{1,0:T(8,128)S(1)}, u32[]{:S(2)}) %copy-start) | copy-done | bytes 12582936
  40.4 0.6 copy-done.35
  41.0 1.0 copy-done.22
  42.0 0.4 copy-done.24
  42.5 0.4 collective-permute-start.6
  42.9 2.0 %collective-permute-start.3 = (bf16[144,4096]{1,0:T(8,128)(2,1)}, bf16[144,4096]{1,0:T(8,128)(2,1)S(1)}, u32[]{:S(2)}, u32[]{:S(2)}) collective-permute-start(bf16[144,4096]{1,0:T(8,128)(2,1)} %get-tuple-element.26.refs_4_), channel_id=1, source_target_pairs={{0,4},{1,5},{4,8},{5,9},{8,12},{9,13},{12,14},{13,15},{14,10},{15,... | collective-permute-start | bytes 3538952 | tf_op jit(solution)/shard_map/ppermute | solution.py:287
  44.9 3.4 %fusion.2 = (bf16[576,768]{1,0:T(8,128)(2,1)}, bf16[576,768]{1,0:T(8,128)(2,1)}, bf16[576,768]{1,0:T(8,128)(2,1)}) fusion(bf16[2304,768]{1,0:T(8,128)(2,1)} %picked.1), kind=kLoop, calls=%fused_computation.12 | loop fusion | bytes 5308416 | tf_op jit(solution)/shard_map/slice | solution.py:299
  48.3 2.3 %copy.30 = bf16[576,768]{0,1:T(8,128)(2,1)} copy(bf16[576,768]{1,0:T(8,128)(2,1)} %get-tuple-element.52) | data formatting | bytes 1769472
  50.7 4.6 %copy-done.1 = f32[768,4096]{1,0:T(8,128)S(1)} copy-done((f32[768,4096]{1,0:T(8,128)S(1)}, f32[768,4096]{1,0:T(8,128)}, u32[]{:S(2)}) %copy-start.1) | copy-done | bytes 12582936
  55.3 2.8 %copy-done.10 = bf16[768,4096]{1,0:T(8,128)(2,1)S(1)} copy-done((bf16[768,4096]{1,0:T(8,128)(2,1)S(1)}, bf16[768,4096]{1,0:T(8,128)(2,1)}, u32[]{:S(2)}) %copy-start.10) | copy-done | bytes 6291480
  58.1 1.2 copy-done.28
  59.3 13.6 %phase_wa.4 = (f32[768,4096]{1,0:T(8,128)S(1)}, bf16[2304,768]{1,0:T(8,128)(2,1)}, f32[8,128]{1,0:T(8,128)S(1)}) custom-call(s32[4]{0:T(128)S(1)} %get-tuple-element.57.refs_0_, s32[1]{0:T(128)S(6)} %mul.9.width_ref.refs_1_, bf16[768,576]{1,0:T(8,128)(2,1)S(1)} %bitcast.20, ...), custom_call_target="tpu_custom_call", output_to_operand_aliasing={{0}: (8, {}), {1}: (9, {})} | custom-call | flops 905969664 | bytes 4718592 | tf_op jit(solution)/shard_map/phase_wa/pallas_call | solution.py:189
  72.9 4.6 %copy-done.2 = f32[768,4096]{1,0:T(8,128)} copy-done((f32[768,4096]{1,0:T(8,128)}, f32[768,4096]{1,0:T(8,128)S(1)}, u32[]{:S(2)}) %copy-start.2) | copy-done | bytes 12582936
  77.5 0.6 copy-done.33
  78.1 1.0 copy-done.26
  79.1 0.5 collective-permute-start.9
  79.6 2.0 %collective-permute-start.7 = (bf16[144,4096]{1,0:T(8,128)(2,1)}, bf16[144,4096]{1,0:T(8,128)(2,1)S(1)}, u32[]{:S(2)}, u32[]{:S(2)}) collective-permute-start(bf16[144,4096]{1,0:T(8,128)(2,1)} %get-tuple-element.31.refs_4_), channel_id=1, source_target_pairs={{0,4},{1,5},{4,8},{5,9},{8,12},{9,13},{12,14},{13,15},{14,10},{15,... | collective-permute-start | bytes 3538952 | tf_op jit(solution)/shard_map/ppermute | solution.py:287
  81.7 2.2 %copy.31 = bf16[576,768]{0,1:T(8,128)(2,1)} copy(bf16[576,768]{1,0:T(8,128)(2,1)} %get-tuple-element.51) | data formatting | bytes 1769472
  84.0 4.6 %copy-done.3 = f32[768,4096]{1,0:T(8,128)S(1)} copy-done((f32[768,4096]{1,0:T(8,128)S(1)}, f32[768,4096]{1,0:T(8,128)}, u32[]{:S(2)}) %copy-start.3) | copy-done | bytes 12582936
  88.6 2.8 %copy-done.11 = bf16[768,4096]{1,0:T(8,128)(2,1)S(1)} copy-done((bf16[768,4096]{1,0:T(8,128)(2,1)S(1)}, bf16[768,4096]{1,0:T(8,128)(2,1)}, u32[]{:S(2)}) %copy-start.11) | copy-done | bytes 6291480
  91.4 1.2 copy-done.29
  92.6 13.6 %phase_wa.5 = (f32[768,4096]{1,0:T(8,128)S(1)}, bf16[2304,768]{1,0:T(8,128)(2,1)}, f32[8,128]{1,0:T(8,128)S(1)}) custom-call(s32[4]{0:T(128)S(1)} %get-tuple-element.56.refs_0_, s32[1]{0:T(128)S(6)} %mul.9.width_ref.refs_1_, bf16[768,576]{1,0:T(8,128)(2,1)S(1)} %bitcast.21, ...), custom_call_target="tpu_custom_call", output_to_operand_aliasing={{0}: (8, {}), {1}: (9, {})} | custom-call | flops 905969664 | bytes 4718592 | tf_op jit(solution)/shard_map/phase_wa/pallas_call | solution.py:189
  106.2 4.6 %copy-done.4 = f32[768,4096]{1,0:T(8,128)} copy-done((f32[768,4096]{1,0:T(8,128)}, f32[768,4096]{1,0:T(8,128)S(1)}, u32[]{:S(2)}) %copy-start.4) | copy-done | bytes 12582936
  110.7 0.6 copy-done.34
  111.3 1.0 copy-done.13
  112.3 0.4 copy-done.15
  112.9 0.4 collective-permute-start.14
  113.3 1.9 slice.62
  115.2 0.9 slice.63
  116.0 2.0 %collective-permute-start.11 = (bf16[144,2048]{1,0:T(8,128)(2,1)}, bf16[144,2048]{1,0:T(8,128)(2,1)S(1)}, u32[]{:S(2)}, u32[]{:S(2)}) collective-permute-start(bf16[144,2048]{1,0:T(8,128)(2,1)} %slice.62), channel_id=1, source_target_pairs={{0,4},{1,5},{4,8},{5,9},{8,12},{9,13},{12,14},{13,15},{14,10},{15,... | collective-permute-start | bytes 1769480 | tf_op jit(solution)/shard_map/ppermute | solution.py:287
  118.1 2.2 %copy.32 = bf16[576,768]{0,1:T(8,128)(2,1)} copy(bf16[576,768]{1,0:T(8,128)(2,1)} %get-tuple-element.50) | data formatting | bytes 1769472
  120.3 4.6 %copy-done.5 = f32[768,4096]{1,0:T(8,128)S(1)} copy-done((f32[768,4096]{1,0:T(8,128)S(1)}, f32[768,4096]{1,0:T(8,128)}, u32[]{:S(2)}) %copy-start.5) | copy-done | bytes 12582936
  124.9 1.2 copy-done.30
  126.1 8.7 %phase_w.2 = (f32[768,4096]{1,0:T(8,128)S(1)}, f32[8,128]{1,0:T(8,128)S(1)}) custom-call(s32[4]{0:T(128)S(1)} %get-tuple-element.55.refs_0_, s32[1]{0:T(128)S(6)} %mul.9.width_ref.refs_1_, bf16[768,576]{1,0:T(8,128)(2,1)S(1)} %bitcast.22, bf16[144,4096]{1,0:T(8,128)(2,1)S(1)} %copy-done.14, ...), custom_call_target="tpu_custom_call", output_to_operand_aliasing={{0}: (7, {})} | custom-call | flops 452984832 | bytes 4718592 | tf_op jit(solution)/shard_map/phase_w/pallas_call | solution.py:189
  134.8 4.6 %copy-done.6 = f32[768,4096]{1,0:T(8,128)} copy-done((f32[768,4096]{1,0:T(8,128)}, f32[768,4096]{1,0:T(8,128)S(1)}, u32[]{:S(2)}) %copy-start.6) | copy-done | bytes 12582936
  139.4 0.6 copy-done.36
  140.0 0.8 copy-done.17
  141.0 0.5 collective-permute-start.16
  141.5 2.1 %copy.33 = bf16[288,768]{0,1:T(8,128)(2,1)} copy(bf16[288,768]{1,0:T(8,128)(2,1)} %get-tuple-element.48) | data formatting | bytes 884736
  143.7 0.5 collective-permute-done.16.refs_6_
  144.2 4.6 %copy-done.7 = f32[768,4096]{1,0:T(8,128)S(1)} copy-done((f32[768,4096]{1,0:T(8,128)S(1)}, f32[768,4096]{1,0:T(8,128)}, u32[]{:S(2)}) %copy-start.7) | copy-done | bytes 12582936
  148.8 1.1 copy-done.20
  149.8 1.1 copy-done.32
  150.9 6.8 %phase_w.3 = (f32[768,4096]{1,0:T(8,128)S(1)}, f32[8,128]{1,0:T(8,128)S(1)}) custom-call(s32[2]{0:T(128)S(1)} %get-tuple-element.59.refs_0_, s32[1]{0:T(128)S(6)} %mul.9.width_ref.refs_1_, bf16[768,288]{1,0:T(8,128)(2,1)S(1)} %bitcast.24, bf16[144,2048]{1,0:T(8,128)(2,1)S(1)} %copy-done.18, ...), custom_call_target="tpu_custom_call", output_to_operand_aliasing={{0}: (7, {})} | custom-call | flops 226492416 | bytes 2359296 | tf_op jit(solution)/shard_map/phase_w/pallas_call | solution.py:189
  157.7 4.6 %copy-done.8 = f32[768,4096]{1,0:T(8,128)} copy-done((f32[768,4096]{1,0:T(8,128)}, f32[768,4096]{1,0:T(8,128)S(1)}, u32[]{:S(2)}) %copy-start.8) | copy-done | bytes 12582936
  162.4 1.9 collective-permute-start.18
  164.3 1.3 collective-permute-start.19
  165.7 2.8 %copy-done.12 = bf16[768,4096]{1,0:T(8,128)(2,1)S(1)} copy-done((bf16[768,4096]{1,0:T(8,128)(2,1)S(1)}, bf16[768,4096]{1,0:T(8,128)(2,1)}, u32[]{:S(2)}) %copy-start.12) | copy-done | bytes 6291480
  168.5 10.4 %phase_a.2 = (bf16[2304,768]{1,0:T(8,128)(2,1)}, f32[8,128]{1,0:T(8,128)}) custom-call(s32[4]{0:T(128)S(1)} %get-tuple-element.55.refs_0_, s32[1]{0:T(128)S(6)} %mul.9.width_ref.refs_1_, bf16[768,4096]{1,0:T(8,128)(2,1)S(1)} %copy-done.12, bf16[144,4096]{1,0:T(8,128)(2,1)S(1)} %copy-done.14, ...), custom_call_target="tpu_custom_call", output_to_operand_aliasing={{0}: (7, {})} | custom-call | flops 452984832 | bytes 4718592 | tf_op jit(solution)/shard_map/phase_a/pallas_call | solution.py:189
  178.9 1.6 collective-permute-start.20
  180.6 2.6 %collective-permute-start.21 = (f32[8,128]{1,0:T(8,128)S(1)}, f32[8,128]{1,0:T(8,128)S(1)}, u32[]{:S(2)}, u32[]{:S(2)}) collective-permute-start(f32[8,128]{1,0:T(8,128)S(1)} %add_add_fusion.1), channel_id=1, source_target_pairs={{0,8},{1,9},{2,10},{3,11},{4,12},{5,13},{6,14},{7,15},{8,0},{9,1},... | collective-permute-start | bytes 12296 | tf_op jit(solution)/shard_map/ppermute | solution.py:266
  183.1 1.3 collective-permute-start.22
  184.5 7.2 %phase_a.3 = (bf16[2304,768]{1,0:T(8,128)(2,1)}, f32[8,128]{1,0:T(8,128)}) custom-call(s32[2]{0:T(128)S(1)} %get-tuple-element.59.refs_0_, s32[1]{0:T(128)S(6)} %mul.9.width_ref.refs_1_, bf16[768,4096]{1,0:T(8,128)(2,1)S(1)} %copy-done.12, bf16[144,2048]{1,0:T(8,128)(2,1)S(1)} %copy-done.18, ...), custom_call_target="tpu_custom_call", output_to_operand_aliasing={{0}: (7, {})} | custom-call | flops 226492416 | bytes 2359296 | tf_op jit(solution)/shard_map/phase_a/pallas_call | solution.py:189
  191.8 5.4 %scale.1 = bf16[768,4096]{1,0:T(8,128)(2,1)} custom-call(f32[768,4096]{1,0:T(8,128)S(1)} %bitcast.19, f32[8,128]{1,0:T(8,128)S(1)} %add_add_fusion.squares_ref), custom_call_target="tpu_custom_call" | custom-call | flops 3145728 | bytes 6291456 | tf_op jit(solution)/shard_map/scale/pallas_call | solution.py:232
  (92 shorter events, 1.2 us)
Async XLA Ops:
  2.7 19.9 %collective-permute-start.2 = (bf16[144,4096]{1,0:T(8,128)(2,1)S(1)}, bf16[144,4096]{1,0:T(8,128)(2,1)}, u32[]{:S(2)}, u32[]{:S(2)}) collective-permute-start(bf16[144,4096]{1,0:T(8,128)(2,1)S(1)} %broadcast_select_fusion.refs_4_), channel_id=1, source_target_pairs={{0,1},{1,0},{2,3},{3,2},{4,5},{5,4},{6,7},{7,6},{8,9},{9,8},{10,11... | collective-permute-start | bytes 3538952 | tf_op jit(solution)/shard_map/ppermute | solution.py:284
  3.2 37.7 %collective-permute-start = (bf16[144,4096]{1,0:T(8,128)(2,1)S(1)}, bf16[144,4096]{1,0:T(8,128)(2,1)S(1)}, u32[]{:S(2)}, u32[]{:S(2)}) collective-permute-start(bf16[144,4096]{1,0:T(8,128)(2,1)S(1)} %broadcast_select_fusion.refs_4_), channel_id=1, source_target_pairs={{0,4},{1,5},{4,8},{5,9},{8,12},{9,13},{12,14},{13,15},{14,10},{15,... | collective-permute-start | bytes 3538952 | tf_op jit(solution)/shard_map/ppermute | solution.py:287
  5.9 35.1 %collective-permute-start.1 = (bf16[144,4096]{1,0:T(8,128)(2,1)S(1)}, bf16[144,4096]{1,0:T(8,128)(2,1)S(1)}, u32[]{:S(2)}, u32[]{:S(2)}) collective-permute-start(bf16[144,4096]{1,0:T(8,128)(2,1)S(1)} %broadcast_select_fusion.refs_4_), channel_id=1, source_target_pairs={{0,2},{1,3},{4,0},{5,1},{8,4},{9,5},{12,8},{13,9},{14,12},{15,13},... | collective-permute-start | bytes 3538952 | tf_op jit(solution)/shard_map/ppermute | solution.py:290
  22.6 2.8 %copy-start.9 = (bf16[768,4096]{1,0:T(8,128)(2,1)S(1)}, bf16[768,4096]{1,0:T(8,128)(2,1)}, u32[]{:S(2)}) copy-start(bf16[768,4096]{1,0:T(8,128)(2,1)} %refs_2_.3) | copy-start | bytes 18874372
  25.4 1.1 copy-start.31
  35.8 4.6 %copy-start = (f32[768,4096]{1,0:T(8,128)}, f32[768,4096]{1,0:T(8,128)S(1)}, u32[]{:S(2)}) copy-start(f32[768,4096]{1,0:T(8,128)S(1)} %get-tuple-element.28.refs_8_) | copy-start | bytes 37748740
  40.3 0.6 copy-start.35
  40.9 1.0 copy-start.22
  41.0 1.4 copy-start.24
  42.4 8.3 %collective-permute-start.5 = (bf16[144,4096]{1,0:T(8,128)(2,1)}, bf16[144,4096]{1,0:T(8,128)(2,1)}, u32[]{:S(2)}, u32[]{:S(2)}) collective-permute-start(bf16[144,4096]{1,0:T(8,128)(2,1)} %get-tuple-element.26.refs_4_), channel_id=1, source_target_pairs={{0,1},{1,0},{2,3},{3,2},{4,5},{5,4},{6,7},{7,6},{8,9},{9,8},{10,11... | collective-permute-start | bytes 3538952 | tf_op jit(solution)/shard_map/ppermute | solution.py:284
  42.5 8.2 %collective-permute-start.6 = (bf16[144,4096]{1,0:T(8,128)(2,1)}, bf16[144,4096]{1,0:T(8,128)(2,1)}, u32[]{:S(2)}, u32[]{:S(2)}) collective-permute-start(bf16[144,4096]{1,0:T(8,128)(2,1)} %get-tuple-element.27.refs_6_), channel_id=1, source_target_pairs={{0,1},{1,0},{2,3},{3,2},{4,5},{5,4},{6,7},{7,6},{8,9},{9,8},{10,11... | collective-permute-start | bytes 3538952 | tf_op jit(solution)/shard_map/ppermute | solution.py:284
  42.9 35.2 %collective-permute-start.3 = (bf16[144,4096]{1,0:T(8,128)(2,1)}, bf16[144,4096]{1,0:T(8,128)(2,1)S(1)}, u32[]{:S(2)}, u32[]{:S(2)}) collective-permute-start(bf16[144,4096]{1,0:T(8,128)(2,1)} %get-tuple-element.26.refs_4_), channel_id=1, source_target_pairs={{0,4},{1,5},{4,8},{5,9},{8,12},{9,13},{12,14},{13,15},{14,10},{15,... | collective-permute-start | bytes 3538952 | tf_op jit(solution)/shard_map/ppermute | solution.py:287
  44.9 33.2 %collective-permute-start.4 = (bf16[144,4096]{1,0:T(8,128)(2,1)}, bf16[144,4096]{1,0:T(8,128)(2,1)}, u32[]{:S(2)}, u32[]{:S(2)}) collective-permute-start(bf16[144,4096]{1,0:T(8,128)(2,1)} %get-tuple-element.27.refs_6_), channel_id=1, source_target_pairs={{0,2},{1,3},{4,0},{5,1},{8,4},{9,5},{12,8},{13,9},{14,12},{15,13},... | collective-permute-start | bytes 3538952 | tf_op jit(solution)/shard_map/ppermute | solution.py:290
  44.9 5.8 %copy-start.25 = (bf16[144,4096]{1,0:T(8,128)(2,1)S(1)}, bf16[144,4096]{1,0:T(8,128)(2,1)}, u32[]{:S(2)}) copy-start(bf16[144,4096]{1,0:T(8,128)(2,1)} %get-tuple-element.27.refs_6_) | copy-start | bytes 3538948
  48.3 2.4 %copy-start.23 = (bf16[144,4096]{1,0:T(8,128)(2,1)S(1)}, bf16[144,4096]{1,0:T(8,128)(2,1)}, u32[]{:S(2)}) copy-start(bf16[144,4096]{1,0:T(8,128)(2,1)} %get-tuple-element.26.refs_4_) | copy-start | bytes 3538948
  50.7 4.6 %copy-start.1 = (f32[768,4096]{1,0:T(8,128)S(1)}, f32[768,4096]{1,0:T(8,128)}, u32[]{:S(2)}) copy-start(f32[768,4096]{1,0:T(8,128)} %copy-done) | copy-start | bytes 37748740
  55.3 2.8 %copy-start.10 = (bf16[768,4096]{1,0:T(8,128)(2,1)S(1)}, bf16[768,4096]{1,0:T(8,128)(2,1)}, u32[]{:S(2)}) copy-start(bf16[768,4096]{1,0:T(8,128)(2,1)} %refs_2_.3) | copy-start | bytes 18874372
  58.1 1.2 copy-start.28
  72.9 4.6 %copy-start.2 = (f32[768,4096]{1,0:T(8,128)}, f32[768,4096]{1,0:T(8,128)S(1)}, u32[]{:S(2)}) copy-start(f32[768,4096]{1,0:T(8,128)S(1)} %get-tuple-element.33.refs_8_) | copy-start | bytes 37748740
  77.5 0.6 copy-start.33
  78.1 1.0 copy-start.26
  79.1 4.9 %copy-start.27 = (bf16[144,4096]{1,0:T(8,128)(2,1)S(1)}, bf16[144,4096]{1,0:T(8,128)(2,1)}, u32[]{:S(2)}) copy-start(bf16[144,4096]{1,0:T(8,128)(2,1)} %get-tuple-element.31.refs_4_) | copy-start | bytes 3538948
  79.1 4.8 %collective-permute-start.10 = (bf16[144,4096]{1,0:T(8,128)(2,1)}, bf16[144,4096]{1,0:T(8,128)(2,1)}, u32[]{:S(2)}, u32[]{:S(2)}) collective-permute-start(bf16[144,4096]{1,0:T(8,128)(2,1)} %get-tuple-element.32.refs_6_), channel_id=1, source_target_pairs={{0,1},{1,0},{2,3},{3,2},{4,5},{5,4},{6,7},{7,6},{8,9},{9,8},{10,11... | collective-permute-start | bytes 3538952 | tf_op jit(solution)/shard_map/ppermute | solution.py:284
  79.1 4.9 %collective-permute-start.9 = (bf16[144,4096]{1,0:T(8,128)(2,1)}, bf16[144,4096]{1,0:T(8,128)(2,1)}, u32[]{:S(2)}, u32[]{:S(2)}) collective-permute-start(bf16[144,4096]{1,0:T(8,128)(2,1)} %get-tuple-element.31.refs_4_), channel_id=1, source_target_pairs={{0,1},{1,0},{2,3},{3,2},{4,5},{5,4},{6,7},{7,6},{8,9},{9,8},{10,11... | collective-permute-start | bytes 3538952 | tf_op jit(solution)/shard_map/ppermute | solution.py:284
  79.6 31.7 %collective-permute-start.7 = (bf16[144,4096]{1,0:T(8,128)(2,1)}, bf16[144,4096]{1,0:T(8,128)(2,1)S(1)}, u32[]{:S(2)}, u32[]{:S(2)}) collective-permute-start(bf16[144,4096]{1,0:T(8,128)(2,1)} %get-tuple-element.31.refs_4_), channel_id=1, source_target_pairs={{0,4},{1,5},{4,8},{5,9},{8,12},{9,13},{12,14},{13,15},{14,10},{15,... | collective-permute-start | bytes 3538952 | tf_op jit(solution)/shard_map/ppermute | solution.py:287
  81.6 29.7 %collective-permute-start.8 = (bf16[144,4096]{1,0:T(8,128)(2,1)}, bf16[144,4096]{1,0:T(8,128)(2,1)S(1)}, u32[]{:S(2)}, u32[]{:S(2)}) collective-permute-start(bf16[144,4096]{1,0:T(8,128)(2,1)} %get-tuple-element.32.refs_6_), channel_id=1, source_target_pairs={{0,2},{1,3},{4,0},{5,1},{8,4},{9,5},{12,8},{13,9},{14,12},{15,13},... | collective-permute-start | bytes 3538952 | tf_op jit(solution)/shard_map/ppermute | solution.py:290
  84.0 4.6 %copy-start.3 = (f32[768,4096]{1,0:T(8,128)S(1)}, f32[768,4096]{1,0:T(8,128)}, u32[]{:S(2)}) copy-start(f32[768,4096]{1,0:T(8,128)} %copy-done.2) | copy-start | bytes 37748740
  88.6 2.8 %copy-start.11 = (bf16[768,4096]{1,0:T(8,128)(2,1)S(1)}, bf16[768,4096]{1,0:T(8,128)(2,1)}, u32[]{:S(2)}) copy-start(bf16[768,4096]{1,0:T(8,128)(2,1)} %refs_2_.3) | copy-start | bytes 18874372
  91.4 1.2 copy-start.29
  106.1 4.6 %copy-start.4 = (f32[768,4096]{1,0:T(8,128)}, f32[768,4096]{1,0:T(8,128)S(1)}, u32[]{:S(2)}) copy-start(f32[768,4096]{1,0:T(8,128)S(1)} %get-tuple-element.38.refs_7_) | copy-start | bytes 37748740
  110.7 0.6 copy-start.34
  111.3 1.0 copy-start.13
  111.3 1.4 copy-start.15
  112.7 2.4 %copy-start.16 = (bf16[144,4096]{1,0:T(8,128)(2,1)S(1)}, bf16[144,4096]{1,0:T(8,128)(2,1)}, u32[]{:S(2)}) copy-start(bf16[144,4096]{1,0:T(8,128)(2,1)} %get-tuple-element.37.refs_5_) | copy-start | bytes 3538948
  112.7 7.6 %collective-permute-start.13 = (bf16[144,4096]{1,0:T(8,128)(2,1)}, bf16[144,4096]{1,0:T(8,128)(2,1)}, u32[]{:S(2)}, u32[]{:S(2)}) collective-permute-start(bf16[144,4096]{1,0:T(8,128)(2,1)} %get-tuple-element.36.refs_3_), channel_id=1, source_target_pairs={{0,1},{1,0},{2,3},{3,2},{4,5},{5,4},{6,7},{7,6},{8,9},{9,8},{10,11... | collective-permute-start | bytes 3538952 | tf_op jit(solution)/shard_map/ppermute | solution.py:284
  112.9 7.4 %collective-permute-start.14 = (bf16[144,4096]{1,0:T(8,128)(2,1)}, bf16[144,4096]{1,0:T(8,128)(2,1)}, u32[]{:S(2)}, u32[]{:S(2)}) collective-permute-start(bf16[144,4096]{1,0:T(8,128)(2,1)} %get-tuple-element.37.refs_5_), channel_id=1, source_target_pairs={{0,1},{1,0},{2,3},{3,2},{4,5},{5,4},{6,7},{7,6},{8,9},{9,8},{10,11... | collective-permute-start | bytes 3538952 | tf_op jit(solution)/shard_map/ppermute | solution.py:284
  116.0 4.3 %copy-start.14 = (bf16[144,4096]{1,0:T(8,128)(2,1)S(1)}, bf16[144,4096]{1,0:T(8,128)(2,1)}, u32[]{:S(2)}) copy-start(bf16[144,4096]{1,0:T(8,128)(2,1)} %get-tuple-element.36.refs_3_) | copy-start | bytes 3538948
  116.0 23.9 %collective-permute-start.11 = (bf16[144,2048]{1,0:T(8,128)(2,1)}, bf16[144,2048]{1,0:T(8,128)(2,1)S(1)}, u32[]{:S(2)}, u32[]{:S(2)}) collective-permute-start(bf16[144,2048]{1,0:T(8,128)(2,1)} %slice.62), channel_id=1, source_target_pairs={{0,4},{1,5},{4,8},{5,9},{8,12},{9,13},{12,14},{13,15},{14,10},{15,... | collective-permute-start | bytes 1769480 | tf_op jit(solution)/shard_map/ppermute | solution.py:287
  118.0 21.9 %collective-permute-start.12 = (bf16[144,2048]{1,0:T(8,128)(2,1)}, bf16[144,2048]{1,0:T(8,128)(2,1)S(1)}, u32[]{:S(2)}, u32[]{:S(2)}) collective-permute-start(bf16[144,2048]{1,0:T(8,128)(2,1)} %slice.63), channel_id=1, source_target_pairs={{0,2},{1,3},{4,0},{5,1},{8,4},{9,5},{12,8},{13,9},{14,12},{15,13},... | collective-permute-start | bytes 1769480 | tf_op jit(solution)/shard_map/ppermute | solution.py:290
  120.3 4.6 %copy-start.5 = (f32[768,4096]{1,0:T(8,128)S(1)}, f32[768,4096]{1,0:T(8,128)}, u32[]{:S(2)}) copy-start(f32[768,4096]{1,0:T(8,128)} %copy-done.4) | copy-start | bytes 37748740
  124.9 1.2 copy-start.30
  134.8 4.6 %copy-start.6 = (f32[768,4096]{1,0:T(8,128)}, f32[768,4096]{1,0:T(8,128)S(1)}, u32[]{:S(2)}) copy-start(f32[768,4096]{1,0:T(8,128)S(1)} %get-tuple-element.45.refs_7_) | copy-start | bytes 37748740
  139.4 0.6 copy-start.36
  140.0 0.8 copy-start.17
  140.0 1.0 copy-start.19
  141.0 3.2 %copy-start.18 = (bf16[144,2048]{1,0:T(8,128)(2,1)S(1)}, bf16[144,2048]{1,0:T(8,128)(2,1)}, u32[]{:S(2)}) copy-start(bf16[144,2048]{1,0:T(8,128)(2,1)} %get-tuple-element.40.refs_3_) | copy-start | bytes 1769476
  141.0 2.7 %collective-permute-start.15 = (bf16[144,2048]{1,0:T(8,128)(2,1)}, bf16[144,2048]{1,0:T(8,128)(2,1)S(1)}, u32[]{:S(2)}, u32[]{:S(2)}) collective-permute-start(bf16[144,2048]{1,0:T(8,128)(2,1)} %get-tuple-element.40.refs_3_), channel_id=1, source_target_pairs={{0,1},{1,0},{2,3},{3,2},{4,5},{5,4},{6,7},{7,6},{8,9},{9,8},{10,11... | collective-permute-start | bytes 1769480 | tf_op jit(solution)/shard_map/ppermute | solution.py:284
  141.0 3.2 %collective-permute-start.16 = (bf16[144,2048]{1,0:T(8,128)(2,1)}, bf16[144,2048]{1,0:T(8,128)(2,1)}, u32[]{:S(2)}, u32[]{:S(2)}) collective-permute-start(bf16[144,2048]{1,0:T(8,128)(2,1)} %get-tuple-element.41.refs_5_), channel_id=1, source_target_pairs={{0,1},{1,0},{2,3},{3,2},{4,5},{5,4},{6,7},{7,6},{8,9},{9,8},{10,11... | collective-permute-start | bytes 1769480 | tf_op jit(solution)/shard_map/ppermute | solution.py:284
  144.2 4.6 %copy-start.7 = (f32[768,4096]{1,0:T(8,128)S(1)}, f32[768,4096]{1,0:T(8,128)}, u32[]{:S(2)}) copy-start(f32[768,4096]{1,0:T(8,128)} %copy-done.6) | copy-start | bytes 37748740
  148.8 1.1 copy-start.20
  149.8 1.1 copy-start.32
  157.7 4.6 %copy-start.8 = (f32[768,4096]{1,0:T(8,128)}, f32[768,4096]{1,0:T(8,128)S(1)}, u32[]{:S(2)}) copy-start(f32[768,4096]{1,0:T(8,128)S(1)} %get-tuple-element.46.w_ref) | copy-start | bytes 37748740
  162.3 16.6 %collective-permute-start.17 = (f32[8,128]{1,0:T(8,128)S(1)}, f32[8,128]{1,0:T(8,128)S(1)}, u32[]{:S(2)}, u32[]{:S(2)}) collective-permute-start(f32[8,128]{1,0:T(8,128)S(1)} %get-tuple-element.47), channel_id=1, source_target_pairs={{0,1},{1,2},{2,3},{3,0},{4,5},{5,6},{6,7},{7,4},{8,9},{9,10},{10,1... | collective-permute-start | bytes 12296 | tf_op jit(solution)/shard_map/ppermute | solution.py:266
  162.4 16.5 %collective-permute-start.18 = (f32[8,128]{1,0:T(8,128)S(1)}, f32[8,128]{1,0:T(8,128)S(1)}, u32[]{:S(2)}, u32[]{:S(2)}) collective-permute-start(f32[8,128]{1,0:T(8,128)S(1)} %get-tuple-element.47), channel_id=1, source_target_pairs={{0,2},{1,3},{2,0},{3,1},{4,6},{5,7},{6,4},{7,5},{8,10},{9,11},{10,... | collective-permute-start | bytes 12296 | tf_op jit(solution)/shard_map/ppermute | solution.py:266
  164.3 14.6 %collective-permute-start.19 = (f32[8,128]{1,0:T(8,128)S(1)}, f32[8,128]{1,0:T(8,128)S(1)}, u32[]{:S(2)}, u32[]{:S(2)}) collective-permute-start(f32[8,128]{1,0:T(8,128)S(1)} %get-tuple-element.47), channel_id=1, source_target_pairs={{0,3},{1,0},{2,1},{3,2},{4,7},{5,4},{6,5},{7,6},{8,11},{9,8},{10,9... | collective-permute-start | bytes 12296 | tf_op jit(solution)/shard_map/ppermute | solution.py:266
  165.7 2.8 %copy-start.12 = (bf16[768,4096]{1,0:T(8,128)(2,1)S(1)}, bf16[768,4096]{1,0:T(8,128)(2,1)}, u32[]{:S(2)}) copy-start(bf16[768,4096]{1,0:T(8,128)(2,1)} %refs_2_.3) | copy-start | bytes 18874372
  168.5 16.0 %copy-start.21 = (bf16[144,2048]{1,0:T(8,128)(2,1)S(1)}, bf16[144,2048]{1,0:T(8,128)(2,1)}, u32[]{:S(2)}) copy-start(bf16[144,2048]{1,0:T(8,128)(2,1)} %get-tuple-element.41.refs_5_) | copy-start | bytes 1769476
  168.5 23.3 %slice-start = ((s8[12582912]{0:T(1024)(128)(4,1)}), s8[4194304]{0:T(1024)(128)(4,1)S(1)}, s32[]{:S(2)}) async-start(s8[12582912]{0:T(1024)(128)(4,1)} %bitcast.18), calls=%async_computation | async-start | bytes 8388608
  168.5 23.3 %slice-start.1 = ((s8[12582912]{0:T(1024)(128)(4,1)}), s8[4194304]{0:T(1024)(128)(4,1)S(1)}, s32[]{:S(2)}) async-start(s8[12582912]{0:T(1024)(128)(4,1)} %bitcast.18), calls=%async_computation.1 | async-start | bytes 8388608
  178.9 12.8 %collective-permute-start.20 = (f32[8,128]{1,0:T(8,128)S(1)}, f32[8,128]{1,0:T(8,128)S(1)}, u32[]{:S(2)}, u32[]{:S(2)}) collective-permute-start(f32[8,128]{1,0:T(8,128)S(1)} %add_add_fusion.1), channel_id=1, source_target_pairs={{0,4},{1,5},{2,6},{3,7},{4,8},{5,9},{6,10},{7,11},{8,12},{9,13},{1... | collective-permute-start | bytes 12296 | tf_op jit(solution)/shard_map/ppermute | solution.py:266
  180.6 11.2 %collective-permute-start.21 = (f32[8,128]{1,0:T(8,128)S(1)}, f32[8,128]{1,0:T(8,128)S(1)}, u32[]{:S(2)}, u32[]{:S(2)}) collective-permute-start(f32[8,128]{1,0:T(8,128)S(1)} %add_add_fusion.1), channel_id=1, source_target_pairs={{0,8},{1,9},{2,10},{3,11},{4,12},{5,13},{6,14},{7,15},{8,0},{9,1},... | collective-permute-start | bytes 12296 | tf_op jit(solution)/shard_map/ppermute | solution.py:266
  183.1 8.6 %collective-permute-start.22 = (f32[8,128]{1,0:T(8,128)S(1)}, f32[8,128]{1,0:T(8,128)S(1)}, u32[]{:S(2)}, u32[]{:S(2)}) collective-permute-start(f32[8,128]{1,0:T(8,128)S(1)} %add_add_fusion.1), channel_id=1, source_target_pairs={{0,12},{1,13},{2,14},{3,15},{4,0},{5,1},{6,2},{7,3},{8,4},{9,5},{1... | collective-permute-start | bytes 12296 | tf_op jit(solution)/shard_map/ppermute | solution.py:266
  184.5 7.3 %slice-start.2 = ((s8[12582912]{0:T(1024)(128)(4,1)}), s8[4194304]{0:T(1024)(128)(4,1)S(1)}, s32[]{:S(2)}) async-start(s8[12582912]{0:T(1024)(128)(4,1)} %bitcast.18), calls=%async_computation.2 | async-start | bytes 8388608

commit v4 on v3

v4 whole, which is shorter than its diff:
```python
import functools

import jax
import jax.numpy as jnp
import numpy as np
from jax import lax
from jax.experimental import pallas as pl
from jax.experimental.pallas import tpu as pltpu
from jax.sharding import PartitionSpec as P

HEADS = 64
HEAD_DIM = 128
SEQ = 16
TILE = 512
MIB = 1024 * 1024


class Ring:
    def __init__(self, devices, columns):
        self.devices = devices
        self.length = devices // 2
        rows = self.length // columns
        if columns == 1:
            self.chips = list(range(rows))
        else:
            self.chips = [2 * z for z in range(rows)]
            self.chips += [2 * z + 1 for z in reversed(range(rows))]
        self.position = {chip: p for p, chip in enumerate(self.chips)}

    def device(self, position, core):
        return 2 * self.chips[position % self.length] + core

    def shift(self, step):
        return [
            (self.device(p, core), self.device(p + step, core))
            for p in range(self.length)
            for core in range(2)
        ]

    def swap(self):
        return [(d, d ^ 1) for d in range(self.devices)]

    def owners(self, offsets):
        table = []
        for d in range(self.devices):
            p, core = self.position[d // 2], d % 2
            row = []
            for offset in offsets:
                row += [self.device(p + offset, core), self.device(p + offset, 1 - core)]
            table.append(row)
        return np.array(table, np.int32)


def live_kernel(seqs_ref, me_ref, grad_ref, out_ref, sem):
    copy = pltpu.make_async_copy(grad_ref, out_ref, sem)
    copy.start()
    copy.wait()
    for s in range(out_ref.shape[0] // SEQ):

        @pl.when(s >= seqs_ref[0])
        def _():
            dead = out_ref.at[s * SEQ : (s + 1) * SEQ]
            dead[...] = jnp.zeros_like(dead)


def live_rows(seq_counts, me, out_grad):
    smem = pl.BlockSpec(memory_space=pltpu.SMEM)
    return pl.pallas_call(
        live_kernel,
        in_specs=[smem, smem, pl.BlockSpec(memory_space=pl.ANY)],
        out_specs=pl.BlockSpec(memory_space=pltpu.VMEM),
        out_shape=pltpu.VMEM(out_grad.shape, out_grad.dtype),
        scratch_shapes=[pltpu.SemaphoreType.DMA],
        compiler_params=pltpu.CompilerParams(vmem_limit_bytes=4 * MIB),
        name="live",
    )(seq_counts, me, pltpu.with_memory_space_constraint(out_grad, pltpu.HBM))


def prep_kernel(counts, rows, table_ref, me_ref, heads_ref, a_ref, *refs):
    at_refs, (block_ref, sems) = refs[: len(counts)], refs[len(counts) :]
    width = heads_ref[0] * HEAD_DIM
    copies = []
    for i in range(sum(counts)):
        owner = table_ref[me_ref[0], i]
        copies.append(
            pltpu.make_async_copy(
                a_ref.at[pl.ds(pl.multiple_of(owner * rows, rows), rows)],
                block_ref.at[pl.ds(i * rows, rows)],
                sems.at[i],
            )
        )
        copies[-1].start()
    begin = 0
    for at_ref, count in zip(at_refs, counts):
        for copy in copies[begin : begin + count]:
            copy.wait()
        block = block_ref[begin * rows : (begin + count) * rows, :]
        column = lax.broadcasted_iota(jnp.int32, block.shape, 1)
        at_ref[...] = jnp.where(column < width, block, jnp.zeros_like(block)).T
        begin += count


def prepared(table, me, head_counts, attn_out, counts, rows):
    slots, capacity = attn_out.shape
    vmem = pl.BlockSpec(memory_space=pltpu.VMEM)
    smem = pl.BlockSpec(memory_space=pltpu.SMEM)
    return pl.pallas_call(
        functools.partial(prep_kernel, counts, rows),
        in_specs=[smem, smem, smem, pl.BlockSpec(memory_space=pl.ANY)],
        out_specs=[vmem] * len(counts),
        out_shape=[pltpu.VMEM((capacity, count * rows), jnp.bfloat16) for count in counts],
        scratch_shapes=[
            pltpu.VMEM((slots, capacity), jnp.bfloat16),
            pltpu.SemaphoreType.DMA((sum(counts),)),
        ],
        compiler_params=pltpu.CompilerParams(vmem_limit_bytes=12 * MIB),
        cost_estimate=pl.CostEstimate(
            flops=0, bytes_accessed=4 * slots * capacity, transcendentals=0
        ),
        name="prep",
    )(table, me, head_counts, pltpu.with_memory_space_constraint(attn_out, pltpu.HBM))


def phase_kernel(spec, *refs):
    do_weight, do_attn, fresh, squares, pieces, halves, rows, begin = spec
    refs = list(refs)
    table_ref, me_ref, heads_ref = refs.pop(0), refs.pop(0), refs.pop(0)
    at_ref = refs.pop(0) if do_weight else None
    weight_ref = refs.pop(0) if do_attn else None
    g_refs = [[refs.pop(0) for _ in range(pieces)] for _ in range(halves)]
    if do_weight and not fresh:
        refs.pop(0)
    if do_attn and not fresh:
        refs.pop(0)
    w_ref = refs.pop(0) if do_weight else None
    out_ref = refs.pop(0) if do_attn else None
    squares_ref = refs.pop(0)
    if do_attn:
        total_ref, block_ref, sems = refs
        total_ref[...] = jnp.zeros_like(total_ref)
    squares_ref[...] = jnp.zeros_like(squares_ref)
    span = g_refs[0][0].shape[1]

    def body(half, j, carry):
        here = pl.ds(pl.multiple_of(j * TILE, TILE), TILE)
        there = pl.ds(pl.multiple_of(half * span + j * TILE, TILE), TILE)
        g = jnp.concatenate([t[:, here] for t in g_refs[half]], axis=0)
        if do_weight:
            w = jnp.dot(at_ref[...], g, preferred_element_type=jnp.float32)
            if not fresh:
                w = w + w_ref[:, there]
            w_ref[:, there] = w
        if squares:
            folded = jnp.sum((w * w).reshape(w.shape[0] // 8, 8, TILE), axis=0)
            total = squares_ref[...]
            for lane in range(0, TILE, 128):
                total = total + folded[:, lane : lane + 128]
            squares_ref[...] = total
        if do_attn:
            total_ref[...] += lax.dot_general(
                g,
                weight_ref[:, there],
                (((1,), (1,)), ((), ())),
                preferred_element_type=jnp.float32,
            )
        return carry

    for half in range(halves):
        lax.fori_loop(0, span // TILE, functools.partial(body, half), 0)
    if do_attn:
        total = total_ref[...]
        column = lax.broadcasted_iota(jnp.int32, total.shape, 1)
        block_ref[...] = jnp.where(column < heads_ref[0] * HEAD_DIM, total, 0.0).astype(jnp.bfloat16)
        copies = []
        for i in range(pieces):
            owner = table_ref[me_ref[0], begin + i]
            copies.append(
                pltpu.make_async_copy(
                    block_ref.at[pl.ds(i * rows, rows)],
                    out_ref.at[pl.ds(pl.multiple_of(owner * rows, rows), rows)],
                    sems.at[i],
                )
            )
            copies[-1].start()
        for copy in copies:
            copy.wait()


def phase(where, begin, at, weight, gs, w, out, slots, squares=False):
    halves, pieces = len(gs), len(gs[0])
    rows = gs[0][0].shape[0]
    features = gs[0][0].shape[1] * halves
    do_weight, do_attn = at is not None, weight is not None
    capacity = at.shape[0] if do_weight else weight.shape[0]
    fresh = (w is None) if do_weight else (out is None)
    vmem = pl.BlockSpec(memory_space=pltpu.VMEM)
    smem = pl.BlockSpec(memory_space=pltpu.SMEM)
    hbm = pl.BlockSpec(memory_space=pl.ANY)

    args, specs, outs, out_specs, aliases, scratch = [], [], [], [], {}, []

    def add(arg, spec):
        args.append(arg)
        specs.append(spec)

    def add_vmem(arg):
        add(pltpu.with_memory_space_constraint(arg, pltpu.VMEM), vmem)

    for scalar in where:
        add(scalar, smem)
    if do_weight:
        add_vmem(at)
    if do_attn:
        add_vmem(weight)
    for group in gs:
        for g in group:
            add_vmem(g)
    if do_weight:
        if not fresh:
            aliases[len(args)] = len(outs)
            add_vmem(w)
        outs.append(pltpu.VMEM((capacity, features), jnp.float32))
        out_specs.append(vmem)
    if do_attn:
        if not fresh:
            aliases[len(args)] = len(outs)
            add(out, hbm)
        outs.append(jax.ShapeDtypeStruct((slots, capacity), jnp.bfloat16))
        out_specs.append(hbm)
        scratch = [
            pltpu.VMEM((rows * pieces, capacity), jnp.float32),
            pltpu.VMEM((rows * pieces, capacity), jnp.bfloat16),
            pltpu.SemaphoreType.DMA((pieces,)),
        ]
    outs.append(pltpu.VMEM((8, 128), jnp.float32))
    out_specs.append(vmem)
    dots = do_weight + do_attn
    return pl.pallas_call(
        functools.partial(
            phase_kernel,
            (do_weight, do_attn, fresh, squares, pieces, halves, rows, begin),
        ),
        in_specs=specs,
        out_specs=out_specs,
        out_shape=outs,
        scratch_shapes=scratch,
        input_output_aliases=aliases,
        compiler_params=pltpu.CompilerParams(vmem_limit_bytes=10 * MIB),
        cost_estimate=pl.CostEstimate(
            flops=dots * capacity * rows * pieces * features // 4,
            bytes_accessed=2 * rows * pieces * features,
            transcendentals=0,
        ),
        name="phase_" + "w" * do_weight + "a" * do_attn,
    )(*args)


def scale_kernel(parts, w_ref, squares_ref, out_ref, block_ref, sems):
    capacity, features = w_ref.shape
    square_sum = jnp.sum(
        jnp.sum(squares_ref[...], axis=0, keepdims=True), axis=1, keepdims=True
    )
    factor = jnp.minimum(
        1.0, 1.0 / jnp.sqrt(square_sum / (HEADS * HEAD_DIM * features) + 1e-06)
    )
    copies = []
    height = capacity // parts
    for i in range(parts):
        part = pl.ds(i * height, height)
        block_ref[part, :] = (w_ref[part, :] * factor).astype(jnp.bfloat16)
        copies.append(pltpu.make_async_copy(block_ref.at[part], out_ref.at[part], sems.at[i]))
        copies[-1].start()
    for copy in copies:
        copy.wait()


def scaled(w, squares):
    capacity, features = w.shape
    vmem = pl.BlockSpec(memory_space=pltpu.VMEM)
    parts = 8
    return pl.pallas_call(
        functools.partial(scale_kernel, parts),
        in_specs=[vmem, vmem],
        out_specs=pl.BlockSpec(memory_space=pl.ANY),
        out_shape=jax.ShapeDtypeStruct((capacity, features), jnp.bfloat16),
        scratch_shapes=[
            pltpu.VMEM((capacity, features), jnp.bfloat16),
            pltpu.SemaphoreType.DMA((parts,)),
        ],
        compiler_params=pltpu.CompilerParams(vmem_limit_bytes=10 * MIB),
        cost_estimate=pl.CostEstimate(
            flops=capacity * features,
            bytes_accessed=2 * capacity * features,
            transcendentals=0,
        ),
        name="scale",
    )(pltpu.with_memory_space_constraint(w, pltpu.VMEM), squares)


def after(done, *arrays):
    vmem = pl.BlockSpec(memory_space=pltpu.VMEM)
    return pl.pallas_call(
        lambda *refs: None,
        in_specs=[vmem] * (len(arrays) + 1),
        out_specs=[vmem] * len(arrays),
        out_shape=[pltpu.VMEM(x.shape, x.dtype) for x in arrays],
        input_output_aliases={i: i for i in range(len(arrays))},
        compiler_params=pltpu.CompilerParams(vmem_limit_bytes=MIB),
        name="after",
    )(*[pltpu.with_memory_space_constraint(x, pltpu.VMEM) for x in (*arrays, done)])


def halve_kernel(ahead_ref, behind_ref, left_ref, right_ref, sems):
    half = left_ref.shape[1]
    copies = [
        pltpu.make_async_copy(ahead_ref.at[:, pl.ds(0, half)], left_ref, sems.at[0]),
        pltpu.make_async_copy(behind_ref.at[:, pl.ds(half, half)], right_ref, sems.at[1]),
    ]
    for copy in copies:
        copy.start()
    for copy in copies:
        copy.wait()


def halved(ahead, behind):
    vmem = pl.BlockSpec(memory_space=pltpu.VMEM)
    rows, features = ahead.shape
    return pl.pallas_call(
        halve_kernel,
        in_specs=[vmem] * 2,
        out_specs=[vmem] * 2,
        out_shape=[pltpu.VMEM((rows, features // 2), ahead.dtype)] * 2,
        scratch_shapes=[pltpu.SemaphoreType.DMA((2,))],
        compiler_params=pltpu.CompilerParams(vmem_limit_bytes=MIB),
        name="halved",
    )(*[pltpu.with_memory_space_constraint(x, pltpu.VMEM) for x in (ahead, behind)])


def exchange(x, devices, stride, radix):
    total = x
    for shift in range(1, radix):
        pairs = []
        for d in range(devices):
            digit = d // stride % radix
            pairs.append((d, d + ((digit + shift) % radix - digit) * stride))
        total = total + lax.ppermute(x, "dp", pairs)
    return total


def on_device(ring, attn_out, out_grad, o_weight, head_counts, seq_counts):
    rows, features = out_grad.shape
    slots = attn_out.shape[0]
    devices, last = ring.devices, ring.length // 2
    offsets = [0] + [s * k for k in range(1, last) for s in (-1, 1)] + [last]
    counts = [2] + [4] * (last - 1) + [2]
    table = jnp.asarray(ring.owners(offsets))
    me = lax.axis_index("dp").astype(jnp.int32).reshape(1)
    where = (table, me, head_counts)
    own = live_rows(seq_counts, me, out_grad)
    ats = prepared(*where, attn_out, counts, rows)
    weight = o_weight

    def swap(x):
        return lax.ppermute(x, "dp", ring.swap())

    def forward(x):
        return lax.ppermute(x, "dp", ring.shift(1))

    def backward(x):
        return lax.ppermute(x, "dp", ring.shift(-1))

    arrived = [[own, swap(own)]]
    ahead, behind = forward(own), backward(own)
    w, out, begin = None, None, 0
    for k in range(last):
        w, out, done = phase(where, begin, ats[k], weight, arrived, w, out, slots)
        begin += counts[k]
        ahead, behind = after(done, ahead, behind)
        if k < last - 1:
            arrived = [[ahead, swap(ahead), behind, swap(behind)]]
            if k + 2 == last:
                ahead, behind = halved(ahead, behind)
            ahead, behind = forward(ahead), backward(behind)
        else:
            arrived = [[ahead, swap(ahead)], [behind, swap(behind)]]
    w, squares = phase(where, begin, ats[last], None, arrived, w, None, slots, True)

    stride, late = 1, 0
    while stride < devices:
        radix = min(4, devices // stride)
        squares = exchange(squares, devices, stride, radix)
        if late < 2:
            gs = [group[late : late + 1] for group in arrived]
            out, done = phase(where, begin + late, None, weight, gs, None, out, slots)
        stride, late = stride * radix, late + 1
    return out, scaled(w, squares)


def solution(mesh):
    placed = (
        P("group", "dp"),
        P(("group", "dp"), None),
        P("dp", None),
        P("dp"),
        P(("group", "dp")),
    )
    ring = Ring(mesh.shape["dp"], 2 if mesh.shape["group"] == 2 else 1)
    return jax.shard_map(
        functools.partial(on_device, ring),
        mesh=mesh,
        in_specs=placed,
        out_specs=(P("group", "dp"), P(("group", "dp"), None)),
        check_vma=False,
    )
```

time: 199 us -> 138 us (0.69)
  local copies, waits for them, and re-layouts: 87 us -> 2.79 us
  waiting for transfers between devices: 0.76 us -> 48.5 us
  Pallas kernels: 85.5 us -> 67.2 us
  starting transfers between devices: 20.3 us -> 17.3 us
    unnamed x85 -> x8, local copies, waits for them, and re-layouts: 77.3 us -> 2.79 us
    ppermute x4, waiting for transfers between devices: 0.01 us -> 35.6 us  [forward(): return lax.ppermute(x, 'dp', ring.shift(1))]
    pallas_call x7, Pallas kernels: 69.5 us -> 59.4 us  [phase(): pl.pallas_call(functools.partial(phase_kernel, (do_weight, do_attn, fresh...]
    slice x6 -> x0, local copies, waits for them, and re-layouts: 8.45 us -> none  [the longest x2 5.53 us: on_device(): at = a[begin * rows:(begin + count) * rows].T]
    pallas_call x6 -> x8, Pallas kernels: 16 us -> 7.77 us  [the longest x1 3.38 us: prepared(): pl.pallas_call(functools.partial(prep_kernel, counts, rows), in_specs=[sm...]
    ppermute x9, waiting for transfers between devices: 0.73 us -> 8.17 us  [swap(): return lax.ppermute(x, 'dp', ring.swap())]
    ppermute x4, waiting for transfers between devices: 0.01 us -> 4.78 us  [backward(): return lax.ppermute(x, 'dp', ring.shift(-1))]
    ppermute x6, starting transfers between devices: 8.97 us -> 5.9 us  [exchange(): total = total + lax.ppermute(x, 'dp', pairs)]
  transfers between devices with their start and end apart: 23 -> 23, of which waited for: 3 -> 15; matrix products, arithmetic and copies ran while one was open for 10% -> 0% of each run, Pallas kernels for 37% -> 42%
where the time goes in v4:
time: 138 us
  Pallas kernels  67.2 us (49%)
  waiting for transfers between devices  48.5 us (35%)
  starting transfers between devices  17.3 us (13%)
  local copies, waits for them, and re-layouts  2.79 us (2%)
  between operations  2.13 us (2%)
    pallas_call x7, Pallas kernels, phase(): pl.pallas_call(functools.partial(phase_kernel, (do_weight, do_attn, fresh...  59.4 us
    ppermute x4, waiting for transfers between devices, forward(): return lax.ppermute(x, 'dp', ring.shift(1))  35.6 us
    ppermute x9, waiting for transfers between devices, swap(): return lax.ppermute(x, 'dp', ring.swap())  8.17 us
    ppermute x4, starting transfers between devices, forward(): return lax.ppermute(x, 'dp', ring.shift(1))  7.38 us
    ppermute x6, starting transfers between devices, exchange(): total = total + lax.ppermute(x, 'dp', pairs)  5.9 us
    ppermute x4, waiting for transfers between devices, backward(): return lax.ppermute(x, 'dp', ring.shift(-1))  4.78 us
    pallas_call x1, Pallas kernels, prepared(): pl.pallas_call(functools.partial(prep_kernel, counts, rows), in_specs=[sm...  3.38 us
    pallas_call x1, Pallas kernels, scaled(): pl.pallas_call(functools.partial(scale_kernel, parts), in_specs=[vmem, vm...  3 us
  transfers between devices with their start and end apart: 23, of which 15 were waited for; matrix products, arithmetic and copies ran while one was open for 0% of the time, Pallas kernels for 42%

profile of v4, /device:TPU:0, one launch (start us, length us, event | category | flops | bytes accessed | tf_op | source)
XLA Modules:
  0.0 137.9 jit_solution(4298475394467421822)
XLA Ops:
  1.3 0.0 copy-start.1
  1.3 1.3 live.1.refs_5_
  2.6 0.5 collective-permute-start.2
  3.1 2.6 %collective-permute-start = (bf16[144,4096]{1,0:T(8,128)(2,1)S(1)}, bf16[144,4096]{1,0:T(8,128)(2,1)S(1)}, u32[]{:S(2)}, u32[]{:S(2)}) collective-permute-start(bf16[144,4096]{1,0:T(8,128)(2,1)S(1)} %live.1.refs_5_), channel_id=1, source_target_pairs={{0,4},{1,5},{4,8},{5,9},{8,12},{9,13},{12,14},{13,15},{14,10},{15,... | collective-permute-start | bytes 3538952 | tf_op jit(solution)/shard_map/ppermute | solution.py:367
  5.7 0.0 collective-permute-start.1
  6.4 0.0 copy-done.1
  6.4 3.4 %prep.1 = (bf16[768,288]{1,0:T(8,128)(2,1)S(1)}, bf16[768,576]{1,0:T(8,128)(2,1)S(1)}, bf16[768,576]{1,0:T(8,128)(2,1)S(1)}, bf16[768,576]{1,0:T(8,128)(2,1)S(1)}, bf16[768,288]{1,0:T(8,128)(2,1)S(1)}) custom-call(s32[16,16]{1,0:T(8,128)S(1)} %copy-done.1, s32[1]{0:T(128)} %bitcast.me_ref.refs_1_, s32[1]{0:T(128)S(6)} %copy.42.heads_ref.refs_2_, ...), custom_call_target="tpu_custom_call" | custom-call | bytes 7077888 | tf_op jit(solution)/shard_map/prep/pallas_call | solution.py:107
  9.8 0.0 collective-permute-done.2.refs_6_
  9.8 0.0 copy-start
  9.8 2.8 %copy-done = bf16[768,4096]{1,0:T(8,128)(2,1)S(1)} copy-done((bf16[768,4096]{1,0:T(8,128)(2,1)S(1)}, bf16[768,4096]{1,0:T(8,128)(2,1)}, u32[]{:S(2)}) %copy-start) | copy-done | bytes 6291480
  12.6 7.8 %phase_wa.4 = (f32[768,4096]{1,0:T(8,128)S(1)}, bf16[2304,768]{1,0:T(8,128)(2,1)}, f32[8,128]{1,0:T(8,128)S(1)}) custom-call(s32[16,16]{1,0:T(8,128)S(1)} %copy-done.1, s32[1]{0:T(128)} %bitcast.me_ref.refs_1_, s32[1]{0:T(128)S(6)} %copy.42.heads_ref.refs_2_, bf16[768,288]{1,0:T(8,128)(2,1)S(1)} %get-tuple-element.33.refs_3_, bf16[768,4096]{1,0:T(8,128)(2,1)S(1)} %copy-done, ...), custom_call_target="tpu_custom_call" | custom-call | flops 452984832 | bytes 2359296 | tf_op jit(solution)/shard_map/phase_wa/pallas_call | solution.py:238
  20.5 11.8 %collective-permute-done.refs_0_ = bf16[144,4096]{1,0:T(8,128)(2,1)S(1)} collective-permute-done((bf16[144,4096]{1,0:T(8,128)(2,1)S(1)}, bf16[144,4096]{1,0:T(8,128)(2,1)S(1)}, u32[]{:S(2)}, u32[]{:S(2)}) %collective-permute-start) | collective-permute-done | bytes 1179680 | tf_op jit(solution)/shard_map/ppermute | solution.py:367
  32.3 1.5 %collective-permute-done.1.refs_1_ = bf16[144,4096]{1,0:T(8,128)(2,1)S(1)} collective-permute-done((bf16[144,4096]{1,0:T(8,128)(2,1)S(1)}, bf16[144,4096]{1,0:T(8,128)(2,1)S(1)}, u32[]{:S(2)}, u32[]{:S(2)}) %collective-permute-start.1) | collective-permute-done | bytes 1179680 | tf_op jit(solution)/shard_map/ppermute | solution.py:370
  33.8 0.0 collective-permute-start.5
  33.8 0.5 collective-permute-start.6
  34.3 1.6 %collective-permute-start.3 = (bf16[144,4096]{1,0:T(8,128)(2,1)S(1)}, bf16[144,4096]{1,0:T(8,128)(2,1)S(1)}, u32[]{:S(2)}, u32[]{:S(2)}) collective-permute-start(bf16[144,4096]{1,0:T(8,128)(2,1)S(1)} %get-tuple-element.35.refs_5_), channel_id=1, source_target_pairs={{0,4},{1,5},{4,8},{5,9},{8,12},{9,13},{12,14},{13,15},{14,10},{15,... | collective-permute-start | bytes 3538952 | tf_op jit(solution)/shard_map/ppermute | solution.py:367
  35.9 0.4 collective-permute-start.4
  36.3 0.3 collective-permute-done.5.refs_6_
  36.6 1.7 %collective-permute-done.6.refs_8_ = bf16[144,4096]{1,0:T(8,128)(2,1)S(1)} collective-permute-done((bf16[144,4096]{1,0:T(8,128)(2,1)S(1)}, bf16[144,4096]{1,0:T(8,128)(2,1)S(1)}, u32[]{:S(2)}, u32[]{:S(2)}) %collective-permute-start.6) | collective-permute-done | bytes 1179680 | tf_op jit(solution)/shard_map/ppermute | solution.py:364
  38.3 11.9 %phase_wa.5 = (f32[768,4096]{1,0:T(8,128)S(1)}, bf16[2304,768]{1,0:T(8,128)(2,1)}, f32[8,128]{1,0:T(8,128)S(1)}) custom-call(s32[16,16]{1,0:T(8,128)S(1)} %copy-done.1, s32[1]{0:T(128)} %bitcast.me_ref.refs_1_, s32[1]{0:T(128)S(6)} %copy.42.heads_ref.refs_2_, ...), custom_call_target="tpu_custom_call", output_to_operand_aliasing={{0}: (9, {}), {1}: (10, {})} | custom-call | flops 905969664 | bytes 4718592 | tf_op jit(solution)/shard_map/phase_wa/pallas_call | solution.py:238
  50.3 11.9 %collective-permute-done.3.refs_0_ = bf16[144,4096]{1,0:T(8,128)(2,1)S(1)} collective-permute-done((bf16[144,4096]{1,0:T(8,128)(2,1)S(1)}, bf16[144,4096]{1,0:T(8,128)(2,1)S(1)}, u32[]{:S(2)}, u32[]{:S(2)}) %collective-permute-start.3) | collective-permute-done | bytes 1179680 | tf_op jit(solution)/shard_map/ppermute | solution.py:367
  62.2 1.3 collective-permute-done.4.refs_1_
  63.5 0.0 collective-permute-start.10
  63.5 0.5 collective-permute-start.9
  64.0 1.6 %collective-permute-start.7 = (bf16[144,4096]{1,0:T(8,128)(2,1)S(1)}, bf16[144,4096]{1,0:T(8,128)(2,1)S(1)}, u32[]{:S(2)}, u32[]{:S(2)}) collective-permute-start(bf16[144,4096]{1,0:T(8,128)(2,1)S(1)} %get-tuple-element.41.refs_5_), channel_id=1, source_target_pairs={{0,4},{1,5},{4,8},{5,9},{8,12},{9,13},{12,14},{13,15},{14,10},{15,... | collective-permute-start | bytes 3538952 | tf_op jit(solution)/shard_map/ppermute | solution.py:367
  65.6 0.4 collective-permute-start.8
  66.0 0.3 collective-permute-done.10.refs_8_
  66.3 1.7 %collective-permute-done.9.refs_6_ = bf16[144,4096]{1,0:T(8,128)(2,1)S(1)} collective-permute-done((bf16[144,4096]{1,0:T(8,128)(2,1)S(1)}, bf16[144,4096]{1,0:T(8,128)(2,1)S(1)}, u32[]{:S(2)}, u32[]{:S(2)}) %collective-permute-start.9) | collective-permute-done | bytes 1179680 | tf_op jit(solution)/shard_map/ppermute | solution.py:364
  68.0 12.0 %phase_wa.6 = (f32[768,4096]{1,0:T(8,128)S(1)}, bf16[2304,768]{1,0:T(8,128)(2,1)}, f32[8,128]{1,0:T(8,128)S(1)}) custom-call(s32[16,16]{1,0:T(8,128)S(1)} %copy-done.1, s32[1]{0:T(128)} %bitcast.me_ref.refs_1_, s32[1]{0:T(128)S(6)} %copy.42.heads_ref.refs_2_, ...), custom_call_target="tpu_custom_call", output_to_operand_aliasing={{0}: (9, {}), {1}: (10, {})} | custom-call | flops 905969664 | bytes 4718592 | tf_op jit(solution)/shard_map/phase_wa/pallas_call | solution.py:238
  80.0 11.9 %collective-permute-done.7.refs_0_ = bf16[144,4096]{1,0:T(8,128)(2,1)S(1)} collective-permute-done((bf16[144,4096]{1,0:T(8,128)(2,1)S(1)}, bf16[144,4096]{1,0:T(8,128)(2,1)S(1)}, u32[]{:S(2)}, u32[]{:S(2)}) %collective-permute-start.7) | collective-permute-done | bytes 1179680 | tf_op jit(solution)/shard_map/ppermute | solution.py:367
  91.9 1.3 collective-permute-done.8.refs_1_
  93.2 0.0 collective-permute-start.13
  93.2 0.5 collective-permute-start.14
  93.7 0.1 halved.1
  93.8 1.6 %collective-permute-start.11 = (bf16[144,2048]{1,0:T(8,128)(2,1)S(1)}, bf16[144,2048]{1,0:T(8,128)(2,1)S(1)}, u32[]{:S(2)}, u32[]{:S(2)}) collective-permute-start(bf16[144,2048]{1,0:T(8,128)(2,1)S(1)} %get-tuple-element.49), channel_id=1, source_target_pairs={{0,4},{1,5},{4,8},{5,9},{8,12},{9,13},{12,14},{13,15},{14,10},{15,... | collective-permute-start | bytes 1769480 | tf_op jit(solution)/shard_map/ppermute | solution.py:367
  95.4 0.5 collective-permute-start.12
  95.9 0.1 collective-permute-done.13.refs_6_
  96.0 1.7 %collective-permute-done.14.refs_8_ = bf16[144,4096]{1,0:T(8,128)(2,1)S(1)} collective-permute-done((bf16[144,4096]{1,0:T(8,128)(2,1)S(1)}, bf16[144,4096]{1,0:T(8,128)(2,1)S(1)}, u32[]{:S(2)}, u32[]{:S(2)}) %collective-permute-start.14) | collective-permute-done | bytes 1179680 | tf_op jit(solution)/shard_map/ppermute | solution.py:364
  97.7 11.9 %phase_wa.7 = (f32[768,4096]{1,0:T(8,128)S(1)}, bf16[2304,768]{1,0:T(8,128)(2,1)}, f32[8,128]{1,0:T(8,128)S(1)}) custom-call(s32[16,16]{1,0:T(8,128)S(1)} %copy-done.1, s32[1]{0:T(128)} %bitcast.me_ref.refs_1_, s32[1]{0:T(128)S(6)} %copy.42.heads_ref.refs_2_, ...), custom_call_target="tpu_custom_call", output_to_operand_aliasing={{0}: (9, {}), {1}: (10, {})} | custom-call | flops 905969664 | bytes 4718592 | tf_op jit(solution)/shard_map/phase_wa/pallas_call | solution.py:238
  109.6 0.0 collective-permute-done.11.refs_0_
  109.7 0.7 collective-permute-done.12.refs_1_
  110.3 0.0 collective-permute-start.15
  110.3 0.5 collective-permute-start.16
  110.8 1.5 %collective-permute-done.15.refs_4_.refs_5_ = bf16[144,2048]{1,0:T(8,128)(2,1)S(1)} collective-permute-done((bf16[144,2048]{1,0:T(8,128)(2,1)S(1)}, bf16[144,2048]{1,0:T(8,128)(2,1)S(1)}, u32[]{:S(2)}, u32[]{:S(2)}) %collective-permute-start.15) | collective-permute-done | bytes 589856 | tf_op jit(solution)/shard_map/ppermute | solution.py:364
  112.3 0.8 collective-permute-done.16.refs_5_.refs_7_
  113.2 0.0 slice-start
  113.2 5.3 %phase_w.1 = (f32[768,4096]{1,0:T(8,128)S(1)}, f32[8,128]{1,0:T(8,128)S(1)}) custom-call(s32[16,16]{1,0:T(8,128)S(1)} %copy-done.1, s32[1]{0:T(128)} %bitcast.me_ref.refs_1_, s32[1]{0:T(128)S(6)} %copy.42.heads_ref.refs_2_, bf16[768,288]{1,0:T(8,128)(2,1)S(1)} %get-tuple-element.60.refs_3_, ...), custom_call_target="tpu_custom_call", output_to_operand_aliasing={{0}: (8, {})} | custom-call | flops 226492416 | bytes 2359296 | tf_op jit(solution)/shard_map/phase_w/pallas_call | solution.py:238
  118.5 0.2 collective-permute-start.17
  118.7 0.5 collective-permute-start.18
  119.1 1.3 collective-permute-start.19
  120.5 0.0 slice-done
  120.5 0.0 slice-done.1
  120.5 5.2 %phase_a.2 = (bf16[2304,768]{1,0:T(8,128)(2,1)}, f32[8,128]{1,0:T(8,128)}) custom-call(s32[16,16]{1,0:T(8,128)S(1)} %copy-done.1, s32[1]{0:T(128)} %bitcast.me_ref.refs_1_, s32[1]{0:T(128)S(6)} %copy.42.heads_ref.refs_2_, bf16[768,4096]{1,0:T(8,128)(2,1)S(1)} %bitcast.2, ...), custom_call_target="tpu_custom_call", output_to_operand_aliasing={{0}: (6, {})} | custom-call | flops 113246208 | bytes 1179648 | tf_op jit(solution)/shard_map/phase_a/pallas_call | solution.py:238
  125.7 0.0 collective-permute-done.17
  125.7 0.0 collective-permute-done.18
  125.8 0.0 collective-permute-done.19
  125.8 0.8 collective-permute-start.20
  126.6 0.5 collective-permute-start.21
  127.1 2.6 %collective-permute-start.22 = (f32[8,128]{1,0:T(8,128)S(1)}, f32[8,128]{1,0:T(8,128)S(1)}, u32[]{:S(2)}, u32[]{:S(2)}) collective-permute-start(f32[8,128]{1,0:T(8,128)S(1)} %add_add_fusion.1), channel_id=1, source_target_pairs={{0,12},{1,13},{2,14},{3,15},{4,0},{5,1},{6,2},{7,3},{8,4},{9,5},{1... | collective-permute-start | bytes 12296 | tf_op jit(solution)/shard_map/ppermute | solution.py:346
  129.7 5.2 %phase_a.3 = (bf16[2304,768]{1,0:T(8,128)(2,1)}, f32[8,128]{1,0:T(8,128)}) custom-call(s32[16,16]{1,0:T(8,128)S(1)} %copy-done.1, s32[1]{0:T(128)} %bitcast.me_ref.refs_1_, s32[1]{0:T(128)S(6)} %copy.42.heads_ref.refs_2_, bf16[768,4096]{1,0:T(8,128)(2,1)S(1)} %bitcast.2, ...), custom_call_target="tpu_custom_call", output_to_operand_aliasing={{0}: (6, {})} | custom-call | flops 113246208 | bytes 1179648 | tf_op jit(solution)/shard_map/phase_a/pallas_call | solution.py:238
  134.9 0.0 collective-permute-done.20
  134.9 0.0 collective-permute-done.21
  134.9 0.0 collective-permute-done.22
  134.9 3.0 %scale.1 = bf16[768,4096]{1,0:T(8,128)(2,1)} custom-call(f32[768,4096]{1,0:T(8,128)S(1)} %get-tuple-element.62.w_ref, f32[8,128]{1,0:T(8,128)S(1)} %add_add_fusion.squares_ref), custom_call_target="tpu_custom_call" | custom-call | flops 3145728 | bytes 6291456 | tf_op jit(solution)/shard_map/scale/pallas_call | solution.py:281
  (8 shorter events, 0.0 us)
Async XLA Ops:
  1.3 5.2 %copy-start.1 = (s32[16,16]{1,0:T(8,128)S(1)}, s32[16,16]{1,0:T(8,128)}, u32[]{:S(2)}) copy-start(s32[16,16]{1,0:T(8,128)} %constant.6.clone.table_ref.refs_0_) | copy-start | bytes 3076
  2.6 7.2 %collective-permute-start.2 = (bf16[144,4096]{1,0:T(8,128)(2,1)S(1)}, bf16[144,4096]{1,0:T(8,128)(2,1)S(1)}, u32[]{:S(2)}, u32[]{:S(2)}) collective-permute-start(bf16[144,4096]{1,0:T(8,128)(2,1)S(1)} %live.1.refs_5_), channel_id=1, source_target_pairs={{0,1},{1,0},{2,3},{3,2},{4,5},{5,4},{6,7},{7,6},{8,9},{9,8},{10,11... | collective-permute-start | bytes 3538952 | tf_op jit(solution)/shard_map/ppermute | solution.py:364
  3.1 29.2 %collective-permute-start = (bf16[144,4096]{1,0:T(8,128)(2,1)S(1)}, bf16[144,4096]{1,0:T(8,128)(2,1)S(1)}, u32[]{:S(2)}, u32[]{:S(2)}) collective-permute-start(bf16[144,4096]{1,0:T(8,128)(2,1)S(1)} %live.1.refs_5_), channel_id=1, source_target_pairs={{0,4},{1,5},{4,8},{5,9},{8,12},{9,13},{12,14},{13,15},{14,10},{15,... | collective-permute-start | bytes 3538952 | tf_op jit(solution)/shard_map/ppermute | solution.py:367
  5.7 28.0 %collective-permute-start.1 = (bf16[144,4096]{1,0:T(8,128)(2,1)S(1)}, bf16[144,4096]{1,0:T(8,128)(2,1)S(1)}, u32[]{:S(2)}, u32[]{:S(2)}) collective-permute-start(bf16[144,4096]{1,0:T(8,128)(2,1)S(1)} %live.1.refs_5_), channel_id=1, source_target_pairs={{0,2},{1,3},{4,0},{5,1},{8,4},{9,5},{12,8},{13,9},{14,12},{15,13},... | collective-permute-start | bytes 3538952 | tf_op jit(solution)/shard_map/ppermute | solution.py:370
  9.8 2.8 %copy-start = (bf16[768,4096]{1,0:T(8,128)(2,1)S(1)}, bf16[768,4096]{1,0:T(8,128)(2,1)}, u32[]{:S(2)}) copy-start(bf16[768,4096]{1,0:T(8,128)(2,1)} %refs_3_.3) | copy-start | bytes 18874372
  33.8 2.8 %collective-permute-start.5 = (bf16[144,4096]{1,0:T(8,128)(2,1)S(1)}, bf16[144,4096]{1,0:T(8,128)(2,1)S(1)}, u32[]{:S(2)}, u32[]{:S(2)}) collective-permute-start(bf16[144,4096]{1,0:T(8,128)(2,1)S(1)} %get-tuple-element.35.refs_5_), channel_id=1, source_target_pairs={{0,1},{1,0},{2,3},{3,2},{4,5},{5,4},{6,7},{7,6},{8,9},{9,8},{10,11... | collective-permute-start | bytes 3538952 | tf_op jit(solution)/shard_map/ppermute | solution.py:364
  33.8 4.5 %collective-permute-start.6 = (bf16[144,4096]{1,0:T(8,128)(2,1)S(1)}, bf16[144,4096]{1,0:T(8,128)(2,1)S(1)}, u32[]{:S(2)}, u32[]{:S(2)}) collective-permute-start(bf16[144,4096]{1,0:T(8,128)(2,1)S(1)} %get-tuple-element.36.refs_7_), channel_id=1, source_target_pairs={{0,1},{1,0},{2,3},{3,2},{4,5},{5,4},{6,7},{7,6},{8,9},{9,8},{10,11... | collective-permute-start | bytes 3538952 | tf_op jit(solution)/shard_map/ppermute | solution.py:364
  34.3 27.9 %collective-permute-start.3 = (bf16[144,4096]{1,0:T(8,128)(2,1)S(1)}, bf16[144,4096]{1,0:T(8,128)(2,1)S(1)}, u32[]{:S(2)}, u32[]{:S(2)}) collective-permute-start(bf16[144,4096]{1,0:T(8,128)(2,1)S(1)} %get-tuple-element.35.refs_5_), channel_id=1, source_target_pairs={{0,4},{1,5},{4,8},{5,9},{8,12},{9,13},{12,14},{13,15},{14,10},{15,... | collective-permute-start | bytes 3538952 | tf_op jit(solution)/shard_map/ppermute | solution.py:367
  35.9 27.6 %collective-permute-start.4 = (bf16[144,4096]{1,0:T(8,128)(2,1)S(1)}, bf16[144,4096]{1,0:T(8,128)(2,1)S(1)}, u32[]{:S(2)}, u32[]{:S(2)}) collective-permute-start(bf16[144,4096]{1,0:T(8,128)(2,1)S(1)} %get-tuple-element.36.refs_7_), channel_id=1, source_target_pairs={{0,2},{1,3},{4,0},{5,1},{8,4},{9,5},{12,8},{13,9},{14,12},{15,13},... | collective-permute-start | bytes 3538952 | tf_op jit(solution)/shard_map/ppermute | solution.py:370
  63.5 2.8 %collective-permute-start.10 = (bf16[144,4096]{1,0:T(8,128)(2,1)S(1)}, bf16[144,4096]{1,0:T(8,128)(2,1)S(1)}, u32[]{:S(2)}, u32[]{:S(2)}) collective-permute-start(bf16[144,4096]{1,0:T(8,128)(2,1)S(1)} %get-tuple-element.42.refs_7_), channel_id=1, source_target_pairs={{0,1},{1,0},{2,3},{3,2},{4,5},{5,4},{6,7},{7,6},{8,9},{9,8},{10,11... | collective-permute-start | bytes 3538952 | tf_op jit(solution)/shard_map/ppermute | solution.py:364
  63.5 4.5 %collective-permute-start.9 = (bf16[144,4096]{1,0:T(8,128)(2,1)S(1)}, bf16[144,4096]{1,0:T(8,128)(2,1)S(1)}, u32[]{:S(2)}, u32[]{:S(2)}) collective-permute-start(bf16[144,4096]{1,0:T(8,128)(2,1)S(1)} %get-tuple-element.41.refs_5_), channel_id=1, source_target_pairs={{0,1},{1,0},{2,3},{3,2},{4,5},{5,4},{6,7},{7,6},{8,9},{9,8},{10,11... | collective-permute-start | bytes 3538952 | tf_op jit(solution)/shard_map/ppermute | solution.py:364
  64.0 27.9 %collective-permute-start.7 = (bf16[144,4096]{1,0:T(8,128)(2,1)S(1)}, bf16[144,4096]{1,0:T(8,128)(2,1)S(1)}, u32[]{:S(2)}, u32[]{:S(2)}) collective-permute-start(bf16[144,4096]{1,0:T(8,128)(2,1)S(1)} %get-tuple-element.41.refs_5_), channel_id=1, source_target_pairs={{0,4},{1,5},{4,8},{5,9},{8,12},{9,13},{12,14},{13,15},{14,10},{15,... | collective-permute-start | bytes 3538952 | tf_op jit(solution)/shard_map/ppermute | solution.py:367
  65.6 27.6 %collective-permute-start.8 = (bf16[144,4096]{1,0:T(8,128)(2,1)S(1)}, bf16[144,4096]{1,0:T(8,128)(2,1)S(1)}, u32[]{:S(2)}, u32[]{:S(2)}) collective-permute-start(bf16[144,4096]{1,0:T(8,128)(2,1)S(1)} %get-tuple-element.42.refs_7_), channel_id=1, source_target_pairs={{0,2},{1,3},{4,0},{5,1},{8,4},{9,5},{12,8},{13,9},{14,12},{15,13},... | collective-permute-start | bytes 3538952 | tf_op jit(solution)/shard_map/ppermute | solution.py:370
  93.2 2.8 %collective-permute-start.13 = (bf16[144,4096]{1,0:T(8,128)(2,1)S(1)}, bf16[144,4096]{1,0:T(8,128)(2,1)S(1)}, u32[]{:S(2)}, u32[]{:S(2)}) collective-permute-start(bf16[144,4096]{1,0:T(8,128)(2,1)S(1)} %get-tuple-element.47.ahead_ref.refs_5_), channel_id=1, source_target_pairs={{0,1},{1,0},{2,3},{3,2},{4,5},{5,4},{6,7},{7,6},{8,9},{9,8},{10,11... | collective-permute-start | bytes 3538952 | tf_op jit(solution)/shard_map/ppermute | solution.py:364
  93.2 4.5 %collective-permute-start.14 = (bf16[144,4096]{1,0:T(8,128)(2,1)S(1)}, bf16[144,4096]{1,0:T(8,128)(2,1)S(1)}, u32[]{:S(2)}, u32[]{:S(2)}) collective-permute-start(bf16[144,4096]{1,0:T(8,128)(2,1)S(1)} %get-tuple-element.48.behind_ref.refs_7_), channel_id=1, source_target_pairs={{0,1},{1,0},{2,3},{3,2},{4,5},{5,4},{6,7},{7,6},{8,9},{9,8},{10,11... | collective-permute-start | bytes 3538952 | tf_op jit(solution)/shard_map/ppermute | solution.py:364
  93.8 15.9 %collective-permute-start.11 = (bf16[144,2048]{1,0:T(8,128)(2,1)S(1)}, bf16[144,2048]{1,0:T(8,128)(2,1)S(1)}, u32[]{:S(2)}, u32[]{:S(2)}) collective-permute-start(bf16[144,2048]{1,0:T(8,128)(2,1)S(1)} %get-tuple-element.49), channel_id=1, source_target_pairs={{0,4},{1,5},{4,8},{5,9},{8,12},{9,13},{12,14},{13,15},{14,10},{15,... | collective-permute-start | bytes 1769480 | tf_op jit(solution)/shard_map/ppermute | solution.py:367
  95.4 15.0 %collective-permute-start.12 = (bf16[144,2048]{1,0:T(8,128)(2,1)S(1)}, bf16[144,2048]{1,0:T(8,128)(2,1)S(1)}, u32[]{:S(2)}, u32[]{:S(2)}) collective-permute-start(bf16[144,2048]{1,0:T(8,128)(2,1)S(1)} %get-tuple-element.50), channel_id=1, source_target_pairs={{0,2},{1,3},{4,0},{5,1},{8,4},{9,5},{12,8},{13,9},{14,12},{15,13},... | collective-permute-start | bytes 1769480 | tf_op jit(solution)/shard_map/ppermute | solution.py:370
  110.3 2.0 %collective-permute-start.15 = (bf16[144,2048]{1,0:T(8,128)(2,1)S(1)}, bf16[144,2048]{1,0:T(8,128)(2,1)S(1)}, u32[]{:S(2)}, u32[]{:S(2)}) collective-permute-start(bf16[144,2048]{1,0:T(8,128)(2,1)S(1)} %get-tuple-element.55.refs_4_), channel_id=1, source_target_pairs={{0,1},{1,0},{2,3},{3,2},{4,5},{5,4},{6,7},{7,6},{8,9},{9,8},{10,11... | collective-permute-start | bytes 1769480 | tf_op jit(solution)/shard_map/ppermute | solution.py:364
  110.3 2.8 %collective-permute-start.16 = (bf16[144,2048]{1,0:T(8,128)(2,1)S(1)}, bf16[144,2048]{1,0:T(8,128)(2,1)S(1)}, u32[]{:S(2)}, u32[]{:S(2)}) collective-permute-start(bf16[144,2048]{1,0:T(8,128)(2,1)S(1)} %get-tuple-element.56.refs_5_.refs_6_), channel_id=1, source_target_pairs={{0,1},{1,0},{2,3},{3,2},{4,5},{5,4},{6,7},{7,6},{8,9},{9,8},{10,11... | collective-permute-start | bytes 1769480 | tf_op jit(solution)/shard_map/ppermute | solution.py:364
  113.2 7.3 %slice-start = ((s8[6291456]{0:T(1024)(128)(4,1)}), s8[4194304]{0:T(1024)(128)(4,1)S(1)}, s32[]{:S(2)}) async-start(s8[6291456]{0:T(1024)(128)(4,1)} %bitcast.1), calls=%async_computation | async-start | bytes 8388608
  113.2 7.3 %slice-start.1 = ((s8[6291456]{0:T(1024)(128)(4,1)}), s8[2097152]{0:T(1024)(128)(4,1)S(1)}, s32[]{:S(2)}) async-start(s8[6291456]{0:T(1024)(128)(4,1)} %bitcast.1), calls=%async_computation.1 | async-start | bytes 4194304
  118.5 7.3 %collective-permute-start.17 = (f32[8,128]{1,0:T(8,128)S(1)}, f32[8,128]{1,0:T(8,128)S(1)}, u32[]{:S(2)}, u32[]{:S(2)}) collective-permute-start(f32[8,128]{1,0:T(8,128)S(1)} %get-tuple-element.63), channel_id=1, source_target_pairs={{0,1},{1,2},{2,3},{3,0},{4,5},{5,6},{6,7},{7,4},{8,9},{9,10},{10,1... | collective-permute-start | bytes 12296 | tf_op jit(solution)/shard_map/ppermute | solution.py:346
  118.7 7.1 %collective-permute-start.18 = (f32[8,128]{1,0:T(8,128)S(1)}, f32[8,128]{1,0:T(8,128)S(1)}, u32[]{:S(2)}, u32[]{:S(2)}) collective-permute-start(f32[8,128]{1,0:T(8,128)S(1)} %get-tuple-element.63), channel_id=1, source_target_pairs={{0,2},{1,3},{2,0},{3,1},{4,6},{5,7},{6,4},{7,5},{8,10},{9,11},{10,... | collective-permute-start | bytes 12296 | tf_op jit(solution)/shard_map/ppermute | solution.py:346
  119.1 6.6 %collective-permute-start.19 = (f32[8,128]{1,0:T(8,128)S(1)}, f32[8,128]{1,0:T(8,128)S(1)}, u32[]{:S(2)}, u32[]{:S(2)}) collective-permute-start(f32[8,128]{1,0:T(8,128)S(1)} %get-tuple-element.63), channel_id=1, source_target_pairs={{0,3},{1,0},{2,1},{3,2},{4,7},{5,4},{6,5},{7,6},{8,11},{9,8},{10,9... | collective-permute-start | bytes 12296 | tf_op jit(solution)/shard_map/ppermute | solution.py:346
  125.8 9.1 %collective-permute-start.20 = (f32[8,128]{1,0:T(8,128)S(1)}, f32[8,128]{1,0:T(8,128)S(1)}, u32[]{:S(2)}, u32[]{:S(2)}) collective-permute-start(f32[8,128]{1,0:T(8,128)S(1)} %add_add_fusion.1), channel_id=1, source_target_pairs={{0,4},{1,5},{2,6},{3,7},{4,8},{5,9},{6,10},{7,11},{8,12},{9,13},{1... | collective-permute-start | bytes 12296 | tf_op jit(solution)/shard_map/ppermute | solution.py:346
  126.6 8.3 %collective-permute-start.21 = (f32[8,128]{1,0:T(8,128)S(1)}, f32[8,128]{1,0:T(8,128)S(1)}, u32[]{:S(2)}, u32[]{:S(2)}) collective-permute-start(f32[8,128]{1,0:T(8,128)S(1)} %add_add_fusion.1), channel_id=1, source_target_pairs={{0,8},{1,9},{2,10},{3,11},{4,12},{5,13},{6,14},{7,15},{8,0},{9,1},... | collective-permute-start | bytes 12296 | tf_op jit(solution)/shard_map/ppermute | solution.py:346
  127.1 7.9 %collective-permute-start.22 = (f32[8,128]{1,0:T(8,128)S(1)}, f32[8,128]{1,0:T(8,128)S(1)}, u32[]{:S(2)}, u32[]{:S(2)}) collective-permute-start(f32[8,128]{1,0:T(8,128)S(1)} %add_add_fusion.1), channel_id=1, source_target_pairs={{0,12},{1,13},{2,14},{3,15},{4,0},{5,1},{6,2},{7,3},{8,4},{9,5},{1... | collective-permute-start | bytes 12296 | tf_op jit(solution)/shard_map/ppermute | solution.py:346

commit v5 on v4

--- a/solution.py
+++ b/solution.py
@@ -11,7 +11,7 @@
 HEADS = 64
 HEAD_DIM = 128
 SEQ = 16
-TILE = 512
+TILE = 1024
 MIB = 1024 * 1024
 
 
@@ -40,21 +40,25 @@
     def swap(self):
         return [(d, d ^ 1) for d in range(self.devices)]
 
-    def owners(self, offsets):
+    def owners(self, groups):
         table = []
         for d in range(self.devices):
             p, core = self.position[d // 2], d % 2
-            row = []
-            for offset in offsets:
-                row += [self.device(p + offset, core), self.device(p + offset, 1 - core)]
-            table.append(row)
+            table.append(
+                [
+                    self.device(p + offset, c)
+                    for offsets in groups
+                    for c in (core, 1 - core)
+                    for offset in offsets
+                ]
+            )
         return np.array(table, np.int32)
 
 
 def live_kernel(seqs_ref, me_ref, grad_ref, out_ref, sem):
-    copy = pltpu.make_async_copy(grad_ref, out_ref, sem)
-    copy.start()
-    copy.wait()
+    load = pltpu.make_async_copy(grad_ref, out_ref, sem)
+    load.start()
+    load.wait()
     for s in range(out_ref.shape[0] // SEQ):
 
         @pl.when(s >= seqs_ref[0])
@@ -122,32 +126,37 @@
 
 
 def phase_kernel(spec, *refs):
-    do_weight, do_attn, fresh, squares, pieces, halves, rows, begin = spec
+    groups, arrays, w_halves, attn, fresh_w, fresh_out, squares, rows, begin = spec
     refs = list(refs)
     table_ref, me_ref, heads_ref = refs.pop(0), refs.pop(0), refs.pop(0)
-    at_ref = refs.pop(0) if do_weight else None
-    weight_ref = refs.pop(0) if do_attn else None
-    g_refs = [[refs.pop(0) for _ in range(pieces)] for _ in range(halves)]
-    if do_weight and not fresh:
+    at_ref = refs.pop(0) if w_halves else None
+    weight_ref = refs.pop(0) if attn else None
+    g_refs = [refs.pop(0) for _ in range(arrays)]
+    if w_halves and not fresh_w:
         refs.pop(0)
-    if do_attn and not fresh:
+    before_ref = refs.pop(0) if attn == "last" else None
+    if attn in ("whole", "last") and not fresh_out:
         refs.pop(0)
-    w_ref = refs.pop(0) if do_weight else None
-    out_ref = refs.pop(0) if do_attn else None
+    w_ref = refs.pop(0) if w_halves else None
+    total_ref = refs.pop(0) if attn == "first" else None
+    out_ref = refs.pop(0) if attn in ("whole", "last") else None
     squares_ref = refs.pop(0)
-    if do_attn:
+    if attn in ("whole", "last"):
         total_ref, block_ref, sems = refs
+    if attn == "last":
+        total_ref[...] = before_ref[...]
+    elif attn:
         total_ref[...] = jnp.zeros_like(total_ref)
     squares_ref[...] = jnp.zeros_like(squares_ref)
-    span = g_refs[0][0].shape[1]
-
-    def body(half, j, carry):
+
+    def body(half, span, pieces, j, carry):
         here = pl.ds(pl.multiple_of(j * TILE, TILE), TILE)
         there = pl.ds(pl.multiple_of(half * span + j * TILE, TILE), TILE)
-        g = jnp.concatenate([t[:, here] for t in g_refs[half]], axis=0)
-        if do_weight:
+        g = [g_refs[i][start : start + count, here] for i, start, count in pieces]
+        g = jnp.concatenate(g, axis=0) if len(g) > 1 else g[0]
+        if half in w_halves:
             w = jnp.dot(at_ref[...], g, preferred_element_type=jnp.float32)
-            if not fresh:
+            if not fresh_w:
                 w = w + w_ref[:, there]
             w_ref[:, there] = w
         if squares:
@@ -156,7 +165,7 @@
             for lane in range(0, TILE, 128):
                 total = total + folded[:, lane : lane + 128]
             squares_ref[...] = total
-        if do_attn:
+        if attn:
             total_ref[...] += lax.dot_general(
                 g,
                 weight_ref[:, there],
@@ -165,14 +174,15 @@
             )
         return carry
 
-    for half in range(halves):
-        lax.fori_loop(0, span // TILE, functools.partial(body, half), 0)
-    if do_attn:
+    for half, span, pieces in groups:
+        lax.fori_loop(0, span // TILE, functools.partial(body, half, span, pieces), 0)
+    if attn in ("whole", "last"):
         total = total_ref[...]
         column = lax.broadcasted_iota(jnp.int32, total.shape, 1)
-        block_ref[...] = jnp.where(column < heads_ref[0] * HEAD_DIM, total, 0.0).astype(jnp.bfloat16)
+        live = column < heads_ref[0] * HEAD_DIM
+        block_ref[...] = jnp.where(live, total, 0.0).astype(jnp.bfloat16)
         copies = []
-        for i in range(pieces):
+        for i in range(total.shape[0] // rows):
             owner = table_ref[me_ref[0], begin + i]
             copies.append(
                 pltpu.make_async_copy(
@@ -186,13 +196,21 @@
             copy.wait()
 
 
-def phase(where, begin, at, weight, gs, w, out, slots, squares=False):
-    halves, pieces = len(gs), len(gs[0])
-    rows = gs[0][0].shape[0]
-    features = gs[0][0].shape[1] * halves
-    do_weight, do_attn = at is not None, weight is not None
-    capacity = at.shape[0] if do_weight else weight.shape[0]
-    fresh = (w is None) if do_weight else (out is None)
+def phase(
+    where, shapes, begin, groups, at=None, w=None, w_halves=(),
+    weight=None, attn=None, before=None, out=None, squares=False,
+):
+    slots, capacity, features, rows = shapes
+    arrays, described = [], []
+    for half, pieces in groups:
+        placed = []
+        for array, start, count in pieces:
+            known = [i for i, x in enumerate(arrays) if x is array]
+            if not known:
+                arrays.append(array)
+            placed.append((known[0] if known else len(arrays) - 1, start, count))
+        described.append((half, pieces[0][0].shape[1], tuple(placed)))
+    height = sum(count for _, _, count in groups[0][1])
     vmem = pl.BlockSpec(memory_space=pltpu.VMEM)
     smem = pl.BlockSpec(memory_space=pltpu.SMEM)
     hbm = pl.BlockSpec(memory_space=pl.ANY)
@@ -208,50 +226,54 @@
 
     for scalar in where:
         add(scalar, smem)
-    if do_weight:
+    if w_halves:
         add_vmem(at)
-    if do_attn:
+    if attn:
         add_vmem(weight)
-    for group in gs:
-        for g in group:
-            add_vmem(g)
-    if do_weight:
-        if not fresh:
+    for array in arrays:
+        add_vmem(array)
+    if w_halves:
+        if w is not None:
             aliases[len(args)] = len(outs)
             add_vmem(w)
         outs.append(pltpu.VMEM((capacity, features), jnp.float32))
         out_specs.append(vmem)
-    if do_attn:
-        if not fresh:
+    if attn == "last":
+        add_vmem(before)
+    if attn == "first":
+        outs.append(pltpu.VMEM((height, capacity), jnp.float32))
+        out_specs.append(vmem)
+    elif attn:
+        if out is not None:
             aliases[len(args)] = len(outs)
             add(out, hbm)
         outs.append(jax.ShapeDtypeStruct((slots, capacity), jnp.bfloat16))
         out_specs.append(hbm)
         scratch = [
-            pltpu.VMEM((rows * pieces, capacity), jnp.float32),
-            pltpu.VMEM((rows * pieces, capacity), jnp.bfloat16),
-            pltpu.SemaphoreType.DMA((pieces,)),
+            pltpu.VMEM((height, capacity), jnp.float32),
+            pltpu.VMEM((height, capacity), jnp.bfloat16),
+            pltpu.SemaphoreType.DMA((height // rows,)),
         ]
     outs.append(pltpu.VMEM((8, 128), jnp.float32))
     out_specs.append(vmem)
-    dots = do_weight + do_attn
-    return pl.pallas_call(
-        functools.partial(
-            phase_kernel,
-            (do_weight, do_attn, fresh, squares, pieces, halves, rows, begin),
-        ),
+    spec = (
+        tuple(described), len(arrays), tuple(w_halves), attn, w is None, out is None,
+        squares, rows, begin,
+    )
+    return pl.pallas_call(
+        functools.partial(phase_kernel, spec),
         in_specs=specs,
         out_specs=out_specs,
         out_shape=outs,
         scratch_shapes=scratch,
         input_output_aliases=aliases,
-        compiler_params=pltpu.CompilerParams(vmem_limit_bytes=10 * MIB),
+        compiler_params=pltpu.CompilerParams(vmem_limit_bytes=12 * MIB),
         cost_estimate=pl.CostEstimate(
-            flops=dots * capacity * rows * pieces * features // 4,
-            bytes_accessed=2 * rows * pieces * features,
+            flops=1,
+            bytes_accessed=1,
             transcendentals=0,
         ),
-        name="phase_" + "w" * do_weight + "a" * do_attn,
+        name="phase_" + "w" * len(w_halves) + "_" + str(attn),
     )(*args)
 
 
@@ -310,30 +332,38 @@
     )(*[pltpu.with_memory_space_constraint(x, pltpu.VMEM) for x in (*arrays, done)])
 
 
-def halve_kernel(ahead_ref, behind_ref, left_ref, right_ref, sems):
-    half = left_ref.shape[1]
-    copies = [
-        pltpu.make_async_copy(ahead_ref.at[:, pl.ds(0, half)], left_ref, sems.at[0]),
-        pltpu.make_async_copy(behind_ref.at[:, pl.ds(half, half)], right_ref, sems.at[1]),
-    ]
-    for copy in copies:
-        copy.start()
+def split_kernel(plan, first_ref, second_ref, *refs):
+    outs, sems = refs[:-1], refs[-1]
+    rows, half = first_ref.shape[0], outs[0].shape[1]
+    copies = []
+    for which, c, out, row in plan:
+        source = (first_ref, second_ref)[which].at[:, pl.ds(c * half, half)]
+        target = outs[out].at[pl.ds(row * rows, rows)]
+        copies.append(pltpu.make_async_copy(source, target, sems.at[len(copies)]))
+        copies[-1].start()
     for copy in copies:
         copy.wait()
 
 
-def halved(ahead, behind):
+def split(first, second, join):
     vmem = pl.BlockSpec(memory_space=pltpu.VMEM)
-    rows, features = ahead.shape
-    return pl.pallas_call(
-        halve_kernel,
+    rows, features = first.shape
+    if join:
+        plan = [(0, 0, 0, 0), (1, 1, 1, 0)]
+        plan += [(which, c, 2 + c, which) for c in range(2) for which in range(2)]
+        heights = [rows, rows, 2 * rows, 2 * rows]
+    else:
+        plan = [(which, c, 2 * which + c, 0) for which in range(2) for c in range(2)]
+        heights = [rows] * 4
+    return pl.pallas_call(
+        functools.partial(split_kernel, plan),
         in_specs=[vmem] * 2,
-        out_specs=[vmem] * 2,
-        out_shape=[pltpu.VMEM((rows, features // 2), ahead.dtype)] * 2,
-        scratch_shapes=[pltpu.SemaphoreType.DMA((2,))],
+        out_specs=[vmem] * 4,
+        out_shape=[pltpu.VMEM((h, features // 2), first.dtype) for h in heights],
+        scratch_shapes=[pltpu.SemaphoreType.DMA((len(plan),))],
         compiler_params=pltpu.CompilerParams(vmem_limit_bytes=MIB),
-        name="halved",
-    )(*[pltpu.with_memory_space_constraint(x, pltpu.VMEM) for x in (ahead, behind)])
+        name="split",
+    )(*[pltpu.with_memory_space_constraint(x, pltpu.VMEM) for x in (first, second)])
 
 
 def exchange(x, devices, stride, radix):
@@ -351,13 +381,11 @@
     rows, features = out_grad.shape
     slots = attn_out.shape[0]
     devices, last = ring.devices, ring.length // 2
-    offsets = [0] + [s * k for k in range(1, last) for s in (-1, 1)] + [last]
-    counts = [2] + [4] * (last - 1) + [2]
-    table = jnp.asarray(ring.owners(offsets))
+    offsets = [[0]] + [[-k, k] for k in range(1, last)] + [[last]]
+    counts = [2] + [4] * (last - 1) + [1, 1]
     me = lax.axis_index("dp").astype(jnp.int32).reshape(1)
-    where = (table, me, head_counts)
-    own = live_rows(seq_counts, me, out_grad)
-    ats = prepared(*where, attn_out, counts, rows)
+    where = (jnp.asarray(ring.owners(offsets)), me, head_counts)
+    shapes = (slots, o_weight.shape[0], features, rows)
     weight = o_weight
 
     def swap(x):
@@ -369,29 +397,64 @@
     def backward(x):
         return lax.ppermute(x, "dp", ring.shift(-1))
 
-    arrived = [[own, swap(own)]]
-    ahead, behind = forward(own), backward(own)
-    w, out, begin = None, None, 0
-    for k in range(last):
-        w, out, done = phase(where, begin, ats[k], weight, arrived, w, out, slots)
+    own = live_rows(seq_counts, me, out_grad)
+    ahead, behind, other = forward(own), backward(own), swap(own)
+    ats = prepared(*where, attn_out, counts, rows)
+    w, out, done = phase(
+        where, shapes, 0, [(0, [(own, 0, rows), (other, 0, rows)])],
+        at=ats[0], w_halves=(0,), weight=weight, attn="whole",
+    )
+    begin = counts[0]
+    for k in range(1, last):
+        (ahead,), (behind,) = after(done, ahead), after(done, behind)
+        if k < last - 1:
+            next_ahead, next_behind = forward(ahead), backward(behind)
+        pieces = split(ahead, behind, k == last - 1)
+        groups = []
+        if k == last - 1:
+            next_ahead, next_behind = forward(pieces[0]), backward(pieces[1])
+            for c in range(2):
+                near = pieces[2 + c]
+                groups.append((c, [(x, 0, 2 * rows) for x in (near, swap(near))]))
+        else:
+            for c in range(2):
+                near = [pieces[c], pieces[2 + c]]
+                far = [swap(x) for x in near]
+                groups.append((c, [(x, 0, rows) for x in near + far]))
+        w, done = phase(
+            where, shapes, begin, groups[:1], at=ats[k], w=w, w_halves=(0,)
+        )
+        w, out, done = phase(
+            where, shapes, begin, groups, at=ats[k], w=w, w_halves=(1,),
+            weight=weight, attn="whole", out=out,
+        )
         begin += counts[k]
-        ahead, behind = after(done, ahead, behind)
-        if k < last - 1:
-            arrived = [[ahead, swap(ahead), behind, swap(behind)]]
-            if k + 2 == last:
-                ahead, behind = halved(ahead, behind)
-            ahead, behind = forward(ahead), backward(behind)
-        else:
-            arrived = [[ahead, swap(ahead)], [behind, swap(behind)]]
-    w, squares = phase(where, begin, ats[last], None, arrived, w, None, slots, True)
+        ahead, behind = next_ahead, next_behind
+
+    both = after(done, ahead, behind)
+    other = [swap(x) for x in both]
+    mine = [(c, [(both[c], 0, rows)]) for c in range(2)]
+    theirs = [(c, [(other[c], 0, rows)]) for c in range(2)]
+    w, done = phase(where, shapes, begin, mine, at=ats[last], w=w, w_halves=(0, 1))
+    w, squares = phase(
+        where, shapes, begin, theirs, at=ats[last + 1], w=w, w_halves=(0, 1), squares=True
+    )
 
     stride, late = 1, 0
     while stride < devices:
         radix = min(4, devices // stride)
         squares = exchange(squares, devices, stride, radix)
-        if late < 2:
-            gs = [group[late : late + 1] for group in arrived]
-            out, done = phase(where, begin + late, None, weight, gs, None, out, slots)
+        pieces = [(x[late], 0, rows) for x in (both, other)] if late < 2 else []
+        if late == 0:
+            before, done = phase(
+                where, shapes, begin, [(late, pieces)], weight=weight, attn="first"
+            )
+            (squares,) = after(done, squares)
+        elif late == 1:
+            out, done = phase(
+                where, shapes, begin, [(late, pieces)], weight=weight, attn="last",
+                before=before, out=out,
+            )
         stride, late = stride * radix, late + 1
     return out, scaled(w, squares)
 

time: 138 us -> 133 us (0.964)
  Pallas kernels: 67.2 us -> 64.2 us
  waiting for transfers between devices: 48.5 us -> 46.6 us
    ppermute x4, waiting for transfers between devices: 4.78 us -> 36.3 us  [backward(): return lax.ppermute(x, 'dp', ring.shift(-1))]
    ppermute x4, waiting for transfers between devices: 35.6 us -> 4.66 us  [forward(): return lax.ppermute(x, 'dp', ring.shift(1))]
    ppermute x4, starting transfers between devices: 1.43 us -> 7.4 us  [backward(): return lax.ppermute(x, 'dp', ring.shift(-1))]
    ppermute x4, starting transfers between devices: 7.38 us -> 1.52 us  [forward(): return lax.ppermute(x, 'dp', ring.shift(1))]
    ppermute x9 -> x13, waiting for transfers between devices: 8.17 us -> 3.31 us  [swap(): return lax.ppermute(x, 'dp', ring.swap())]
    pallas_call x8 -> x14, Pallas kernels: 59.5 us -> 56.4 us  [the longest x11 55.7 us: phase(): pl.pallas_call(functools.partial(phase_kernel, spec), in_specs=specs, out...]
    ppermute x6, waiting for transfers between devices: 0.02 us -> 2.31 us  [exchange(): total = total + lax.ppermute(x, 'dp', pairs)]
  transfers between devices with their start and end apart: 23 -> 27, of which waited for: 15 -> 13; matrix products, arithmetic and copies ran while one was open for 0% -> 0% of each run, Pallas kernels for 42% -> 42%
where the time goes in v5:
time: 133 us
  Pallas kernels  64.2 us (48%)
  waiting for transfers between devices  46.6 us (35%)
  starting transfers between devices  17.2 us (13%)
  local copies, waits for them, and re-layouts  2.8 us (2%)
  between operations  2.34 us (2%)
    pallas_call x11, Pallas kernels, phase(): pl.pallas_call(functools.partial(phase_kernel, spec), in_specs=specs, out...  55.7 us
    ppermute x4, waiting for transfers between devices, backward(): return lax.ppermute(x, 'dp', ring.shift(-1))  36.3 us
    ppermute x4, starting transfers between devices, backward(): return lax.ppermute(x, 'dp', ring.shift(-1))  7.4 us
    ppermute x6, starting transfers between devices, exchange(): total = total + lax.ppermute(x, 'dp', pairs)  5.49 us
    ppermute x4, waiting for transfers between devices, forward(): return lax.ppermute(x, 'dp', ring.shift(1))  4.66 us
    pallas_call x1, Pallas kernels, prepared(): pl.pallas_call(functools.partial(prep_kernel, counts, rows), in_specs=[sm...  3.49 us
    ppermute x13, waiting for transfers between devices, swap(): return lax.ppermute(x, 'dp', ring.swap())  3.31 us
    pallas_call x1, Pallas kernels, scaled(): pl.pallas_call(functools.partial(scale_kernel, parts), in_specs=[vmem, vm...  3 us
  transfers between devices with their start and end apart: 27, of which 13 were waited for; matrix products, arithmetic and copies ran while one was open for 0% of the time, Pallas kernels for 42%

profile of v5, /device:TPU:0, one launch (start us, length us, event | category | flops | bytes accessed | tf_op | source)
XLA Modules:
  0.0 133.1 jit_solution(10284294040279983902)
XLA Ops:
  1.3 0.0 copy-start.1
  1.3 1.3 live.1.refs_5_
  2.6 0.5 collective-permute-start.1
  3.1 2.6 %collective-permute-start.3 = (bf16[144,4096]{1,0:T(8,128)(2,1)S(1)}, bf16[144,4096]{1,0:T(8,128)(2,1)S(1)}, u32[]{:S(2)}, u32[]{:S(2)}) collective-permute-start(bf16[144,4096]{1,0:T(8,128)(2,1)S(1)} %live.1.refs_5_), channel_id=1, source_target_pairs={{0,2},{1,3},{4,0},{5,1},{8,4},{9,5},{12,8},{13,9},{14,12},{15,13},... | collective-permute-start | bytes 3538952 | tf_op jit(solution)/shard_map/ppermute | solution.py:398
  5.7 0.2 collective-permute-start
  6.5 3.5 %prep.1 = (bf16[768,288]{1,0:T(8,128)(2,1)S(1)}, bf16[768,576]{1,0:T(8,128)(2,1)S(1)}, bf16[768,576]{1,0:T(8,128)(2,1)S(1)}, bf16[768,576]{1,0:T(8,128)(2,1)S(1)...) custom-call(s32[16,16]{1,0:T(8,128)S(1)} %copy-done.1, s32[1]{0:T(128)} %bitcast.me_ref.refs_1_, ...), custom_call_target="tpu_custom_call" | custom-call | bytes 7077888 | tf_op jit(solution)/shard_map/prep/pallas_call | solution.py:111
  10.0 0.0 collective-permute-done.1.refs_6_
  10.0 0.0 copy-start
  10.0 2.8 %copy-done = bf16[768,4096]{1,0:T(8,128)(2,1)S(1)} copy-done((bf16[768,4096]{1,0:T(8,128)(2,1)S(1)}, bf16[768,4096]{1,0:T(8,128)(2,1)}, u32[]{:S(2)}) %copy-start) | copy-done | bytes 6291480
  12.8 7.3 %phase_w_whole.4 = (f32[768,4096]{1,0:T(8,128)S(1)}, bf16[2304,768]{1,0:T(8,128)(2,1)}, f32[8,128]{1,0:T(8,128)S(1)}) custom-call(s32[16,16]{1,0:T(8,128)S(1)} %copy-done.1, s32[1]{0:T(128)} %bitcast.me_ref.refs_1_, s32[1]{0:T(128)S(6)} %copy.50.heads_ref.refs_2_, bf16[768,288]{1,0:T(8,128)(2,1)S(1)} %get-tuple-element.43.refs_3_, ...), custom_call_target="tpu_custom_call" | custom-call | flops 1 | bytes 1 | tf_op jit(solution)/shard_map/phase_w_whole/pallas_call | solution.py:263
  20.1 12.3 %collective-permute-done.3.refs_0_ = bf16[144,4096]{1,0:T(8,128)(2,1)S(1)} collective-permute-done((bf16[144,4096]{1,0:T(8,128)(2,1)S(1)}, bf16[144,4096]{1,0:T(8,128)(2,1)S(1)}, u32[]{:S(2)}, u32[]{:S(2)}) %collective-permute-start.3) | collective-permute-done | bytes 1179680 | tf_op jit(solution)/shard_map/ppermute | solution.py:398
  32.3 1.4 %collective-permute-done.refs_0_ = bf16[144,4096]{1,0:T(8,128)(2,1)S(1)} collective-permute-done((bf16[144,4096]{1,0:T(8,128)(2,1)S(1)}, bf16[144,4096]{1,0:T(8,128)(2,1)S(1)}, u32[]{:S(2)}, u32[]{:S(2)}) %collective-permute-start) | collective-permute-done | bytes 1179680 | tf_op jit(solution)/shard_map/ppermute | solution.py:395
  33.7 0.2 split.3
  33.9 0.1 collective-permute-start.4
  34.0 1.6 %collective-permute-start.9 = (bf16[144,4096]{1,0:T(8,128)(2,1)S(1)}, bf16[144,4096]{1,0:T(8,128)(2,1)S(1)}, u32[]{:S(2)}, u32[]{:S(2)}) collective-permute-start(bf16[144,4096]{1,0:T(8,128)(2,1)S(1)} %after.9.second_ref), channel_id=1, source_target_pairs={{0,2},{1,3},{4,0},{5,1},{8,4},{9,5},{12,8},{13,9},{14,12},{15,13},... | collective-permute-start | bytes 3538952 | tf_op jit(solution)/shard_map/ppermute | solution.py:398
  35.6 0.4 collective-permute-start.2
  36.1 0.0 collective-permute-start.5
  36.1 0.5 collective-permute-start.6
  36.6 0.0 collective-permute-done.4.refs_6_.refs_7_
  36.6 0.0 collective-permute-start.7
  36.6 1.5 %collective-permute-done.5.refs_7_.refs_8_ = bf16[144,2048]{1,0:T(8,128)(2,1)S(1)} collective-permute-done((bf16[144,2048]{1,0:T(8,128)(2,1)S(1)}, bf16[144,2048]{1,0:T(8,128)(2,1)S(1)}, u32[]{:S(2)}, u32[]{:S(2)}) %collective-permute-start.5) | collective-permute-done | bytes 589856 | tf_op jit(solution)/shard_map/ppermute | solution.py:392
  38.1 3.5 %phase_w_None.3 = (f32[768,4096]{1,0:T(8,128)S(1)}, f32[8,128]{1,0:T(8,128)}) custom-call(s32[16,16]{1,0:T(8,128)S(1)} %copy-done.1, s32[1]{0:T(128)} %bitcast.me_ref.refs_1_, s32[1]{0:T(128)S(6)} %copy.50.heads_ref.refs_2_, bf16[768,576]{1,0:T(8,128)(2,1)S(1)} %get-tuple-element.45.refs_3_, ...), custom_call_target="tpu_custom_call", output_to_operand_aliasing={{0}: (8, {})} | custom-call | flops 1 | bytes 1 | tf_op jit(solution)/shard_map/phase_w_None/pallas_call | solution.py:263
  41.6 0.0 collective-permute-done.6.refs_11_
  41.6 0.0 collective-permute-done.7.refs_12_
  41.7 8.8 %phase_w_whole.5 = (f32[768,4096]{1,0:T(8,128)S(1)}, bf16[2304,768]{1,0:T(8,128)(2,1)}, f32[8,128]{1,0:T(8,128)S(1)}) custom-call(s32[16,16]{1,0:T(8,128)S(1)} %copy-done.1, s32[1]{0:T(128)} %bitcast.me_ref.refs_1_, s32[1]{0:T(128)S(6)} %copy.50.heads_ref.refs_2_, ...), custom_call_target="tpu_custom_call", output_to_operand_aliasing={{0}: (13, {}), {1}: (14, {})} | custom-call | flops 1 | bytes 1 | tf_op jit(solution)/shard_map/phase_w_whole/pallas_call | solution.py:263
  50.4 11.9 %collective-permute-done.9.refs_0_ = bf16[144,4096]{1,0:T(8,128)(2,1)S(1)} collective-permute-done((bf16[144,4096]{1,0:T(8,128)(2,1)S(1)}, bf16[144,4096]{1,0:T(8,128)(2,1)S(1)}, u32[]{:S(2)}, u32[]{:S(2)}) %collective-permute-start.9) | collective-permute-done | bytes 1179680 | tf_op jit(solution)/shard_map/ppermute | solution.py:398
  62.4 1.3 collective-permute-done.2.refs_0_
  63.7 0.2 split.4
  63.9 0.1 collective-permute-start.10
  64.0 1.6 %collective-permute-start.14 = (bf16[144,4096]{1,0:T(8,128)(2,1)S(1)}, bf16[144,4096]{1,0:T(8,128)(2,1)S(1)}, u32[]{:S(2)}, u32[]{:S(2)}) collective-permute-start(bf16[144,4096]{1,0:T(8,128)(2,1)S(1)} %after.11.second_ref), channel_id=1, source_target_pairs={{0,2},{1,3},{4,0},{5,1},{8,4},{9,5},{12,8},{13,9},{14,12},{15,13},... | collective-permute-start | bytes 3538952 | tf_op jit(solution)/shard_map/ppermute | solution.py:398
  65.6 0.5 collective-permute-start.8
  66.1 0.5 collective-permute-start.12
  66.6 0.0 collective-permute-done.10.refs_6_.refs_7_
  66.6 0.0 collective-permute-start.13
  66.6 1.5 %collective-permute-done.11.refs_7_.refs_8_ = bf16[144,2048]{1,0:T(8,128)(2,1)S(1)} collective-permute-done((bf16[144,2048]{1,0:T(8,128)(2,1)S(1)}, bf16[144,2048]{1,0:T(8,128)(2,1)S(1)}, u32[]{:S(2)}, u32[]{:S(2)}) %collective-permute-start.11) | collective-permute-done | bytes 589856 | tf_op jit(solution)/shard_map/ppermute | solution.py:392
  68.1 3.5 %phase_w_None.4 = (f32[768,4096]{1,0:T(8,128)S(1)}, f32[8,128]{1,0:T(8,128)}) custom-call(s32[16,16]{1,0:T(8,128)S(1)} %copy-done.1, s32[1]{0:T(128)} %bitcast.me_ref.refs_1_, s32[1]{0:T(128)S(6)} %copy.50.heads_ref.refs_2_, bf16[768,576]{1,0:T(8,128)(2,1)S(1)} %get-tuple-element.54.refs_3_, ...), custom_call_target="tpu_custom_call", output_to_operand_aliasing={{0}: (8, {})} | custom-call | flops 1 | bytes 1 | tf_op jit(solution)/shard_map/phase_w_None/pallas_call | solution.py:263
  71.6 8.8 %phase_w_whole.6 = (f32[768,4096]{1,0:T(8,128)S(1)}, bf16[2304,768]{1,0:T(8,128)(2,1)}, f32[8,128]{1,0:T(8,128)S(1)}) custom-call(s32[16,16]{1,0:T(8,128)S(1)} %copy-done.1, s32[1]{0:T(128)} %bitcast.me_ref.refs_1_, s32[1]{0:T(128)S(6)} %copy.50.heads_ref.refs_2_, ...), custom_call_target="tpu_custom_call", output_to_operand_aliasing={{0}: (13, {}), {1}: (14, {})} | custom-call | flops 1 | bytes 1 | tf_op jit(solution)/shard_map/phase_w_whole/pallas_call | solution.py:263
  80.4 11.9 %collective-permute-done.14.refs_0_ = bf16[144,4096]{1,0:T(8,128)(2,1)S(1)} collective-permute-done((bf16[144,4096]{1,0:T(8,128)(2,1)S(1)}, bf16[144,4096]{1,0:T(8,128)(2,1)S(1)}, u32[]{:S(2)}, u32[]{:S(2)}) %collective-permute-start.14) | collective-permute-done | bytes 1179680 | tf_op jit(solution)/shard_map/ppermute | solution.py:398
  92.3 1.3 collective-permute-done.8.refs_0_
  93.6 0.3 split.5
  93.9 0.1 collective-permute-start.17
  94.0 0.5 collective-permute-start.18
  94.5 0.5 collective-permute-start.15
  95.0 1.6 %collective-permute-start.16 = (bf16[144,2048]{1,0:T(8,128)(2,1)S(1)}, bf16[144,2048]{1,0:T(8,128)(2,1)S(1)}, u32[]{:S(2)}, u32[]{:S(2)}) collective-permute-start(bf16[144,2048]{1,0:T(8,128)(2,1)S(1)} %get-tuple-element.64), channel_id=1, source_target_pairs={{0,2},{1,3},{4,0},{5,1},{8,4},{9,5},{12,8},{13,9},{14,12},{15,13},... | collective-permute-start | bytes 1769480 | tf_op jit(solution)/shard_map/ppermute | solution.py:398
  96.5 0.3 collective-permute-done.17.refs_5_.refs_6_
  96.9 3.5 %phase_w_None.5 = (f32[768,4096]{1,0:T(8,128)S(1)}, f32[8,128]{1,0:T(8,128)}) custom-call(s32[16,16]{1,0:T(8,128)S(1)} %copy-done.1, s32[1]{0:T(128)} %bitcast.me_ref.refs_1_, s32[1]{0:T(128)S(6)} %copy.50.heads_ref.refs_2_, bf16[768,576]{1,0:T(8,128)(2,1)S(1)} %get-tuple-element.65.refs_3_, ...), custom_call_target="tpu_custom_call", output_to_operand_aliasing={{0}: (6, {})} | custom-call | flops 1 | bytes 1 | tf_op jit(solution)/shard_map/phase_w_None/pallas_call | solution.py:263
  100.4 8.8 %phase_w_whole.7 = (f32[768,4096]{1,0:T(8,128)S(1)}, bf16[2304,768]{1,0:T(8,128)(2,1)}, f32[8,128]{1,0:T(8,128)S(1)}) custom-call(s32[16,16]{1,0:T(8,128)S(1)} %copy-done.1, s32[1]{0:T(128)} %bitcast.me_ref.refs_1_, s32[1]{0:T(128)S(6)} %copy.50.heads_ref.refs_2_, ...), custom_call_target="tpu_custom_call", output_to_operand_aliasing={{0}: (9, {}), {1}: (10, {})} | custom-call | flops 1 | bytes 1 | tf_op jit(solution)/shard_map/phase_w_whole/pallas_call | solution.py:263
  109.1 0.7 collective-permute-done.15.refs_0_
  109.8 0.2 collective-permute-done.16.refs_1_
  110.0 0.5 collective-permute-start.20
  110.5 3.0 %phase_ww_None.2 = (f32[768,4096]{1,0:T(8,128)S(1)}, f32[8,128]{1,0:T(8,128)}) custom-call(s32[16,16]{1,0:T(8,128)S(1)} %copy-done.1, s32[1]{0:T(128)} %bitcast.me_ref.refs_1_, s32[1]{0:T(128)S(6)} %copy.50.heads_ref.refs_2_, bf16[768,144]{1,0:T(8,128)(2,1)S(1)} %get-tuple-element.78.refs_3_, ...), custom_call_target="tpu_custom_call", output_to_operand_aliasing={{0}: (6, {})} | custom-call | flops 1 | bytes 1 | tf_op jit(solution)/shard_map/phase_ww_None/pallas_call | solution.py:263
  113.5 0.0 slice-start
  113.6 3.0 %phase_ww_None.3 = (f32[768,4096]{1,0:T(8,128)S(1)}, f32[8,128]{1,0:T(8,128)S(1)}) custom-call(s32[16,16]{1,0:T(8,128)S(1)} %copy-done.1, s32[1]{0:T(128)} %bitcast.me_ref.refs_1_, s32[1]{0:T(128)S(6)} %copy.50.heads_ref.refs_2_, bf16[768,144]{1,0:T(8,128)(2,1)S(1)} %get-tuple-element.77.refs_3_, ...), custom_call_target="tpu_custom_call", output_to_operand_aliasing={{0}: (6, {})} | custom-call | flops 1 | bytes 1 | tf_op jit(solution)/shard_map/phase_ww_None/pallas_call | solution.py:263
  116.6 1.2 collective-permute-start.23
  117.8 0.5 collective-permute-start.22
  118.3 0.2 collective-permute-start.21
  118.4 2.0 %phase__first.1 = (f32[288,768]{1,0:T(8,128)S(1)}, f32[8,128]{1,0:T(8,128)S(1)}) custom-call(s32[16,16]{1,0:T(8,128)S(1)} %copy-done.1, s32[1]{0:T(128)} %bitcast.me_ref.refs_1_, s32[1]{0:T(128)S(6)} %copy.50.heads_ref.refs_2_, bf16[768,4096]{1,0:T(8,128)(2,1)S(1)} %bitcast.2, bf16[144,2048]{1,0:T(8,128)(2,1)S(1)} %get-tuple-element.73.refs_4_, ...), custom_call_target="tpu_custom_call" | custom-call | flops 1 | bytes 1 | tf_op jit(solution)/shard_map/phase__first/pallas_call | solution.py:263
  120.5 0.9 collective-permute-done.22
  121.4 1.5 %collective-permute-start.26 = (f32[8,128]{1,0:T(8,128)S(1)}, f32[8,128]{1,0:T(8,128)S(1)}, u32[]{:S(2)}, u32[]{:S(2)}) collective-permute-start(f32[8,128]{1,0:T(8,128)S(1)} %after.15), channel_id=1, source_target_pairs={{0,12},{1,13},{2,14},{3,15},{4,0},{5,1},{6,2},{7,3},{8,4},{9,5},{1... | collective-permute-start | bytes 12296 | tf_op jit(solution)/shard_map/ppermute | solution.py:376
  122.9 1.6 %collective-permute-start.25 = (f32[8,128]{1,0:T(8,128)S(1)}, f32[8,128]{1,0:T(8,128)S(1)}, u32[]{:S(2)}, u32[]{:S(2)}) collective-permute-start(f32[8,128]{1,0:T(8,128)S(1)} %after.15), channel_id=1, source_target_pairs={{0,8},{1,9},{2,10},{3,11},{4,12},{5,13},{6,14},{7,15},{8,0},{9,1},... | collective-permute-start | bytes 12296 | tf_op jit(solution)/shard_map/ppermute | solution.py:376
  124.5 0.5 collective-permute-start.24
  125.0 3.5 %phase__last.1 = (bf16[2304,768]{1,0:T(8,128)(2,1)}, f32[8,128]{1,0:T(8,128)}) custom-call(s32[16,16]{1,0:T(8,128)S(1)} %copy-done.1, s32[1]{0:T(128)} %bitcast.me_ref.refs_1_, s32[1]{0:T(128)S(6)} %copy.50.heads_ref.refs_2_, bf16[768,4096]{1,0:T(8,128)(2,1)S(1)} %bitcast.2, ...), custom_call_target="tpu_custom_call", output_to_operand_aliasing={{0}: (7, {})} | custom-call | flops 1 | bytes 1 | tf_op jit(solution)/shard_map/phase__last/pallas_call | solution.py:263
  128.5 1.4 %collective-permute-done.24 = f32[8,128]{1,0:T(8,128)S(1)} collective-permute-done((f32[8,128]{1,0:T(8,128)S(1)}, f32[8,128]{1,0:T(8,128)S(1)}, u32[]{:S(2)}, u32[]{:S(2)}) %collective-permute-start.24) | collective-permute-done | bytes 4128 | tf_op jit(solution)/shard_map/ppermute | solution.py:376
  129.9 3.0 %scale.1 = bf16[768,4096]{1,0:T(8,128)(2,1)} custom-call(f32[768,4096]{1,0:T(8,128)S(1)} %get-tuple-element.81.w_ref, f32[8,128]{1,0:T(8,128)S(1)} %add_add_fusion.squares_ref), custom_call_target="tpu_custom_call" | custom-call | flops 3145728 | bytes 6291456 | tf_op jit(solution)/shard_map/scale/pallas_call | solution.py:303
  (26 shorter events, 0.1 us)
Async XLA Ops:
  1.3 5.2 %copy-start.1 = (s32[16,16]{1,0:T(8,128)S(1)}, s32[16,16]{1,0:T(8,128)}, u32[]{:S(2)}) copy-start(s32[16,16]{1,0:T(8,128)} %constant.6.clone.table_ref.refs_0_) | copy-start | bytes 3076
  2.6 7.4 %collective-permute-start.1 = (bf16[144,4096]{1,0:T(8,128)(2,1)S(1)}, bf16[144,4096]{1,0:T(8,128)(2,1)S(1)}, u32[]{:S(2)}, u32[]{:S(2)}) collective-permute-start(bf16[144,4096]{1,0:T(8,128)(2,1)S(1)} %live.1.refs_5_), channel_id=1, source_target_pairs={{0,1},{1,0},{2,3},{3,2},{4,5},{5,4},{6,7},{7,6},{8,9},{9,8},{10,11... | collective-permute-start | bytes 3538952 | tf_op jit(solution)/shard_map/ppermute | solution.py:392
  3.1 29.2 %collective-permute-start.3 = (bf16[144,4096]{1,0:T(8,128)(2,1)S(1)}, bf16[144,4096]{1,0:T(8,128)(2,1)S(1)}, u32[]{:S(2)}, u32[]{:S(2)}) collective-permute-start(bf16[144,4096]{1,0:T(8,128)(2,1)S(1)} %live.1.refs_5_), channel_id=1, source_target_pairs={{0,2},{1,3},{4,0},{5,1},{8,4},{9,5},{12,8},{13,9},{14,12},{15,13},... | collective-permute-start | bytes 3538952 | tf_op jit(solution)/shard_map/ppermute | solution.py:398
  5.7 28.0 %collective-permute-start = (bf16[144,4096]{1,0:T(8,128)(2,1)S(1)}, bf16[144,4096]{1,0:T(8,128)(2,1)S(1)}, u32[]{:S(2)}, u32[]{:S(2)}) collective-permute-start(bf16[144,4096]{1,0:T(8,128)(2,1)S(1)} %live.1.refs_5_), channel_id=1, source_target_pairs={{0,4},{1,5},{4,8},{5,9},{8,12},{9,13},{12,14},{13,15},{14,10},{15,... | collective-permute-start | bytes 3538952 | tf_op jit(solution)/shard_map/ppermute | solution.py:395
  10.0 2.8 %copy-start = (bf16[768,4096]{1,0:T(8,128)(2,1)S(1)}, bf16[768,4096]{1,0:T(8,128)(2,1)}, u32[]{:S(2)}) copy-start(bf16[768,4096]{1,0:T(8,128)(2,1)} %refs_3_.3) | copy-start | bytes 18874372
  33.9 2.7 %collective-permute-start.4 = (bf16[144,2048]{1,0:T(8,128)(2,1)S(1)}, bf16[144,2048]{1,0:T(8,128)(2,1)S(1)}, u32[]{:S(2)}, u32[]{:S(2)}) collective-permute-start(bf16[144,2048]{1,0:T(8,128)(2,1)S(1)} %get-tuple-element.46.refs_4_.refs_5_), channel_id=1, source_target_pairs={{0,1},{1,0},{2,3},{3,2},{4,5},{5,4},{6,7},{7,6},{8,9},{9,8},{10,11... | collective-permute-start | bytes 1769480 | tf_op jit(solution)/shard_map/ppermute | solution.py:392
  34.0 28.4 %collective-permute-start.9 = (bf16[144,4096]{1,0:T(8,128)(2,1)S(1)}, bf16[144,4096]{1,0:T(8,128)(2,1)S(1)}, u32[]{:S(2)}, u32[]{:S(2)}) collective-permute-start(bf16[144,4096]{1,0:T(8,128)(2,1)S(1)} %after.9.second_ref), channel_id=1, source_target_pairs={{0,2},{1,3},{4,0},{5,1},{8,4},{9,5},{12,8},{13,9},{14,12},{15,13},... | collective-permute-start | bytes 3538952 | tf_op jit(solution)/shard_map/ppermute | solution.py:398
  35.6 28.0 %collective-permute-start.2 = (bf16[144,4096]{1,0:T(8,128)(2,1)S(1)}, bf16[144,4096]{1,0:T(8,128)(2,1)S(1)}, u32[]{:S(2)}, u32[]{:S(2)}) collective-permute-start(bf16[144,4096]{1,0:T(8,128)(2,1)S(1)} %after.8.first_ref), channel_id=1, source_target_pairs={{0,4},{1,5},{4,8},{5,9},{8,12},{9,13},{12,14},{13,15},{14,10},{15,... | collective-permute-start | bytes 3538952 | tf_op jit(solution)/shard_map/ppermute | solution.py:395
  36.1 2.0 %collective-permute-start.5 = (bf16[144,2048]{1,0:T(8,128)(2,1)S(1)}, bf16[144,2048]{1,0:T(8,128)(2,1)S(1)}, u32[]{:S(2)}, u32[]{:S(2)}) collective-permute-start(bf16[144,2048]{1,0:T(8,128)(2,1)S(1)} %get-tuple-element.47.refs_5_.refs_6_), channel_id=1, source_target_pairs={{0,1},{1,0},{2,3},{3,2},{4,5},{5,4},{6,7},{7,6},{8,9},{9,8},{10,11... | collective-permute-start | bytes 1769480 | tf_op jit(solution)/shard_map/ppermute | solution.py:392
  36.1 5.5 %collective-permute-start.6 = (bf16[144,2048]{1,0:T(8,128)(2,1)S(1)}, bf16[144,2048]{1,0:T(8,128)(2,1)S(1)}, u32[]{:S(2)}, u32[]{:S(2)}) collective-permute-start(bf16[144,2048]{1,0:T(8,128)(2,1)S(1)} %get-tuple-element.48.refs_9_), channel_id=1, source_target_pairs={{0,1},{1,0},{2,3},{3,2},{4,5},{5,4},{6,7},{7,6},{8,9},{9,8},{10,11... | collective-permute-start | bytes 1769480 | tf_op jit(solution)/shard_map/ppermute | solution.py:392
  36.6 5.0 %collective-permute-start.7 = (bf16[144,2048]{1,0:T(8,128)(2,1)S(1)}, bf16[144,2048]{1,0:T(8,128)(2,1)S(1)}, u32[]{:S(2)}, u32[]{:S(2)}) collective-permute-start(bf16[144,2048]{1,0:T(8,128)(2,1)S(1)} %get-tuple-element.49.refs_10_), channel_id=1, source_target_pairs={{0,1},{1,0},{2,3},{3,2},{4,5},{5,4},{6,7},{7,6},{8,9},{9,8},{10,11... | collective-permute-start | bytes 1769480 | tf_op jit(solution)/shard_map/ppermute | solution.py:392
  63.9 2.7 %collective-permute-start.10 = (bf16[144,2048]{1,0:T(8,128)(2,1)S(1)}, bf16[144,2048]{1,0:T(8,128)(2,1)S(1)}, u32[]{:S(2)}, u32[]{:S(2)}) collective-permute-start(bf16[144,2048]{1,0:T(8,128)(2,1)S(1)} %get-tuple-element.55.refs_4_.refs_5_), channel_id=1, source_target_pairs={{0,1},{1,0},{2,3},{3,2},{4,5},{5,4},{6,7},{7,6},{8,9},{9,8},{10,11... | collective-permute-start | bytes 1769480 | tf_op jit(solution)/shard_map/ppermute | solution.py:392
  64.0 28.4 %collective-permute-start.14 = (bf16[144,4096]{1,0:T(8,128)(2,1)S(1)}, bf16[144,4096]{1,0:T(8,128)(2,1)S(1)}, u32[]{:S(2)}, u32[]{:S(2)}) collective-permute-start(bf16[144,4096]{1,0:T(8,128)(2,1)S(1)} %after.11.second_ref), channel_id=1, source_target_pairs={{0,2},{1,3},{4,0},{5,1},{8,4},{9,5},{12,8},{13,9},{14,12},{15,13},... | collective-permute-start | bytes 3538952 | tf_op jit(solution)/shard_map/ppermute | solution.py:398
  65.6 28.0 %collective-permute-start.8 = (bf16[144,4096]{1,0:T(8,128)(2,1)S(1)}, bf16[144,4096]{1,0:T(8,128)(2,1)S(1)}, u32[]{:S(2)}, u32[]{:S(2)}) collective-permute-start(bf16[144,4096]{1,0:T(8,128)(2,1)S(1)} %after.10.first_ref), channel_id=1, source_target_pairs={{0,4},{1,5},{4,8},{5,9},{8,12},{9,13},{12,14},{13,15},{14,10},{15,... | collective-permute-start | bytes 3538952 | tf_op jit(solution)/shard_map/ppermute | solution.py:395
  66.1 2.0 %collective-permute-start.11 = (bf16[144,2048]{1,0:T(8,128)(2,1)S(1)}, bf16[144,2048]{1,0:T(8,128)(2,1)S(1)}, u32[]{:S(2)}, u32[]{:S(2)}) collective-permute-start(bf16[144,2048]{1,0:T(8,128)(2,1)S(1)} %get-tuple-element.56.refs_5_.refs_6_), channel_id=1, source_target_pairs={{0,1},{1,0},{2,3},{3,2},{4,5},{5,4},{6,7},{7,6},{8,9},{9,8},{10,11... | collective-permute-start | bytes 1769480 | tf_op jit(solution)/shard_map/ppermute | solution.py:392
  66.1 5.5 %collective-permute-start.12 = (bf16[144,2048]{1,0:T(8,128)(2,1)S(1)}, bf16[144,2048]{1,0:T(8,128)(2,1)S(1)}, u32[]{:S(2)}, u32[]{:S(2)}) collective-permute-start(bf16[144,2048]{1,0:T(8,128)(2,1)S(1)} %get-tuple-element.57.refs_9_), channel_id=1, source_target_pairs={{0,1},{1,0},{2,3},{3,2},{4,5},{5,4},{6,7},{7,6},{8,9},{9,8},{10,11... | collective-permute-start | bytes 1769480 | tf_op jit(solution)/shard_map/ppermute | solution.py:392
  66.6 5.0 %collective-permute-start.13 = (bf16[144,2048]{1,0:T(8,128)(2,1)S(1)}, bf16[144,2048]{1,0:T(8,128)(2,1)S(1)}, u32[]{:S(2)}, u32[]{:S(2)}) collective-permute-start(bf16[144,2048]{1,0:T(8,128)(2,1)S(1)} %get-tuple-element.58.refs_10_), channel_id=1, source_target_pairs={{0,1},{1,0},{2,3},{3,2},{4,5},{5,4},{6,7},{7,6},{8,9},{9,8},{10,11... | collective-permute-start | bytes 1769480 | tf_op jit(solution)/shard_map/ppermute | solution.py:392
  93.9 2.9 %collective-permute-start.17 = (bf16[288,2048]{1,0:T(8,128)(2,1)S(1)}, bf16[288,2048]{1,0:T(8,128)(2,1)S(1)}, u32[]{:S(2)}, u32[]{:S(2)}) collective-permute-start(bf16[288,2048]{1,0:T(8,128)(2,1)S(1)} %get-tuple-element.66.refs_4_.refs_5_), channel_id=1, source_target_pairs={{0,1},{1,0},{2,3},{3,2},{4,5},{5,4},{6,7},{7,6},{8,9},{9,8},{10,11... | collective-permute-start | bytes 3538952 | tf_op jit(solution)/shard_map/ppermute | solution.py:392
  94.0 6.3 %collective-permute-start.18 = (bf16[288,2048]{1,0:T(8,128)(2,1)S(1)}, bf16[288,2048]{1,0:T(8,128)(2,1)S(1)}, u32[]{:S(2)}, u32[]{:S(2)}) collective-permute-start(bf16[288,2048]{1,0:T(8,128)(2,1)S(1)} %get-tuple-element.67.refs_7_), channel_id=1, source_target_pairs={{0,1},{1,0},{2,3},{3,2},{4,5},{5,4},{6,7},{7,6},{8,9},{9,8},{10,11... | collective-permute-start | bytes 3538952 | tf_op jit(solution)/shard_map/ppermute | solution.py:392
  94.5 15.3 %collective-permute-start.15 = (bf16[144,2048]{1,0:T(8,128)(2,1)S(1)}, bf16[144,2048]{1,0:T(8,128)(2,1)S(1)}, u32[]{:S(2)}, u32[]{:S(2)}) collective-permute-start(bf16[144,2048]{1,0:T(8,128)(2,1)S(1)} %get-tuple-element.63), channel_id=1, source_target_pairs={{0,4},{1,5},{4,8},{5,9},{8,12},{9,13},{12,14},{13,15},{14,10},{15,... | collective-permute-start | bytes 1769480 | tf_op jit(solution)/shard_map/ppermute | solution.py:395
  95.0 15.0 %collective-permute-start.16 = (bf16[144,2048]{1,0:T(8,128)(2,1)S(1)}, bf16[144,2048]{1,0:T(8,128)(2,1)S(1)}, u32[]{:S(2)}, u32[]{:S(2)}) collective-permute-start(bf16[144,2048]{1,0:T(8,128)(2,1)S(1)} %get-tuple-element.64), channel_id=1, source_target_pairs={{0,2},{1,3},{4,0},{5,1},{8,4},{9,5},{12,8},{13,9},{14,12},{15,13},... | collective-permute-start | bytes 1769480 | tf_op jit(solution)/shard_map/ppermute | solution.py:398
  110.0 3.5 %collective-permute-start.19 = (bf16[144,2048]{1,0:T(8,128)(2,1)S(1)}, bf16[144,2048]{1,0:T(8,128)(2,1)S(1)}, u32[]{:S(2)}, u32[]{:S(2)}) collective-permute-start(bf16[144,2048]{1,0:T(8,128)(2,1)S(1)} %get-tuple-element.72.refs_4_.refs_5_), channel_id=1, source_target_pairs={{0,1},{1,0},{2,3},{3,2},{4,5},{5,4},{6,7},{7,6},{8,9},{9,8},{10,11... | collective-permute-start | bytes 1769480 | tf_op jit(solution)/shard_map/ppermute | solution.py:392
  110.0 3.5 %collective-permute-start.20 = (bf16[144,2048]{1,0:T(8,128)(2,1)S(1)}, bf16[144,2048]{1,0:T(8,128)(2,1)S(1)}, u32[]{:S(2)}, u32[]{:S(2)}) collective-permute-start(bf16[144,2048]{1,0:T(8,128)(2,1)S(1)} %get-tuple-element.73.refs_4_), channel_id=1, source_target_pairs={{0,1},{1,0},{2,3},{3,2},{4,5},{5,4},{6,7},{7,6},{8,9},{9,8},{10,11... | collective-permute-start | bytes 1769480 | tf_op jit(solution)/shard_map/ppermute | solution.py:392
  113.5 4.9 %slice-start = ((s8[6291456]{0:T(1024)(128)(4,1)}), s8[4194304]{0:T(1024)(128)(4,1)S(1)}, s32[]{:S(2)}) async-start(s8[6291456]{0:T(1024)(128)(4,1)} %bitcast.1), calls=%async_computation | async-start | bytes 8388608
  113.5 4.9 %slice-start.1 = ((s8[6291456]{0:T(1024)(128)(4,1)}), s8[2097152]{0:T(1024)(128)(4,1)S(1)}, s32[]{:S(2)}) async-start(s8[6291456]{0:T(1024)(128)(4,1)} %bitcast.1), calls=%async_computation.1 | async-start | bytes 4194304
  116.6 3.9 %collective-permute-start.23 = (f32[8,128]{1,0:T(8,128)S(1)}, f32[8,128]{1,0:T(8,128)S(1)}, u32[]{:S(2)}, u32[]{:S(2)}) collective-permute-start(f32[8,128]{1,0:T(8,128)S(1)} %get-tuple-element.82), channel_id=1, source_target_pairs={{0,3},{1,0},{2,1},{3,2},{4,7},{5,4},{6,5},{7,6},{8,11},{9,8},{10,9... | collective-permute-start | bytes 12296 | tf_op jit(solution)/shard_map/ppermute | solution.py:376
  117.8 3.6 %collective-permute-start.22 = (f32[8,128]{1,0:T(8,128)S(1)}, f32[8,128]{1,0:T(8,128)S(1)}, u32[]{:S(2)}, u32[]{:S(2)}) collective-permute-start(f32[8,128]{1,0:T(8,128)S(1)} %get-tuple-element.82), channel_id=1, source_target_pairs={{0,2},{1,3},{2,0},{3,1},{4,6},{5,7},{6,4},{7,5},{8,10},{9,11},{10,... | collective-permute-start | bytes 12296 | tf_op jit(solution)/shard_map/ppermute | solution.py:376
  118.3 3.1 %collective-permute-start.21 = (f32[8,128]{1,0:T(8,128)S(1)}, f32[8,128]{1,0:T(8,128)S(1)}, u32[]{:S(2)}, u32[]{:S(2)}) collective-permute-start(f32[8,128]{1,0:T(8,128)S(1)} %get-tuple-element.82), channel_id=1, source_target_pairs={{0,1},{1,2},{2,3},{3,0},{4,5},{5,6},{6,7},{7,4},{8,9},{9,10},{10,1... | collective-permute-start | bytes 12296 | tf_op jit(solution)/shard_map/ppermute | solution.py:376
  121.4 7.1 %collective-permute-start.26 = (f32[8,128]{1,0:T(8,128)S(1)}, f32[8,128]{1,0:T(8,128)S(1)}, u32[]{:S(2)}, u32[]{:S(2)}) collective-permute-start(f32[8,128]{1,0:T(8,128)S(1)} %after.15), channel_id=1, source_target_pairs={{0,12},{1,13},{2,14},{3,15},{4,0},{5,1},{6,2},{7,3},{8,4},{9,5},{1... | collective-permute-start | bytes 12296 | tf_op jit(solution)/shard_map/ppermute | solution.py:376
  122.9 5.6 %collective-permute-start.25 = (f32[8,128]{1,0:T(8,128)S(1)}, f32[8,128]{1,0:T(8,128)S(1)}, u32[]{:S(2)}, u32[]{:S(2)}) collective-permute-start(f32[8,128]{1,0:T(8,128)S(1)} %after.15), channel_id=1, source_target_pairs={{0,8},{1,9},{2,10},{3,11},{4,12},{5,13},{6,14},{7,15},{8,0},{9,1},... | collective-permute-start | bytes 12296 | tf_op jit(solution)/shard_map/ppermute | solution.py:376
  124.5 5.4 %collective-permute-start.24 = (f32[8,128]{1,0:T(8,128)S(1)}, f32[8,128]{1,0:T(8,128)S(1)}, u32[]{:S(2)}, u32[]{:S(2)}) collective-permute-start(f32[8,128]{1,0:T(8,128)S(1)} %after.15), channel_id=1, source_target_pairs={{0,4},{1,5},{2,6},{3,7},{4,8},{5,9},{6,10},{7,11},{8,12},{9,13},{1... | collective-permute-start | bytes 12296 | tf_op jit(solution)/shard_map/ppermute | solution.py:376

commit v6 on v5

--- a/solution.py
+++ b/solution.py
@@ -11,7 +11,8 @@
 HEADS = 64
 HEAD_DIM = 128
 SEQ = 16
-TILE = 1024
+TILE = 512
+CHUNKS = (1024, 1536, 1536)
 MIB = 1024 * 1024
 
 
@@ -33,6 +34,13 @@
     def shift(self, step):
         return [
             (self.device(p, core), self.device(p + step, core))
+            for p in range(self.length)
+            for core in range(2)
+        ]
+
+    def across(self):
+        return [
+            (self.device(p, core), self.device(p + 1 - 2 * core, core))
             for p in range(self.length)
             for core in range(2)
         ]
@@ -80,64 +88,84 @@
     )(seq_counts, me, pltpu.with_memory_space_constraint(out_grad, pltpu.HBM))
 
 
-def prep_kernel(counts, rows, table_ref, me_ref, heads_ref, a_ref, *refs):
-    at_refs, (block_ref, sems) = refs[: len(counts)], refs[len(counts) :]
-    width = heads_ref[0] * HEAD_DIM
-    copies = []
-    for i in range(sum(counts)):
-        owner = table_ref[me_ref[0], i]
-        copies.append(
-            pltpu.make_async_copy(
-                a_ref.at[pl.ds(pl.multiple_of(owner * rows, rows), rows)],
-                block_ref.at[pl.ds(i * rows, rows)],
-                sems.at[i],
+def prep_kernel(core, counts, rows, table_ref, me_ref, heads_ref, own_ref, a_ref, *refs):
+    n = len(counts)
+    refs = refs[1:] if core else refs[n:]
+    at_refs, (block_ref, sems) = refs[-n - 2 : -2], refs[-2:]
+    if not core:
+        half = refs[0].shape[1]
+        copies = [
+            pltpu.make_async_copy(own_ref.at[:, pl.ds(i * half, half)], refs[i], sems.at[i])
+            for i in range(2)
+        ]
+        for copy in copies:
+            copy.start()
+        for copy in copies:
+            copy.wait()
+
+    @pl.when(me_ref[0] % 2 == core)
+    def _():
+        width = heads_ref[0] * HEAD_DIM
+        copies = []
+        for i in range(sum(counts)):
+            owner = table_ref[me_ref[0], i]
+            copies.append(
+                pltpu.make_async_copy(
+                    a_ref.at[pl.ds(pl.multiple_of(owner * rows, rows), rows)],
+                    block_ref.at[pl.ds(i * rows, rows)],
+                    sems.at[i],
+                )
             )
-        )
-        copies[-1].start()
-    begin = 0
-    for at_ref, count in zip(at_refs, counts):
-        for copy in copies[begin : begin + count]:
-            copy.wait()
-        block = block_ref[begin * rows : (begin + count) * rows, :]
-        column = lax.broadcasted_iota(jnp.int32, block.shape, 1)
-        at_ref[...] = jnp.where(column < width, block, jnp.zeros_like(block)).T
-        begin += count
-
-
-def prepared(table, me, head_counts, attn_out, counts, rows):
+            copies[-1].start()
+        begin = 0
+        for at_ref, count in zip(at_refs, counts):
+            for copy in copies[begin : begin + count]:
+                copy.wait()
+            block = block_ref[begin * rows : (begin + count) * rows, :]
+            column = lax.broadcasted_iota(jnp.int32, block.shape, 1)
+            at_ref[...] = jnp.where(column < width, block, jnp.zeros_like(block)).T
+            begin += count
+
+
+def prepared(core, where, own, attn_out, counts, ats=()):
     slots, capacity = attn_out.shape
+    rows, features = own.shape
     vmem = pl.BlockSpec(memory_space=pltpu.VMEM)
     smem = pl.BlockSpec(memory_space=pltpu.SMEM)
-    return pl.pallas_call(
-        functools.partial(prep_kernel, counts, rows),
-        in_specs=[smem, smem, smem, pl.BlockSpec(memory_space=pl.ANY)],
-        out_specs=[vmem] * len(counts),
-        out_shape=[pltpu.VMEM((capacity, count * rows), jnp.bfloat16) for count in counts],
+    owns = [own.shape] if core else [(rows, features // 2)] * 2
+    outs = [pltpu.VMEM(shape, own.dtype) for shape in owns]
+    outs += [pltpu.VMEM((capacity, count * rows), jnp.bfloat16) for count in counts]
+    own, *ats = [pltpu.with_memory_space_constraint(x, pltpu.VMEM) for x in (own, *ats)]
+    results = pl.pallas_call(
+        functools.partial(prep_kernel, core, counts, rows),
+        in_specs=[smem] * 3 + [vmem, pl.BlockSpec(memory_space=pl.ANY)] + [vmem] * len(ats),
+        out_specs=[vmem] * len(outs),
+        out_shape=outs,
         scratch_shapes=[
             pltpu.VMEM((slots, capacity), jnp.bfloat16),
             pltpu.SemaphoreType.DMA((sum(counts),)),
         ],
+        input_output_aliases={3: 0} if core else {5 + i: 2 + i for i in range(len(ats))},
         compiler_params=pltpu.CompilerParams(vmem_limit_bytes=12 * MIB),
-        cost_estimate=pl.CostEstimate(
-            flops=0, bytes_accessed=4 * slots * capacity, transcendentals=0
-        ),
+        cost_estimate=pl.CostEstimate(flops=1, bytes_accessed=1, transcendentals=0),
         name="prep",
-    )(table, me, head_counts, pltpu.with_memory_space_constraint(attn_out, pltpu.HBM))
+    )(*where, own, pltpu.with_memory_space_constraint(attn_out, pltpu.HBM), *ats)
+    return results[: len(owns)], results[len(owns) :]
 
 
 def phase_kernel(spec, *refs):
-    groups, arrays, w_halves, attn, fresh_w, fresh_out, squares, rows, begin = spec
+    groups, arrays, do_w, attn, fresh_w, fresh_out, squares, rows, begin = spec
     refs = list(refs)
     table_ref, me_ref, heads_ref = refs.pop(0), refs.pop(0), refs.pop(0)
-    at_ref = refs.pop(0) if w_halves else None
+    at_ref = refs.pop(0) if do_w else None
     weight_ref = refs.pop(0) if attn else None
     g_refs = [refs.pop(0) for _ in range(arrays)]
-    if w_halves and not fresh_w:
+    if do_w and not fresh_w:
         refs.pop(0)
     before_ref = refs.pop(0) if attn == "last" else None
     if attn in ("whole", "last") and not fresh_out:
         refs.pop(0)
-    w_ref = refs.pop(0) if w_halves else None
+    w_ref = refs.pop(0) if do_w else None
     total_ref = refs.pop(0) if attn == "first" else None
     out_ref = refs.pop(0) if attn in ("whole", "last") else None
     squares_ref = refs.pop(0)
@@ -149,12 +177,12 @@
         total_ref[...] = jnp.zeros_like(total_ref)
     squares_ref[...] = jnp.zeros_like(squares_ref)
 
-    def body(half, span, pieces, j, carry):
-        here = pl.ds(pl.multiple_of(j * TILE, TILE), TILE)
-        there = pl.ds(pl.multiple_of(half * span + j * TILE, TILE), TILE)
+    def body(first, column, pieces, j, carry):
+        here = pl.ds(pl.multiple_of(column + j * TILE, TILE), TILE)
+        there = pl.ds(pl.multiple_of(first + j * TILE, TILE), TILE)
         g = [g_refs[i][start : start + count, here] for i, start, count in pieces]
         g = jnp.concatenate(g, axis=0) if len(g) > 1 else g[0]
-        if half in w_halves:
+        if do_w:
             w = jnp.dot(at_ref[...], g, preferred_element_type=jnp.float32)
             if not fresh_w:
                 w = w + w_ref[:, there]
@@ -174,8 +202,9 @@
             )
         return carry
 
-    for half, span, pieces in groups:
-        lax.fori_loop(0, span // TILE, functools.partial(body, half, span, pieces), 0)
+    for first, width, column, pieces in groups:
+        step = functools.partial(body, first, column, pieces)
+        lax.fori_loop(0, width // TILE, step, 0)
     if attn in ("whole", "last"):
         total = total_ref[...]
         column = lax.broadcasted_iota(jnp.int32, total.shape, 1)
@@ -197,20 +226,21 @@
 
 
 def phase(
-    where, shapes, begin, groups, at=None, w=None, w_halves=(),
+    where, shapes, begin, groups, at=None, w=None,
     weight=None, attn=None, before=None, out=None, squares=False,
 ):
     slots, capacity, features, rows = shapes
+    do_w = at is not None
     arrays, described = [], []
-    for half, pieces in groups:
+    for first, width, column, pieces in groups:
         placed = []
         for array, start, count in pieces:
             known = [i for i, x in enumerate(arrays) if x is array]
             if not known:
                 arrays.append(array)
             placed.append((known[0] if known else len(arrays) - 1, start, count))
-        described.append((half, pieces[0][0].shape[1], tuple(placed)))
-    height = sum(count for _, _, count in groups[0][1])
+        described.append((first, width, column, tuple(placed)))
+    height = sum(count for _, _, count in groups[0][3])
     vmem = pl.BlockSpec(memory_space=pltpu.VMEM)
     smem = pl.BlockSpec(memory_space=pltpu.SMEM)
     hbm = pl.BlockSpec(memory_space=pl.ANY)
@@ -226,13 +256,13 @@
 
     for scalar in where:
         add(scalar, smem)
-    if w_halves:
+    if do_w:
         add_vmem(at)
     if attn:
         add_vmem(weight)
     for array in arrays:
         add_vmem(array)
-    if w_halves:
+    if do_w:
         if w is not None:
             aliases[len(args)] = len(outs)
             add_vmem(w)
@@ -257,7 +287,7 @@
     outs.append(pltpu.VMEM((8, 128), jnp.float32))
     out_specs.append(vmem)
     spec = (
-        tuple(described), len(arrays), tuple(w_halves), attn, w is None, out is None,
+        tuple(described), len(arrays), do_w, attn, w is None, out is None,
         squares, rows, begin,
     )
     return pl.pallas_call(
@@ -273,7 +303,7 @@
             bytes_accessed=1,
             transcendentals=0,
         ),
-        name="phase_" + "w" * len(w_halves) + "_" + str(attn),
+        name="phase_" + "w" * do_w + "_" + str(attn),
     )(*args)
 
 
@@ -332,35 +362,55 @@
     )(*[pltpu.with_memory_space_constraint(x, pltpu.VMEM) for x in (*arrays, done)])
 
 
-def split_kernel(plan, first_ref, second_ref, *refs):
+def choose_kernel(me_ref, first_ref, second_ref, done_ref, out_ref, sem):
+    for core, ref in enumerate((first_ref, second_ref)):
+
+        @pl.when(me_ref[0] % 2 == core)
+        def _():
+            copy = pltpu.make_async_copy(ref, out_ref, sem)
+            copy.start()
+            copy.wait()
+
+
+def chosen(me, done, first, second):
+    vmem = pl.BlockSpec(memory_space=pltpu.VMEM)
+    arrays = (first, second, done)
+    return pl.pallas_call(
+        choose_kernel,
+        in_specs=[pl.BlockSpec(memory_space=pltpu.SMEM)] + [vmem] * 3,
+        out_specs=vmem,
+        out_shape=pltpu.VMEM(first.shape, first.dtype),
+        scratch_shapes=[pltpu.SemaphoreType.DMA],
+        compiler_params=pltpu.CompilerParams(vmem_limit_bytes=MIB),
+        name="chosen",
+    )(me, *[pltpu.with_memory_space_constraint(x, pltpu.VMEM) for x in arrays])
+
+
+def split_kernel(first_ref, second_ref, *refs):
     outs, sems = refs[:-1], refs[-1]
-    rows, half = first_ref.shape[0], outs[0].shape[1]
-    copies = []
-    for which, c, out, row in plan:
-        source = (first_ref, second_ref)[which].at[:, pl.ds(c * half, half)]
-        target = outs[out].at[pl.ds(row * rows, rows)]
-        copies.append(pltpu.make_async_copy(source, target, sems.at[len(copies)]))
-        copies[-1].start()
+    rows = first_ref.shape[0]
+    copies, column = [], 0
+    for out in outs:
+        width = out.shape[1]
+        for i, ref in enumerate((first_ref, second_ref)):
+            source = ref.at[:, pl.ds(column, width)]
+            target = out.at[pl.ds(i * rows, rows)]
+            copies.append(pltpu.make_async_copy(source, target, sems.at[len(copies)]))
+            copies[-1].start()
+        column += width
     for copy in copies:
         copy.wait()
 
 
-def split(first, second, join):
+def split(first, second):
     vmem = pl.BlockSpec(memory_space=pltpu.VMEM)
-    rows, features = first.shape
-    if join:
-        plan = [(0, 0, 0, 0), (1, 1, 1, 0)]
-        plan += [(which, c, 2 + c, which) for c in range(2) for which in range(2)]
-        heights = [rows, rows, 2 * rows, 2 * rows]
-    else:
-        plan = [(which, c, 2 * which + c, 0) for which in range(2) for c in range(2)]
-        heights = [rows] * 4
+    rows = first.shape[0]
     return pl.pallas_call(
-        functools.partial(split_kernel, plan),
+        split_kernel,
         in_specs=[vmem] * 2,
-        out_specs=[vmem] * 4,
-        out_shape=[pltpu.VMEM((h, features // 2), first.dtype) for h in heights],
-        scratch_shapes=[pltpu.SemaphoreType.DMA((len(plan),))],
+        out_specs=[vmem] * len(CHUNKS),
+        out_shape=[pltpu.VMEM((2 * rows, width), first.dtype) for width in CHUNKS],
+        scratch_shapes=[pltpu.SemaphoreType.DMA((2 * len(CHUNKS),))],
         compiler_params=pltpu.CompilerParams(vmem_limit_bytes=MIB),
         name="split",
     )(*[pltpu.with_memory_space_constraint(x, pltpu.VMEM) for x in (first, second)])
@@ -388,71 +438,62 @@
     shapes = (slots, o_weight.shape[0], features, rows)
     weight = o_weight
 
-    def swap(x):
-        return lax.ppermute(x, "dp", ring.swap())
-
-    def forward(x):
-        return lax.ppermute(x, "dp", ring.shift(1))
-
-    def backward(x):
-        return lax.ppermute(x, "dp", ring.shift(-1))
+    def send(x, pairs):
+        return lax.ppermute(x, "dp", pairs)
 
     own = live_rows(seq_counts, me, out_grad)
-    ahead, behind, other = forward(own), backward(own), swap(own)
-    ats = prepared(*where, attn_out, counts, rows)
+    (own,), ats = prepared(1, where, own, attn_out, counts)
+    ahead, behind = send(own, ring.shift(1)), send(own, ring.shift(-1))
+    owns, ats = prepared(0, where, own, attn_out, counts, ats)
+    half, groups = features // 2, []
+    for c, near in enumerate(owns):
+        pieces = [(near, 0, rows), (send(near, ring.swap()), 0, rows)]
+        groups.append((c * half, half, 0, pieces))
     w, out, done = phase(
-        where, shapes, 0, [(0, [(own, 0, rows), (other, 0, rows)])],
-        at=ats[0], w_halves=(0,), weight=weight, attn="whole",
+        where, shapes, 0, groups, at=ats[0], weight=weight, attn="whole"
     )
     begin = counts[0]
     for k in range(1, last):
-        (ahead,), (behind,) = after(done, ahead), after(done, behind)
         if k < last - 1:
-            next_ahead, next_behind = forward(ahead), backward(behind)
-        pieces = split(ahead, behind, k == last - 1)
-        groups = []
-        if k == last - 1:
-            next_ahead, next_behind = forward(pieces[0]), backward(pieces[1])
-            for c in range(2):
-                near = pieces[2 + c]
-                groups.append((c, [(x, 0, 2 * rows) for x in (near, swap(near))]))
+            ahead, behind = after(done, ahead, behind)
+            following = send(ahead, ring.shift(1)), send(behind, ring.shift(-1))
         else:
-            for c in range(2):
-                near = [pieces[c], pieces[2 + c]]
-                far = [swap(x) for x in near]
-                groups.append((c, [(x, 0, rows) for x in near + far]))
-        w, done = phase(
-            where, shapes, begin, groups[:1], at=ats[k], w=w, w_halves=(0,)
-        )
+            following = send(chosen(me, done, ahead, behind), ring.across())
+        groups, first = [], 0
+        for near in split(ahead, behind):
+            far = send(near, ring.swap())
+            pieces = [(near, 0, 2 * rows), (far, 0, 2 * rows)]
+            groups.append((first, near.shape[1], 0, pieces))
+            first += near.shape[1]
         w, out, done = phase(
-            where, shapes, begin, groups, at=ats[k], w=w, w_halves=(1,),
+            where, shapes, begin, groups, at=ats[k], w=w,
             weight=weight, attn="whole", out=out,
         )
         begin += counts[k]
-        ahead, behind = next_ahead, next_behind
-
-    both = after(done, ahead, behind)
-    other = [swap(x) for x in both]
-    mine = [(c, [(both[c], 0, rows)]) for c in range(2)]
-    theirs = [(c, [(other[c], 0, rows)]) for c in range(2)]
-    w, done = phase(where, shapes, begin, mine, at=ats[last], w=w, w_halves=(0, 1))
+        if k < last - 1:
+            ahead, behind = following
+
+    (near,) = after(done, following)
+    far = send(near, ring.swap())
+    w, done = phase(
+        where, shapes, begin, [(0, features, 0, [(near, 0, rows)])], at=ats[last], w=w
+    )
     w, squares = phase(
-        where, shapes, begin, theirs, at=ats[last + 1], w=w, w_halves=(0, 1), squares=True
+        where, shapes, begin, [(0, features, 0, [(far, 0, rows)])], at=ats[last + 1], w=w,
+        squares=True,
     )
 
     stride, late = 1, 0
     while stride < devices:
         radix = min(4, devices // stride)
         squares = exchange(squares, devices, stride, radix)
-        pieces = [(x[late], 0, rows) for x in (both, other)] if late < 2 else []
+        groups = [(late * half, half, late * half, [(x, 0, rows) for x in (near, far)])]
         if late == 0:
-            before, done = phase(
-                where, shapes, begin, [(late, pieces)], weight=weight, attn="first"
-            )
+            before, done = phase(where, shapes, begin, groups, weight=weight, attn="first")
             (squares,) = after(done, squares)
         elif late == 1:
             out, done = phase(
-                where, shapes, begin, [(late, pieces)], weight=weight, attn="last",
+                where, shapes, begin, groups, weight=weight, attn="last",
                 before=before, out=out,
             )
         stride, late = stride * radix, late + 1

time: 133 us -> 136 us (1.023)
  Pallas kernels: 64.2 us -> 68.1 us
  local copies, waits for them, and re-layouts: 2.8 us -> 0.02 us
  waiting for transfers between devices: 46.6 us -> 48.9 us
    ppermute x21 -> x19, waiting for transfers between devices: 44.3 us -> 47.3 us  [send(): return lax.ppermute(x, 'dp', pairs)]
    unnamed x8 -> x6, local copies, waits for them, and re-layouts: 2.8 us -> 0.02 us
    pallas_call x11 -> x8, Pallas kernels: 55.7 us -> 58.3 us  [phase(): pl.pallas_call(functools.partial(phase_kernel, spec), in_specs=specs, out...]
    pallas_call x4 -> x6, Pallas kernels: 4.19 us -> 5.46 us  [the longest x2 4.41 us: prepared(): pl.pallas_call(functools.partial(prep_kernel, core, counts, rows), in_spe...]
    ppermute x21 -> x19, starting transfers between devices: 11.7 us -> 12.3 us  [send(): return lax.ppermute(x, 'dp', pairs)]
  transfers between devices with their start and end apart: 27 -> 25, of which waited for: 13 -> 13; matrix products, arithmetic and copies ran while one was open for 0% -> 0% of each run, Pallas kernels for 42% -> 43%
where the time goes in v6:
time: 136 us
  Pallas kernels  68.1 us (50%)
  waiting for transfers between devices  48.9 us (36%)
  starting transfers between devices  16.7 us (12%)
  between operations  2.32 us (2%)
    pallas_call x8, Pallas kernels, phase(): pl.pallas_call(functools.partial(phase_kernel, spec), in_specs=specs, out...  58.3 us
    ppermute x19, waiting for transfers between devices, send(): return lax.ppermute(x, 'dp', pairs)  47.3 us
    ppermute x19, starting transfers between devices, send(): return lax.ppermute(x, 'dp', pairs)  12.3 us
    pallas_call x2, Pallas kernels, prepared(): pl.pallas_call(functools.partial(prep_kernel, core, counts, rows), in_spe...  4.41 us
    ppermute x6, starting transfers between devices, exchange(): total = total + lax.ppermute(x, 'dp', pairs)  4.37 us
    pallas_call x1, Pallas kernels, scaled(): pl.pallas_call(functools.partial(scale_kernel, parts), in_specs=[vmem, vm...  3 us
  transfers between devices with their start and end apart: 25, of which 13 were waited for; matrix products, arithmetic and copies ran while one was open for 0% of the time, Pallas kernels for 43%

profile of v6, /device:TPU:0, one launch (start us, length us, event | category | flops | bytes accessed | tf_op | source)
XLA Modules:
  0.0 136.0 jit_solution(17342872769825982655)
XLA Ops:
  1.9 0.0 copy-start
  1.9 1.3 live.1.own_ref
  3.3 0.0 slice-start
  3.3 0.8 prep.2
  4.1 3.1 %collective-permute-start = (bf16[144,4096]{1,0:T(8,128)(2,1)S(1)}, bf16[144,4096]{1,0:T(8,128)(2,1)S(1)}, u32[]{:S(2)}, u32[]{:S(2)}) collective-permute-start(bf16[144,4096]{1,0:T(8,128)(2,1)S(1)} %get-tuple-element.48.own_ref), channel_id=1, source_target_pairs={{0,4},{1,5},{4,8},{5,9},{8,12},{9,13},{12,14},{13,15},{14,10},{15,... | collective-permute-start | bytes 3538952 | tf_op jit(solution)/shard_map/ppermute | solution.py:442
  7.2 0.0 collective-permute-start.1
  7.2 3.6 %prep.3 = (bf16[144,2048]{1,0:T(8,128)(2,1)S(1)}, bf16[144,2048]{1,0:T(8,128)(2,1)S(1)}, bf16[768,288]{1,0:T(8,128)(2,1)S(1)}, bf16[768,576]{1,0:T(8,128)(2,1)S(...) custom-call(s32[16,16]{1,0:T(8,128)S(1)} %copy-done, ...), custom_call_target="tpu_custom_call", output_to_operand_aliasing={{2}: (5, {}), {3}: (6, {}), {4}: (7, {}), {5}: (8, {}), {6}... | custom-call | flops 1 | bytes 1 | tf_op jit(solution)/shard_map/prep/pallas_call | solution.py:139
  10.8 0.1 collective-permute-start.2
  10.8 0.5 collective-permute-start.3
  11.3 1.5 %collective-permute-done.2.refs_6_ = bf16[144,2048]{1,0:T(8,128)(2,1)S(1)} collective-permute-done((bf16[144,2048]{1,0:T(8,128)(2,1)S(1)}, bf16[144,2048]{1,0:T(8,128)(2,1)S(1)}, u32[]{:S(2)}, u32[]{:S(2)}) %collective-permute-start.2) | collective-permute-done | bytes 589856 | tf_op jit(solution)/shard_map/ppermute | solution.py:442
  12.8 0.8 collective-permute-done.3.refs_8_
  13.7 7.8 %phase_w_whole.4 = (f32[768,4096]{1,0:T(8,128)S(1)}, bf16[2304,768]{1,0:T(8,128)(2,1)}, f32[8,128]{1,0:T(8,128)S(1)}) custom-call(s32[16,16]{1,0:T(8,128)S(1)} %copy-done, s32[1]{0:T(128)} %bitcast.me_ref.refs_1_, s32[1]{0:T(128)S(6)} %copy.52.heads_ref.refs_2_, bf16[768,288]{1,0:T(8,128)(2,1)S(1)} %get-tuple-element.55.refs_3_, ...), custom_call_target="tpu_custom_call" | custom-call | flops 1 | bytes 1 | tf_op jit(solution)/shard_map/phase_w_whole/pallas_call | solution.py:293
  21.5 10.2 %collective-permute-done.refs_0_ = bf16[144,4096]{1,0:T(8,128)(2,1)S(1)} collective-permute-done((bf16[144,4096]{1,0:T(8,128)(2,1)S(1)}, bf16[144,4096]{1,0:T(8,128)(2,1)S(1)}, u32[]{:S(2)}, u32[]{:S(2)}) %collective-permute-start) | collective-permute-done | bytes 1179680 | tf_op jit(solution)/shard_map/ppermute | solution.py:442
  31.7 2.7 %collective-permute-done.1.refs_1_ = bf16[144,4096]{1,0:T(8,128)(2,1)S(1)} collective-permute-done((bf16[144,4096]{1,0:T(8,128)(2,1)S(1)}, bf16[144,4096]{1,0:T(8,128)(2,1)S(1)}, u32[]{:S(2)}, u32[]{:S(2)}) %collective-permute-start.1) | collective-permute-done | bytes 1179680 | tf_op jit(solution)/shard_map/ppermute | solution.py:442
  34.4 1.5 %collective-permute-start.4 = (bf16[144,4096]{1,0:T(8,128)(2,1)S(1)}, bf16[144,4096]{1,0:T(8,128)(2,1)S(1)}, u32[]{:S(2)}, u32[]{:S(2)}) collective-permute-start(bf16[144,4096]{1,0:T(8,128)(2,1)S(1)} %get-tuple-element.59.first_ref), channel_id=1, source_target_pairs={{0,4},{1,5},{4,8},{5,9},{8,12},{9,13},{12,14},{13,15},{14,10},{15,... | collective-permute-start | bytes 3538952 | tf_op jit(solution)/shard_map/ppermute | solution.py:442
  35.9 0.5 collective-permute-start.5
  36.4 0.3 split.3
  36.7 1.0 collective-permute-start.7
  37.6 0.1 collective-permute-start.8
  37.7 0.4 collective-permute-start.6
  38.2 3.7 %collective-permute-done.6.refs_6_ = bf16[288,1024]{1,0:T(8,128)(2,1)S(1)} collective-permute-done((bf16[288,1024]{1,0:T(8,128)(2,1)S(1)}, bf16[288,1024]{1,0:T(8,128)(2,1)S(1)}, u32[]{:S(2)}, u32[]{:S(2)}) %collective-permute-start.6) | collective-permute-done | bytes 589856 | tf_op jit(solution)/shard_map/ppermute | solution.py:442
  41.8 0.0 collective-permute-done.7.refs_8_
  41.8 0.0 collective-permute-done.8.refs_10_
  41.8 12.3 %phase_w_whole.5 = (f32[768,4096]{1,0:T(8,128)S(1)}, bf16[2304,768]{1,0:T(8,128)(2,1)}, f32[8,128]{1,0:T(8,128)S(1)}) custom-call(s32[16,16]{1,0:T(8,128)S(1)} %copy-done, s32[1]{0:T(128)} %bitcast.me_ref.refs_1_, s32[1]{0:T(128)S(6)} %copy.52.heads_ref.refs_2_, ...), custom_call_target="tpu_custom_call", output_to_operand_aliasing={{0}: (11, {}), {1}: (12, {})} | custom-call | flops 1 | bytes 1 | tf_op jit(solution)/shard_map/phase_w_whole/pallas_call | solution.py:293
  54.1 8.7 %collective-permute-done.4.refs_0_ = bf16[144,4096]{1,0:T(8,128)(2,1)S(1)} collective-permute-done((bf16[144,4096]{1,0:T(8,128)(2,1)S(1)}, bf16[144,4096]{1,0:T(8,128)(2,1)S(1)}, u32[]{:S(2)}, u32[]{:S(2)}) %collective-permute-start.4) | collective-permute-done | bytes 1179680 | tf_op jit(solution)/shard_map/ppermute | solution.py:442
  62.8 1.7 %collective-permute-done.5.refs_1_ = bf16[144,4096]{1,0:T(8,128)(2,1)S(1)} collective-permute-done((bf16[144,4096]{1,0:T(8,128)(2,1)S(1)}, bf16[144,4096]{1,0:T(8,128)(2,1)S(1)}, u32[]{:S(2)}, u32[]{:S(2)}) %collective-permute-start.5) | collective-permute-done | bytes 1179680 | tf_op jit(solution)/shard_map/ppermute | solution.py:442
  64.5 1.6 %collective-permute-start.9 = (bf16[144,4096]{1,0:T(8,128)(2,1)S(1)}, bf16[144,4096]{1,0:T(8,128)(2,1)S(1)}, u32[]{:S(2)}, u32[]{:S(2)}) collective-permute-start(bf16[144,4096]{1,0:T(8,128)(2,1)S(1)} %get-tuple-element.68.first_ref), channel_id=1, source_target_pairs={{0,4},{1,5},{4,8},{5,9},{8,12},{9,13},{12,14},{13,15},{14,10},{15,... | collective-permute-start | bytes 3538952 | tf_op jit(solution)/shard_map/ppermute | solution.py:442
  66.1 0.4 collective-permute-start.10
  66.6 0.3 split.4
  66.8 0.1 collective-permute-start.12
  66.9 0.5 collective-permute-start.13
  67.4 0.1 collective-permute-start.11
  67.5 3.9 %collective-permute-done.11.refs_6_ = bf16[288,1024]{1,0:T(8,128)(2,1)S(1)} collective-permute-done((bf16[288,1024]{1,0:T(8,128)(2,1)S(1)}, bf16[288,1024]{1,0:T(8,128)(2,1)S(1)}, u32[]{:S(2)}, u32[]{:S(2)}) %collective-permute-start.11) | collective-permute-done | bytes 589856 | tf_op jit(solution)/shard_map/ppermute | solution.py:442
  71.4 0.0 collective-permute-done.12.refs_8_
  71.4 0.0 collective-permute-done.13.refs_10_
  71.4 12.3 %phase_w_whole.6 = (f32[768,4096]{1,0:T(8,128)S(1)}, bf16[2304,768]{1,0:T(8,128)(2,1)}, f32[8,128]{1,0:T(8,128)S(1)}) custom-call(s32[16,16]{1,0:T(8,128)S(1)} %copy-done, s32[1]{0:T(128)} %bitcast.me_ref.refs_1_, s32[1]{0:T(128)S(6)} %copy.52.heads_ref.refs_2_, ...), custom_call_target="tpu_custom_call", output_to_operand_aliasing={{0}: (11, {}), {1}: (12, {})} | custom-call | flops 1 | bytes 1 | tf_op jit(solution)/shard_map/phase_w_whole/pallas_call | solution.py:293
  83.7 8.8 %collective-permute-done.9.first_ref = bf16[144,4096]{1,0:T(8,128)(2,1)S(1)} collective-permute-done((bf16[144,4096]{1,0:T(8,128)(2,1)S(1)}, bf16[144,4096]{1,0:T(8,128)(2,1)S(1)}, u32[]{:S(2)}, u32[]{:S(2)}) %collective-permute-start.9) | collective-permute-done | bytes 1179680 | tf_op jit(solution)/shard_map/ppermute | solution.py:442
  92.5 1.3 collective-permute-done.10.second_ref
  93.8 0.3 chosen.1
  94.1 1.6 %collective-permute-start.14 = (bf16[144,4096]{1,0:T(8,128)(2,1)S(1)}, bf16[144,4096]{1,0:T(8,128)(2,1)S(1)}, u32[]{:S(2)}, u32[]{:S(2)}) collective-permute-start(bf16[144,4096]{1,0:T(8,128)(2,1)S(1)} %chosen.1), channel_id=1, source_target_pairs={{0,4},{1,3},{4,8},{5,1},{8,12},{9,5},{12,14},{13,9},{14,10},{15,13... | collective-permute-start | bytes 3538952 | tf_op jit(solution)/shard_map/ppermute | solution.py:442
  95.7 0.3 split.5
  96.0 0.1 collective-permute-start.16
  96.1 0.5 collective-permute-start.17
  96.6 0.1 collective-permute-start.15
  96.6 3.9 %collective-permute-done.15.refs_6_ = bf16[288,1024]{1,0:T(8,128)(2,1)S(1)} collective-permute-done((bf16[288,1024]{1,0:T(8,128)(2,1)S(1)}, bf16[288,1024]{1,0:T(8,128)(2,1)S(1)}, u32[]{:S(2)}, u32[]{:S(2)}) %collective-permute-start.15) | collective-permute-done | bytes 589856 | tf_op jit(solution)/shard_map/ppermute | solution.py:442
  100.6 0.0 collective-permute-done.16.refs_8_
  100.6 0.0 collective-permute-done.17.refs_10_
  100.6 12.3 %phase_w_whole.7 = (f32[768,4096]{1,0:T(8,128)S(1)}, bf16[2304,768]{1,0:T(8,128)(2,1)}, f32[8,128]{1,0:T(8,128)S(1)}) custom-call(s32[16,16]{1,0:T(8,128)S(1)} %copy-done, s32[1]{0:T(128)} %bitcast.me_ref.refs_1_, s32[1]{0:T(128)S(6)} %copy.52.heads_ref.refs_2_, ...), custom_call_target="tpu_custom_call", output_to_operand_aliasing={{0}: (11, {}), {1}: (12, {})} | custom-call | flops 1 | bytes 1 | tf_op jit(solution)/shard_map/phase_w_whole/pallas_call | solution.py:293
  112.9 0.0 collective-permute-done.14.refs_0_
  112.9 0.2 collective-permute-start.18
  113.1 3.8 %phase_w_None.2 = (f32[768,4096]{1,0:T(8,128)S(1)}, f32[8,128]{1,0:T(8,128)}) custom-call(s32[16,16]{1,0:T(8,128)S(1)} %copy-done, s32[1]{0:T(128)} %bitcast.me_ref.refs_1_, s32[1]{0:T(128)S(6)} %copy.52.heads_ref.refs_2_, bf16[768,144]{1,0:T(8,128)(2,1)S(1)} %get-tuple-element.88.refs_3_, ...), custom_call_target="tpu_custom_call", output_to_operand_aliasing={{0}: (5, {})} | custom-call | flops 1 | bytes 1 | tf_op jit(solution)/shard_map/phase_w_None/pallas_call | solution.py:293
  116.9 3.6 %phase_w_None.3 = (f32[768,4096]{1,0:T(8,128)S(1)}, f32[8,128]{1,0:T(8,128)S(1)}) custom-call(s32[16,16]{1,0:T(8,128)S(1)} %copy-done, s32[1]{0:T(128)} %bitcast.me_ref.refs_1_, s32[1]{0:T(128)S(6)} %copy.52.heads_ref.refs_2_, bf16[768,144]{1,0:T(8,128)(2,1)S(1)} %get-tuple-element.87.refs_3_, ...), custom_call_target="tpu_custom_call", output_to_operand_aliasing={{0}: (5, {})} | custom-call | flops 1 | bytes 1 | tf_op jit(solution)/shard_map/phase_w_None/pallas_call | solution.py:293
  120.5 0.5 collective-permute-start.21
  120.9 1.5 %collective-permute-start.20 = (f32[8,128]{1,0:T(8,128)S(1)}, f32[8,128]{1,0:T(8,128)S(1)}, u32[]{:S(2)}, u32[]{:S(2)}) collective-permute-start(f32[8,128]{1,0:T(8,128)S(1)} %get-tuple-element.92), channel_id=1, source_target_pairs={{0,2},{1,3},{2,0},{3,1},{4,6},{5,7},{6,4},{7,5},{8,10},{9,11},{10,... | collective-permute-start | bytes 12296 | tf_op jit(solution)/shard_map/ppermute | solution.py:426
  122.4 2.5 %phase__first.1 = (f32[288,768]{1,0:T(8,128)S(1)}, f32[8,128]{1,0:T(8,128)S(1)}) custom-call(s32[16,16]{1,0:T(8,128)S(1)} %copy-done, s32[1]{0:T(128)} %bitcast.me_ref.refs_1_, s32[1]{0:T(128)S(6)} %copy.52.heads_ref.refs_2_, bf16[768,4096]{1,0:T(8,128)(2,1)S(1)} %bitcast.2, bf16[144,4096]{1,0:T(8,128)(2,1)S(1)} %after.6.refs_4_, ...), custom_call_target="tpu_custom_call" | custom-call | flops 1 | bytes 1 | tf_op jit(solution)/shard_map/phase__first/pallas_call | solution.py:293
  125.0 0.5 collective-permute-done.19
  125.5 0.2 collective-permute-start.24
  125.7 1.7 %collective-permute-start.23 = (f32[8,128]{1,0:T(8,128)S(1)}, f32[8,128]{1,0:T(8,128)S(1)}, u32[]{:S(2)}, u32[]{:S(2)}) collective-permute-start(f32[8,128]{1,0:T(8,128)S(1)} %after.7), channel_id=1, source_target_pairs={{0,8},{1,9},{2,10},{3,11},{4,12},{5,13},{6,14},{7,15},{8,0},{9,1},... | collective-permute-start | bytes 12296 | tf_op jit(solution)/shard_map/ppermute | solution.py:426
  127.4 0.5 collective-permute-start.22
  127.9 3.9 %phase__last.1 = (bf16[2304,768]{1,0:T(8,128)(2,1)}, f32[8,128]{1,0:T(8,128)}) custom-call(s32[16,16]{1,0:T(8,128)S(1)} %copy-done, s32[1]{0:T(128)} %bitcast.me_ref.refs_1_, s32[1]{0:T(128)S(6)} %copy.52.heads_ref.refs_2_, bf16[768,4096]{1,0:T(8,128)(2,1)S(1)} %bitcast.2, bf16[144,4096]{1,0:T(8,128)(2,1)S(1)} %after.6.refs_4_, ...), custom_call_target="tpu_custom_call", output_to_operand_aliasing={{0}: (7, {})} | custom-call | flops 1 | bytes 1 | tf_op jit(solution)/shard_map/phase__last/pallas_call | solution.py:293
  131.8 0.0 collective-permute-done.24
  131.8 0.0 collective-permute-done.23
  131.8 1.0 collective-permute-done.22
  132.8 3.0 %scale.1 = bf16[768,4096]{1,0:T(8,128)(2,1)} custom-call(f32[768,4096]{1,0:T(8,128)S(1)} %get-tuple-element.91.w_ref, f32[8,128]{1,0:T(8,128)S(1)} %add_add_fusion.squares_ref), custom_call_target="tpu_custom_call" | custom-call | flops 3145728 | bytes 6291456 | tf_op jit(solution)/shard_map/scale/pallas_call | solution.py:333
  (15 shorter events, 0.0 us)
Async XLA Ops:
  1.9 1.3 copy-start
  3.3 10.4 %slice-start = ((s8[6291456]{0:T(1024)(128)(4,1)}), s8[4194304]{0:T(1024)(128)(4,1)S(1)}, s32[]{:S(2)}) async-start(s8[6291456]{0:T(1024)(128)(4,1)} %bitcast.1), calls=%async_computation | async-start | bytes 8388608
  4.1 27.6 %collective-permute-start = (bf16[144,4096]{1,0:T(8,128)(2,1)S(1)}, bf16[144,4096]{1,0:T(8,128)(2,1)S(1)}, u32[]{:S(2)}, u32[]{:S(2)}) collective-permute-start(bf16[144,4096]{1,0:T(8,128)(2,1)S(1)} %get-tuple-element.48.own_ref), channel_id=1, source_target_pairs={{0,4},{1,5},{4,8},{5,9},{8,12},{9,13},{12,14},{13,15},{14,10},{15,... | collective-permute-start | bytes 3538952 | tf_op jit(solution)/shard_map/ppermute | solution.py:442
  7.2 27.2 %collective-permute-start.1 = (bf16[144,4096]{1,0:T(8,128)(2,1)S(1)}, bf16[144,4096]{1,0:T(8,128)(2,1)S(1)}, u32[]{:S(2)}, u32[]{:S(2)}) collective-permute-start(bf16[144,4096]{1,0:T(8,128)(2,1)S(1)} %get-tuple-element.48.own_ref), channel_id=1, source_target_pairs={{0,2},{1,3},{4,0},{5,1},{8,4},{9,5},{12,8},{13,9},{14,12},{15,13},... | collective-permute-start | bytes 3538952 | tf_op jit(solution)/shard_map/ppermute | solution.py:442
  7.2 6.5 %slice-start.1 = ((s8[6291456]{0:T(1024)(128)(4,1)}), s8[2097152]{0:T(1024)(128)(4,1)S(1)}, s32[]{:S(2)}) async-start(s8[6291456]{0:T(1024)(128)(4,1)} %bitcast.1), calls=%async_computation.1 | async-start | bytes 4194304
  10.8 2.1 %collective-permute-start.2 = (bf16[144,2048]{1,0:T(8,128)(2,1)S(1)}, bf16[144,2048]{1,0:T(8,128)(2,1)S(1)}, u32[]{:S(2)}, u32[]{:S(2)}) collective-permute-start(bf16[144,2048]{1,0:T(8,128)(2,1)S(1)} %get-tuple-element.56.refs_5_), channel_id=1, source_target_pairs={{0,1},{1,0},{2,3},{3,2},{4,5},{5,4},{6,7},{7,6},{8,9},{9,8},{10,11... | collective-permute-start | bytes 1769480 | tf_op jit(solution)/shard_map/ppermute | solution.py:442
  10.8 2.8 %collective-permute-start.3 = (bf16[144,2048]{1,0:T(8,128)(2,1)S(1)}, bf16[144,2048]{1,0:T(8,128)(2,1)S(1)}, u32[]{:S(2)}, u32[]{:S(2)}) collective-permute-start(bf16[144,2048]{1,0:T(8,128)(2,1)S(1)} %get-tuple-element.57.refs_7_), channel_id=1, source_target_pairs={{0,1},{1,0},{2,3},{3,2},{4,5},{5,4},{6,7},{7,6},{8,9},{9,8},{10,11... | collective-permute-start | bytes 1769480 | tf_op jit(solution)/shard_map/ppermute | solution.py:442
  34.4 28.4 %collective-permute-start.4 = (bf16[144,4096]{1,0:T(8,128)(2,1)S(1)}, bf16[144,4096]{1,0:T(8,128)(2,1)S(1)}, u32[]{:S(2)}, u32[]{:S(2)}) collective-permute-start(bf16[144,4096]{1,0:T(8,128)(2,1)S(1)} %get-tuple-element.59.first_ref), channel_id=1, source_target_pairs={{0,4},{1,5},{4,8},{5,9},{8,12},{9,13},{12,14},{13,15},{14,10},{15,... | collective-permute-start | bytes 3538952 | tf_op jit(solution)/shard_map/ppermute | solution.py:442
  35.9 28.6 %collective-permute-start.5 = (bf16[144,4096]{1,0:T(8,128)(2,1)S(1)}, bf16[144,4096]{1,0:T(8,128)(2,1)S(1)}, u32[]{:S(2)}, u32[]{:S(2)}) collective-permute-start(bf16[144,4096]{1,0:T(8,128)(2,1)S(1)} %get-tuple-element.60.second_ref), channel_id=1, source_target_pairs={{0,2},{1,3},{4,0},{5,1},{8,4},{9,5},{12,8},{13,9},{14,12},{15,13},... | collective-permute-start | bytes 3538952 | tf_op jit(solution)/shard_map/ppermute | solution.py:442
  36.7 5.1 %collective-permute-start.7 = (bf16[288,1536]{1,0:T(8,128)(2,1)S(1)}, bf16[288,1536]{1,0:T(8,128)(2,1)S(1)}, u32[]{:S(2)}, u32[]{:S(2)}) collective-permute-start(bf16[288,1536]{1,0:T(8,128)(2,1)S(1)} %get-tuple-element.63.refs_7_), channel_id=1, source_target_pairs={{0,1},{1,0},{2,3},{3,2},{4,5},{5,4},{6,7},{7,6},{8,9},{9,8},{10,11... | collective-permute-start | bytes 2654216 | tf_op jit(solution)/shard_map/ppermute | solution.py:442
  37.6 4.2 %collective-permute-start.8 = (bf16[288,1536]{1,0:T(8,128)(2,1)S(1)}, bf16[288,1536]{1,0:T(8,128)(2,1)S(1)}, u32[]{:S(2)}, u32[]{:S(2)}) collective-permute-start(bf16[288,1536]{1,0:T(8,128)(2,1)S(1)} %get-tuple-element.64.refs_9_), channel_id=1, source_target_pairs={{0,1},{1,0},{2,3},{3,2},{4,5},{5,4},{6,7},{7,6},{8,9},{9,8},{10,11... | collective-permute-start | bytes 2654216 | tf_op jit(solution)/shard_map/ppermute | solution.py:442
  37.7 4.1 %collective-permute-start.6 = (bf16[288,1024]{1,0:T(8,128)(2,1)S(1)}, bf16[288,1024]{1,0:T(8,128)(2,1)S(1)}, u32[]{:S(2)}, u32[]{:S(2)}) collective-permute-start(bf16[288,1024]{1,0:T(8,128)(2,1)S(1)} %get-tuple-element.62.refs_5_), channel_id=1, source_target_pairs={{0,1},{1,0},{2,3},{3,2},{4,5},{5,4},{6,7},{7,6},{8,9},{9,8},{10,11... | collective-permute-start | bytes 1769480 | tf_op jit(solution)/shard_map/ppermute | solution.py:442
  64.5 28.0 %collective-permute-start.9 = (bf16[144,4096]{1,0:T(8,128)(2,1)S(1)}, bf16[144,4096]{1,0:T(8,128)(2,1)S(1)}, u32[]{:S(2)}, u32[]{:S(2)}) collective-permute-start(bf16[144,4096]{1,0:T(8,128)(2,1)S(1)} %get-tuple-element.68.first_ref), channel_id=1, source_target_pairs={{0,4},{1,5},{4,8},{5,9},{8,12},{9,13},{12,14},{13,15},{14,10},{15,... | collective-permute-start | bytes 3538952 | tf_op jit(solution)/shard_map/ppermute | solution.py:442
  66.1 27.7 %collective-permute-start.10 = (bf16[144,4096]{1,0:T(8,128)(2,1)S(1)}, bf16[144,4096]{1,0:T(8,128)(2,1)S(1)}, u32[]{:S(2)}, u32[]{:S(2)}) collective-permute-start(bf16[144,4096]{1,0:T(8,128)(2,1)S(1)} %get-tuple-element.69.second_ref), channel_id=1, source_target_pairs={{0,2},{1,3},{4,0},{5,1},{8,4},{9,5},{12,8},{13,9},{14,12},{15,13},... | collective-permute-start | bytes 3538952 | tf_op jit(solution)/shard_map/ppermute | solution.py:442
  66.8 4.6 %collective-permute-start.12 = (bf16[288,1536]{1,0:T(8,128)(2,1)S(1)}, bf16[288,1536]{1,0:T(8,128)(2,1)S(1)}, u32[]{:S(2)}, u32[]{:S(2)}) collective-permute-start(bf16[288,1536]{1,0:T(8,128)(2,1)S(1)} %get-tuple-element.72.refs_7_), channel_id=1, source_target_pairs={{0,1},{1,0},{2,3},{3,2},{4,5},{5,4},{6,7},{7,6},{8,9},{9,8},{10,11... | collective-permute-start | bytes 2654216 | tf_op jit(solution)/shard_map/ppermute | solution.py:442
  66.9 4.5 %collective-permute-start.13 = (bf16[288,1536]{1,0:T(8,128)(2,1)S(1)}, bf16[288,1536]{1,0:T(8,128)(2,1)S(1)}, u32[]{:S(2)}, u32[]{:S(2)}) collective-permute-start(bf16[288,1536]{1,0:T(8,128)(2,1)S(1)} %get-tuple-element.73.refs_9_), channel_id=1, source_target_pairs={{0,1},{1,0},{2,3},{3,2},{4,5},{5,4},{6,7},{7,6},{8,9},{9,8},{10,11... | collective-permute-start | bytes 2654216 | tf_op jit(solution)/shard_map/ppermute | solution.py:442
  67.4 4.0 %collective-permute-start.11 = (bf16[288,1024]{1,0:T(8,128)(2,1)S(1)}, bf16[288,1024]{1,0:T(8,128)(2,1)S(1)}, u32[]{:S(2)}, u32[]{:S(2)}) collective-permute-start(bf16[288,1024]{1,0:T(8,128)(2,1)S(1)} %get-tuple-element.71.refs_5_), channel_id=1, source_target_pairs={{0,1},{1,0},{2,3},{3,2},{4,5},{5,4},{6,7},{7,6},{8,9},{9,8},{10,11... | collective-permute-start | bytes 1769480 | tf_op jit(solution)/shard_map/ppermute | solution.py:442
  94.1 18.7 %collective-permute-start.14 = (bf16[144,4096]{1,0:T(8,128)(2,1)S(1)}, bf16[144,4096]{1,0:T(8,128)(2,1)S(1)}, u32[]{:S(2)}, u32[]{:S(2)}) collective-permute-start(bf16[144,4096]{1,0:T(8,128)(2,1)S(1)} %chosen.1), channel_id=1, source_target_pairs={{0,4},{1,3},{4,8},{5,1},{8,12},{9,5},{12,14},{13,9},{14,10},{15,13... | collective-permute-start | bytes 3538952 | tf_op jit(solution)/shard_map/ppermute | solution.py:442
  96.0 4.6 %collective-permute-start.16 = (bf16[288,1536]{1,0:T(8,128)(2,1)S(1)}, bf16[288,1536]{1,0:T(8,128)(2,1)S(1)}, u32[]{:S(2)}, u32[]{:S(2)}) collective-permute-start(bf16[288,1536]{1,0:T(8,128)(2,1)S(1)} %get-tuple-element.79.refs_7_), channel_id=1, source_target_pairs={{0,1},{1,0},{2,3},{3,2},{4,5},{5,4},{6,7},{7,6},{8,9},{9,8},{10,11... | collective-permute-start | bytes 2654216 | tf_op jit(solution)/shard_map/ppermute | solution.py:442
  96.1 4.5 %collective-permute-start.17 = (bf16[288,1536]{1,0:T(8,128)(2,1)S(1)}, bf16[288,1536]{1,0:T(8,128)(2,1)S(1)}, u32[]{:S(2)}, u32[]{:S(2)}) collective-permute-start(bf16[288,1536]{1,0:T(8,128)(2,1)S(1)} %get-tuple-element.80.refs_9_), channel_id=1, source_target_pairs={{0,1},{1,0},{2,3},{3,2},{4,5},{5,4},{6,7},{7,6},{8,9},{9,8},{10,11... | collective-permute-start | bytes 2654216 | tf_op jit(solution)/shard_map/ppermute | solution.py:442
  96.6 4.0 %collective-permute-start.15 = (bf16[288,1024]{1,0:T(8,128)(2,1)S(1)}, bf16[288,1024]{1,0:T(8,128)(2,1)S(1)}, u32[]{:S(2)}, u32[]{:S(2)}) collective-permute-start(bf16[288,1024]{1,0:T(8,128)(2,1)S(1)} %get-tuple-element.78.refs_5_), channel_id=1, source_target_pairs={{0,1},{1,0},{2,3},{3,2},{4,5},{5,4},{6,7},{7,6},{8,9},{9,8},{10,11... | collective-permute-start | bytes 1769480 | tf_op jit(solution)/shard_map/ppermute | solution.py:442
  112.9 4.0 %collective-permute-start.18 = (bf16[144,4096]{1,0:T(8,128)(2,1)S(1)}, bf16[144,4096]{1,0:T(8,128)(2,1)S(1)}, u32[]{:S(2)}, u32[]{:S(2)}) collective-permute-start(bf16[144,4096]{1,0:T(8,128)(2,1)S(1)} %after.6.refs_4_), channel_id=1, source_target_pairs={{0,1},{1,0},{2,3},{3,2},{4,5},{5,4},{6,7},{7,6},{8,9},{9,8},{10,11... | collective-permute-start | bytes 3538952 | tf_op jit(solution)/shard_map/ppermute | solution.py:442
  120.5 4.5 %collective-permute-start.21 = (f32[8,128]{1,0:T(8,128)S(1)}, f32[8,128]{1,0:T(8,128)S(1)}, u32[]{:S(2)}, u32[]{:S(2)}) collective-permute-start(f32[8,128]{1,0:T(8,128)S(1)} %get-tuple-element.92), channel_id=1, source_target_pairs={{0,3},{1,0},{2,1},{3,2},{4,7},{5,4},{6,5},{7,6},{8,11},{9,8},{10,9... | collective-permute-start | bytes 12296 | tf_op jit(solution)/shard_map/ppermute | solution.py:426
  120.9 4.0 %collective-permute-start.20 = (f32[8,128]{1,0:T(8,128)S(1)}, f32[8,128]{1,0:T(8,128)S(1)}, u32[]{:S(2)}, u32[]{:S(2)}) collective-permute-start(f32[8,128]{1,0:T(8,128)S(1)} %get-tuple-element.92), channel_id=1, source_target_pairs={{0,2},{1,3},{2,0},{3,1},{4,6},{5,7},{6,4},{7,5},{8,10},{9,11},{10,... | collective-permute-start | bytes 12296 | tf_op jit(solution)/shard_map/ppermute | solution.py:426
  122.4 3.0 %collective-permute-start.19 = (f32[8,128]{1,0:T(8,128)S(1)}, f32[8,128]{1,0:T(8,128)S(1)}, u32[]{:S(2)}, u32[]{:S(2)}) collective-permute-start(f32[8,128]{1,0:T(8,128)S(1)} %get-tuple-element.92), channel_id=1, source_target_pairs={{0,1},{1,2},{2,3},{3,0},{4,5},{5,6},{6,7},{7,4},{8,9},{9,10},{10,1... | collective-permute-start | bytes 12296 | tf_op jit(solution)/shard_map/ppermute | solution.py:426
  125.5 6.3 %collective-permute-start.24 = (f32[8,128]{1,0:T(8,128)S(1)}, f32[8,128]{1,0:T(8,128)S(1)}, u32[]{:S(2)}, u32[]{:S(2)}) collective-permute-start(f32[8,128]{1,0:T(8,128)S(1)} %after.7), channel_id=1, source_target_pairs={{0,12},{1,13},{2,14},{3,15},{4,0},{5,1},{6,2},{7,3},{8,4},{9,5},{1... | collective-permute-start | bytes 12296 | tf_op jit(solution)/shard_map/ppermute | solution.py:426
  125.7 6.1 %collective-permute-start.23 = (f32[8,128]{1,0:T(8,128)S(1)}, f32[8,128]{1,0:T(8,128)S(1)}, u32[]{:S(2)}, u32[]{:S(2)}) collective-permute-start(f32[8,128]{1,0:T(8,128)S(1)} %after.7), channel_id=1, source_target_pairs={{0,8},{1,9},{2,10},{3,11},{4,12},{5,13},{6,14},{7,15},{8,0},{9,1},... | collective-permute-start | bytes 12296 | tf_op jit(solution)/shard_map/ppermute | solution.py:426
  127.4 5.4 %collective-permute-start.22 = (f32[8,128]{1,0:T(8,128)S(1)}, f32[8,128]{1,0:T(8,128)S(1)}, u32[]{:S(2)}, u32[]{:S(2)}) collective-permute-start(f32[8,128]{1,0:T(8,128)S(1)} %after.7), channel_id=1, source_target_pairs={{0,4},{1,5},{2,6},{3,7},{4,8},{5,9},{6,10},{7,11},{8,12},{9,13},{1... | collective-permute-start | bytes 12296 | tf_op jit(solution)/shard_map/ppermute | solution.py:426

commit v7 on v5

--- a/solution.py
+++ b/solution.py
@@ -11,7 +11,7 @@
 HEADS = 64
 HEAD_DIM = 128
 SEQ = 16
-TILE = 1024
+TILE = 512
 MIB = 1024 * 1024
 
 
@@ -30,28 +30,34 @@
     def device(self, position, core):
         return 2 * self.chips[position % self.length] + core
 
-    def shift(self, step):
+    def along(self):
         return [
-            (self.device(p, core), self.device(p + step, core))
+            (self.device(p, core), self.device(p + 1 - 2 * core, core))
             for p in range(self.length)
             for core in range(2)
         ]
 
+    def crossing(self):
+        return [
+            (self.device(p, core), self.device(p - 1 + 2 * core, 1 - core))
+            for p in range(self.length)
+            for core in range(2)
+        ]
+
     def swap(self):
         return [(d, d ^ 1) for d in range(self.devices)]
 
-    def owners(self, groups):
-        table = []
+    def owners(self):
+        table, last = [], self.length // 2
         for d in range(self.devices):
             p, core = self.position[d // 2], d % 2
-            table.append(
-                [
-                    self.device(p + offset, c)
-                    for offsets in groups
-                    for c in (core, 1 - core)
-                    for offset in offsets
-                ]
-            )
+            row = [d, d ^ 1]
+            for k in range(1, last + 1):
+                step = k if core else -k
+                row += [self.device(p + step, core), self.device(p - step, 1 - core)]
+                if k < last:
+                    row += [self.device(p + step, 1 - core), self.device(p - step, core)]
+            table.append(row)
         return np.array(table, np.int32)
 
 
@@ -80,8 +86,16 @@
     )(seq_counts, me, pltpu.with_memory_space_constraint(out_grad, pltpu.HBM))
 
 
-def prep_kernel(counts, rows, table_ref, me_ref, heads_ref, a_ref, *refs):
-    at_refs, (block_ref, sems) = refs[: len(counts)], refs[len(counts) :]
+def prep_kernel(counts, rows, table_ref, me_ref, heads_ref, own_ref, a_ref, *refs):
+    copy_ref, left_ref, right_ref, *at_refs, block_ref, sems, own_sems = refs
+    half = left_ref.shape[1]
+    owns = [
+        pltpu.make_async_copy(own_ref, copy_ref, own_sems.at[0]),
+        pltpu.make_async_copy(own_ref.at[:, pl.ds(0, half)], left_ref, own_sems.at[1]),
+        pltpu.make_async_copy(own_ref.at[:, pl.ds(half, half)], right_ref, own_sems.at[2]),
+    ]
+    for copy in owns:
+        copy.start()
     width = heads_ref[0] * HEAD_DIM
     copies = []
     for i in range(sum(counts)):
@@ -102,42 +116,51 @@
         column = lax.broadcasted_iota(jnp.int32, block.shape, 1)
         at_ref[...] = jnp.where(column < width, block, jnp.zeros_like(block)).T
         begin += count
-
-
-def prepared(table, me, head_counts, attn_out, counts, rows):
+    for copy in owns:
+        copy.wait()
+
+
+def prepared(where, own, attn_out, counts):
     slots, capacity = attn_out.shape
+    rows, features = own.shape
     vmem = pl.BlockSpec(memory_space=pltpu.VMEM)
     smem = pl.BlockSpec(memory_space=pltpu.SMEM)
-    return pl.pallas_call(
+    outs = [(rows, features), (rows, features // 2), (rows, features // 2)]
+    outs += [(capacity, count * rows) for count in counts]
+    copy, left, right, *ats = pl.pallas_call(
         functools.partial(prep_kernel, counts, rows),
-        in_specs=[smem, smem, smem, pl.BlockSpec(memory_space=pl.ANY)],
-        out_specs=[vmem] * len(counts),
-        out_shape=[pltpu.VMEM((capacity, count * rows), jnp.bfloat16) for count in counts],
+        in_specs=[smem] * 3 + [vmem, pl.BlockSpec(memory_space=pl.ANY)],
+        out_specs=[vmem] * len(outs),
+        out_shape=[pltpu.VMEM(shape, jnp.bfloat16) for shape in outs],
         scratch_shapes=[
             pltpu.VMEM((slots, capacity), jnp.bfloat16),
             pltpu.SemaphoreType.DMA((sum(counts),)),
+            pltpu.SemaphoreType.DMA((3,)),
         ],
         compiler_params=pltpu.CompilerParams(vmem_limit_bytes=12 * MIB),
-        cost_estimate=pl.CostEstimate(
-            flops=0, bytes_accessed=4 * slots * capacity, transcendentals=0
-        ),
+        cost_estimate=pl.CostEstimate(flops=1, bytes_accessed=1, transcendentals=0),
         name="prep",
-    )(table, me, head_counts, pltpu.with_memory_space_constraint(attn_out, pltpu.HBM))
+    )(
+        *where,
+        pltpu.with_memory_space_constraint(own, pltpu.VMEM),
+        pltpu.with_memory_space_constraint(attn_out, pltpu.HBM),
+    )
+    return copy, (left, right), ats
 
 
 def phase_kernel(spec, *refs):
-    groups, arrays, w_halves, attn, fresh_w, fresh_out, squares, rows, begin = spec
+    groups, arrays, do_w, attn, fresh_w, fresh_out, squares, rows, begin = spec
     refs = list(refs)
     table_ref, me_ref, heads_ref = refs.pop(0), refs.pop(0), refs.pop(0)
-    at_ref = refs.pop(0) if w_halves else None
+    at_ref = refs.pop(0) if do_w else None
     weight_ref = refs.pop(0) if attn else None
     g_refs = [refs.pop(0) for _ in range(arrays)]
-    if w_halves and not fresh_w:
+    if do_w and not fresh_w:
         refs.pop(0)
     before_ref = refs.pop(0) if attn == "last" else None
     if attn in ("whole", "last") and not fresh_out:
         refs.pop(0)
-    w_ref = refs.pop(0) if w_halves else None
+    w_ref = refs.pop(0) if do_w else None
     total_ref = refs.pop(0) if attn == "first" else None
     out_ref = refs.pop(0) if attn in ("whole", "last") else None
     squares_ref = refs.pop(0)
@@ -149,12 +172,12 @@
         total_ref[...] = jnp.zeros_like(total_ref)
     squares_ref[...] = jnp.zeros_like(squares_ref)
 
-    def body(half, span, pieces, j, carry):
-        here = pl.ds(pl.multiple_of(j * TILE, TILE), TILE)
-        there = pl.ds(pl.multiple_of(half * span + j * TILE, TILE), TILE)
+    def body(first, column, pieces, j, carry):
+        here = pl.ds(pl.multiple_of(column + j * TILE, TILE), TILE)
+        there = pl.ds(pl.multiple_of(first + j * TILE, TILE), TILE)
         g = [g_refs[i][start : start + count, here] for i, start, count in pieces]
         g = jnp.concatenate(g, axis=0) if len(g) > 1 else g[0]
-        if half in w_halves:
+        if do_w:
             w = jnp.dot(at_ref[...], g, preferred_element_type=jnp.float32)
             if not fresh_w:
                 w = w + w_ref[:, there]
@@ -174,8 +197,9 @@
             )
         return carry
 
-    for half, span, pieces in groups:
-        lax.fori_loop(0, span // TILE, functools.partial(body, half, span, pieces), 0)
+    for first, width, column, pieces in groups:
+        step = functools.partial(body, first, column, pieces)
+        lax.fori_loop(0, width // TILE, step, 0)
     if attn in ("whole", "last"):
         total = total_ref[...]
         column = lax.broadcasted_iota(jnp.int32, total.shape, 1)
@@ -197,20 +221,21 @@
 
 
 def phase(
-    where, shapes, begin, groups, at=None, w=None, w_halves=(),
+    where, shapes, begin, groups, at=None, w=None,
     weight=None, attn=None, before=None, out=None, squares=False,
 ):
     slots, capacity, features, rows = shapes
+    do_w = at is not None
     arrays, described = [], []
-    for half, pieces in groups:
+    for first, width, column, pieces in groups:
         placed = []
         for array, start, count in pieces:
             known = [i for i, x in enumerate(arrays) if x is array]
             if not known:
                 arrays.append(array)
             placed.append((known[0] if known else len(arrays) - 1, start, count))
-        described.append((half, pieces[0][0].shape[1], tuple(placed)))
-    height = sum(count for _, _, count in groups[0][1])
+        described.append((first, width, column, tuple(placed)))
+    height = sum(count for _, _, count in groups[0][3])
     vmem = pl.BlockSpec(memory_space=pltpu.VMEM)
     smem = pl.BlockSpec(memory_space=pltpu.SMEM)
     hbm = pl.BlockSpec(memory_space=pl.ANY)
@@ -226,13 +251,13 @@
 
     for scalar in where:
         add(scalar, smem)
-    if w_halves:
+    if do_w:
         add_vmem(at)
     if attn:
         add_vmem(weight)
     for array in arrays:
         add_vmem(array)
-    if w_halves:
+    if do_w:
         if w is not None:
             aliases[len(args)] = len(outs)
             add_vmem(w)
@@ -257,7 +282,7 @@
     outs.append(pltpu.VMEM((8, 128), jnp.float32))
     out_specs.append(vmem)
     spec = (
-        tuple(described), len(arrays), tuple(w_halves), attn, w is None, out is None,
+        tuple(described), len(arrays), do_w, attn, w is None, out is None,
         squares, rows, begin,
     )
     return pl.pallas_call(
@@ -273,7 +298,7 @@
             bytes_accessed=1,
             transcendentals=0,
         ),
-        name="phase_" + "w" * len(w_halves) + "_" + str(attn),
+        name="phase_" + "w" * do_w + "_" + str(attn),
     )(*args)
 
 
@@ -332,38 +357,30 @@
     )(*[pltpu.with_memory_space_constraint(x, pltpu.VMEM) for x in (*arrays, done)])
 
 
-def split_kernel(plan, first_ref, second_ref, *refs):
-    outs, sems = refs[:-1], refs[-1]
-    rows, half = first_ref.shape[0], outs[0].shape[1]
-    copies = []
-    for which, c, out, row in plan:
-        source = (first_ref, second_ref)[which].at[:, pl.ds(c * half, half)]
-        target = outs[out].at[pl.ds(row * rows, rows)]
-        copies.append(pltpu.make_async_copy(source, target, sems.at[len(copies)]))
-        copies[-1].start()
+def split_kernel(x_ref, left_ref, right_ref, sems):
+    half = left_ref.shape[1]
+    copies = [
+        pltpu.make_async_copy(x_ref.at[:, pl.ds(0, half)], left_ref, sems.at[0]),
+        pltpu.make_async_copy(x_ref.at[:, pl.ds(half, half)], right_ref, sems.at[1]),
+    ]
+    for copy in copies:
+        copy.start()
     for copy in copies:
         copy.wait()
 
 
-def split(first, second, join):
+def split(x):
     vmem = pl.BlockSpec(memory_space=pltpu.VMEM)
-    rows, features = first.shape
-    if join:
-        plan = [(0, 0, 0, 0), (1, 1, 1, 0)]
-        plan += [(which, c, 2 + c, which) for c in range(2) for which in range(2)]
-        heights = [rows, rows, 2 * rows, 2 * rows]
-    else:
-        plan = [(which, c, 2 * which + c, 0) for which in range(2) for c in range(2)]
-        heights = [rows] * 4
+    rows, features = x.shape
     return pl.pallas_call(
-        functools.partial(split_kernel, plan),
-        in_specs=[vmem] * 2,
-        out_specs=[vmem] * 4,
-        out_shape=[pltpu.VMEM((h, features // 2), first.dtype) for h in heights],
-        scratch_shapes=[pltpu.SemaphoreType.DMA((len(plan),))],
+        split_kernel,
+        in_specs=[vmem],
+        out_specs=[vmem] * 2,
+        out_shape=[pltpu.VMEM((rows, features // 2), x.dtype)] * 2,
+        scratch_shapes=[pltpu.SemaphoreType.DMA((2,))],
         compiler_params=pltpu.CompilerParams(vmem_limit_bytes=MIB),
         name="split",
-    )(*[pltpu.with_memory_space_constraint(x, pltpu.VMEM) for x in (first, second)])
+    )(pltpu.with_memory_space_constraint(x, pltpu.VMEM))
 
 
 def exchange(x, devices, stride, radix):
@@ -381,78 +398,67 @@
     rows, features = out_grad.shape
     slots = attn_out.shape[0]
     devices, last = ring.devices, ring.length // 2
-    offsets = [[0]] + [[-k, k] for k in range(1, last)] + [[last]]
-    counts = [2] + [4] * (last - 1) + [1, 1]
+    counts = [2] + [4] * (last - 2) + [2, 2, 1, 1]
     me = lax.axis_index("dp").astype(jnp.int32).reshape(1)
-    where = (jnp.asarray(ring.owners(offsets)), me, head_counts)
+    where = (jnp.asarray(ring.owners()), me, head_counts)
     shapes = (slots, o_weight.shape[0], features, rows)
-    weight = o_weight
-
-    def swap(x):
-        return lax.ppermute(x, "dp", ring.swap())
-
-    def forward(x):
-        return lax.ppermute(x, "dp", ring.shift(1))
-
-    def backward(x):
-        return lax.ppermute(x, "dp", ring.shift(-1))
+    weight, half = o_weight, features // 2
+
+    def send(x, pairs):
+        return lax.ppermute(x, "dp", pairs)
+
+    def swapped(halves):
+        return [send(x, ring.swap()) for x in halves]
+
+    def grouped(*pairs):
+        return [(c * half, half, 0, [(x[c], 0, rows) for x in pairs]) for c in range(2)]
 
     own = live_rows(seq_counts, me, out_grad)
-    ahead, behind, other = forward(own), backward(own), swap(own)
-    ats = prepared(*where, attn_out, counts, rows)
+    x = send(own, ring.along())
+    own, near, ats = prepared(where, own, attn_out, counts)
+    y = send(own, ring.crossing())
     w, out, done = phase(
-        where, shapes, 0, [(0, [(own, 0, rows), (other, 0, rows)])],
-        at=ats[0], w_halves=(0,), weight=weight, attn="whole",
-    )
-    begin = counts[0]
-    for k in range(1, last):
-        (ahead,), (behind,) = after(done, ahead), after(done, behind)
-        if k < last - 1:
-            next_ahead, next_behind = forward(ahead), backward(behind)
-        pieces = split(ahead, behind, k == last - 1)
-        groups = []
-        if k == last - 1:
-            next_ahead, next_behind = forward(pieces[0]), backward(pieces[1])
-            for c in range(2):
-                near = pieces[2 + c]
-                groups.append((c, [(x, 0, 2 * rows) for x in (near, swap(near))]))
-        else:
-            for c in range(2):
-                near = [pieces[c], pieces[2 + c]]
-                far = [swap(x) for x in near]
-                groups.append((c, [(x, 0, rows) for x in near + far]))
-        w, done = phase(
-            where, shapes, begin, groups[:1], at=ats[k], w=w, w_halves=(0,)
-        )
-        w, out, done = phase(
-            where, shapes, begin, groups, at=ats[k], w=w, w_halves=(1,),
+        where, shapes, 0, grouped(near, swapped(near)), at=ats[0], weight=weight, attn="whole"
+    )
+
+    def dots(k, *pairs):
+        return phase(
+            where, shapes, sum(counts[:k]), grouped(*pairs), at=ats[k], w=w,
             weight=weight, attn="whole", out=out,
         )
-        begin += counts[k]
-        ahead, behind = next_ahead, next_behind
-
-    both = after(done, ahead, behind)
-    other = [swap(x) for x in both]
-    mine = [(c, [(both[c], 0, rows)]) for c in range(2)]
-    theirs = [(c, [(other[c], 0, rows)]) for c in range(2)]
-    w, done = phase(where, shapes, begin, mine, at=ats[last], w=w, w_halves=(0, 1))
-    w, squares = phase(
-        where, shapes, begin, theirs, at=ats[last + 1], w=w, w_halves=(0, 1), squares=True
-    )
+
+    for k in range(1, last):
+        (x,) = after(done, x)
+        x, near_x = send(x, ring.along()), split(x)
+        far_x = swapped(near_x)
+        if k == last - 1:
+            w, out, done = dots(k, near_x, far_x)
+        (y,) = after(done, y)
+        y, near_y = send(y, ring.along()) if k < last - 1 else None, split(y)
+        far_y = swapped(near_y)
+        if k < last - 1:
+            w, out, done = dots(k, near_x, far_x, near_y, far_y)
+        else:
+            w, out, done = dots(k + 1, near_y, far_y)
+
+    (x,) = after(done, x)
+    near = split(x)
+    far = swapped(near)
+    begin = sum(counts[:-2])
+    w, done = phase(where, shapes, begin, grouped(near), at=ats[-2], w=w)
+    w, squares = phase(where, shapes, begin, grouped(far), at=ats[-1], w=w, squares=True)
 
     stride, late = 1, 0
     while stride < devices:
         radix = min(4, devices // stride)
         squares = exchange(squares, devices, stride, radix)
-        pieces = [(x[late], 0, rows) for x in (both, other)] if late < 2 else []
+        groups = grouped(near, far)[late : late + 1]
         if late == 0:
-            before, done = phase(
-                where, shapes, begin, [(late, pieces)], weight=weight, attn="first"
-            )
+            before, done = phase(where, shapes, begin, groups, weight=weight, attn="first")
             (squares,) = after(done, squares)
         elif late == 1:
             out, done = phase(
-                where, shapes, begin, [(late, pieces)], weight=weight, attn="last",
+                where, shapes, begin, groups, weight=weight, attn="last",
                 before=before, out=out,
             )
         stride, late = stride * radix, late + 1

time: 133 us -> 122 us (0.917)
  waiting for transfers between devices: 46.6 us -> 22 us
  starting transfers between devices: 17.2 us -> 26 us
  Pallas kernels: 64.2 us -> 70.4 us
  local copies, waits for them, and re-layouts: 2.8 us -> 0.7 us
    ppermute x21 -> x23, waiting for transfers between devices: 44.3 us -> 20.9 us  [send(): return lax.ppermute(x, 'dp', pairs)]
    ppermute x21 -> x23, starting transfers between devices: 11.7 us -> 19.1 us  [send(): return lax.ppermute(x, 'dp', pairs)]
    pallas_call x11 -> x9, Pallas kernels: 55.7 us -> 61.3 us  [phase(): pl.pallas_call(functools.partial(phase_kernel, spec), in_specs=specs, out...]
    unnamed x8 -> x6, local copies, waits for them, and re-layouts: 2.8 us -> 0.7 us
    ppermute x6, starting transfers between devices: 5.49 us -> 6.96 us  [exchange(): total = total + lax.ppermute(x, 'dp', pairs)]
  transfers between devices with their start and end apart: 27 -> 29, of which waited for: 13 -> 15; matrix products, arithmetic and copies ran while one was open for 0% -> 0% of each run, Pallas kernels for 42% -> 51%
where the time goes in v7:
time: 122 us; the launch traced here: 121 us
  Pallas kernels  70.4 us (58%)
  starting transfers between devices  26 us (21%)
  waiting for transfers between devices  22 us (18%)
  between operations  2.39 us (2%)
    pallas_call x9, Pallas kernels, phase(): pl.pallas_call(functools.partial(phase_kernel, spec), in_specs=specs, out...  61.3 us
    ppermute x23, waiting for transfers between devices, send(): return lax.ppermute(x, 'dp', pairs)  20.9 us
    ppermute x23, starting transfers between devices, send(): return lax.ppermute(x, 'dp', pairs)  19.1 us
    ppermute x6, starting transfers between devices, exchange(): total = total + lax.ppermute(x, 'dp', pairs)  6.96 us
    pallas_call x1, Pallas kernels, prepared(): pl.pallas_call(functools.partial(prep_kernel, counts, rows), in_specs=[sm...  3.95 us
    pallas_call x1, Pallas kernels, scaled(): pl.pallas_call(functools.partial(scale_kernel, parts), in_specs=[vmem, vm...  3 us
  transfers between devices with their start and end apart: 29, of which 15 were waited for; matrix products, arithmetic and copies ran while one was open for 0% of the time, Pallas kernels for 51%

profile of v7, /device:TPU:0, one launch (start us, length us, event | category | flops | bytes accessed | tf_op | source)
XLA Modules:
  0.0 121.5 jit_solution(10367115709450883120)
XLA Ops:
  1.3 1.4 %live.1.own_ref = bf16[144,4096]{1,0:T(8,128)(2,1)S(1)} custom-call(s32[1]{0:T(128)S(6)} %copy.47.seqs_ref, s32[1]{0:T(128)} %bitcast.me_ref.refs_1_, bf16[144,4096]{1,0:T(8,128)(2,1)} %grad_ref.1), custom_call_target="tpu_custom_call" | custom-call | tf_op jit(solution)/shard_map/live/pallas_call | solution.py:78
  2.7 3.1 %collective-permute-start = (bf16[144,4096]{1,0:T(8,128)(2,1)S(1)}, bf16[144,4096]{1,0:T(8,128)(2,1)S(1)}, u32[]{:S(2)}, u32[]{:S(2)}) collective-permute-start(bf16[144,4096]{1,0:T(8,128)(2,1)S(1)} %live.1.own_ref), channel_id=1, source_target_pairs={{0,4},{1,3},{4,8},{5,1},{8,12},{9,5},{12,14},{13,9},{14,10},{15,13... | collective-permute-start | bytes 3538952 | tf_op jit(solution)/shard_map/ppermute | solution.py:408
  6.5 0.0 copy-start.1
  6.5 0.7 copy-done.1
  7.2 3.9 %prep.1 = (bf16[144,4096]{1,0:T(8,128)(2,1)S(1)}, bf16[144,2048]{1,0:T(8,128)(2,1)S(1)}, bf16[144,2048]{1,0:T(8,128)(2,1)S(1)}, bf16[768,288]{1,0:T(8,128)(2,1)S...) custom-call(s32[16,16]{1,0:T(8,128)S(1)} %copy-done.1, ...), custom_call_target="tpu_custom_call" | custom-call | flops 1 | bytes 1 | tf_op jit(solution)/shard_map/prep/pallas_call | solution.py:130
  11.1 0.1 collective-permute-start.1
  11.2 0.5 collective-permute-start.2
  11.7 0.7 collective-permute-start.5
  12.4 0.8 collective-permute-done.1.refs_6_
  13.2 0.8 collective-permute-done.2.refs_8_
  14.0 7.8 %phase_w_whole.5 = (f32[768,4096]{1,0:T(8,128)S(1)}, bf16[2304,768]{1,0:T(8,128)(2,1)}, f32[8,128]{1,0:T(8,128)S(1)}) custom-call(s32[16,16]{1,0:T(8,128)S(1)} %copy-done.2, s32[1]{0:T(128)} %bitcast.me_ref.refs_1_, s32[1]{0:T(128)S(6)} %copy.46.heads_ref.refs_2_, bf16[768,288]{1,0:T(8,128)(2,1)S(1)} %get-tuple-element.47.refs_3_, ...), custom_call_target="tpu_custom_call" | custom-call | flops 1 | bytes 1 | tf_op jit(solution)/shard_map/phase_w_whole/pallas_call | solution.py:288
  21.9 3.3 %collective-permute-done.refs_0_ = bf16[144,4096]{1,0:T(8,128)(2,1)S(1)} collective-permute-done((bf16[144,4096]{1,0:T(8,128)(2,1)S(1)}, bf16[144,4096]{1,0:T(8,128)(2,1)S(1)}, u32[]{:S(2)}, u32[]{:S(2)}) %collective-permute-start) | collective-permute-done | bytes 1179680 | tf_op jit(solution)/shard_map/ppermute | solution.py:408
  25.2 0.1 split.7
  25.3 0.1 collective-permute-start.4
  25.4 2.5 %collective-permute-start.3 = (bf16[144,4096]{1,0:T(8,128)(2,1)S(1)}, bf16[144,4096]{1,0:T(8,128)(2,1)S(1)}, u32[]{:S(2)}, u32[]{:S(2)}) collective-permute-start(bf16[144,4096]{1,0:T(8,128)(2,1)S(1)} %after.8.x_ref), channel_id=1, source_target_pairs={{0,4},{1,3},{4,8},{5,1},{8,12},{9,5},{12,14},{13,9},{14,10},{15,13... | collective-permute-start | bytes 3538952 | tf_op jit(solution)/shard_map/ppermute | solution.py:408
  27.9 6.9 %collective-permute-done.5.refs_0_ = bf16[144,4096]{1,0:T(8,128)(2,1)S(1)} collective-permute-done((bf16[144,4096]{1,0:T(8,128)(2,1)S(1)}, bf16[144,4096]{1,0:T(8,128)(2,1)S(1)}, u32[]{:S(2)}, u32[]{:S(2)}) %collective-permute-start.5) | collective-permute-done | bytes 1179680 | tf_op jit(solution)/shard_map/ppermute | solution.py:408
  34.8 0.1 split.8
  34.9 3.0 %collective-permute-start.11 = (bf16[144,4096]{1,0:T(8,128)(2,1)S(1)}, bf16[144,4096]{1,0:T(8,128)(2,1)S(1)}, u32[]{:S(2)}, u32[]{:S(2)}) collective-permute-start(bf16[144,4096]{1,0:T(8,128)(2,1)S(1)} %after.9.x_ref), channel_id=1, source_target_pairs={{0,4},{1,3},{4,8},{5,1},{8,12},{9,5},{12,14},{13,9},{14,10},{15,13... | collective-permute-start | bytes 3538952 | tf_op jit(solution)/shard_map/ppermute | solution.py:408
  37.9 0.0 collective-permute-start.7
  37.9 0.5 collective-permute-start.6
  38.4 0.0 collective-permute-start.8
  38.4 1.5 %collective-permute-done.7.refs_10_ = bf16[144,2048]{1,0:T(8,128)(2,1)S(1)} collective-permute-done((bf16[144,2048]{1,0:T(8,128)(2,1)S(1)}, bf16[144,2048]{1,0:T(8,128)(2,1)S(1)}, u32[]{:S(2)}, u32[]{:S(2)}) %collective-permute-start.7) | collective-permute-done | bytes 589856 | tf_op jit(solution)/shard_map/ppermute | solution.py:408
  39.9 0.8 collective-permute-done.6.refs_8_
  40.8 0.8 collective-permute-done.8.refs_12_
  41.6 12.0 %phase_w_whole.6 = (f32[768,4096]{1,0:T(8,128)S(1)}, bf16[2304,768]{1,0:T(8,128)(2,1)}, f32[8,128]{1,0:T(8,128)S(1)}) custom-call(s32[16,16]{1,0:T(8,128)S(1)} %copy-done.2, s32[1]{0:T(128)} %bitcast.me_ref.refs_1_, s32[1]{0:T(128)S(6)} %copy.46.heads_ref.refs_2_, ...), custom_call_target="tpu_custom_call", output_to_operand_aliasing={{0}: (13, {}), {1}: (14, {})} | custom-call | flops 1 | bytes 1 | tf_op jit(solution)/shard_map/phase_w_whole/pallas_call | solution.py:288
  53.6 1.6 %collective-permute-start.9 = (bf16[144,4096]{1,0:T(8,128)(2,1)S(1)}, bf16[144,4096]{1,0:T(8,128)(2,1)S(1)}, u32[]{:S(2)}, u32[]{:S(2)}) collective-permute-start(bf16[144,4096]{1,0:T(8,128)(2,1)S(1)} %after.10.x_ref), channel_id=1, source_target_pairs={{0,4},{1,3},{4,8},{5,1},{8,12},{9,5},{12,14},{13,9},{14,10},{15,13... | collective-permute-start | bytes 3538952 | tf_op jit(solution)/shard_map/ppermute | solution.py:408
  55.2 0.1 split.9
  55.3 0.1 collective-permute-start.10
  55.4 0.5 collective-permute-start.13
  55.9 2.0 %collective-permute-done.11.refs_0_ = bf16[144,4096]{1,0:T(8,128)(2,1)S(1)} collective-permute-done((bf16[144,4096]{1,0:T(8,128)(2,1)S(1)}, bf16[144,4096]{1,0:T(8,128)(2,1)S(1)}, u32[]{:S(2)}, u32[]{:S(2)}) %collective-permute-start.11) | collective-permute-done | bytes 1179680 | tf_op jit(solution)/shard_map/ppermute | solution.py:408
  57.9 0.1 split.10
  58.0 0.1 collective-permute-start.12
  58.1 0.5 collective-permute-start.14
  58.6 2.1 %collective-permute-start.16 = (bf16[144,4096]{1,0:T(8,128)(2,1)S(1)}, bf16[144,4096]{1,0:T(8,128)(2,1)S(1)}, u32[]{:S(2)}, u32[]{:S(2)}) collective-permute-start(bf16[144,4096]{1,0:T(8,128)(2,1)S(1)} %after.11.x_ref), channel_id=1, source_target_pairs={{0,4},{1,3},{4,8},{5,1},{8,12},{9,5},{12,14},{13,9},{14,10},{15,13... | collective-permute-start | bytes 3538952 | tf_op jit(solution)/shard_map/ppermute | solution.py:408
  60.6 0.3 collective-permute-done.14.refs_12_
  60.9 12.0 %phase_w_whole.7 = (f32[768,4096]{1,0:T(8,128)S(1)}, bf16[2304,768]{1,0:T(8,128)(2,1)}, f32[8,128]{1,0:T(8,128)S(1)}) custom-call(s32[16,16]{1,0:T(8,128)S(1)} %copy-done.2, s32[1]{0:T(128)} %bitcast.me_ref.refs_1_, s32[1]{0:T(128)S(6)} %copy.46.heads_ref.refs_2_, ...), custom_call_target="tpu_custom_call", output_to_operand_aliasing={{0}: (13, {}), {1}: (14, {})} | custom-call | flops 1 | bytes 1 | tf_op jit(solution)/shard_map/phase_w_whole/pallas_call | solution.py:288
  72.9 0.1 split.11
  73.0 0.2 collective-permute-start.17
  73.2 0.4 collective-permute-start.18
  73.6 2.1 %collective-permute-start.15 = (bf16[144,4096]{1,0:T(8,128)(2,1)S(1)}, bf16[144,4096]{1,0:T(8,128)(2,1)S(1)}, u32[]{:S(2)}, u32[]{:S(2)}) collective-permute-start(bf16[144,4096]{1,0:T(8,128)(2,1)S(1)} %after.12.x_ref), channel_id=1, source_target_pairs={{0,4},{1,3},{4,8},{5,1},{8,12},{9,5},{12,14},{13,9},{14,10},{15,13... | collective-permute-start | bytes 3538952 | tf_op jit(solution)/shard_map/ppermute | solution.py:408
  75.6 0.3 collective-permute-done.18.refs_8_
  75.9 7.9 %phase_w_whole.8 = (f32[768,4096]{1,0:T(8,128)S(1)}, bf16[2304,768]{1,0:T(8,128)(2,1)}, f32[8,128]{1,0:T(8,128)S(1)}) custom-call(s32[16,16]{1,0:T(8,128)S(1)} %copy-done.2, s32[1]{0:T(128)} %bitcast.me_ref.refs_1_, s32[1]{0:T(128)S(6)} %copy.46.heads_ref.refs_2_, ...), custom_call_target="tpu_custom_call", output_to_operand_aliasing={{0}: (9, {}), {1}: (10, {})} | custom-call | flops 1 | bytes 1 | tf_op jit(solution)/shard_map/phase_w_whole/pallas_call | solution.py:288
  83.8 0.1 split.12
  83.9 0.2 collective-permute-start.19
  84.2 0.4 collective-permute-start.20
  84.5 1.5 %collective-permute-done.19.refs_6_ = bf16[144,2048]{1,0:T(8,128)(2,1)S(1)} collective-permute-done((bf16[144,2048]{1,0:T(8,128)(2,1)S(1)}, bf16[144,2048]{1,0:T(8,128)(2,1)S(1)}, u32[]{:S(2)}, u32[]{:S(2)}) %collective-permute-start.19) | collective-permute-done | bytes 589856 | tf_op jit(solution)/shard_map/ppermute | solution.py:408
  86.0 0.8 collective-permute-done.20.refs_8_
  86.9 7.9 %phase_w_whole.9 = (f32[768,4096]{1,0:T(8,128)S(1)}, bf16[2304,768]{1,0:T(8,128)(2,1)}, f32[8,128]{1,0:T(8,128)S(1)}) custom-call(s32[16,16]{1,0:T(8,128)S(1)} %copy-done.2, s32[1]{0:T(128)} %bitcast.me_ref.refs_1_, s32[1]{0:T(128)S(6)} %copy.46.heads_ref.refs_2_, ...), custom_call_target="tpu_custom_call", output_to_operand_aliasing={{0}: (9, {}), {1}: (10, {})} | custom-call | flops 1 | bytes 1 | tf_op jit(solution)/shard_map/phase_w_whole/pallas_call | solution.py:288
  94.8 1.0 collective-permute-done.15.refs_0_
  95.8 0.1 split.13
  95.9 0.1 collective-permute-start.21
  96.0 0.5 collective-permute-start.22
  96.5 3.8 %phase_w_None.2 = (f32[768,4096]{1,0:T(8,128)S(1)}, f32[8,128]{1,0:T(8,128)}) custom-call(s32[16,16]{1,0:T(8,128)S(1)} %copy-done.2, s32[1]{0:T(128)} %bitcast.me_ref.refs_1_, s32[1]{0:T(128)S(6)} %copy.46.heads_ref.refs_2_, bf16[768,144]{1,0:T(8,128)(2,1)S(1)} %get-tuple-element.86.refs_3_, ...), custom_call_target="tpu_custom_call", output_to_operand_aliasing={{0}: (6, {})} | custom-call | flops 1 | bytes 1 | tf_op jit(solution)/shard_map/phase_w_None/pallas_call | solution.py:288
  100.3 3.6 %phase_w_None.3 = (f32[768,4096]{1,0:T(8,128)S(1)}, f32[8,128]{1,0:T(8,128)S(1)}) custom-call(s32[16,16]{1,0:T(8,128)S(1)} %copy-done.2, s32[1]{0:T(128)} %bitcast.me_ref.refs_1_, s32[1]{0:T(128)S(6)} %copy.46.heads_ref.refs_2_, bf16[768,144]{1,0:T(8,128)(2,1)S(1)} %get-tuple-element.85.refs_3_, ...), custom_call_target="tpu_custom_call", output_to_operand_aliasing={{0}: (6, {})} | custom-call | flops 1 | bytes 1 | tf_op jit(solution)/shard_map/phase_w_None/pallas_call | solution.py:288
  103.9 1.8 %collective-permute-start.25 = (f32[8,128]{1,0:T(8,128)S(1)}, f32[8,128]{1,0:T(8,128)S(1)}, u32[]{:S(2)}, u32[]{:S(2)}) collective-permute-start(f32[8,128]{1,0:T(8,128)S(1)} %get-tuple-element.90), channel_id=1, source_target_pairs={{0,3},{1,0},{2,1},{3,2},{4,7},{5,4},{6,5},{7,6},{8,11},{9,8},{10,9... | collective-permute-start | bytes 12296 | tf_op jit(solution)/shard_map/ppermute | solution.py:393
  105.7 0.4 collective-permute-start.24
  106.1 0.2 collective-permute-start.23
  106.2 2.5 %phase__first.1 = (f32[288,768]{1,0:T(8,128)S(1)}, f32[8,128]{1,0:T(8,128)S(1)}) custom-call(s32[16,16]{1,0:T(8,128)S(1)} %copy-done.2, s32[1]{0:T(128)} %bitcast.me_ref.refs_1_, s32[1]{0:T(128)S(6)} %copy.46.heads_ref.refs_2_, bf16[768,4096]{1,0:T(8,128)(2,1)S(1)} %copy-done, bf16[144,2048]{1,0:T(8,128)(2,1)S(1)} %get-tuple-element.81.refs_4_, ...), custom_call_target="tpu_custom_call" | custom-call | flops 1 | bytes 1 | tf_op jit(solution)/shard_map/phase__first/pallas_call | solution.py:288
  108.7 0.6 collective-permute-done.24
  109.3 3.6 %collective-permute-start.28 = (f32[8,128]{1,0:T(8,128)S(1)}, f32[8,128]{1,0:T(8,128)S(1)}, u32[]{:S(2)}, u32[]{:S(2)}) collective-permute-start(f32[8,128]{1,0:T(8,128)S(1)} %after.15), channel_id=1, source_target_pairs={{0,12},{1,13},{2,14},{3,15},{4,0},{5,1},{6,2},{7,3},{8,4},{9,5},{1... | collective-permute-start | bytes 12296 | tf_op jit(solution)/shard_map/ppermute | solution.py:393
  112.9 1.0 collective-permute-start.26
  113.9 3.9 %phase__last.1 = (bf16[2304,768]{1,0:T(8,128)(2,1)}, f32[8,128]{1,0:T(8,128)}) custom-call(s32[16,16]{1,0:T(8,128)S(1)} %copy-done.2, s32[1]{0:T(128)} %bitcast.me_ref.refs_1_, s32[1]{0:T(128)S(6)} %copy.46.heads_ref.refs_2_, bf16[768,4096]{1,0:T(8,128)(2,1)S(1)} %copy-done, ...), custom_call_target="tpu_custom_call", output_to_operand_aliasing={{0}: (7, {})} | custom-call | flops 1 | bytes 1 | tf_op jit(solution)/shard_map/phase__last/pallas_call | solution.py:288
  117.8 0.5 collective-permute-done.26
  118.3 3.0 %scale.1 = bf16[768,4096]{1,0:T(8,128)(2,1)} custom-call(f32[768,4096]{1,0:T(8,128)S(1)} %get-tuple-element.89.w_ref, f32[8,128]{1,0:T(8,128)S(1)} %add_add_fusion.squares_ref), custom_call_target="tpu_custom_call" | custom-call | flops 3145728 | bytes 6291456 | tf_op jit(solution)/shard_map/scale/pallas_call | solution.py:328
  (29 shorter events, 0.1 us)
Async XLA Ops:
  1.3 12.8 %copy-start = (bf16[768,4096]{1,0:T(8,128)(2,1)S(1)}, bf16[768,4096]{1,0:T(8,128)(2,1)}, u32[]{:S(2)}) copy-start(bf16[768,4096]{1,0:T(8,128)(2,1)} %refs_3_.3) | copy-start | bytes 18874372
  2.7 22.5 %collective-permute-start = (bf16[144,4096]{1,0:T(8,128)(2,1)S(1)}, bf16[144,4096]{1,0:T(8,128)(2,1)S(1)}, u32[]{:S(2)}, u32[]{:S(2)}) collective-permute-start(bf16[144,4096]{1,0:T(8,128)(2,1)S(1)} %live.1.own_ref), channel_id=1, source_target_pairs={{0,4},{1,3},{4,8},{5,1},{8,12},{9,5},{12,14},{13,9},{14,10},{15,13... | collective-permute-start | bytes 3538952 | tf_op jit(solution)/shard_map/ppermute | solution.py:408
  6.5 0.7 copy-start.1
  7.2 6.9 %copy-start.2 = (s32[16,16]{1,0:T(8,128)S(1)}, s32[16,16]{1,0:T(8,128)}, u32[]{:S(2)}) copy-start(s32[16,16]{1,0:T(8,128)} %constant.6.clone.table_ref.refs_0_) | copy-start | bytes 3076
  11.1 2.1 %collective-permute-start.1 = (bf16[144,2048]{1,0:T(8,128)(2,1)S(1)}, bf16[144,2048]{1,0:T(8,128)(2,1)S(1)}, u32[]{:S(2)}, u32[]{:S(2)}) collective-permute-start(bf16[144,2048]{1,0:T(8,128)(2,1)S(1)} %get-tuple-element.48.refs_5_), channel_id=1, source_target_pairs={{0,1},{1,0},{2,3},{3,2},{4,5},{5,4},{6,7},{7,6},{8,9},{9,8},{10,11... | collective-permute-start | bytes 1769480 | tf_op jit(solution)/shard_map/ppermute | solution.py:408
  11.2 2.8 %collective-permute-start.2 = (bf16[144,2048]{1,0:T(8,128)(2,1)S(1)}, bf16[144,2048]{1,0:T(8,128)(2,1)S(1)}, u32[]{:S(2)}, u32[]{:S(2)}) collective-permute-start(bf16[144,2048]{1,0:T(8,128)(2,1)S(1)} %get-tuple-element.49.refs_7_), channel_id=1, source_target_pairs={{0,1},{1,0},{2,3},{3,2},{4,5},{5,4},{6,7},{7,6},{8,9},{9,8},{10,11... | collective-permute-start | bytes 1769480 | tf_op jit(solution)/shard_map/ppermute | solution.py:408
  11.7 23.1 %collective-permute-start.5 = (bf16[144,4096]{1,0:T(8,128)(2,1)S(1)}, bf16[144,4096]{1,0:T(8,128)(2,1)S(1)}, u32[]{:S(2)}, u32[]{:S(2)}) collective-permute-start(bf16[144,4096]{1,0:T(8,128)(2,1)S(1)} %get-tuple-element.53), channel_id=1, source_target_pairs={{0,3},{1,4},{4,1},{5,8},{8,5},{9,12},{12,9},{13,14},{14,13},{15,10... | collective-permute-start | bytes 3538952 | tf_op jit(solution)/shard_map/ppermute | solution.py:408
  25.3 13.1 %collective-permute-start.4 = (bf16[144,2048]{1,0:T(8,128)(2,1)S(1)}, bf16[144,2048]{1,0:T(8,128)(2,1)S(1)}, u32[]{:S(2)}, u32[]{:S(2)}) collective-permute-start(bf16[144,2048]{1,0:T(8,128)(2,1)S(1)} %get-tuple-element.52.refs_5_), channel_id=1, source_target_pairs={{0,1},{1,0},{2,3},{3,2},{4,5},{5,4},{6,7},{7,6},{8,9},{9,8},{10,11... | collective-permute-start | bytes 1769480 | tf_op jit(solution)/shard_map/ppermute | solution.py:408
  25.4 28.2 %collective-permute-start.3 = (bf16[144,4096]{1,0:T(8,128)(2,1)S(1)}, bf16[144,4096]{1,0:T(8,128)(2,1)S(1)}, u32[]{:S(2)}, u32[]{:S(2)}) collective-permute-start(bf16[144,4096]{1,0:T(8,128)(2,1)S(1)} %after.8.x_ref), channel_id=1, source_target_pairs={{0,4},{1,3},{4,8},{5,1},{8,12},{9,5},{12,14},{13,9},{14,10},{15,13... | collective-permute-start | bytes 3538952 | tf_op jit(solution)/shard_map/ppermute | solution.py:408
  34.9 23.0 %collective-permute-start.11 = (bf16[144,4096]{1,0:T(8,128)(2,1)S(1)}, bf16[144,4096]{1,0:T(8,128)(2,1)S(1)}, u32[]{:S(2)}, u32[]{:S(2)}) collective-permute-start(bf16[144,4096]{1,0:T(8,128)(2,1)S(1)} %after.9.x_ref), channel_id=1, source_target_pairs={{0,4},{1,3},{4,8},{5,1},{8,12},{9,5},{12,14},{13,9},{14,10},{15,13... | collective-permute-start | bytes 3538952 | tf_op jit(solution)/shard_map/ppermute | solution.py:408
  37.9 2.0 %collective-permute-start.7 = (bf16[144,2048]{1,0:T(8,128)(2,1)S(1)}, bf16[144,2048]{1,0:T(8,128)(2,1)S(1)}, u32[]{:S(2)}, u32[]{:S(2)}) collective-permute-start(bf16[144,2048]{1,0:T(8,128)(2,1)S(1)} %get-tuple-element.55.refs_9_), channel_id=1, source_target_pairs={{0,1},{1,0},{2,3},{3,2},{4,5},{5,4},{6,7},{7,6},{8,9},{9,8},{10,11... | collective-permute-start | bytes 1769480 | tf_op jit(solution)/shard_map/ppermute | solution.py:408
  37.9 2.8 %collective-permute-start.6 = (bf16[144,2048]{1,0:T(8,128)(2,1)S(1)}, bf16[144,2048]{1,0:T(8,128)(2,1)S(1)}, u32[]{:S(2)}, u32[]{:S(2)}) collective-permute-start(bf16[144,2048]{1,0:T(8,128)(2,1)S(1)} %get-tuple-element.54.refs_7_), channel_id=1, source_target_pairs={{0,1},{1,0},{2,3},{3,2},{4,5},{5,4},{6,7},{7,6},{8,9},{9,8},{10,11... | collective-permute-start | bytes 1769480 | tf_op jit(solution)/shard_map/ppermute | solution.py:408
  38.4 3.2 %collective-permute-start.8 = (bf16[144,2048]{1,0:T(8,128)(2,1)S(1)}, bf16[144,2048]{1,0:T(8,128)(2,1)S(1)}, u32[]{:S(2)}, u32[]{:S(2)}) collective-permute-start(bf16[144,2048]{1,0:T(8,128)(2,1)S(1)} %get-tuple-element.56.refs_11_), channel_id=1, source_target_pairs={{0,1},{1,0},{2,3},{3,2},{4,5},{5,4},{6,7},{7,6},{8,9},{9,8},{10,11... | collective-permute-start | bytes 1769480 | tf_op jit(solution)/shard_map/ppermute | solution.py:408
  53.6 19.3 %collective-permute-start.9 = (bf16[144,4096]{1,0:T(8,128)(2,1)S(1)}, bf16[144,4096]{1,0:T(8,128)(2,1)S(1)}, u32[]{:S(2)}, u32[]{:S(2)}) collective-permute-start(bf16[144,4096]{1,0:T(8,128)(2,1)S(1)} %after.10.x_ref), channel_id=1, source_target_pairs={{0,4},{1,3},{4,8},{5,1},{8,12},{9,5},{12,14},{13,9},{14,10},{15,13... | collective-permute-start | bytes 3538952 | tf_op jit(solution)/shard_map/ppermute | solution.py:408
  55.3 3.2 %collective-permute-start.10 = (bf16[144,2048]{1,0:T(8,128)(2,1)S(1)}, bf16[144,2048]{1,0:T(8,128)(2,1)S(1)}, u32[]{:S(2)}, u32[]{:S(2)}) collective-permute-start(bf16[144,2048]{1,0:T(8,128)(2,1)S(1)} %get-tuple-element.61.refs_5_), channel_id=1, source_target_pairs={{0,1},{1,0},{2,3},{3,2},{4,5},{5,4},{6,7},{7,6},{8,9},{9,8},{10,11... | collective-permute-start | bytes 1769480 | tf_op jit(solution)/shard_map/ppermute | solution.py:408
  55.4 5.2 %collective-permute-start.13 = (bf16[144,2048]{1,0:T(8,128)(2,1)S(1)}, bf16[144,2048]{1,0:T(8,128)(2,1)S(1)}, u32[]{:S(2)}, u32[]{:S(2)}) collective-permute-start(bf16[144,2048]{1,0:T(8,128)(2,1)S(1)} %get-tuple-element.63.refs_9_), channel_id=1, source_target_pairs={{0,1},{1,0},{2,3},{3,2},{4,5},{5,4},{6,7},{7,6},{8,9},{9,8},{10,11... | collective-permute-start | bytes 1769480 | tf_op jit(solution)/shard_map/ppermute | solution.py:408
  58.0 2.6 %collective-permute-start.12 = (bf16[144,2048]{1,0:T(8,128)(2,1)S(1)}, bf16[144,2048]{1,0:T(8,128)(2,1)S(1)}, u32[]{:S(2)}, u32[]{:S(2)}) collective-permute-start(bf16[144,2048]{1,0:T(8,128)(2,1)S(1)} %get-tuple-element.62.refs_7_), channel_id=1, source_target_pairs={{0,1},{1,0},{2,3},{3,2},{4,5},{5,4},{6,7},{7,6},{8,9},{9,8},{10,11... | collective-permute-start | bytes 1769480 | tf_op jit(solution)/shard_map/ppermute | solution.py:408
  58.1 2.8 %collective-permute-start.14 = (bf16[144,2048]{1,0:T(8,128)(2,1)S(1)}, bf16[144,2048]{1,0:T(8,128)(2,1)S(1)}, u32[]{:S(2)}, u32[]{:S(2)}) collective-permute-start(bf16[144,2048]{1,0:T(8,128)(2,1)S(1)} %get-tuple-element.64.refs_11_), channel_id=1, source_target_pairs={{0,1},{1,0},{2,3},{3,2},{4,5},{5,4},{6,7},{7,6},{8,9},{9,8},{10,11... | collective-permute-start | bytes 1769480 | tf_op jit(solution)/shard_map/ppermute | solution.py:408
  58.6 25.3 %collective-permute-start.16 = (bf16[144,4096]{1,0:T(8,128)(2,1)S(1)}, bf16[144,4096]{1,0:T(8,128)(2,1)S(1)}, u32[]{:S(2)}, u32[]{:S(2)}) collective-permute-start(bf16[144,4096]{1,0:T(8,128)(2,1)S(1)} %after.11.x_ref), channel_id=1, source_target_pairs={{0,4},{1,3},{4,8},{5,1},{8,12},{9,5},{12,14},{13,9},{14,10},{15,13... | collective-permute-start | bytes 3538952 | tf_op jit(solution)/shard_map/ppermute | solution.py:408
  73.0 2.6 %collective-permute-start.17 = (bf16[144,2048]{1,0:T(8,128)(2,1)S(1)}, bf16[144,2048]{1,0:T(8,128)(2,1)S(1)}, u32[]{:S(2)}, u32[]{:S(2)}) collective-permute-start(bf16[144,2048]{1,0:T(8,128)(2,1)S(1)} %get-tuple-element.70.refs_5_), channel_id=1, source_target_pairs={{0,1},{1,0},{2,3},{3,2},{4,5},{5,4},{6,7},{7,6},{8,9},{9,8},{10,11... | collective-permute-start | bytes 1769480 | tf_op jit(solution)/shard_map/ppermute | solution.py:408
  73.2 2.7 %collective-permute-start.18 = (bf16[144,2048]{1,0:T(8,128)(2,1)S(1)}, bf16[144,2048]{1,0:T(8,128)(2,1)S(1)}, u32[]{:S(2)}, u32[]{:S(2)}) collective-permute-start(bf16[144,2048]{1,0:T(8,128)(2,1)S(1)} %get-tuple-element.71.refs_7_), channel_id=1, source_target_pairs={{0,1},{1,0},{2,3},{3,2},{4,5},{5,4},{6,7},{7,6},{8,9},{9,8},{10,11... | collective-permute-start | bytes 1769480 | tf_op jit(solution)/shard_map/ppermute | solution.py:408
  73.6 22.2 %collective-permute-start.15 = (bf16[144,4096]{1,0:T(8,128)(2,1)S(1)}, bf16[144,4096]{1,0:T(8,128)(2,1)S(1)}, u32[]{:S(2)}, u32[]{:S(2)}) collective-permute-start(bf16[144,4096]{1,0:T(8,128)(2,1)S(1)} %after.12.x_ref), channel_id=1, source_target_pairs={{0,4},{1,3},{4,8},{5,1},{8,12},{9,5},{12,14},{13,9},{14,10},{15,13... | collective-permute-start | bytes 3538952 | tf_op jit(solution)/shard_map/ppermute | solution.py:408
  83.9 2.1 %collective-permute-start.19 = (bf16[144,2048]{1,0:T(8,128)(2,1)S(1)}, bf16[144,2048]{1,0:T(8,128)(2,1)S(1)}, u32[]{:S(2)}, u32[]{:S(2)}) collective-permute-start(bf16[144,2048]{1,0:T(8,128)(2,1)S(1)} %get-tuple-element.75.refs_5_), channel_id=1, source_target_pairs={{0,1},{1,0},{2,3},{3,2},{4,5},{5,4},{6,7},{7,6},{8,9},{9,8},{10,11... | collective-permute-start | bytes 1769480 | tf_op jit(solution)/shard_map/ppermute | solution.py:408
  84.2 2.7 %collective-permute-start.20 = (bf16[144,2048]{1,0:T(8,128)(2,1)S(1)}, bf16[144,2048]{1,0:T(8,128)(2,1)S(1)}, u32[]{:S(2)}, u32[]{:S(2)}) collective-permute-start(bf16[144,2048]{1,0:T(8,128)(2,1)S(1)} %get-tuple-element.76.refs_7_), channel_id=1, source_target_pairs={{0,1},{1,0},{2,3},{3,2},{4,5},{5,4},{6,7},{7,6},{8,9},{9,8},{10,11... | collective-permute-start | bytes 1769480 | tf_op jit(solution)/shard_map/ppermute | solution.py:408
  95.9 4.4 %collective-permute-start.21 = (bf16[144,2048]{1,0:T(8,128)(2,1)S(1)}, bf16[144,2048]{1,0:T(8,128)(2,1)S(1)}, u32[]{:S(2)}, u32[]{:S(2)}) collective-permute-start(bf16[144,2048]{1,0:T(8,128)(2,1)S(1)} %get-tuple-element.80.refs_4_.refs_5_), channel_id=1, source_target_pairs={{0,1},{1,0},{2,3},{3,2},{4,5},{5,4},{6,7},{7,6},{8,9},{9,8},{10,11... | collective-permute-start | bytes 1769480 | tf_op jit(solution)/shard_map/ppermute | solution.py:408
  96.0 4.3 %collective-permute-start.22 = (bf16[144,2048]{1,0:T(8,128)(2,1)S(1)}, bf16[144,2048]{1,0:T(8,128)(2,1)S(1)}, u32[]{:S(2)}, u32[]{:S(2)}) collective-permute-start(bf16[144,2048]{1,0:T(8,128)(2,1)S(1)} %get-tuple-element.81.refs_4_), channel_id=1, source_target_pairs={{0,1},{1,0},{2,3},{3,2},{4,5},{5,4},{6,7},{7,6},{8,9},{9,8},{10,11... | collective-permute-start | bytes 1769480 | tf_op jit(solution)/shard_map/ppermute | solution.py:408
  103.9 4.8 %collective-permute-start.25 = (f32[8,128]{1,0:T(8,128)S(1)}, f32[8,128]{1,0:T(8,128)S(1)}, u32[]{:S(2)}, u32[]{:S(2)}) collective-permute-start(f32[8,128]{1,0:T(8,128)S(1)} %get-tuple-element.90), channel_id=1, source_target_pairs={{0,3},{1,0},{2,1},{3,2},{4,7},{5,4},{6,5},{7,6},{8,11},{9,8},{10,9... | collective-permute-start | bytes 12296 | tf_op jit(solution)/shard_map/ppermute | solution.py:393
  105.7 3.6 %collective-permute-start.24 = (f32[8,128]{1,0:T(8,128)S(1)}, f32[8,128]{1,0:T(8,128)S(1)}, u32[]{:S(2)}, u32[]{:S(2)}) collective-permute-start(f32[8,128]{1,0:T(8,128)S(1)} %get-tuple-element.90), channel_id=1, source_target_pairs={{0,2},{1,3},{2,0},{3,1},{4,6},{5,7},{6,4},{7,5},{8,10},{9,11},{10,... | collective-permute-start | bytes 12296 | tf_op jit(solution)/shard_map/ppermute | solution.py:393
  106.1 3.2 %collective-permute-start.23 = (f32[8,128]{1,0:T(8,128)S(1)}, f32[8,128]{1,0:T(8,128)S(1)}, u32[]{:S(2)}, u32[]{:S(2)}) collective-permute-start(f32[8,128]{1,0:T(8,128)S(1)} %get-tuple-element.90), channel_id=1, source_target_pairs={{0,1},{1,2},{2,3},{3,0},{4,5},{5,6},{6,7},{7,4},{8,9},{9,10},{10,1... | collective-permute-start | bytes 12296 | tf_op jit(solution)/shard_map/ppermute | solution.py:393
  109.3 8.5 %collective-permute-start.28 = (f32[8,128]{1,0:T(8,128)S(1)}, f32[8,128]{1,0:T(8,128)S(1)}, u32[]{:S(2)}, u32[]{:S(2)}) collective-permute-start(f32[8,128]{1,0:T(8,128)S(1)} %after.15), channel_id=1, source_target_pairs={{0,12},{1,13},{2,14},{3,15},{4,0},{5,1},{6,2},{7,3},{8,4},{9,5},{1... | collective-permute-start | bytes 12296 | tf_op jit(solution)/shard_map/ppermute | solution.py:393
  112.9 4.9 %collective-permute-start.27 = (f32[8,128]{1,0:T(8,128)S(1)}, f32[8,128]{1,0:T(8,128)S(1)}, u32[]{:S(2)}, u32[]{:S(2)}) collective-permute-start(f32[8,128]{1,0:T(8,128)S(1)} %after.15), channel_id=1, source_target_pairs={{0,8},{1,9},{2,10},{3,11},{4,12},{5,13},{6,14},{7,15},{8,0},{9,1},... | collective-permute-start | bytes 12296 | tf_op jit(solution)/shard_map/ppermute | solution.py:393
  112.9 5.4 %collective-permute-start.26 = (f32[8,128]{1,0:T(8,128)S(1)}, f32[8,128]{1,0:T(8,128)S(1)}, u32[]{:S(2)}, u32[]{:S(2)}) collective-permute-start(f32[8,128]{1,0:T(8,128)S(1)} %after.15), channel_id=1, source_target_pairs={{0,4},{1,5},{2,6},{3,7},{4,8},{5,9},{6,10},{7,11},{8,12},{9,13},{1... | collective-permute-start | bytes 12296 | tf_op jit(solution)/shard_map/ppermute | solution.py:393

commit v8 on v7

--- a/solution.py
+++ b/solution.py
@@ -11,7 +11,7 @@
 HEADS = 64
 HEAD_DIM = 128
 SEQ = 16
-TILE = 512
+TILE = 1024
 MIB = 1024 * 1024
 
 
@@ -86,7 +86,7 @@
     )(seq_counts, me, pltpu.with_memory_space_constraint(out_grad, pltpu.HBM))
 
 
-def prep_kernel(counts, rows, table_ref, me_ref, heads_ref, own_ref, a_ref, *refs):
+def prep_kernel(spans, rows, table_ref, me_ref, heads_ref, own_ref, a_ref, *refs):
     copy_ref, left_ref, right_ref, *at_refs, block_ref, sems, own_sems = refs
     half = left_ref.shape[1]
     owns = [
@@ -98,7 +98,7 @@
         copy.start()
     width = heads_ref[0] * HEAD_DIM
     copies = []
-    for i in range(sum(counts)):
+    for i in range(block_ref.shape[0] // rows):
         owner = table_ref[me_ref[0], i]
         copies.append(
             pltpu.make_async_copy(
@@ -108,33 +108,33 @@
             )
         )
         copies[-1].start()
-    begin = 0
-    for at_ref, count in zip(at_refs, counts):
-        for copy in copies[begin : begin + count]:
+    waited = 0
+    for at_ref, (begin, count) in zip(at_refs, spans):
+        for copy in copies[waited : begin + count]:
             copy.wait()
+        waited = max(waited, begin + count)
         block = block_ref[begin * rows : (begin + count) * rows, :]
         column = lax.broadcasted_iota(jnp.int32, block.shape, 1)
         at_ref[...] = jnp.where(column < width, block, jnp.zeros_like(block)).T
-        begin += count
     for copy in owns:
         copy.wait()
 
 
-def prepared(where, own, attn_out, counts):
+def prepared(where, own, attn_out, spans):
     slots, capacity = attn_out.shape
     rows, features = own.shape
     vmem = pl.BlockSpec(memory_space=pltpu.VMEM)
     smem = pl.BlockSpec(memory_space=pltpu.SMEM)
     outs = [(rows, features), (rows, features // 2), (rows, features // 2)]
-    outs += [(capacity, count * rows) for count in counts]
+    outs += [(capacity, count * rows) for _, count in spans]
     copy, left, right, *ats = pl.pallas_call(
-        functools.partial(prep_kernel, counts, rows),
+        functools.partial(prep_kernel, spans, rows),
         in_specs=[smem] * 3 + [vmem, pl.BlockSpec(memory_space=pl.ANY)],
         out_specs=[vmem] * len(outs),
         out_shape=[pltpu.VMEM(shape, jnp.bfloat16) for shape in outs],
         scratch_shapes=[
             pltpu.VMEM((slots, capacity), jnp.bfloat16),
-            pltpu.SemaphoreType.DMA((sum(counts),)),
+            pltpu.SemaphoreType.DMA((slots // rows,)),
             pltpu.SemaphoreType.DMA((3,)),
         ],
         compiler_params=pltpu.CompilerParams(vmem_limit_bytes=12 * MIB),
@@ -158,6 +158,7 @@
     if do_w and not fresh_w:
         refs.pop(0)
     before_ref = refs.pop(0) if attn == "last" else None
+    added_ref = refs.pop(0) if squares == "added" else None
     if attn in ("whole", "last") and not fresh_out:
         refs.pop(0)
     w_ref = refs.pop(0) if do_w else None
@@ -170,7 +171,10 @@
         total_ref[...] = before_ref[...]
     elif attn:
         total_ref[...] = jnp.zeros_like(total_ref)
-    squares_ref[...] = jnp.zeros_like(squares_ref)
+    if squares == "added":
+        squares_ref[...] = added_ref[...]
+    else:
+        squares_ref[...] = jnp.zeros_like(squares_ref)
 
     def body(first, column, pieces, j, carry):
         here = pl.ds(pl.multiple_of(column + j * TILE, TILE), TILE)
@@ -222,7 +226,7 @@
 
 def phase(
     where, shapes, begin, groups, at=None, w=None,
-    weight=None, attn=None, before=None, out=None, squares=False,
+    weight=None, attn=None, before=None, out=None, squares=None, added=None,
 ):
     slots, capacity, features, rows = shapes
     do_w = at is not None
@@ -265,6 +269,8 @@
         out_specs.append(vmem)
     if attn == "last":
         add_vmem(before)
+    if squares == "added":
+        add_vmem(added)
     if attn == "first":
         outs.append(pltpu.VMEM((height, capacity), jnp.float32))
         out_specs.append(vmem)
@@ -398,7 +404,8 @@
     rows, features = out_grad.shape
     slots = attn_out.shape[0]
     devices, last = ring.devices, ring.length // 2
-    counts = [2] + [4] * (last - 2) + [2, 2, 1, 1]
+    steps = 2 * last
+    spans = [(2 * i, 2) for i in range(steps)]
     me = lax.axis_index("dp").astype(jnp.int32).reshape(1)
     where = (jnp.asarray(ring.owners()), me, head_counts)
     shapes = (slots, o_weight.shape[0], features, rows)
@@ -411,42 +418,43 @@
         return [send(x, ring.swap()) for x in halves]
 
     def grouped(*pairs):
-        return [(c * half, half, 0, [(x[c], 0, rows) for x in pairs]) for c in range(2)]
+        return [
+            (c * half, half, 0, [(x[c], 0, rows) for x in pairs])
+            for c in range(min(len(x) for x in pairs))
+        ]
 
     own = live_rows(seq_counts, me, out_grad)
     x = send(own, ring.along())
-    own, near, ats = prepared(where, own, attn_out, counts)
+    own, near, ats = prepared(where, own, attn_out, spans)
     y = send(own, ring.crossing())
     w, out, done = phase(
         where, shapes, 0, grouped(near, swapped(near)), at=ats[0], weight=weight, attn="whole"
     )
-
-    def dots(k, *pairs):
-        return phase(
-            where, shapes, sum(counts[:k]), grouped(*pairs), at=ats[k], w=w,
-            weight=weight, attn="whole", out=out,
-        )
 
     for k in range(1, last):
         (x,) = after(done, x)
         x, near_x = send(x, ring.along()), split(x)
         far_x = swapped(near_x)
-        if k == last - 1:
-            w, out, done = dots(k, near_x, far_x)
+        i, groups = 2 * k - 1, grouped(near_x, far_x)
+        w, done = phase(where, shapes, 2 * i, groups, at=ats[i], w=w)
         (y,) = after(done, y)
         y, near_y = send(y, ring.along()) if k < last - 1 else None, split(y)
         far_y = swapped(near_y)
-        if k < last - 1:
-            w, out, done = dots(k, near_x, far_x, near_y, far_y)
-        else:
-            w, out, done = dots(k + 1, near_y, far_y)
-
-    (x,) = after(done, x)
+        i, groups = 2 * k, grouped(near_y, far_y)
+        w, added = phase(where, shapes, 2 * i, groups, at=ats[i], w=w)
+        groups = grouped(near_x, far_x, near_y, far_y)
+        out, done = phase(
+            where, shapes, 2 * i - 2, groups, weight=weight, attn="whole", out=out
+        )
+
+    x, _ = after(done, x, added)
     near = split(x)
     far = swapped(near)
-    begin = sum(counts[:-2])
-    w, done = phase(where, shapes, begin, grouped(near), at=ats[-2], w=w)
-    w, squares = phase(where, shapes, begin, grouped(far), at=ats[-1], w=w, squares=True)
+    begin, groups = 2 * steps - 2, grouped(near, far)
+    w, squares = phase(where, shapes, begin, groups[:1], at=ats[-1], w=w, squares="new")
+    w, squares = phase(
+        where, shapes, begin, groups[1:], at=ats[-1], w=w, squares="added", added=squares
+    )
 
     stride, late = 1, 0
     while stride < devices:

time: 122 us -> 123 us (level)
  waiting for transfers between devices: 22 us -> 18.6 us
  Pallas kernels: 70.4 us -> 73.6 us
    ppermute x23, waiting for transfers between devices: 20.9 us -> 16.7 us  [send(): return lax.ppermute(x, 'dp', pairs)]
    pallas_call x9 -> x14, Pallas kernels: 61.3 us -> 64.5 us  [phase(): pl.pallas_call(functools.partial(phase_kernel, spec), in_specs=specs, out...]
  transfers between devices with their start and end apart: 29 -> 29, of which waited for: 15 -> 14; matrix products, arithmetic and copies ran while one was open for 0% -> 0% of each run, Pallas kernels for 51% -> 54%
where the time goes in v8:
time: 123 us; the launch traced here: 122 us
  Pallas kernels  73.6 us (60%)
  starting transfers between devices  27 us (22%)
  waiting for transfers between devices  18.6 us (15%)
  between operations  2.45 us (2%)
    pallas_call x14, Pallas kernels, phase(): pl.pallas_call(functools.partial(phase_kernel, spec), in_specs=specs, out...  64.5 us
    ppermute x23, starting transfers between devices, send(): return lax.ppermute(x, 'dp', pairs)  20 us
    ppermute x23, waiting for transfers between devices, send(): return lax.ppermute(x, 'dp', pairs)  16.7 us
    ppermute x6, starting transfers between devices, exchange(): total = total + lax.ppermute(x, 'dp', pairs)  6.99 us
    pallas_call x1, Pallas kernels, prepared(): pl.pallas_call(functools.partial(prep_kernel, spans, rows), in_specs=[sme...  3.93 us
    pallas_call x1, Pallas kernels, scaled(): pl.pallas_call(functools.partial(scale_kernel, parts), in_specs=[vmem, vm...  3 us
  transfers between devices with their start and end apart: 29, of which 14 were waited for; matrix products, arithmetic and copies ran while one was open for 0% of the time, Pallas kernels for 54%

profile of v8, /device:TPU:0, one launch (start us, length us, event | category | flops | bytes accessed | tf_op | source)
XLA Modules:
  0.0 122.3 jit_solution(4131545668448011777)
XLA Ops:
  1.3 1.4 %live.1.own_ref = bf16[144,4096]{1,0:T(8,128)(2,1)S(1)} custom-call(s32[1]{0:T(128)S(6)} %copy.51.seqs_ref, s32[1]{0:T(128)} %bitcast.me_ref.refs_1_, bf16[144,4096]{1,0:T(8,128)(2,1)} %grad_ref.1), custom_call_target="tpu_custom_call" | custom-call | tf_op jit(solution)/shard_map/live/pallas_call | solution.py:78
  2.7 3.1 %collective-permute-start = (bf16[144,4096]{1,0:T(8,128)(2,1)S(1)}, bf16[144,4096]{1,0:T(8,128)(2,1)S(1)}, u32[]{:S(2)}, u32[]{:S(2)}) collective-permute-start(bf16[144,4096]{1,0:T(8,128)(2,1)S(1)} %live.1.own_ref), channel_id=1, source_target_pairs={{0,4},{1,3},{4,8},{5,1},{8,12},{9,5},{12,14},{13,9},{14,10},{15,13... | collective-permute-start | bytes 3538952 | tf_op jit(solution)/shard_map/ppermute | solution.py:415
  6.5 0.7 copy-done.1
  7.2 3.9 %prep.1 = (bf16[144,4096]{1,0:T(8,128)(2,1)S(1)}, bf16[144,2048]{1,0:T(8,128)(2,1)S(1)}, bf16[144,2048]{1,0:T(8,128)(2,1)S(1)}, bf16[768,288]{1,0:T(8,128)(2,1)S...) custom-call(s32[16,16]{1,0:T(8,128)S(1)} %copy-done.1, ...), custom_call_target="tpu_custom_call" | custom-call | flops 1 | bytes 1 | tf_op jit(solution)/shard_map/prep/pallas_call | solution.py:130
  11.1 0.1 collective-permute-start.1
  11.2 0.5 collective-permute-start.2
  11.7 0.7 collective-permute-start.5
  12.4 0.8 collective-permute-done.1.refs_6_
  13.2 0.8 collective-permute-done.2.refs_8_
  14.0 7.2 %phase_w_whole.1 = (f32[768,4096]{1,0:T(8,128)S(1)}, bf16[2304,768]{1,0:T(8,128)(2,1)}, f32[8,128]{1,0:T(8,128)S(1)}) custom-call(s32[16,16]{1,0:T(8,128)S(1)} %copy-done.1, s32[1]{0:T(128)} %bitcast.me_ref.refs_1_, s32[1]{0:T(128)S(6)} %copy.50.heads_ref.refs_2_, bf16[768,288]{1,0:T(8,128)(2,1)S(1)} %get-tuple-element.54.refs_3_, ...), custom_call_target="tpu_custom_call" | custom-call | flops 1 | bytes 1 | tf_op jit(solution)/shard_map/phase_w_whole/pallas_call | solution.py:294
  21.3 4.0 %collective-permute-done.refs_0_ = bf16[144,4096]{1,0:T(8,128)(2,1)S(1)} collective-permute-done((bf16[144,4096]{1,0:T(8,128)(2,1)S(1)}, bf16[144,4096]{1,0:T(8,128)(2,1)S(1)}, u32[]{:S(2)}, u32[]{:S(2)}) %collective-permute-start) | collective-permute-done | bytes 1179680 | tf_op jit(solution)/shard_map/ppermute | solution.py:415
  25.3 0.1 split.7
  25.4 0.1 collective-permute-start.4
  25.5 0.5 collective-permute-start.6
  26.0 2.5 %collective-permute-start.3 = (bf16[144,4096]{1,0:T(8,128)(2,1)S(1)}, bf16[144,4096]{1,0:T(8,128)(2,1)S(1)}, u32[]{:S(2)}, u32[]{:S(2)}) collective-permute-start(bf16[144,4096]{1,0:T(8,128)(2,1)S(1)} %after.8.x_ref), channel_id=1, source_target_pairs={{0,4},{1,3},{4,8},{5,1},{8,12},{9,5},{12,14},{13,9},{14,10},{15,13... | collective-permute-start | bytes 3538952 | tf_op jit(solution)/shard_map/ppermute | solution.py:415
  28.4 4.6 %phase_w_None.8 = (f32[768,4096]{1,0:T(8,128)S(1)}, f32[8,128]{1,0:T(8,128)S(1)}) custom-call(s32[16,16]{1,0:T(8,128)S(1)} %copy-done.1, s32[1]{0:T(128)} %bitcast.me_ref.refs_1_, s32[1]{0:T(128)S(6)} %copy.50.heads_ref.refs_2_, bf16[768,288]{1,0:T(8,128)(2,1)S(1)} %get-tuple-element.60.refs_3_, ...), custom_call_target="tpu_custom_call", output_to_operand_aliasing={{0}: (8, {})} | custom-call | flops 1 | bytes 1 | tf_op jit(solution)/shard_map/phase_w_None/pallas_call | solution.py:294
  33.0 1.3 %collective-permute-done.5.refs_0_ = bf16[144,4096]{1,0:T(8,128)(2,1)S(1)} collective-permute-done((bf16[144,4096]{1,0:T(8,128)(2,1)S(1)}, bf16[144,4096]{1,0:T(8,128)(2,1)S(1)}, u32[]{:S(2)}, u32[]{:S(2)}) %collective-permute-start.5) | collective-permute-done | bytes 1179680 | tf_op jit(solution)/shard_map/ppermute | solution.py:415
  34.3 0.1 split.8
  34.4 0.6 collective-permute-start.7
  35.1 0.1 collective-permute-start.8
  35.2 2.8 %collective-permute-start.11 = (bf16[144,4096]{1,0:T(8,128)(2,1)S(1)}, bf16[144,4096]{1,0:T(8,128)(2,1)S(1)}, u32[]{:S(2)}, u32[]{:S(2)}) collective-permute-start(bf16[144,4096]{1,0:T(8,128)(2,1)S(1)} %after.9.x_ref), channel_id=1, source_target_pairs={{0,4},{1,3},{4,8},{5,1},{8,12},{9,5},{12,14},{13,9},{14,10},{15,13... | collective-permute-start | bytes 3538952 | tf_op jit(solution)/shard_map/ppermute | solution.py:415
  38.0 6.3 %phase__whole.3 = (bf16[2304,768]{1,0:T(8,128)(2,1)}, f32[8,128]{1,0:T(8,128)S(1)}) custom-call(s32[16,16]{1,0:T(8,128)S(1)} %copy-done.1, s32[1]{0:T(128)} %bitcast.me_ref.refs_1_, s32[1]{0:T(128)S(6)} %copy.50.heads_ref.refs_2_, bf16[768,4096]{1,0:T(8,128)(2,1)S(1)} %copy-done, ...), custom_call_target="tpu_custom_call", output_to_operand_aliasing={{0}: (12, {})} | custom-call | flops 1 | bytes 1 | tf_op jit(solution)/shard_map/phase__whole/pallas_call | solution.py:294
  44.3 1.0 collective-permute-done.3.refs_0_
  45.2 0.1 split.9
  45.4 0.5 collective-permute-start.12
  45.9 2.1 %collective-permute-start.9 = (bf16[144,4096]{1,0:T(8,128)(2,1)S(1)}, bf16[144,4096]{1,0:T(8,128)(2,1)S(1)}, u32[]{:S(2)}, u32[]{:S(2)}) collective-permute-start(bf16[144,4096]{1,0:T(8,128)(2,1)S(1)} %after.10.x_ref), channel_id=1, source_target_pairs={{0,4},{1,3},{4,8},{5,1},{8,12},{9,5},{12,14},{13,9},{14,10},{15,13... | collective-permute-start | bytes 3538952 | tf_op jit(solution)/shard_map/ppermute | solution.py:415
  48.0 4.6 %phase_w_None.9 = (f32[768,4096]{1,0:T(8,128)S(1)}, f32[8,128]{1,0:T(8,128)}) custom-call(s32[16,16]{1,0:T(8,128)S(1)} %copy-done.1, s32[1]{0:T(128)} %bitcast.me_ref.refs_1_, s32[1]{0:T(128)S(6)} %copy.50.heads_ref.refs_2_, bf16[768,288]{1,0:T(8,128)(2,1)S(1)} %get-tuple-element.71.refs_3_, ...), custom_call_target="tpu_custom_call", output_to_operand_aliasing={{0}: (8, {})} | custom-call | flops 1 | bytes 1 | tf_op jit(solution)/shard_map/phase_w_None/pallas_call | solution.py:294
  52.6 4.6 %phase_w_None.10 = (f32[768,4096]{1,0:T(8,128)S(1)}, f32[8,128]{1,0:T(8,128)S(1)}) custom-call(s32[16,16]{1,0:T(8,128)S(1)} %copy-done.1, s32[1]{0:T(128)} %bitcast.me_ref.refs_1_, s32[1]{0:T(128)S(6)} %copy.50.heads_ref.refs_2_, bf16[768,288]{1,0:T(8,128)(2,1)S(1)} %get-tuple-element.69.refs_3_, ...), custom_call_target="tpu_custom_call", output_to_operand_aliasing={{0}: (8, {})} | custom-call | flops 1 | bytes 1 | tf_op jit(solution)/shard_map/phase_w_None/pallas_call | solution.py:294
  57.2 0.7 collective-permute-done.11.refs_0_
  57.9 0.1 split.10
  58.0 0.5 collective-permute-start.14
  58.5 2.1 %collective-permute-start.16 = (bf16[144,4096]{1,0:T(8,128)(2,1)S(1)}, bf16[144,4096]{1,0:T(8,128)(2,1)S(1)}, u32[]{:S(2)}, u32[]{:S(2)}) collective-permute-start(bf16[144,4096]{1,0:T(8,128)(2,1)S(1)} %after.11.x_ref), channel_id=1, source_target_pairs={{0,4},{1,3},{4,8},{5,1},{8,12},{9,5},{12,14},{13,9},{14,10},{15,13... | collective-permute-start | bytes 3538952 | tf_op jit(solution)/shard_map/ppermute | solution.py:415
  60.6 0.2 collective-permute-done.14.refs_11_.refs_7_
  60.9 6.3 %phase__whole.4 = (bf16[2304,768]{1,0:T(8,128)(2,1)}, f32[8,128]{1,0:T(8,128)S(1)}) custom-call(s32[16,16]{1,0:T(8,128)S(1)} %copy-done.1, s32[1]{0:T(128)} %bitcast.me_ref.refs_1_, s32[1]{0:T(128)S(6)} %copy.50.heads_ref.refs_2_, bf16[768,4096]{1,0:T(8,128)(2,1)S(1)} %copy-done, ...), custom_call_target="tpu_custom_call", output_to_operand_aliasing={{0}: (12, {})} | custom-call | flops 1 | bytes 1 | tf_op jit(solution)/shard_map/phase__whole/pallas_call | solution.py:294
  67.2 3.3 %collective-permute-done.9.refs_0_ = bf16[144,4096]{1,0:T(8,128)(2,1)S(1)} collective-permute-done((bf16[144,4096]{1,0:T(8,128)(2,1)S(1)}, bf16[144,4096]{1,0:T(8,128)(2,1)S(1)}, u32[]{:S(2)}, u32[]{:S(2)}) %collective-permute-start.9) | collective-permute-done | bytes 1179680 | tf_op jit(solution)/shard_map/ppermute | solution.py:415
  70.5 0.1 split.11
  70.7 0.5 collective-permute-start.18
  71.2 2.1 %collective-permute-start.15 = (bf16[144,4096]{1,0:T(8,128)(2,1)S(1)}, bf16[144,4096]{1,0:T(8,128)(2,1)S(1)}, u32[]{:S(2)}, u32[]{:S(2)}) collective-permute-start(bf16[144,4096]{1,0:T(8,128)(2,1)S(1)} %after.12.x_ref), channel_id=1, source_target_pairs={{0,4},{1,3},{4,8},{5,1},{8,12},{9,5},{12,14},{13,9},{14,10},{15,13... | collective-permute-start | bytes 3538952 | tf_op jit(solution)/shard_map/ppermute | solution.py:415
  73.3 4.6 %phase_w_None.11 = (f32[768,4096]{1,0:T(8,128)S(1)}, f32[8,128]{1,0:T(8,128)}) custom-call(s32[16,16]{1,0:T(8,128)S(1)} %copy-done.1, s32[1]{0:T(128)} %bitcast.me_ref.refs_1_, s32[1]{0:T(128)S(6)} %copy.50.heads_ref.refs_2_, bf16[768,288]{1,0:T(8,128)(2,1)S(1)} %get-tuple-element.83.refs_3_, ...), custom_call_target="tpu_custom_call", output_to_operand_aliasing={{0}: (8, {})} | custom-call | flops 1 | bytes 1 | tf_op jit(solution)/shard_map/phase_w_None/pallas_call | solution.py:294
  77.9 4.6 %phase_w_None.12 = (f32[768,4096]{1,0:T(8,128)S(1)}, f32[8,128]{1,0:T(8,128)S(1)}) custom-call(s32[16,16]{1,0:T(8,128)S(1)} %copy-done.1, s32[1]{0:T(128)} %bitcast.me_ref.refs_1_, s32[1]{0:T(128)S(6)} %copy.50.heads_ref.refs_2_, bf16[768,288]{1,0:T(8,128)(2,1)S(1)} %get-tuple-element.80.refs_3_, ...), custom_call_target="tpu_custom_call", output_to_operand_aliasing={{0}: (8, {})} | custom-call | flops 1 | bytes 1 | tf_op jit(solution)/shard_map/phase_w_None/pallas_call | solution.py:294
  82.5 0.7 collective-permute-done.16.refs_0_
  83.1 0.1 split.12
  83.2 0.1 collective-permute-start.19
  83.3 0.5 collective-permute-start.20
  83.8 1.5 %collective-permute-done.19.refs_5_.refs_7_ = bf16[144,2048]{1,0:T(8,128)(2,1)S(1)} collective-permute-done((bf16[144,2048]{1,0:T(8,128)(2,1)S(1)}, bf16[144,2048]{1,0:T(8,128)(2,1)S(1)}, u32[]{:S(2)}, u32[]{:S(2)}) %collective-permute-start.19) | collective-permute-done | bytes 589856 | tf_op jit(solution)/shard_map/ppermute | solution.py:415
  85.3 0.8 collective-permute-done.20.refs_7_.refs_11_
  86.2 6.3 %phase__whole.5 = (bf16[2304,768]{1,0:T(8,128)(2,1)}, f32[8,128]{1,0:T(8,128)S(1)}) custom-call(s32[16,16]{1,0:T(8,128)S(1)} %copy-done.1, s32[1]{0:T(128)} %bitcast.me_ref.refs_1_, s32[1]{0:T(128)S(6)} %copy.50.heads_ref.refs_2_, bf16[768,4096]{1,0:T(8,128)(2,1)S(1)} %copy-done, ...), custom_call_target="tpu_custom_call", output_to_operand_aliasing={{0}: (12, {})} | custom-call | flops 1 | bytes 1 | tf_op jit(solution)/shard_map/phase__whole/pallas_call | solution.py:294
  92.5 4.6 %phase_w_None.13 = (f32[768,4096]{1,0:T(8,128)S(1)}, f32[8,128]{1,0:T(8,128)S(1)}) custom-call(s32[16,16]{1,0:T(8,128)S(1)} %copy-done.1, s32[1]{0:T(128)} %bitcast.me_ref.refs_1_, s32[1]{0:T(128)S(6)} %copy.50.heads_ref.refs_2_, bf16[768,288]{1,0:T(8,128)(2,1)S(1)} %get-tuple-element.79.refs_3_, ...), custom_call_target="tpu_custom_call", output_to_operand_aliasing={{0}: (8, {})} | custom-call | flops 1 | bytes 1 | tf_op jit(solution)/shard_map/phase_w_None/pallas_call | solution.py:294
  97.1 0.1 split.13
  97.2 0.2 collective-permute-start.22
  97.4 0.4 collective-permute-start.21
  97.8 1.5 %collective-permute-done.22.refs_5_ = bf16[144,2048]{1,0:T(8,128)(2,1)S(1)} collective-permute-done((bf16[144,2048]{1,0:T(8,128)(2,1)S(1)}, bf16[144,2048]{1,0:T(8,128)(2,1)S(1)}, u32[]{:S(2)}, u32[]{:S(2)}) %collective-permute-start.22) | collective-permute-done | bytes 589856 | tf_op jit(solution)/shard_map/ppermute | solution.py:415
  99.3 2.7 %phase_w_None.14 = (f32[768,4096]{1,0:T(8,128)S(1)}, f32[8,128]{1,0:T(8,128)S(1)}) custom-call(s32[16,16]{1,0:T(8,128)S(1)} %copy-done.1, s32[1]{0:T(128)} %bitcast.me_ref.refs_1_, s32[1]{0:T(128)S(6)} %copy.50.heads_ref.refs_2_, bf16[768,288]{1,0:T(8,128)(2,1)S(1)} %get-tuple-element.99.refs_3_, ...), custom_call_target="tpu_custom_call", output_to_operand_aliasing={{0}: (6, {})} | custom-call | flops 1 | bytes 1 | tf_op jit(solution)/shard_map/phase_w_None/pallas_call | solution.py:294
  102.0 2.7 %phase_w_None.15 = (f32[768,4096]{1,0:T(8,128)S(1)}, f32[8,128]{1,0:T(8,128)S(1)}) custom-call(s32[16,16]{1,0:T(8,128)S(1)} %copy-done.1, s32[1]{0:T(128)} %bitcast.me_ref.refs_1_, s32[1]{0:T(128)S(6)} %copy.50.heads_ref.refs_2_, bf16[768,288]{1,0:T(8,128)(2,1)S(1)} %get-tuple-element.99.refs_3_, ...), custom_call_target="tpu_custom_call", output_to_operand_aliasing={{0}: (6, {})} | custom-call | flops 1 | bytes 1 | tf_op jit(solution)/shard_map/phase_w_None/pallas_call | solution.py:294
  104.7 1.8 %collective-permute-start.25 = (f32[8,128]{1,0:T(8,128)S(1)}, f32[8,128]{1,0:T(8,128)S(1)}, u32[]{:S(2)}, u32[]{:S(2)}) collective-permute-start(f32[8,128]{1,0:T(8,128)S(1)} %get-tuple-element.104), channel_id=1, source_target_pairs={{0,3},{1,0},{2,1},{3,2},{4,7},{5,4},{6,5},{7,6},{8,11},{9,8},{10,9... | collective-permute-start | bytes 12296 | tf_op jit(solution)/shard_map/ppermute | solution.py:399
  106.5 0.3 collective-permute-start.24
  106.8 0.2 collective-permute-start.23
  107.0 2.0 %phase__first.1 = (f32[288,768]{1,0:T(8,128)S(1)}, f32[8,128]{1,0:T(8,128)S(1)}) custom-call(s32[16,16]{1,0:T(8,128)S(1)} %copy-done.1, s32[1]{0:T(128)} %bitcast.me_ref.refs_1_, s32[1]{0:T(128)S(6)} %copy.50.heads_ref.refs_2_, bf16[768,4096]{1,0:T(8,128)(2,1)S(1)} %copy-done, bf16[144,2048]{1,0:T(8,128)(2,1)S(1)} %get-tuple-element.95.refs_4_, ...), custom_call_target="tpu_custom_call" | custom-call | flops 1 | bytes 1 | tf_op jit(solution)/shard_map/phase__first/pallas_call | solution.py:294
  109.0 1.1 collective-permute-done.24
  110.1 3.6 %collective-permute-start.28 = (f32[8,128]{1,0:T(8,128)S(1)}, f32[8,128]{1,0:T(8,128)S(1)}, u32[]{:S(2)}, u32[]{:S(2)}) collective-permute-start(f32[8,128]{1,0:T(8,128)S(1)} %after.15), channel_id=1, source_target_pairs={{0,12},{1,13},{2,14},{3,15},{4,0},{5,1},{6,2},{7,3},{8,4},{9,5},{1... | collective-permute-start | bytes 12296 | tf_op jit(solution)/shard_map/ppermute | solution.py:399
  113.8 1.0 collective-permute-start.26
  114.8 3.5 %phase__last.1 = (bf16[2304,768]{1,0:T(8,128)(2,1)}, f32[8,128]{1,0:T(8,128)}) custom-call(s32[16,16]{1,0:T(8,128)S(1)} %copy-done.1, s32[1]{0:T(128)} %bitcast.me_ref.refs_1_, s32[1]{0:T(128)S(6)} %copy.50.heads_ref.refs_2_, bf16[768,4096]{1,0:T(8,128)(2,1)S(1)} %copy-done, ...), custom_call_target="tpu_custom_call", output_to_operand_aliasing={{0}: (7, {})} | custom-call | flops 1 | bytes 1 | tf_op jit(solution)/shard_map/phase__last/pallas_call | solution.py:294
  118.3 0.9 collective-permute-done.26
  119.2 3.0 %scale.1 = bf16[768,4096]{1,0:T(8,128)(2,1)} custom-call(f32[768,4096]{1,0:T(8,128)S(1)} %get-tuple-element.103.w_ref, f32[8,128]{1,0:T(8,128)S(1)} %add_add_fusion.squares_ref), custom_call_target="tpu_custom_call" | custom-call | flops 3145728 | bytes 6291456 | tf_op jit(solution)/shard_map/scale/pallas_call | solution.py:334
  (32 shorter events, 0.3 us)
Async XLA Ops:
  1.3 12.7 %copy-start = (bf16[768,4096]{1,0:T(8,128)(2,1)S(1)}, bf16[768,4096]{1,0:T(8,128)(2,1)}, u32[]{:S(2)}) copy-start(bf16[768,4096]{1,0:T(8,128)(2,1)} %refs_3_.9) | copy-start | bytes 18874372
  2.7 22.5 %collective-permute-start = (bf16[144,4096]{1,0:T(8,128)(2,1)S(1)}, bf16[144,4096]{1,0:T(8,128)(2,1)S(1)}, u32[]{:S(2)}, u32[]{:S(2)}) collective-permute-start(bf16[144,4096]{1,0:T(8,128)(2,1)S(1)} %live.1.own_ref), channel_id=1, source_target_pairs={{0,4},{1,3},{4,8},{5,1},{8,12},{9,5},{12,14},{13,9},{14,10},{15,13... | collective-permute-start | bytes 3538952 | tf_op jit(solution)/shard_map/ppermute | solution.py:415
  6.5 0.7 copy-start.1
  11.1 2.1 %collective-permute-start.1 = (bf16[144,2048]{1,0:T(8,128)(2,1)S(1)}, bf16[144,2048]{1,0:T(8,128)(2,1)S(1)}, u32[]{:S(2)}, u32[]{:S(2)}) collective-permute-start(bf16[144,2048]{1,0:T(8,128)(2,1)S(1)} %get-tuple-element.55.refs_5_), channel_id=1, source_target_pairs={{0,1},{1,0},{2,3},{3,2},{4,5},{5,4},{6,7},{7,6},{8,9},{9,8},{10,11... | collective-permute-start | bytes 1769480 | tf_op jit(solution)/shard_map/ppermute | solution.py:415
  11.2 2.8 %collective-permute-start.2 = (bf16[144,2048]{1,0:T(8,128)(2,1)S(1)}, bf16[144,2048]{1,0:T(8,128)(2,1)S(1)}, u32[]{:S(2)}, u32[]{:S(2)}) collective-permute-start(bf16[144,2048]{1,0:T(8,128)(2,1)S(1)} %get-tuple-element.56.refs_7_), channel_id=1, source_target_pairs={{0,1},{1,0},{2,3},{3,2},{4,5},{5,4},{6,7},{7,6},{8,9},{9,8},{10,11... | collective-permute-start | bytes 1769480 | tf_op jit(solution)/shard_map/ppermute | solution.py:415
  11.7 22.6 %collective-permute-start.5 = (bf16[144,4096]{1,0:T(8,128)(2,1)S(1)}, bf16[144,4096]{1,0:T(8,128)(2,1)S(1)}, u32[]{:S(2)}, u32[]{:S(2)}) collective-permute-start(bf16[144,4096]{1,0:T(8,128)(2,1)S(1)} %get-tuple-element.59), channel_id=1, source_target_pairs={{0,3},{1,4},{4,1},{5,8},{8,5},{9,12},{12,9},{13,14},{14,13},{15,10... | collective-permute-start | bytes 3538952 | tf_op jit(solution)/shard_map/ppermute | solution.py:415
  25.4 3.1 %collective-permute-start.4 = (bf16[144,2048]{1,0:T(8,128)(2,1)S(1)}, bf16[144,2048]{1,0:T(8,128)(2,1)S(1)}, u32[]{:S(2)}, u32[]{:S(2)}) collective-permute-start(bf16[144,2048]{1,0:T(8,128)(2,1)S(1)} %get-tuple-element.58.refs_4_), channel_id=1, source_target_pairs={{0,1},{1,0},{2,3},{3,2},{4,5},{5,4},{6,7},{7,6},{8,9},{9,8},{10,11... | collective-permute-start | bytes 1769480 | tf_op jit(solution)/shard_map/ppermute | solution.py:415
  25.5 3.0 %collective-permute-start.6 = (bf16[144,2048]{1,0:T(8,128)(2,1)S(1)}, bf16[144,2048]{1,0:T(8,128)(2,1)S(1)}, u32[]{:S(2)}, u32[]{:S(2)}) collective-permute-start(bf16[144,2048]{1,0:T(8,128)(2,1)S(1)} %get-tuple-element.61.refs_6_.refs_8_), channel_id=1, source_target_pairs={{0,1},{1,0},{2,3},{3,2},{4,5},{5,4},{6,7},{7,6},{8,9},{9,8},{10,11... | collective-permute-start | bytes 1769480 | tf_op jit(solution)/shard_map/ppermute | solution.py:415
  26.0 19.3 %collective-permute-start.3 = (bf16[144,4096]{1,0:T(8,128)(2,1)S(1)}, bf16[144,4096]{1,0:T(8,128)(2,1)S(1)}, u32[]{:S(2)}, u32[]{:S(2)}) collective-permute-start(bf16[144,4096]{1,0:T(8,128)(2,1)S(1)} %after.8.x_ref), channel_id=1, source_target_pairs={{0,4},{1,3},{4,8},{5,1},{8,12},{9,5},{12,14},{13,9},{14,10},{15,13... | collective-permute-start | bytes 3538952 | tf_op jit(solution)/shard_map/ppermute | solution.py:415
  34.4 3.5 %collective-permute-start.7 = (bf16[144,2048]{1,0:T(8,128)(2,1)S(1)}, bf16[144,2048]{1,0:T(8,128)(2,1)S(1)}, u32[]{:S(2)}, u32[]{:S(2)}) collective-permute-start(bf16[144,2048]{1,0:T(8,128)(2,1)S(1)} %get-tuple-element.64.refs_6_.refs_4_), channel_id=1, source_target_pairs={{0,1},{1,0},{2,3},{3,2},{4,5},{5,4},{6,7},{7,6},{8,9},{9,8},{10,11... | collective-permute-start | bytes 1769480 | tf_op jit(solution)/shard_map/ppermute | solution.py:415
  35.1 2.9 %collective-permute-start.8 = (bf16[144,2048]{1,0:T(8,128)(2,1)S(1)}, bf16[144,2048]{1,0:T(8,128)(2,1)S(1)}, u32[]{:S(2)}, u32[]{:S(2)}) collective-permute-start(bf16[144,2048]{1,0:T(8,128)(2,1)S(1)} %get-tuple-element.65.refs_10_.refs_6_), channel_id=1, source_target_pairs={{0,1},{1,0},{2,3},{3,2},{4,5},{5,4},{6,7},{7,6},{8,9},{9,8},{10,11... | collective-permute-start | bytes 1769480 | tf_op jit(solution)/shard_map/ppermute | solution.py:415
  35.2 22.7 %collective-permute-start.11 = (bf16[144,4096]{1,0:T(8,128)(2,1)S(1)}, bf16[144,4096]{1,0:T(8,128)(2,1)S(1)}, u32[]{:S(2)}, u32[]{:S(2)}) collective-permute-start(bf16[144,4096]{1,0:T(8,128)(2,1)S(1)} %after.9.x_ref), channel_id=1, source_target_pairs={{0,4},{1,3},{4,8},{5,1},{8,12},{9,5},{12,14},{13,9},{14,10},{15,13... | collective-permute-start | bytes 3538952 | tf_op jit(solution)/shard_map/ppermute | solution.py:415
  45.3 7.3 %collective-permute-start.10 = (bf16[144,2048]{1,0:T(8,128)(2,1)S(1)}, bf16[144,2048]{1,0:T(8,128)(2,1)S(1)}, u32[]{:S(2)}, u32[]{:S(2)}) collective-permute-start(bf16[144,2048]{1,0:T(8,128)(2,1)S(1)} %get-tuple-element.68.refs_4_), channel_id=1, source_target_pairs={{0,1},{1,0},{2,3},{3,2},{4,5},{5,4},{6,7},{7,6},{8,9},{9,8},{10,11... | collective-permute-start | bytes 1769480 | tf_op jit(solution)/shard_map/ppermute | solution.py:415
  45.4 7.2 %collective-permute-start.12 = (bf16[144,2048]{1,0:T(8,128)(2,1)S(1)}, bf16[144,2048]{1,0:T(8,128)(2,1)S(1)}, u32[]{:S(2)}, u32[]{:S(2)}) collective-permute-start(bf16[144,2048]{1,0:T(8,128)(2,1)S(1)} %get-tuple-element.70.refs_6_.refs_8_), channel_id=1, source_target_pairs={{0,1},{1,0},{2,3},{3,2},{4,5},{5,4},{6,7},{7,6},{8,9},{9,8},{10,11... | collective-permute-start | bytes 1769480 | tf_op jit(solution)/shard_map/ppermute | solution.py:415
  45.9 24.6 %collective-permute-start.9 = (bf16[144,4096]{1,0:T(8,128)(2,1)S(1)}, bf16[144,4096]{1,0:T(8,128)(2,1)S(1)}, u32[]{:S(2)}, u32[]{:S(2)}) collective-permute-start(bf16[144,4096]{1,0:T(8,128)(2,1)S(1)} %after.10.x_ref), channel_id=1, source_target_pairs={{0,4},{1,3},{4,8},{5,1},{8,12},{9,5},{12,14},{13,9},{14,10},{15,13... | collective-permute-start | bytes 3538952 | tf_op jit(solution)/shard_map/ppermute | solution.py:415
  58.0 2.7 %collective-permute-start.13 = (bf16[144,2048]{1,0:T(8,128)(2,1)S(1)}, bf16[144,2048]{1,0:T(8,128)(2,1)S(1)}, u32[]{:S(2)}, u32[]{:S(2)}) collective-permute-start(bf16[144,2048]{1,0:T(8,128)(2,1)S(1)} %get-tuple-element.75.refs_6_.refs_4_), channel_id=1, source_target_pairs={{0,1},{1,0},{2,3},{3,2},{4,5},{5,4},{6,7},{7,6},{8,9},{9,8},{10,11... | collective-permute-start | bytes 1769480 | tf_op jit(solution)/shard_map/ppermute | solution.py:415
  58.0 2.8 %collective-permute-start.14 = (bf16[144,2048]{1,0:T(8,128)(2,1)S(1)}, bf16[144,2048]{1,0:T(8,128)(2,1)S(1)}, u32[]{:S(2)}, u32[]{:S(2)}) collective-permute-start(bf16[144,2048]{1,0:T(8,128)(2,1)S(1)} %get-tuple-element.76.refs_10_.refs_6_), channel_id=1, source_target_pairs={{0,1},{1,0},{2,3},{3,2},{4,5},{5,4},{6,7},{7,6},{8,9},{9,8},{10,11... | collective-permute-start | bytes 1769480 | tf_op jit(solution)/shard_map/ppermute | solution.py:415
  58.5 24.6 %collective-permute-start.16 = (bf16[144,4096]{1,0:T(8,128)(2,1)S(1)}, bf16[144,4096]{1,0:T(8,128)(2,1)S(1)}, u32[]{:S(2)}, u32[]{:S(2)}) collective-permute-start(bf16[144,4096]{1,0:T(8,128)(2,1)S(1)} %after.11.x_ref), channel_id=1, source_target_pairs={{0,4},{1,3},{4,8},{5,1},{8,12},{9,5},{12,14},{13,9},{14,10},{15,13... | collective-permute-start | bytes 3538952 | tf_op jit(solution)/shard_map/ppermute | solution.py:415
  70.6 7.2 %collective-permute-start.17 = (bf16[144,2048]{1,0:T(8,128)(2,1)S(1)}, bf16[144,2048]{1,0:T(8,128)(2,1)S(1)}, u32[]{:S(2)}, u32[]{:S(2)}) collective-permute-start(bf16[144,2048]{1,0:T(8,128)(2,1)S(1)} %get-tuple-element.81.refs_4_), channel_id=1, source_target_pairs={{0,1},{1,0},{2,3},{3,2},{4,5},{5,4},{6,7},{7,6},{8,9},{9,8},{10,11... | collective-permute-start | bytes 1769480 | tf_op jit(solution)/shard_map/ppermute | solution.py:415
  70.7 7.2 %collective-permute-start.18 = (bf16[144,2048]{1,0:T(8,128)(2,1)S(1)}, bf16[144,2048]{1,0:T(8,128)(2,1)S(1)}, u32[]{:S(2)}, u32[]{:S(2)}) collective-permute-start(bf16[144,2048]{1,0:T(8,128)(2,1)S(1)} %get-tuple-element.82.refs_6_.refs_8_), channel_id=1, source_target_pairs={{0,1},{1,0},{2,3},{3,2},{4,5},{5,4},{6,7},{7,6},{8,9},{9,8},{10,11... | collective-permute-start | bytes 1769480 | tf_op jit(solution)/shard_map/ppermute | solution.py:415
  71.2 25.9 %collective-permute-start.15 = (bf16[144,4096]{1,0:T(8,128)(2,1)S(1)}, bf16[144,4096]{1,0:T(8,128)(2,1)S(1)}, u32[]{:S(2)}, u32[]{:S(2)}) collective-permute-start(bf16[144,4096]{1,0:T(8,128)(2,1)S(1)} %after.12.x_ref), channel_id=1, source_target_pairs={{0,4},{1,3},{4,8},{5,1},{8,12},{9,5},{12,14},{13,9},{14,10},{15,13... | collective-permute-start | bytes 3538952 | tf_op jit(solution)/shard_map/ppermute | solution.py:415
  83.2 2.1 %collective-permute-start.19 = (bf16[144,2048]{1,0:T(8,128)(2,1)S(1)}, bf16[144,2048]{1,0:T(8,128)(2,1)S(1)}, u32[]{:S(2)}, u32[]{:S(2)}) collective-permute-start(bf16[144,2048]{1,0:T(8,128)(2,1)S(1)} %get-tuple-element.87.refs_4_.refs_6_), channel_id=1, source_target_pairs={{0,1},{1,0},{2,3},{3,2},{4,5},{5,4},{6,7},{7,6},{8,9},{9,8},{10,11... | collective-permute-start | bytes 1769480 | tf_op jit(solution)/shard_map/ppermute | solution.py:415
  83.3 2.8 %collective-permute-start.20 = (bf16[144,2048]{1,0:T(8,128)(2,1)S(1)}, bf16[144,2048]{1,0:T(8,128)(2,1)S(1)}, u32[]{:S(2)}, u32[]{:S(2)}) collective-permute-start(bf16[144,2048]{1,0:T(8,128)(2,1)S(1)} %get-tuple-element.88.refs_6_.refs_10_), channel_id=1, source_target_pairs={{0,1},{1,0},{2,3},{3,2},{4,5},{5,4},{6,7},{7,6},{8,9},{9,8},{10,11... | collective-permute-start | bytes 1769480 | tf_op jit(solution)/shard_map/ppermute | solution.py:415
  97.2 2.1 %collective-permute-start.22 = (bf16[144,2048]{1,0:T(8,128)(2,1)S(1)}, bf16[144,2048]{1,0:T(8,128)(2,1)S(1)}, u32[]{:S(2)}, u32[]{:S(2)}) collective-permute-start(bf16[144,2048]{1,0:T(8,128)(2,1)S(1)} %get-tuple-element.95.refs_4_), channel_id=1, source_target_pairs={{0,1},{1,0},{2,3},{3,2},{4,5},{5,4},{6,7},{7,6},{8,9},{9,8},{10,11... | collective-permute-start | bytes 1769480 | tf_op jit(solution)/shard_map/ppermute | solution.py:415
  97.4 4.5 %collective-permute-start.21 = (bf16[144,2048]{1,0:T(8,128)(2,1)S(1)}, bf16[144,2048]{1,0:T(8,128)(2,1)S(1)}, u32[]{:S(2)}, u32[]{:S(2)}) collective-permute-start(bf16[144,2048]{1,0:T(8,128)(2,1)S(1)} %get-tuple-element.94.refs_4_), channel_id=1, source_target_pairs={{0,1},{1,0},{2,3},{3,2},{4,5},{5,4},{6,7},{7,6},{8,9},{9,8},{10,11... | collective-permute-start | bytes 1769480 | tf_op jit(solution)/shard_map/ppermute | solution.py:415
  104.7 4.4 %collective-permute-start.25 = (f32[8,128]{1,0:T(8,128)S(1)}, f32[8,128]{1,0:T(8,128)S(1)}, u32[]{:S(2)}, u32[]{:S(2)}) collective-permute-start(f32[8,128]{1,0:T(8,128)S(1)} %get-tuple-element.104), channel_id=1, source_target_pairs={{0,3},{1,0},{2,1},{3,2},{4,7},{5,4},{6,5},{7,6},{8,11},{9,8},{10,9... | collective-permute-start | bytes 12296 | tf_op jit(solution)/shard_map/ppermute | solution.py:399
  106.5 3.6 %collective-permute-start.24 = (f32[8,128]{1,0:T(8,128)S(1)}, f32[8,128]{1,0:T(8,128)S(1)}, u32[]{:S(2)}, u32[]{:S(2)}) collective-permute-start(f32[8,128]{1,0:T(8,128)S(1)} %get-tuple-element.104), channel_id=1, source_target_pairs={{0,2},{1,3},{2,0},{3,1},{4,6},{5,7},{6,4},{7,5},{8,10},{9,11},{10,... | collective-permute-start | bytes 12296 | tf_op jit(solution)/shard_map/ppermute | solution.py:399
  106.8 3.3 %collective-permute-start.23 = (f32[8,128]{1,0:T(8,128)S(1)}, f32[8,128]{1,0:T(8,128)S(1)}, u32[]{:S(2)}, u32[]{:S(2)}) collective-permute-start(f32[8,128]{1,0:T(8,128)S(1)} %get-tuple-element.104), channel_id=1, source_target_pairs={{0,1},{1,2},{2,3},{3,0},{4,5},{5,6},{6,7},{7,4},{8,9},{9,10},{10,1... | collective-permute-start | bytes 12296 | tf_op jit(solution)/shard_map/ppermute | solution.py:399
  110.1 8.1 %collective-permute-start.28 = (f32[8,128]{1,0:T(8,128)S(1)}, f32[8,128]{1,0:T(8,128)S(1)}, u32[]{:S(2)}, u32[]{:S(2)}) collective-permute-start(f32[8,128]{1,0:T(8,128)S(1)} %after.15), channel_id=1, source_target_pairs={{0,12},{1,13},{2,14},{3,15},{4,0},{5,1},{6,2},{7,3},{8,4},{9,5},{1... | collective-permute-start | bytes 12296 | tf_op jit(solution)/shard_map/ppermute | solution.py:399
  113.8 4.5 %collective-permute-start.27 = (f32[8,128]{1,0:T(8,128)S(1)}, f32[8,128]{1,0:T(8,128)S(1)}, u32[]{:S(2)}, u32[]{:S(2)}) collective-permute-start(f32[8,128]{1,0:T(8,128)S(1)} %after.15), channel_id=1, source_target_pairs={{0,8},{1,9},{2,10},{3,11},{4,12},{5,13},{6,14},{7,15},{8,0},{9,1},... | collective-permute-start | bytes 12296 | tf_op jit(solution)/shard_map/ppermute | solution.py:399
  113.8 5.4 %collective-permute-start.26 = (f32[8,128]{1,0:T(8,128)S(1)}, f32[8,128]{1,0:T(8,128)S(1)}, u32[]{:S(2)}, u32[]{:S(2)}) collective-permute-start(f32[8,128]{1,0:T(8,128)S(1)} %after.15), channel_id=1, source_target_pairs={{0,4},{1,5},{2,6},{3,7},{4,8},{5,9},{6,10},{7,11},{8,12},{9,13},{1... | collective-permute-start | bytes 12296 | tf_op jit(solution)/shard_map/ppermute | solution.py:399

commit v9 on v8

--- a/solution.py
+++ b/solution.py
@@ -149,7 +149,7 @@
 
 
 def phase_kernel(spec, *refs):
-    groups, arrays, do_w, attn, fresh_w, fresh_out, squares, rows, begin = spec
+    groups, arrays, do_w, w_from, attn, fresh_w, fresh_out, squares, rows, begin = spec
     refs = list(refs)
     table_ref, me_ref, heads_ref = refs.pop(0), refs.pop(0), refs.pop(0)
     at_ref = refs.pop(0) if do_w else None
@@ -180,9 +180,9 @@
         here = pl.ds(pl.multiple_of(column + j * TILE, TILE), TILE)
         there = pl.ds(pl.multiple_of(first + j * TILE, TILE), TILE)
         g = [g_refs[i][start : start + count, here] for i, start, count in pieces]
-        g = jnp.concatenate(g, axis=0) if len(g) > 1 else g[0]
         if do_w:
-            w = jnp.dot(at_ref[...], g, preferred_element_type=jnp.float32)
+            fresh = jnp.concatenate(g[w_from:], axis=0) if len(g) > w_from + 1 else g[-1]
+            w = jnp.dot(at_ref[...], fresh, preferred_element_type=jnp.float32)
             if not fresh_w:
                 w = w + w_ref[:, there]
             w_ref[:, there] = w
@@ -194,7 +194,7 @@
             squares_ref[...] = total
         if attn:
             total_ref[...] += lax.dot_general(
-                g,
+                jnp.concatenate(g, axis=0),
                 weight_ref[:, there],
                 (((1,), (1,)), ((), ())),
                 preferred_element_type=jnp.float32,
@@ -227,6 +227,7 @@
 def phase(
     where, shapes, begin, groups, at=None, w=None,
     weight=None, attn=None, before=None, out=None, squares=None, added=None,
+    w_from=0,
 ):
     slots, capacity, features, rows = shapes
     do_w = at is not None
@@ -288,7 +289,7 @@
     outs.append(pltpu.VMEM((8, 128), jnp.float32))
     out_specs.append(vmem)
     spec = (
-        tuple(described), len(arrays), do_w, attn, w is None, out is None,
+        tuple(described), len(arrays), do_w, w_from, attn, w is None, out is None,
         squares, rows, begin,
     )
     return pl.pallas_call(
@@ -389,14 +390,21 @@
     )(pltpu.with_memory_space_constraint(x, pltpu.VMEM))
 
 
-def exchange(x, devices, stride, radix):
+def rounds(devices):
+    bits = [1 << i for i in range(devices.bit_length() - 1)]
+    if len(bits) >= 4:
+        bits = bits[1:3] + [bits[0]] + bits[3:]
+    masks = []
+    while bits:
+        pair, bits = bits[:2], bits[2:]
+        masks.append(pair + [sum(pair)] if len(pair) == 2 else pair)
+    return masks
+
+
+def exchange(x, devices, masks):
     total = x
-    for shift in range(1, radix):
-        pairs = []
-        for d in range(devices):
-            digit = d // stride % radix
-            pairs.append((d, d + ((digit + shift) % radix - digit) * stride))
-        total = total + lax.ppermute(x, "dp", pairs)
+    for mask in masks:
+        total = total + lax.ppermute(x, "dp", [(d, d ^ mask) for d in range(devices)])
     return total
 
 
@@ -405,7 +413,11 @@
     slots = attn_out.shape[0]
     devices, last = ring.devices, ring.length // 2
     steps = 2 * last
-    spans = [(2 * i, 2) for i in range(steps)]
+    spans = [(0, 2)]
+    for k in range(1, last):
+        joint = k < last - 1
+        spans += [(4 * k - 2, 4), None] if joint else [(4 * k - 2, 2), (4 * k, 2)]
+    spans += [(2 * steps - 2, 1), (2 * steps - 1, 1)]
     me = lax.axis_index("dp").astype(jnp.int32).reshape(1)
     where = (jnp.asarray(ring.owners()), me, head_counts)
     shapes = (slots, o_weight.shape[0], features, rows)
@@ -425,7 +437,8 @@
 
     own = live_rows(seq_counts, me, out_grad)
     x = send(own, ring.along())
-    own, near, ats = prepared(where, own, attn_out, spans)
+    own, near, ats = prepared(where, own, attn_out, [x for x in spans if x])
+    ats = [ats.pop(0) if x else None for x in spans]
     y = send(own, ring.crossing())
     w, out, done = phase(
         where, shapes, 0, grouped(near, swapped(near)), at=ats[0], weight=weight, attn="whole"
@@ -435,41 +448,55 @@
         (x,) = after(done, x)
         x, near_x = send(x, ring.along()), split(x)
         far_x = swapped(near_x)
-        i, groups = 2 * k - 1, grouped(near_x, far_x)
-        w, done = phase(where, shapes, 2 * i, groups, at=ats[i], w=w)
+        i = 2 * k - 1
+        if k == last - 1:
+            held = held + [near_x, far_x]
+            w, out, done = phase(
+                where, shapes, 2 * (i + 1) - len(held), grouped(*held), at=ats[i], w=w,
+                w_from=len(held) - 2, weight=weight, attn="whole", out=out,
+            )
         (y,) = after(done, y)
         y, near_y = send(y, ring.along()) if k < last - 1 else None, split(y)
         far_y = swapped(near_y)
-        i, groups = 2 * k, grouped(near_y, far_y)
-        w, added = phase(where, shapes, 2 * i, groups, at=ats[i], w=w)
         groups = grouped(near_x, far_x, near_y, far_y)
-        out, done = phase(
-            where, shapes, 2 * i - 2, groups, weight=weight, attn="whole", out=out
-        )
-
-    x, _ = after(done, x, added)
+        if k == last - 1:
+            w, out, done = phase(
+                where, shapes, 2 * (i + 1), grouped(near_y, far_y), at=ats[i + 1], w=w,
+                weight=weight, attn="whole", out=out,
+            )
+        elif k == last - 2:
+            held = [near_x, far_x, near_y, far_y]
+            w, done = phase(where, shapes, 2 * i, groups, at=ats[i], w=w)
+        else:
+            w, out, done = phase(
+                where, shapes, 2 * i, groups, at=ats[i], w=w,
+                weight=weight, attn="whole", out=out,
+            )
+
+    (x,) = after(done, x)
     near = split(x)
     far = swapped(near)
-    begin, groups = 2 * steps - 2, grouped(near, far)
-    w, squares = phase(where, shapes, begin, groups[:1], at=ats[-1], w=w, squares="new")
-    w, squares = phase(
-        where, shapes, begin, groups[1:], at=ats[-1], w=w, squares="added", added=squares
-    )
-
-    stride, late = 1, 0
-    while stride < devices:
-        radix = min(4, devices // stride)
-        squares = exchange(squares, devices, stride, radix)
-        groups = grouped(near, far)[late : late + 1]
+    begin = 2 * steps - 2
+    w, done = phase(where, shapes, begin, grouped(near), at=ats[-2], w=w)
+    w, squares = phase(where, shapes, begin, grouped(far), at=ats[-1], w=w, squares="new")
+
+    pieces = [group[3] for group in grouped(near, far)]
+    parts = [
+        [(0, half, 0, pieces[0]), (half, half // 2, 0, pieces[1])],
+        [(half + half // 2, half // 2, half // 2, pieces[1])],
+    ]
+    for late, masks in enumerate(rounds(devices)):
+        squares = exchange(squares, devices, masks)
         if late == 0:
-            before, done = phase(where, shapes, begin, groups, weight=weight, attn="first")
+            before, done = phase(
+                where, shapes, begin, parts[0], weight=weight, attn="first"
+            )
             (squares,) = after(done, squares)
         elif late == 1:
             out, done = phase(
-                where, shapes, begin, groups, weight=weight, attn="last",
+                where, shapes, begin, parts[1], weight=weight, attn="last",
                 before=before, out=out,
             )
-        stride, late = stride * radix, late + 1
     return out, scaled(w, squares)
 
 

time: 123 us -> 119 us (0.967)
  Pallas kernels: 73.6 us -> 64.5 us
  waiting for transfers between devices: 18.6 us -> 25.5 us
  starting transfers between devices: 27 us -> 25.6 us
    pallas_call x14 -> x9, Pallas kernels: 64.5 us -> 55.4 us  [phase(): pl.pallas_call(functools.partial(phase_kernel, spec), in_specs=specs, out...]
    ppermute x23, waiting for transfers between devices: 16.7 us -> 24.6 us  [send(): return lax.ppermute(x, 'dp', pairs)]
  transfers between devices with their start and end apart: 29 -> 29, of which waited for: 14 -> 16; matrix products, arithmetic and copies ran while one was open for 0% -> 0% of each run, Pallas kernels for 54% -> 48%
where the time goes in v9:
time: 119 us
  Pallas kernels  64.5 us (54%)
  starting transfers between devices  25.6 us (22%)
  waiting for transfers between devices  25.5 us (21%)
  between operations  2.39 us (2%)
    pallas_call x9, Pallas kernels, phase(): pl.pallas_call(functools.partial(phase_kernel, spec), in_specs=specs, out...  55.4 us
    ppermute x23, waiting for transfers between devices, send(): return lax.ppermute(x, 'dp', pairs)  24.6 us
    ppermute x23, starting transfers between devices, send(): return lax.ppermute(x, 'dp', pairs)  19.1 us
    ppermute x6, starting transfers between devices, exchange(): lax.ppermute(x, 'dp', [(d, d ^ mask) for d in range(devices)])  6.5 us
    pallas_call x1, Pallas kernels, prepared(): pl.pallas_call(functools.partial(prep_kernel, spans, rows), in_specs=[sme...  3.95 us
    pallas_call x1, Pallas kernels, scaled(): pl.pallas_call(functools.partial(scale_kernel, parts), in_specs=[vmem, vm...  3 us
  transfers between devices with their start and end apart: 29, of which 16 were waited for; matrix products, arithmetic and copies ran while one was open for 0% of the time, Pallas kernels for 48%

profile of v9, /device:TPU:0, one launch (start us, length us, event | category | flops | bytes accessed | tf_op | source)
XLA Modules:
  0.0 118.7 jit_solution(16354862465417277091)
XLA Ops:
  1.3 1.4 %live.1.own_ref = bf16[144,4096]{1,0:T(8,128)(2,1)S(1)} custom-call(s32[1]{0:T(128)S(6)} %copy.45.seqs_ref, s32[1]{0:T(128)} %bitcast.me_ref.refs_1_, bf16[144,4096]{1,0:T(8,128)(2,1)} %grad_ref.1), custom_call_target="tpu_custom_call" | custom-call | tf_op jit(solution)/shard_map/live/pallas_call | solution.py:78
  2.7 3.1 %collective-permute-start = (bf16[144,4096]{1,0:T(8,128)(2,1)S(1)}, bf16[144,4096]{1,0:T(8,128)(2,1)S(1)}, u32[]{:S(2)}, u32[]{:S(2)}) collective-permute-start(bf16[144,4096]{1,0:T(8,128)(2,1)S(1)} %live.1.own_ref), channel_id=1, source_target_pairs={{0,4},{1,3},{4,8},{5,1},{8,12},{9,5},{12,14},{13,9},{14,10},{15,13... | collective-permute-start | bytes 3538952 | tf_op jit(solution)/shard_map/ppermute | solution.py:427
  6.5 0.7 copy-done.1
  7.2 3.9 %prep.1 = (bf16[144,4096]{1,0:T(8,128)(2,1)S(1)}, bf16[144,2048]{1,0:T(8,128)(2,1)S(1)}, bf16[144,2048]{1,0:T(8,128)(2,1)S(1)}, bf16[768,288]{1,0:T(8,128)(2,1)S...) custom-call(s32[16,16]{1,0:T(8,128)S(1)} %copy-done.1, ...), custom_call_target="tpu_custom_call" | custom-call | flops 1 | bytes 1 | tf_op jit(solution)/shard_map/prep/pallas_call | solution.py:130
  11.1 0.1 collective-permute-start.1
  11.2 0.5 collective-permute-start.2
  11.7 0.7 collective-permute-start.5
  12.4 0.8 collective-permute-done.1.refs_6_
  13.2 0.8 collective-permute-done.2.refs_8_
  14.0 7.3 %phase_w_whole.4 = (f32[768,4096]{1,0:T(8,128)S(1)}, bf16[2304,768]{1,0:T(8,128)(2,1)}, f32[8,128]{1,0:T(8,128)S(1)}) custom-call(s32[16,16]{1,0:T(8,128)S(1)} %copy-done.1, s32[1]{0:T(128)} %bitcast.me_ref.refs_1_, s32[1]{0:T(128)S(6)} %copy.44.heads_ref.refs_2_, bf16[768,288]{1,0:T(8,128)(2,1)S(1)} %get-tuple-element.46.refs_3_, ...), custom_call_target="tpu_custom_call" | custom-call | flops 1 | bytes 1 | tf_op jit(solution)/shard_map/phase_w_whole/pallas_call | solution.py:295
  21.3 3.9 %collective-permute-done.refs_0_ = bf16[144,4096]{1,0:T(8,128)(2,1)S(1)} collective-permute-done((bf16[144,4096]{1,0:T(8,128)(2,1)S(1)}, bf16[144,4096]{1,0:T(8,128)(2,1)S(1)}, u32[]{:S(2)}, u32[]{:S(2)}) %collective-permute-start) | collective-permute-done | bytes 1179680 | tf_op jit(solution)/shard_map/ppermute | solution.py:427
  25.2 0.1 split.7
  25.3 0.1 collective-permute-start.4
  25.4 2.5 %collective-permute-start.3 = (bf16[144,4096]{1,0:T(8,128)(2,1)S(1)}, bf16[144,4096]{1,0:T(8,128)(2,1)S(1)}, u32[]{:S(2)}, u32[]{:S(2)}) collective-permute-start(bf16[144,4096]{1,0:T(8,128)(2,1)S(1)} %after.8.x_ref), channel_id=1, source_target_pairs={{0,4},{1,3},{4,8},{5,1},{8,12},{9,5},{12,14},{13,9},{14,10},{15,13... | collective-permute-start | bytes 3538952 | tf_op jit(solution)/shard_map/ppermute | solution.py:427
  27.9 6.8 %collective-permute-done.5.refs_0_ = bf16[144,4096]{1,0:T(8,128)(2,1)S(1)} collective-permute-done((bf16[144,4096]{1,0:T(8,128)(2,1)S(1)}, bf16[144,4096]{1,0:T(8,128)(2,1)S(1)}, u32[]{:S(2)}, u32[]{:S(2)}) %collective-permute-start.5) | collective-permute-done | bytes 1179680 | tf_op jit(solution)/shard_map/ppermute | solution.py:427
  34.8 0.1 split.8
  34.9 3.0 %collective-permute-start.11 = (bf16[144,4096]{1,0:T(8,128)(2,1)S(1)}, bf16[144,4096]{1,0:T(8,128)(2,1)S(1)}, u32[]{:S(2)}, u32[]{:S(2)}) collective-permute-start(bf16[144,4096]{1,0:T(8,128)(2,1)S(1)} %after.9.x_ref), channel_id=1, source_target_pairs={{0,4},{1,3},{4,8},{5,1},{8,12},{9,5},{12,14},{13,9},{14,10},{15,13... | collective-permute-start | bytes 3538952 | tf_op jit(solution)/shard_map/ppermute | solution.py:427
  37.9 0.5 collective-permute-start.6
  38.4 1.5 %collective-permute-done.7.refs_10_ = bf16[144,2048]{1,0:T(8,128)(2,1)S(1)} collective-permute-done((bf16[144,2048]{1,0:T(8,128)(2,1)S(1)}, bf16[144,2048]{1,0:T(8,128)(2,1)S(1)}, u32[]{:S(2)}, u32[]{:S(2)}) %collective-permute-start.7) | collective-permute-done | bytes 589856 | tf_op jit(solution)/shard_map/ppermute | solution.py:427
  39.9 0.8 collective-permute-done.6.refs_8_
  40.7 0.8 collective-permute-done.8.refs_12_
  41.6 11.2 %phase_w_whole.5 = (f32[768,4096]{1,0:T(8,128)S(1)}, bf16[2304,768]{1,0:T(8,128)(2,1)}, f32[8,128]{1,0:T(8,128)S(1)}) custom-call(s32[16,16]{1,0:T(8,128)S(1)} %copy-done.1, s32[1]{0:T(128)} %bitcast.me_ref.refs_1_, s32[1]{0:T(128)S(6)} %copy.44.heads_ref.refs_2_, ...), custom_call_target="tpu_custom_call", output_to_operand_aliasing={{0}: (13, {}), {1}: (14, {})} | custom-call | flops 1 | bytes 1 | tf_op jit(solution)/shard_map/phase_w_whole/pallas_call | solution.py:295
  52.8 1.6 %collective-permute-start.9 = (bf16[144,4096]{1,0:T(8,128)(2,1)S(1)}, bf16[144,4096]{1,0:T(8,128)(2,1)S(1)}, u32[]{:S(2)}, u32[]{:S(2)}) collective-permute-start(bf16[144,4096]{1,0:T(8,128)(2,1)S(1)} %after.10.x_ref), channel_id=1, source_target_pairs={{0,4},{1,3},{4,8},{5,1},{8,12},{9,5},{12,14},{13,9},{14,10},{15,13... | collective-permute-start | bytes 3538952 | tf_op jit(solution)/shard_map/ppermute | solution.py:427
  54.5 0.1 split.9
  54.6 0.1 collective-permute-start.10
  54.6 0.5 collective-permute-start.13
  55.1 2.7 %collective-permute-done.11.refs_0_ = bf16[144,4096]{1,0:T(8,128)(2,1)S(1)} collective-permute-done((bf16[144,4096]{1,0:T(8,128)(2,1)S(1)}, bf16[144,4096]{1,0:T(8,128)(2,1)S(1)}, u32[]{:S(2)}, u32[]{:S(2)}) %collective-permute-start.11) | collective-permute-done | bytes 1179680 | tf_op jit(solution)/shard_map/ppermute | solution.py:427
  57.9 0.1 split.10
  58.0 0.1 collective-permute-start.12
  58.0 0.5 collective-permute-start.14
  58.5 2.1 %collective-permute-start.16 = (bf16[144,4096]{1,0:T(8,128)(2,1)S(1)}, bf16[144,4096]{1,0:T(8,128)(2,1)S(1)}, u32[]{:S(2)}, u32[]{:S(2)}) collective-permute-start(bf16[144,4096]{1,0:T(8,128)(2,1)S(1)} %after.11.x_ref), channel_id=1, source_target_pairs={{0,4},{1,3},{4,8},{5,1},{8,12},{9,5},{12,14},{13,9},{14,10},{15,13... | collective-permute-start | bytes 3538952 | tf_op jit(solution)/shard_map/ppermute | solution.py:427
  60.6 0.2 collective-permute-done.14.refs_11_.refs_14_
  60.9 6.3 %phase_w_None.3 = (f32[768,4096]{1,0:T(8,128)S(1)}, f32[8,128]{1,0:T(8,128)S(1)}) custom-call(s32[16,16]{1,0:T(8,128)S(1)} %copy-done.2, s32[1]{0:T(128)} %bitcast.me_ref.refs_1_, s32[1]{0:T(128)S(6)} %copy.44.heads_ref.refs_2_, bf16[768,576]{1,0:T(8,128)(2,1)S(1)} %get-tuple-element.59.refs_3_, ...), custom_call_target="tpu_custom_call", output_to_operand_aliasing={{0}: (12, {})} | custom-call | flops 1 | bytes 1 | tf_op jit(solution)/shard_map/phase_w_None/pallas_call | solution.py:295
  67.2 3.3 %collective-permute-done.9.refs_0_ = bf16[144,4096]{1,0:T(8,128)(2,1)S(1)} collective-permute-done((bf16[144,4096]{1,0:T(8,128)(2,1)S(1)}, bf16[144,4096]{1,0:T(8,128)(2,1)S(1)}, u32[]{:S(2)}, u32[]{:S(2)}) %collective-permute-start.9) | collective-permute-done | bytes 1179680 | tf_op jit(solution)/shard_map/ppermute | solution.py:427
  70.5 0.1 split.11
  70.6 0.1 collective-permute-start.17
  70.7 0.5 collective-permute-start.18
  71.2 2.1 %collective-permute-start.15 = (bf16[144,4096]{1,0:T(8,128)(2,1)S(1)}, bf16[144,4096]{1,0:T(8,128)(2,1)S(1)}, u32[]{:S(2)}, u32[]{:S(2)}) collective-permute-start(bf16[144,4096]{1,0:T(8,128)(2,1)S(1)} %after.12.x_ref), channel_id=1, source_target_pairs={{0,4},{1,3},{4,8},{5,1},{8,12},{9,5},{12,14},{13,9},{14,10},{15,13... | collective-permute-start | bytes 3538952 | tf_op jit(solution)/shard_map/ppermute | solution.py:427
  73.3 0.3 collective-permute-done.18.refs_16_
  73.5 11.7 %phase_w_whole.6 = (f32[768,4096]{1,0:T(8,128)S(1)}, bf16[2304,768]{1,0:T(8,128)(2,1)}, f32[8,128]{1,0:T(8,128)S(1)}) custom-call(s32[16,16]{1,0:T(8,128)S(1)} %copy-done.2, s32[1]{0:T(128)} %bitcast.me_ref.refs_1_, s32[1]{0:T(128)S(6)} %copy.44.heads_ref.refs_2_, ...), custom_call_target="tpu_custom_call", output_to_operand_aliasing={{0}: (17, {}), {1}: (18, {})} | custom-call | flops 1 | bytes 1 | tf_op jit(solution)/shard_map/phase_w_whole/pallas_call | solution.py:295
  85.2 0.1 split.12
  85.3 0.2 collective-permute-start.19
  85.5 0.4 collective-permute-start.20
  85.9 1.5 %collective-permute-done.19.refs_6_ = bf16[144,2048]{1,0:T(8,128)(2,1)S(1)} collective-permute-done((bf16[144,2048]{1,0:T(8,128)(2,1)S(1)}, bf16[144,2048]{1,0:T(8,128)(2,1)S(1)}, u32[]{:S(2)}, u32[]{:S(2)}) %collective-permute-start.19) | collective-permute-done | bytes 589856 | tf_op jit(solution)/shard_map/ppermute | solution.py:427
  87.4 0.8 collective-permute-done.20.refs_8_
  88.2 7.4 %phase_w_whole.7 = (f32[768,4096]{1,0:T(8,128)S(1)}, bf16[2304,768]{1,0:T(8,128)(2,1)}, f32[8,128]{1,0:T(8,128)S(1)}) custom-call(s32[16,16]{1,0:T(8,128)S(1)} %copy-done.2, s32[1]{0:T(128)} %bitcast.me_ref.refs_1_, s32[1]{0:T(128)S(6)} %copy.44.heads_ref.refs_2_, ...), custom_call_target="tpu_custom_call", output_to_operand_aliasing={{0}: (9, {}), {1}: (10, {})} | custom-call | flops 1 | bytes 1 | tf_op jit(solution)/shard_map/phase_w_whole/pallas_call | solution.py:295
  95.7 0.1 collective-permute-done.15.refs_0_
  95.8 0.1 split.13
  95.9 0.1 collective-permute-start.22
  96.0 0.5 collective-permute-start.21
  96.5 3.0 %phase_w_None.4 = (f32[768,4096]{1,0:T(8,128)S(1)}, f32[8,128]{1,0:T(8,128)}) custom-call(s32[16,16]{1,0:T(8,128)S(1)} %copy-done.2, s32[1]{0:T(128)} %bitcast.me_ref.refs_1_, s32[1]{0:T(128)S(6)} %copy.44.heads_ref.refs_2_, bf16[768,144]{1,0:T(8,128)(2,1)S(1)} %get-tuple-element.84.refs_3_, ...), custom_call_target="tpu_custom_call", output_to_operand_aliasing={{0}: (6, {})} | custom-call | flops 1 | bytes 1 | tf_op jit(solution)/shard_map/phase_w_None/pallas_call | solution.py:295
  99.5 3.0 %phase_w_None.5 = (f32[768,4096]{1,0:T(8,128)S(1)}, f32[8,128]{1,0:T(8,128)S(1)}) custom-call(s32[16,16]{1,0:T(8,128)S(1)} %copy-done.2, s32[1]{0:T(128)} %bitcast.me_ref.refs_1_, s32[1]{0:T(128)S(6)} %copy.44.heads_ref.refs_2_, bf16[768,144]{1,0:T(8,128)(2,1)S(1)} %get-tuple-element.83.refs_3_, ...), custom_call_target="tpu_custom_call", output_to_operand_aliasing={{0}: (6, {})} | custom-call | flops 1 | bytes 1 | tf_op jit(solution)/shard_map/phase_w_None/pallas_call | solution.py:295
  102.5 3.1 %collective-permute-start.25 = (f32[8,128]{1,0:T(8,128)S(1)}, f32[8,128]{1,0:T(8,128)S(1)}, u32[]{:S(2)}, u32[]{:S(2)}) collective-permute-start(f32[8,128]{1,0:T(8,128)S(1)} %get-tuple-element.88), channel_id=1, source_target_pairs={{0,6},{1,7},{2,4},{3,5},{4,2},{5,3},{6,0},{7,1},{8,14},{9,15},{10,... | collective-permute-start | bytes 12296 | tf_op jit(solution)/shard_map/ppermute | solution.py:407
  105.6 0.4 collective-permute-start.24
  106.0 0.2 collective-permute-start.23
  106.2 2.9 %phase__first.1 = (f32[288,768]{1,0:T(8,128)S(1)}, f32[8,128]{1,0:T(8,128)S(1)}) custom-call(s32[16,16]{1,0:T(8,128)S(1)} %copy-done.2, s32[1]{0:T(128)} %bitcast.me_ref.refs_1_, s32[1]{0:T(128)S(6)} %copy.44.heads_ref.refs_2_, bf16[768,4096]{1,0:T(8,128)(2,1)S(1)} %copy-done, bf16[144,2048]{1,0:T(8,128)(2,1)S(1)} %get-tuple-element.79.refs_4_, ...), custom_call_target="tpu_custom_call" | custom-call | flops 1 | bytes 1 | tf_op jit(solution)/shard_map/phase__first/pallas_call | solution.py:295
  109.2 0.0 collective-permute-done.24
  109.2 0.4 collective-permute-done.23
  109.6 1.4 %collective-permute-start.28 = (f32[8,128]{1,0:T(8,128)S(1)}, f32[8,128]{1,0:T(8,128)S(1)}, u32[]{:S(2)}, u32[]{:S(2)}) collective-permute-start(f32[8,128]{1,0:T(8,128)S(1)} %after.15), channel_id=1, source_target_pairs={{0,9},{1,8},{2,11},{3,10},{4,13},{5,12},{6,15},{7,14},{8,1},{9,0},... | collective-permute-start | bytes 12296 | tf_op jit(solution)/shard_map/ppermute | solution.py:407
  111.0 1.3 %collective-permute-start.27 = (f32[8,128]{1,0:T(8,128)S(1)}, f32[8,128]{1,0:T(8,128)S(1)}, u32[]{:S(2)}, u32[]{:S(2)}) collective-permute-start(f32[8,128]{1,0:T(8,128)S(1)} %after.15), channel_id=1, source_target_pairs={{0,8},{1,9},{2,10},{3,11},{4,12},{5,13},{6,14},{7,15},{8,0},{9,1},... | collective-permute-start | bytes 12296 | tf_op jit(solution)/shard_map/ppermute | solution.py:407
  112.3 0.1 collective-permute-start.26
  112.4 2.7 %phase__last.1 = (bf16[2304,768]{1,0:T(8,128)(2,1)}, f32[8,128]{1,0:T(8,128)}) custom-call(s32[16,16]{1,0:T(8,128)S(1)} %copy-done.2, s32[1]{0:T(128)} %bitcast.me_ref.refs_1_, s32[1]{0:T(128)S(6)} %copy.44.heads_ref.refs_2_, bf16[768,4096]{1,0:T(8,128)(2,1)S(1)} %copy-done, ...), custom_call_target="tpu_custom_call", output_to_operand_aliasing={{0}: (7, {})} | custom-call | flops 1 | bytes 1 | tf_op jit(solution)/shard_map/phase__last/pallas_call | solution.py:295
  115.1 0.4 collective-permute-done.27
  115.5 3.0 %scale.1 = bf16[768,4096]{1,0:T(8,128)(2,1)} custom-call(f32[768,4096]{1,0:T(8,128)S(1)} %get-tuple-element.87.w_ref, f32[8,128]{1,0:T(8,128)S(1)} %add_add_fusion.squares_ref), custom_call_target="tpu_custom_call" | custom-call | flops 3145728 | bytes 6291456 | tf_op jit(solution)/shard_map/scale/pallas_call | solution.py:335
  (29 shorter events, 0.1 us)
Async XLA Ops:
  1.3 12.8 %copy-start = (bf16[768,4096]{1,0:T(8,128)(2,1)S(1)}, bf16[768,4096]{1,0:T(8,128)(2,1)}, u32[]{:S(2)}) copy-start(bf16[768,4096]{1,0:T(8,128)(2,1)} %refs_3_.3) | copy-start | bytes 18874372
  2.7 22.5 %collective-permute-start = (bf16[144,4096]{1,0:T(8,128)(2,1)S(1)}, bf16[144,4096]{1,0:T(8,128)(2,1)S(1)}, u32[]{:S(2)}, u32[]{:S(2)}) collective-permute-start(bf16[144,4096]{1,0:T(8,128)(2,1)S(1)} %live.1.own_ref), channel_id=1, source_target_pairs={{0,4},{1,3},{4,8},{5,1},{8,12},{9,5},{12,14},{13,9},{14,10},{15,13... | collective-permute-start | bytes 3538952 | tf_op jit(solution)/shard_map/ppermute | solution.py:427
  6.5 0.7 copy-start.1
  11.1 2.1 %collective-permute-start.1 = (bf16[144,2048]{1,0:T(8,128)(2,1)S(1)}, bf16[144,2048]{1,0:T(8,128)(2,1)S(1)}, u32[]{:S(2)}, u32[]{:S(2)}) collective-permute-start(bf16[144,2048]{1,0:T(8,128)(2,1)S(1)} %get-tuple-element.47.refs_5_), channel_id=1, source_target_pairs={{0,1},{1,0},{2,3},{3,2},{4,5},{5,4},{6,7},{7,6},{8,9},{9,8},{10,11... | collective-permute-start | bytes 1769480 | tf_op jit(solution)/shard_map/ppermute | solution.py:427
  11.2 2.8 %collective-permute-start.2 = (bf16[144,2048]{1,0:T(8,128)(2,1)S(1)}, bf16[144,2048]{1,0:T(8,128)(2,1)S(1)}, u32[]{:S(2)}, u32[]{:S(2)}) collective-permute-start(bf16[144,2048]{1,0:T(8,128)(2,1)S(1)} %get-tuple-element.48.refs_7_), channel_id=1, source_target_pairs={{0,1},{1,0},{2,3},{3,2},{4,5},{5,4},{6,7},{7,6},{8,9},{9,8},{10,11... | collective-permute-start | bytes 1769480 | tf_op jit(solution)/shard_map/ppermute | solution.py:427
  11.7 23.1 %collective-permute-start.5 = (bf16[144,4096]{1,0:T(8,128)(2,1)S(1)}, bf16[144,4096]{1,0:T(8,128)(2,1)S(1)}, u32[]{:S(2)}, u32[]{:S(2)}) collective-permute-start(bf16[144,4096]{1,0:T(8,128)(2,1)S(1)} %get-tuple-element.52), channel_id=1, source_target_pairs={{0,3},{1,4},{4,1},{5,8},{8,5},{9,12},{12,9},{13,14},{14,13},{15,10... | collective-permute-start | bytes 3538952 | tf_op jit(solution)/shard_map/ppermute | solution.py:427
  25.3 13.1 %collective-permute-start.4 = (bf16[144,2048]{1,0:T(8,128)(2,1)S(1)}, bf16[144,2048]{1,0:T(8,128)(2,1)S(1)}, u32[]{:S(2)}, u32[]{:S(2)}) collective-permute-start(bf16[144,2048]{1,0:T(8,128)(2,1)S(1)} %get-tuple-element.51.refs_5_), channel_id=1, source_target_pairs={{0,1},{1,0},{2,3},{3,2},{4,5},{5,4},{6,7},{7,6},{8,9},{9,8},{10,11... | collective-permute-start | bytes 1769480 | tf_op jit(solution)/shard_map/ppermute | solution.py:427
  25.4 27.4 %collective-permute-start.3 = (bf16[144,4096]{1,0:T(8,128)(2,1)S(1)}, bf16[144,4096]{1,0:T(8,128)(2,1)S(1)}, u32[]{:S(2)}, u32[]{:S(2)}) collective-permute-start(bf16[144,4096]{1,0:T(8,128)(2,1)S(1)} %after.8.x_ref), channel_id=1, source_target_pairs={{0,4},{1,3},{4,8},{5,1},{8,12},{9,5},{12,14},{13,9},{14,10},{15,13... | collective-permute-start | bytes 3538952 | tf_op jit(solution)/shard_map/ppermute | solution.py:427
  34.9 23.0 %collective-permute-start.11 = (bf16[144,4096]{1,0:T(8,128)(2,1)S(1)}, bf16[144,4096]{1,0:T(8,128)(2,1)S(1)}, u32[]{:S(2)}, u32[]{:S(2)}) collective-permute-start(bf16[144,4096]{1,0:T(8,128)(2,1)S(1)} %after.9.x_ref), channel_id=1, source_target_pairs={{0,4},{1,3},{4,8},{5,1},{8,12},{9,5},{12,14},{13,9},{14,10},{15,13... | collective-permute-start | bytes 3538952 | tf_op jit(solution)/shard_map/ppermute | solution.py:427
  37.9 2.0 %collective-permute-start.7 = (bf16[144,2048]{1,0:T(8,128)(2,1)S(1)}, bf16[144,2048]{1,0:T(8,128)(2,1)S(1)}, u32[]{:S(2)}, u32[]{:S(2)}) collective-permute-start(bf16[144,2048]{1,0:T(8,128)(2,1)S(1)} %get-tuple-element.54.refs_9_), channel_id=1, source_target_pairs={{0,1},{1,0},{2,3},{3,2},{4,5},{5,4},{6,7},{7,6},{8,9},{9,8},{10,11... | collective-permute-start | bytes 1769480 | tf_op jit(solution)/shard_map/ppermute | solution.py:427
  37.9 2.8 %collective-permute-start.6 = (bf16[144,2048]{1,0:T(8,128)(2,1)S(1)}, bf16[144,2048]{1,0:T(8,128)(2,1)S(1)}, u32[]{:S(2)}, u32[]{:S(2)}) collective-permute-start(bf16[144,2048]{1,0:T(8,128)(2,1)S(1)} %get-tuple-element.53.refs_7_), channel_id=1, source_target_pairs={{0,1},{1,0},{2,3},{3,2},{4,5},{5,4},{6,7},{7,6},{8,9},{9,8},{10,11... | collective-permute-start | bytes 1769480 | tf_op jit(solution)/shard_map/ppermute | solution.py:427
  38.4 3.2 %collective-permute-start.8 = (bf16[144,2048]{1,0:T(8,128)(2,1)S(1)}, bf16[144,2048]{1,0:T(8,128)(2,1)S(1)}, u32[]{:S(2)}, u32[]{:S(2)}) collective-permute-start(bf16[144,2048]{1,0:T(8,128)(2,1)S(1)} %get-tuple-element.55.refs_11_), channel_id=1, source_target_pairs={{0,1},{1,0},{2,3},{3,2},{4,5},{5,4},{6,7},{7,6},{8,9},{9,8},{10,11... | collective-permute-start | bytes 1769480 | tf_op jit(solution)/shard_map/ppermute | solution.py:427
  52.8 17.7 %collective-permute-start.9 = (bf16[144,4096]{1,0:T(8,128)(2,1)S(1)}, bf16[144,4096]{1,0:T(8,128)(2,1)S(1)}, u32[]{:S(2)}, u32[]{:S(2)}) collective-permute-start(bf16[144,4096]{1,0:T(8,128)(2,1)S(1)} %after.10.x_ref), channel_id=1, source_target_pairs={{0,4},{1,3},{4,8},{5,1},{8,12},{9,5},{12,14},{13,9},{14,10},{15,13... | collective-permute-start | bytes 3538952 | tf_op jit(solution)/shard_map/ppermute | solution.py:427
  54.6 4.0 %collective-permute-start.10 = (bf16[144,2048]{1,0:T(8,128)(2,1)S(1)}, bf16[144,2048]{1,0:T(8,128)(2,1)S(1)}, u32[]{:S(2)}, u32[]{:S(2)}) collective-permute-start(bf16[144,2048]{1,0:T(8,128)(2,1)S(1)} %get-tuple-element.60.refs_4_.refs_5_), channel_id=1, source_target_pairs={{0,1},{1,0},{2,3},{3,2},{4,5},{5,4},{6,7},{7,6},{8,9},{9,8},{10,11... | collective-permute-start | bytes 1769480 | tf_op jit(solution)/shard_map/ppermute | solution.py:427
  54.6 6.0 %collective-permute-start.13 = (bf16[144,2048]{1,0:T(8,128)(2,1)S(1)}, bf16[144,2048]{1,0:T(8,128)(2,1)S(1)}, u32[]{:S(2)}, u32[]{:S(2)}) collective-permute-start(bf16[144,2048]{1,0:T(8,128)(2,1)S(1)} %get-tuple-element.62.refs_8_.refs_11_), channel_id=1, source_target_pairs={{0,1},{1,0},{2,3},{3,2},{4,5},{5,4},{6,7},{7,6},{8,9},{9,8},{10,11... | collective-permute-start | bytes 1769480 | tf_op jit(solution)/shard_map/ppermute | solution.py:427
  57.9 3.0 %copy-start.2 = (s32[16,16]{1,0:T(8,128)S(1)}, s32[16,16]{1,0:T(8,128)}, u32[]{:S(2)}) copy-start(s32[16,16]{1,0:T(8,128)} %constant.6.clone.table_ref.refs_0_) | copy-start | bytes 3076
  58.0 2.7 %collective-permute-start.12 = (bf16[144,2048]{1,0:T(8,128)(2,1)S(1)}, bf16[144,2048]{1,0:T(8,128)(2,1)S(1)}, u32[]{:S(2)}, u32[]{:S(2)}) collective-permute-start(bf16[144,2048]{1,0:T(8,128)(2,1)S(1)} %get-tuple-element.61.refs_6_.refs_7_), channel_id=1, source_target_pairs={{0,1},{1,0},{2,3},{3,2},{4,5},{5,4},{6,7},{7,6},{8,9},{9,8},{10,11... | collective-permute-start | bytes 1769480 | tf_op jit(solution)/shard_map/ppermute | solution.py:427
  58.0 2.8 %collective-permute-start.14 = (bf16[144,2048]{1,0:T(8,128)(2,1)S(1)}, bf16[144,2048]{1,0:T(8,128)(2,1)S(1)}, u32[]{:S(2)}, u32[]{:S(2)}) collective-permute-start(bf16[144,2048]{1,0:T(8,128)(2,1)S(1)} %get-tuple-element.63.refs_10_.refs_13_), channel_id=1, source_target_pairs={{0,1},{1,0},{2,3},{3,2},{4,5},{5,4},{6,7},{7,6},{8,9},{9,8},{10,11... | collective-permute-start | bytes 1769480 | tf_op jit(solution)/shard_map/ppermute | solution.py:427
  58.5 26.6 %collective-permute-start.16 = (bf16[144,4096]{1,0:T(8,128)(2,1)S(1)}, bf16[144,4096]{1,0:T(8,128)(2,1)S(1)}, u32[]{:S(2)}, u32[]{:S(2)}) collective-permute-start(bf16[144,4096]{1,0:T(8,128)(2,1)S(1)} %after.11.x_ref), channel_id=1, source_target_pairs={{0,4},{1,3},{4,8},{5,1},{8,12},{9,5},{12,14},{13,9},{14,10},{15,13... | collective-permute-start | bytes 3538952 | tf_op jit(solution)/shard_map/ppermute | solution.py:427
  70.6 2.7 %collective-permute-start.17 = (bf16[144,2048]{1,0:T(8,128)(2,1)S(1)}, bf16[144,2048]{1,0:T(8,128)(2,1)S(1)}, u32[]{:S(2)}, u32[]{:S(2)}) collective-permute-start(bf16[144,2048]{1,0:T(8,128)(2,1)S(1)} %get-tuple-element.68.refs_9_), channel_id=1, source_target_pairs={{0,1},{1,0},{2,3},{3,2},{4,5},{5,4},{6,7},{7,6},{8,9},{9,8},{10,11... | collective-permute-start | bytes 1769480 | tf_op jit(solution)/shard_map/ppermute | solution.py:427
  70.7 2.8 %collective-permute-start.18 = (bf16[144,2048]{1,0:T(8,128)(2,1)S(1)}, bf16[144,2048]{1,0:T(8,128)(2,1)S(1)}, u32[]{:S(2)}, u32[]{:S(2)}) collective-permute-start(bf16[144,2048]{1,0:T(8,128)(2,1)S(1)} %get-tuple-element.69.refs_15_), channel_id=1, source_target_pairs={{0,1},{1,0},{2,3},{3,2},{4,5},{5,4},{6,7},{7,6},{8,9},{9,8},{10,11... | collective-permute-start | bytes 1769480 | tf_op jit(solution)/shard_map/ppermute | solution.py:427
  71.2 24.6 %collective-permute-start.15 = (bf16[144,4096]{1,0:T(8,128)(2,1)S(1)}, bf16[144,4096]{1,0:T(8,128)(2,1)S(1)}, u32[]{:S(2)}, u32[]{:S(2)}) collective-permute-start(bf16[144,4096]{1,0:T(8,128)(2,1)S(1)} %after.12.x_ref), channel_id=1, source_target_pairs={{0,4},{1,3},{4,8},{5,1},{8,12},{9,5},{12,14},{13,9},{14,10},{15,13... | collective-permute-start | bytes 3538952 | tf_op jit(solution)/shard_map/ppermute | solution.py:427
  85.3 2.1 %collective-permute-start.19 = (bf16[144,2048]{1,0:T(8,128)(2,1)S(1)}, bf16[144,2048]{1,0:T(8,128)(2,1)S(1)}, u32[]{:S(2)}, u32[]{:S(2)}) collective-permute-start(bf16[144,2048]{1,0:T(8,128)(2,1)S(1)} %get-tuple-element.73.refs_5_), channel_id=1, source_target_pairs={{0,1},{1,0},{2,3},{3,2},{4,5},{5,4},{6,7},{7,6},{8,9},{9,8},{10,11... | collective-permute-start | bytes 1769480 | tf_op jit(solution)/shard_map/ppermute | solution.py:427
  85.5 2.7 %collective-permute-start.20 = (bf16[144,2048]{1,0:T(8,128)(2,1)S(1)}, bf16[144,2048]{1,0:T(8,128)(2,1)S(1)}, u32[]{:S(2)}, u32[]{:S(2)}) collective-permute-start(bf16[144,2048]{1,0:T(8,128)(2,1)S(1)} %get-tuple-element.74.refs_7_), channel_id=1, source_target_pairs={{0,1},{1,0},{2,3},{3,2},{4,5},{5,4},{6,7},{7,6},{8,9},{9,8},{10,11... | collective-permute-start | bytes 1769480 | tf_op jit(solution)/shard_map/ppermute | solution.py:427
  95.9 3.6 %collective-permute-start.22 = (bf16[144,2048]{1,0:T(8,128)(2,1)S(1)}, bf16[144,2048]{1,0:T(8,128)(2,1)S(1)}, u32[]{:S(2)}, u32[]{:S(2)}) collective-permute-start(bf16[144,2048]{1,0:T(8,128)(2,1)S(1)} %get-tuple-element.79.refs_4_), channel_id=1, source_target_pairs={{0,1},{1,0},{2,3},{3,2},{4,5},{5,4},{6,7},{7,6},{8,9},{9,8},{10,11... | collective-permute-start | bytes 1769480 | tf_op jit(solution)/shard_map/ppermute | solution.py:427
  96.0 3.5 %collective-permute-start.21 = (bf16[144,2048]{1,0:T(8,128)(2,1)S(1)}, bf16[144,2048]{1,0:T(8,128)(2,1)S(1)}, u32[]{:S(2)}, u32[]{:S(2)}) collective-permute-start(bf16[144,2048]{1,0:T(8,128)(2,1)S(1)} %get-tuple-element.78.refs_6_.refs_4_.refs_5_), channel_id=1, source_target_pairs={{0,1},{1,0},{2,3},{3,2},{4,5},{5,4},{6,7},{7,6},{8,9},{9,8},{10,11... | collective-permute-start | bytes 1769480 | tf_op jit(solution)/shard_map/ppermute | solution.py:427
  102.5 6.7 %collective-permute-start.25 = (f32[8,128]{1,0:T(8,128)S(1)}, f32[8,128]{1,0:T(8,128)S(1)}, u32[]{:S(2)}, u32[]{:S(2)}) collective-permute-start(f32[8,128]{1,0:T(8,128)S(1)} %get-tuple-element.88), channel_id=1, source_target_pairs={{0,6},{1,7},{2,4},{3,5},{4,2},{5,3},{6,0},{7,1},{8,14},{9,15},{10,... | collective-permute-start | bytes 12296 | tf_op jit(solution)/shard_map/ppermute | solution.py:407
  105.6 3.6 %collective-permute-start.24 = (f32[8,128]{1,0:T(8,128)S(1)}, f32[8,128]{1,0:T(8,128)S(1)}, u32[]{:S(2)}, u32[]{:S(2)}) collective-permute-start(f32[8,128]{1,0:T(8,128)S(1)} %get-tuple-element.88), channel_id=1, source_target_pairs={{0,4},{1,5},{2,6},{3,7},{4,0},{5,1},{6,2},{7,3},{8,12},{9,13},{10,... | collective-permute-start | bytes 12296 | tf_op jit(solution)/shard_map/ppermute | solution.py:407
  106.0 3.6 %collective-permute-start.23 = (f32[8,128]{1,0:T(8,128)S(1)}, f32[8,128]{1,0:T(8,128)S(1)}, u32[]{:S(2)}, u32[]{:S(2)}) collective-permute-start(f32[8,128]{1,0:T(8,128)S(1)} %get-tuple-element.88), channel_id=1, source_target_pairs={{0,2},{1,3},{2,0},{3,1},{4,6},{5,7},{6,4},{7,5},{8,10},{9,11},{10,... | collective-permute-start | bytes 12296 | tf_op jit(solution)/shard_map/ppermute | solution.py:407
  109.6 5.5 %collective-permute-start.28 = (f32[8,128]{1,0:T(8,128)S(1)}, f32[8,128]{1,0:T(8,128)S(1)}, u32[]{:S(2)}, u32[]{:S(2)}) collective-permute-start(f32[8,128]{1,0:T(8,128)S(1)} %after.15), channel_id=1, source_target_pairs={{0,9},{1,8},{2,11},{3,10},{4,13},{5,12},{6,15},{7,14},{8,1},{9,0},... | collective-permute-start | bytes 12296 | tf_op jit(solution)/shard_map/ppermute | solution.py:407
  111.0 4.5 %collective-permute-start.27 = (f32[8,128]{1,0:T(8,128)S(1)}, f32[8,128]{1,0:T(8,128)S(1)}, u32[]{:S(2)}, u32[]{:S(2)}) collective-permute-start(f32[8,128]{1,0:T(8,128)S(1)} %after.15), channel_id=1, source_target_pairs={{0,8},{1,9},{2,10},{3,11},{4,12},{5,13},{6,14},{7,15},{8,0},{9,1},... | collective-permute-start | bytes 12296 | tf_op jit(solution)/shard_map/ppermute | solution.py:407
  112.3 3.2 %collective-permute-start.26 = (f32[8,128]{1,0:T(8,128)S(1)}, f32[8,128]{1,0:T(8,128)S(1)}, u32[]{:S(2)}, u32[]{:S(2)}) collective-permute-start(f32[8,128]{1,0:T(8,128)S(1)} %after.15), channel_id=1, source_target_pairs={{0,1},{1,0},{2,3},{3,2},{4,5},{5,4},{6,7},{7,6},{8,9},{9,8},{10,11... | collective-permute-start | bytes 12296 | tf_op jit(solution)/shard_map/ppermute | solution.py:407

commit v10 on v9

--- a/solution.py
+++ b/solution.py
@@ -61,41 +61,28 @@
         return np.array(table, np.int32)
 
 
-def live_kernel(seqs_ref, me_ref, grad_ref, out_ref, sem):
-    load = pltpu.make_async_copy(grad_ref, out_ref, sem)
-    load.start()
-    load.wait()
-    for s in range(out_ref.shape[0] // SEQ):
-
-        @pl.when(s >= seqs_ref[0])
+def zero_dead(count, ref):
+    for s in range(ref.shape[0] // SEQ):
+
+        @pl.when(s >= count)
         def _():
-            dead = out_ref.at[s * SEQ : (s + 1) * SEQ]
+            dead = ref.at[s * SEQ : (s + 1) * SEQ]
             dead[...] = jnp.zeros_like(dead)
 
 
-def live_rows(seq_counts, me, out_grad):
-    smem = pl.BlockSpec(memory_space=pltpu.SMEM)
-    return pl.pallas_call(
-        live_kernel,
-        in_specs=[smem, smem, pl.BlockSpec(memory_space=pl.ANY)],
-        out_specs=pl.BlockSpec(memory_space=pltpu.VMEM),
-        out_shape=pltpu.VMEM(out_grad.shape, out_grad.dtype),
-        scratch_shapes=[pltpu.SemaphoreType.DMA],
-        compiler_params=pltpu.CompilerParams(vmem_limit_bytes=4 * MIB),
-        name="live",
-    )(seq_counts, me, pltpu.with_memory_space_constraint(out_grad, pltpu.HBM))
-
-
-def prep_kernel(spans, rows, table_ref, me_ref, heads_ref, own_ref, a_ref, *refs):
-    copy_ref, left_ref, right_ref, *at_refs, block_ref, sems, own_sems = refs
+def prep_kernel(
+    spans, rows, table_ref, me_ref, heads_ref, seqs_ref, grad_ref, a_ref, *refs
+):
+    copy_ref, left_ref, right_ref, count_ref, *at_refs, block_ref, sems, own_sems = refs
     half = left_ref.shape[1]
     owns = [
-        pltpu.make_async_copy(own_ref, copy_ref, own_sems.at[0]),
-        pltpu.make_async_copy(own_ref.at[:, pl.ds(0, half)], left_ref, own_sems.at[1]),
-        pltpu.make_async_copy(own_ref.at[:, pl.ds(half, half)], right_ref, own_sems.at[2]),
+        pltpu.make_async_copy(grad_ref, copy_ref, own_sems.at[0]),
+        pltpu.make_async_copy(grad_ref.at[:, pl.ds(0, half)], left_ref, own_sems.at[1]),
+        pltpu.make_async_copy(grad_ref.at[:, pl.ds(half, half)], right_ref, own_sems.at[2]),
     ]
     for copy in owns:
         copy.start()
+    count_ref[...] = jnp.full(count_ref.shape, seqs_ref[0], jnp.int32)
     width = heads_ref[0] * HEAD_DIM
     copies = []
     for i in range(block_ref.shape[0] // rows):
@@ -118,20 +105,24 @@
         at_ref[...] = jnp.where(column < width, block, jnp.zeros_like(block)).T
     for copy in owns:
         copy.wait()
-
-
-def prepared(where, own, attn_out, spans):
+    zero_dead(seqs_ref[0], left_ref)
+    zero_dead(seqs_ref[0], right_ref)
+
+
+def prepared(where, seq_counts, out_grad, attn_out, spans):
     slots, capacity = attn_out.shape
-    rows, features = own.shape
+    rows, features = out_grad.shape
     vmem = pl.BlockSpec(memory_space=pltpu.VMEM)
     smem = pl.BlockSpec(memory_space=pltpu.SMEM)
     outs = [(rows, features), (rows, features // 2), (rows, features // 2)]
     outs += [(capacity, count * rows) for _, count in spans]
-    copy, left, right, *ats = pl.pallas_call(
+    shapes = [pltpu.VMEM(shape, jnp.bfloat16) for shape in outs]
+    shapes.insert(3, pltpu.VMEM((8, 128), jnp.int32))
+    copy, left, right, count, *ats = pl.pallas_call(
         functools.partial(prep_kernel, spans, rows),
-        in_specs=[smem] * 3 + [vmem, pl.BlockSpec(memory_space=pl.ANY)],
-        out_specs=[vmem] * len(outs),
-        out_shape=[pltpu.VMEM(shape, jnp.bfloat16) for shape in outs],
+        in_specs=[smem] * 4 + [pl.BlockSpec(memory_space=pl.ANY)] * 2,
+        out_specs=[vmem] * len(shapes),
+        out_shape=shapes,
         scratch_shapes=[
             pltpu.VMEM((slots, capacity), jnp.bfloat16),
             pltpu.SemaphoreType.DMA((slots // rows,)),
@@ -142,10 +133,48 @@
         name="prep",
     )(
         *where,
-        pltpu.with_memory_space_constraint(own, pltpu.VMEM),
+        seq_counts,
+        pltpu.with_memory_space_constraint(out_grad, pltpu.HBM),
         pltpu.with_memory_space_constraint(attn_out, pltpu.HBM),
     )
-    return copy, (left, right), ats
+    return copy, (left, right), count, ats
+
+
+def flip_kernel(x_ref, out_ref):
+    width = 512
+    for i in range(x_ref.shape[1] // width):
+        part = slice(i * width, (i + 1) * width)
+        out_ref[part, :] = x_ref[:, part].T
+
+
+def flipped(x):
+    vmem = pl.BlockSpec(memory_space=pltpu.VMEM)
+    return pl.pallas_call(
+        flip_kernel,
+        in_specs=[vmem],
+        out_specs=vmem,
+        out_shape=pltpu.VMEM(x.shape[::-1], x.dtype),
+        compiler_params=pltpu.CompilerParams(vmem_limit_bytes=8 * MIB),
+        cost_estimate=pl.CostEstimate(flops=1, bytes_accessed=1, transcendentals=0),
+        name="flipped",
+    )(pltpu.with_memory_space_constraint(x, pltpu.VMEM))
+
+
+def arrive_kernel(count_ref, x_ref, done_ref, out_ref):
+    zero_dead(count_ref[0, 0], out_ref)
+
+
+def arrived(done, count, x):
+    vmem = pl.BlockSpec(memory_space=pltpu.VMEM)
+    return pl.pallas_call(
+        arrive_kernel,
+        in_specs=[pl.BlockSpec(memory_space=pltpu.SMEM), vmem, vmem],
+        out_specs=vmem,
+        out_shape=pltpu.VMEM(x.shape, x.dtype),
+        input_output_aliases={1: 0},
+        compiler_params=pltpu.CompilerParams(vmem_limit_bytes=MIB),
+        name="arrived",
+    )(count, *[pltpu.with_memory_space_constraint(x, pltpu.VMEM) for x in (x, done)])
 
 
 def phase_kernel(spec, *refs):
@@ -195,8 +224,8 @@
         if attn:
             total_ref[...] += lax.dot_general(
                 jnp.concatenate(g, axis=0),
-                weight_ref[:, there],
-                (((1,), (1,)), ((), ())),
+                weight_ref[there, :],
+                (((1,), (0,)), ((), ())),
                 preferred_element_type=jnp.float32,
             )
         return carry
@@ -421,7 +450,7 @@
     me = lax.axis_index("dp").astype(jnp.int32).reshape(1)
     where = (jnp.asarray(ring.owners()), me, head_counts)
     shapes = (slots, o_weight.shape[0], features, rows)
-    weight, half = o_weight, features // 2
+    half = features // 2
 
     def send(x, pairs):
         return lax.ppermute(x, "dp", pairs)
@@ -435,17 +464,19 @@
             for c in range(min(len(x) for x in pairs))
         ]
 
-    own = live_rows(seq_counts, me, out_grad)
-    x = send(own, ring.along())
-    own, near, ats = prepared(where, own, attn_out, [x for x in spans if x])
+    x = send(out_grad, ring.along())
+    own, near, count, ats = prepared(
+        where, seq_counts, out_grad, attn_out, [x for x in spans if x]
+    )
     ats = [ats.pop(0) if x else None for x in spans]
     y = send(own, ring.crossing())
-    w, out, done = phase(
-        where, shapes, 0, grouped(near, swapped(near)), at=ats[0], weight=weight, attn="whole"
-    )
+    counts = send(count, ring.along()), send(count, ring.crossing())
+    first = [near, swapped(near)]
+    w, done = phase(where, shapes, 0, grouped(*first), at=ats[0])
+    weight, out = flipped(o_weight), None
 
     for k in range(1, last):
-        (x,) = after(done, x)
+        x = arrived(done, counts[0], x) if k == 1 else after(done, x)[0]
         x, near_x = send(x, ring.along()), split(x)
         far_x = swapped(near_x)
         i = 2 * k - 1
@@ -455,7 +486,7 @@
                 where, shapes, 2 * (i + 1) - len(held), grouped(*held), at=ats[i], w=w,
                 w_from=len(held) - 2, weight=weight, attn="whole", out=out,
             )
-        (y,) = after(done, y)
+        y = arrived(weight, counts[1], y) if k == 1 else after(done, y)[0]
         y, near_y = send(y, ring.along()) if k < last - 1 else None, split(y)
         far_y = swapped(near_y)
         groups = grouped(near_x, far_x, near_y, far_y)
@@ -468,10 +499,12 @@
             held = [near_x, far_x, near_y, far_y]
             w, done = phase(where, shapes, 2 * i, groups, at=ats[i], w=w)
         else:
+            groups = grouped(*first, near_x, far_x, near_y, far_y)
             w, out, done = phase(
-                where, shapes, 2 * i, groups, at=ats[i], w=w,
-                weight=weight, attn="whole", out=out,
-            )
+                where, shapes, 2 * i - len(first), groups, at=ats[i], w=w,
+                w_from=len(first), weight=weight, attn="whole", out=out,
+            )
+            first = []
 
     (x,) = after(done, x)
     near = split(x)

time: 119 us -> 138 us (1.16)
  waiting for transfers between devices: 25.5 us -> 41.3 us
  local copies, waits for them, and re-layouts: 0.7 us -> 3.66 us
    ppermute x23 -> x25, waiting for transfers between devices: 24.6 us -> 40.8 us  [send(): return lax.ppermute(x, 'dp', pairs)]
    unnamed x6 -> x8, local copies, waits for them, and re-layouts: 0.7 us -> 3.66 us
    pallas_call x1 -> x3, Pallas kernels: 1.43 us -> 2.97 us  [the longest x1 1.67 us: flipped(): pl.pallas_call(flip_kernel, in_specs=[vmem], out_specs=vmem, out_shape=pl...]
    ppermute x23 -> x25, starting transfers between devices: 19.1 us -> 18.8 us  [send(): return lax.ppermute(x, 'dp', pairs)]
  transfers between devices with their start and end apart: 29 -> 31, of which waited for: 16 -> 15; matrix products, arithmetic and copies ran while one was open for 0% -> 0% of each run, Pallas kernels for 48% -> 40%
where the time goes in v10:
time: 138 us
  Pallas kernels  65.1 us (47%)
  waiting for transfers between devices  41.3 us (30%)
  starting transfers between devices  25.2 us (18%)
  local copies, waits for them, and re-layouts  3.66 us (3%)
  between operations  2.41 us (2%)
    pallas_call x9, Pallas kernels, phase(): pl.pallas_call(functools.partial(phase_kernel, spec), in_specs=specs, out...  54.4 us
    ppermute x25, waiting for transfers between devices, send(): return lax.ppermute(x, 'dp', pairs)  40.8 us
    ppermute x25, starting transfers between devices, send(): return lax.ppermute(x, 'dp', pairs)  18.8 us
    ppermute x6, starting transfers between devices, exchange(): lax.ppermute(x, 'dp', [(d, d ^ mask) for d in range(devices)])  6.37 us
    pallas_call x1, Pallas kernels, prepared(): pl.pallas_call(functools.partial(prep_kernel, spans, rows), in_specs=[sme...  3.96 us
    unnamed x8, local copies, waits for them, and re-layouts  3.66 us
    pallas_call x1, Pallas kernels, scaled(): pl.pallas_call(functools.partial(scale_kernel, parts), in_specs=[vmem, vm...  3 us
  transfers between devices with their start and end apart: 31, of which 15 were waited for; matrix products, arithmetic and copies ran while one was open for 0% of the time, Pallas kernels for 40%

profile of v10, /device:TPU:0, one launch (start us, length us, event | category | flops | bytes accessed | tf_op | source)
XLA Modules:
  0.0 137.7 jit_solution(3583716214815128074)
XLA Ops:
  1.9 0.7 copy-done.1
  2.6 4.0 %prep.1 = (bf16[144,4096]{1,0:T(8,128)(2,1)S(1)}, bf16[144,2048]{1,0:T(8,128)(2,1)S(1)}, bf16[144,2048]{1,0:T(8,128)(2,1)S(1)}, s32[8,128]{1,0:T(8,128)S(1)}, bf...) custom-call(s32[16,16]{1,0:T(8,128)S(1)} %copy-done.1, ...), custom_call_target="tpu_custom_call" | custom-call | flops 1 | bytes 1 | tf_op jit(solution)/shard_map/prep/pallas_call | solution.py:121
  6.6 2.5 %collective-permute-start.7 = (bf16[144,4096]{1,0:T(8,128)(2,1)S(1)}, bf16[144,4096]{1,0:T(8,128)(2,1)S(1)}, u32[]{:S(2)}, u32[]{:S(2)}) collective-permute-start(bf16[144,4096]{1,0:T(8,128)(2,1)S(1)} %get-tuple-element.53), channel_id=1, source_target_pairs={{0,3},{1,4},{4,1},{5,8},{8,5},{9,12},{12,9},{13,14},{14,13},{15,10... | collective-permute-start | bytes 3538952 | tf_op jit(solution)/shard_map/ppermute | solution.py:456
  9.1 0.7 collective-permute-start.1
  9.8 0.5 collective-permute-start.3
  10.3 1.3 collective-permute-start.6
  11.6 23.9 %collective-permute-done.6.count_ref = s32[8,128]{1,0:T(8,128)S(1)} collective-permute-done((s32[8,128]{1,0:T(8,128)S(1)}, s32[8,128]{1,0:T(8,128)S(1)}, u32[]{:S(2)}, u32[]{:S(2)}) %collective-permute-start.6) | collective-permute-done | bytes 4128 | tf_op jit(solution)/shard_map/ppermute | solution.py:456
  35.5 2.0 %collective-permute-start = (s32[8,128]{1,0:T(8,128)S(1)}, s32[8,128]{1,0:T(8,128)S(1)}, u32[]{:S(2)}, u32[]{:S(2)}) collective-permute-start(s32[8,128]{1,0:T(8,128)S(1)} %get-tuple-element.46), channel_id=1, source_target_pairs={{0,4},{1,3},{4,8},{5,1},{8,12},{9,5},{12,14},{13,9},{14,10},{15,13... | collective-permute-start | bytes 12296 | tf_op jit(solution)/shard_map/ppermute | solution.py:456
  37.4 2.8 %copy-done = bf16[768,4096]{1,0:T(8,128)(2,1)S(1)} copy-done((bf16[768,4096]{1,0:T(8,128)(2,1)S(1)}, bf16[768,4096]{1,0:T(8,128)(2,1)}, u32[]{:S(2)}) %copy-start) | copy-done | bytes 6291480
  40.2 1.7 %flipped.1.done_ref.refs_4_.refs_3_ = bf16[4096,768]{1,0:T(8,128)(2,1)S(1)} custom-call(bf16[768,4096]{1,0:T(8,128)(2,1)S(1)} %copy-done), custom_call_target="tpu_custom_call" | custom-call | flops 1 | bytes 1 | tf_op jit(solution)/shard_map/flipped/pallas_call | solution.py:152
  41.9 0.7 arrived.3.x_ref
  42.6 0.1 split.8
  42.7 0.4 collective-permute-start.8
  43.1 0.2 copy-done.2
  43.3 4.6 %phase_w_None.4 = (f32[768,4096]{1,0:T(8,128)S(1)}, f32[8,128]{1,0:T(8,128)S(1)}) custom-call(s32[16,16]{1,0:T(8,128)S(1)} %copy-done.2, s32[1]{0:T(128)} %bitcast.me_ref.refs_1_, s32[1]{0:T(128)S(6)} %copy.42.heads_ref.refs_2_, bf16[768,288]{1,0:T(8,128)(2,1)S(1)} %get-tuple-element.47.refs_3_, bf16[144,2048]{1,0:T(8,128)(2,1)S(1)} %get-tuple-element.48.refs_4_.refs_5_, ...), custom_call_target="tpu_custom_call" | custom-call | flops 1 | bytes 1 | tf_op jit(solution)/shard_map/phase_w_None/pallas_call | solution.py:324
  47.9 0.7 arrived.2.x_ref
  48.5 1.6 %collective-permute-start.4 = (bf16[144,4096]{1,0:T(8,128)(2,1)S(1)}, bf16[144,4096]{1,0:T(8,128)(2,1)S(1)}, u32[]{:S(2)}, u32[]{:S(2)}) collective-permute-start(bf16[144,4096]{1,0:T(8,128)(2,1)S(1)} %arrived.2.x_ref), channel_id=1, source_target_pairs={{0,4},{1,3},{4,8},{5,1},{8,12},{9,5},{12,14},{13,9},{14,10},{15,13... | collective-permute-start | bytes 3538952 | tf_op jit(solution)/shard_map/ppermute | solution.py:456
  50.2 1.6 %collective-permute-start.13 = (bf16[144,4096]{1,0:T(8,128)(2,1)S(1)}, bf16[144,4096]{1,0:T(8,128)(2,1)S(1)}, u32[]{:S(2)}, u32[]{:S(2)}) collective-permute-start(bf16[144,4096]{1,0:T(8,128)(2,1)S(1)} %arrived.3.x_ref), channel_id=1, source_target_pairs={{0,4},{1,3},{4,8},{5,1},{8,12},{9,5},{12,14},{13,9},{14,10},{15,13... | collective-permute-start | bytes 3538952 | tf_op jit(solution)/shard_map/ppermute | solution.py:456
  51.8 0.1 split.7
  51.9 0.5 collective-permute-start.5
  52.4 0.1 collective-permute-start.9
  52.5 1.4 %collective-permute-done.10.refs_16_ = bf16[144,2048]{1,0:T(8,128)(2,1)S(1)} collective-permute-done((bf16[144,2048]{1,0:T(8,128)(2,1)S(1)}, bf16[144,2048]{1,0:T(8,128)(2,1)S(1)}, u32[]{:S(2)}, u32[]{:S(2)}) %collective-permute-start.10) | collective-permute-done | bytes 589856 | tf_op jit(solution)/shard_map/ppermute | solution.py:456
  53.9 0.8 collective-permute-done.5.refs_8_
  54.8 0.8 collective-permute-done.9.refs_14_
  55.6 13.2 %phase_w_whole.3 = (f32[768,4096]{1,0:T(8,128)S(1)}, bf16[2304,768]{1,0:T(8,128)(2,1)}, f32[8,128]{1,0:T(8,128)S(1)}) custom-call(s32[16,16]{1,0:T(8,128)S(1)} %copy-done.2, s32[1]{0:T(128)} %bitcast.me_ref.refs_1_, s32[1]{0:T(128)S(6)} %copy.42.heads_ref.refs_2_, bf16[768,576]{1,0:T(8,128)(2,1)S(1)} %get-tuple-element.51.refs_3_, ...), custom_call_target="tpu_custom_call", output_to_operand_aliasing={{0}: (17, {})} | custom-call | flops 1 | bytes 1 | tf_op jit(solution)/shard_map/phase_w_whole/pallas_call | solution.py:324
  68.9 1.5 %collective-permute-start.11 = (bf16[144,4096]{1,0:T(8,128)(2,1)S(1)}, bf16[144,4096]{1,0:T(8,128)(2,1)S(1)}, u32[]{:S(2)}, u32[]{:S(2)}) collective-permute-start(bf16[144,4096]{1,0:T(8,128)(2,1)S(1)} %after.6.x_ref), channel_id=1, source_target_pairs={{0,4},{1,3},{4,8},{5,1},{8,12},{9,5},{12,14},{13,9},{14,10},{15,13... | collective-permute-start | bytes 3538952 | tf_op jit(solution)/shard_map/ppermute | solution.py:456
  70.4 7.0 %collective-permute-done.13.refs_0_ = bf16[144,4096]{1,0:T(8,128)(2,1)S(1)} collective-permute-done((bf16[144,4096]{1,0:T(8,128)(2,1)S(1)}, bf16[144,4096]{1,0:T(8,128)(2,1)S(1)}, u32[]{:S(2)}, u32[]{:S(2)}) %collective-permute-start.13) | collective-permute-done | bytes 1179680 | tf_op jit(solution)/shard_map/ppermute | solution.py:456
  77.4 0.1 split.10
  77.6 0.1 split.9
  77.7 0.6 collective-permute-start.16
  78.3 0.1 collective-permute-start.12
  78.4 0.4 collective-permute-start.15
  78.8 0.8 collective-permute-done.14.refs_7_.refs_8_
  79.6 1.6 %collective-permute-start.18 = (bf16[144,4096]{1,0:T(8,128)(2,1)S(1)}, bf16[144,4096]{1,0:T(8,128)(2,1)S(1)}, u32[]{:S(2)}, u32[]{:S(2)}) collective-permute-start(bf16[144,4096]{1,0:T(8,128)(2,1)S(1)} %after.7.x_ref), channel_id=1, source_target_pairs={{0,4},{1,3},{4,8},{5,1},{8,12},{9,5},{12,14},{13,9},{14,10},{15,13... | collective-permute-start | bytes 3538952 | tf_op jit(solution)/shard_map/ppermute | solution.py:456
  81.2 0.1 collective-permute-done.12.refs_5_.refs_6_
  81.3 0.8 collective-permute-done.15.refs_9_.refs_12_
  82.1 6.3 %phase_w_None.5 = (f32[768,4096]{1,0:T(8,128)S(1)}, f32[8,128]{1,0:T(8,128)S(1)}) custom-call(s32[16,16]{1,0:T(8,128)S(1)} %copy-done.2, s32[1]{0:T(128)} %bitcast.me_ref.refs_1_, s32[1]{0:T(128)S(6)} %copy.42.heads_ref.refs_2_, bf16[768,576]{1,0:T(8,128)(2,1)S(1)} %get-tuple-element.59.refs_3_, ...), custom_call_target="tpu_custom_call", output_to_operand_aliasing={{0}: (12, {})} | custom-call | flops 1 | bytes 1 | tf_op jit(solution)/shard_map/phase_w_None/pallas_call | solution.py:324
  88.4 1.7 %collective-permute-done.11.refs_0_ = bf16[144,4096]{1,0:T(8,128)(2,1)S(1)} collective-permute-done((bf16[144,4096]{1,0:T(8,128)(2,1)S(1)}, bf16[144,4096]{1,0:T(8,128)(2,1)S(1)}, u32[]{:S(2)}, u32[]{:S(2)}) %collective-permute-start.11) | collective-permute-done | bytes 1179680 | tf_op jit(solution)/shard_map/ppermute | solution.py:456
  90.1 0.1 split.11
  90.3 0.5 collective-permute-start.20
  90.8 1.6 %collective-permute-start.17 = (bf16[144,4096]{1,0:T(8,128)(2,1)S(1)}, bf16[144,4096]{1,0:T(8,128)(2,1)S(1)}, u32[]{:S(2)}, u32[]{:S(2)}) collective-permute-start(bf16[144,4096]{1,0:T(8,128)(2,1)S(1)} %after.8.x_ref), channel_id=1, source_target_pairs={{0,4},{1,3},{4,8},{5,1},{8,12},{9,5},{12,14},{13,9},{14,10},{15,13... | collective-permute-start | bytes 3538952 | tf_op jit(solution)/shard_map/ppermute | solution.py:456
  92.3 0.7 collective-permute-done.20.refs_16_
  93.1 11.5 %phase_w_whole.4 = (f32[768,4096]{1,0:T(8,128)S(1)}, bf16[2304,768]{1,0:T(8,128)(2,1)}, f32[8,128]{1,0:T(8,128)S(1)}) custom-call(s32[16,16]{1,0:T(8,128)S(1)} %copy-done.2, s32[1]{0:T(128)} %bitcast.me_ref.refs_1_, s32[1]{0:T(128)S(6)} %copy.42.heads_ref.refs_2_, ...), custom_call_target="tpu_custom_call", output_to_operand_aliasing={{0}: (17, {}), {1}: (18, {})} | custom-call | flops 1 | bytes 1 | tf_op jit(solution)/shard_map/phase_w_whole/pallas_call | solution.py:324
  104.7 0.1 split.12
  104.8 0.2 collective-permute-start.21
  105.0 0.4 collective-permute-start.22
  105.3 1.5 %collective-permute-done.21.refs_6_ = bf16[144,2048]{1,0:T(8,128)(2,1)S(1)} collective-permute-done((bf16[144,2048]{1,0:T(8,128)(2,1)S(1)}, bf16[144,2048]{1,0:T(8,128)(2,1)S(1)}, u32[]{:S(2)}, u32[]{:S(2)}) %collective-permute-start.21) | collective-permute-done | bytes 589856 | tf_op jit(solution)/shard_map/ppermute | solution.py:456
  106.8 0.8 collective-permute-done.22.refs_8_
  107.7 7.4 %phase_w_whole.5 = (f32[768,4096]{1,0:T(8,128)S(1)}, bf16[2304,768]{1,0:T(8,128)(2,1)}, f32[8,128]{1,0:T(8,128)S(1)}) custom-call(s32[16,16]{1,0:T(8,128)S(1)} %copy-done.2, s32[1]{0:T(128)} %bitcast.me_ref.refs_1_, s32[1]{0:T(128)S(6)} %copy.42.heads_ref.refs_2_, ...), custom_call_target="tpu_custom_call", output_to_operand_aliasing={{0}: (9, {}), {1}: (10, {})} | custom-call | flops 1 | bytes 1 | tf_op jit(solution)/shard_map/phase_w_whole/pallas_call | solution.py:324
  115.1 0.3 collective-permute-done.17.refs_0_
  115.3 0.1 split.13
  115.5 0.5 collective-permute-start.23
  116.0 2.9 %phase_w_None.6 = (f32[768,4096]{1,0:T(8,128)S(1)}, f32[8,128]{1,0:T(8,128)}) custom-call(s32[16,16]{1,0:T(8,128)S(1)} %copy-done.2, s32[1]{0:T(128)} %bitcast.me_ref.refs_1_, s32[1]{0:T(128)S(6)} %copy.42.heads_ref.refs_2_, bf16[768,144]{1,0:T(8,128)(2,1)S(1)} %get-tuple-element.84.refs_3_, ...), custom_call_target="tpu_custom_call", output_to_operand_aliasing={{0}: (6, {})} | custom-call | flops 1 | bytes 1 | tf_op jit(solution)/shard_map/phase_w_None/pallas_call | solution.py:324
  119.0 3.0 %phase_w_None.7 = (f32[768,4096]{1,0:T(8,128)S(1)}, f32[8,128]{1,0:T(8,128)S(1)}) custom-call(s32[16,16]{1,0:T(8,128)S(1)} %copy-done.2, s32[1]{0:T(128)} %bitcast.me_ref.refs_1_, s32[1]{0:T(128)S(6)} %copy.42.heads_ref.refs_2_, bf16[768,144]{1,0:T(8,128)(2,1)S(1)} %get-tuple-element.83.refs_3_, ...), custom_call_target="tpu_custom_call", output_to_operand_aliasing={{0}: (6, {})} | custom-call | flops 1 | bytes 1 | tf_op jit(solution)/shard_map/phase_w_None/pallas_call | solution.py:324
  122.0 2.4 %collective-permute-start.27 = (f32[8,128]{1,0:T(8,128)S(1)}, f32[8,128]{1,0:T(8,128)S(1)}, u32[]{:S(2)}, u32[]{:S(2)}) collective-permute-start(f32[8,128]{1,0:T(8,128)S(1)} %get-tuple-element.88), channel_id=1, source_target_pairs={{0,6},{1,7},{2,4},{3,5},{4,2},{5,3},{6,0},{7,1},{8,14},{9,15},{10,... | collective-permute-start | bytes 12296 | tf_op jit(solution)/shard_map/ppermute | solution.py:436
  124.4 0.4 collective-permute-start.26
  124.8 0.7 collective-permute-start.25
  125.5 2.8 %phase__first.1 = (f32[288,768]{1,0:T(8,128)S(1)}, f32[8,128]{1,0:T(8,128)S(1)}) custom-call(s32[16,16]{1,0:T(8,128)S(1)} %copy-done.2, s32[1]{0:T(128)} %bitcast.me_ref.refs_1_, s32[1]{0:T(128)S(6)} %copy.42.heads_ref.refs_2_, bf16[4096,768]{1,0:T(8,128)(2,1)S(1)} %flipped.1.done_ref.refs_4_.refs_3_, bf16[144,2048]{1,0:T(8,128)(2,1)S(1)} %get-tuple-element.79.refs_4_, ...), custom_call_target="tpu_custom_call" | custom-call | flops 1 | bytes 1 | tf_op jit(solution)/shard_map/phase__first/pallas_call | solution.py:324
  128.4 1.5 %collective-permute-start.30 = (f32[8,128]{1,0:T(8,128)S(1)}, f32[8,128]{1,0:T(8,128)S(1)}, u32[]{:S(2)}, u32[]{:S(2)}) collective-permute-start(f32[8,128]{1,0:T(8,128)S(1)} %after.11), channel_id=1, source_target_pairs={{0,9},{1,8},{2,11},{3,10},{4,13},{5,12},{6,15},{7,14},{8,1},{9,0},... | collective-permute-start | bytes 12296 | tf_op jit(solution)/shard_map/ppermute | solution.py:436
  129.9 1.2 collective-permute-start.29
  131.2 0.1 collective-permute-start.28
  131.3 2.7 %phase__last.1 = (bf16[2304,768]{1,0:T(8,128)(2,1)}, f32[8,128]{1,0:T(8,128)}) custom-call(s32[16,16]{1,0:T(8,128)S(1)} %copy-done.2, s32[1]{0:T(128)} %bitcast.me_ref.refs_1_, s32[1]{0:T(128)S(6)} %copy.42.heads_ref.refs_2_, bf16[4096,768]{1,0:T(8,128)(2,1)S(1)} %flipped.1.done_ref.refs_4_.refs_3_, ...), custom_call_target="tpu_custom_call", output_to_operand_aliasing={{0}: (7, {})} | custom-call | flops 1 | bytes 1 | tf_op jit(solution)/shard_map/phase__last/pallas_call | solution.py:324
  133.9 0.5 collective-permute-done.29
  134.5 3.0 %scale.1 = bf16[768,4096]{1,0:T(8,128)(2,1)} custom-call(f32[768,4096]{1,0:T(8,128)S(1)} %get-tuple-element.87.w_ref, f32[8,128]{1,0:T(8,128)S(1)} %add_add_fusion.squares_ref), custom_call_target="tpu_custom_call" | custom-call | flops 3145728 | bytes 6291456 | tf_op jit(solution)/shard_map/scale/pallas_call | solution.py:364
  (35 shorter events, 0.5 us)
Async XLA Ops:
  1.9 0.7 copy-start.1
  2.6 6.4 %copy-start.3 = (bf16[144,4096]{1,0:T(8,128)(2,1)S(1)}, bf16[144,4096]{1,0:T(8,128)(2,1)}, u32[]{:S(2)}) copy-start(bf16[144,4096]{1,0:T(8,128)(2,1)} %grad_ref.1) | copy-start | bytes 3538948
  6.6 35.3 %collective-permute-start.7 = (bf16[144,4096]{1,0:T(8,128)(2,1)S(1)}, bf16[144,4096]{1,0:T(8,128)(2,1)S(1)}, u32[]{:S(2)}, u32[]{:S(2)}) collective-permute-start(bf16[144,4096]{1,0:T(8,128)(2,1)S(1)} %get-tuple-element.53), channel_id=1, source_target_pairs={{0,3},{1,4},{4,1},{5,8},{8,5},{9,12},{12,9},{13,14},{14,13},{15,10... | collective-permute-start | bytes 3538952 | tf_op jit(solution)/shard_map/ppermute | solution.py:456
  9.1 38.8 %collective-permute-start.1 = (bf16[144,4096]{1,0:T(8,128)(2,1)S(1)}, bf16[144,4096]{1,0:T(8,128)(2,1)S(1)}, u32[]{:S(2)}, u32[]{:S(2)}) collective-permute-start(bf16[144,4096]{1,0:T(8,128)(2,1)S(1)} %copy-done.3), channel_id=1, source_target_pairs={{0,4},{1,3},{4,8},{5,1},{8,12},{9,5},{12,14},{13,9},{14,10},{15,13... | collective-permute-start | bytes 3538952 | tf_op jit(solution)/shard_map/ppermute | solution.py:456
  9.8 33.3 %collective-permute-start.2 = (bf16[144,2048]{1,0:T(8,128)(2,1)S(1)}, bf16[144,2048]{1,0:T(8,128)(2,1)S(1)}, u32[]{:S(2)}, u32[]{:S(2)}) collective-permute-start(bf16[144,2048]{1,0:T(8,128)(2,1)S(1)} %get-tuple-element.48.refs_4_.refs_5_), channel_id=1, source_target_pairs={{0,1},{1,0},{2,3},{3,2},{4,5},{5,4},{6,7},{7,6},{8,9},{9,8},{10,11... | collective-permute-start | bytes 1769480 | tf_op jit(solution)/shard_map/ppermute | solution.py:456
  9.8 33.3 %collective-permute-start.3 = (bf16[144,2048]{1,0:T(8,128)(2,1)S(1)}, bf16[144,2048]{1,0:T(8,128)(2,1)S(1)}, u32[]{:S(2)}, u32[]{:S(2)}) collective-permute-start(bf16[144,2048]{1,0:T(8,128)(2,1)S(1)} %get-tuple-element.49.refs_6_.refs_11_), channel_id=1, source_target_pairs={{0,1},{1,0},{2,3},{3,2},{4,5},{5,4},{6,7},{7,6},{8,9},{9,8},{10,11... | collective-permute-start | bytes 1769480 | tf_op jit(solution)/shard_map/ppermute | solution.py:456
  10.3 25.2 %collective-permute-start.6 = (s32[8,128]{1,0:T(8,128)S(1)}, s32[8,128]{1,0:T(8,128)S(1)}, u32[]{:S(2)}, u32[]{:S(2)}) collective-permute-start(s32[8,128]{1,0:T(8,128)S(1)} %get-tuple-element.46), channel_id=1, source_target_pairs={{0,3},{1,4},{4,1},{5,8},{8,5},{9,12},{12,9},{13,14},{14,13},{15,10... | collective-permute-start | bytes 12296 | tf_op jit(solution)/shard_map/ppermute | solution.py:456
  35.5 12.4 %collective-permute-start = (s32[8,128]{1,0:T(8,128)S(1)}, s32[8,128]{1,0:T(8,128)S(1)}, u32[]{:S(2)}, u32[]{:S(2)}) collective-permute-start(s32[8,128]{1,0:T(8,128)S(1)} %get-tuple-element.46), channel_id=1, source_target_pairs={{0,4},{1,3},{4,8},{5,1},{8,12},{9,5},{12,14},{13,9},{14,10},{15,13... | collective-permute-start | bytes 12296 | tf_op jit(solution)/shard_map/ppermute | solution.py:456
  37.4 2.8 %copy-start = (bf16[768,4096]{1,0:T(8,128)(2,1)S(1)}, bf16[768,4096]{1,0:T(8,128)(2,1)}, u32[]{:S(2)}) copy-start(bf16[768,4096]{1,0:T(8,128)(2,1)} %x_ref.1) | copy-start | bytes 18874372
  42.6 0.7 copy-start.2
  42.7 9.8 %collective-permute-start.8 = (bf16[144,2048]{1,0:T(8,128)(2,1)S(1)}, bf16[144,2048]{1,0:T(8,128)(2,1)S(1)}, u32[]{:S(2)}, u32[]{:S(2)}) collective-permute-start(bf16[144,2048]{1,0:T(8,128)(2,1)S(1)} %get-tuple-element.54.refs_9_), channel_id=1, source_target_pairs={{0,1},{1,0},{2,3},{3,2},{4,5},{5,4},{6,7},{7,6},{8,9},{9,8},{10,11... | collective-permute-start | bytes 1769480 | tf_op jit(solution)/shard_map/ppermute | solution.py:456
  48.5 20.3 %collective-permute-start.4 = (bf16[144,4096]{1,0:T(8,128)(2,1)S(1)}, bf16[144,4096]{1,0:T(8,128)(2,1)S(1)}, u32[]{:S(2)}, u32[]{:S(2)}) collective-permute-start(bf16[144,4096]{1,0:T(8,128)(2,1)S(1)} %arrived.2.x_ref), channel_id=1, source_target_pairs={{0,4},{1,3},{4,8},{5,1},{8,12},{9,5},{12,14},{13,9},{14,10},{15,13... | collective-permute-start | bytes 3538952 | tf_op jit(solution)/shard_map/ppermute | solution.py:456
  50.2 27.3 %collective-permute-start.13 = (bf16[144,4096]{1,0:T(8,128)(2,1)S(1)}, bf16[144,4096]{1,0:T(8,128)(2,1)S(1)}, u32[]{:S(2)}, u32[]{:S(2)}) collective-permute-start(bf16[144,4096]{1,0:T(8,128)(2,1)S(1)} %arrived.3.x_ref), channel_id=1, source_target_pairs={{0,4},{1,3},{4,8},{5,1},{8,12},{9,5},{12,14},{13,9},{14,10},{15,13... | collective-permute-start | bytes 3538952 | tf_op jit(solution)/shard_map/ppermute | solution.py:456
  51.9 2.1 %collective-permute-start.10 = (bf16[144,2048]{1,0:T(8,128)(2,1)S(1)}, bf16[144,2048]{1,0:T(8,128)(2,1)S(1)}, u32[]{:S(2)}, u32[]{:S(2)}) collective-permute-start(bf16[144,2048]{1,0:T(8,128)(2,1)S(1)} %get-tuple-element.56.refs_15_), channel_id=1, source_target_pairs={{0,1},{1,0},{2,3},{3,2},{4,5},{5,4},{6,7},{7,6},{8,9},{9,8},{10,11... | collective-permute-start | bytes 1769480 | tf_op jit(solution)/shard_map/ppermute | solution.py:456
  51.9 2.8 %collective-permute-start.5 = (bf16[144,2048]{1,0:T(8,128)(2,1)S(1)}, bf16[144,2048]{1,0:T(8,128)(2,1)S(1)}, u32[]{:S(2)}, u32[]{:S(2)}) collective-permute-start(bf16[144,2048]{1,0:T(8,128)(2,1)S(1)} %get-tuple-element.52.refs_7_), channel_id=1, source_target_pairs={{0,1},{1,0},{2,3},{3,2},{4,5},{5,4},{6,7},{7,6},{8,9},{9,8},{10,11... | collective-permute-start | bytes 1769480 | tf_op jit(solution)/shard_map/ppermute | solution.py:456
  52.4 3.2 %collective-permute-start.9 = (bf16[144,2048]{1,0:T(8,128)(2,1)S(1)}, bf16[144,2048]{1,0:T(8,128)(2,1)S(1)}, u32[]{:S(2)}, u32[]{:S(2)}) collective-permute-start(bf16[144,2048]{1,0:T(8,128)(2,1)S(1)} %get-tuple-element.55.refs_13_), channel_id=1, source_target_pairs={{0,1},{1,0},{2,3},{3,2},{4,5},{5,4},{6,7},{7,6},{8,9},{9,8},{10,11... | collective-permute-start | bytes 1769480 | tf_op jit(solution)/shard_map/ppermute | solution.py:456
  68.9 21.2 %collective-permute-start.11 = (bf16[144,4096]{1,0:T(8,128)(2,1)S(1)}, bf16[144,4096]{1,0:T(8,128)(2,1)S(1)}, u32[]{:S(2)}, u32[]{:S(2)}) collective-permute-start(bf16[144,4096]{1,0:T(8,128)(2,1)S(1)} %after.6.x_ref), channel_id=1, source_target_pairs={{0,4},{1,3},{4,8},{5,1},{8,12},{9,5},{12,14},{13,9},{14,10},{15,13... | collective-permute-start | bytes 3538952 | tf_op jit(solution)/shard_map/ppermute | solution.py:456
  77.5 2.1 %collective-permute-start.14 = (bf16[144,2048]{1,0:T(8,128)(2,1)S(1)}, bf16[144,2048]{1,0:T(8,128)(2,1)S(1)}, u32[]{:S(2)}, u32[]{:S(2)}) collective-permute-start(bf16[144,2048]{1,0:T(8,128)(2,1)S(1)} %get-tuple-element.61.refs_6_.refs_7_), channel_id=1, source_target_pairs={{0,1},{1,0},{2,3},{3,2},{4,5},{5,4},{6,7},{7,6},{8,9},{9,8},{10,11... | collective-permute-start | bytes 1769480 | tf_op jit(solution)/shard_map/ppermute | solution.py:456
  77.7 3.5 %collective-permute-start.16 = (bf16[144,2048]{1,0:T(8,128)(2,1)S(1)}, bf16[144,2048]{1,0:T(8,128)(2,1)S(1)}, u32[]{:S(2)}, u32[]{:S(2)}) collective-permute-start(bf16[144,2048]{1,0:T(8,128)(2,1)S(1)} %get-tuple-element.63.refs_10_.refs_13_), channel_id=1, source_target_pairs={{0,1},{1,0},{2,3},{3,2},{4,5},{5,4},{6,7},{7,6},{8,9},{9,8},{10,11... | collective-permute-start | bytes 1769480 | tf_op jit(solution)/shard_map/ppermute | solution.py:456
  78.3 3.0 %collective-permute-start.12 = (bf16[144,2048]{1,0:T(8,128)(2,1)S(1)}, bf16[144,2048]{1,0:T(8,128)(2,1)S(1)}, u32[]{:S(2)}, u32[]{:S(2)}) collective-permute-start(bf16[144,2048]{1,0:T(8,128)(2,1)S(1)} %get-tuple-element.60.refs_4_.refs_5_), channel_id=1, source_target_pairs={{0,1},{1,0},{2,3},{3,2},{4,5},{5,4},{6,7},{7,6},{8,9},{9,8},{10,11... | collective-permute-start | bytes 1769480 | tf_op jit(solution)/shard_map/ppermute | solution.py:456
  78.4 3.8 %collective-permute-start.15 = (bf16[144,2048]{1,0:T(8,128)(2,1)S(1)}, bf16[144,2048]{1,0:T(8,128)(2,1)S(1)}, u32[]{:S(2)}, u32[]{:S(2)}) collective-permute-start(bf16[144,2048]{1,0:T(8,128)(2,1)S(1)} %get-tuple-element.62.refs_8_.refs_11_), channel_id=1, source_target_pairs={{0,1},{1,0},{2,3},{3,2},{4,5},{5,4},{6,7},{7,6},{8,9},{9,8},{10,11... | collective-permute-start | bytes 1769480 | tf_op jit(solution)/shard_map/ppermute | solution.py:456
  79.6 25.0 %collective-permute-start.18 = (bf16[144,4096]{1,0:T(8,128)(2,1)S(1)}, bf16[144,4096]{1,0:T(8,128)(2,1)S(1)}, u32[]{:S(2)}, u32[]{:S(2)}) collective-permute-start(bf16[144,4096]{1,0:T(8,128)(2,1)S(1)} %after.7.x_ref), channel_id=1, source_target_pairs={{0,4},{1,3},{4,8},{5,1},{8,12},{9,5},{12,14},{13,9},{14,10},{15,13... | collective-permute-start | bytes 3538952 | tf_op jit(solution)/shard_map/ppermute | solution.py:456
  90.2 2.2 %collective-permute-start.19 = (bf16[144,2048]{1,0:T(8,128)(2,1)S(1)}, bf16[144,2048]{1,0:T(8,128)(2,1)S(1)}, u32[]{:S(2)}, u32[]{:S(2)}) collective-permute-start(bf16[144,2048]{1,0:T(8,128)(2,1)S(1)} %get-tuple-element.68.refs_9_), channel_id=1, source_target_pairs={{0,1},{1,0},{2,3},{3,2},{4,5},{5,4},{6,7},{7,6},{8,9},{9,8},{10,11... | collective-permute-start | bytes 1769480 | tf_op jit(solution)/shard_map/ppermute | solution.py:456
  90.3 2.8 %collective-permute-start.20 = (bf16[144,2048]{1,0:T(8,128)(2,1)S(1)}, bf16[144,2048]{1,0:T(8,128)(2,1)S(1)}, u32[]{:S(2)}, u32[]{:S(2)}) collective-permute-start(bf16[144,2048]{1,0:T(8,128)(2,1)S(1)} %get-tuple-element.69.refs_15_), channel_id=1, source_target_pairs={{0,1},{1,0},{2,3},{3,2},{4,5},{5,4},{6,7},{7,6},{8,9},{9,8},{10,11... | collective-permute-start | bytes 1769480 | tf_op jit(solution)/shard_map/ppermute | solution.py:456
  90.8 24.6 %collective-permute-start.17 = (bf16[144,4096]{1,0:T(8,128)(2,1)S(1)}, bf16[144,4096]{1,0:T(8,128)(2,1)S(1)}, u32[]{:S(2)}, u32[]{:S(2)}) collective-permute-start(bf16[144,4096]{1,0:T(8,128)(2,1)S(1)} %after.8.x_ref), channel_id=1, source_target_pairs={{0,4},{1,3},{4,8},{5,1},{8,12},{9,5},{12,14},{13,9},{14,10},{15,13... | collective-permute-start | bytes 3538952 | tf_op jit(solution)/shard_map/ppermute | solution.py:456
  104.8 2.1 %collective-permute-start.21 = (bf16[144,2048]{1,0:T(8,128)(2,1)S(1)}, bf16[144,2048]{1,0:T(8,128)(2,1)S(1)}, u32[]{:S(2)}, u32[]{:S(2)}) collective-permute-start(bf16[144,2048]{1,0:T(8,128)(2,1)S(1)} %get-tuple-element.73.refs_5_), channel_id=1, source_target_pairs={{0,1},{1,0},{2,3},{3,2},{4,5},{5,4},{6,7},{7,6},{8,9},{9,8},{10,11... | collective-permute-start | bytes 1769480 | tf_op jit(solution)/shard_map/ppermute | solution.py:456
  105.0 2.7 %collective-permute-start.22 = (bf16[144,2048]{1,0:T(8,128)(2,1)S(1)}, bf16[144,2048]{1,0:T(8,128)(2,1)S(1)}, u32[]{:S(2)}, u32[]{:S(2)}) collective-permute-start(bf16[144,2048]{1,0:T(8,128)(2,1)S(1)} %get-tuple-element.74.refs_7_), channel_id=1, source_target_pairs={{0,1},{1,0},{2,3},{3,2},{4,5},{5,4},{6,7},{7,6},{8,9},{9,8},{10,11... | collective-permute-start | bytes 1769480 | tf_op jit(solution)/shard_map/ppermute | solution.py:456
  115.5 3.5 %collective-permute-start.24 = (bf16[144,2048]{1,0:T(8,128)(2,1)S(1)}, bf16[144,2048]{1,0:T(8,128)(2,1)S(1)}, u32[]{:S(2)}, u32[]{:S(2)}) collective-permute-start(bf16[144,2048]{1,0:T(8,128)(2,1)S(1)} %get-tuple-element.79.refs_4_), channel_id=1, source_target_pairs={{0,1},{1,0},{2,3},{3,2},{4,5},{5,4},{6,7},{7,6},{8,9},{9,8},{10,11... | collective-permute-start | bytes 1769480 | tf_op jit(solution)/shard_map/ppermute | solution.py:456
  115.5 3.5 %collective-permute-start.23 = (bf16[144,2048]{1,0:T(8,128)(2,1)S(1)}, bf16[144,2048]{1,0:T(8,128)(2,1)S(1)}, u32[]{:S(2)}, u32[]{:S(2)}) collective-permute-start(bf16[144,2048]{1,0:T(8,128)(2,1)S(1)} %get-tuple-element.78.refs_6_.refs_4_.refs_5_), channel_id=1, source_target_pairs={{0,1},{1,0},{2,3},{3,2},{4,5},{5,4},{6,7},{7,6},{8,9},{9,8},{10,11... | collective-permute-start | bytes 1769480 | tf_op jit(solution)/shard_map/ppermute | solution.py:456
  122.0 6.4 %collective-permute-start.27 = (f32[8,128]{1,0:T(8,128)S(1)}, f32[8,128]{1,0:T(8,128)S(1)}, u32[]{:S(2)}, u32[]{:S(2)}) collective-permute-start(f32[8,128]{1,0:T(8,128)S(1)} %get-tuple-element.88), channel_id=1, source_target_pairs={{0,6},{1,7},{2,4},{3,5},{4,2},{5,3},{6,0},{7,1},{8,14},{9,15},{10,... | collective-permute-start | bytes 12296 | tf_op jit(solution)/shard_map/ppermute | solution.py:436
  124.4 4.0 %collective-permute-start.26 = (f32[8,128]{1,0:T(8,128)S(1)}, f32[8,128]{1,0:T(8,128)S(1)}, u32[]{:S(2)}, u32[]{:S(2)}) collective-permute-start(f32[8,128]{1,0:T(8,128)S(1)} %get-tuple-element.88), channel_id=1, source_target_pairs={{0,4},{1,5},{2,6},{3,7},{4,0},{5,1},{6,2},{7,3},{8,12},{9,13},{10,... | collective-permute-start | bytes 12296 | tf_op jit(solution)/shard_map/ppermute | solution.py:436
  124.8 3.6 %collective-permute-start.25 = (f32[8,128]{1,0:T(8,128)S(1)}, f32[8,128]{1,0:T(8,128)S(1)}, u32[]{:S(2)}, u32[]{:S(2)}) collective-permute-start(f32[8,128]{1,0:T(8,128)S(1)} %get-tuple-element.88), channel_id=1, source_target_pairs={{0,2},{1,3},{2,0},{3,1},{4,6},{5,7},{6,4},{7,5},{8,10},{9,11},{10,... | collective-permute-start | bytes 12296 | tf_op jit(solution)/shard_map/ppermute | solution.py:436
  128.4 5.5 %collective-permute-start.30 = (f32[8,128]{1,0:T(8,128)S(1)}, f32[8,128]{1,0:T(8,128)S(1)}, u32[]{:S(2)}, u32[]{:S(2)}) collective-permute-start(f32[8,128]{1,0:T(8,128)S(1)} %after.11), channel_id=1, source_target_pairs={{0,9},{1,8},{2,11},{3,10},{4,13},{5,12},{6,15},{7,14},{8,1},{9,0},... | collective-permute-start | bytes 12296 | tf_op jit(solution)/shard_map/ppermute | solution.py:436
  129.9 4.5 %collective-permute-start.29 = (f32[8,128]{1,0:T(8,128)S(1)}, f32[8,128]{1,0:T(8,128)S(1)}, u32[]{:S(2)}, u32[]{:S(2)}) collective-permute-start(f32[8,128]{1,0:T(8,128)S(1)} %after.11), channel_id=1, source_target_pairs={{0,8},{1,9},{2,10},{3,11},{4,12},{5,13},{6,14},{7,15},{8,0},{9,1},... | collective-permute-start | bytes 12296 | tf_op jit(solution)/shard_map/ppermute | solution.py:436
  131.2 3.3 %collective-permute-start.28 = (f32[8,128]{1,0:T(8,128)S(1)}, f32[8,128]{1,0:T(8,128)S(1)}, u32[]{:S(2)}, u32[]{:S(2)}) collective-permute-start(f32[8,128]{1,0:T(8,128)S(1)} %after.11), channel_id=1, source_target_pairs={{0,1},{1,0},{2,3},{3,2},{4,5},{5,4},{6,7},{7,6},{8,9},{9,8},{10,11... | collective-permute-start | bytes 12296 | tf_op jit(solution)/shard_map/ppermute | solution.py:436

commit v11 on v10

--- a/solution.py
+++ b/solution.py
@@ -140,26 +140,6 @@
     return copy, (left, right), count, ats
 
 
-def flip_kernel(x_ref, out_ref):
-    width = 512
-    for i in range(x_ref.shape[1] // width):
-        part = slice(i * width, (i + 1) * width)
-        out_ref[part, :] = x_ref[:, part].T
-
-
-def flipped(x):
-    vmem = pl.BlockSpec(memory_space=pltpu.VMEM)
-    return pl.pallas_call(
-        flip_kernel,
-        in_specs=[vmem],
-        out_specs=vmem,
-        out_shape=pltpu.VMEM(x.shape[::-1], x.dtype),
-        compiler_params=pltpu.CompilerParams(vmem_limit_bytes=8 * MIB),
-        cost_estimate=pl.CostEstimate(flops=1, bytes_accessed=1, transcendentals=0),
-        name="flipped",
-    )(pltpu.with_memory_space_constraint(x, pltpu.VMEM))
-
-
 def arrive_kernel(count_ref, x_ref, done_ref, out_ref):
     zero_dead(count_ref[0, 0], out_ref)
 
@@ -224,8 +204,8 @@
         if attn:
             total_ref[...] += lax.dot_general(
                 jnp.concatenate(g, axis=0),
-                weight_ref[there, :],
-                (((1,), (0,)), ((), ())),
+                weight_ref[:, there],
+                (((1,), (1,)), ((), ())),
                 preferred_element_type=jnp.float32,
             )
         return carry
@@ -450,7 +430,7 @@
     me = lax.axis_index("dp").astype(jnp.int32).reshape(1)
     where = (jnp.asarray(ring.owners()), me, head_counts)
     shapes = (slots, o_weight.shape[0], features, rows)
-    half = features // 2
+    weight, half = o_weight, features // 2
 
     def send(x, pairs):
         return lax.ppermute(x, "dp", pairs)
@@ -471,9 +451,9 @@
     ats = [ats.pop(0) if x else None for x in spans]
     y = send(own, ring.crossing())
     counts = send(count, ring.along()), send(count, ring.crossing())
-    first = [near, swapped(near)]
-    w, done = phase(where, shapes, 0, grouped(*first), at=ats[0])
-    weight, out = flipped(o_weight), None
+    w, out, done = phase(
+        where, shapes, 0, grouped(near, swapped(near)), at=ats[0], weight=weight, attn="whole"
+    )
 
     for k in range(1, last):
         x = arrived(done, counts[0], x) if k == 1 else after(done, x)[0]
@@ -486,7 +466,7 @@
                 where, shapes, 2 * (i + 1) - len(held), grouped(*held), at=ats[i], w=w,
                 w_from=len(held) - 2, weight=weight, attn="whole", out=out,
             )
-        y = arrived(weight, counts[1], y) if k == 1 else after(done, y)[0]
+        y = arrived(done, counts[1], y) if k == 1 else after(done, y)[0]
         y, near_y = send(y, ring.along()) if k < last - 1 else None, split(y)
         far_y = swapped(near_y)
         groups = grouped(near_x, far_x, near_y, far_y)
@@ -499,12 +479,10 @@
             held = [near_x, far_x, near_y, far_y]
             w, done = phase(where, shapes, 2 * i, groups, at=ats[i], w=w)
         else:
-            groups = grouped(*first, near_x, far_x, near_y, far_y)
             w, out, done = phase(
-                where, shapes, 2 * i - len(first), groups, at=ats[i], w=w,
-                w_from=len(first), weight=weight, attn="whole", out=out,
-            )
-            first = []
+                where, shapes, 2 * i, groups, at=ats[i], w=w,
+                weight=weight, attn="whole", out=out,
+            )
 
     (x,) = after(done, x)
     near = split(x)

time: 138 us -> 117 us (0.85)
  waiting for transfers between devices: 41.3 us -> 17.9 us
  starting transfers between devices: 25.2 us -> 28.8 us
    ppermute x25, waiting for transfers between devices: 40.8 us -> 17 us  [send(): return lax.ppermute(x, 'dp', pairs)]
    ppermute x25, starting transfers between devices: 18.8 us -> 22.3 us  [send(): return lax.ppermute(x, 'dp', pairs)]
    pallas_call x1 -> x0, Pallas kernels: 1.67 us -> none  [flipped(): pl.pallas_call(flip_kernel, in_specs=[vmem], out_specs=vmem, out_shape=pl...]
  transfers between devices with their start and end apart: 31 -> 31, of which waited for: 15 -> 14; matrix products, arithmetic and copies ran while one was open for 0% -> 0% of each run, Pallas kernels for 40% -> 50%
where the time goes in v11:
time: 117 us
  Pallas kernels  64.4 us (55%)
  starting transfers between devices  28.8 us (25%)
  waiting for transfers between devices  17.9 us (15%)
  local copies, waits for them, and re-layouts  3.49 us (3%)
  between operations  2.42 us (2%)
    pallas_call x9, Pallas kernels, phase(): pl.pallas_call(functools.partial(phase_kernel, spec), in_specs=specs, out...  55.4 us
    ppermute x25, starting transfers between devices, send(): return lax.ppermute(x, 'dp', pairs)  22.3 us
    ppermute x25, waiting for transfers between devices, send(): return lax.ppermute(x, 'dp', pairs)  17 us
    ppermute x6, starting transfers between devices, exchange(): lax.ppermute(x, 'dp', [(d, d ^ mask) for d in range(devices)])  6.5 us
    pallas_call x1, Pallas kernels, prepared(): pl.pallas_call(functools.partial(prep_kernel, spans, rows), in_specs=[sme...  3.96 us
    unnamed x8, local copies, waits for them, and re-layouts  3.49 us
    pallas_call x1, Pallas kernels, scaled(): pl.pallas_call(functools.partial(scale_kernel, parts), in_specs=[vmem, vm...  3 us
  transfers between devices with their start and end apart: 31, of which 14 were waited for; matrix products, arithmetic and copies ran while one was open for 0% of the time, Pallas kernels for 50%

profile of v11, /device:TPU:0, one launch (start us, length us, event | category | flops | bytes accessed | tf_op | source)
XLA Modules:
  0.0 117.0 jit_solution(14007180377500773919)
XLA Ops:
  0.6 3.1 %collective-permute-start.1 = (bf16[144,4096]{1,0:T(8,128)(2,1)}, bf16[144,4096]{1,0:T(8,128)(2,1)S(1)}, u32[]{:S(2)}, u32[]{:S(2)}) collective-permute-start(bf16[144,4096]{1,0:T(8,128)(2,1)} %grad_ref.1), channel_id=1, source_target_pairs={{0,4},{1,3},{4,8},{5,1},{8,12},{9,5},{12,14},{13,9},{14,10},{15,13... | collective-permute-start | bytes 3538952 | tf_op jit(solution)/shard_map/ppermute | solution.py:436
  5.0 0.7 copy-done.1
  5.7 4.0 %prep.1 = (bf16[144,4096]{1,0:T(8,128)(2,1)S(1)}, bf16[144,2048]{1,0:T(8,128)(2,1)S(1)}, bf16[144,2048]{1,0:T(8,128)(2,1)S(1)}, s32[8,128]{1,0:T(8,128)S(1)}, bf...) custom-call(s32[16,16]{1,0:T(8,128)S(1)} %copy-done.1, ...), custom_call_target="tpu_custom_call" | custom-call | flops 1 | bytes 1 | tf_op jit(solution)/shard_map/prep/pallas_call | solution.py:121
  9.7 0.1 collective-permute-start.2
  9.7 0.5 collective-permute-start.3
  10.2 0.7 collective-permute-start.7
  10.9 1.0 collective-permute-start
  12.0 0.6 collective-permute-done.3.refs_8_
  12.6 2.8 %copy-done = bf16[768,4096]{1,0:T(8,128)(2,1)S(1)} copy-done((bf16[768,4096]{1,0:T(8,128)(2,1)S(1)}, bf16[768,4096]{1,0:T(8,128)(2,1)}, u32[]{:S(2)}) %copy-start) | copy-done | bytes 6291480
  15.4 7.3 %phase_w_whole.4 = (f32[768,4096]{1,0:T(8,128)S(1)}, bf16[2304,768]{1,0:T(8,128)(2,1)}, f32[8,128]{1,0:T(8,128)S(1)}) custom-call(s32[16,16]{1,0:T(8,128)S(1)} %copy-done.1, s32[1]{0:T(128)} %bitcast.me_ref.refs_1_, s32[1]{0:T(128)S(6)} %copy.44.heads_ref.refs_2_, bf16[768,288]{1,0:T(8,128)(2,1)S(1)} %get-tuple-element.48.refs_3_, ...), custom_call_target="tpu_custom_call" | custom-call | flops 1 | bytes 1 | tf_op jit(solution)/shard_map/phase_w_whole/pallas_call | solution.py:304
  22.6 0.4 collective-permute-done.count_ref
  23.0 0.7 arrived.2.x_ref
  23.6 0.1 split.7
  23.8 0.1 collective-permute-start.5
  23.8 2.5 %collective-permute-start.4 = (bf16[144,4096]{1,0:T(8,128)(2,1)S(1)}, bf16[144,4096]{1,0:T(8,128)(2,1)S(1)}, u32[]{:S(2)}, u32[]{:S(2)}) collective-permute-start(bf16[144,4096]{1,0:T(8,128)(2,1)S(1)} %arrived.2.x_ref), channel_id=1, source_target_pairs={{0,4},{1,3},{4,8},{5,1},{8,12},{9,5},{12,14},{13,9},{14,10},{15,13... | collective-permute-start | bytes 3538952 | tf_op jit(solution)/shard_map/ppermute | solution.py:436
  26.3 2.2 %collective-permute-start.6 = (s32[8,128]{1,0:T(8,128)S(1)}, s32[8,128]{1,0:T(8,128)S(1)}, u32[]{:S(2)}, u32[]{:S(2)}) collective-permute-start(s32[8,128]{1,0:T(8,128)S(1)} %get-tuple-element.47), channel_id=1, source_target_pairs={{0,3},{1,4},{4,1},{5,8},{8,5},{9,12},{12,9},{13,14},{14,13},{15,10... | collective-permute-start | bytes 12296 | tf_op jit(solution)/shard_map/ppermute | solution.py:436
  28.5 4.2 %collective-permute-done.6.count_ref = s32[8,128]{1,0:T(8,128)S(1)} collective-permute-done((s32[8,128]{1,0:T(8,128)S(1)}, s32[8,128]{1,0:T(8,128)S(1)}, u32[]{:S(2)}, u32[]{:S(2)}) %collective-permute-start.6) | collective-permute-done | bytes 4128 | tf_op jit(solution)/shard_map/ppermute | solution.py:436
  32.8 0.6 arrived.3.x_ref
  33.4 0.1 split.8
  33.5 3.0 %collective-permute-start.13 = (bf16[144,4096]{1,0:T(8,128)(2,1)S(1)}, bf16[144,4096]{1,0:T(8,128)(2,1)S(1)}, u32[]{:S(2)}, u32[]{:S(2)}) collective-permute-start(bf16[144,4096]{1,0:T(8,128)(2,1)S(1)} %arrived.3.x_ref), channel_id=1, source_target_pairs={{0,4},{1,3},{4,8},{5,1},{8,12},{9,5},{12,14},{13,9},{14,10},{15,13... | collective-permute-start | bytes 3538952 | tf_op jit(solution)/shard_map/ppermute | solution.py:436
  36.5 0.5 collective-permute-start.8
  37.1 1.5 %collective-permute-done.9.refs_10_ = bf16[144,2048]{1,0:T(8,128)(2,1)S(1)} collective-permute-done((bf16[144,2048]{1,0:T(8,128)(2,1)S(1)}, bf16[144,2048]{1,0:T(8,128)(2,1)S(1)}, u32[]{:S(2)}, u32[]{:S(2)}) %collective-permute-start.9) | collective-permute-done | bytes 589856 | tf_op jit(solution)/shard_map/ppermute | solution.py:436
  38.5 0.8 collective-permute-done.8.refs_8_
  39.4 0.8 collective-permute-done.10.refs_12_
  40.2 11.1 %phase_w_whole.5 = (f32[768,4096]{1,0:T(8,128)S(1)}, bf16[2304,768]{1,0:T(8,128)(2,1)}, f32[8,128]{1,0:T(8,128)S(1)}) custom-call(s32[16,16]{1,0:T(8,128)S(1)} %copy-done.1, s32[1]{0:T(128)} %bitcast.me_ref.refs_1_, s32[1]{0:T(128)S(6)} %copy.44.heads_ref.refs_2_, ...), custom_call_target="tpu_custom_call", output_to_operand_aliasing={{0}: (13, {}), {1}: (14, {})} | custom-call | flops 1 | bytes 1 | tf_op jit(solution)/shard_map/phase_w_whole/pallas_call | solution.py:304
  51.4 1.6 %collective-permute-start.11 = (bf16[144,4096]{1,0:T(8,128)(2,1)S(1)}, bf16[144,4096]{1,0:T(8,128)(2,1)S(1)}, u32[]{:S(2)}, u32[]{:S(2)}) collective-permute-start(bf16[144,4096]{1,0:T(8,128)(2,1)S(1)} %after.6.x_ref), channel_id=1, source_target_pairs={{0,4},{1,3},{4,8},{5,1},{8,12},{9,5},{12,14},{13,9},{14,10},{15,13... | collective-permute-start | bytes 3538952 | tf_op jit(solution)/shard_map/ppermute | solution.py:436
  53.0 0.1 split.9
  53.1 0.1 collective-permute-start.12
  53.2 0.5 collective-permute-start.15
  53.7 2.4 %collective-permute-done.13.refs_0_ = bf16[144,4096]{1,0:T(8,128)(2,1)S(1)} collective-permute-done((bf16[144,4096]{1,0:T(8,128)(2,1)S(1)}, bf16[144,4096]{1,0:T(8,128)(2,1)S(1)}, u32[]{:S(2)}, u32[]{:S(2)}) %collective-permute-start.13) | collective-permute-done | bytes 1179680 | tf_op jit(solution)/shard_map/ppermute | solution.py:436
  56.1 0.1 split.10
  56.2 0.1 collective-permute-start.14
  56.2 0.5 collective-permute-start.16
  56.7 2.1 %collective-permute-start.18 = (bf16[144,4096]{1,0:T(8,128)(2,1)S(1)}, bf16[144,4096]{1,0:T(8,128)(2,1)S(1)}, u32[]{:S(2)}, u32[]{:S(2)}) collective-permute-start(bf16[144,4096]{1,0:T(8,128)(2,1)S(1)} %after.7.x_ref), channel_id=1, source_target_pairs={{0,4},{1,3},{4,8},{5,1},{8,12},{9,5},{12,14},{13,9},{14,10},{15,13... | collective-permute-start | bytes 3538952 | tf_op jit(solution)/shard_map/ppermute | solution.py:436
  58.8 0.2 collective-permute-done.16.refs_11_.refs_14_
  59.1 6.3 %phase_w_None.3 = (f32[768,4096]{1,0:T(8,128)S(1)}, f32[8,128]{1,0:T(8,128)S(1)}) custom-call(s32[16,16]{1,0:T(8,128)S(1)} %copy-done.1, s32[1]{0:T(128)} %bitcast.me_ref.refs_1_, s32[1]{0:T(128)S(6)} %copy.44.heads_ref.refs_2_, bf16[768,576]{1,0:T(8,128)(2,1)S(1)} %get-tuple-element.61.refs_3_, ...), custom_call_target="tpu_custom_call", output_to_operand_aliasing={{0}: (12, {})} | custom-call | flops 1 | bytes 1 | tf_op jit(solution)/shard_map/phase_w_None/pallas_call | solution.py:304
  65.3 3.4 %collective-permute-done.11.refs_0_ = bf16[144,4096]{1,0:T(8,128)(2,1)S(1)} collective-permute-done((bf16[144,4096]{1,0:T(8,128)(2,1)S(1)}, bf16[144,4096]{1,0:T(8,128)(2,1)S(1)}, u32[]{:S(2)}, u32[]{:S(2)}) %collective-permute-start.11) | collective-permute-done | bytes 1179680 | tf_op jit(solution)/shard_map/ppermute | solution.py:436
  68.7 0.1 split.11
  68.9 0.5 collective-permute-start.20
  69.4 2.1 %collective-permute-start.17 = (bf16[144,4096]{1,0:T(8,128)(2,1)S(1)}, bf16[144,4096]{1,0:T(8,128)(2,1)S(1)}, u32[]{:S(2)}, u32[]{:S(2)}) collective-permute-start(bf16[144,4096]{1,0:T(8,128)(2,1)S(1)} %after.8.x_ref), channel_id=1, source_target_pairs={{0,4},{1,3},{4,8},{5,1},{8,12},{9,5},{12,14},{13,9},{14,10},{15,13... | collective-permute-start | bytes 3538952 | tf_op jit(solution)/shard_map/ppermute | solution.py:436
  71.5 0.3 collective-permute-done.20.refs_16_
  71.7 11.7 %phase_w_whole.6 = (f32[768,4096]{1,0:T(8,128)S(1)}, bf16[2304,768]{1,0:T(8,128)(2,1)}, f32[8,128]{1,0:T(8,128)S(1)}) custom-call(s32[16,16]{1,0:T(8,128)S(1)} %copy-done.1, s32[1]{0:T(128)} %bitcast.me_ref.refs_1_, s32[1]{0:T(128)S(6)} %copy.44.heads_ref.refs_2_, ...), custom_call_target="tpu_custom_call", output_to_operand_aliasing={{0}: (17, {}), {1}: (18, {})} | custom-call | flops 1 | bytes 1 | tf_op jit(solution)/shard_map/phase_w_whole/pallas_call | solution.py:304
  83.5 0.1 split.12
  83.6 0.2 collective-permute-start.21
  83.8 0.4 collective-permute-start.22
  84.2 1.5 %collective-permute-done.21.refs_6_ = bf16[144,2048]{1,0:T(8,128)(2,1)S(1)} collective-permute-done((bf16[144,2048]{1,0:T(8,128)(2,1)S(1)}, bf16[144,2048]{1,0:T(8,128)(2,1)S(1)}, u32[]{:S(2)}, u32[]{:S(2)}) %collective-permute-start.21) | collective-permute-done | bytes 589856 | tf_op jit(solution)/shard_map/ppermute | solution.py:436
  85.6 0.8 collective-permute-done.22.refs_8_
  86.5 7.5 %phase_w_whole.7 = (f32[768,4096]{1,0:T(8,128)S(1)}, bf16[2304,768]{1,0:T(8,128)(2,1)}, f32[8,128]{1,0:T(8,128)S(1)}) custom-call(s32[16,16]{1,0:T(8,128)S(1)} %copy-done.1, s32[1]{0:T(128)} %bitcast.me_ref.refs_1_, s32[1]{0:T(128)S(6)} %copy.44.heads_ref.refs_2_, ...), custom_call_target="tpu_custom_call", output_to_operand_aliasing={{0}: (9, {}), {1}: (10, {})} | custom-call | flops 1 | bytes 1 | tf_op jit(solution)/shard_map/phase_w_whole/pallas_call | solution.py:304
  94.0 0.1 split.13
  94.1 0.2 collective-permute-start.24
  94.3 0.4 collective-permute-start.23
  94.7 3.0 %phase_w_None.4 = (f32[768,4096]{1,0:T(8,128)S(1)}, f32[8,128]{1,0:T(8,128)}) custom-call(s32[16,16]{1,0:T(8,128)S(1)} %copy-done.1, s32[1]{0:T(128)} %bitcast.me_ref.refs_1_, s32[1]{0:T(128)S(6)} %copy.44.heads_ref.refs_2_, bf16[768,144]{1,0:T(8,128)(2,1)S(1)} %get-tuple-element.86.refs_3_, ...), custom_call_target="tpu_custom_call", output_to_operand_aliasing={{0}: (6, {})} | custom-call | flops 1 | bytes 1 | tf_op jit(solution)/shard_map/phase_w_None/pallas_call | solution.py:304
  97.7 3.0 %phase_w_None.5 = (f32[768,4096]{1,0:T(8,128)S(1)}, f32[8,128]{1,0:T(8,128)S(1)}) custom-call(s32[16,16]{1,0:T(8,128)S(1)} %copy-done.1, s32[1]{0:T(128)} %bitcast.me_ref.refs_1_, s32[1]{0:T(128)S(6)} %copy.44.heads_ref.refs_2_, bf16[768,144]{1,0:T(8,128)(2,1)S(1)} %get-tuple-element.85.refs_3_, ...), custom_call_target="tpu_custom_call", output_to_operand_aliasing={{0}: (6, {})} | custom-call | flops 1 | bytes 1 | tf_op jit(solution)/shard_map/phase_w_None/pallas_call | solution.py:304
  100.7 3.1 %collective-permute-start.27 = (f32[8,128]{1,0:T(8,128)S(1)}, f32[8,128]{1,0:T(8,128)S(1)}, u32[]{:S(2)}, u32[]{:S(2)}) collective-permute-start(f32[8,128]{1,0:T(8,128)S(1)} %get-tuple-element.90), channel_id=1, source_target_pairs={{0,6},{1,7},{2,4},{3,5},{4,2},{5,3},{6,0},{7,1},{8,14},{9,15},{10,... | collective-permute-start | bytes 12296 | tf_op jit(solution)/shard_map/ppermute | solution.py:416
  103.8 0.4 collective-permute-start.26
  104.3 0.2 collective-permute-start.25
  104.5 2.9 %phase__first.1 = (f32[288,768]{1,0:T(8,128)S(1)}, f32[8,128]{1,0:T(8,128)S(1)}) custom-call(s32[16,16]{1,0:T(8,128)S(1)} %copy-done.1, s32[1]{0:T(128)} %bitcast.me_ref.refs_1_, s32[1]{0:T(128)S(6)} %copy.44.heads_ref.refs_2_, bf16[768,4096]{1,0:T(8,128)(2,1)S(1)} %bitcast.2, bf16[144,2048]{1,0:T(8,128)(2,1)S(1)} %get-tuple-element.81.refs_4_, ...), custom_call_target="tpu_custom_call" | custom-call | flops 1 | bytes 1 | tf_op jit(solution)/shard_map/phase__first/pallas_call | solution.py:304
  107.4 0.4 collective-permute-done.25
  107.9 1.4 %collective-permute-start.30 = (f32[8,128]{1,0:T(8,128)S(1)}, f32[8,128]{1,0:T(8,128)S(1)}, u32[]{:S(2)}, u32[]{:S(2)}) collective-permute-start(f32[8,128]{1,0:T(8,128)S(1)} %after.11), channel_id=1, source_target_pairs={{0,9},{1,8},{2,11},{3,10},{4,13},{5,12},{6,15},{7,14},{8,1},{9,0},... | collective-permute-start | bytes 12296 | tf_op jit(solution)/shard_map/ppermute | solution.py:416
  109.3 1.2 %collective-permute-start.29 = (f32[8,128]{1,0:T(8,128)S(1)}, f32[8,128]{1,0:T(8,128)S(1)}, u32[]{:S(2)}, u32[]{:S(2)}) collective-permute-start(f32[8,128]{1,0:T(8,128)S(1)} %after.11), channel_id=1, source_target_pairs={{0,8},{1,9},{2,10},{3,11},{4,12},{5,13},{6,14},{7,15},{8,0},{9,1},... | collective-permute-start | bytes 12296 | tf_op jit(solution)/shard_map/ppermute | solution.py:416
  110.6 0.1 collective-permute-start.28
  110.6 2.7 %phase__last.1 = (bf16[2304,768]{1,0:T(8,128)(2,1)}, f32[8,128]{1,0:T(8,128)}) custom-call(s32[16,16]{1,0:T(8,128)S(1)} %copy-done.1, s32[1]{0:T(128)} %bitcast.me_ref.refs_1_, s32[1]{0:T(128)S(6)} %copy.44.heads_ref.refs_2_, bf16[768,4096]{1,0:T(8,128)(2,1)S(1)} %bitcast.2, ...), custom_call_target="tpu_custom_call", output_to_operand_aliasing={{0}: (7, {})} | custom-call | flops 1 | bytes 1 | tf_op jit(solution)/shard_map/phase__last/pallas_call | solution.py:304
  113.4 0.4 collective-permute-done.29
  113.8 3.0 %scale.1 = bf16[768,4096]{1,0:T(8,128)(2,1)} custom-call(f32[768,4096]{1,0:T(8,128)S(1)} %get-tuple-element.89.w_ref, f32[8,128]{1,0:T(8,128)S(1)} %add_add_fusion.squares_ref), custom_call_target="tpu_custom_call" | custom-call | flops 3145728 | bytes 6291456 | tf_op jit(solution)/shard_map/scale/pallas_call | solution.py:344
  (35 shorter events, 0.2 us)
Async XLA Ops:
  0.6 22.4 %collective-permute-start.1 = (bf16[144,4096]{1,0:T(8,128)(2,1)}, bf16[144,4096]{1,0:T(8,128)(2,1)S(1)}, u32[]{:S(2)}, u32[]{:S(2)}) collective-permute-start(bf16[144,4096]{1,0:T(8,128)(2,1)} %grad_ref.1), channel_id=1, source_target_pairs={{0,4},{1,3},{4,8},{5,1},{8,12},{9,5},{12,14},{13,9},{14,10},{15,13... | collective-permute-start | bytes 3538952 | tf_op jit(solution)/shard_map/ppermute | solution.py:436
  5.0 0.7 copy-start.1
  9.7 2.3 %collective-permute-start.2 = (bf16[144,2048]{1,0:T(8,128)(2,1)S(1)}, bf16[144,2048]{1,0:T(8,128)(2,1)S(1)}, u32[]{:S(2)}, u32[]{:S(2)}) collective-permute-start(bf16[144,2048]{1,0:T(8,128)(2,1)S(1)} %get-tuple-element.49.refs_5_), channel_id=1, source_target_pairs={{0,1},{1,0},{2,3},{3,2},{4,5},{5,4},{6,7},{7,6},{8,9},{9,8},{10,11... | collective-permute-start | bytes 1769480 | tf_op jit(solution)/shard_map/ppermute | solution.py:436
  9.7 2.8 %collective-permute-start.3 = (bf16[144,2048]{1,0:T(8,128)(2,1)S(1)}, bf16[144,2048]{1,0:T(8,128)(2,1)S(1)}, u32[]{:S(2)}, u32[]{:S(2)}) collective-permute-start(bf16[144,2048]{1,0:T(8,128)(2,1)S(1)} %get-tuple-element.50.refs_7_), channel_id=1, source_target_pairs={{0,1},{1,0},{2,3},{3,2},{4,5},{5,4},{6,7},{7,6},{8,9},{9,8},{10,11... | collective-permute-start | bytes 1769480 | tf_op jit(solution)/shard_map/ppermute | solution.py:436
  10.2 22.5 %collective-permute-start.7 = (bf16[144,4096]{1,0:T(8,128)(2,1)S(1)}, bf16[144,4096]{1,0:T(8,128)(2,1)S(1)}, u32[]{:S(2)}, u32[]{:S(2)}) collective-permute-start(bf16[144,4096]{1,0:T(8,128)(2,1)S(1)} %get-tuple-element.54), channel_id=1, source_target_pairs={{0,3},{1,4},{4,1},{5,8},{8,5},{9,12},{12,9},{13,14},{14,13},{15,10... | collective-permute-start | bytes 3538952 | tf_op jit(solution)/shard_map/ppermute | solution.py:436
  10.9 12.1 %collective-permute-start = (s32[8,128]{1,0:T(8,128)S(1)}, s32[8,128]{1,0:T(8,128)S(1)}, u32[]{:S(2)}, u32[]{:S(2)}) collective-permute-start(s32[8,128]{1,0:T(8,128)S(1)} %get-tuple-element.47), channel_id=1, source_target_pairs={{0,4},{1,3},{4,8},{5,1},{8,12},{9,5},{12,14},{13,9},{14,10},{15,13... | collective-permute-start | bytes 12296 | tf_op jit(solution)/shard_map/ppermute | solution.py:436
  12.6 2.8 %copy-start = (bf16[768,4096]{1,0:T(8,128)(2,1)S(1)}, bf16[768,4096]{1,0:T(8,128)(2,1)}, u32[]{:S(2)}) copy-start(bf16[768,4096]{1,0:T(8,128)(2,1)} %refs_3_.3) | copy-start | bytes 18874372
  23.8 13.3 %collective-permute-start.5 = (bf16[144,2048]{1,0:T(8,128)(2,1)S(1)}, bf16[144,2048]{1,0:T(8,128)(2,1)S(1)}, u32[]{:S(2)}, u32[]{:S(2)}) collective-permute-start(bf16[144,2048]{1,0:T(8,128)(2,1)S(1)} %get-tuple-element.53.refs_5_), channel_id=1, source_target_pairs={{0,1},{1,0},{2,3},{3,2},{4,5},{5,4},{6,7},{7,6},{8,9},{9,8},{10,11... | collective-permute-start | bytes 1769480 | tf_op jit(solution)/shard_map/ppermute | solution.py:436
  23.8 27.5 %collective-permute-start.4 = (bf16[144,4096]{1,0:T(8,128)(2,1)S(1)}, bf16[144,4096]{1,0:T(8,128)(2,1)S(1)}, u32[]{:S(2)}, u32[]{:S(2)}) collective-permute-start(bf16[144,4096]{1,0:T(8,128)(2,1)S(1)} %arrived.2.x_ref), channel_id=1, source_target_pairs={{0,4},{1,3},{4,8},{5,1},{8,12},{9,5},{12,14},{13,9},{14,10},{15,13... | collective-permute-start | bytes 3538952 | tf_op jit(solution)/shard_map/ppermute | solution.py:436
  26.3 6.4 %collective-permute-start.6 = (s32[8,128]{1,0:T(8,128)S(1)}, s32[8,128]{1,0:T(8,128)S(1)}, u32[]{:S(2)}, u32[]{:S(2)}) collective-permute-start(s32[8,128]{1,0:T(8,128)S(1)} %get-tuple-element.47), channel_id=1, source_target_pairs={{0,3},{1,4},{4,1},{5,8},{8,5},{9,12},{12,9},{13,14},{14,13},{15,10... | collective-permute-start | bytes 12296 | tf_op jit(solution)/shard_map/ppermute | solution.py:436
  33.5 22.5 %collective-permute-start.13 = (bf16[144,4096]{1,0:T(8,128)(2,1)S(1)}, bf16[144,4096]{1,0:T(8,128)(2,1)S(1)}, u32[]{:S(2)}, u32[]{:S(2)}) collective-permute-start(bf16[144,4096]{1,0:T(8,128)(2,1)S(1)} %arrived.3.x_ref), channel_id=1, source_target_pairs={{0,4},{1,3},{4,8},{5,1},{8,12},{9,5},{12,14},{13,9},{14,10},{15,13... | collective-permute-start | bytes 3538952 | tf_op jit(solution)/shard_map/ppermute | solution.py:436
  36.5 2.0 %collective-permute-start.9 = (bf16[144,2048]{1,0:T(8,128)(2,1)S(1)}, bf16[144,2048]{1,0:T(8,128)(2,1)S(1)}, u32[]{:S(2)}, u32[]{:S(2)}) collective-permute-start(bf16[144,2048]{1,0:T(8,128)(2,1)S(1)} %get-tuple-element.56.refs_9_), channel_id=1, source_target_pairs={{0,1},{1,0},{2,3},{3,2},{4,5},{5,4},{6,7},{7,6},{8,9},{9,8},{10,11... | collective-permute-start | bytes 1769480 | tf_op jit(solution)/shard_map/ppermute | solution.py:436
  36.5 2.8 %collective-permute-start.8 = (bf16[144,2048]{1,0:T(8,128)(2,1)S(1)}, bf16[144,2048]{1,0:T(8,128)(2,1)S(1)}, u32[]{:S(2)}, u32[]{:S(2)}) collective-permute-start(bf16[144,2048]{1,0:T(8,128)(2,1)S(1)} %get-tuple-element.55.refs_7_), channel_id=1, source_target_pairs={{0,1},{1,0},{2,3},{3,2},{4,5},{5,4},{6,7},{7,6},{8,9},{9,8},{10,11... | collective-permute-start | bytes 1769480 | tf_op jit(solution)/shard_map/ppermute | solution.py:436
  37.1 3.2 %collective-permute-start.10 = (bf16[144,2048]{1,0:T(8,128)(2,1)S(1)}, bf16[144,2048]{1,0:T(8,128)(2,1)S(1)}, u32[]{:S(2)}, u32[]{:S(2)}) collective-permute-start(bf16[144,2048]{1,0:T(8,128)(2,1)S(1)} %get-tuple-element.57.refs_11_), channel_id=1, source_target_pairs={{0,1},{1,0},{2,3},{3,2},{4,5},{5,4},{6,7},{7,6},{8,9},{9,8},{10,11... | collective-permute-start | bytes 1769480 | tf_op jit(solution)/shard_map/ppermute | solution.py:436
  51.4 17.3 %collective-permute-start.11 = (bf16[144,4096]{1,0:T(8,128)(2,1)S(1)}, bf16[144,4096]{1,0:T(8,128)(2,1)S(1)}, u32[]{:S(2)}, u32[]{:S(2)}) collective-permute-start(bf16[144,4096]{1,0:T(8,128)(2,1)S(1)} %after.6.x_ref), channel_id=1, source_target_pairs={{0,4},{1,3},{4,8},{5,1},{8,12},{9,5},{12,14},{13,9},{14,10},{15,13... | collective-permute-start | bytes 3538952 | tf_op jit(solution)/shard_map/ppermute | solution.py:436
  53.1 3.6 %collective-permute-start.12 = (bf16[144,2048]{1,0:T(8,128)(2,1)S(1)}, bf16[144,2048]{1,0:T(8,128)(2,1)S(1)}, u32[]{:S(2)}, u32[]{:S(2)}) collective-permute-start(bf16[144,2048]{1,0:T(8,128)(2,1)S(1)} %get-tuple-element.62.refs_4_.refs_5_), channel_id=1, source_target_pairs={{0,1},{1,0},{2,3},{3,2},{4,5},{5,4},{6,7},{7,6},{8,9},{9,8},{10,11... | collective-permute-start | bytes 1769480 | tf_op jit(solution)/shard_map/ppermute | solution.py:436
  53.2 5.6 %collective-permute-start.15 = (bf16[144,2048]{1,0:T(8,128)(2,1)S(1)}, bf16[144,2048]{1,0:T(8,128)(2,1)S(1)}, u32[]{:S(2)}, u32[]{:S(2)}) collective-permute-start(bf16[144,2048]{1,0:T(8,128)(2,1)S(1)} %get-tuple-element.64.refs_8_.refs_11_), channel_id=1, source_target_pairs={{0,1},{1,0},{2,3},{3,2},{4,5},{5,4},{6,7},{7,6},{8,9},{9,8},{10,11... | collective-permute-start | bytes 1769480 | tf_op jit(solution)/shard_map/ppermute | solution.py:436
  56.2 2.7 %collective-permute-start.14 = (bf16[144,2048]{1,0:T(8,128)(2,1)S(1)}, bf16[144,2048]{1,0:T(8,128)(2,1)S(1)}, u32[]{:S(2)}, u32[]{:S(2)}) collective-permute-start(bf16[144,2048]{1,0:T(8,128)(2,1)S(1)} %get-tuple-element.63.refs_6_.refs_7_), channel_id=1, source_target_pairs={{0,1},{1,0},{2,3},{3,2},{4,5},{5,4},{6,7},{7,6},{8,9},{9,8},{10,11... | collective-permute-start | bytes 1769480 | tf_op jit(solution)/shard_map/ppermute | solution.py:436
  56.2 2.8 %collective-permute-start.16 = (bf16[144,2048]{1,0:T(8,128)(2,1)S(1)}, bf16[144,2048]{1,0:T(8,128)(2,1)S(1)}, u32[]{:S(2)}, u32[]{:S(2)}) collective-permute-start(bf16[144,2048]{1,0:T(8,128)(2,1)S(1)} %get-tuple-element.65.refs_10_.refs_13_), channel_id=1, source_target_pairs={{0,1},{1,0},{2,3},{3,2},{4,5},{5,4},{6,7},{7,6},{8,9},{9,8},{10,11... | collective-permute-start | bytes 1769480 | tf_op jit(solution)/shard_map/ppermute | solution.py:436
  56.7 26.7 %collective-permute-start.18 = (bf16[144,4096]{1,0:T(8,128)(2,1)S(1)}, bf16[144,4096]{1,0:T(8,128)(2,1)S(1)}, u32[]{:S(2)}, u32[]{:S(2)}) collective-permute-start(bf16[144,4096]{1,0:T(8,128)(2,1)S(1)} %after.7.x_ref), channel_id=1, source_target_pairs={{0,4},{1,3},{4,8},{5,1},{8,12},{9,5},{12,14},{13,9},{14,10},{15,13... | collective-permute-start | bytes 3538952 | tf_op jit(solution)/shard_map/ppermute | solution.py:436
  68.8 2.7 %collective-permute-start.19 = (bf16[144,2048]{1,0:T(8,128)(2,1)S(1)}, bf16[144,2048]{1,0:T(8,128)(2,1)S(1)}, u32[]{:S(2)}, u32[]{:S(2)}) collective-permute-start(bf16[144,2048]{1,0:T(8,128)(2,1)S(1)} %get-tuple-element.70.refs_9_), channel_id=1, source_target_pairs={{0,1},{1,0},{2,3},{3,2},{4,5},{5,4},{6,7},{7,6},{8,9},{9,8},{10,11... | collective-permute-start | bytes 1769480 | tf_op jit(solution)/shard_map/ppermute | solution.py:436
  68.9 2.8 %collective-permute-start.20 = (bf16[144,2048]{1,0:T(8,128)(2,1)S(1)}, bf16[144,2048]{1,0:T(8,128)(2,1)S(1)}, u32[]{:S(2)}, u32[]{:S(2)}) collective-permute-start(bf16[144,2048]{1,0:T(8,128)(2,1)S(1)} %get-tuple-element.71.refs_15_), channel_id=1, source_target_pairs={{0,1},{1,0},{2,3},{3,2},{4,5},{5,4},{6,7},{7,6},{8,9},{9,8},{10,11... | collective-permute-start | bytes 1769480 | tf_op jit(solution)/shard_map/ppermute | solution.py:436
  69.4 24.6 %collective-permute-start.17 = (bf16[144,4096]{1,0:T(8,128)(2,1)S(1)}, bf16[144,4096]{1,0:T(8,128)(2,1)S(1)}, u32[]{:S(2)}, u32[]{:S(2)}) collective-permute-start(bf16[144,4096]{1,0:T(8,128)(2,1)S(1)} %after.8.x_ref), channel_id=1, source_target_pairs={{0,4},{1,3},{4,8},{5,1},{8,12},{9,5},{12,14},{13,9},{14,10},{15,13... | collective-permute-start | bytes 3538952 | tf_op jit(solution)/shard_map/ppermute | solution.py:436
  83.6 2.1 %collective-permute-start.21 = (bf16[144,2048]{1,0:T(8,128)(2,1)S(1)}, bf16[144,2048]{1,0:T(8,128)(2,1)S(1)}, u32[]{:S(2)}, u32[]{:S(2)}) collective-permute-start(bf16[144,2048]{1,0:T(8,128)(2,1)S(1)} %get-tuple-element.75.refs_5_), channel_id=1, source_target_pairs={{0,1},{1,0},{2,3},{3,2},{4,5},{5,4},{6,7},{7,6},{8,9},{9,8},{10,11... | collective-permute-start | bytes 1769480 | tf_op jit(solution)/shard_map/ppermute | solution.py:436
  83.8 2.7 %collective-permute-start.22 = (bf16[144,2048]{1,0:T(8,128)(2,1)S(1)}, bf16[144,2048]{1,0:T(8,128)(2,1)S(1)}, u32[]{:S(2)}, u32[]{:S(2)}) collective-permute-start(bf16[144,2048]{1,0:T(8,128)(2,1)S(1)} %get-tuple-element.76.refs_7_), channel_id=1, source_target_pairs={{0,1},{1,0},{2,3},{3,2},{4,5},{5,4},{6,7},{7,6},{8,9},{9,8},{10,11... | collective-permute-start | bytes 1769480 | tf_op jit(solution)/shard_map/ppermute | solution.py:436
  94.1 3.6 %collective-permute-start.24 = (bf16[144,2048]{1,0:T(8,128)(2,1)S(1)}, bf16[144,2048]{1,0:T(8,128)(2,1)S(1)}, u32[]{:S(2)}, u32[]{:S(2)}) collective-permute-start(bf16[144,2048]{1,0:T(8,128)(2,1)S(1)} %get-tuple-element.81.refs_4_), channel_id=1, source_target_pairs={{0,1},{1,0},{2,3},{3,2},{4,5},{5,4},{6,7},{7,6},{8,9},{9,8},{10,11... | collective-permute-start | bytes 1769480 | tf_op jit(solution)/shard_map/ppermute | solution.py:436
  94.3 3.4 %collective-permute-start.23 = (bf16[144,2048]{1,0:T(8,128)(2,1)S(1)}, bf16[144,2048]{1,0:T(8,128)(2,1)S(1)}, u32[]{:S(2)}, u32[]{:S(2)}) collective-permute-start(bf16[144,2048]{1,0:T(8,128)(2,1)S(1)} %get-tuple-element.80.refs_6_.refs_4_.refs_5_), channel_id=1, source_target_pairs={{0,1},{1,0},{2,3},{3,2},{4,5},{5,4},{6,7},{7,6},{8,9},{9,8},{10,11... | collective-permute-start | bytes 1769480 | tf_op jit(solution)/shard_map/ppermute | solution.py:436
  97.7 6.8 %slice-start = ((s8[6291456]{0:T(1024)(128)(4,1)}), s8[4194304]{0:T(1024)(128)(4,1)S(1)}, s32[]{:S(2)}) async-start(s8[6291456]{0:T(1024)(128)(4,1)} %bitcast.1), calls=%async_computation | async-start | bytes 8388608
  97.7 6.8 %slice-start.1 = ((s8[6291456]{0:T(1024)(128)(4,1)}), s8[2097152]{0:T(1024)(128)(4,1)S(1)}, s32[]{:S(2)}) async-start(s8[6291456]{0:T(1024)(128)(4,1)} %bitcast.1), calls=%async_computation.1 | async-start | bytes 4194304
  100.7 6.7 %collective-permute-start.27 = (f32[8,128]{1,0:T(8,128)S(1)}, f32[8,128]{1,0:T(8,128)S(1)}, u32[]{:S(2)}, u32[]{:S(2)}) collective-permute-start(f32[8,128]{1,0:T(8,128)S(1)} %get-tuple-element.90), channel_id=1, source_target_pairs={{0,6},{1,7},{2,4},{3,5},{4,2},{5,3},{6,0},{7,1},{8,14},{9,15},{10,... | collective-permute-start | bytes 12296 | tf_op jit(solution)/shard_map/ppermute | solution.py:416
  103.8 3.6 %collective-permute-start.26 = (f32[8,128]{1,0:T(8,128)S(1)}, f32[8,128]{1,0:T(8,128)S(1)}, u32[]{:S(2)}, u32[]{:S(2)}) collective-permute-start(f32[8,128]{1,0:T(8,128)S(1)} %get-tuple-element.90), channel_id=1, source_target_pairs={{0,4},{1,5},{2,6},{3,7},{4,0},{5,1},{6,2},{7,3},{8,12},{9,13},{10,... | collective-permute-start | bytes 12296 | tf_op jit(solution)/shard_map/ppermute | solution.py:416
  104.3 3.6 %collective-permute-start.25 = (f32[8,128]{1,0:T(8,128)S(1)}, f32[8,128]{1,0:T(8,128)S(1)}, u32[]{:S(2)}, u32[]{:S(2)}) collective-permute-start(f32[8,128]{1,0:T(8,128)S(1)} %get-tuple-element.90), channel_id=1, source_target_pairs={{0,2},{1,3},{2,0},{3,1},{4,6},{5,7},{6,4},{7,5},{8,10},{9,11},{10,... | collective-permute-start | bytes 12296 | tf_op jit(solution)/shard_map/ppermute | solution.py:416
  107.9 5.5 %collective-permute-start.30 = (f32[8,128]{1,0:T(8,128)S(1)}, f32[8,128]{1,0:T(8,128)S(1)}, u32[]{:S(2)}, u32[]{:S(2)}) collective-permute-start(f32[8,128]{1,0:T(8,128)S(1)} %after.11), channel_id=1, source_target_pairs={{0,9},{1,8},{2,11},{3,10},{4,13},{5,12},{6,15},{7,14},{8,1},{9,0},... | collective-permute-start | bytes 12296 | tf_op jit(solution)/shard_map/ppermute | solution.py:416
  109.3 4.5 %collective-permute-start.29 = (f32[8,128]{1,0:T(8,128)S(1)}, f32[8,128]{1,0:T(8,128)S(1)}, u32[]{:S(2)}, u32[]{:S(2)}) collective-permute-start(f32[8,128]{1,0:T(8,128)S(1)} %after.11), channel_id=1, source_target_pairs={{0,8},{1,9},{2,10},{3,11},{4,12},{5,13},{6,14},{7,15},{8,0},{9,1},... | collective-permute-start | bytes 12296 | tf_op jit(solution)/shard_map/ppermute | solution.py:416
  110.6 3.3 %collective-permute-start.28 = (f32[8,128]{1,0:T(8,128)S(1)}, f32[8,128]{1,0:T(8,128)S(1)}, u32[]{:S(2)}, u32[]{:S(2)}) collective-permute-start(f32[8,128]{1,0:T(8,128)S(1)} %after.11), channel_id=1, source_target_pairs={{0,1},{1,0},{2,3},{3,2},{4,5},{5,4},{6,7},{7,6},{8,9},{9,8},{10,11... | collective-permute-start | bytes 12296 | tf_op jit(solution)/shard_map/ppermute | solution.py:416

commit v12 on v11

--- a/solution.py
+++ b/solution.py
@@ -158,7 +158,8 @@
 
 
 def phase_kernel(spec, *refs):
-    groups, arrays, do_w, w_from, attn, fresh_w, fresh_out, squares, rows, begin = spec
+    groups, arrays, do_w, w_from, attn, has_before, fresh_w, fresh_out, squares = spec[:9]
+    rows, begin = spec[9:]
     refs = list(refs)
     table_ref, me_ref, heads_ref = refs.pop(0), refs.pop(0), refs.pop(0)
     at_ref = refs.pop(0) if do_w else None
@@ -166,18 +167,19 @@
     g_refs = [refs.pop(0) for _ in range(arrays)]
     if do_w and not fresh_w:
         refs.pop(0)
-    before_ref = refs.pop(0) if attn == "last" else None
+    before_ref = refs.pop(0) if has_before else None
     added_ref = refs.pop(0) if squares == "added" else None
     if attn in ("whole", "last") and not fresh_out:
         refs.pop(0)
     w_ref = refs.pop(0) if do_w else None
-    total_ref = refs.pop(0) if attn == "first" else None
+    total_ref = refs.pop(0) if attn == "part" else None
     out_ref = refs.pop(0) if attn in ("whole", "last") else None
     squares_ref = refs.pop(0)
     if attn in ("whole", "last"):
         total_ref, block_ref, sems = refs
-    if attn == "last":
-        total_ref[...] = before_ref[...]
+    if has_before:
+        if attn == "last":
+            total_ref[...] = before_ref[...]
     elif attn:
         total_ref[...] = jnp.zeros_like(total_ref)
     if squares == "added":
@@ -277,11 +279,13 @@
             add_vmem(w)
         outs.append(pltpu.VMEM((capacity, features), jnp.float32))
         out_specs.append(vmem)
-    if attn == "last":
+    if before is not None:
+        if attn == "part":
+            aliases[len(args)] = len(outs)
         add_vmem(before)
     if squares == "added":
         add_vmem(added)
-    if attn == "first":
+    if attn == "part":
         outs.append(pltpu.VMEM((height, capacity), jnp.float32))
         out_specs.append(vmem)
     elif attn:
@@ -298,8 +302,8 @@
     outs.append(pltpu.VMEM((8, 128), jnp.float32))
     out_specs.append(vmem)
     spec = (
-        tuple(described), len(arrays), do_w, w_from, attn, w is None, out is None,
-        squares, rows, begin,
+        tuple(described), len(arrays), do_w, w_from, attn, before is not None, w is None,
+        out is None, squares, rows, begin,
     )
     return pl.pallas_call(
         functools.partial(phase_kernel, spec),
@@ -318,10 +322,12 @@
     )(*args)
 
 
-def scale_kernel(parts, w_ref, squares_ref, out_ref, block_ref, sems):
+def scale_kernel(parts, w_ref, squares_ref, other_ref, out_ref, block_ref, sems):
     capacity, features = w_ref.shape
     square_sum = jnp.sum(
-        jnp.sum(squares_ref[...], axis=0, keepdims=True), axis=1, keepdims=True
+        jnp.sum(squares_ref[...] + other_ref[...], axis=0, keepdims=True),
+        axis=1,
+        keepdims=True,
     )
     factor = jnp.minimum(
         1.0, 1.0 / jnp.sqrt(square_sum / (HEADS * HEAD_DIM * features) + 1e-06)
@@ -337,13 +343,13 @@
         copy.wait()
 
 
-def scaled(w, squares):
+def scaled(w, squares, other):
     capacity, features = w.shape
     vmem = pl.BlockSpec(memory_space=pltpu.VMEM)
     parts = 8
     return pl.pallas_call(
         functools.partial(scale_kernel, parts),
-        in_specs=[vmem, vmem],
+        in_specs=[vmem] * 3,
         out_specs=pl.BlockSpec(memory_space=pl.ANY),
         out_shape=jax.ShapeDtypeStruct((capacity, features), jnp.bfloat16),
         scratch_shapes=[
@@ -357,7 +363,7 @@
             transcendentals=0,
         ),
         name="scale",
-    )(pltpu.with_memory_space_constraint(w, pltpu.VMEM), squares)
+    )(*[pltpu.with_memory_space_constraint(x, pltpu.VMEM) for x in (w, squares, other)])
 
 
 def after(done, *arrays):
@@ -403,18 +409,23 @@
     bits = [1 << i for i in range(devices.bit_length() - 1)]
     if len(bits) >= 4:
         bits = bits[1:3] + [bits[0]] + bits[3:]
-    masks = []
-    while bits:
-        pair, bits = bits[:2], bits[2:]
-        masks.append(pair + [sum(pair)] if len(pair) == 2 else pair)
-    return masks
-
-
-def exchange(x, devices, masks):
-    total = x
-    for mask in masks:
-        total = total + lax.ppermute(x, "dp", [(d, d ^ mask) for d in range(devices)])
-    return total
+    return bits
+
+
+def sum_kernel(x_ref, y_ref, done_ref, out_ref):
+    out_ref[...] = x_ref[...] + y_ref[...]
+
+
+def summed(done, x, y):
+    vmem = pl.BlockSpec(memory_space=pltpu.VMEM)
+    return pl.pallas_call(
+        sum_kernel,
+        in_specs=[vmem] * 3,
+        out_specs=vmem,
+        out_shape=pltpu.VMEM(x.shape, x.dtype),
+        compiler_params=pltpu.CompilerParams(vmem_limit_bytes=MIB),
+        name="summed",
+    )(*[pltpu.with_memory_space_constraint(x, pltpu.VMEM) for x in (x, y, done)])
 
 
 def on_device(ring, attn_out, out_grad, o_weight, head_counts, seq_counts):
@@ -461,10 +472,9 @@
         far_x = swapped(near_x)
         i = 2 * k - 1
         if k == last - 1:
-            held = held + [near_x, far_x]
             w, out, done = phase(
-                where, shapes, 2 * (i + 1) - len(held), grouped(*held), at=ats[i], w=w,
-                w_from=len(held) - 2, weight=weight, attn="whole", out=out,
+                where, shapes, 2 * i, grouped(near_x, far_x), at=ats[i], w=w,
+                weight=weight, attn="whole", out=out,
             )
         y = arrived(done, counts[1], y) if k == 1 else after(done, y)[0]
         y, near_y = send(y, ring.along()) if k < last - 1 else None, split(y)
@@ -475,9 +485,6 @@
                 where, shapes, 2 * (i + 1), grouped(near_y, far_y), at=ats[i + 1], w=w,
                 weight=weight, attn="whole", out=out,
             )
-        elif k == last - 2:
-            held = [near_x, far_x, near_y, far_y]
-            w, done = phase(where, shapes, 2 * i, groups, at=ats[i], w=w)
         else:
             w, out, done = phase(
                 where, shapes, 2 * i, groups, at=ats[i], w=w,
@@ -491,24 +498,29 @@
     w, done = phase(where, shapes, begin, grouped(near), at=ats[-2], w=w)
     w, squares = phase(where, shapes, begin, grouped(far), at=ats[-1], w=w, squares="new")
 
-    pieces = [group[3] for group in grouped(near, far)]
-    parts = [
-        [(0, half, 0, pieces[0]), (half, half // 2, 0, pieces[1])],
-        [(half + half // 2, half // 2, half // 2, pieces[1])],
-    ]
-    for late, masks in enumerate(rounds(devices)):
-        squares = exchange(squares, devices, masks)
-        if late == 0:
-            before, done = phase(
-                where, shapes, begin, parts[0], weight=weight, attn="first"
-            )
-            (squares,) = after(done, squares)
-        elif late == 1:
-            out, done = phase(
-                where, shapes, begin, parts[1], weight=weight, attn="last",
-                before=before, out=out,
-            )
-    return out, scaled(w, squares)
+    bits = rounds(devices)
+    parts = 4 if len(bits) >= 4 else 1
+    width = features // parts
+    before = None
+    for late, bit in enumerate(bits):
+        other = send(squares, [(d, d ^ bit) for d in range(devices)])
+        done = squares
+        if late < parts:
+            first = late * width
+            pieces = grouped(near, far)[first // half][3]
+            groups = [(first, width, first % half, pieces)]
+            if late < parts - 1:
+                before, done = phase(
+                    where, shapes, begin, groups, weight=weight, attn="part", before=before
+                )
+            else:
+                out, done = phase(
+                    where, shapes, begin, groups, weight=weight, attn="last",
+                    before=before, out=out,
+                )
+        if late < len(bits) - 1:
+            squares = summed(done, squares, other)
+    return out, scaled(w, squares, other)
 
 
 def solution(mesh):

time: 117 us -> 119 us (1.017)
  Pallas kernels: 64.4 us -> 66.4 us
  waiting for transfers between devices: 17.9 us -> 16.6 us
    ppermute x25 -> x29, starting transfers between devices: 22.3 us -> 29.5 us  [send(): return lax.ppermute(x, 'dp', pairs)]
    ppermute x6 -> x0, starting transfers between devices: 6.5 us -> none  [exchange(): lax.ppermute(x, 'dp', [(d, d ^ mask) for d in range(devices)])]
    pallas_call x9 -> x11, Pallas kernels: 55.4 us -> 57.4 us  [phase(): pl.pallas_call(functools.partial(phase_kernel, spec), in_specs=specs, out...]
    ppermute x25 -> x29, waiting for transfers between devices: 17 us -> 16.6 us  [send(): return lax.ppermute(x, 'dp', pairs)]
    pallas_call x1 -> x4, Pallas kernels: 3 us -> 3.02 us  [the longest x1 3 us: scaled(): pl.pallas_call(functools.partial(scale_kernel, parts), in_specs=[vmem] *...]
  transfers between devices with their start and end apart: 31 -> 29, of which waited for: 14 -> 15; matrix products, arithmetic and copies ran while one was open for 0% -> 0% of each run, Pallas kernels for 50% -> 51%
where the time goes in v12:
time: 119 us; the launch traced here: 118 us
  Pallas kernels  66.4 us (56%)
  starting transfers between devices  29.5 us (25%)
  waiting for transfers between devices  16.6 us (14%)
  local copies, waits for them, and re-layouts  3.49 us (3%)
  between operations  2.41 us (2%)
    pallas_call x11, Pallas kernels, phase(): pl.pallas_call(functools.partial(phase_kernel, spec), in_specs=specs, out...  57.4 us
    ppermute x29, starting transfers between devices, send(): return lax.ppermute(x, 'dp', pairs)  29.5 us
    ppermute x29, waiting for transfers between devices, send(): return lax.ppermute(x, 'dp', pairs)  16.6 us
    pallas_call x1, Pallas kernels, prepared(): pl.pallas_call(functools.partial(prep_kernel, spans, rows), in_specs=[sme...  3.96 us
    unnamed x8, local copies, waits for them, and re-layouts  3.49 us
    pallas_call x1, Pallas kernels, scaled(): pl.pallas_call(functools.partial(scale_kernel, parts), in_specs=[vmem] *...  3 us
  transfers between devices with their start and end apart: 29, of which 15 were waited for; matrix products, arithmetic and copies ran while one was open for 0% of the time, Pallas kernels for 51%

profile of v12, /device:TPU:0, one launch (start us, length us, event | category | flops | bytes accessed | tf_op | source)
XLA Modules:
  0.0 118.4 jit_solution(12403581255584778212)
XLA Ops:
  0.6 3.1 %collective-permute-start.1 = (bf16[144,4096]{1,0:T(8,128)(2,1)}, bf16[144,4096]{1,0:T(8,128)(2,1)S(1)}, u32[]{:S(2)}, u32[]{:S(2)}) collective-permute-start(bf16[144,4096]{1,0:T(8,128)(2,1)} %grad_ref.1), channel_id=1, source_target_pairs={{0,4},{1,3},{4,8},{5,1},{8,12},{9,5},{12,14},{13,9},{14,10},{15,13... | collective-permute-start | bytes 3538952 | tf_op jit(solution)/shard_map/ppermute | solution.py:447
  5.0 0.7 copy-done.1
  5.7 4.0 %prep.1 = (bf16[144,4096]{1,0:T(8,128)(2,1)S(1)}, bf16[144,2048]{1,0:T(8,128)(2,1)S(1)}, bf16[144,2048]{1,0:T(8,128)(2,1)S(1)}, s32[8,128]{1,0:T(8,128)S(1)}, bf...) custom-call(s32[16,16]{1,0:T(8,128)S(1)} %copy-done.1, ...), custom_call_target="tpu_custom_call" | custom-call | flops 1 | bytes 1 | tf_op jit(solution)/shard_map/prep/pallas_call | solution.py:121
  9.7 0.1 collective-permute-start.2
  9.8 0.5 collective-permute-start.3
  10.2 0.7 collective-permute-start.7
  10.9 1.0 collective-permute-start
  12.0 0.6 collective-permute-done.3.refs_8_
  12.6 2.8 %copy-done = bf16[768,4096]{1,0:T(8,128)(2,1)S(1)} copy-done((bf16[768,4096]{1,0:T(8,128)(2,1)S(1)}, bf16[768,4096]{1,0:T(8,128)(2,1)}, u32[]{:S(2)}) %copy-start) | copy-done | bytes 6291480
  15.4 7.2 %phase_w_whole.5 = (f32[768,4096]{1,0:T(8,128)S(1)}, bf16[2304,768]{1,0:T(8,128)(2,1)}, f32[8,128]{1,0:T(8,128)S(1)}) custom-call(s32[16,16]{1,0:T(8,128)S(1)} %copy-done.1, s32[1]{0:T(128)} %bitcast.me_ref.refs_1_, s32[1]{0:T(128)S(6)} %copy.48.heads_ref.refs_2_, bf16[768,288]{1,0:T(8,128)(2,1)S(1)} %get-tuple-element.53.refs_3_, ...), custom_call_target="tpu_custom_call" | custom-call | flops 1 | bytes 1 | tf_op jit(solution)/shard_map/phase_w_whole/pallas_call | solution.py:308
  22.6 0.4 collective-permute-done.count_ref
  23.0 0.7 arrived.2.x_ref
  23.6 0.1 split.7
  23.8 0.1 collective-permute-start.5
  23.8 2.5 %collective-permute-start.4 = (bf16[144,4096]{1,0:T(8,128)(2,1)S(1)}, bf16[144,4096]{1,0:T(8,128)(2,1)S(1)}, u32[]{:S(2)}, u32[]{:S(2)}) collective-permute-start(bf16[144,4096]{1,0:T(8,128)(2,1)S(1)} %arrived.2.x_ref), channel_id=1, source_target_pairs={{0,4},{1,3},{4,8},{5,1},{8,12},{9,5},{12,14},{13,9},{14,10},{15,13... | collective-permute-start | bytes 3538952 | tf_op jit(solution)/shard_map/ppermute | solution.py:447
  26.4 2.2 %collective-permute-start.6 = (s32[8,128]{1,0:T(8,128)S(1)}, s32[8,128]{1,0:T(8,128)S(1)}, u32[]{:S(2)}, u32[]{:S(2)}) collective-permute-start(s32[8,128]{1,0:T(8,128)S(1)} %get-tuple-element.52), channel_id=1, source_target_pairs={{0,3},{1,4},{4,1},{5,8},{8,5},{9,12},{12,9},{13,14},{14,13},{15,10... | collective-permute-start | bytes 12296 | tf_op jit(solution)/shard_map/ppermute | solution.py:447
  28.5 4.2 %collective-permute-done.6.count_ref = s32[8,128]{1,0:T(8,128)S(1)} collective-permute-done((s32[8,128]{1,0:T(8,128)S(1)}, s32[8,128]{1,0:T(8,128)S(1)}, u32[]{:S(2)}, u32[]{:S(2)}) %collective-permute-start.6) | collective-permute-done | bytes 4128 | tf_op jit(solution)/shard_map/ppermute | solution.py:447
  32.8 0.7 arrived.3.x_ref
  33.4 0.1 split.8
  33.5 3.0 %collective-permute-start.13 = (bf16[144,4096]{1,0:T(8,128)(2,1)S(1)}, bf16[144,4096]{1,0:T(8,128)(2,1)S(1)}, u32[]{:S(2)}, u32[]{:S(2)}) collective-permute-start(bf16[144,4096]{1,0:T(8,128)(2,1)S(1)} %arrived.3.x_ref), channel_id=1, source_target_pairs={{0,4},{1,3},{4,8},{5,1},{8,12},{9,5},{12,14},{13,9},{14,10},{15,13... | collective-permute-start | bytes 3538952 | tf_op jit(solution)/shard_map/ppermute | solution.py:447
  36.5 0.5 collective-permute-start.8
  37.0 1.5 %collective-permute-done.9.refs_10_ = bf16[144,2048]{1,0:T(8,128)(2,1)S(1)} collective-permute-done((bf16[144,2048]{1,0:T(8,128)(2,1)S(1)}, bf16[144,2048]{1,0:T(8,128)(2,1)S(1)}, u32[]{:S(2)}, u32[]{:S(2)}) %collective-permute-start.9) | collective-permute-done | bytes 589856 | tf_op jit(solution)/shard_map/ppermute | solution.py:447
  38.5 0.8 collective-permute-done.8.refs_8_
  39.4 0.8 collective-permute-done.10.refs_12_
  40.2 11.3 %phase_w_whole.6 = (f32[768,4096]{1,0:T(8,128)S(1)}, bf16[2304,768]{1,0:T(8,128)(2,1)}, f32[8,128]{1,0:T(8,128)S(1)}) custom-call(s32[16,16]{1,0:T(8,128)S(1)} %copy-done.1, s32[1]{0:T(128)} %bitcast.me_ref.refs_1_, s32[1]{0:T(128)S(6)} %copy.48.heads_ref.refs_2_, ...), custom_call_target="tpu_custom_call", output_to_operand_aliasing={{0}: (13, {}), {1}: (14, {})} | custom-call | flops 1 | bytes 1 | tf_op jit(solution)/shard_map/phase_w_whole/pallas_call | solution.py:308
  51.5 1.6 %collective-permute-start.11 = (bf16[144,4096]{1,0:T(8,128)(2,1)S(1)}, bf16[144,4096]{1,0:T(8,128)(2,1)S(1)}, u32[]{:S(2)}, u32[]{:S(2)}) collective-permute-start(bf16[144,4096]{1,0:T(8,128)(2,1)S(1)} %after.5.x_ref), channel_id=1, source_target_pairs={{0,4},{1,3},{4,8},{5,1},{8,12},{9,5},{12,14},{13,9},{14,10},{15,13... | collective-permute-start | bytes 3538952 | tf_op jit(solution)/shard_map/ppermute | solution.py:447
  53.1 0.1 split.9
  53.3 0.1 collective-permute-start.12
  53.3 0.5 collective-permute-start.15
  53.8 2.2 %collective-permute-done.13.refs_0_ = bf16[144,4096]{1,0:T(8,128)(2,1)S(1)} collective-permute-done((bf16[144,4096]{1,0:T(8,128)(2,1)S(1)}, bf16[144,4096]{1,0:T(8,128)(2,1)S(1)}, u32[]{:S(2)}, u32[]{:S(2)}) %collective-permute-start.13) | collective-permute-done | bytes 1179680 | tf_op jit(solution)/shard_map/ppermute | solution.py:447
  56.1 0.1 split.10
  56.2 0.5 collective-permute-start.16
  56.7 2.1 %collective-permute-start.18 = (bf16[144,4096]{1,0:T(8,128)(2,1)S(1)}, bf16[144,4096]{1,0:T(8,128)(2,1)S(1)}, u32[]{:S(2)}, u32[]{:S(2)}) collective-permute-start(bf16[144,4096]{1,0:T(8,128)(2,1)S(1)} %after.6.x_ref), channel_id=1, source_target_pairs={{0,4},{1,3},{4,8},{5,1},{8,12},{9,5},{12,14},{13,9},{14,10},{15,13... | collective-permute-start | bytes 3538952 | tf_op jit(solution)/shard_map/ppermute | solution.py:447
  58.8 0.2 collective-permute-done.16.refs_12_
  59.1 11.3 %phase_w_whole.7 = (f32[768,4096]{1,0:T(8,128)S(1)}, bf16[2304,768]{1,0:T(8,128)(2,1)}, f32[8,128]{1,0:T(8,128)S(1)}) custom-call(s32[16,16]{1,0:T(8,128)S(1)} %copy-done.1, s32[1]{0:T(128)} %bitcast.me_ref.refs_1_, s32[1]{0:T(128)S(6)} %copy.48.heads_ref.refs_2_, ...), custom_call_target="tpu_custom_call", output_to_operand_aliasing={{0}: (13, {}), {1}: (14, {})} | custom-call | flops 1 | bytes 1 | tf_op jit(solution)/shard_map/phase_w_whole/pallas_call | solution.py:308
  70.4 0.1 split.11
  70.5 0.2 collective-permute-start.19
  70.7 0.4 collective-permute-start.20
  71.0 2.1 %collective-permute-start.17 = (bf16[144,4096]{1,0:T(8,128)(2,1)S(1)}, bf16[144,4096]{1,0:T(8,128)(2,1)S(1)}, u32[]{:S(2)}, u32[]{:S(2)}) collective-permute-start(bf16[144,4096]{1,0:T(8,128)(2,1)S(1)} %after.7.x_ref), channel_id=1, source_target_pairs={{0,4},{1,3},{4,8},{5,1},{8,12},{9,5},{12,14},{13,9},{14,10},{15,13... | collective-permute-start | bytes 3538952 | tf_op jit(solution)/shard_map/ppermute | solution.py:447
  73.1 0.3 collective-permute-done.20.refs_8_
  73.4 7.5 %phase_w_whole.8 = (f32[768,4096]{1,0:T(8,128)S(1)}, bf16[2304,768]{1,0:T(8,128)(2,1)}, f32[8,128]{1,0:T(8,128)S(1)}) custom-call(s32[16,16]{1,0:T(8,128)S(1)} %copy-done.1, s32[1]{0:T(128)} %bitcast.me_ref.refs_1_, s32[1]{0:T(128)S(6)} %copy.48.heads_ref.refs_2_, ...), custom_call_target="tpu_custom_call", output_to_operand_aliasing={{0}: (9, {}), {1}: (10, {})} | custom-call | flops 1 | bytes 1 | tf_op jit(solution)/shard_map/phase_w_whole/pallas_call | solution.py:308
  80.9 0.5 collective-permute-done.18.refs_0_
  81.3 0.1 split.12
  81.4 0.1 collective-permute-start.21
  81.5 0.5 collective-permute-start.22
  82.0 1.5 %collective-permute-done.21.refs_6_ = bf16[144,2048]{1,0:T(8,128)(2,1)S(1)} collective-permute-done((bf16[144,2048]{1,0:T(8,128)(2,1)S(1)}, bf16[144,2048]{1,0:T(8,128)(2,1)S(1)}, u32[]{:S(2)}, u32[]{:S(2)}) %collective-permute-start.21) | collective-permute-done | bytes 589856 | tf_op jit(solution)/shard_map/ppermute | solution.py:447
  83.5 0.8 collective-permute-done.22.refs_8_
  84.4 7.5 %phase_w_whole.9 = (f32[768,4096]{1,0:T(8,128)S(1)}, bf16[2304,768]{1,0:T(8,128)(2,1)}, f32[8,128]{1,0:T(8,128)S(1)}) custom-call(s32[16,16]{1,0:T(8,128)S(1)} %copy-done.1, s32[1]{0:T(128)} %bitcast.me_ref.refs_1_, s32[1]{0:T(128)S(6)} %copy.48.heads_ref.refs_2_, ...), custom_call_target="tpu_custom_call", output_to_operand_aliasing={{0}: (9, {}), {1}: (10, {})} | custom-call | flops 1 | bytes 1 | tf_op jit(solution)/shard_map/phase_w_whole/pallas_call | solution.py:308
  91.8 2.1 %collective-permute-done.17.refs_0_ = bf16[144,4096]{1,0:T(8,128)(2,1)S(1)} collective-permute-done((bf16[144,4096]{1,0:T(8,128)(2,1)S(1)}, bf16[144,4096]{1,0:T(8,128)(2,1)S(1)}, u32[]{:S(2)}, u32[]{:S(2)}) %collective-permute-start.17) | collective-permute-done | bytes 1179680 | tf_op jit(solution)/shard_map/ppermute | solution.py:447
  94.0 0.1 split.13
  94.1 0.1 collective-permute-start.23
  94.2 0.5 collective-permute-start.24
  94.7 3.0 %phase_w_None.2 = (f32[768,4096]{1,0:T(8,128)S(1)}, f32[8,128]{1,0:T(8,128)}) custom-call(s32[16,16]{1,0:T(8,128)S(1)} %copy-done.1, s32[1]{0:T(128)} %bitcast.me_ref.refs_1_, s32[1]{0:T(128)S(6)} %copy.48.heads_ref.refs_2_, bf16[768,144]{1,0:T(8,128)(2,1)S(1)} %get-tuple-element.94.refs_3_, ...), custom_call_target="tpu_custom_call", output_to_operand_aliasing={{0}: (6, {})} | custom-call | flops 1 | bytes 1 | tf_op jit(solution)/shard_map/phase_w_None/pallas_call | solution.py:308
  97.7 3.0 %phase_w_None.3 = (f32[768,4096]{1,0:T(8,128)S(1)}, f32[8,128]{1,0:T(8,128)S(1)}) custom-call(s32[16,16]{1,0:T(8,128)S(1)} %copy-done.1, s32[1]{0:T(128)} %bitcast.me_ref.refs_1_, s32[1]{0:T(128)S(6)} %copy.48.heads_ref.refs_2_, bf16[768,144]{1,0:T(8,128)(2,1)S(1)} %get-tuple-element.93.refs_3_, ...), custom_call_target="tpu_custom_call", output_to_operand_aliasing={{0}: (6, {})} | custom-call | flops 1 | bytes 1 | tf_op jit(solution)/shard_map/phase_w_None/pallas_call | solution.py:308
  100.7 2.1 %collective-permute-start.25 = (f32[8,128]{1,0:T(8,128)S(1)}, f32[8,128]{1,0:T(8,128)S(1)}, u32[]{:S(2)}, u32[]{:S(2)}) collective-permute-start(f32[8,128]{1,0:T(8,128)S(1)} %get-tuple-element.98.x_ref), channel_id=1, source_target_pairs={{0,2},{1,3},{2,0},{3,1},{4,6},{5,7},{6,4},{7,5},{8,10},{9,11},{10,... | collective-permute-start | bytes 12296 | tf_op jit(solution)/shard_map/ppermute | solution.py:447
  102.8 1.3 %phase__part.3 = (f32[288,768]{1,0:T(8,128)S(1)}, f32[8,128]{1,0:T(8,128)S(1)}) custom-call(s32[16,16]{1,0:T(8,128)S(1)} %copy-done.1, s32[1]{0:T(128)} %bitcast.me_ref.refs_1_, s32[1]{0:T(128)S(6)} %copy.48.heads_ref.refs_2_, bf16[768,4096]{1,0:T(8,128)(2,1)S(1)} %bitcast.2, bf16[144,2048]{1,0:T(8,128)(2,1)S(1)} %get-tuple-element.87.refs_4_, ...), custom_call_target="tpu_custom_call" | custom-call | flops 1 | bytes 1 | tf_op jit(solution)/shard_map/phase__part/pallas_call | solution.py:308
  104.1 0.2 collective-permute-done.25.y_ref
  104.4 2.1 %collective-permute-start.26 = (f32[8,128]{1,0:T(8,128)S(1)}, f32[8,128]{1,0:T(8,128)S(1)}, u32[]{:S(2)}, u32[]{:S(2)}) collective-permute-start(f32[8,128]{1,0:T(8,128)S(1)} %summed.3.x_ref), channel_id=1, source_target_pairs={{0,4},{1,5},{2,6},{3,7},{4,0},{5,1},{6,2},{7,3},{8,12},{9,13},{10,... | collective-permute-start | bytes 12296 | tf_op jit(solution)/shard_map/ppermute | solution.py:447
  106.5 1.3 %phase__part.4 = (f32[288,768]{1,0:T(8,128)S(1)}, f32[8,128]{1,0:T(8,128)S(1)}) custom-call(s32[16,16]{1,0:T(8,128)S(1)} %copy-done.1, s32[1]{0:T(128)} %bitcast.me_ref.refs_1_, s32[1]{0:T(128)S(6)} %copy.48.heads_ref.refs_2_, bf16[768,4096]{1,0:T(8,128)(2,1)S(1)} %bitcast.2, ...), custom_call_target="tpu_custom_call", output_to_operand_aliasing={{0}: (6, {})} | custom-call | flops 1 | bytes 1 | tf_op jit(solution)/shard_map/phase__part/pallas_call | solution.py:308
  107.8 0.2 collective-permute-done.26.y_ref
  108.0 1.3 %phase__part.5 = (f32[288,768]{1,0:T(8,128)S(1)}, f32[8,128]{1,0:T(8,128)S(1)}) custom-call(s32[16,16]{1,0:T(8,128)S(1)} %copy-done.1, s32[1]{0:T(128)} %bitcast.me_ref.refs_1_, s32[1]{0:T(128)S(6)} %copy.48.heads_ref.refs_2_, bf16[768,4096]{1,0:T(8,128)(2,1)S(1)} %bitcast.2, ...), custom_call_target="tpu_custom_call", output_to_operand_aliasing={{0}: (6, {})} | custom-call | flops 1 | bytes 1 | tf_op jit(solution)/shard_map/phase__part/pallas_call | solution.py:308
  109.4 3.1 %collective-permute-start.28 = (f32[8,128]{1,0:T(8,128)S(1)}, f32[8,128]{1,0:T(8,128)S(1)}, u32[]{:S(2)}, u32[]{:S(2)}) collective-permute-start(f32[8,128]{1,0:T(8,128)S(1)} %summed.5.squares_ref), channel_id=1, source_target_pairs={{0,8},{1,9},{2,10},{3,11},{4,12},{5,13},{6,14},{7,15},{8,0},{9,1},... | collective-permute-start | bytes 12296 | tf_op jit(solution)/shard_map/ppermute | solution.py:447
  112.5 2.7 %phase__last.1 = (bf16[2304,768]{1,0:T(8,128)(2,1)}, f32[8,128]{1,0:T(8,128)}) custom-call(s32[16,16]{1,0:T(8,128)S(1)} %copy-done.1, s32[1]{0:T(128)} %bitcast.me_ref.refs_1_, s32[1]{0:T(128)S(6)} %copy.48.heads_ref.refs_2_, bf16[768,4096]{1,0:T(8,128)(2,1)S(1)} %bitcast.2, ...), custom_call_target="tpu_custom_call", output_to_operand_aliasing={{0}: (7, {})} | custom-call | flops 1 | bytes 1 | tf_op jit(solution)/shard_map/phase__last/pallas_call | solution.py:308
  115.2 3.0 %scale.1 = bf16[768,4096]{1,0:T(8,128)(2,1)} custom-call(f32[768,4096]{1,0:T(8,128)S(1)} %get-tuple-element.97.w_ref, f32[8,128]{1,0:T(8,128)S(1)} %summed.5.squares_ref, f32[8,128]{1,0:T(8,128)S(1)} %collective-permute-done.28.other_ref), custom_call_target="tpu_custom_call" | custom-call | flops 3145728 | bytes 6291456 | tf_op jit(solution)/shard_map/scale/pallas_call | solution.py:350
  (33 shorter events, 0.2 us)
Async XLA Ops:
  0.6 22.4 %collective-permute-start.1 = (bf16[144,4096]{1,0:T(8,128)(2,1)}, bf16[144,4096]{1,0:T(8,128)(2,1)S(1)}, u32[]{:S(2)}, u32[]{:S(2)}) collective-permute-start(bf16[144,4096]{1,0:T(8,128)(2,1)} %grad_ref.1), channel_id=1, source_target_pairs={{0,4},{1,3},{4,8},{5,1},{8,12},{9,5},{12,14},{13,9},{14,10},{15,13... | collective-permute-start | bytes 3538952 | tf_op jit(solution)/shard_map/ppermute | solution.py:447
  5.0 0.7 copy-start.1
  9.7 2.3 %collective-permute-start.2 = (bf16[144,2048]{1,0:T(8,128)(2,1)S(1)}, bf16[144,2048]{1,0:T(8,128)(2,1)S(1)}, u32[]{:S(2)}, u32[]{:S(2)}) collective-permute-start(bf16[144,2048]{1,0:T(8,128)(2,1)S(1)} %get-tuple-element.54.refs_5_), channel_id=1, source_target_pairs={{0,1},{1,0},{2,3},{3,2},{4,5},{5,4},{6,7},{7,6},{8,9},{9,8},{10,11... | collective-permute-start | bytes 1769480 | tf_op jit(solution)/shard_map/ppermute | solution.py:447
  9.8 2.8 %collective-permute-start.3 = (bf16[144,2048]{1,0:T(8,128)(2,1)S(1)}, bf16[144,2048]{1,0:T(8,128)(2,1)S(1)}, u32[]{:S(2)}, u32[]{:S(2)}) collective-permute-start(bf16[144,2048]{1,0:T(8,128)(2,1)S(1)} %get-tuple-element.55.refs_7_), channel_id=1, source_target_pairs={{0,1},{1,0},{2,3},{3,2},{4,5},{5,4},{6,7},{7,6},{8,9},{9,8},{10,11... | collective-permute-start | bytes 1769480 | tf_op jit(solution)/shard_map/ppermute | solution.py:447
  10.2 22.5 %collective-permute-start.7 = (bf16[144,4096]{1,0:T(8,128)(2,1)S(1)}, bf16[144,4096]{1,0:T(8,128)(2,1)S(1)}, u32[]{:S(2)}, u32[]{:S(2)}) collective-permute-start(bf16[144,4096]{1,0:T(8,128)(2,1)S(1)} %get-tuple-element.59), channel_id=1, source_target_pairs={{0,3},{1,4},{4,1},{5,8},{8,5},{9,12},{12,9},{13,14},{14,13},{15,10... | collective-permute-start | bytes 3538952 | tf_op jit(solution)/shard_map/ppermute | solution.py:447
  10.9 12.1 %collective-permute-start = (s32[8,128]{1,0:T(8,128)S(1)}, s32[8,128]{1,0:T(8,128)S(1)}, u32[]{:S(2)}, u32[]{:S(2)}) collective-permute-start(s32[8,128]{1,0:T(8,128)S(1)} %get-tuple-element.52), channel_id=1, source_target_pairs={{0,4},{1,3},{4,8},{5,1},{8,12},{9,5},{12,14},{13,9},{14,10},{15,13... | collective-permute-start | bytes 12296 | tf_op jit(solution)/shard_map/ppermute | solution.py:447
  12.6 2.8 %copy-start = (bf16[768,4096]{1,0:T(8,128)(2,1)S(1)}, bf16[768,4096]{1,0:T(8,128)(2,1)}, u32[]{:S(2)}) copy-start(bf16[768,4096]{1,0:T(8,128)(2,1)} %refs_3_.7) | copy-start | bytes 18874372
  23.8 13.3 %collective-permute-start.5 = (bf16[144,2048]{1,0:T(8,128)(2,1)S(1)}, bf16[144,2048]{1,0:T(8,128)(2,1)S(1)}, u32[]{:S(2)}, u32[]{:S(2)}) collective-permute-start(bf16[144,2048]{1,0:T(8,128)(2,1)S(1)} %get-tuple-element.58.refs_5_), channel_id=1, source_target_pairs={{0,1},{1,0},{2,3},{3,2},{4,5},{5,4},{6,7},{7,6},{8,9},{9,8},{10,11... | collective-permute-start | bytes 1769480 | tf_op jit(solution)/shard_map/ppermute | solution.py:447
  23.8 27.6 %collective-permute-start.4 = (bf16[144,4096]{1,0:T(8,128)(2,1)S(1)}, bf16[144,4096]{1,0:T(8,128)(2,1)S(1)}, u32[]{:S(2)}, u32[]{:S(2)}) collective-permute-start(bf16[144,4096]{1,0:T(8,128)(2,1)S(1)} %arrived.2.x_ref), channel_id=1, source_target_pairs={{0,4},{1,3},{4,8},{5,1},{8,12},{9,5},{12,14},{13,9},{14,10},{15,13... | collective-permute-start | bytes 3538952 | tf_op jit(solution)/shard_map/ppermute | solution.py:447
  26.4 6.4 %collective-permute-start.6 = (s32[8,128]{1,0:T(8,128)S(1)}, s32[8,128]{1,0:T(8,128)S(1)}, u32[]{:S(2)}, u32[]{:S(2)}) collective-permute-start(s32[8,128]{1,0:T(8,128)S(1)} %get-tuple-element.52), channel_id=1, source_target_pairs={{0,3},{1,4},{4,1},{5,8},{8,5},{9,12},{12,9},{13,14},{14,13},{15,10... | collective-permute-start | bytes 12296 | tf_op jit(solution)/shard_map/ppermute | solution.py:447
  33.5 22.5 %collective-permute-start.13 = (bf16[144,4096]{1,0:T(8,128)(2,1)S(1)}, bf16[144,4096]{1,0:T(8,128)(2,1)S(1)}, u32[]{:S(2)}, u32[]{:S(2)}) collective-permute-start(bf16[144,4096]{1,0:T(8,128)(2,1)S(1)} %arrived.3.x_ref), channel_id=1, source_target_pairs={{0,4},{1,3},{4,8},{5,1},{8,12},{9,5},{12,14},{13,9},{14,10},{15,13... | collective-permute-start | bytes 3538952 | tf_op jit(solution)/shard_map/ppermute | solution.py:447
  36.5 2.0 %collective-permute-start.9 = (bf16[144,2048]{1,0:T(8,128)(2,1)S(1)}, bf16[144,2048]{1,0:T(8,128)(2,1)S(1)}, u32[]{:S(2)}, u32[]{:S(2)}) collective-permute-start(bf16[144,2048]{1,0:T(8,128)(2,1)S(1)} %get-tuple-element.61.refs_9_), channel_id=1, source_target_pairs={{0,1},{1,0},{2,3},{3,2},{4,5},{5,4},{6,7},{7,6},{8,9},{9,8},{10,11... | collective-permute-start | bytes 1769480 | tf_op jit(solution)/shard_map/ppermute | solution.py:447
  36.5 2.8 %collective-permute-start.8 = (bf16[144,2048]{1,0:T(8,128)(2,1)S(1)}, bf16[144,2048]{1,0:T(8,128)(2,1)S(1)}, u32[]{:S(2)}, u32[]{:S(2)}) collective-permute-start(bf16[144,2048]{1,0:T(8,128)(2,1)S(1)} %get-tuple-element.60.refs_7_), channel_id=1, source_target_pairs={{0,1},{1,0},{2,3},{3,2},{4,5},{5,4},{6,7},{7,6},{8,9},{9,8},{10,11... | collective-permute-start | bytes 1769480 | tf_op jit(solution)/shard_map/ppermute | solution.py:447
  37.0 3.2 %collective-permute-start.10 = (bf16[144,2048]{1,0:T(8,128)(2,1)S(1)}, bf16[144,2048]{1,0:T(8,128)(2,1)S(1)}, u32[]{:S(2)}, u32[]{:S(2)}) collective-permute-start(bf16[144,2048]{1,0:T(8,128)(2,1)S(1)} %get-tuple-element.62.refs_11_), channel_id=1, source_target_pairs={{0,1},{1,0},{2,3},{3,2},{4,5},{5,4},{6,7},{7,6},{8,9},{9,8},{10,11... | collective-permute-start | bytes 1769480 | tf_op jit(solution)/shard_map/ppermute | solution.py:447
  51.5 18.8 %collective-permute-start.11 = (bf16[144,4096]{1,0:T(8,128)(2,1)S(1)}, bf16[144,4096]{1,0:T(8,128)(2,1)S(1)}, u32[]{:S(2)}, u32[]{:S(2)}) collective-permute-start(bf16[144,4096]{1,0:T(8,128)(2,1)S(1)} %after.5.x_ref), channel_id=1, source_target_pairs={{0,4},{1,3},{4,8},{5,1},{8,12},{9,5},{12,14},{13,9},{14,10},{15,13... | collective-permute-start | bytes 3538952 | tf_op jit(solution)/shard_map/ppermute | solution.py:447
  53.3 3.5 %collective-permute-start.12 = (bf16[144,2048]{1,0:T(8,128)(2,1)S(1)}, bf16[144,2048]{1,0:T(8,128)(2,1)S(1)}, u32[]{:S(2)}, u32[]{:S(2)}) collective-permute-start(bf16[144,2048]{1,0:T(8,128)(2,1)S(1)} %get-tuple-element.67.refs_5_), channel_id=1, source_target_pairs={{0,1},{1,0},{2,3},{3,2},{4,5},{5,4},{6,7},{7,6},{8,9},{9,8},{10,11... | collective-permute-start | bytes 1769480 | tf_op jit(solution)/shard_map/ppermute | solution.py:447
  53.3 5.5 %collective-permute-start.15 = (bf16[144,2048]{1,0:T(8,128)(2,1)S(1)}, bf16[144,2048]{1,0:T(8,128)(2,1)S(1)}, u32[]{:S(2)}, u32[]{:S(2)}) collective-permute-start(bf16[144,2048]{1,0:T(8,128)(2,1)S(1)} %get-tuple-element.69.refs_9_), channel_id=1, source_target_pairs={{0,1},{1,0},{2,3},{3,2},{4,5},{5,4},{6,7},{7,6},{8,9},{9,8},{10,11... | collective-permute-start | bytes 1769480 | tf_op jit(solution)/shard_map/ppermute | solution.py:447
  56.2 2.7 %collective-permute-start.14 = (bf16[144,2048]{1,0:T(8,128)(2,1)S(1)}, bf16[144,2048]{1,0:T(8,128)(2,1)S(1)}, u32[]{:S(2)}, u32[]{:S(2)}) collective-permute-start(bf16[144,2048]{1,0:T(8,128)(2,1)S(1)} %get-tuple-element.68.refs_7_), channel_id=1, source_target_pairs={{0,1},{1,0},{2,3},{3,2},{4,5},{5,4},{6,7},{7,6},{8,9},{9,8},{10,11... | collective-permute-start | bytes 1769480 | tf_op jit(solution)/shard_map/ppermute | solution.py:447
  56.2 2.8 %collective-permute-start.16 = (bf16[144,2048]{1,0:T(8,128)(2,1)S(1)}, bf16[144,2048]{1,0:T(8,128)(2,1)S(1)}, u32[]{:S(2)}, u32[]{:S(2)}) collective-permute-start(bf16[144,2048]{1,0:T(8,128)(2,1)S(1)} %get-tuple-element.70.refs_11_), channel_id=1, source_target_pairs={{0,1},{1,0},{2,3},{3,2},{4,5},{5,4},{6,7},{7,6},{8,9},{9,8},{10,11... | collective-permute-start | bytes 1769480 | tf_op jit(solution)/shard_map/ppermute | solution.py:447
  56.7 24.6 %collective-permute-start.18 = (bf16[144,4096]{1,0:T(8,128)(2,1)S(1)}, bf16[144,4096]{1,0:T(8,128)(2,1)S(1)}, u32[]{:S(2)}, u32[]{:S(2)}) collective-permute-start(bf16[144,4096]{1,0:T(8,128)(2,1)S(1)} %after.6.x_ref), channel_id=1, source_target_pairs={{0,4},{1,3},{4,8},{5,1},{8,12},{9,5},{12,14},{13,9},{14,10},{15,13... | collective-permute-start | bytes 3538952 | tf_op jit(solution)/shard_map/ppermute | solution.py:447
  70.5 2.7 %collective-permute-start.19 = (bf16[144,2048]{1,0:T(8,128)(2,1)S(1)}, bf16[144,2048]{1,0:T(8,128)(2,1)S(1)}, u32[]{:S(2)}, u32[]{:S(2)}) collective-permute-start(bf16[144,2048]{1,0:T(8,128)(2,1)S(1)} %get-tuple-element.76.refs_5_), channel_id=1, source_target_pairs={{0,1},{1,0},{2,3},{3,2},{4,5},{5,4},{6,7},{7,6},{8,9},{9,8},{10,11... | collective-permute-start | bytes 1769480 | tf_op jit(solution)/shard_map/ppermute | solution.py:447
  70.7 2.7 %collective-permute-start.20 = (bf16[144,2048]{1,0:T(8,128)(2,1)S(1)}, bf16[144,2048]{1,0:T(8,128)(2,1)S(1)}, u32[]{:S(2)}, u32[]{:S(2)}) collective-permute-start(bf16[144,2048]{1,0:T(8,128)(2,1)S(1)} %get-tuple-element.77.refs_7_), channel_id=1, source_target_pairs={{0,1},{1,0},{2,3},{3,2},{4,5},{5,4},{6,7},{7,6},{8,9},{9,8},{10,11... | collective-permute-start | bytes 1769480 | tf_op jit(solution)/shard_map/ppermute | solution.py:447
  71.0 22.9 %collective-permute-start.17 = (bf16[144,4096]{1,0:T(8,128)(2,1)S(1)}, bf16[144,4096]{1,0:T(8,128)(2,1)S(1)}, u32[]{:S(2)}, u32[]{:S(2)}) collective-permute-start(bf16[144,4096]{1,0:T(8,128)(2,1)S(1)} %after.7.x_ref), channel_id=1, source_target_pairs={{0,4},{1,3},{4,8},{5,1},{8,12},{9,5},{12,14},{13,9},{14,10},{15,13... | collective-permute-start | bytes 3538952 | tf_op jit(solution)/shard_map/ppermute | solution.py:447
  81.4 2.1 %collective-permute-start.21 = (bf16[144,2048]{1,0:T(8,128)(2,1)S(1)}, bf16[144,2048]{1,0:T(8,128)(2,1)S(1)}, u32[]{:S(2)}, u32[]{:S(2)}) collective-permute-start(bf16[144,2048]{1,0:T(8,128)(2,1)S(1)} %get-tuple-element.81.refs_5_), channel_id=1, source_target_pairs={{0,1},{1,0},{2,3},{3,2},{4,5},{5,4},{6,7},{7,6},{8,9},{9,8},{10,11... | collective-permute-start | bytes 1769480 | tf_op jit(solution)/shard_map/ppermute | solution.py:447
  81.5 2.8 %collective-permute-start.22 = (bf16[144,2048]{1,0:T(8,128)(2,1)S(1)}, bf16[144,2048]{1,0:T(8,128)(2,1)S(1)}, u32[]{:S(2)}, u32[]{:S(2)}) collective-permute-start(bf16[144,2048]{1,0:T(8,128)(2,1)S(1)} %get-tuple-element.82.refs_7_), channel_id=1, source_target_pairs={{0,1},{1,0},{2,3},{3,2},{4,5},{5,4},{6,7},{7,6},{8,9},{9,8},{10,11... | collective-permute-start | bytes 1769480 | tf_op jit(solution)/shard_map/ppermute | solution.py:447
  94.1 3.6 %collective-permute-start.23 = (bf16[144,2048]{1,0:T(8,128)(2,1)S(1)}, bf16[144,2048]{1,0:T(8,128)(2,1)S(1)}, u32[]{:S(2)}, u32[]{:S(2)}) collective-permute-start(bf16[144,2048]{1,0:T(8,128)(2,1)S(1)} %get-tuple-element.86.refs_4_.refs_5_), channel_id=1, source_target_pairs={{0,1},{1,0},{2,3},{3,2},{4,5},{5,4},{6,7},{7,6},{8,9},{9,8},{10,11... | collective-permute-start | bytes 1769480 | tf_op jit(solution)/shard_map/ppermute | solution.py:447
  94.2 3.5 %collective-permute-start.24 = (bf16[144,2048]{1,0:T(8,128)(2,1)S(1)}, bf16[144,2048]{1,0:T(8,128)(2,1)S(1)}, u32[]{:S(2)}, u32[]{:S(2)}) collective-permute-start(bf16[144,2048]{1,0:T(8,128)(2,1)S(1)} %get-tuple-element.87.refs_4_), channel_id=1, source_target_pairs={{0,1},{1,0},{2,3},{3,2},{4,5},{5,4},{6,7},{7,6},{8,9},{9,8},{10,11... | collective-permute-start | bytes 1769480 | tf_op jit(solution)/shard_map/ppermute | solution.py:447
  97.7 5.1 %slice-start = ((s8[6291456]{0:T(1024)(128)(4,1)}), s8[4194304]{0:T(1024)(128)(4,1)S(1)}, s32[]{:S(2)}) async-start(s8[6291456]{0:T(1024)(128)(4,1)} %bitcast.1), calls=%async_computation | async-start | bytes 8388608
  97.7 5.1 %slice-start.1 = ((s8[6291456]{0:T(1024)(128)(4,1)}), s8[2097152]{0:T(1024)(128)(4,1)S(1)}, s32[]{:S(2)}) async-start(s8[6291456]{0:T(1024)(128)(4,1)} %bitcast.1), calls=%async_computation.1 | async-start | bytes 4194304
  100.7 3.7 %collective-permute-start.25 = (f32[8,128]{1,0:T(8,128)S(1)}, f32[8,128]{1,0:T(8,128)S(1)}, u32[]{:S(2)}, u32[]{:S(2)}) collective-permute-start(f32[8,128]{1,0:T(8,128)S(1)} %get-tuple-element.98.x_ref), channel_id=1, source_target_pairs={{0,2},{1,3},{2,0},{3,1},{4,6},{5,7},{6,4},{7,5},{8,10},{9,11},{10,... | collective-permute-start | bytes 12296 | tf_op jit(solution)/shard_map/ppermute | solution.py:447
  104.4 3.7 %collective-permute-start.26 = (f32[8,128]{1,0:T(8,128)S(1)}, f32[8,128]{1,0:T(8,128)S(1)}, u32[]{:S(2)}, u32[]{:S(2)}) collective-permute-start(f32[8,128]{1,0:T(8,128)S(1)} %summed.3.x_ref), channel_id=1, source_target_pairs={{0,4},{1,5},{2,6},{3,7},{4,0},{5,1},{6,2},{7,3},{8,12},{9,13},{10,... | collective-permute-start | bytes 12296 | tf_op jit(solution)/shard_map/ppermute | solution.py:447
  108.0 1.3 %collective-permute-start.27 = (f32[8,128]{1,0:T(8,128)S(1)}, f32[8,128]{1,0:T(8,128)S(1)}, u32[]{:S(2)}, u32[]{:S(2)}) collective-permute-start(f32[8,128]{1,0:T(8,128)S(1)} %summed.4.x_ref), channel_id=1, source_target_pairs={{0,1},{1,0},{2,3},{3,2},{4,5},{5,4},{6,7},{7,6},{8,9},{9,8},{10,11... | collective-permute-start | bytes 12296 | tf_op jit(solution)/shard_map/ppermute | solution.py:447
  109.4 5.8 %collective-permute-start.28 = (f32[8,128]{1,0:T(8,128)S(1)}, f32[8,128]{1,0:T(8,128)S(1)}, u32[]{:S(2)}, u32[]{:S(2)}) collective-permute-start(f32[8,128]{1,0:T(8,128)S(1)} %summed.5.squares_ref), channel_id=1, source_target_pairs={{0,8},{1,9},{2,10},{3,11},{4,12},{5,13},{6,14},{7,15},{8,0},{9,1},... | collective-permute-start | bytes 12296 | tf_op jit(solution)/shard_map/ppermute | solution.py:447

commit v13 on v11

--- a/solution.py
+++ b/solution.py
@@ -158,7 +158,8 @@
 
 
 def phase_kernel(spec, *refs):
-    groups, arrays, do_w, w_from, attn, fresh_w, fresh_out, squares, rows, begin = spec
+    groups, arrays, do_w, w_from, attn, has_before, fresh_w, fresh_out, squares = spec[:9]
+    rows, begin = spec[9:]
     refs = list(refs)
     table_ref, me_ref, heads_ref = refs.pop(0), refs.pop(0), refs.pop(0)
     at_ref = refs.pop(0) if do_w else None
@@ -166,18 +167,19 @@
     g_refs = [refs.pop(0) for _ in range(arrays)]
     if do_w and not fresh_w:
         refs.pop(0)
-    before_ref = refs.pop(0) if attn == "last" else None
+    before_ref = refs.pop(0) if has_before else None
     added_ref = refs.pop(0) if squares == "added" else None
     if attn in ("whole", "last") and not fresh_out:
         refs.pop(0)
     w_ref = refs.pop(0) if do_w else None
-    total_ref = refs.pop(0) if attn == "first" else None
+    total_ref = refs.pop(0) if attn == "part" else None
     out_ref = refs.pop(0) if attn in ("whole", "last") else None
     squares_ref = refs.pop(0)
     if attn in ("whole", "last"):
         total_ref, block_ref, sems = refs
-    if attn == "last":
-        total_ref[...] = before_ref[...]
+    if has_before:
+        if attn == "last":
+            total_ref[...] = before_ref[...]
     elif attn:
         total_ref[...] = jnp.zeros_like(total_ref)
     if squares == "added":
@@ -277,11 +279,13 @@
             add_vmem(w)
         outs.append(pltpu.VMEM((capacity, features), jnp.float32))
         out_specs.append(vmem)
-    if attn == "last":
+    if before is not None:
+        if attn == "part":
+            aliases[len(args)] = len(outs)
         add_vmem(before)
     if squares == "added":
         add_vmem(added)
-    if attn == "first":
+    if attn == "part":
         outs.append(pltpu.VMEM((height, capacity), jnp.float32))
         out_specs.append(vmem)
     elif attn:
@@ -298,8 +302,8 @@
     outs.append(pltpu.VMEM((8, 128), jnp.float32))
     out_specs.append(vmem)
     spec = (
-        tuple(described), len(arrays), do_w, w_from, attn, w is None, out is None,
-        squares, rows, begin,
+        tuple(described), len(arrays), do_w, w_from, attn, before is not None, w is None,
+        out is None, squares, rows, begin,
     )
     return pl.pallas_call(
         functools.partial(phase_kernel, spec),
@@ -318,7 +322,10 @@
     )(*args)
 
 
-def scale_kernel(parts, w_ref, squares_ref, out_ref, block_ref, sems):
+def finish_kernel(
+    parts, begin, table_ref, me_ref, heads_ref, w_ref, squares_ref, weight_ref,
+    near_ref, far_ref, before_ref, _, out_ref, grad_ref, scaled_ref, rows_ref, sems, row_sems,
+):
     capacity, features = w_ref.shape
     square_sum = jnp.sum(
         jnp.sum(squares_ref[...], axis=0, keepdims=True), axis=1, keepdims=True
@@ -330,34 +337,65 @@
     height = capacity // parts
     for i in range(parts):
         part = pl.ds(i * height, height)
-        block_ref[part, :] = (w_ref[part, :] * factor).astype(jnp.bfloat16)
-        copies.append(pltpu.make_async_copy(block_ref.at[part], out_ref.at[part], sems.at[i]))
+        scaled_ref[part, :] = (w_ref[part, :] * factor).astype(jnp.bfloat16)
+        copies.append(pltpu.make_async_copy(scaled_ref.at[part], grad_ref.at[part], sems.at[i]))
+        copies[-1].start()
+    rows, half = near_ref.shape
+    total = before_ref[...]
+    for start in range(0, half, TILE):
+        here = slice(start, start + TILE)
+        there = slice(features - half + start, features - half + start + TILE)
+        total = total + lax.dot_general(
+            jnp.concatenate([near_ref[:, here], far_ref[:, here]], axis=0),
+            weight_ref[:, there],
+            (((1,), (1,)), ((), ())),
+            preferred_element_type=jnp.float32,
+        )
+    column = lax.broadcasted_iota(jnp.int32, total.shape, 1)
+    live = column < heads_ref[0] * HEAD_DIM
+    rows_ref[...] = jnp.where(live, total, 0.0).astype(jnp.bfloat16)
+    for i in range(2):
+        owner = table_ref[me_ref[0], begin + i]
+        target = out_ref.at[pl.ds(pl.multiple_of(owner * rows, rows), rows)]
+        copies.append(
+            pltpu.make_async_copy(rows_ref.at[pl.ds(i * rows, rows)], target, row_sems.at[i])
+        )
         copies[-1].start()
     for copy in copies:
         copy.wait()
 
 
-def scaled(w, squares):
+def finished(where, begin, w, squares, weight, near, far, before, out):
     capacity, features = w.shape
+    rows = near.shape[0]
     vmem = pl.BlockSpec(memory_space=pltpu.VMEM)
+    smem = pl.BlockSpec(memory_space=pltpu.SMEM)
+    hbm = pl.BlockSpec(memory_space=pl.ANY)
     parts = 8
+    arrays = (w, squares, weight, near, far, before)
     return pl.pallas_call(
-        functools.partial(scale_kernel, parts),
-        in_specs=[vmem, vmem],
-        out_specs=pl.BlockSpec(memory_space=pl.ANY),
-        out_shape=jax.ShapeDtypeStruct((capacity, features), jnp.bfloat16),
+        functools.partial(finish_kernel, parts, begin),
+        in_specs=[smem] * 3 + [vmem] * len(arrays) + [hbm],
+        out_specs=[hbm] * 2,
+        out_shape=[
+            jax.ShapeDtypeStruct(out.shape, out.dtype),
+            jax.ShapeDtypeStruct((capacity, features), jnp.bfloat16),
+        ],
         scratch_shapes=[
             pltpu.VMEM((capacity, features), jnp.bfloat16),
+            pltpu.VMEM((2 * rows, capacity), jnp.bfloat16),
             pltpu.SemaphoreType.DMA((parts,)),
+            pltpu.SemaphoreType.DMA((2,)),
         ],
-        compiler_params=pltpu.CompilerParams(vmem_limit_bytes=10 * MIB),
+        input_output_aliases={3 + len(arrays): 0},
+        compiler_params=pltpu.CompilerParams(vmem_limit_bytes=14 * MIB),
         cost_estimate=pl.CostEstimate(
             flops=capacity * features,
             bytes_accessed=2 * capacity * features,
             transcendentals=0,
         ),
-        name="scale",
-    )(pltpu.with_memory_space_constraint(w, pltpu.VMEM), squares)
+        name="finish",
+    )(*where, *[pltpu.with_memory_space_constraint(x, pltpu.VMEM) for x in arrays], out)
 
 
 def after(done, *arrays):
@@ -461,10 +499,9 @@
         far_x = swapped(near_x)
         i = 2 * k - 1
         if k == last - 1:
-            held = held + [near_x, far_x]
             w, out, done = phase(
-                where, shapes, 2 * (i + 1) - len(held), grouped(*held), at=ats[i], w=w,
-                w_from=len(held) - 2, weight=weight, attn="whole", out=out,
+                where, shapes, 2 * i, grouped(near_x, far_x), at=ats[i], w=w,
+                weight=weight, attn="whole", out=out,
             )
         y = arrived(done, counts[1], y) if k == 1 else after(done, y)[0]
         y, near_y = send(y, ring.along()) if k < last - 1 else None, split(y)
@@ -475,9 +512,6 @@
                 where, shapes, 2 * (i + 1), grouped(near_y, far_y), at=ats[i + 1], w=w,
                 weight=weight, attn="whole", out=out,
             )
-        elif k == last - 2:
-            held = [near_x, far_x, near_y, far_y]
-            w, done = phase(where, shapes, 2 * i, groups, at=ats[i], w=w)
         else:
             w, out, done = phase(
                 where, shapes, 2 * i, groups, at=ats[i], w=w,
@@ -491,24 +525,18 @@
     w, done = phase(where, shapes, begin, grouped(near), at=ats[-2], w=w)
     w, squares = phase(where, shapes, begin, grouped(far), at=ats[-1], w=w, squares="new")
 
-    pieces = [group[3] for group in grouped(near, far)]
-    parts = [
-        [(0, half, 0, pieces[0]), (half, half // 2, 0, pieces[1])],
-        [(half + half // 2, half // 2, half // 2, pieces[1])],
-    ]
+    before, part = None, half // 2
     for late, masks in enumerate(rounds(devices)):
         squares = exchange(squares, devices, masks)
-        if late == 0:
+        if late < 2:
+            groups = [(late * part, part, late * part, grouped(near, far)[0][3])]
             before, done = phase(
-                where, shapes, begin, parts[0], weight=weight, attn="first"
+                where, shapes, begin, groups, weight=weight, attn="part", before=before
             )
             (squares,) = after(done, squares)
-        elif late == 1:
-            out, done = phase(
-                where, shapes, begin, parts[1], weight=weight, attn="last",
-                before=before, out=out,
-            )
-    return out, scaled(w, squares)
+    return finished(
+        where, begin, w, squares, weight, near[1], far[1], before, out
+    )
 
 
 def solution(mesh):

time: 117 us -> 119 us (1.017); the launches traced: 117 us -> 118 us
  waiting for transfers between devices: 17.9 us -> 19.1 us
    pallas_call x9, Pallas kernels: 55.4 us -> 53.3 us  [phase(): pl.pallas_call(functools.partial(phase_kernel, spec), in_specs=specs, out...]
    ppermute x6, waiting for transfers between devices: 0.92 us -> 3.03 us  [exchange(): lax.ppermute(x, 'dp', [(d, d ^ mask) for d in range(devices)])]
    pallas_call x1, Pallas kernels: 3 us -> 4.75 us  [finished(): pl.pallas_call(functools.partial(finish_kernel, parts, begin), in_specs=[...]
    unnamed x8 -> x10, local copies, waits for them, and re-layouts: 3.49 us -> 3.49 us
  transfers between devices with their start and end apart: 31 -> 31, of which waited for: 14 -> 16; matrix products, arithmetic and copies ran while one was open for 0% -> 0% of each run, Pallas kernels for 50% -> 48%
where the time goes in v13:
time: 119 us; the launch traced here: 118 us
  Pallas kernels  64.1 us (54%)
  starting transfers between devices  28.8 us (24%)
  waiting for transfers between devices  19.1 us (16%)
  local copies, waits for them, and re-layouts  3.49 us (3%)
  between operations  2.4 us (2%)
    pallas_call x9, Pallas kernels, phase(): pl.pallas_call(functools.partial(phase_kernel, spec), in_specs=specs, out...  53.3 us
    ppermute x25, starting transfers between devices, send(): return lax.ppermute(x, 'dp', pairs)  22.3 us
    ppermute x25, waiting for transfers between devices, send(): return lax.ppermute(x, 'dp', pairs)  16.1 us
    ppermute x6, starting transfers between devices, exchange(): lax.ppermute(x, 'dp', [(d, d ^ mask) for d in range(devices)])  6.5 us
    pallas_call x1, Pallas kernels, finished(): pl.pallas_call(functools.partial(finish_kernel, parts, begin), in_specs=[...  4.75 us
    pallas_call x1, Pallas kernels, prepared(): pl.pallas_call(functools.partial(prep_kernel, spans, rows), in_specs=[sme...  3.96 us
    unnamed x10, local copies, waits for them, and re-layouts  3.49 us
    ppermute x6, waiting for transfers between devices, exchange(): lax.ppermute(x, 'dp', [(d, d ^ mask) for d in range(devices)])  3.03 us
  transfers between devices with their start and end apart: 31, of which 16 were waited for; matrix products, arithmetic and copies ran while one was open for 0% of the time, Pallas kernels for 48%

profile of v13, /device:TPU:0, one launch (start us, length us, event | category | flops | bytes accessed | tf_op | source)
XLA Modules:
  0.0 117.8 jit_solution(7034799473568882587)
XLA Ops:
  0.6 3.1 %collective-permute-start.1 = (bf16[144,4096]{1,0:T(8,128)(2,1)}, bf16[144,4096]{1,0:T(8,128)(2,1)S(1)}, u32[]{:S(2)}, u32[]{:S(2)}) collective-permute-start(bf16[144,4096]{1,0:T(8,128)(2,1)} %grad_ref.1), channel_id=1, source_target_pairs={{0,4},{1,3},{4,8},{5,1},{8,12},{9,5},{12,14},{13,9},{14,10},{15,13... | collective-permute-start | bytes 3538952 | tf_op jit(solution)/shard_map/ppermute | solution.py:474
  5.0 0.7 copy-done.1
  5.7 4.0 %prep.1 = (bf16[144,4096]{1,0:T(8,128)(2,1)S(1)}, bf16[144,2048]{1,0:T(8,128)(2,1)S(1)}, bf16[144,2048]{1,0:T(8,128)(2,1)S(1)}, s32[8,128]{1,0:T(8,128)S(1)}, bf...) custom-call(s32[16,16]{1,0:T(8,128)S(1)} %copy-done.1, ...), custom_call_target="tpu_custom_call" | custom-call | flops 1 | bytes 1 | tf_op jit(solution)/shard_map/prep/pallas_call | solution.py:121
  9.7 0.1 collective-permute-start.2
  9.8 0.5 collective-permute-start.3
  10.2 0.7 collective-permute-start.7
  10.9 1.0 collective-permute-start
  12.0 0.6 collective-permute-done.3.refs_8_
  12.6 2.8 %copy-done = bf16[768,4096]{1,0:T(8,128)(2,1)S(1)} copy-done((bf16[768,4096]{1,0:T(8,128)(2,1)S(1)}, bf16[768,4096]{1,0:T(8,128)(2,1)}, u32[]{:S(2)}) %copy-start) | copy-done | bytes 6291480
  15.4 7.2 %phase_w_whole.5 = (f32[768,4096]{1,0:T(8,128)S(1)}, bf16[2304,768]{1,0:T(8,128)(2,1)}, f32[8,128]{1,0:T(8,128)S(1)}) custom-call(s32[16,16]{1,0:T(8,128)S(1)} %copy-done.1, s32[1]{0:T(128)} %bitcast.me_ref.refs_1_, s32[1]{0:T(128)S(6)} %copy.50.heads_ref.refs_2_, bf16[768,288]{1,0:T(8,128)(2,1)S(1)} %get-tuple-element.51.refs_3_, ...), custom_call_target="tpu_custom_call" | custom-call | flops 1 | bytes 1 | tf_op jit(solution)/shard_map/phase_w_whole/pallas_call | solution.py:308
  22.6 0.4 collective-permute-done.count_ref
  23.0 0.7 arrived.2.x_ref
  23.6 0.1 split.7
  23.8 0.1 collective-permute-start.5
  23.8 2.5 %collective-permute-start.4 = (bf16[144,4096]{1,0:T(8,128)(2,1)S(1)}, bf16[144,4096]{1,0:T(8,128)(2,1)S(1)}, u32[]{:S(2)}, u32[]{:S(2)}) collective-permute-start(bf16[144,4096]{1,0:T(8,128)(2,1)S(1)} %arrived.2.x_ref), channel_id=1, source_target_pairs={{0,4},{1,3},{4,8},{5,1},{8,12},{9,5},{12,14},{13,9},{14,10},{15,13... | collective-permute-start | bytes 3538952 | tf_op jit(solution)/shard_map/ppermute | solution.py:474
  26.4 2.2 %collective-permute-start.6 = (s32[8,128]{1,0:T(8,128)S(1)}, s32[8,128]{1,0:T(8,128)S(1)}, u32[]{:S(2)}, u32[]{:S(2)}) collective-permute-start(s32[8,128]{1,0:T(8,128)S(1)} %get-tuple-element.50), channel_id=1, source_target_pairs={{0,3},{1,4},{4,1},{5,8},{8,5},{9,12},{12,9},{13,14},{14,13},{15,10... | collective-permute-start | bytes 12296 | tf_op jit(solution)/shard_map/ppermute | solution.py:474
  28.5 4.2 %collective-permute-done.6.count_ref = s32[8,128]{1,0:T(8,128)S(1)} collective-permute-done((s32[8,128]{1,0:T(8,128)S(1)}, s32[8,128]{1,0:T(8,128)S(1)}, u32[]{:S(2)}, u32[]{:S(2)}) %collective-permute-start.6) | collective-permute-done | bytes 4128 | tf_op jit(solution)/shard_map/ppermute | solution.py:474
  32.8 0.7 arrived.3.x_ref
  33.4 0.1 split.8
  33.5 3.0 %collective-permute-start.13 = (bf16[144,4096]{1,0:T(8,128)(2,1)S(1)}, bf16[144,4096]{1,0:T(8,128)(2,1)S(1)}, u32[]{:S(2)}, u32[]{:S(2)}) collective-permute-start(bf16[144,4096]{1,0:T(8,128)(2,1)S(1)} %arrived.3.x_ref), channel_id=1, source_target_pairs={{0,4},{1,3},{4,8},{5,1},{8,12},{9,5},{12,14},{13,9},{14,10},{15,13... | collective-permute-start | bytes 3538952 | tf_op jit(solution)/shard_map/ppermute | solution.py:474
  36.5 0.5 collective-permute-start.8
  37.1 1.5 %collective-permute-done.9.refs_10_ = bf16[144,2048]{1,0:T(8,128)(2,1)S(1)} collective-permute-done((bf16[144,2048]{1,0:T(8,128)(2,1)S(1)}, bf16[144,2048]{1,0:T(8,128)(2,1)S(1)}, u32[]{:S(2)}, u32[]{:S(2)}) %collective-permute-start.9) | collective-permute-done | bytes 589856 | tf_op jit(solution)/shard_map/ppermute | solution.py:474
  38.5 0.8 collective-permute-done.8.refs_8_
  39.4 0.8 collective-permute-done.10.refs_12_
  40.2 11.3 %phase_w_whole.6 = (f32[768,4096]{1,0:T(8,128)S(1)}, bf16[2304,768]{1,0:T(8,128)(2,1)}, f32[8,128]{1,0:T(8,128)S(1)}) custom-call(s32[16,16]{1,0:T(8,128)S(1)} %copy-done.1, s32[1]{0:T(128)} %bitcast.me_ref.refs_1_, s32[1]{0:T(128)S(6)} %copy.50.heads_ref.refs_2_, ...), custom_call_target="tpu_custom_call", output_to_operand_aliasing={{0}: (13, {}), {1}: (14, {})} | custom-call | flops 1 | bytes 1 | tf_op jit(solution)/shard_map/phase_w_whole/pallas_call | solution.py:308
  51.5 1.6 %collective-permute-start.11 = (bf16[144,4096]{1,0:T(8,128)(2,1)S(1)}, bf16[144,4096]{1,0:T(8,128)(2,1)S(1)}, u32[]{:S(2)}, u32[]{:S(2)}) collective-permute-start(bf16[144,4096]{1,0:T(8,128)(2,1)S(1)} %after.7.x_ref), channel_id=1, source_target_pairs={{0,4},{1,3},{4,8},{5,1},{8,12},{9,5},{12,14},{13,9},{14,10},{15,13... | collective-permute-start | bytes 3538952 | tf_op jit(solution)/shard_map/ppermute | solution.py:474
  53.1 0.1 split.9
  53.3 0.1 collective-permute-start.12
  53.3 0.5 collective-permute-start.15
  53.8 2.2 %collective-permute-done.13.refs_0_ = bf16[144,4096]{1,0:T(8,128)(2,1)S(1)} collective-permute-done((bf16[144,4096]{1,0:T(8,128)(2,1)S(1)}, bf16[144,4096]{1,0:T(8,128)(2,1)S(1)}, u32[]{:S(2)}, u32[]{:S(2)}) %collective-permute-start.13) | collective-permute-done | bytes 1179680 | tf_op jit(solution)/shard_map/ppermute | solution.py:474
  56.1 0.1 split.10
  56.2 0.5 collective-permute-start.16
  56.7 2.1 %collective-permute-start.18 = (bf16[144,4096]{1,0:T(8,128)(2,1)S(1)}, bf16[144,4096]{1,0:T(8,128)(2,1)S(1)}, u32[]{:S(2)}, u32[]{:S(2)}) collective-permute-start(bf16[144,4096]{1,0:T(8,128)(2,1)S(1)} %after.8.x_ref), channel_id=1, source_target_pairs={{0,4},{1,3},{4,8},{5,1},{8,12},{9,5},{12,14},{13,9},{14,10},{15,13... | collective-permute-start | bytes 3538952 | tf_op jit(solution)/shard_map/ppermute | solution.py:474
  58.8 0.2 collective-permute-done.16.refs_12_
  59.1 11.3 %phase_w_whole.7 = (f32[768,4096]{1,0:T(8,128)S(1)}, bf16[2304,768]{1,0:T(8,128)(2,1)}, f32[8,128]{1,0:T(8,128)S(1)}) custom-call(s32[16,16]{1,0:T(8,128)S(1)} %copy-done.1, s32[1]{0:T(128)} %bitcast.me_ref.refs_1_, s32[1]{0:T(128)S(6)} %copy.50.heads_ref.refs_2_, ...), custom_call_target="tpu_custom_call", output_to_operand_aliasing={{0}: (13, {}), {1}: (14, {})} | custom-call | flops 1 | bytes 1 | tf_op jit(solution)/shard_map/phase_w_whole/pallas_call | solution.py:308
  70.4 0.1 split.11
  70.5 0.2 collective-permute-start.19
  70.7 0.4 collective-permute-start.20
  71.0 2.1 %collective-permute-start.17 = (bf16[144,4096]{1,0:T(8,128)(2,1)S(1)}, bf16[144,4096]{1,0:T(8,128)(2,1)S(1)}, u32[]{:S(2)}, u32[]{:S(2)}) collective-permute-start(bf16[144,4096]{1,0:T(8,128)(2,1)S(1)} %after.9.x_ref), channel_id=1, source_target_pairs={{0,4},{1,3},{4,8},{5,1},{8,12},{9,5},{12,14},{13,9},{14,10},{15,13... | collective-permute-start | bytes 3538952 | tf_op jit(solution)/shard_map/ppermute | solution.py:474
  73.1 0.3 collective-permute-done.20.refs_8_
  73.4 7.5 %phase_w_whole.8 = (f32[768,4096]{1,0:T(8,128)S(1)}, bf16[2304,768]{1,0:T(8,128)(2,1)}, f32[8,128]{1,0:T(8,128)S(1)}) custom-call(s32[16,16]{1,0:T(8,128)S(1)} %copy-done.1, s32[1]{0:T(128)} %bitcast.me_ref.refs_1_, s32[1]{0:T(128)S(6)} %copy.50.heads_ref.refs_2_, ...), custom_call_target="tpu_custom_call", output_to_operand_aliasing={{0}: (9, {}), {1}: (10, {})} | custom-call | flops 1 | bytes 1 | tf_op jit(solution)/shard_map/phase_w_whole/pallas_call | solution.py:308
  80.9 0.5 collective-permute-done.18.refs_0_
  81.3 0.1 split.12
  81.5 0.5 collective-permute-start.22
  82.0 1.5 %collective-permute-done.21.refs_6_ = bf16[144,2048]{1,0:T(8,128)(2,1)S(1)} collective-permute-done((bf16[144,2048]{1,0:T(8,128)(2,1)S(1)}, bf16[144,2048]{1,0:T(8,128)(2,1)S(1)}, u32[]{:S(2)}, u32[]{:S(2)}) %collective-permute-start.21) | collective-permute-done | bytes 589856 | tf_op jit(solution)/shard_map/ppermute | solution.py:474
  83.5 0.8 collective-permute-done.22.refs_8_
  84.4 7.5 %phase_w_whole.9 = (f32[768,4096]{1,0:T(8,128)S(1)}, bf16[2304,768]{1,0:T(8,128)(2,1)}, f32[8,128]{1,0:T(8,128)S(1)}) custom-call(s32[16,16]{1,0:T(8,128)S(1)} %copy-done.1, s32[1]{0:T(128)} %bitcast.me_ref.refs_1_, s32[1]{0:T(128)S(6)} %copy.50.heads_ref.refs_2_, ...), custom_call_target="tpu_custom_call", output_to_operand_aliasing={{0}: (9, {}), {1}: (10, {})} | custom-call | flops 1 | bytes 1 | tf_op jit(solution)/shard_map/phase_w_whole/pallas_call | solution.py:308
  91.8 2.1 %collective-permute-done.17.refs_0_ = bf16[144,4096]{1,0:T(8,128)(2,1)S(1)} collective-permute-done((bf16[144,4096]{1,0:T(8,128)(2,1)S(1)}, bf16[144,4096]{1,0:T(8,128)(2,1)S(1)}, u32[]{:S(2)}, u32[]{:S(2)}) %collective-permute-start.17) | collective-permute-done | bytes 1179680 | tf_op jit(solution)/shard_map/ppermute | solution.py:474
  94.0 0.1 split.13
  94.2 0.5 collective-permute-start.23
  94.7 3.0 %phase_w_None.2 = (f32[768,4096]{1,0:T(8,128)S(1)}, f32[8,128]{1,0:T(8,128)}) custom-call(s32[16,16]{1,0:T(8,128)S(1)} %copy-done.1, s32[1]{0:T(128)} %bitcast.me_ref.refs_1_, s32[1]{0:T(128)S(6)} %copy.50.heads_ref.refs_2_, bf16[768,144]{1,0:T(8,128)(2,1)S(1)} %get-tuple-element.86.refs_3_, ...), custom_call_target="tpu_custom_call", output_to_operand_aliasing={{0}: (6, {})} | custom-call | flops 1 | bytes 1 | tf_op jit(solution)/shard_map/phase_w_None/pallas_call | solution.py:308
  97.7 2.9 %phase_w_None.3 = (f32[768,4096]{1,0:T(8,128)S(1)}, f32[8,128]{1,0:T(8,128)S(1)}) custom-call(s32[16,16]{1,0:T(8,128)S(1)} %copy-done.1, s32[1]{0:T(128)} %bitcast.me_ref.refs_1_, s32[1]{0:T(128)S(6)} %copy.50.heads_ref.refs_2_, bf16[768,144]{1,0:T(8,128)(2,1)S(1)} %get-tuple-element.49.refs_3_, ...), custom_call_target="tpu_custom_call", output_to_operand_aliasing={{0}: (6, {})} | custom-call | flops 1 | bytes 1 | tf_op jit(solution)/shard_map/phase_w_None/pallas_call | solution.py:308
  100.6 3.1 %collective-permute-start.27 = (f32[8,128]{1,0:T(8,128)S(1)}, f32[8,128]{1,0:T(8,128)S(1)}, u32[]{:S(2)}, u32[]{:S(2)}) collective-permute-start(f32[8,128]{1,0:T(8,128)S(1)} %get-tuple-element.90), channel_id=1, source_target_pairs={{0,6},{1,7},{2,4},{3,5},{4,2},{5,3},{6,0},{7,1},{8,14},{9,15},{10,... | collective-permute-start | bytes 12296 | tf_op jit(solution)/shard_map/ppermute | solution.py:454
  103.7 0.4 collective-permute-start.26
  104.2 0.2 collective-permute-start.25
  104.4 1.3 %phase__part.2 = (f32[288,768]{1,0:T(8,128)S(1)}, f32[8,128]{1,0:T(8,128)S(1)}) custom-call(s32[16,16]{1,0:T(8,128)S(1)} %copy-done.1, s32[1]{0:T(128)} %bitcast.me_ref.refs_1_, s32[1]{0:T(128)S(6)} %copy.50.heads_ref.refs_2_, bf16[768,4096]{1,0:T(8,128)(2,1)S(1)} %bitcast.2, bf16[144,2048]{1,0:T(8,128)(2,1)S(1)} %get-tuple-element.84.refs_4_, ...), custom_call_target="tpu_custom_call" | custom-call | flops 1 | bytes 1 | tf_op jit(solution)/shard_map/phase__part/pallas_call | solution.py:308
  105.7 1.6 %collective-permute-done.26 = f32[8,128]{1,0:T(8,128)S(1)} collective-permute-done((f32[8,128]{1,0:T(8,128)S(1)}, f32[8,128]{1,0:T(8,128)S(1)}, u32[]{:S(2)}, u32[]{:S(2)}) %collective-permute-start.26) | collective-permute-done | bytes 4128 | tf_op jit(solution)/shard_map/ppermute | solution.py:454
  107.4 0.4 collective-permute-done.25
  107.8 0.6 collective-permute-start.30
  108.4 2.1 %collective-permute-start.29 = (f32[8,128]{1,0:T(8,128)S(1)}, f32[8,128]{1,0:T(8,128)S(1)}, u32[]{:S(2)}, u32[]{:S(2)}) collective-permute-start(f32[8,128]{1,0:T(8,128)S(1)} %after.12), channel_id=1, source_target_pairs={{0,8},{1,9},{2,10},{3,11},{4,12},{5,13},{6,14},{7,15},{8,0},{9,1},... | collective-permute-start | bytes 12296 | tf_op jit(solution)/shard_map/ppermute | solution.py:454
  110.5 0.1 collective-permute-start.28
  110.6 1.3 %phase__part.3 = (f32[288,768]{1,0:T(8,128)S(1)}, f32[8,128]{1,0:T(8,128)S(1)}) custom-call(s32[16,16]{1,0:T(8,128)S(1)} %copy-done.1, s32[1]{0:T(128)} %bitcast.me_ref.refs_1_, s32[1]{0:T(128)S(6)} %copy.50.heads_ref.refs_2_, bf16[768,4096]{1,0:T(8,128)(2,1)S(1)} %bitcast.2, ...), custom_call_target="tpu_custom_call", output_to_operand_aliasing={{0}: (6, {})} | custom-call | flops 1 | bytes 1 | tf_op jit(solution)/shard_map/phase__part/pallas_call | solution.py:308
  111.9 1.0 collective-permute-done.29
  112.9 4.7 %finish.1 = (bf16[2304,768]{1,0:T(8,128)(2,1)}, bf16[768,4096]{1,0:T(8,128)(2,1)}) custom-call(s32[16,16]{1,0:T(8,128)S(1)} %copy-done.2, s32[1]{0:T(128)} %bitcast.me_ref.refs_1_, s32[1]{0:T(128)S(6)} %copy.50.heads_ref.refs_2_, f32[768,4096]{1,0:T(8,128)S(1)} %get-tuple-element.89.w_ref, ...), custom_call_target="tpu_custom_call", output_to_operand_aliasing={{0}: (9, {})} | custom-call | flops 3145728 | bytes 6291456 | tf_op jit(solution)/shard_map/finish/pallas_call | solution.py:376
  (38 shorter events, 0.3 us)
Async XLA Ops:
  0.6 22.4 %collective-permute-start.1 = (bf16[144,4096]{1,0:T(8,128)(2,1)}, bf16[144,4096]{1,0:T(8,128)(2,1)S(1)}, u32[]{:S(2)}, u32[]{:S(2)}) collective-permute-start(bf16[144,4096]{1,0:T(8,128)(2,1)} %grad_ref.1), channel_id=1, source_target_pairs={{0,4},{1,3},{4,8},{5,1},{8,12},{9,5},{12,14},{13,9},{14,10},{15,13... | collective-permute-start | bytes 3538952 | tf_op jit(solution)/shard_map/ppermute | solution.py:474
  5.0 0.7 copy-start.1
  9.7 2.3 %collective-permute-start.2 = (bf16[144,2048]{1,0:T(8,128)(2,1)S(1)}, bf16[144,2048]{1,0:T(8,128)(2,1)S(1)}, u32[]{:S(2)}, u32[]{:S(2)}) collective-permute-start(bf16[144,2048]{1,0:T(8,128)(2,1)S(1)} %get-tuple-element.52.refs_5_), channel_id=1, source_target_pairs={{0,1},{1,0},{2,3},{3,2},{4,5},{5,4},{6,7},{7,6},{8,9},{9,8},{10,11... | collective-permute-start | bytes 1769480 | tf_op jit(solution)/shard_map/ppermute | solution.py:474
  9.8 2.8 %collective-permute-start.3 = (bf16[144,2048]{1,0:T(8,128)(2,1)S(1)}, bf16[144,2048]{1,0:T(8,128)(2,1)S(1)}, u32[]{:S(2)}, u32[]{:S(2)}) collective-permute-start(bf16[144,2048]{1,0:T(8,128)(2,1)S(1)} %get-tuple-element.53.refs_7_), channel_id=1, source_target_pairs={{0,1},{1,0},{2,3},{3,2},{4,5},{5,4},{6,7},{7,6},{8,9},{9,8},{10,11... | collective-permute-start | bytes 1769480 | tf_op jit(solution)/shard_map/ppermute | solution.py:474
  10.2 22.5 %collective-permute-start.7 = (bf16[144,4096]{1,0:T(8,128)(2,1)S(1)}, bf16[144,4096]{1,0:T(8,128)(2,1)S(1)}, u32[]{:S(2)}, u32[]{:S(2)}) collective-permute-start(bf16[144,4096]{1,0:T(8,128)(2,1)S(1)} %get-tuple-element.57), channel_id=1, source_target_pairs={{0,3},{1,4},{4,1},{5,8},{8,5},{9,12},{12,9},{13,14},{14,13},{15,10... | collective-permute-start | bytes 3538952 | tf_op jit(solution)/shard_map/ppermute | solution.py:474
  10.9 12.1 %collective-permute-start = (s32[8,128]{1,0:T(8,128)S(1)}, s32[8,128]{1,0:T(8,128)S(1)}, u32[]{:S(2)}, u32[]{:S(2)}) collective-permute-start(s32[8,128]{1,0:T(8,128)S(1)} %get-tuple-element.50), channel_id=1, source_target_pairs={{0,4},{1,3},{4,8},{5,1},{8,12},{9,5},{12,14},{13,9},{14,10},{15,13... | collective-permute-start | bytes 12296 | tf_op jit(solution)/shard_map/ppermute | solution.py:474
  12.6 2.8 %copy-start = (bf16[768,4096]{1,0:T(8,128)(2,1)S(1)}, bf16[768,4096]{1,0:T(8,128)(2,1)}, u32[]{:S(2)}) copy-start(bf16[768,4096]{1,0:T(8,128)(2,1)} %weight_ref.1) | copy-start | bytes 18874372
  23.8 13.3 %collective-permute-start.5 = (bf16[144,2048]{1,0:T(8,128)(2,1)S(1)}, bf16[144,2048]{1,0:T(8,128)(2,1)S(1)}, u32[]{:S(2)}, u32[]{:S(2)}) collective-permute-start(bf16[144,2048]{1,0:T(8,128)(2,1)S(1)} %get-tuple-element.56.refs_5_), channel_id=1, source_target_pairs={{0,1},{1,0},{2,3},{3,2},{4,5},{5,4},{6,7},{7,6},{8,9},{9,8},{10,11... | collective-permute-start | bytes 1769480 | tf_op jit(solution)/shard_map/ppermute | solution.py:474
  23.8 27.7 %collective-permute-start.4 = (bf16[144,4096]{1,0:T(8,128)(2,1)S(1)}, bf16[144,4096]{1,0:T(8,128)(2,1)S(1)}, u32[]{:S(2)}, u32[]{:S(2)}) collective-permute-start(bf16[144,4096]{1,0:T(8,128)(2,1)S(1)} %arrived.2.x_ref), channel_id=1, source_target_pairs={{0,4},{1,3},{4,8},{5,1},{8,12},{9,5},{12,14},{13,9},{14,10},{15,13... | collective-permute-start | bytes 3538952 | tf_op jit(solution)/shard_map/ppermute | solution.py:474
  26.4 6.4 %collective-permute-start.6 = (s32[8,128]{1,0:T(8,128)S(1)}, s32[8,128]{1,0:T(8,128)S(1)}, u32[]{:S(2)}, u32[]{:S(2)}) collective-permute-start(s32[8,128]{1,0:T(8,128)S(1)} %get-tuple-element.50), channel_id=1, source_target_pairs={{0,3},{1,4},{4,1},{5,8},{8,5},{9,12},{12,9},{13,14},{14,13},{15,10... | collective-permute-start | bytes 12296 | tf_op jit(solution)/shard_map/ppermute | solution.py:474
  33.5 22.5 %collective-permute-start.13 = (bf16[144,4096]{1,0:T(8,128)(2,1)S(1)}, bf16[144,4096]{1,0:T(8,128)(2,1)S(1)}, u32[]{:S(2)}, u32[]{:S(2)}) collective-permute-start(bf16[144,4096]{1,0:T(8,128)(2,1)S(1)} %arrived.3.x_ref), channel_id=1, source_target_pairs={{0,4},{1,3},{4,8},{5,1},{8,12},{9,5},{12,14},{13,9},{14,10},{15,13... | collective-permute-start | bytes 3538952 | tf_op jit(solution)/shard_map/ppermute | solution.py:474
  36.5 2.0 %collective-permute-start.9 = (bf16[144,2048]{1,0:T(8,128)(2,1)S(1)}, bf16[144,2048]{1,0:T(8,128)(2,1)S(1)}, u32[]{:S(2)}, u32[]{:S(2)}) collective-permute-start(bf16[144,2048]{1,0:T(8,128)(2,1)S(1)} %get-tuple-element.59.refs_9_), channel_id=1, source_target_pairs={{0,1},{1,0},{2,3},{3,2},{4,5},{5,4},{6,7},{7,6},{8,9},{9,8},{10,11... | collective-permute-start | bytes 1769480 | tf_op jit(solution)/shard_map/ppermute | solution.py:474
  36.5 2.8 %collective-permute-start.8 = (bf16[144,2048]{1,0:T(8,128)(2,1)S(1)}, bf16[144,2048]{1,0:T(8,128)(2,1)S(1)}, u32[]{:S(2)}, u32[]{:S(2)}) collective-permute-start(bf16[144,2048]{1,0:T(8,128)(2,1)S(1)} %get-tuple-element.58.refs_7_), channel_id=1, source_target_pairs={{0,1},{1,0},{2,3},{3,2},{4,5},{5,4},{6,7},{7,6},{8,9},{9,8},{10,11... | collective-permute-start | bytes 1769480 | tf_op jit(solution)/shard_map/ppermute | solution.py:474
  37.1 3.2 %collective-permute-start.10 = (bf16[144,2048]{1,0:T(8,128)(2,1)S(1)}, bf16[144,2048]{1,0:T(8,128)(2,1)S(1)}, u32[]{:S(2)}, u32[]{:S(2)}) collective-permute-start(bf16[144,2048]{1,0:T(8,128)(2,1)S(1)} %get-tuple-element.60.refs_11_), channel_id=1, source_target_pairs={{0,1},{1,0},{2,3},{3,2},{4,5},{5,4},{6,7},{7,6},{8,9},{9,8},{10,11... | collective-permute-start | bytes 1769480 | tf_op jit(solution)/shard_map/ppermute | solution.py:474
  51.5 18.8 %collective-permute-start.11 = (bf16[144,4096]{1,0:T(8,128)(2,1)S(1)}, bf16[144,4096]{1,0:T(8,128)(2,1)S(1)}, u32[]{:S(2)}, u32[]{:S(2)}) collective-permute-start(bf16[144,4096]{1,0:T(8,128)(2,1)S(1)} %after.7.x_ref), channel_id=1, source_target_pairs={{0,4},{1,3},{4,8},{5,1},{8,12},{9,5},{12,14},{13,9},{14,10},{15,13... | collective-permute-start | bytes 3538952 | tf_op jit(solution)/shard_map/ppermute | solution.py:474
  53.3 3.5 %collective-permute-start.12 = (bf16[144,2048]{1,0:T(8,128)(2,1)S(1)}, bf16[144,2048]{1,0:T(8,128)(2,1)S(1)}, u32[]{:S(2)}, u32[]{:S(2)}) collective-permute-start(bf16[144,2048]{1,0:T(8,128)(2,1)S(1)} %get-tuple-element.65.refs_5_), channel_id=1, source_target_pairs={{0,1},{1,0},{2,3},{3,2},{4,5},{5,4},{6,7},{7,6},{8,9},{9,8},{10,11... | collective-permute-start | bytes 1769480 | tf_op jit(solution)/shard_map/ppermute | solution.py:474
  53.3 5.5 %collective-permute-start.15 = (bf16[144,2048]{1,0:T(8,128)(2,1)S(1)}, bf16[144,2048]{1,0:T(8,128)(2,1)S(1)}, u32[]{:S(2)}, u32[]{:S(2)}) collective-permute-start(bf16[144,2048]{1,0:T(8,128)(2,1)S(1)} %get-tuple-element.67.refs_9_), channel_id=1, source_target_pairs={{0,1},{1,0},{2,3},{3,2},{4,5},{5,4},{6,7},{7,6},{8,9},{9,8},{10,11... | collective-permute-start | bytes 1769480 | tf_op jit(solution)/shard_map/ppermute | solution.py:474
  56.2 2.7 %collective-permute-start.14 = (bf16[144,2048]{1,0:T(8,128)(2,1)S(1)}, bf16[144,2048]{1,0:T(8,128)(2,1)S(1)}, u32[]{:S(2)}, u32[]{:S(2)}) collective-permute-start(bf16[144,2048]{1,0:T(8,128)(2,1)S(1)} %get-tuple-element.66.refs_7_), channel_id=1, source_target_pairs={{0,1},{1,0},{2,3},{3,2},{4,5},{5,4},{6,7},{7,6},{8,9},{9,8},{10,11... | collective-permute-start | bytes 1769480 | tf_op jit(solution)/shard_map/ppermute | solution.py:474
  56.2 2.8 %collective-permute-start.16 = (bf16[144,2048]{1,0:T(8,128)(2,1)S(1)}, bf16[144,2048]{1,0:T(8,128)(2,1)S(1)}, u32[]{:S(2)}, u32[]{:S(2)}) collective-permute-start(bf16[144,2048]{1,0:T(8,128)(2,1)S(1)} %get-tuple-element.68.refs_11_), channel_id=1, source_target_pairs={{0,1},{1,0},{2,3},{3,2},{4,5},{5,4},{6,7},{7,6},{8,9},{9,8},{10,11... | collective-permute-start | bytes 1769480 | tf_op jit(solution)/shard_map/ppermute | solution.py:474
  56.7 24.6 %collective-permute-start.18 = (bf16[144,4096]{1,0:T(8,128)(2,1)S(1)}, bf16[144,4096]{1,0:T(8,128)(2,1)S(1)}, u32[]{:S(2)}, u32[]{:S(2)}) collective-permute-start(bf16[144,4096]{1,0:T(8,128)(2,1)S(1)} %after.8.x_ref), channel_id=1, source_target_pairs={{0,4},{1,3},{4,8},{5,1},{8,12},{9,5},{12,14},{13,9},{14,10},{15,13... | collective-permute-start | bytes 3538952 | tf_op jit(solution)/shard_map/ppermute | solution.py:474
  70.5 2.7 %collective-permute-start.19 = (bf16[144,2048]{1,0:T(8,128)(2,1)S(1)}, bf16[144,2048]{1,0:T(8,128)(2,1)S(1)}, u32[]{:S(2)}, u32[]{:S(2)}) collective-permute-start(bf16[144,2048]{1,0:T(8,128)(2,1)S(1)} %get-tuple-element.74.refs_5_), channel_id=1, source_target_pairs={{0,1},{1,0},{2,3},{3,2},{4,5},{5,4},{6,7},{7,6},{8,9},{9,8},{10,11... | collective-permute-start | bytes 1769480 | tf_op jit(solution)/shard_map/ppermute | solution.py:474
  70.7 2.7 %collective-permute-start.20 = (bf16[144,2048]{1,0:T(8,128)(2,1)S(1)}, bf16[144,2048]{1,0:T(8,128)(2,1)S(1)}, u32[]{:S(2)}, u32[]{:S(2)}) collective-permute-start(bf16[144,2048]{1,0:T(8,128)(2,1)S(1)} %get-tuple-element.75.refs_7_), channel_id=1, source_target_pairs={{0,1},{1,0},{2,3},{3,2},{4,5},{5,4},{6,7},{7,6},{8,9},{9,8},{10,11... | collective-permute-start | bytes 1769480 | tf_op jit(solution)/shard_map/ppermute | solution.py:474
  71.0 22.9 %collective-permute-start.17 = (bf16[144,4096]{1,0:T(8,128)(2,1)S(1)}, bf16[144,4096]{1,0:T(8,128)(2,1)S(1)}, u32[]{:S(2)}, u32[]{:S(2)}) collective-permute-start(bf16[144,4096]{1,0:T(8,128)(2,1)S(1)} %after.9.x_ref), channel_id=1, source_target_pairs={{0,4},{1,3},{4,8},{5,1},{8,12},{9,5},{12,14},{13,9},{14,10},{15,13... | collective-permute-start | bytes 3538952 | tf_op jit(solution)/shard_map/ppermute | solution.py:474
  81.4 2.1 %collective-permute-start.21 = (bf16[144,2048]{1,0:T(8,128)(2,1)S(1)}, bf16[144,2048]{1,0:T(8,128)(2,1)S(1)}, u32[]{:S(2)}, u32[]{:S(2)}) collective-permute-start(bf16[144,2048]{1,0:T(8,128)(2,1)S(1)} %get-tuple-element.79.refs_5_), channel_id=1, source_target_pairs={{0,1},{1,0},{2,3},{3,2},{4,5},{5,4},{6,7},{7,6},{8,9},{9,8},{10,11... | collective-permute-start | bytes 1769480 | tf_op jit(solution)/shard_map/ppermute | solution.py:474
  81.5 2.8 %collective-permute-start.22 = (bf16[144,2048]{1,0:T(8,128)(2,1)S(1)}, bf16[144,2048]{1,0:T(8,128)(2,1)S(1)}, u32[]{:S(2)}, u32[]{:S(2)}) collective-permute-start(bf16[144,2048]{1,0:T(8,128)(2,1)S(1)} %get-tuple-element.80.refs_7_), channel_id=1, source_target_pairs={{0,1},{1,0},{2,3},{3,2},{4,5},{5,4},{6,7},{7,6},{8,9},{9,8},{10,11... | collective-permute-start | bytes 1769480 | tf_op jit(solution)/shard_map/ppermute | solution.py:474
  94.1 3.6 %collective-permute-start.24 = (bf16[144,2048]{1,0:T(8,128)(2,1)S(1)}, bf16[144,2048]{1,0:T(8,128)(2,1)S(1)}, u32[]{:S(2)}, u32[]{:S(2)}) collective-permute-start(bf16[144,2048]{1,0:T(8,128)(2,1)S(1)} %get-tuple-element.85.refs_5_.near_ref), channel_id=1, source_target_pairs={{0,1},{1,0},{2,3},{3,2},{4,5},{5,4},{6,7},{7,6},{8,9},{9,8},{10,11... | collective-permute-start | bytes 1769480 | tf_op jit(solution)/shard_map/ppermute | solution.py:474
  94.2 3.5 %collective-permute-start.23 = (bf16[144,2048]{1,0:T(8,128)(2,1)S(1)}, bf16[144,2048]{1,0:T(8,128)(2,1)S(1)}, u32[]{:S(2)}, u32[]{:S(2)}) collective-permute-start(bf16[144,2048]{1,0:T(8,128)(2,1)S(1)} %get-tuple-element.84.refs_4_), channel_id=1, source_target_pairs={{0,1},{1,0},{2,3},{3,2},{4,5},{5,4},{6,7},{7,6},{8,9},{9,8},{10,11... | collective-permute-start | bytes 1769480 | tf_op jit(solution)/shard_map/ppermute | solution.py:474
  97.7 6.7 %slice-start = ((s8[6291456]{0:T(1024)(128)(4,1)}), s8[4194304]{0:T(1024)(128)(4,1)S(1)}, s32[]{:S(2)}) async-start(s8[6291456]{0:T(1024)(128)(4,1)} %bitcast.1), calls=%async_computation | async-start | bytes 8388608
  97.7 6.7 %slice-start.1 = ((s8[6291456]{0:T(1024)(128)(4,1)}), s8[2097152]{0:T(1024)(128)(4,1)S(1)}, s32[]{:S(2)}) async-start(s8[6291456]{0:T(1024)(128)(4,1)} %bitcast.1), calls=%async_computation.1 | async-start | bytes 4194304
  100.6 5.1 %collective-permute-start.27 = (f32[8,128]{1,0:T(8,128)S(1)}, f32[8,128]{1,0:T(8,128)S(1)}, u32[]{:S(2)}, u32[]{:S(2)}) collective-permute-start(f32[8,128]{1,0:T(8,128)S(1)} %get-tuple-element.90), channel_id=1, source_target_pairs={{0,6},{1,7},{2,4},{3,5},{4,2},{5,3},{6,0},{7,1},{8,14},{9,15},{10,... | collective-permute-start | bytes 12296 | tf_op jit(solution)/shard_map/ppermute | solution.py:454
  103.7 3.6 %collective-permute-start.26 = (f32[8,128]{1,0:T(8,128)S(1)}, f32[8,128]{1,0:T(8,128)S(1)}, u32[]{:S(2)}, u32[]{:S(2)}) collective-permute-start(f32[8,128]{1,0:T(8,128)S(1)} %get-tuple-element.90), channel_id=1, source_target_pairs={{0,4},{1,5},{2,6},{3,7},{4,0},{5,1},{6,2},{7,3},{8,12},{9,13},{10,... | collective-permute-start | bytes 12296 | tf_op jit(solution)/shard_map/ppermute | solution.py:454
  104.2 3.6 %collective-permute-start.25 = (f32[8,128]{1,0:T(8,128)S(1)}, f32[8,128]{1,0:T(8,128)S(1)}, u32[]{:S(2)}, u32[]{:S(2)}) collective-permute-start(f32[8,128]{1,0:T(8,128)S(1)} %get-tuple-element.90), channel_id=1, source_target_pairs={{0,2},{1,3},{2,0},{3,1},{4,6},{5,7},{6,4},{7,5},{8,10},{9,11},{10,... | collective-permute-start | bytes 12296 | tf_op jit(solution)/shard_map/ppermute | solution.py:454
  107.8 4.1 %collective-permute-start.30 = (f32[8,128]{1,0:T(8,128)S(1)}, f32[8,128]{1,0:T(8,128)S(1)}, u32[]{:S(2)}, u32[]{:S(2)}) collective-permute-start(f32[8,128]{1,0:T(8,128)S(1)} %after.12), channel_id=1, source_target_pairs={{0,9},{1,8},{2,11},{3,10},{4,13},{5,12},{6,15},{7,14},{8,1},{9,0},... | collective-permute-start | bytes 12296 | tf_op jit(solution)/shard_map/ppermute | solution.py:454
  108.4 4.5 %collective-permute-start.29 = (f32[8,128]{1,0:T(8,128)S(1)}, f32[8,128]{1,0:T(8,128)S(1)}, u32[]{:S(2)}, u32[]{:S(2)}) collective-permute-start(f32[8,128]{1,0:T(8,128)S(1)} %after.12), channel_id=1, source_target_pairs={{0,8},{1,9},{2,10},{3,11},{4,12},{5,13},{6,14},{7,15},{8,0},{9,1},... | collective-permute-start | bytes 12296 | tf_op jit(solution)/shard_map/ppermute | solution.py:454
  110.5 2.4 %collective-permute-start.28 = (f32[8,128]{1,0:T(8,128)S(1)}, f32[8,128]{1,0:T(8,128)S(1)}, u32[]{:S(2)}, u32[]{:S(2)}) collective-permute-start(f32[8,128]{1,0:T(8,128)S(1)} %after.12), channel_id=1, source_target_pairs={{0,1},{1,0},{2,3},{3,2},{4,5},{5,4},{6,7},{7,6},{8,9},{9,8},{10,11... | collective-permute-start | bytes 12296 | tf_op jit(solution)/shard_map/ppermute | solution.py:454
  110.6 2.3 %copy-start.2 = (s32[16,16]{1,0:T(8,128)S(1)}, s32[16,16]{1,0:T(8,128)}, u32[]{:S(2)}) copy-start(s32[16,16]{1,0:T(8,128)} %constant.6.clone.table_ref.refs_0_) | copy-start | bytes 3076

commit v14 on v11

--- a/solution.py
+++ b/solution.py
@@ -340,7 +340,7 @@
 def scaled(w, squares):
     capacity, features = w.shape
     vmem = pl.BlockSpec(memory_space=pltpu.VMEM)
-    parts = 8
+    parts = capacity // 48
     return pl.pallas_call(
         functools.partial(scale_kernel, parts),
         in_specs=[vmem, vmem],
@@ -461,10 +461,9 @@
         far_x = swapped(near_x)
         i = 2 * k - 1
         if k == last - 1:
-            held = held + [near_x, far_x]
             w, out, done = phase(
-                where, shapes, 2 * (i + 1) - len(held), grouped(*held), at=ats[i], w=w,
-                w_from=len(held) - 2, weight=weight, attn="whole", out=out,
+                where, shapes, 2 * i, grouped(near_x, far_x), at=ats[i], w=w,
+                weight=weight, attn="whole", out=out,
             )
         y = arrived(done, counts[1], y) if k == 1 else after(done, y)[0]
         y, near_y = send(y, ring.along()) if k < last - 1 else None, split(y)
@@ -475,9 +474,6 @@
                 where, shapes, 2 * (i + 1), grouped(near_y, far_y), at=ats[i + 1], w=w,
                 weight=weight, attn="whole", out=out,
             )
-        elif k == last - 2:
-            held = [near_x, far_x, near_y, far_y]
-            w, done = phase(where, shapes, 2 * i, groups, at=ats[i], w=w)
         else:
             w, out, done = phase(
                 where, shapes, 2 * i, groups, at=ats[i], w=w,

time: 117 us -> 117 us (level)
  transfers between devices with their start and end apart: 31 -> 31, of which waited for: 14 -> 16; matrix products, arithmetic and copies ran while one was open for 0% -> 0% of each run, Pallas kernels for 50% -> 51%
where the time goes in v14:
time: 117 us
  Pallas kernels  65.1 us (56%)
  starting transfers between devices  28.8 us (25%)
  waiting for transfers between devices  16.9 us (14%)
  local copies, waits for them, and re-layouts  3.49 us (3%)
  between operations  2.39 us (2%)
    pallas_call x9, Pallas kernels, phase(): pl.pallas_call(functools.partial(phase_kernel, spec), in_specs=specs, out...  56.1 us
    ppermute x25, starting transfers between devices, send(): return lax.ppermute(x, 'dp', pairs)  22.3 us
    ppermute x25, waiting for transfers between devices, send(): return lax.ppermute(x, 'dp', pairs)  16.1 us
    ppermute x6, starting transfers between devices, exchange(): lax.ppermute(x, 'dp', [(d, d ^ mask) for d in range(devices)])  6.5 us
    pallas_call x1, Pallas kernels, prepared(): pl.pallas_call(functools.partial(prep_kernel, spans, rows), in_specs=[sme...  3.96 us
    unnamed x8, local copies, waits for them, and re-layouts  3.49 us
    pallas_call x1, Pallas kernels, scaled(): pl.pallas_call(functools.partial(scale_kernel, parts), in_specs=[vmem, vm...  2.96 us
  transfers between devices with their start and end apart: 31, of which 16 were waited for; matrix products, arithmetic and copies ran while one was open for 0% of the time, Pallas kernels for 51%

profile of v14, /device:TPU:0, one launch (start us, length us, event | category | flops | bytes accessed | tf_op | source)
XLA Modules:
  0.0 116.6 jit_solution(17631893921853127798)
XLA Ops:
  0.6 3.1 %collective-permute-start.1 = (bf16[144,4096]{1,0:T(8,128)(2,1)}, bf16[144,4096]{1,0:T(8,128)(2,1)S(1)}, u32[]{:S(2)}, u32[]{:S(2)}) collective-permute-start(bf16[144,4096]{1,0:T(8,128)(2,1)} %grad_ref.1), channel_id=1, source_target_pairs={{0,4},{1,3},{4,8},{5,1},{8,12},{9,5},{12,14},{13,9},{14,10},{15,13... | collective-permute-start | bytes 3538952 | tf_op jit(solution)/shard_map/ppermute | solution.py:436
  5.0 0.7 copy-done.1
  5.7 4.0 %prep.1 = (bf16[144,4096]{1,0:T(8,128)(2,1)S(1)}, bf16[144,2048]{1,0:T(8,128)(2,1)S(1)}, bf16[144,2048]{1,0:T(8,128)(2,1)S(1)}, s32[8,128]{1,0:T(8,128)S(1)}, bf...) custom-call(s32[16,16]{1,0:T(8,128)S(1)} %copy-done.1, ...), custom_call_target="tpu_custom_call" | custom-call | flops 1 | bytes 1 | tf_op jit(solution)/shard_map/prep/pallas_call | solution.py:121
  9.7 0.1 collective-permute-start.2
  9.8 0.5 collective-permute-start.3
  10.2 0.7 collective-permute-start.7
  10.9 1.0 collective-permute-start
  12.0 0.6 collective-permute-done.3.refs_8_
  12.6 2.8 %copy-done = bf16[768,4096]{1,0:T(8,128)(2,1)S(1)} copy-done((bf16[768,4096]{1,0:T(8,128)(2,1)S(1)}, bf16[768,4096]{1,0:T(8,128)(2,1)}, u32[]{:S(2)}) %copy-start) | copy-done | bytes 6291480
  15.4 7.2 %phase_w_whole.5 = (f32[768,4096]{1,0:T(8,128)S(1)}, bf16[2304,768]{1,0:T(8,128)(2,1)}, f32[8,128]{1,0:T(8,128)S(1)}) custom-call(s32[16,16]{1,0:T(8,128)S(1)} %copy-done.1, s32[1]{0:T(128)} %bitcast.me_ref.refs_1_, s32[1]{0:T(128)S(6)} %copy.46.heads_ref.refs_2_, bf16[768,288]{1,0:T(8,128)(2,1)S(1)} %get-tuple-element.49.refs_3_, ...), custom_call_target="tpu_custom_call" | custom-call | flops 1 | bytes 1 | tf_op jit(solution)/shard_map/phase_w_whole/pallas_call | solution.py:304
  22.6 0.4 collective-permute-done.count_ref
  23.0 0.7 arrived.2.x_ref
  23.6 0.1 split.7
  23.8 2.5 %collective-permute-start.4 = (bf16[144,4096]{1,0:T(8,128)(2,1)S(1)}, bf16[144,4096]{1,0:T(8,128)(2,1)S(1)}, u32[]{:S(2)}, u32[]{:S(2)}) collective-permute-start(bf16[144,4096]{1,0:T(8,128)(2,1)S(1)} %arrived.2.x_ref), channel_id=1, source_target_pairs={{0,4},{1,3},{4,8},{5,1},{8,12},{9,5},{12,14},{13,9},{14,10},{15,13... | collective-permute-start | bytes 3538952 | tf_op jit(solution)/shard_map/ppermute | solution.py:436
  26.4 2.2 %collective-permute-start.6 = (s32[8,128]{1,0:T(8,128)S(1)}, s32[8,128]{1,0:T(8,128)S(1)}, u32[]{:S(2)}, u32[]{:S(2)}) collective-permute-start(s32[8,128]{1,0:T(8,128)S(1)} %get-tuple-element.48), channel_id=1, source_target_pairs={{0,3},{1,4},{4,1},{5,8},{8,5},{9,12},{12,9},{13,14},{14,13},{15,10... | collective-permute-start | bytes 12296 | tf_op jit(solution)/shard_map/ppermute | solution.py:436
  28.5 4.2 %collective-permute-done.6.count_ref = s32[8,128]{1,0:T(8,128)S(1)} collective-permute-done((s32[8,128]{1,0:T(8,128)S(1)}, s32[8,128]{1,0:T(8,128)S(1)}, u32[]{:S(2)}, u32[]{:S(2)}) %collective-permute-start.6) | collective-permute-done | bytes 4128 | tf_op jit(solution)/shard_map/ppermute | solution.py:436
  32.8 0.7 arrived.3.x_ref
  33.4 0.1 split.8
  33.5 3.0 %collective-permute-start.13 = (bf16[144,4096]{1,0:T(8,128)(2,1)S(1)}, bf16[144,4096]{1,0:T(8,128)(2,1)S(1)}, u32[]{:S(2)}, u32[]{:S(2)}) collective-permute-start(bf16[144,4096]{1,0:T(8,128)(2,1)S(1)} %arrived.3.x_ref), channel_id=1, source_target_pairs={{0,4},{1,3},{4,8},{5,1},{8,12},{9,5},{12,14},{13,9},{14,10},{15,13... | collective-permute-start | bytes 3538952 | tf_op jit(solution)/shard_map/ppermute | solution.py:436
  36.5 0.5 collective-permute-start.8
  37.0 1.5 %collective-permute-done.9.refs_10_ = bf16[144,2048]{1,0:T(8,128)(2,1)S(1)} collective-permute-done((bf16[144,2048]{1,0:T(8,128)(2,1)S(1)}, bf16[144,2048]{1,0:T(8,128)(2,1)S(1)}, u32[]{:S(2)}, u32[]{:S(2)}) %collective-permute-start.9) | collective-permute-done | bytes 589856 | tf_op jit(solution)/shard_map/ppermute | solution.py:436
  38.5 0.8 collective-permute-done.8.refs_8_
  39.4 0.8 collective-permute-done.10.refs_12_
  40.2 11.3 %phase_w_whole.6 = (f32[768,4096]{1,0:T(8,128)S(1)}, bf16[2304,768]{1,0:T(8,128)(2,1)}, f32[8,128]{1,0:T(8,128)S(1)}) custom-call(s32[16,16]{1,0:T(8,128)S(1)} %copy-done.1, s32[1]{0:T(128)} %bitcast.me_ref.refs_1_, s32[1]{0:T(128)S(6)} %copy.46.heads_ref.refs_2_, ...), custom_call_target="tpu_custom_call", output_to_operand_aliasing={{0}: (13, {}), {1}: (14, {})} | custom-call | flops 1 | bytes 1 | tf_op jit(solution)/shard_map/phase_w_whole/pallas_call | solution.py:304
  51.5 1.6 %collective-permute-start.11 = (bf16[144,4096]{1,0:T(8,128)(2,1)S(1)}, bf16[144,4096]{1,0:T(8,128)(2,1)S(1)}, u32[]{:S(2)}, u32[]{:S(2)}) collective-permute-start(bf16[144,4096]{1,0:T(8,128)(2,1)S(1)} %after.6.x_ref), channel_id=1, source_target_pairs={{0,4},{1,3},{4,8},{5,1},{8,12},{9,5},{12,14},{13,9},{14,10},{15,13... | collective-permute-start | bytes 3538952 | tf_op jit(solution)/shard_map/ppermute | solution.py:436
  53.1 0.1 split.9
  53.3 0.5 collective-permute-start.15
  53.8 2.2 %collective-permute-done.13.refs_0_ = bf16[144,4096]{1,0:T(8,128)(2,1)S(1)} collective-permute-done((bf16[144,4096]{1,0:T(8,128)(2,1)S(1)}, bf16[144,4096]{1,0:T(8,128)(2,1)S(1)}, u32[]{:S(2)}, u32[]{:S(2)}) %collective-permute-start.13) | collective-permute-done | bytes 1179680 | tf_op jit(solution)/shard_map/ppermute | solution.py:436
  56.1 0.1 split.10
  56.2 0.5 collective-permute-start.16
  56.7 2.1 %collective-permute-start.18 = (bf16[144,4096]{1,0:T(8,128)(2,1)S(1)}, bf16[144,4096]{1,0:T(8,128)(2,1)S(1)}, u32[]{:S(2)}, u32[]{:S(2)}) collective-permute-start(bf16[144,4096]{1,0:T(8,128)(2,1)S(1)} %after.7.x_ref), channel_id=1, source_target_pairs={{0,4},{1,3},{4,8},{5,1},{8,12},{9,5},{12,14},{13,9},{14,10},{15,13... | collective-permute-start | bytes 3538952 | tf_op jit(solution)/shard_map/ppermute | solution.py:436
  58.8 0.2 collective-permute-done.16.refs_12_
  59.1 11.3 %phase_w_whole.7 = (f32[768,4096]{1,0:T(8,128)S(1)}, bf16[2304,768]{1,0:T(8,128)(2,1)}, f32[8,128]{1,0:T(8,128)S(1)}) custom-call(s32[16,16]{1,0:T(8,128)S(1)} %copy-done.1, s32[1]{0:T(128)} %bitcast.me_ref.refs_1_, s32[1]{0:T(128)S(6)} %copy.46.heads_ref.refs_2_, ...), custom_call_target="tpu_custom_call", output_to_operand_aliasing={{0}: (13, {}), {1}: (14, {})} | custom-call | flops 1 | bytes 1 | tf_op jit(solution)/shard_map/phase_w_whole/pallas_call | solution.py:304
  70.4 0.1 split.11
  70.5 0.2 collective-permute-start.19
  70.7 0.4 collective-permute-start.20
  71.0 2.1 %collective-permute-start.17 = (bf16[144,4096]{1,0:T(8,128)(2,1)S(1)}, bf16[144,4096]{1,0:T(8,128)(2,1)S(1)}, u32[]{:S(2)}, u32[]{:S(2)}) collective-permute-start(bf16[144,4096]{1,0:T(8,128)(2,1)S(1)} %after.8.x_ref), channel_id=1, source_target_pairs={{0,4},{1,3},{4,8},{5,1},{8,12},{9,5},{12,14},{13,9},{14,10},{15,13... | collective-permute-start | bytes 3538952 | tf_op jit(solution)/shard_map/ppermute | solution.py:436
  73.1 0.3 collective-permute-done.20.refs_8_
  73.4 7.5 %phase_w_whole.8 = (f32[768,4096]{1,0:T(8,128)S(1)}, bf16[2304,768]{1,0:T(8,128)(2,1)}, f32[8,128]{1,0:T(8,128)S(1)}) custom-call(s32[16,16]{1,0:T(8,128)S(1)} %copy-done.1, s32[1]{0:T(128)} %bitcast.me_ref.refs_1_, s32[1]{0:T(128)S(6)} %copy.46.heads_ref.refs_2_, ...), custom_call_target="tpu_custom_call", output_to_operand_aliasing={{0}: (9, {}), {1}: (10, {})} | custom-call | flops 1 | bytes 1 | tf_op jit(solution)/shard_map/phase_w_whole/pallas_call | solution.py:304
  80.9 0.5 collective-permute-done.18.refs_0_
  81.3 0.1 split.12
  81.4 0.1 collective-permute-start.21
  81.5 0.5 collective-permute-start.22
  82.0 1.5 %collective-permute-done.21.refs_6_ = bf16[144,2048]{1,0:T(8,128)(2,1)S(1)} collective-permute-done((bf16[144,2048]{1,0:T(8,128)(2,1)S(1)}, bf16[144,2048]{1,0:T(8,128)(2,1)S(1)}, u32[]{:S(2)}, u32[]{:S(2)}) %collective-permute-start.21) | collective-permute-done | bytes 589856 | tf_op jit(solution)/shard_map/ppermute | solution.py:436
  83.5 0.8 collective-permute-done.22.refs_8_
  84.4 7.5 %phase_w_whole.9 = (f32[768,4096]{1,0:T(8,128)S(1)}, bf16[2304,768]{1,0:T(8,128)(2,1)}, f32[8,128]{1,0:T(8,128)S(1)}) custom-call(s32[16,16]{1,0:T(8,128)S(1)} %copy-done.1, s32[1]{0:T(128)} %bitcast.me_ref.refs_1_, s32[1]{0:T(128)S(6)} %copy.46.heads_ref.refs_2_, ...), custom_call_target="tpu_custom_call", output_to_operand_aliasing={{0}: (9, {}), {1}: (10, {})} | custom-call | flops 1 | bytes 1 | tf_op jit(solution)/shard_map/phase_w_whole/pallas_call | solution.py:304
  91.8 2.1 %collective-permute-done.17.refs_0_ = bf16[144,4096]{1,0:T(8,128)(2,1)S(1)} collective-permute-done((bf16[144,4096]{1,0:T(8,128)(2,1)S(1)}, bf16[144,4096]{1,0:T(8,128)(2,1)S(1)}, u32[]{:S(2)}, u32[]{:S(2)}) %collective-permute-start.17) | collective-permute-done | bytes 1179680 | tf_op jit(solution)/shard_map/ppermute | solution.py:436
  94.0 0.1 split.13
  94.1 0.1 collective-permute-start.24
  94.2 0.5 collective-permute-start.23
  94.7 3.0 %phase_w_None.2 = (f32[768,4096]{1,0:T(8,128)S(1)}, f32[8,128]{1,0:T(8,128)}) custom-call(s32[16,16]{1,0:T(8,128)S(1)} %copy-done.1, s32[1]{0:T(128)} %bitcast.me_ref.refs_1_, s32[1]{0:T(128)S(6)} %copy.46.heads_ref.refs_2_, bf16[768,144]{1,0:T(8,128)(2,1)S(1)} %get-tuple-element.88.refs_3_, ...), custom_call_target="tpu_custom_call", output_to_operand_aliasing={{0}: (6, {})} | custom-call | flops 1 | bytes 1 | tf_op jit(solution)/shard_map/phase_w_None/pallas_call | solution.py:304
  97.7 3.0 %phase_w_None.3 = (f32[768,4096]{1,0:T(8,128)S(1)}, f32[8,128]{1,0:T(8,128)S(1)}) custom-call(s32[16,16]{1,0:T(8,128)S(1)} %copy-done.1, s32[1]{0:T(128)} %bitcast.me_ref.refs_1_, s32[1]{0:T(128)S(6)} %copy.46.heads_ref.refs_2_, bf16[768,144]{1,0:T(8,128)(2,1)S(1)} %get-tuple-element.87.refs_3_, ...), custom_call_target="tpu_custom_call", output_to_operand_aliasing={{0}: (6, {})} | custom-call | flops 1 | bytes 1 | tf_op jit(solution)/shard_map/phase_w_None/pallas_call | solution.py:304
  100.7 3.1 %collective-permute-start.27 = (f32[8,128]{1,0:T(8,128)S(1)}, f32[8,128]{1,0:T(8,128)S(1)}, u32[]{:S(2)}, u32[]{:S(2)}) collective-permute-start(f32[8,128]{1,0:T(8,128)S(1)} %get-tuple-element.92), channel_id=1, source_target_pairs={{0,6},{1,7},{2,4},{3,5},{4,2},{5,3},{6,0},{7,1},{8,14},{9,15},{10,... | collective-permute-start | bytes 12296 | tf_op jit(solution)/shard_map/ppermute | solution.py:416
  103.8 0.4 collective-permute-start.26
  104.2 0.2 collective-permute-start.25
  104.4 2.7 %phase__first.1 = (f32[288,768]{1,0:T(8,128)S(1)}, f32[8,128]{1,0:T(8,128)S(1)}) custom-call(s32[16,16]{1,0:T(8,128)S(1)} %copy-done.1, s32[1]{0:T(128)} %bitcast.me_ref.refs_1_, s32[1]{0:T(128)S(6)} %copy.46.heads_ref.refs_2_, bf16[768,4096]{1,0:T(8,128)(2,1)S(1)} %bitcast.2, bf16[144,2048]{1,0:T(8,128)(2,1)S(1)} %get-tuple-element.83.refs_4_, ...), custom_call_target="tpu_custom_call" | custom-call | flops 1 | bytes 1 | tf_op jit(solution)/shard_map/phase__first/pallas_call | solution.py:304
  107.2 0.2 collective-permute-done.26
  107.4 0.4 collective-permute-done.25
  107.9 1.2 collective-permute-start.30
  109.0 1.5 %collective-permute-start.29 = (f32[8,128]{1,0:T(8,128)S(1)}, f32[8,128]{1,0:T(8,128)S(1)}, u32[]{:S(2)}, u32[]{:S(2)}) collective-permute-start(f32[8,128]{1,0:T(8,128)S(1)} %after.11), channel_id=1, source_target_pairs={{0,8},{1,9},{2,10},{3,11},{4,12},{5,13},{6,14},{7,15},{8,0},{9,1},... | collective-permute-start | bytes 12296 | tf_op jit(solution)/shard_map/ppermute | solution.py:416
  110.5 0.1 collective-permute-start.28
  110.6 2.7 %phase__last.1 = (bf16[2304,768]{1,0:T(8,128)(2,1)}, f32[8,128]{1,0:T(8,128)}) custom-call(s32[16,16]{1,0:T(8,128)S(1)} %copy-done.1, s32[1]{0:T(128)} %bitcast.me_ref.refs_1_, s32[1]{0:T(128)S(6)} %copy.46.heads_ref.refs_2_, bf16[768,4096]{1,0:T(8,128)(2,1)S(1)} %bitcast.2, ...), custom_call_target="tpu_custom_call", output_to_operand_aliasing={{0}: (7, {})} | custom-call | flops 1 | bytes 1 | tf_op jit(solution)/shard_map/phase__last/pallas_call | solution.py:304
  113.3 0.2 collective-permute-done.29
  113.5 3.0 %scale.1 = bf16[768,4096]{1,0:T(8,128)(2,1)} custom-call(f32[768,4096]{1,0:T(8,128)S(1)} %get-tuple-element.91.w_ref, f32[8,128]{1,0:T(8,128)S(1)} %add_add_fusion.squares_ref), custom_call_target="tpu_custom_call" | custom-call | flops 3145728 | bytes 6291456 | tf_op jit(solution)/shard_map/scale/pallas_call | solution.py:344
  (35 shorter events, 0.3 us)
Async XLA Ops:
  0.6 22.4 %collective-permute-start.1 = (bf16[144,4096]{1,0:T(8,128)(2,1)}, bf16[144,4096]{1,0:T(8,128)(2,1)S(1)}, u32[]{:S(2)}, u32[]{:S(2)}) collective-permute-start(bf16[144,4096]{1,0:T(8,128)(2,1)} %grad_ref.1), channel_id=1, source_target_pairs={{0,4},{1,3},{4,8},{5,1},{8,12},{9,5},{12,14},{13,9},{14,10},{15,13... | collective-permute-start | bytes 3538952 | tf_op jit(solution)/shard_map/ppermute | solution.py:436
  5.0 0.7 copy-start.1
  9.7 2.3 %collective-permute-start.2 = (bf16[144,2048]{1,0:T(8,128)(2,1)S(1)}, bf16[144,2048]{1,0:T(8,128)(2,1)S(1)}, u32[]{:S(2)}, u32[]{:S(2)}) collective-permute-start(bf16[144,2048]{1,0:T(8,128)(2,1)S(1)} %get-tuple-element.50.refs_5_), channel_id=1, source_target_pairs={{0,1},{1,0},{2,3},{3,2},{4,5},{5,4},{6,7},{7,6},{8,9},{9,8},{10,11... | collective-permute-start | bytes 1769480 | tf_op jit(solution)/shard_map/ppermute | solution.py:436
  9.8 2.8 %collective-permute-start.3 = (bf16[144,2048]{1,0:T(8,128)(2,1)S(1)}, bf16[144,2048]{1,0:T(8,128)(2,1)S(1)}, u32[]{:S(2)}, u32[]{:S(2)}) collective-permute-start(bf16[144,2048]{1,0:T(8,128)(2,1)S(1)} %get-tuple-element.51.refs_7_), channel_id=1, source_target_pairs={{0,1},{1,0},{2,3},{3,2},{4,5},{5,4},{6,7},{7,6},{8,9},{9,8},{10,11... | collective-permute-start | bytes 1769480 | tf_op jit(solution)/shard_map/ppermute | solution.py:436
  10.2 22.5 %collective-permute-start.7 = (bf16[144,4096]{1,0:T(8,128)(2,1)S(1)}, bf16[144,4096]{1,0:T(8,128)(2,1)S(1)}, u32[]{:S(2)}, u32[]{:S(2)}) collective-permute-start(bf16[144,4096]{1,0:T(8,128)(2,1)S(1)} %get-tuple-element.55), channel_id=1, source_target_pairs={{0,3},{1,4},{4,1},{5,8},{8,5},{9,12},{12,9},{13,14},{14,13},{15,10... | collective-permute-start | bytes 3538952 | tf_op jit(solution)/shard_map/ppermute | solution.py:436
  10.9 12.1 %collective-permute-start = (s32[8,128]{1,0:T(8,128)S(1)}, s32[8,128]{1,0:T(8,128)S(1)}, u32[]{:S(2)}, u32[]{:S(2)}) collective-permute-start(s32[8,128]{1,0:T(8,128)S(1)} %get-tuple-element.48), channel_id=1, source_target_pairs={{0,4},{1,3},{4,8},{5,1},{8,12},{9,5},{12,14},{13,9},{14,10},{15,13... | collective-permute-start | bytes 12296 | tf_op jit(solution)/shard_map/ppermute | solution.py:436
  12.6 2.8 %copy-start = (bf16[768,4096]{1,0:T(8,128)(2,1)S(1)}, bf16[768,4096]{1,0:T(8,128)(2,1)}, u32[]{:S(2)}) copy-start(bf16[768,4096]{1,0:T(8,128)(2,1)} %refs_3_.3) | copy-start | bytes 18874372
  23.8 13.3 %collective-permute-start.5 = (bf16[144,2048]{1,0:T(8,128)(2,1)S(1)}, bf16[144,2048]{1,0:T(8,128)(2,1)S(1)}, u32[]{:S(2)}, u32[]{:S(2)}) collective-permute-start(bf16[144,2048]{1,0:T(8,128)(2,1)S(1)} %get-tuple-element.54.refs_5_), channel_id=1, source_target_pairs={{0,1},{1,0},{2,3},{3,2},{4,5},{5,4},{6,7},{7,6},{8,9},{9,8},{10,11... | collective-permute-start | bytes 1769480 | tf_op jit(solution)/shard_map/ppermute | solution.py:436
  23.8 27.7 %collective-permute-start.4 = (bf16[144,4096]{1,0:T(8,128)(2,1)S(1)}, bf16[144,4096]{1,0:T(8,128)(2,1)S(1)}, u32[]{:S(2)}, u32[]{:S(2)}) collective-permute-start(bf16[144,4096]{1,0:T(8,128)(2,1)S(1)} %arrived.2.x_ref), channel_id=1, source_target_pairs={{0,4},{1,3},{4,8},{5,1},{8,12},{9,5},{12,14},{13,9},{14,10},{15,13... | collective-permute-start | bytes 3538952 | tf_op jit(solution)/shard_map/ppermute | solution.py:436
  26.4 6.4 %collective-permute-start.6 = (s32[8,128]{1,0:T(8,128)S(1)}, s32[8,128]{1,0:T(8,128)S(1)}, u32[]{:S(2)}, u32[]{:S(2)}) collective-permute-start(s32[8,128]{1,0:T(8,128)S(1)} %get-tuple-element.48), channel_id=1, source_target_pairs={{0,3},{1,4},{4,1},{5,8},{8,5},{9,12},{12,9},{13,14},{14,13},{15,10... | collective-permute-start | bytes 12296 | tf_op jit(solution)/shard_map/ppermute | solution.py:436
  33.5 22.5 %collective-permute-start.13 = (bf16[144,4096]{1,0:T(8,128)(2,1)S(1)}, bf16[144,4096]{1,0:T(8,128)(2,1)S(1)}, u32[]{:S(2)}, u32[]{:S(2)}) collective-permute-start(bf16[144,4096]{1,0:T(8,128)(2,1)S(1)} %arrived.3.x_ref), channel_id=1, source_target_pairs={{0,4},{1,3},{4,8},{5,1},{8,12},{9,5},{12,14},{13,9},{14,10},{15,13... | collective-permute-start | bytes 3538952 | tf_op jit(solution)/shard_map/ppermute | solution.py:436
  36.5 2.0 %collective-permute-start.9 = (bf16[144,2048]{1,0:T(8,128)(2,1)S(1)}, bf16[144,2048]{1,0:T(8,128)(2,1)S(1)}, u32[]{:S(2)}, u32[]{:S(2)}) collective-permute-start(bf16[144,2048]{1,0:T(8,128)(2,1)S(1)} %get-tuple-element.57.refs_9_), channel_id=1, source_target_pairs={{0,1},{1,0},{2,3},{3,2},{4,5},{5,4},{6,7},{7,6},{8,9},{9,8},{10,11... | collective-permute-start | bytes 1769480 | tf_op jit(solution)/shard_map/ppermute | solution.py:436
  36.5 2.8 %collective-permute-start.8 = (bf16[144,2048]{1,0:T(8,128)(2,1)S(1)}, bf16[144,2048]{1,0:T(8,128)(2,1)S(1)}, u32[]{:S(2)}, u32[]{:S(2)}) collective-permute-start(bf16[144,2048]{1,0:T(8,128)(2,1)S(1)} %get-tuple-element.56.refs_7_), channel_id=1, source_target_pairs={{0,1},{1,0},{2,3},{3,2},{4,5},{5,4},{6,7},{7,6},{8,9},{9,8},{10,11... | collective-permute-start | bytes 1769480 | tf_op jit(solution)/shard_map/ppermute | solution.py:436
  37.0 3.2 %collective-permute-start.10 = (bf16[144,2048]{1,0:T(8,128)(2,1)S(1)}, bf16[144,2048]{1,0:T(8,128)(2,1)S(1)}, u32[]{:S(2)}, u32[]{:S(2)}) collective-permute-start(bf16[144,2048]{1,0:T(8,128)(2,1)S(1)} %get-tuple-element.58.refs_11_), channel_id=1, source_target_pairs={{0,1},{1,0},{2,3},{3,2},{4,5},{5,4},{6,7},{7,6},{8,9},{9,8},{10,11... | collective-permute-start | bytes 1769480 | tf_op jit(solution)/shard_map/ppermute | solution.py:436
  51.5 18.8 %collective-permute-start.11 = (bf16[144,4096]{1,0:T(8,128)(2,1)S(1)}, bf16[144,4096]{1,0:T(8,128)(2,1)S(1)}, u32[]{:S(2)}, u32[]{:S(2)}) collective-permute-start(bf16[144,4096]{1,0:T(8,128)(2,1)S(1)} %after.6.x_ref), channel_id=1, source_target_pairs={{0,4},{1,3},{4,8},{5,1},{8,12},{9,5},{12,14},{13,9},{14,10},{15,13... | collective-permute-start | bytes 3538952 | tf_op jit(solution)/shard_map/ppermute | solution.py:436
  53.2 3.5 %collective-permute-start.12 = (bf16[144,2048]{1,0:T(8,128)(2,1)S(1)}, bf16[144,2048]{1,0:T(8,128)(2,1)S(1)}, u32[]{:S(2)}, u32[]{:S(2)}) collective-permute-start(bf16[144,2048]{1,0:T(8,128)(2,1)S(1)} %get-tuple-element.63.refs_5_), channel_id=1, source_target_pairs={{0,1},{1,0},{2,3},{3,2},{4,5},{5,4},{6,7},{7,6},{8,9},{9,8},{10,11... | collective-permute-start | bytes 1769480 | tf_op jit(solution)/shard_map/ppermute | solution.py:436
  53.3 5.5 %collective-permute-start.15 = (bf16[144,2048]{1,0:T(8,128)(2,1)S(1)}, bf16[144,2048]{1,0:T(8,128)(2,1)S(1)}, u32[]{:S(2)}, u32[]{:S(2)}) collective-permute-start(bf16[144,2048]{1,0:T(8,128)(2,1)S(1)} %get-tuple-element.65.refs_9_), channel_id=1, source_target_pairs={{0,1},{1,0},{2,3},{3,2},{4,5},{5,4},{6,7},{7,6},{8,9},{9,8},{10,11... | collective-permute-start | bytes 1769480 | tf_op jit(solution)/shard_map/ppermute | solution.py:436
  56.2 2.7 %collective-permute-start.14 = (bf16[144,2048]{1,0:T(8,128)(2,1)S(1)}, bf16[144,2048]{1,0:T(8,128)(2,1)S(1)}, u32[]{:S(2)}, u32[]{:S(2)}) collective-permute-start(bf16[144,2048]{1,0:T(8,128)(2,1)S(1)} %get-tuple-element.64.refs_7_), channel_id=1, source_target_pairs={{0,1},{1,0},{2,3},{3,2},{4,5},{5,4},{6,7},{7,6},{8,9},{9,8},{10,11... | collective-permute-start | bytes 1769480 | tf_op jit(solution)/shard_map/ppermute | solution.py:436
  56.2 2.8 %collective-permute-start.16 = (bf16[144,2048]{1,0:T(8,128)(2,1)S(1)}, bf16[144,2048]{1,0:T(8,128)(2,1)S(1)}, u32[]{:S(2)}, u32[]{:S(2)}) collective-permute-start(bf16[144,2048]{1,0:T(8,128)(2,1)S(1)} %get-tuple-element.66.refs_11_), channel_id=1, source_target_pairs={{0,1},{1,0},{2,3},{3,2},{4,5},{5,4},{6,7},{7,6},{8,9},{9,8},{10,11... | collective-permute-start | bytes 1769480 | tf_op jit(solution)/shard_map/ppermute | solution.py:436
  56.7 24.6 %collective-permute-start.18 = (bf16[144,4096]{1,0:T(8,128)(2,1)S(1)}, bf16[144,4096]{1,0:T(8,128)(2,1)S(1)}, u32[]{:S(2)}, u32[]{:S(2)}) collective-permute-start(bf16[144,4096]{1,0:T(8,128)(2,1)S(1)} %after.7.x_ref), channel_id=1, source_target_pairs={{0,4},{1,3},{4,8},{5,1},{8,12},{9,5},{12,14},{13,9},{14,10},{15,13... | collective-permute-start | bytes 3538952 | tf_op jit(solution)/shard_map/ppermute | solution.py:436
  70.5 2.7 %collective-permute-start.19 = (bf16[144,2048]{1,0:T(8,128)(2,1)S(1)}, bf16[144,2048]{1,0:T(8,128)(2,1)S(1)}, u32[]{:S(2)}, u32[]{:S(2)}) collective-permute-start(bf16[144,2048]{1,0:T(8,128)(2,1)S(1)} %get-tuple-element.72.refs_5_), channel_id=1, source_target_pairs={{0,1},{1,0},{2,3},{3,2},{4,5},{5,4},{6,7},{7,6},{8,9},{9,8},{10,11... | collective-permute-start | bytes 1769480 | tf_op jit(solution)/shard_map/ppermute | solution.py:436
  70.7 2.7 %collective-permute-start.20 = (bf16[144,2048]{1,0:T(8,128)(2,1)S(1)}, bf16[144,2048]{1,0:T(8,128)(2,1)S(1)}, u32[]{:S(2)}, u32[]{:S(2)}) collective-permute-start(bf16[144,2048]{1,0:T(8,128)(2,1)S(1)} %get-tuple-element.73.refs_7_), channel_id=1, source_target_pairs={{0,1},{1,0},{2,3},{3,2},{4,5},{5,4},{6,7},{7,6},{8,9},{9,8},{10,11... | collective-permute-start | bytes 1769480 | tf_op jit(solution)/shard_map/ppermute | solution.py:436
  71.0 22.9 %collective-permute-start.17 = (bf16[144,4096]{1,0:T(8,128)(2,1)S(1)}, bf16[144,4096]{1,0:T(8,128)(2,1)S(1)}, u32[]{:S(2)}, u32[]{:S(2)}) collective-permute-start(bf16[144,4096]{1,0:T(8,128)(2,1)S(1)} %after.8.x_ref), channel_id=1, source_target_pairs={{0,4},{1,3},{4,8},{5,1},{8,12},{9,5},{12,14},{13,9},{14,10},{15,13... | collective-permute-start | bytes 3538952 | tf_op jit(solution)/shard_map/ppermute | solution.py:436
  81.4 2.1 %collective-permute-start.21 = (bf16[144,2048]{1,0:T(8,128)(2,1)S(1)}, bf16[144,2048]{1,0:T(8,128)(2,1)S(1)}, u32[]{:S(2)}, u32[]{:S(2)}) collective-permute-start(bf16[144,2048]{1,0:T(8,128)(2,1)S(1)} %get-tuple-element.77.refs_5_), channel_id=1, source_target_pairs={{0,1},{1,0},{2,3},{3,2},{4,5},{5,4},{6,7},{7,6},{8,9},{9,8},{10,11... | collective-permute-start | bytes 1769480 | tf_op jit(solution)/shard_map/ppermute | solution.py:436
  81.5 2.8 %collective-permute-start.22 = (bf16[144,2048]{1,0:T(8,128)(2,1)S(1)}, bf16[144,2048]{1,0:T(8,128)(2,1)S(1)}, u32[]{:S(2)}, u32[]{:S(2)}) collective-permute-start(bf16[144,2048]{1,0:T(8,128)(2,1)S(1)} %get-tuple-element.78.refs_7_), channel_id=1, source_target_pairs={{0,1},{1,0},{2,3},{3,2},{4,5},{5,4},{6,7},{7,6},{8,9},{9,8},{10,11... | collective-permute-start | bytes 1769480 | tf_op jit(solution)/shard_map/ppermute | solution.py:436
  94.1 3.6 %collective-permute-start.24 = (bf16[144,2048]{1,0:T(8,128)(2,1)S(1)}, bf16[144,2048]{1,0:T(8,128)(2,1)S(1)}, u32[]{:S(2)}, u32[]{:S(2)}) collective-permute-start(bf16[144,2048]{1,0:T(8,128)(2,1)S(1)} %get-tuple-element.83.refs_4_), channel_id=1, source_target_pairs={{0,1},{1,0},{2,3},{3,2},{4,5},{5,4},{6,7},{7,6},{8,9},{9,8},{10,11... | collective-permute-start | bytes 1769480 | tf_op jit(solution)/shard_map/ppermute | solution.py:436
  94.2 3.5 %collective-permute-start.23 = (bf16[144,2048]{1,0:T(8,128)(2,1)S(1)}, bf16[144,2048]{1,0:T(8,128)(2,1)S(1)}, u32[]{:S(2)}, u32[]{:S(2)}) collective-permute-start(bf16[144,2048]{1,0:T(8,128)(2,1)S(1)} %get-tuple-element.82.refs_6_.refs_4_.refs_5_), channel_id=1, source_target_pairs={{0,1},{1,0},{2,3},{3,2},{4,5},{5,4},{6,7},{7,6},{8,9},{9,8},{10,11... | collective-permute-start | bytes 1769480 | tf_op jit(solution)/shard_map/ppermute | solution.py:436
  97.7 6.8 %slice-start = ((s8[6291456]{0:T(1024)(128)(4,1)}), s8[4194304]{0:T(1024)(128)(4,1)S(1)}, s32[]{:S(2)}) async-start(s8[6291456]{0:T(1024)(128)(4,1)} %bitcast.1), calls=%async_computation | async-start | bytes 8388608
  97.7 6.8 %slice-start.1 = ((s8[6291456]{0:T(1024)(128)(4,1)}), s8[2097152]{0:T(1024)(128)(4,1)S(1)}, s32[]{:S(2)}) async-start(s8[6291456]{0:T(1024)(128)(4,1)} %bitcast.1), calls=%async_computation.1 | async-start | bytes 4194304
  100.7 6.5 %collective-permute-start.27 = (f32[8,128]{1,0:T(8,128)S(1)}, f32[8,128]{1,0:T(8,128)S(1)}, u32[]{:S(2)}, u32[]{:S(2)}) collective-permute-start(f32[8,128]{1,0:T(8,128)S(1)} %get-tuple-element.92), channel_id=1, source_target_pairs={{0,6},{1,7},{2,4},{3,5},{4,2},{5,3},{6,0},{7,1},{8,14},{9,15},{10,... | collective-permute-start | bytes 12296 | tf_op jit(solution)/shard_map/ppermute | solution.py:416
  103.8 3.6 %collective-permute-start.26 = (f32[8,128]{1,0:T(8,128)S(1)}, f32[8,128]{1,0:T(8,128)S(1)}, u32[]{:S(2)}, u32[]{:S(2)}) collective-permute-start(f32[8,128]{1,0:T(8,128)S(1)} %get-tuple-element.92), channel_id=1, source_target_pairs={{0,4},{1,5},{2,6},{3,7},{4,0},{5,1},{6,2},{7,3},{8,12},{9,13},{10,... | collective-permute-start | bytes 12296 | tf_op jit(solution)/shard_map/ppermute | solution.py:416
  104.2 3.6 %collective-permute-start.25 = (f32[8,128]{1,0:T(8,128)S(1)}, f32[8,128]{1,0:T(8,128)S(1)}, u32[]{:S(2)}, u32[]{:S(2)}) collective-permute-start(f32[8,128]{1,0:T(8,128)S(1)} %get-tuple-element.92), channel_id=1, source_target_pairs={{0,2},{1,3},{2,0},{3,1},{4,6},{5,7},{6,4},{7,5},{8,10},{9,11},{10,... | collective-permute-start | bytes 12296 | tf_op jit(solution)/shard_map/ppermute | solution.py:416
  107.9 5.5 %collective-permute-start.30 = (f32[8,128]{1,0:T(8,128)S(1)}, f32[8,128]{1,0:T(8,128)S(1)}, u32[]{:S(2)}, u32[]{:S(2)}) collective-permute-start(f32[8,128]{1,0:T(8,128)S(1)} %after.11), channel_id=1, source_target_pairs={{0,9},{1,8},{2,11},{3,10},{4,13},{5,12},{6,15},{7,14},{8,1},{9,0},... | collective-permute-start | bytes 12296 | tf_op jit(solution)/shard_map/ppermute | solution.py:416
  109.0 4.5 %collective-permute-start.29 = (f32[8,128]{1,0:T(8,128)S(1)}, f32[8,128]{1,0:T(8,128)S(1)}, u32[]{:S(2)}, u32[]{:S(2)}) collective-permute-start(f32[8,128]{1,0:T(8,128)S(1)} %after.11), channel_id=1, source_target_pairs={{0,8},{1,9},{2,10},{3,11},{4,12},{5,13},{6,14},{7,15},{8,0},{9,1},... | collective-permute-start | bytes 12296 | tf_op jit(solution)/shard_map/ppermute | solution.py:416
  110.5 3.0 %collective-permute-start.28 = (f32[8,128]{1,0:T(8,128)S(1)}, f32[8,128]{1,0:T(8,128)S(1)}, u32[]{:S(2)}, u32[]{:S(2)}) collective-permute-start(f32[8,128]{1,0:T(8,128)S(1)} %after.11), channel_id=1, source_target_pairs={{0,1},{1,0},{2,3},{3,2},{4,5},{5,4},{6,7},{7,6},{8,9},{9,8},{10,11... | collective-permute-start | bytes 12296 | tf_op jit(solution)/shard_map/ppermute | solution.py:416

commit v15 on v14

--- a/solution.py
+++ b/solution.py
@@ -401,8 +401,6 @@
 
 def rounds(devices):
     bits = [1 << i for i in range(devices.bit_length() - 1)]
-    if len(bits) >= 4:
-        bits = bits[1:3] + [bits[0]] + bits[3:]
     masks = []
     while bits:
         pair, bits = bits[:2], bits[2:]
@@ -488,10 +486,7 @@
     w, squares = phase(where, shapes, begin, grouped(far), at=ats[-1], w=w, squares="new")
 
     pieces = [group[3] for group in grouped(near, far)]
-    parts = [
-        [(0, half, 0, pieces[0]), (half, half // 2, 0, pieces[1])],
-        [(half + half // 2, half // 2, half // 2, pieces[1])],
-    ]
+    parts = [[(c * half, half, 0, pieces[c])] for c in range(2)]
     for late, masks in enumerate(rounds(devices)):
         squares = exchange(squares, devices, masks)
         if late == 0:

time: 117 us -> 118 us (level)
  transfers between devices with their start and end apart: 31 -> 31, of which waited for: 16 -> 15; matrix products, arithmetic and copies ran while one was open for 0% -> 0% of each run, Pallas kernels for 51% -> 50%
where the time goes in v15:
time: 118 us; the launch traced here: 117 us
  Pallas kernels  65.2 us (55%)
  starting transfers between devices  28.9 us (24%)
  waiting for transfers between devices  17.4 us (15%)
  local copies, waits for them, and re-layouts  3.49 us (3%)
  between operations  2.4 us (2%)
    pallas_call x9, Pallas kernels, phase(): pl.pallas_call(functools.partial(phase_kernel, spec), in_specs=specs, out...  56.2 us
    ppermute x25, starting transfers between devices, send(): return lax.ppermute(x, 'dp', pairs)  22.2 us
    ppermute x25, waiting for transfers between devices, send(): return lax.ppermute(x, 'dp', pairs)  16.1 us
    ppermute x6, starting transfers between devices, exchange(): lax.ppermute(x, 'dp', [(d, d ^ mask) for d in range(devices)])  6.65 us
    pallas_call x1, Pallas kernels, prepared(): pl.pallas_call(functools.partial(prep_kernel, spans, rows), in_specs=[sme...  3.96 us
    unnamed x8, local copies, waits for them, and re-layouts  3.49 us
    pallas_call x1, Pallas kernels, scaled(): pl.pallas_call(functools.partial(scale_kernel, parts), in_specs=[vmem, vm...  2.96 us
  transfers between devices with their start and end apart: 31, of which 15 were waited for; matrix products, arithmetic and copies ran while one was open for 0% of the time, Pallas kernels for 50%

profile of v15, /device:TPU:0, one launch (start us, length us, event | category | flops | bytes accessed | tf_op | source)
XLA Modules:
  0.0 117.4 jit_solution(1616634271022185670)
XLA Ops:
  0.6 3.1 %collective-permute-start.1 = (bf16[144,4096]{1,0:T(8,128)(2,1)}, bf16[144,4096]{1,0:T(8,128)(2,1)S(1)}, u32[]{:S(2)}, u32[]{:S(2)}) collective-permute-start(bf16[144,4096]{1,0:T(8,128)(2,1)} %grad_ref.1), channel_id=1, source_target_pairs={{0,4},{1,3},{4,8},{5,1},{8,12},{9,5},{12,14},{13,9},{14,10},{15,13... | collective-permute-start | bytes 3538952 | tf_op jit(solution)/shard_map/ppermute | solution.py:434
  5.0 0.7 copy-done.1
  5.7 4.0 %prep.1 = (bf16[144,4096]{1,0:T(8,128)(2,1)S(1)}, bf16[144,2048]{1,0:T(8,128)(2,1)S(1)}, bf16[144,2048]{1,0:T(8,128)(2,1)S(1)}, s32[8,128]{1,0:T(8,128)S(1)}, bf...) custom-call(s32[16,16]{1,0:T(8,128)S(1)} %copy-done.1, ...), custom_call_target="tpu_custom_call" | custom-call | flops 1 | bytes 1 | tf_op jit(solution)/shard_map/prep/pallas_call | solution.py:121
  9.7 0.1 collective-permute-start.2
  9.8 0.5 collective-permute-start.3
  10.2 0.7 collective-permute-start.7
  10.9 1.0 collective-permute-start
  12.0 0.6 collective-permute-done.3.refs_8_
  12.6 2.8 %copy-done = bf16[768,4096]{1,0:T(8,128)(2,1)S(1)} copy-done((bf16[768,4096]{1,0:T(8,128)(2,1)S(1)}, bf16[768,4096]{1,0:T(8,128)(2,1)}, u32[]{:S(2)}) %copy-start) | copy-done | bytes 6291480
  15.4 7.2 %phase_w_whole.5 = (f32[768,4096]{1,0:T(8,128)S(1)}, bf16[2304,768]{1,0:T(8,128)(2,1)}, f32[8,128]{1,0:T(8,128)S(1)}) custom-call(s32[16,16]{1,0:T(8,128)S(1)} %copy-done.1, s32[1]{0:T(128)} %bitcast.me_ref.refs_1_, s32[1]{0:T(128)S(6)} %copy.46.heads_ref.refs_2_, bf16[768,288]{1,0:T(8,128)(2,1)S(1)} %get-tuple-element.49.refs_3_, ...), custom_call_target="tpu_custom_call" | custom-call | flops 1 | bytes 1 | tf_op jit(solution)/shard_map/phase_w_whole/pallas_call | solution.py:304
  22.6 0.4 collective-permute-done.count_ref
  23.0 0.7 arrived.2.x_ref
  23.6 0.1 split.7
  23.8 0.1 collective-permute-start.5
  23.8 2.5 %collective-permute-start.4 = (bf16[144,4096]{1,0:T(8,128)(2,1)S(1)}, bf16[144,4096]{1,0:T(8,128)(2,1)S(1)}, u32[]{:S(2)}, u32[]{:S(2)}) collective-permute-start(bf16[144,4096]{1,0:T(8,128)(2,1)S(1)} %arrived.2.x_ref), channel_id=1, source_target_pairs={{0,4},{1,3},{4,8},{5,1},{8,12},{9,5},{12,14},{13,9},{14,10},{15,13... | collective-permute-start | bytes 3538952 | tf_op jit(solution)/shard_map/ppermute | solution.py:434
  26.4 2.2 %collective-permute-start.6 = (s32[8,128]{1,0:T(8,128)S(1)}, s32[8,128]{1,0:T(8,128)S(1)}, u32[]{:S(2)}, u32[]{:S(2)}) collective-permute-start(s32[8,128]{1,0:T(8,128)S(1)} %get-tuple-element.48), channel_id=1, source_target_pairs={{0,3},{1,4},{4,1},{5,8},{8,5},{9,12},{12,9},{13,14},{14,13},{15,10... | collective-permute-start | bytes 12296 | tf_op jit(solution)/shard_map/ppermute | solution.py:434
  28.5 4.2 %collective-permute-done.6.count_ref = s32[8,128]{1,0:T(8,128)S(1)} collective-permute-done((s32[8,128]{1,0:T(8,128)S(1)}, s32[8,128]{1,0:T(8,128)S(1)}, u32[]{:S(2)}, u32[]{:S(2)}) %collective-permute-start.6) | collective-permute-done | bytes 4128 | tf_op jit(solution)/shard_map/ppermute | solution.py:434
  32.8 0.7 arrived.3.x_ref
  33.4 0.1 split.8
  33.5 3.0 %collective-permute-start.13 = (bf16[144,4096]{1,0:T(8,128)(2,1)S(1)}, bf16[144,4096]{1,0:T(8,128)(2,1)S(1)}, u32[]{:S(2)}, u32[]{:S(2)}) collective-permute-start(bf16[144,4096]{1,0:T(8,128)(2,1)S(1)} %arrived.3.x_ref), channel_id=1, source_target_pairs={{0,4},{1,3},{4,8},{5,1},{8,12},{9,5},{12,14},{13,9},{14,10},{15,13... | collective-permute-start | bytes 3538952 | tf_op jit(solution)/shard_map/ppermute | solution.py:434
  36.5 0.5 collective-permute-start.8
  37.1 1.5 %collective-permute-done.9.refs_10_ = bf16[144,2048]{1,0:T(8,128)(2,1)S(1)} collective-permute-done((bf16[144,2048]{1,0:T(8,128)(2,1)S(1)}, bf16[144,2048]{1,0:T(8,128)(2,1)S(1)}, u32[]{:S(2)}, u32[]{:S(2)}) %collective-permute-start.9) | collective-permute-done | bytes 589856 | tf_op jit(solution)/shard_map/ppermute | solution.py:434
  38.5 0.8 collective-permute-done.8.refs_8_
  39.4 0.8 collective-permute-done.10.refs_12_
  40.2 11.3 %phase_w_whole.6 = (f32[768,4096]{1,0:T(8,128)S(1)}, bf16[2304,768]{1,0:T(8,128)(2,1)}, f32[8,128]{1,0:T(8,128)S(1)}) custom-call(s32[16,16]{1,0:T(8,128)S(1)} %copy-done.1, s32[1]{0:T(128)} %bitcast.me_ref.refs_1_, s32[1]{0:T(128)S(6)} %copy.46.heads_ref.refs_2_, ...), custom_call_target="tpu_custom_call", output_to_operand_aliasing={{0}: (13, {}), {1}: (14, {})} | custom-call | flops 1 | bytes 1 | tf_op jit(solution)/shard_map/phase_w_whole/pallas_call | solution.py:304
  51.5 1.6 %collective-permute-start.11 = (bf16[144,4096]{1,0:T(8,128)(2,1)S(1)}, bf16[144,4096]{1,0:T(8,128)(2,1)S(1)}, u32[]{:S(2)}, u32[]{:S(2)}) collective-permute-start(bf16[144,4096]{1,0:T(8,128)(2,1)S(1)} %after.6.x_ref), channel_id=1, source_target_pairs={{0,4},{1,3},{4,8},{5,1},{8,12},{9,5},{12,14},{13,9},{14,10},{15,13... | collective-permute-start | bytes 3538952 | tf_op jit(solution)/shard_map/ppermute | solution.py:434
  53.1 0.1 split.9
  53.2 0.1 collective-permute-start.12
  53.3 0.5 collective-permute-start.15
  53.8 2.2 %collective-permute-done.13.refs_0_ = bf16[144,4096]{1,0:T(8,128)(2,1)S(1)} collective-permute-done((bf16[144,4096]{1,0:T(8,128)(2,1)S(1)}, bf16[144,4096]{1,0:T(8,128)(2,1)S(1)}, u32[]{:S(2)}, u32[]{:S(2)}) %collective-permute-start.13) | collective-permute-done | bytes 1179680 | tf_op jit(solution)/shard_map/ppermute | solution.py:434
  56.1 0.1 split.10
  56.2 0.1 collective-permute-start.14
  56.2 0.5 collective-permute-start.16
  56.7 2.1 %collective-permute-start.18 = (bf16[144,4096]{1,0:T(8,128)(2,1)S(1)}, bf16[144,4096]{1,0:T(8,128)(2,1)S(1)}, u32[]{:S(2)}, u32[]{:S(2)}) collective-permute-start(bf16[144,4096]{1,0:T(8,128)(2,1)S(1)} %after.7.x_ref), channel_id=1, source_target_pairs={{0,4},{1,3},{4,8},{5,1},{8,12},{9,5},{12,14},{13,9},{14,10},{15,13... | collective-permute-start | bytes 3538952 | tf_op jit(solution)/shard_map/ppermute | solution.py:434
  58.8 0.2 collective-permute-done.16.refs_12_
  59.1 11.3 %phase_w_whole.7 = (f32[768,4096]{1,0:T(8,128)S(1)}, bf16[2304,768]{1,0:T(8,128)(2,1)}, f32[8,128]{1,0:T(8,128)S(1)}) custom-call(s32[16,16]{1,0:T(8,128)S(1)} %copy-done.1, s32[1]{0:T(128)} %bitcast.me_ref.refs_1_, s32[1]{0:T(128)S(6)} %copy.46.heads_ref.refs_2_, ...), custom_call_target="tpu_custom_call", output_to_operand_aliasing={{0}: (13, {}), {1}: (14, {})} | custom-call | flops 1 | bytes 1 | tf_op jit(solution)/shard_map/phase_w_whole/pallas_call | solution.py:304
  70.4 0.1 split.11
  70.5 0.2 collective-permute-start.19
  70.7 0.4 collective-permute-start.20
  71.0 2.1 %collective-permute-start.17 = (bf16[144,4096]{1,0:T(8,128)(2,1)S(1)}, bf16[144,4096]{1,0:T(8,128)(2,1)S(1)}, u32[]{:S(2)}, u32[]{:S(2)}) collective-permute-start(bf16[144,4096]{1,0:T(8,128)(2,1)S(1)} %after.8.x_ref), channel_id=1, source_target_pairs={{0,4},{1,3},{4,8},{5,1},{8,12},{9,5},{12,14},{13,9},{14,10},{15,13... | collective-permute-start | bytes 3538952 | tf_op jit(solution)/shard_map/ppermute | solution.py:434
  73.1 0.3 collective-permute-done.20.refs_8_
  73.4 7.5 %phase_w_whole.8 = (f32[768,4096]{1,0:T(8,128)S(1)}, bf16[2304,768]{1,0:T(8,128)(2,1)}, f32[8,128]{1,0:T(8,128)S(1)}) custom-call(s32[16,16]{1,0:T(8,128)S(1)} %copy-done.1, s32[1]{0:T(128)} %bitcast.me_ref.refs_1_, s32[1]{0:T(128)S(6)} %copy.46.heads_ref.refs_2_, ...), custom_call_target="tpu_custom_call", output_to_operand_aliasing={{0}: (9, {}), {1}: (10, {})} | custom-call | flops 1 | bytes 1 | tf_op jit(solution)/shard_map/phase_w_whole/pallas_call | solution.py:304
  80.9 0.5 collective-permute-done.18.refs_0_
  81.3 0.1 split.12
  81.4 0.1 collective-permute-start.21
  81.5 0.5 collective-permute-start.22
  82.0 1.5 %collective-permute-done.21.refs_6_ = bf16[144,2048]{1,0:T(8,128)(2,1)S(1)} collective-permute-done((bf16[144,2048]{1,0:T(8,128)(2,1)S(1)}, bf16[144,2048]{1,0:T(8,128)(2,1)S(1)}, u32[]{:S(2)}, u32[]{:S(2)}) %collective-permute-start.21) | collective-permute-done | bytes 589856 | tf_op jit(solution)/shard_map/ppermute | solution.py:434
  83.5 0.8 collective-permute-done.22.refs_8_
  84.4 7.5 %phase_w_whole.9 = (f32[768,4096]{1,0:T(8,128)S(1)}, bf16[2304,768]{1,0:T(8,128)(2,1)}, f32[8,128]{1,0:T(8,128)S(1)}) custom-call(s32[16,16]{1,0:T(8,128)S(1)} %copy-done.1, s32[1]{0:T(128)} %bitcast.me_ref.refs_1_, s32[1]{0:T(128)S(6)} %copy.46.heads_ref.refs_2_, ...), custom_call_target="tpu_custom_call", output_to_operand_aliasing={{0}: (9, {}), {1}: (10, {})} | custom-call | flops 1 | bytes 1 | tf_op jit(solution)/shard_map/phase_w_whole/pallas_call | solution.py:304
  91.8 2.1 %collective-permute-done.17.refs_0_ = bf16[144,4096]{1,0:T(8,128)(2,1)S(1)} collective-permute-done((bf16[144,4096]{1,0:T(8,128)(2,1)S(1)}, bf16[144,4096]{1,0:T(8,128)(2,1)S(1)}, u32[]{:S(2)}, u32[]{:S(2)}) %collective-permute-start.17) | collective-permute-done | bytes 1179680 | tf_op jit(solution)/shard_map/ppermute | solution.py:434
  94.0 0.1 split.13
  94.1 0.1 collective-permute-start.23
  94.2 0.5 collective-permute-start.24
  94.7 3.0 %phase_w_None.2 = (f32[768,4096]{1,0:T(8,128)S(1)}, f32[8,128]{1,0:T(8,128)}) custom-call(s32[16,16]{1,0:T(8,128)S(1)} %copy-done.1, s32[1]{0:T(128)} %bitcast.me_ref.refs_1_, s32[1]{0:T(128)S(6)} %copy.46.heads_ref.refs_2_, bf16[768,144]{1,0:T(8,128)(2,1)S(1)} %get-tuple-element.88.refs_3_, ...), custom_call_target="tpu_custom_call", output_to_operand_aliasing={{0}: (6, {})} | custom-call | flops 1 | bytes 1 | tf_op jit(solution)/shard_map/phase_w_None/pallas_call | solution.py:304
  97.7 3.0 %phase_w_None.3 = (f32[768,4096]{1,0:T(8,128)S(1)}, f32[8,128]{1,0:T(8,128)S(1)}) custom-call(s32[16,16]{1,0:T(8,128)S(1)} %copy-done.1, s32[1]{0:T(128)} %bitcast.me_ref.refs_1_, s32[1]{0:T(128)S(6)} %copy.46.heads_ref.refs_2_, bf16[768,144]{1,0:T(8,128)(2,1)S(1)} %get-tuple-element.87.refs_3_, ...), custom_call_target="tpu_custom_call", output_to_operand_aliasing={{0}: (6, {})} | custom-call | flops 1 | bytes 1 | tf_op jit(solution)/shard_map/phase_w_None/pallas_call | solution.py:304
  100.7 1.8 %collective-permute-start.27 = (f32[8,128]{1,0:T(8,128)S(1)}, f32[8,128]{1,0:T(8,128)S(1)}, u32[]{:S(2)}, u32[]{:S(2)}) collective-permute-start(f32[8,128]{1,0:T(8,128)S(1)} %get-tuple-element.92), channel_id=1, source_target_pairs={{0,3},{1,2},{2,1},{3,0},{4,7},{5,6},{6,5},{7,4},{8,11},{9,10},{10,... | collective-permute-start | bytes 12296 | tf_op jit(solution)/shard_map/ppermute | solution.py:414
  102.5 0.4 collective-permute-start.26
  102.9 2.0 %phase__first.1 = (f32[288,768]{1,0:T(8,128)S(1)}, f32[8,128]{1,0:T(8,128)S(1)}) custom-call(s32[16,16]{1,0:T(8,128)S(1)} %copy-done.1, s32[1]{0:T(128)} %bitcast.me_ref.refs_1_, s32[1]{0:T(128)S(6)} %copy.46.heads_ref.refs_2_, bf16[768,4096]{1,0:T(8,128)(2,1)S(1)} %bitcast.2, bf16[144,2048]{1,0:T(8,128)(2,1)S(1)} %get-tuple-element.83.refs_4_, ...), custom_call_target="tpu_custom_call" | custom-call | flops 1 | bytes 1 | tf_op jit(solution)/shard_map/phase__first/pallas_call | solution.py:304
  105.0 1.1 collective-permute-done.26
  106.1 3.7 %collective-permute-start.30 = (f32[8,128]{1,0:T(8,128)S(1)}, f32[8,128]{1,0:T(8,128)S(1)}, u32[]{:S(2)}, u32[]{:S(2)}) collective-permute-start(f32[8,128]{1,0:T(8,128)S(1)} %after.11), channel_id=1, source_target_pairs={{0,12},{1,13},{2,14},{3,15},{4,8},{5,9},{6,10},{7,11},{8,4},{9,5},... | collective-permute-start | bytes 12296 | tf_op jit(solution)/shard_map/ppermute | solution.py:414
  109.8 0.8 collective-permute-start.28
  110.6 3.5 %phase__last.1 = (bf16[2304,768]{1,0:T(8,128)(2,1)}, f32[8,128]{1,0:T(8,128)}) custom-call(s32[16,16]{1,0:T(8,128)S(1)} %copy-done.1, s32[1]{0:T(128)} %bitcast.me_ref.refs_1_, s32[1]{0:T(128)S(6)} %copy.46.heads_ref.refs_2_, bf16[768,4096]{1,0:T(8,128)(2,1)S(1)} %bitcast.2, ...), custom_call_target="tpu_custom_call", output_to_operand_aliasing={{0}: (7, {})} | custom-call | flops 1 | bytes 1 | tf_op jit(solution)/shard_map/phase__last/pallas_call | solution.py:304
  114.0 0.3 collective-permute-done.29
  114.3 3.0 %scale.1 = bf16[768,4096]{1,0:T(8,128)(2,1)} custom-call(f32[768,4096]{1,0:T(8,128)S(1)} %get-tuple-element.91.w_ref, f32[8,128]{1,0:T(8,128)S(1)} %add_add_fusion.squares_ref), custom_call_target="tpu_custom_call" | custom-call | flops 3145728 | bytes 6291456 | tf_op jit(solution)/shard_map/scale/pallas_call | solution.py:344
  (35 shorter events, 0.1 us)
Async XLA Ops:
  0.6 22.4 %collective-permute-start.1 = (bf16[144,4096]{1,0:T(8,128)(2,1)}, bf16[144,4096]{1,0:T(8,128)(2,1)S(1)}, u32[]{:S(2)}, u32[]{:S(2)}) collective-permute-start(bf16[144,4096]{1,0:T(8,128)(2,1)} %grad_ref.1), channel_id=1, source_target_pairs={{0,4},{1,3},{4,8},{5,1},{8,12},{9,5},{12,14},{13,9},{14,10},{15,13... | collective-permute-start | bytes 3538952 | tf_op jit(solution)/shard_map/ppermute | solution.py:434
  5.0 0.7 copy-start.1
  9.7 2.3 %collective-permute-start.2 = (bf16[144,2048]{1,0:T(8,128)(2,1)S(1)}, bf16[144,2048]{1,0:T(8,128)(2,1)S(1)}, u32[]{:S(2)}, u32[]{:S(2)}) collective-permute-start(bf16[144,2048]{1,0:T(8,128)(2,1)S(1)} %get-tuple-element.50.refs_5_), channel_id=1, source_target_pairs={{0,1},{1,0},{2,3},{3,2},{4,5},{5,4},{6,7},{7,6},{8,9},{9,8},{10,11... | collective-permute-start | bytes 1769480 | tf_op jit(solution)/shard_map/ppermute | solution.py:434
  9.8 2.8 %collective-permute-start.3 = (bf16[144,2048]{1,0:T(8,128)(2,1)S(1)}, bf16[144,2048]{1,0:T(8,128)(2,1)S(1)}, u32[]{:S(2)}, u32[]{:S(2)}) collective-permute-start(bf16[144,2048]{1,0:T(8,128)(2,1)S(1)} %get-tuple-element.51.refs_7_), channel_id=1, source_target_pairs={{0,1},{1,0},{2,3},{3,2},{4,5},{5,4},{6,7},{7,6},{8,9},{9,8},{10,11... | collective-permute-start | bytes 1769480 | tf_op jit(solution)/shard_map/ppermute | solution.py:434
  10.2 22.5 %collective-permute-start.7 = (bf16[144,4096]{1,0:T(8,128)(2,1)S(1)}, bf16[144,4096]{1,0:T(8,128)(2,1)S(1)}, u32[]{:S(2)}, u32[]{:S(2)}) collective-permute-start(bf16[144,4096]{1,0:T(8,128)(2,1)S(1)} %get-tuple-element.55), channel_id=1, source_target_pairs={{0,3},{1,4},{4,1},{5,8},{8,5},{9,12},{12,9},{13,14},{14,13},{15,10... | collective-permute-start | bytes 3538952 | tf_op jit(solution)/shard_map/ppermute | solution.py:434
  10.9 12.1 %collective-permute-start = (s32[8,128]{1,0:T(8,128)S(1)}, s32[8,128]{1,0:T(8,128)S(1)}, u32[]{:S(2)}, u32[]{:S(2)}) collective-permute-start(s32[8,128]{1,0:T(8,128)S(1)} %get-tuple-element.48), channel_id=1, source_target_pairs={{0,4},{1,3},{4,8},{5,1},{8,12},{9,5},{12,14},{13,9},{14,10},{15,13... | collective-permute-start | bytes 12296 | tf_op jit(solution)/shard_map/ppermute | solution.py:434
  12.6 2.8 %copy-start = (bf16[768,4096]{1,0:T(8,128)(2,1)S(1)}, bf16[768,4096]{1,0:T(8,128)(2,1)}, u32[]{:S(2)}) copy-start(bf16[768,4096]{1,0:T(8,128)(2,1)} %refs_3_.3) | copy-start | bytes 18874372
  23.8 13.3 %collective-permute-start.5 = (bf16[144,2048]{1,0:T(8,128)(2,1)S(1)}, bf16[144,2048]{1,0:T(8,128)(2,1)S(1)}, u32[]{:S(2)}, u32[]{:S(2)}) collective-permute-start(bf16[144,2048]{1,0:T(8,128)(2,1)S(1)} %get-tuple-element.54.refs_5_), channel_id=1, source_target_pairs={{0,1},{1,0},{2,3},{3,2},{4,5},{5,4},{6,7},{7,6},{8,9},{9,8},{10,11... | collective-permute-start | bytes 1769480 | tf_op jit(solution)/shard_map/ppermute | solution.py:434
  23.8 27.7 %collective-permute-start.4 = (bf16[144,4096]{1,0:T(8,128)(2,1)S(1)}, bf16[144,4096]{1,0:T(8,128)(2,1)S(1)}, u32[]{:S(2)}, u32[]{:S(2)}) collective-permute-start(bf16[144,4096]{1,0:T(8,128)(2,1)S(1)} %arrived.2.x_ref), channel_id=1, source_target_pairs={{0,4},{1,3},{4,8},{5,1},{8,12},{9,5},{12,14},{13,9},{14,10},{15,13... | collective-permute-start | bytes 3538952 | tf_op jit(solution)/shard_map/ppermute | solution.py:434
  26.4 6.4 %collective-permute-start.6 = (s32[8,128]{1,0:T(8,128)S(1)}, s32[8,128]{1,0:T(8,128)S(1)}, u32[]{:S(2)}, u32[]{:S(2)}) collective-permute-start(s32[8,128]{1,0:T(8,128)S(1)} %get-tuple-element.48), channel_id=1, source_target_pairs={{0,3},{1,4},{4,1},{5,8},{8,5},{9,12},{12,9},{13,14},{14,13},{15,10... | collective-permute-start | bytes 12296 | tf_op jit(solution)/shard_map/ppermute | solution.py:434
  33.5 22.5 %collective-permute-start.13 = (bf16[144,4096]{1,0:T(8,128)(2,1)S(1)}, bf16[144,4096]{1,0:T(8,128)(2,1)S(1)}, u32[]{:S(2)}, u32[]{:S(2)}) collective-permute-start(bf16[144,4096]{1,0:T(8,128)(2,1)S(1)} %arrived.3.x_ref), channel_id=1, source_target_pairs={{0,4},{1,3},{4,8},{5,1},{8,12},{9,5},{12,14},{13,9},{14,10},{15,13... | collective-permute-start | bytes 3538952 | tf_op jit(solution)/shard_map/ppermute | solution.py:434
  36.5 2.0 %collective-permute-start.9 = (bf16[144,2048]{1,0:T(8,128)(2,1)S(1)}, bf16[144,2048]{1,0:T(8,128)(2,1)S(1)}, u32[]{:S(2)}, u32[]{:S(2)}) collective-permute-start(bf16[144,2048]{1,0:T(8,128)(2,1)S(1)} %get-tuple-element.57.refs_9_), channel_id=1, source_target_pairs={{0,1},{1,0},{2,3},{3,2},{4,5},{5,4},{6,7},{7,6},{8,9},{9,8},{10,11... | collective-permute-start | bytes 1769480 | tf_op jit(solution)/shard_map/ppermute | solution.py:434
  36.5 2.8 %collective-permute-start.8 = (bf16[144,2048]{1,0:T(8,128)(2,1)S(1)}, bf16[144,2048]{1,0:T(8,128)(2,1)S(1)}, u32[]{:S(2)}, u32[]{:S(2)}) collective-permute-start(bf16[144,2048]{1,0:T(8,128)(2,1)S(1)} %get-tuple-element.56.refs_7_), channel_id=1, source_target_pairs={{0,1},{1,0},{2,3},{3,2},{4,5},{5,4},{6,7},{7,6},{8,9},{9,8},{10,11... | collective-permute-start | bytes 1769480 | tf_op jit(solution)/shard_map/ppermute | solution.py:434
  37.1 3.2 %collective-permute-start.10 = (bf16[144,2048]{1,0:T(8,128)(2,1)S(1)}, bf16[144,2048]{1,0:T(8,128)(2,1)S(1)}, u32[]{:S(2)}, u32[]{:S(2)}) collective-permute-start(bf16[144,2048]{1,0:T(8,128)(2,1)S(1)} %get-tuple-element.58.refs_11_), channel_id=1, source_target_pairs={{0,1},{1,0},{2,3},{3,2},{4,5},{5,4},{6,7},{7,6},{8,9},{9,8},{10,11... | collective-permute-start | bytes 1769480 | tf_op jit(solution)/shard_map/ppermute | solution.py:434
  51.5 18.8 %collective-permute-start.11 = (bf16[144,4096]{1,0:T(8,128)(2,1)S(1)}, bf16[144,4096]{1,0:T(8,128)(2,1)S(1)}, u32[]{:S(2)}, u32[]{:S(2)}) collective-permute-start(bf16[144,4096]{1,0:T(8,128)(2,1)S(1)} %after.6.x_ref), channel_id=1, source_target_pairs={{0,4},{1,3},{4,8},{5,1},{8,12},{9,5},{12,14},{13,9},{14,10},{15,13... | collective-permute-start | bytes 3538952 | tf_op jit(solution)/shard_map/ppermute | solution.py:434
  53.2 3.5 %collective-permute-start.12 = (bf16[144,2048]{1,0:T(8,128)(2,1)S(1)}, bf16[144,2048]{1,0:T(8,128)(2,1)S(1)}, u32[]{:S(2)}, u32[]{:S(2)}) collective-permute-start(bf16[144,2048]{1,0:T(8,128)(2,1)S(1)} %get-tuple-element.63.refs_5_), channel_id=1, source_target_pairs={{0,1},{1,0},{2,3},{3,2},{4,5},{5,4},{6,7},{7,6},{8,9},{9,8},{10,11... | collective-permute-start | bytes 1769480 | tf_op jit(solution)/shard_map/ppermute | solution.py:434
  53.3 5.5 %collective-permute-start.15 = (bf16[144,2048]{1,0:T(8,128)(2,1)S(1)}, bf16[144,2048]{1,0:T(8,128)(2,1)S(1)}, u32[]{:S(2)}, u32[]{:S(2)}) collective-permute-start(bf16[144,2048]{1,0:T(8,128)(2,1)S(1)} %get-tuple-element.65.refs_9_), channel_id=1, source_target_pairs={{0,1},{1,0},{2,3},{3,2},{4,5},{5,4},{6,7},{7,6},{8,9},{9,8},{10,11... | collective-permute-start | bytes 1769480 | tf_op jit(solution)/shard_map/ppermute | solution.py:434
  56.2 2.7 %collective-permute-start.14 = (bf16[144,2048]{1,0:T(8,128)(2,1)S(1)}, bf16[144,2048]{1,0:T(8,128)(2,1)S(1)}, u32[]{:S(2)}, u32[]{:S(2)}) collective-permute-start(bf16[144,2048]{1,0:T(8,128)(2,1)S(1)} %get-tuple-element.64.refs_7_), channel_id=1, source_target_pairs={{0,1},{1,0},{2,3},{3,2},{4,5},{5,4},{6,7},{7,6},{8,9},{9,8},{10,11... | collective-permute-start | bytes 1769480 | tf_op jit(solution)/shard_map/ppermute | solution.py:434
  56.2 2.8 %collective-permute-start.16 = (bf16[144,2048]{1,0:T(8,128)(2,1)S(1)}, bf16[144,2048]{1,0:T(8,128)(2,1)S(1)}, u32[]{:S(2)}, u32[]{:S(2)}) collective-permute-start(bf16[144,2048]{1,0:T(8,128)(2,1)S(1)} %get-tuple-element.66.refs_11_), channel_id=1, source_target_pairs={{0,1},{1,0},{2,3},{3,2},{4,5},{5,4},{6,7},{7,6},{8,9},{9,8},{10,11... | collective-permute-start | bytes 1769480 | tf_op jit(solution)/shard_map/ppermute | solution.py:434
  56.7 24.6 %collective-permute-start.18 = (bf16[144,4096]{1,0:T(8,128)(2,1)S(1)}, bf16[144,4096]{1,0:T(8,128)(2,1)S(1)}, u32[]{:S(2)}, u32[]{:S(2)}) collective-permute-start(bf16[144,4096]{1,0:T(8,128)(2,1)S(1)} %after.7.x_ref), channel_id=1, source_target_pairs={{0,4},{1,3},{4,8},{5,1},{8,12},{9,5},{12,14},{13,9},{14,10},{15,13... | collective-permute-start | bytes 3538952 | tf_op jit(solution)/shard_map/ppermute | solution.py:434
  70.5 2.7 %collective-permute-start.19 = (bf16[144,2048]{1,0:T(8,128)(2,1)S(1)}, bf16[144,2048]{1,0:T(8,128)(2,1)S(1)}, u32[]{:S(2)}, u32[]{:S(2)}) collective-permute-start(bf16[144,2048]{1,0:T(8,128)(2,1)S(1)} %get-tuple-element.72.refs_5_), channel_id=1, source_target_pairs={{0,1},{1,0},{2,3},{3,2},{4,5},{5,4},{6,7},{7,6},{8,9},{9,8},{10,11... | collective-permute-start | bytes 1769480 | tf_op jit(solution)/shard_map/ppermute | solution.py:434
  70.7 2.7 %collective-permute-start.20 = (bf16[144,2048]{1,0:T(8,128)(2,1)S(1)}, bf16[144,2048]{1,0:T(8,128)(2,1)S(1)}, u32[]{:S(2)}, u32[]{:S(2)}) collective-permute-start(bf16[144,2048]{1,0:T(8,128)(2,1)S(1)} %get-tuple-element.73.refs_7_), channel_id=1, source_target_pairs={{0,1},{1,0},{2,3},{3,2},{4,5},{5,4},{6,7},{7,6},{8,9},{9,8},{10,11... | collective-permute-start | bytes 1769480 | tf_op jit(solution)/shard_map/ppermute | solution.py:434
  71.0 22.9 %collective-permute-start.17 = (bf16[144,4096]{1,0:T(8,128)(2,1)S(1)}, bf16[144,4096]{1,0:T(8,128)(2,1)S(1)}, u32[]{:S(2)}, u32[]{:S(2)}) collective-permute-start(bf16[144,4096]{1,0:T(8,128)(2,1)S(1)} %after.8.x_ref), channel_id=1, source_target_pairs={{0,4},{1,3},{4,8},{5,1},{8,12},{9,5},{12,14},{13,9},{14,10},{15,13... | collective-permute-start | bytes 3538952 | tf_op jit(solution)/shard_map/ppermute | solution.py:434
  81.4 2.1 %collective-permute-start.21 = (bf16[144,2048]{1,0:T(8,128)(2,1)S(1)}, bf16[144,2048]{1,0:T(8,128)(2,1)S(1)}, u32[]{:S(2)}, u32[]{:S(2)}) collective-permute-start(bf16[144,2048]{1,0:T(8,128)(2,1)S(1)} %get-tuple-element.77.refs_5_), channel_id=1, source_target_pairs={{0,1},{1,0},{2,3},{3,2},{4,5},{5,4},{6,7},{7,6},{8,9},{9,8},{10,11... | collective-permute-start | bytes 1769480 | tf_op jit(solution)/shard_map/ppermute | solution.py:434
  81.5 2.8 %collective-permute-start.22 = (bf16[144,2048]{1,0:T(8,128)(2,1)S(1)}, bf16[144,2048]{1,0:T(8,128)(2,1)S(1)}, u32[]{:S(2)}, u32[]{:S(2)}) collective-permute-start(bf16[144,2048]{1,0:T(8,128)(2,1)S(1)} %get-tuple-element.78.refs_7_), channel_id=1, source_target_pairs={{0,1},{1,0},{2,3},{3,2},{4,5},{5,4},{6,7},{7,6},{8,9},{9,8},{10,11... | collective-permute-start | bytes 1769480 | tf_op jit(solution)/shard_map/ppermute | solution.py:434
  94.1 3.6 %collective-permute-start.23 = (bf16[144,2048]{1,0:T(8,128)(2,1)S(1)}, bf16[144,2048]{1,0:T(8,128)(2,1)S(1)}, u32[]{:S(2)}, u32[]{:S(2)}) collective-permute-start(bf16[144,2048]{1,0:T(8,128)(2,1)S(1)} %get-tuple-element.82.refs_4_.refs_5_), channel_id=1, source_target_pairs={{0,1},{1,0},{2,3},{3,2},{4,5},{5,4},{6,7},{7,6},{8,9},{9,8},{10,11... | collective-permute-start | bytes 1769480 | tf_op jit(solution)/shard_map/ppermute | solution.py:434
  94.2 3.5 %collective-permute-start.24 = (bf16[144,2048]{1,0:T(8,128)(2,1)S(1)}, bf16[144,2048]{1,0:T(8,128)(2,1)S(1)}, u32[]{:S(2)}, u32[]{:S(2)}) collective-permute-start(bf16[144,2048]{1,0:T(8,128)(2,1)S(1)} %get-tuple-element.83.refs_4_), channel_id=1, source_target_pairs={{0,1},{1,0},{2,3},{3,2},{4,5},{5,4},{6,7},{7,6},{8,9},{9,8},{10,11... | collective-permute-start | bytes 1769480 | tf_op jit(solution)/shard_map/ppermute | solution.py:434
  97.7 5.2 %slice-start = ((s8[6291456]{0:T(1024)(128)(4,1)}), s8[4194304]{0:T(1024)(128)(4,1)S(1)}, s32[]{:S(2)}) async-start(s8[6291456]{0:T(1024)(128)(4,1)} %bitcast.1), calls=%async_computation | async-start | bytes 8388608
  97.7 5.2 %slice-start.1 = ((s8[6291456]{0:T(1024)(128)(4,1)}), s8[2097152]{0:T(1024)(128)(4,1)S(1)}, s32[]{:S(2)}) async-start(s8[6291456]{0:T(1024)(128)(4,1)} %bitcast.1), calls=%async_computation.1 | async-start | bytes 4194304
  100.7 4.3 %collective-permute-start.27 = (f32[8,128]{1,0:T(8,128)S(1)}, f32[8,128]{1,0:T(8,128)S(1)}, u32[]{:S(2)}, u32[]{:S(2)}) collective-permute-start(f32[8,128]{1,0:T(8,128)S(1)} %get-tuple-element.92), channel_id=1, source_target_pairs={{0,3},{1,2},{2,1},{3,0},{4,7},{5,6},{6,5},{7,4},{8,11},{9,10},{10,... | collective-permute-start | bytes 12296 | tf_op jit(solution)/shard_map/ppermute | solution.py:414
  102.5 3.6 %collective-permute-start.26 = (f32[8,128]{1,0:T(8,128)S(1)}, f32[8,128]{1,0:T(8,128)S(1)}, u32[]{:S(2)}, u32[]{:S(2)}) collective-permute-start(f32[8,128]{1,0:T(8,128)S(1)} %get-tuple-element.92), channel_id=1, source_target_pairs={{0,2},{1,3},{2,0},{3,1},{4,6},{5,7},{6,4},{7,5},{8,10},{9,11},{10,... | collective-permute-start | bytes 12296 | tf_op jit(solution)/shard_map/ppermute | solution.py:414
  102.9 3.2 %collective-permute-start.25 = (f32[8,128]{1,0:T(8,128)S(1)}, f32[8,128]{1,0:T(8,128)S(1)}, u32[]{:S(2)}, u32[]{:S(2)}) collective-permute-start(f32[8,128]{1,0:T(8,128)S(1)} %get-tuple-element.92), channel_id=1, source_target_pairs={{0,1},{1,0},{2,3},{3,2},{4,5},{5,4},{6,7},{7,6},{8,9},{9,8},{10,11... | collective-permute-start | bytes 12296 | tf_op jit(solution)/shard_map/ppermute | solution.py:414
  106.1 7.9 %collective-permute-start.30 = (f32[8,128]{1,0:T(8,128)S(1)}, f32[8,128]{1,0:T(8,128)S(1)}, u32[]{:S(2)}, u32[]{:S(2)}) collective-permute-start(f32[8,128]{1,0:T(8,128)S(1)} %after.11), channel_id=1, source_target_pairs={{0,12},{1,13},{2,14},{3,15},{4,8},{5,9},{6,10},{7,11},{8,4},{9,5},... | collective-permute-start | bytes 12296 | tf_op jit(solution)/shard_map/ppermute | solution.py:414
  109.8 4.5 %collective-permute-start.29 = (f32[8,128]{1,0:T(8,128)S(1)}, f32[8,128]{1,0:T(8,128)S(1)}, u32[]{:S(2)}, u32[]{:S(2)}) collective-permute-start(f32[8,128]{1,0:T(8,128)S(1)} %after.11), channel_id=1, source_target_pairs={{0,8},{1,9},{2,10},{3,11},{4,12},{5,13},{6,14},{7,15},{8,0},{9,1},... | collective-permute-start | bytes 12296 | tf_op jit(solution)/shard_map/ppermute | solution.py:414
  109.8 4.5 %collective-permute-start.28 = (f32[8,128]{1,0:T(8,128)S(1)}, f32[8,128]{1,0:T(8,128)S(1)}, u32[]{:S(2)}, u32[]{:S(2)}) collective-permute-start(f32[8,128]{1,0:T(8,128)S(1)} %after.11), channel_id=1, source_target_pairs={{0,4},{1,5},{2,6},{3,7},{4,0},{5,1},{6,2},{7,3},{8,12},{9,13},{10,... | collective-permute-start | bytes 12296 | tf_op jit(solution)/shard_map/ppermute | solution.py:414

commit v16 on v14

--- a/solution.py
+++ b/solution.py
@@ -164,8 +164,7 @@
     at_ref = refs.pop(0) if do_w else None
     weight_ref = refs.pop(0) if attn else None
     g_refs = [refs.pop(0) for _ in range(arrays)]
-    if do_w and not fresh_w:
-        refs.pop(0)
+    w_before_ref = refs.pop(0) if do_w and not fresh_w else None
     before_ref = refs.pop(0) if attn == "last" else None
     added_ref = refs.pop(0) if squares == "added" else None
     if attn in ("whole", "last") and not fresh_out:
@@ -193,7 +192,7 @@
             fresh = jnp.concatenate(g[w_from:], axis=0) if len(g) > w_from + 1 else g[-1]
             w = jnp.dot(at_ref[...], fresh, preferred_element_type=jnp.float32)
             if not fresh_w:
-                w = w + w_ref[:, there]
+                w = w + w_before_ref[:, there]
             w_ref[:, there] = w
         if squares:
             folded = jnp.sum((w * w).reshape(w.shape[0] // 8, 8, TILE), axis=0)
@@ -401,8 +400,6 @@
 
 def rounds(devices):
     bits = [1 << i for i in range(devices.bit_length() - 1)]
-    if len(bits) >= 4:
-        bits = bits[1:3] + [bits[0]] + bits[3:]
     masks = []
     while bits:
         pair, bits = bits[:2], bits[2:]

time: 117 us -> 120 us (1.026)
  Pallas kernels: 65.1 us -> 70.7 us
  waiting for transfers between devices: 16.9 us -> 14 us
    pallas_call x9, Pallas kernels: 56.1 us -> 61.7 us  [phase(): pl.pallas_call(functools.partial(phase_kernel, spec), in_specs=specs, out...]
    ppermute x25, waiting for transfers between devices: 16.1 us -> 12.6 us  [send(): return lax.ppermute(x, 'dp', pairs)]
  transfers between devices with their start and end apart: 31 -> 31, of which waited for: 16 -> 13; matrix products, arithmetic and copies ran while one was open for 0% -> 0% of each run, Pallas kernels for 51% -> 53%
where the time goes in v16:
time: 120 us
  Pallas kernels  70.7 us (59%)
  starting transfers between devices  28.9 us (24%)
  waiting for transfers between devices  14 us (12%)
  local copies, waits for them, and re-layouts  3.49 us (3%)
  between operations  2.45 us (2%)
    pallas_call x9, Pallas kernels, phase(): pl.pallas_call(functools.partial(phase_kernel, spec), in_specs=specs, out...  61.7 us
    ppermute x25, starting transfers between devices, send(): return lax.ppermute(x, 'dp', pairs)  22.3 us
    ppermute x25, waiting for transfers between devices, send(): return lax.ppermute(x, 'dp', pairs)  12.6 us
    ppermute x6, starting transfers between devices, exchange(): lax.ppermute(x, 'dp', [(d, d ^ mask) for d in range(devices)])  6.66 us
    pallas_call x1, Pallas kernels, prepared(): pl.pallas_call(functools.partial(prep_kernel, spans, rows), in_specs=[sme...  3.96 us
    unnamed x8, local copies, waits for them, and re-layouts  3.49 us
    pallas_call x1, Pallas kernels, scaled(): pl.pallas_call(functools.partial(scale_kernel, parts), in_specs=[vmem, vm...  2.96 us
  transfers between devices with their start and end apart: 31, of which 13 were waited for; matrix products, arithmetic and copies ran while one was open for 0% of the time, Pallas kernels for 53%

profile of v16, /device:TPU:0, one launch (start us, length us, event | category | flops | bytes accessed | tf_op | source)
XLA Modules:
  0.0 119.5 jit_solution(15110548691951577272)
XLA Ops:
  0.6 3.1 %collective-permute-start.1 = (bf16[144,4096]{1,0:T(8,128)(2,1)}, bf16[144,4096]{1,0:T(8,128)(2,1)S(1)}, u32[]{:S(2)}, u32[]{:S(2)}) collective-permute-start(bf16[144,4096]{1,0:T(8,128)(2,1)} %grad_ref.1), channel_id=1, source_target_pairs={{0,4},{1,3},{4,8},{5,1},{8,12},{9,5},{12,14},{13,9},{14,10},{15,13... | collective-permute-start | bytes 3538952 | tf_op jit(solution)/shard_map/ppermute | solution.py:433
  5.0 0.7 copy-done.1
  5.7 4.0 %prep.1 = (bf16[144,4096]{1,0:T(8,128)(2,1)S(1)}, bf16[144,2048]{1,0:T(8,128)(2,1)S(1)}, bf16[144,2048]{1,0:T(8,128)(2,1)S(1)}, s32[8,128]{1,0:T(8,128)S(1)}, bf...) custom-call(s32[16,16]{1,0:T(8,128)S(1)} %copy-done.1, ...), custom_call_target="tpu_custom_call" | custom-call | flops 1 | bytes 1 | tf_op jit(solution)/shard_map/prep/pallas_call | solution.py:121
  9.7 0.1 collective-permute-start.2
  9.8 0.5 collective-permute-start.3
  10.2 0.7 collective-permute-start.7
  10.9 1.0 collective-permute-start
  12.0 0.6 collective-permute-done.3.refs_8_
  12.6 2.8 %copy-done = bf16[768,4096]{1,0:T(8,128)(2,1)S(1)} copy-done((bf16[768,4096]{1,0:T(8,128)(2,1)S(1)}, bf16[768,4096]{1,0:T(8,128)(2,1)}, u32[]{:S(2)}) %copy-start) | copy-done | bytes 6291480
  15.4 7.2 %phase_w_whole.5 = (f32[768,4096]{1,0:T(8,128)S(1)}, bf16[2304,768]{1,0:T(8,128)(2,1)}, f32[8,128]{1,0:T(8,128)S(1)}) custom-call(s32[16,16]{1,0:T(8,128)S(1)} %copy-done.1, s32[1]{0:T(128)} %bitcast.me_ref.refs_1_, s32[1]{0:T(128)S(6)} %copy.46.heads_ref.refs_2_, bf16[768,288]{1,0:T(8,128)(2,1)S(1)} %get-tuple-element.49.refs_3_, ...), custom_call_target="tpu_custom_call" | custom-call | flops 1 | bytes 1 | tf_op jit(solution)/shard_map/phase_w_whole/pallas_call | solution.py:303
  22.6 0.4 collective-permute-done.count_ref
  23.0 0.7 arrived.2.x_ref
  23.6 0.1 split.7
  23.8 0.1 collective-permute-start.5
  23.8 2.5 %collective-permute-start.4 = (bf16[144,4096]{1,0:T(8,128)(2,1)S(1)}, bf16[144,4096]{1,0:T(8,128)(2,1)S(1)}, u32[]{:S(2)}, u32[]{:S(2)}) collective-permute-start(bf16[144,4096]{1,0:T(8,128)(2,1)S(1)} %arrived.2.x_ref), channel_id=1, source_target_pairs={{0,4},{1,3},{4,8},{5,1},{8,12},{9,5},{12,14},{13,9},{14,10},{15,13... | collective-permute-start | bytes 3538952 | tf_op jit(solution)/shard_map/ppermute | solution.py:433
  26.4 2.2 %collective-permute-start.6 = (s32[8,128]{1,0:T(8,128)S(1)}, s32[8,128]{1,0:T(8,128)S(1)}, u32[]{:S(2)}, u32[]{:S(2)}) collective-permute-start(s32[8,128]{1,0:T(8,128)S(1)} %get-tuple-element.48), channel_id=1, source_target_pairs={{0,3},{1,4},{4,1},{5,8},{8,5},{9,12},{12,9},{13,14},{14,13},{15,10... | collective-permute-start | bytes 12296 | tf_op jit(solution)/shard_map/ppermute | solution.py:433
  28.5 4.2 %collective-permute-done.6.count_ref = s32[8,128]{1,0:T(8,128)S(1)} collective-permute-done((s32[8,128]{1,0:T(8,128)S(1)}, s32[8,128]{1,0:T(8,128)S(1)}, u32[]{:S(2)}, u32[]{:S(2)}) %collective-permute-start.6) | collective-permute-done | bytes 4128 | tf_op jit(solution)/shard_map/ppermute | solution.py:433
  32.8 0.7 arrived.3.x_ref
  33.4 0.1 split.8
  33.5 3.0 %collective-permute-start.13 = (bf16[144,4096]{1,0:T(8,128)(2,1)S(1)}, bf16[144,4096]{1,0:T(8,128)(2,1)S(1)}, u32[]{:S(2)}, u32[]{:S(2)}) collective-permute-start(bf16[144,4096]{1,0:T(8,128)(2,1)S(1)} %arrived.3.x_ref), channel_id=1, source_target_pairs={{0,4},{1,3},{4,8},{5,1},{8,12},{9,5},{12,14},{13,9},{14,10},{15,13... | collective-permute-start | bytes 3538952 | tf_op jit(solution)/shard_map/ppermute | solution.py:433
  36.5 0.5 collective-permute-start.8
  37.1 1.5 %collective-permute-done.9.refs_10_ = bf16[144,2048]{1,0:T(8,128)(2,1)S(1)} collective-permute-done((bf16[144,2048]{1,0:T(8,128)(2,1)S(1)}, bf16[144,2048]{1,0:T(8,128)(2,1)S(1)}, u32[]{:S(2)}, u32[]{:S(2)}) %collective-permute-start.9) | collective-permute-done | bytes 589856 | tf_op jit(solution)/shard_map/ppermute | solution.py:433
  38.5 0.8 collective-permute-done.8.refs_8_
  39.4 0.8 collective-permute-done.10.refs_12_
  40.2 12.1 %phase_w_whole.6 = (f32[768,4096]{1,0:T(8,128)S(1)}, bf16[2304,768]{1,0:T(8,128)(2,1)}, f32[8,128]{1,0:T(8,128)S(1)}) custom-call(s32[16,16]{1,0:T(8,128)S(1)} %copy-done.1, s32[1]{0:T(128)} %bitcast.me_ref.refs_1_, s32[1]{0:T(128)S(6)} %copy.46.heads_ref.refs_2_, ...), custom_call_target="tpu_custom_call", output_to_operand_aliasing={{0}: (13, {}), {1}: (14, {})} | custom-call | flops 1 | bytes 1 | tf_op jit(solution)/shard_map/phase_w_whole/pallas_call | solution.py:303
  52.4 1.6 %collective-permute-start.11 = (bf16[144,4096]{1,0:T(8,128)(2,1)S(1)}, bf16[144,4096]{1,0:T(8,128)(2,1)S(1)}, u32[]{:S(2)}, u32[]{:S(2)}) collective-permute-start(bf16[144,4096]{1,0:T(8,128)(2,1)S(1)} %after.6.x_ref), channel_id=1, source_target_pairs={{0,4},{1,3},{4,8},{5,1},{8,12},{9,5},{12,14},{13,9},{14,10},{15,13... | collective-permute-start | bytes 3538952 | tf_op jit(solution)/shard_map/ppermute | solution.py:433
  54.0 0.1 split.9
  54.1 0.1 collective-permute-start.12
  54.2 0.5 collective-permute-start.15
  54.7 1.4 %collective-permute-done.13.refs_0_ = bf16[144,4096]{1,0:T(8,128)(2,1)S(1)} collective-permute-done((bf16[144,4096]{1,0:T(8,128)(2,1)S(1)}, bf16[144,4096]{1,0:T(8,128)(2,1)S(1)}, u32[]{:S(2)}, u32[]{:S(2)}) %collective-permute-start.13) | collective-permute-done | bytes 1179680 | tf_op jit(solution)/shard_map/ppermute | solution.py:433
  56.1 0.1 split.10
  56.2 0.1 collective-permute-start.14
  56.2 0.5 collective-permute-start.16
  56.7 2.1 %collective-permute-start.18 = (bf16[144,4096]{1,0:T(8,128)(2,1)S(1)}, bf16[144,4096]{1,0:T(8,128)(2,1)S(1)}, u32[]{:S(2)}, u32[]{:S(2)}) collective-permute-start(bf16[144,4096]{1,0:T(8,128)(2,1)S(1)} %after.7.x_ref), channel_id=1, source_target_pairs={{0,4},{1,3},{4,8},{5,1},{8,12},{9,5},{12,14},{13,9},{14,10},{15,13... | collective-permute-start | bytes 3538952 | tf_op jit(solution)/shard_map/ppermute | solution.py:433
  58.8 0.2 collective-permute-done.16.refs_12_
  59.1 12.1 %phase_w_whole.7 = (f32[768,4096]{1,0:T(8,128)S(1)}, bf16[2304,768]{1,0:T(8,128)(2,1)}, f32[8,128]{1,0:T(8,128)S(1)}) custom-call(s32[16,16]{1,0:T(8,128)S(1)} %copy-done.1, s32[1]{0:T(128)} %bitcast.me_ref.refs_1_, s32[1]{0:T(128)S(6)} %copy.46.heads_ref.refs_2_, ...), custom_call_target="tpu_custom_call", output_to_operand_aliasing={{0}: (13, {}), {1}: (14, {})} | custom-call | flops 1 | bytes 1 | tf_op jit(solution)/shard_map/phase_w_whole/pallas_call | solution.py:303
  71.2 0.1 split.11
  71.3 0.2 collective-permute-start.19
  71.5 0.4 collective-permute-start.20
  71.9 2.1 %collective-permute-start.17 = (bf16[144,4096]{1,0:T(8,128)(2,1)S(1)}, bf16[144,4096]{1,0:T(8,128)(2,1)S(1)}, u32[]{:S(2)}, u32[]{:S(2)}) collective-permute-start(bf16[144,4096]{1,0:T(8,128)(2,1)S(1)} %after.8.x_ref), channel_id=1, source_target_pairs={{0,4},{1,3},{4,8},{5,1},{8,12},{9,5},{12,14},{13,9},{14,10},{15,13... | collective-permute-start | bytes 3538952 | tf_op jit(solution)/shard_map/ppermute | solution.py:433
  74.0 0.3 collective-permute-done.20.refs_8_
  74.2 8.4 %phase_w_whole.8 = (f32[768,4096]{1,0:T(8,128)S(1)}, bf16[2304,768]{1,0:T(8,128)(2,1)}, f32[8,128]{1,0:T(8,128)S(1)}) custom-call(s32[16,16]{1,0:T(8,128)S(1)} %copy-done.1, s32[1]{0:T(128)} %bitcast.me_ref.refs_1_, s32[1]{0:T(128)S(6)} %copy.46.heads_ref.refs_2_, ...), custom_call_target="tpu_custom_call", output_to_operand_aliasing={{0}: (9, {}), {1}: (10, {})} | custom-call | flops 1 | bytes 1 | tf_op jit(solution)/shard_map/phase_w_whole/pallas_call | solution.py:303
  82.7 0.1 split.12
  82.8 0.2 collective-permute-start.21
  83.0 0.4 collective-permute-start.22
  83.4 1.5 %collective-permute-done.21.refs_6_ = bf16[144,2048]{1,0:T(8,128)(2,1)S(1)} collective-permute-done((bf16[144,2048]{1,0:T(8,128)(2,1)S(1)}, bf16[144,2048]{1,0:T(8,128)(2,1)S(1)}, u32[]{:S(2)}, u32[]{:S(2)}) %collective-permute-start.21) | collective-permute-done | bytes 589856 | tf_op jit(solution)/shard_map/ppermute | solution.py:433
  84.9 0.8 collective-permute-done.22.refs_8_
  85.7 8.4 %phase_w_whole.9 = (f32[768,4096]{1,0:T(8,128)S(1)}, bf16[2304,768]{1,0:T(8,128)(2,1)}, f32[8,128]{1,0:T(8,128)S(1)}) custom-call(s32[16,16]{1,0:T(8,128)S(1)} %copy-done.1, s32[1]{0:T(128)} %bitcast.me_ref.refs_1_, s32[1]{0:T(128)S(6)} %copy.46.heads_ref.refs_2_, ...), custom_call_target="tpu_custom_call", output_to_operand_aliasing={{0}: (9, {}), {1}: (10, {})} | custom-call | flops 1 | bytes 1 | tf_op jit(solution)/shard_map/phase_w_whole/pallas_call | solution.py:303
  94.2 0.1 split.13
  94.3 0.2 collective-permute-start.24
  94.5 0.4 collective-permute-start.23
  94.9 3.9 %phase_w_None.2 = (f32[768,4096]{1,0:T(8,128)S(1)}, f32[8,128]{1,0:T(8,128)}) custom-call(s32[16,16]{1,0:T(8,128)S(1)} %copy-done.1, s32[1]{0:T(128)} %bitcast.me_ref.refs_1_, s32[1]{0:T(128)S(6)} %copy.46.heads_ref.refs_2_, bf16[768,144]{1,0:T(8,128)(2,1)S(1)} %get-tuple-element.88.refs_3_, ...), custom_call_target="tpu_custom_call", output_to_operand_aliasing={{0}: (6, {})} | custom-call | flops 1 | bytes 1 | tf_op jit(solution)/shard_map/phase_w_None/pallas_call | solution.py:303
  98.9 0.0 slice-start
  98.9 3.8 %phase_w_None.3 = (f32[768,4096]{1,0:T(8,128)S(1)}, f32[8,128]{1,0:T(8,128)S(1)}) custom-call(s32[16,16]{1,0:T(8,128)S(1)} %copy-done.1, s32[1]{0:T(128)} %bitcast.me_ref.refs_1_, s32[1]{0:T(128)S(6)} %copy.46.heads_ref.refs_2_, bf16[768,144]{1,0:T(8,128)(2,1)S(1)} %get-tuple-element.87.refs_3_, ...), custom_call_target="tpu_custom_call", output_to_operand_aliasing={{0}: (6, {})} | custom-call | flops 1 | bytes 1 | tf_op jit(solution)/shard_map/phase_w_None/pallas_call | solution.py:303
  102.7 1.8 %collective-permute-start.27 = (f32[8,128]{1,0:T(8,128)S(1)}, f32[8,128]{1,0:T(8,128)S(1)}, u32[]{:S(2)}, u32[]{:S(2)}) collective-permute-start(f32[8,128]{1,0:T(8,128)S(1)} %get-tuple-element.92), channel_id=1, source_target_pairs={{0,3},{1,2},{2,1},{3,0},{4,7},{5,6},{6,5},{7,4},{8,11},{9,10},{10,... | collective-permute-start | bytes 12296 | tf_op jit(solution)/shard_map/ppermute | solution.py:413
  104.5 0.3 collective-permute-start.26
  104.9 0.0 collective-permute-start.25
  104.9 2.9 %phase__first.1 = (f32[288,768]{1,0:T(8,128)S(1)}, f32[8,128]{1,0:T(8,128)S(1)}) custom-call(s32[16,16]{1,0:T(8,128)S(1)} %copy-done.1, s32[1]{0:T(128)} %bitcast.me_ref.refs_1_, s32[1]{0:T(128)S(6)} %copy.46.heads_ref.refs_2_, bf16[768,4096]{1,0:T(8,128)(2,1)S(1)} %bitcast.2, bf16[144,2048]{1,0:T(8,128)(2,1)S(1)} %get-tuple-element.83.refs_4_, ...), custom_call_target="tpu_custom_call" | custom-call | flops 1 | bytes 1 | tf_op jit(solution)/shard_map/phase__first/pallas_call | solution.py:303
  107.9 0.3 collective-permute-done.26
  108.2 3.7 %collective-permute-start.30 = (f32[8,128]{1,0:T(8,128)S(1)}, f32[8,128]{1,0:T(8,128)S(1)}, u32[]{:S(2)}, u32[]{:S(2)}) collective-permute-start(f32[8,128]{1,0:T(8,128)S(1)} %after.11), channel_id=1, source_target_pairs={{0,12},{1,13},{2,14},{3,15},{4,8},{5,9},{6,10},{7,11},{8,4},{9,5},... | collective-permute-start | bytes 12296 | tf_op jit(solution)/shard_map/ppermute | solution.py:413
  111.9 0.8 collective-permute-start.28
  112.6 2.7 %phase__last.1 = (bf16[2304,768]{1,0:T(8,128)(2,1)}, f32[8,128]{1,0:T(8,128)}) custom-call(s32[16,16]{1,0:T(8,128)S(1)} %copy-done.1, s32[1]{0:T(128)} %bitcast.me_ref.refs_1_, s32[1]{0:T(128)S(6)} %copy.46.heads_ref.refs_2_, bf16[768,4096]{1,0:T(8,128)(2,1)S(1)} %bitcast.2, ...), custom_call_target="tpu_custom_call", output_to_operand_aliasing={{0}: (7, {})} | custom-call | flops 1 | bytes 1 | tf_op jit(solution)/shard_map/phase__last/pallas_call | solution.py:303
  115.4 1.0 collective-permute-done.29
  116.4 3.0 %scale.1 = bf16[768,4096]{1,0:T(8,128)(2,1)} custom-call(f32[768,4096]{1,0:T(8,128)S(1)} %get-tuple-element.91.w_ref, f32[8,128]{1,0:T(8,128)S(1)} %add_add_fusion.squares_ref), custom_call_target="tpu_custom_call" | custom-call | flops 3145728 | bytes 6291456 | tf_op jit(solution)/shard_map/scale/pallas_call | solution.py:343
  (35 shorter events, 0.1 us)
Async XLA Ops:
  0.6 22.4 %collective-permute-start.1 = (bf16[144,4096]{1,0:T(8,128)(2,1)}, bf16[144,4096]{1,0:T(8,128)(2,1)S(1)}, u32[]{:S(2)}, u32[]{:S(2)}) collective-permute-start(bf16[144,4096]{1,0:T(8,128)(2,1)} %grad_ref.1), channel_id=1, source_target_pairs={{0,4},{1,3},{4,8},{5,1},{8,12},{9,5},{12,14},{13,9},{14,10},{15,13... | collective-permute-start | bytes 3538952 | tf_op jit(solution)/shard_map/ppermute | solution.py:433
  5.0 0.7 copy-start.1
  9.7 2.3 %collective-permute-start.2 = (bf16[144,2048]{1,0:T(8,128)(2,1)S(1)}, bf16[144,2048]{1,0:T(8,128)(2,1)S(1)}, u32[]{:S(2)}, u32[]{:S(2)}) collective-permute-start(bf16[144,2048]{1,0:T(8,128)(2,1)S(1)} %get-tuple-element.50.refs_5_), channel_id=1, source_target_pairs={{0,1},{1,0},{2,3},{3,2},{4,5},{5,4},{6,7},{7,6},{8,9},{9,8},{10,11... | collective-permute-start | bytes 1769480 | tf_op jit(solution)/shard_map/ppermute | solution.py:433
  9.8 2.8 %collective-permute-start.3 = (bf16[144,2048]{1,0:T(8,128)(2,1)S(1)}, bf16[144,2048]{1,0:T(8,128)(2,1)S(1)}, u32[]{:S(2)}, u32[]{:S(2)}) collective-permute-start(bf16[144,2048]{1,0:T(8,128)(2,1)S(1)} %get-tuple-element.51.refs_7_), channel_id=1, source_target_pairs={{0,1},{1,0},{2,3},{3,2},{4,5},{5,4},{6,7},{7,6},{8,9},{9,8},{10,11... | collective-permute-start | bytes 1769480 | tf_op jit(solution)/shard_map/ppermute | solution.py:433
  10.2 22.5 %collective-permute-start.7 = (bf16[144,4096]{1,0:T(8,128)(2,1)S(1)}, bf16[144,4096]{1,0:T(8,128)(2,1)S(1)}, u32[]{:S(2)}, u32[]{:S(2)}) collective-permute-start(bf16[144,4096]{1,0:T(8,128)(2,1)S(1)} %get-tuple-element.55), channel_id=1, source_target_pairs={{0,3},{1,4},{4,1},{5,8},{8,5},{9,12},{12,9},{13,14},{14,13},{15,10... | collective-permute-start | bytes 3538952 | tf_op jit(solution)/shard_map/ppermute | solution.py:433
  10.9 12.1 %collective-permute-start = (s32[8,128]{1,0:T(8,128)S(1)}, s32[8,128]{1,0:T(8,128)S(1)}, u32[]{:S(2)}, u32[]{:S(2)}) collective-permute-start(s32[8,128]{1,0:T(8,128)S(1)} %get-tuple-element.48), channel_id=1, source_target_pairs={{0,4},{1,3},{4,8},{5,1},{8,12},{9,5},{12,14},{13,9},{14,10},{15,13... | collective-permute-start | bytes 12296 | tf_op jit(solution)/shard_map/ppermute | solution.py:433
  12.6 2.8 %copy-start = (bf16[768,4096]{1,0:T(8,128)(2,1)S(1)}, bf16[768,4096]{1,0:T(8,128)(2,1)}, u32[]{:S(2)}) copy-start(bf16[768,4096]{1,0:T(8,128)(2,1)} %refs_3_.3) | copy-start | bytes 18874372
  23.8 13.3 %collective-permute-start.5 = (bf16[144,2048]{1,0:T(8,128)(2,1)S(1)}, bf16[144,2048]{1,0:T(8,128)(2,1)S(1)}, u32[]{:S(2)}, u32[]{:S(2)}) collective-permute-start(bf16[144,2048]{1,0:T(8,128)(2,1)S(1)} %get-tuple-element.54.refs_5_), channel_id=1, source_target_pairs={{0,1},{1,0},{2,3},{3,2},{4,5},{5,4},{6,7},{7,6},{8,9},{9,8},{10,11... | collective-permute-start | bytes 1769480 | tf_op jit(solution)/shard_map/ppermute | solution.py:433
  23.8 28.5 %collective-permute-start.4 = (bf16[144,4096]{1,0:T(8,128)(2,1)S(1)}, bf16[144,4096]{1,0:T(8,128)(2,1)S(1)}, u32[]{:S(2)}, u32[]{:S(2)}) collective-permute-start(bf16[144,4096]{1,0:T(8,128)(2,1)S(1)} %arrived.2.x_ref), channel_id=1, source_target_pairs={{0,4},{1,3},{4,8},{5,1},{8,12},{9,5},{12,14},{13,9},{14,10},{15,13... | collective-permute-start | bytes 3538952 | tf_op jit(solution)/shard_map/ppermute | solution.py:433
  26.4 6.4 %collective-permute-start.6 = (s32[8,128]{1,0:T(8,128)S(1)}, s32[8,128]{1,0:T(8,128)S(1)}, u32[]{:S(2)}, u32[]{:S(2)}) collective-permute-start(s32[8,128]{1,0:T(8,128)S(1)} %get-tuple-element.48), channel_id=1, source_target_pairs={{0,3},{1,4},{4,1},{5,8},{8,5},{9,12},{12,9},{13,14},{14,13},{15,10... | collective-permute-start | bytes 12296 | tf_op jit(solution)/shard_map/ppermute | solution.py:433
  33.5 22.5 %collective-permute-start.13 = (bf16[144,4096]{1,0:T(8,128)(2,1)S(1)}, bf16[144,4096]{1,0:T(8,128)(2,1)S(1)}, u32[]{:S(2)}, u32[]{:S(2)}) collective-permute-start(bf16[144,4096]{1,0:T(8,128)(2,1)S(1)} %arrived.3.x_ref), channel_id=1, source_target_pairs={{0,4},{1,3},{4,8},{5,1},{8,12},{9,5},{12,14},{13,9},{14,10},{15,13... | collective-permute-start | bytes 3538952 | tf_op jit(solution)/shard_map/ppermute | solution.py:433
  36.5 2.0 %collective-permute-start.9 = (bf16[144,2048]{1,0:T(8,128)(2,1)S(1)}, bf16[144,2048]{1,0:T(8,128)(2,1)S(1)}, u32[]{:S(2)}, u32[]{:S(2)}) collective-permute-start(bf16[144,2048]{1,0:T(8,128)(2,1)S(1)} %get-tuple-element.57.refs_9_), channel_id=1, source_target_pairs={{0,1},{1,0},{2,3},{3,2},{4,5},{5,4},{6,7},{7,6},{8,9},{9,8},{10,11... | collective-permute-start | bytes 1769480 | tf_op jit(solution)/shard_map/ppermute | solution.py:433
  36.5 2.8 %collective-permute-start.8 = (bf16[144,2048]{1,0:T(8,128)(2,1)S(1)}, bf16[144,2048]{1,0:T(8,128)(2,1)S(1)}, u32[]{:S(2)}, u32[]{:S(2)}) collective-permute-start(bf16[144,2048]{1,0:T(8,128)(2,1)S(1)} %get-tuple-element.56.refs_7_), channel_id=1, source_target_pairs={{0,1},{1,0},{2,3},{3,2},{4,5},{5,4},{6,7},{7,6},{8,9},{9,8},{10,11... | collective-permute-start | bytes 1769480 | tf_op jit(solution)/shard_map/ppermute | solution.py:433
  37.0 3.2 %collective-permute-start.10 = (bf16[144,2048]{1,0:T(8,128)(2,1)S(1)}, bf16[144,2048]{1,0:T(8,128)(2,1)S(1)}, u32[]{:S(2)}, u32[]{:S(2)}) collective-permute-start(bf16[144,2048]{1,0:T(8,128)(2,1)S(1)} %get-tuple-element.58.refs_11_), channel_id=1, source_target_pairs={{0,1},{1,0},{2,3},{3,2},{4,5},{5,4},{6,7},{7,6},{8,9},{9,8},{10,11... | collective-permute-start | bytes 1769480 | tf_op jit(solution)/shard_map/ppermute | solution.py:433
  52.4 18.8 %collective-permute-start.11 = (bf16[144,4096]{1,0:T(8,128)(2,1)S(1)}, bf16[144,4096]{1,0:T(8,128)(2,1)S(1)}, u32[]{:S(2)}, u32[]{:S(2)}) collective-permute-start(bf16[144,4096]{1,0:T(8,128)(2,1)S(1)} %after.6.x_ref), channel_id=1, source_target_pairs={{0,4},{1,3},{4,8},{5,1},{8,12},{9,5},{12,14},{13,9},{14,10},{15,13... | collective-permute-start | bytes 3538952 | tf_op jit(solution)/shard_map/ppermute | solution.py:433
  54.1 2.6 %collective-permute-start.12 = (bf16[144,2048]{1,0:T(8,128)(2,1)S(1)}, bf16[144,2048]{1,0:T(8,128)(2,1)S(1)}, u32[]{:S(2)}, u32[]{:S(2)}) collective-permute-start(bf16[144,2048]{1,0:T(8,128)(2,1)S(1)} %get-tuple-element.63.refs_5_), channel_id=1, source_target_pairs={{0,1},{1,0},{2,3},{3,2},{4,5},{5,4},{6,7},{7,6},{8,9},{9,8},{10,11... | collective-permute-start | bytes 1769480 | tf_op jit(solution)/shard_map/ppermute | solution.py:433
  54.2 4.6 %collective-permute-start.15 = (bf16[144,2048]{1,0:T(8,128)(2,1)S(1)}, bf16[144,2048]{1,0:T(8,128)(2,1)S(1)}, u32[]{:S(2)}, u32[]{:S(2)}) collective-permute-start(bf16[144,2048]{1,0:T(8,128)(2,1)S(1)} %get-tuple-element.65.refs_9_), channel_id=1, source_target_pairs={{0,1},{1,0},{2,3},{3,2},{4,5},{5,4},{6,7},{7,6},{8,9},{9,8},{10,11... | collective-permute-start | bytes 1769480 | tf_op jit(solution)/shard_map/ppermute | solution.py:433
  56.2 2.7 %collective-permute-start.14 = (bf16[144,2048]{1,0:T(8,128)(2,1)S(1)}, bf16[144,2048]{1,0:T(8,128)(2,1)S(1)}, u32[]{:S(2)}, u32[]{:S(2)}) collective-permute-start(bf16[144,2048]{1,0:T(8,128)(2,1)S(1)} %get-tuple-element.64.refs_7_), channel_id=1, source_target_pairs={{0,1},{1,0},{2,3},{3,2},{4,5},{5,4},{6,7},{7,6},{8,9},{9,8},{10,11... | collective-permute-start | bytes 1769480 | tf_op jit(solution)/shard_map/ppermute | solution.py:433
  56.2 2.8 %collective-permute-start.16 = (bf16[144,2048]{1,0:T(8,128)(2,1)S(1)}, bf16[144,2048]{1,0:T(8,128)(2,1)S(1)}, u32[]{:S(2)}, u32[]{:S(2)}) collective-permute-start(bf16[144,2048]{1,0:T(8,128)(2,1)S(1)} %get-tuple-element.66.refs_11_), channel_id=1, source_target_pairs={{0,1},{1,0},{2,3},{3,2},{4,5},{5,4},{6,7},{7,6},{8,9},{9,8},{10,11... | collective-permute-start | bytes 1769480 | tf_op jit(solution)/shard_map/ppermute | solution.py:433
  56.7 25.9 %collective-permute-start.18 = (bf16[144,4096]{1,0:T(8,128)(2,1)S(1)}, bf16[144,4096]{1,0:T(8,128)(2,1)S(1)}, u32[]{:S(2)}, u32[]{:S(2)}) collective-permute-start(bf16[144,4096]{1,0:T(8,128)(2,1)S(1)} %after.7.x_ref), channel_id=1, source_target_pairs={{0,4},{1,3},{4,8},{5,1},{8,12},{9,5},{12,14},{13,9},{14,10},{15,13... | collective-permute-start | bytes 3538952 | tf_op jit(solution)/shard_map/ppermute | solution.py:433
  71.3 2.7 %collective-permute-start.19 = (bf16[144,2048]{1,0:T(8,128)(2,1)S(1)}, bf16[144,2048]{1,0:T(8,128)(2,1)S(1)}, u32[]{:S(2)}, u32[]{:S(2)}) collective-permute-start(bf16[144,2048]{1,0:T(8,128)(2,1)S(1)} %get-tuple-element.72.refs_5_), channel_id=1, source_target_pairs={{0,1},{1,0},{2,3},{3,2},{4,5},{5,4},{6,7},{7,6},{8,9},{9,8},{10,11... | collective-permute-start | bytes 1769480 | tf_op jit(solution)/shard_map/ppermute | solution.py:433
  71.5 2.7 %collective-permute-start.20 = (bf16[144,2048]{1,0:T(8,128)(2,1)S(1)}, bf16[144,2048]{1,0:T(8,128)(2,1)S(1)}, u32[]{:S(2)}, u32[]{:S(2)}) collective-permute-start(bf16[144,2048]{1,0:T(8,128)(2,1)S(1)} %get-tuple-element.73.refs_7_), channel_id=1, source_target_pairs={{0,1},{1,0},{2,3},{3,2},{4,5},{5,4},{6,7},{7,6},{8,9},{9,8},{10,11... | collective-permute-start | bytes 1769480 | tf_op jit(solution)/shard_map/ppermute | solution.py:433
  71.9 22.3 %collective-permute-start.17 = (bf16[144,4096]{1,0:T(8,128)(2,1)S(1)}, bf16[144,4096]{1,0:T(8,128)(2,1)S(1)}, u32[]{:S(2)}, u32[]{:S(2)}) collective-permute-start(bf16[144,4096]{1,0:T(8,128)(2,1)S(1)} %after.8.x_ref), channel_id=1, source_target_pairs={{0,4},{1,3},{4,8},{5,1},{8,12},{9,5},{12,14},{13,9},{14,10},{15,13... | collective-permute-start | bytes 3538952 | tf_op jit(solution)/shard_map/ppermute | solution.py:433
  82.8 2.1 %collective-permute-start.21 = (bf16[144,2048]{1,0:T(8,128)(2,1)S(1)}, bf16[144,2048]{1,0:T(8,128)(2,1)S(1)}, u32[]{:S(2)}, u32[]{:S(2)}) collective-permute-start(bf16[144,2048]{1,0:T(8,128)(2,1)S(1)} %get-tuple-element.77.refs_5_), channel_id=1, source_target_pairs={{0,1},{1,0},{2,3},{3,2},{4,5},{5,4},{6,7},{7,6},{8,9},{9,8},{10,11... | collective-permute-start | bytes 1769480 | tf_op jit(solution)/shard_map/ppermute | solution.py:433
  83.0 2.7 %collective-permute-start.22 = (bf16[144,2048]{1,0:T(8,128)(2,1)S(1)}, bf16[144,2048]{1,0:T(8,128)(2,1)S(1)}, u32[]{:S(2)}, u32[]{:S(2)}) collective-permute-start(bf16[144,2048]{1,0:T(8,128)(2,1)S(1)} %get-tuple-element.78.refs_7_), channel_id=1, source_target_pairs={{0,1},{1,0},{2,3},{3,2},{4,5},{5,4},{6,7},{7,6},{8,9},{9,8},{10,11... | collective-permute-start | bytes 1769480 | tf_op jit(solution)/shard_map/ppermute | solution.py:433
  94.3 4.5 %collective-permute-start.24 = (bf16[144,2048]{1,0:T(8,128)(2,1)S(1)}, bf16[144,2048]{1,0:T(8,128)(2,1)S(1)}, u32[]{:S(2)}, u32[]{:S(2)}) collective-permute-start(bf16[144,2048]{1,0:T(8,128)(2,1)S(1)} %get-tuple-element.83.refs_4_), channel_id=1, source_target_pairs={{0,1},{1,0},{2,3},{3,2},{4,5},{5,4},{6,7},{7,6},{8,9},{9,8},{10,11... | collective-permute-start | bytes 1769480 | tf_op jit(solution)/shard_map/ppermute | solution.py:433
  94.5 4.3 %collective-permute-start.23 = (bf16[144,2048]{1,0:T(8,128)(2,1)S(1)}, bf16[144,2048]{1,0:T(8,128)(2,1)S(1)}, u32[]{:S(2)}, u32[]{:S(2)}) collective-permute-start(bf16[144,2048]{1,0:T(8,128)(2,1)S(1)} %get-tuple-element.82.refs_6_.refs_4_.refs_5_), channel_id=1, source_target_pairs={{0,1},{1,0},{2,3},{3,2},{4,5},{5,4},{6,7},{7,6},{8,9},{9,8},{10,11... | collective-permute-start | bytes 1769480 | tf_op jit(solution)/shard_map/ppermute | solution.py:433
  98.9 6.1 %slice-start = ((s8[6291456]{0:T(1024)(128)(4,1)}), s8[4194304]{0:T(1024)(128)(4,1)S(1)}, s32[]{:S(2)}) async-start(s8[6291456]{0:T(1024)(128)(4,1)} %bitcast.1), calls=%async_computation | async-start | bytes 8388608
  98.9 6.0 %slice-start.1 = ((s8[6291456]{0:T(1024)(128)(4,1)}), s8[2097152]{0:T(1024)(128)(4,1)S(1)}, s32[]{:S(2)}) async-start(s8[6291456]{0:T(1024)(128)(4,1)} %bitcast.1), calls=%async_computation.1 | async-start | bytes 4194304
  102.7 5.1 %collective-permute-start.27 = (f32[8,128]{1,0:T(8,128)S(1)}, f32[8,128]{1,0:T(8,128)S(1)}, u32[]{:S(2)}, u32[]{:S(2)}) collective-permute-start(f32[8,128]{1,0:T(8,128)S(1)} %get-tuple-element.92), channel_id=1, source_target_pairs={{0,3},{1,2},{2,1},{3,0},{4,7},{5,6},{6,5},{7,4},{8,11},{9,10},{10,... | collective-permute-start | bytes 12296 | tf_op jit(solution)/shard_map/ppermute | solution.py:413
  104.5 3.6 %collective-permute-start.26 = (f32[8,128]{1,0:T(8,128)S(1)}, f32[8,128]{1,0:T(8,128)S(1)}, u32[]{:S(2)}, u32[]{:S(2)}) collective-permute-start(f32[8,128]{1,0:T(8,128)S(1)} %get-tuple-element.92), channel_id=1, source_target_pairs={{0,2},{1,3},{2,0},{3,1},{4,6},{5,7},{6,4},{7,5},{8,10},{9,11},{10,... | collective-permute-start | bytes 12296 | tf_op jit(solution)/shard_map/ppermute | solution.py:413
  104.9 3.3 %collective-permute-start.25 = (f32[8,128]{1,0:T(8,128)S(1)}, f32[8,128]{1,0:T(8,128)S(1)}, u32[]{:S(2)}, u32[]{:S(2)}) collective-permute-start(f32[8,128]{1,0:T(8,128)S(1)} %get-tuple-element.92), channel_id=1, source_target_pairs={{0,1},{1,0},{2,3},{3,2},{4,5},{5,4},{6,7},{7,6},{8,9},{9,8},{10,11... | collective-permute-start | bytes 12296 | tf_op jit(solution)/shard_map/ppermute | solution.py:413
  108.2 7.2 %collective-permute-start.30 = (f32[8,128]{1,0:T(8,128)S(1)}, f32[8,128]{1,0:T(8,128)S(1)}, u32[]{:S(2)}, u32[]{:S(2)}) collective-permute-start(f32[8,128]{1,0:T(8,128)S(1)} %after.11), channel_id=1, source_target_pairs={{0,12},{1,13},{2,14},{3,15},{4,8},{5,9},{6,10},{7,11},{8,4},{9,5},... | collective-permute-start | bytes 12296 | tf_op jit(solution)/shard_map/ppermute | solution.py:413
  111.9 4.5 %collective-permute-start.29 = (f32[8,128]{1,0:T(8,128)S(1)}, f32[8,128]{1,0:T(8,128)S(1)}, u32[]{:S(2)}, u32[]{:S(2)}) collective-permute-start(f32[8,128]{1,0:T(8,128)S(1)} %after.11), channel_id=1, source_target_pairs={{0,8},{1,9},{2,10},{3,11},{4,12},{5,13},{6,14},{7,15},{8,0},{9,1},... | collective-permute-start | bytes 12296 | tf_op jit(solution)/shard_map/ppermute | solution.py:413
  111.9 4.5 %collective-permute-start.28 = (f32[8,128]{1,0:T(8,128)S(1)}, f32[8,128]{1,0:T(8,128)S(1)}, u32[]{:S(2)}, u32[]{:S(2)}) collective-permute-start(f32[8,128]{1,0:T(8,128)S(1)} %after.11), channel_id=1, source_target_pairs={{0,4},{1,5},{2,6},{3,7},{4,0},{5,1},{6,2},{7,3},{8,12},{9,13},{10,... | collective-permute-start | bytes 12296 | tf_op jit(solution)/shard_map/ppermute | solution.py:413

commit v17 on v14

--- a/solution.py
+++ b/solution.py
@@ -70,19 +70,43 @@
             dead[...] = jnp.zeros_like(dead)
 
 
-def prep_kernel(
-    spans, rows, table_ref, me_ref, heads_ref, seqs_ref, grad_ref, a_ref, *refs
-):
-    copy_ref, left_ref, right_ref, count_ref, *at_refs, block_ref, sems, own_sems = refs
+def stage_kernel(me_ref, seqs_ref, grad_ref, copy_ref, left_ref, right_ref, count_ref, sems):
     half = left_ref.shape[1]
-    owns = [
-        pltpu.make_async_copy(grad_ref, copy_ref, own_sems.at[0]),
-        pltpu.make_async_copy(grad_ref.at[:, pl.ds(0, half)], left_ref, own_sems.at[1]),
-        pltpu.make_async_copy(grad_ref.at[:, pl.ds(half, half)], right_ref, own_sems.at[2]),
+    copies = [
+        pltpu.make_async_copy(grad_ref, copy_ref, sems.at[0]),
+        pltpu.make_async_copy(grad_ref.at[:, pl.ds(0, half)], left_ref, sems.at[1]),
+        pltpu.make_async_copy(grad_ref.at[:, pl.ds(half, half)], right_ref, sems.at[2]),
     ]
-    for copy in owns:
+    for copy in copies:
         copy.start()
     count_ref[...] = jnp.full(count_ref.shape, seqs_ref[0], jnp.int32)
+    for copy in copies:
+        copy.wait()
+    zero_dead(seqs_ref[0], left_ref)
+    zero_dead(seqs_ref[0], right_ref)
+
+
+def staged(me, seq_counts, out_grad):
+    rows, features = out_grad.shape
+    vmem = pl.BlockSpec(memory_space=pltpu.VMEM)
+    smem = pl.BlockSpec(memory_space=pltpu.SMEM)
+    outs = [(rows, features), (rows, features // 2), (rows, features // 2)]
+    shapes = [pltpu.VMEM(shape, jnp.bfloat16) for shape in outs]
+    copy, left, right, count = pl.pallas_call(
+        stage_kernel,
+        in_specs=[smem, smem, pl.BlockSpec(memory_space=pl.ANY)],
+        out_specs=[vmem] * 4,
+        out_shape=shapes + [pltpu.VMEM((8, 128), jnp.int32)],
+        scratch_shapes=[pltpu.SemaphoreType.DMA((3,))],
+        compiler_params=pltpu.CompilerParams(vmem_limit_bytes=2 * MIB),
+        cost_estimate=pl.CostEstimate(flops=1, bytes_accessed=1, transcendentals=0),
+        name="stage",
+    )(me, seq_counts, pltpu.with_memory_space_constraint(out_grad, pltpu.HBM))
+    return copy, (left, right), count
+
+
+def prep_kernel(spans, rows, table_ref, me_ref, heads_ref, _, a_ref, *refs):
+    *at_refs, block_ref, sems = refs
     width = heads_ref[0] * HEAD_DIM
     copies = []
     for i in range(block_ref.shape[0] // rows):
@@ -103,41 +127,29 @@
         block = block_ref[begin * rows : (begin + count) * rows, :]
         column = lax.broadcasted_iota(jnp.int32, block.shape, 1)
         at_ref[...] = jnp.where(column < width, block, jnp.zeros_like(block)).T
-    for copy in owns:
-        copy.wait()
-    zero_dead(seqs_ref[0], left_ref)
-    zero_dead(seqs_ref[0], right_ref)
-
-
-def prepared(where, seq_counts, out_grad, attn_out, spans):
+
+
+def prepared(where, count, attn_out, spans, rows):
     slots, capacity = attn_out.shape
-    rows, features = out_grad.shape
     vmem = pl.BlockSpec(memory_space=pltpu.VMEM)
     smem = pl.BlockSpec(memory_space=pltpu.SMEM)
-    outs = [(rows, features), (rows, features // 2), (rows, features // 2)]
-    outs += [(capacity, count * rows) for _, count in spans]
-    shapes = [pltpu.VMEM(shape, jnp.bfloat16) for shape in outs]
-    shapes.insert(3, pltpu.VMEM((8, 128), jnp.int32))
-    copy, left, right, count, *ats = pl.pallas_call(
+    return pl.pallas_call(
         functools.partial(prep_kernel, spans, rows),
-        in_specs=[smem] * 4 + [pl.BlockSpec(memory_space=pl.ANY)] * 2,
-        out_specs=[vmem] * len(shapes),
-        out_shape=shapes,
+        in_specs=[smem] * 3 + [vmem, pl.BlockSpec(memory_space=pl.ANY)],
+        out_specs=[vmem] * len(spans),
+        out_shape=[pltpu.VMEM((capacity, n * rows), jnp.bfloat16) for _, n in spans],
         scratch_shapes=[
             pltpu.VMEM((slots, capacity), jnp.bfloat16),
             pltpu.SemaphoreType.DMA((slots // rows,)),
-            pltpu.SemaphoreType.DMA((3,)),
         ],
         compiler_params=pltpu.CompilerParams(vmem_limit_bytes=12 * MIB),
         cost_estimate=pl.CostEstimate(flops=1, bytes_accessed=1, transcendentals=0),
         name="prep",
     )(
         *where,
-        seq_counts,
-        pltpu.with_memory_space_constraint(out_grad, pltpu.HBM),
+        pltpu.with_memory_space_constraint(count, pltpu.VMEM),
         pltpu.with_memory_space_constraint(attn_out, pltpu.HBM),
     )
-    return copy, (left, right), count, ats
 
 
 def arrive_kernel(count_ref, x_ref, done_ref, out_ref):
@@ -445,9 +457,8 @@
         ]
 
     x = send(out_grad, ring.along())
-    own, near, count, ats = prepared(
-        where, seq_counts, out_grad, attn_out, [x for x in spans if x]
-    )
+    own, near, count = staged(me, seq_counts, out_grad)
+    ats = list(prepared(where, count, attn_out, [x for x in spans if x], rows))
     ats = [ats.pop(0) if x else None for x in spans]
     y = send(own, ring.crossing())
     counts = send(count, ring.along()), send(count, ring.crossing())

time: 117 us -> 119 us (1.017)
  waiting for transfers between devices: 16.9 us -> 20.4 us
  starting transfers between devices: 28.8 us -> 25.9 us
  Pallas kernels: 65.1 us -> 66.3 us
    ppermute x25, waiting for transfers between devices: 16.1 us -> 19.3 us  [send(): return lax.ppermute(x, 'dp', pairs)]
    ppermute x25, starting transfers between devices: 22.3 us -> 19.4 us  [send(): return lax.ppermute(x, 'dp', pairs)]
    pallas_call x0 -> x1, Pallas kernels: none -> 1.63 us  [staged(): pl.pallas_call(stage_kernel, in_specs=[smem, smem, pl.BlockSpec(memory_sp...]
    unnamed x8 -> x10, local copies, waits for them, and re-layouts: 3.49 us -> 3.49 us
  transfers between devices with their start and end apart: 31 -> 31, of which waited for: 16 -> 17; matrix products, arithmetic and copies ran while one was open for 0% -> 0% of each run, Pallas kernels for 51% -> 51%
where the time goes in v17:
time: 119 us; the launch traced here: 118 us
  Pallas kernels  66.3 us (56%)
  starting transfers between devices  25.9 us (22%)
  waiting for transfers between devices  20.4 us (17%)
  local copies, waits for them, and re-layouts  3.49 us (3%)
  between operations  2.43 us (2%)
    pallas_call x9, Pallas kernels, phase(): pl.pallas_call(functools.partial(phase_kernel, spec), in_specs=specs, out...  56.1 us
    ppermute x25, starting transfers between devices, send(): return lax.ppermute(x, 'dp', pairs)  19.4 us
    ppermute x25, waiting for transfers between devices, send(): return lax.ppermute(x, 'dp', pairs)  19.3 us
    ppermute x6, starting transfers between devices, exchange(): lax.ppermute(x, 'dp', [(d, d ^ mask) for d in range(devices)])  6.51 us
    pallas_call x1, Pallas kernels, prepared(): pl.pallas_call(functools.partial(prep_kernel, spans, rows), in_specs=[sme...  3.59 us
    unnamed x10, local copies, waits for them, and re-layouts  3.49 us
    pallas_call x1, Pallas kernels, scaled(): pl.pallas_call(functools.partial(scale_kernel, parts), in_specs=[vmem, vm...  2.96 us
  transfers between devices with their start and end apart: 31, of which 17 were waited for; matrix products, arithmetic and copies ran while one was open for 0% of the time, Pallas kernels for 51%

profile of v17, /device:TPU:0, one launch (start us, length us, event | category | flops | bytes accessed | tf_op | source)
XLA Modules:
  0.0 118.5 jit_solution(13512749365688182833)
XLA Ops:
  0.6 3.1 %collective-permute-start.1 = (bf16[144,4096]{1,0:T(8,128)(2,1)}, bf16[144,4096]{1,0:T(8,128)(2,1)S(1)}, u32[]{:S(2)}, u32[]{:S(2)}) collective-permute-start(bf16[144,4096]{1,0:T(8,128)(2,1)} %grad_ref.1), channel_id=1, source_target_pairs={{0,4},{1,3},{4,8},{5,1},{8,12},{9,5},{12,14},{13,9},{14,10},{15,13... | collective-permute-start | bytes 3538952 | tf_op jit(solution)/shard_map/ppermute | solution.py:448
  4.4 1.6 %stage.1 = (bf16[144,4096]{1,0:T(8,128)(2,1)S(1)}, bf16[144,2048]{1,0:T(8,128)(2,1)S(1)}, bf16[144,2048]{1,0:T(8,128)(2,1)S(1)}, s32[8,128]{1,0:T(8,128)S(1)}) custom-call(s32[1]{0:T(128)} %bitcast.me_ref.refs_1_, s32[1]{0:T(128)S(6)} %copy.47.seqs_ref, bf16[144,4096]{1,0:T(8,128)(2,1)} %grad_ref.1), custom_call_target="tpu_custom_call" | custom-call | flops 1 | bytes 1 | tf_op jit(solution)/shard_map/stage/pallas_call | solution.py:95
  6.1 0.5 collective-permute-start.3
  6.6 0.7 collective-permute-start.7
  7.3 1.0 collective-permute-start
  9.0 0.7 copy-done.1
  9.6 3.6 %prep.1 = (bf16[768,288]{1,0:T(8,128)(2,1)S(1)}, bf16[768,576]{1,0:T(8,128)(2,1)S(1)}, bf16[768,576]{1,0:T(8,128)(2,1)S(1)}, bf16[768,288]{1,0:T(8,128)(2,1)S(1)...) custom-call(s32[16,16]{1,0:T(8,128)S(1)} %copy-done.1, ...), custom_call_target="tpu_custom_call" | custom-call | flops 1 | bytes 1 | tf_op jit(solution)/shard_map/prep/pallas_call | solution.py:136
  13.3 2.8 %copy-done = bf16[768,4096]{1,0:T(8,128)(2,1)S(1)} copy-done((bf16[768,4096]{1,0:T(8,128)(2,1)S(1)}, bf16[768,4096]{1,0:T(8,128)(2,1)}, u32[]{:S(2)}) %copy-start) | copy-done | bytes 6291480
  16.1 7.2 %phase_w_whole.5 = (f32[768,4096]{1,0:T(8,128)S(1)}, bf16[2304,768]{1,0:T(8,128)(2,1)}, f32[8,128]{1,0:T(8,128)S(1)}) custom-call(s32[16,16]{1,0:T(8,128)S(1)} %copy-done.2, s32[1]{0:T(128)} %bitcast.me_ref.refs_1_, s32[1]{0:T(128)S(6)} %copy.46.heads_ref.refs_2_, bf16[768,288]{1,0:T(8,128)(2,1)S(1)} %get-tuple-element.49.refs_3_, ...), custom_call_target="tpu_custom_call" | custom-call | flops 1 | bytes 1 | tf_op jit(solution)/shard_map/phase_w_whole/pallas_call | solution.py:316
  23.3 3.3 %collective-permute-done.count_ref = s32[8,128]{1,0:T(8,128)S(1)} collective-permute-done((s32[8,128]{1,0:T(8,128)S(1)}, s32[8,128]{1,0:T(8,128)S(1)}, u32[]{:S(2)}, u32[]{:S(2)}) %collective-permute-start) | collective-permute-done | bytes 4128 | tf_op jit(solution)/shard_map/ppermute | solution.py:448
  26.6 0.7 arrived.2.x_ref
  27.3 0.1 split.7
  27.5 2.5 %collective-permute-start.4 = (bf16[144,4096]{1,0:T(8,128)(2,1)S(1)}, bf16[144,4096]{1,0:T(8,128)(2,1)S(1)}, u32[]{:S(2)}, u32[]{:S(2)}) collective-permute-start(bf16[144,4096]{1,0:T(8,128)(2,1)S(1)} %arrived.2.x_ref), channel_id=1, source_target_pairs={{0,4},{1,3},{4,8},{5,1},{8,12},{9,5},{12,14},{13,9},{14,10},{15,13... | collective-permute-start | bytes 3538952 | tf_op jit(solution)/shard_map/ppermute | solution.py:448
  30.0 2.2 %collective-permute-start.6 = (s32[8,128]{1,0:T(8,128)S(1)}, s32[8,128]{1,0:T(8,128)S(1)}, u32[]{:S(2)}, u32[]{:S(2)}) collective-permute-start(s32[8,128]{1,0:T(8,128)S(1)} %get-tuple-element.48._), channel_id=1, source_target_pairs={{0,3},{1,4},{4,1},{5,8},{8,5},{9,12},{12,9},{13,14},{14,13},{15,10... | collective-permute-start | bytes 12296 | tf_op jit(solution)/shard_map/ppermute | solution.py:448
  32.2 1.3 %collective-permute-done.6.count_ref = s32[8,128]{1,0:T(8,128)S(1)} collective-permute-done((s32[8,128]{1,0:T(8,128)S(1)}, s32[8,128]{1,0:T(8,128)S(1)}, u32[]{:S(2)}, u32[]{:S(2)}) %collective-permute-start.6) | collective-permute-done | bytes 4128 | tf_op jit(solution)/shard_map/ppermute | solution.py:448
  33.5 0.6 arrived.3.x_ref
  34.2 0.1 split.8
  34.3 1.2 collective-permute-start.13
  35.5 1.1 collective-permute-start.9
  36.6 0.5 collective-permute-start.10
  37.1 1.1 collective-permute-done.9.refs_10_
  38.2 0.8 collective-permute-done.8.refs_8_
  39.0 0.8 collective-permute-done.10.refs_12_
  39.9 11.2 %phase_w_whole.6 = (f32[768,4096]{1,0:T(8,128)S(1)}, bf16[2304,768]{1,0:T(8,128)(2,1)}, f32[8,128]{1,0:T(8,128)S(1)}) custom-call(s32[16,16]{1,0:T(8,128)S(1)} %copy-done.2, s32[1]{0:T(128)} %bitcast.me_ref.refs_1_, s32[1]{0:T(128)S(6)} %copy.46.heads_ref.refs_2_, ...), custom_call_target="tpu_custom_call", output_to_operand_aliasing={{0}: (13, {}), {1}: (14, {})} | custom-call | flops 1 | bytes 1 | tf_op jit(solution)/shard_map/phase_w_whole/pallas_call | solution.py:316
  51.1 1.2 collective-permute-start.11
  52.3 0.1 split.9
  52.4 0.6 collective-permute-start.12
  53.1 4.6 %collective-permute-done.13.refs_0_ = bf16[144,4096]{1,0:T(8,128)(2,1)S(1)} collective-permute-done((bf16[144,4096]{1,0:T(8,128)(2,1)S(1)}, bf16[144,4096]{1,0:T(8,128)(2,1)S(1)}, u32[]{:S(2)}, u32[]{:S(2)}) %collective-permute-start.13) | collective-permute-done | bytes 1179680 | tf_op jit(solution)/shard_map/ppermute | solution.py:448
  57.7 0.1 split.10
  57.9 0.5 collective-permute-start.16
  58.4 1.2 collective-permute-start.18
  59.6 0.3 collective-permute-done.14.refs_8_
  59.9 0.8 collective-permute-done.16.refs_12_
  60.7 11.2 %phase_w_whole.7 = (f32[768,4096]{1,0:T(8,128)S(1)}, bf16[2304,768]{1,0:T(8,128)(2,1)}, f32[8,128]{1,0:T(8,128)S(1)}) custom-call(s32[16,16]{1,0:T(8,128)S(1)} %copy-done.2, s32[1]{0:T(128)} %bitcast.me_ref.refs_1_, s32[1]{0:T(128)S(6)} %copy.46.heads_ref.refs_2_, ...), custom_call_target="tpu_custom_call", output_to_operand_aliasing={{0}: (13, {}), {1}: (14, {})} | custom-call | flops 1 | bytes 1 | tf_op jit(solution)/shard_map/phase_w_whole/pallas_call | solution.py:316
  72.0 0.1 split.11
  72.1 0.2 collective-permute-start.19
  72.3 0.4 collective-permute-start.20
  72.7 1.1 collective-permute-start.17
  73.9 0.3 collective-permute-done.19.refs_6_
  74.2 0.8 collective-permute-done.20.refs_8_
  75.0 7.5 %phase_w_whole.8 = (f32[768,4096]{1,0:T(8,128)S(1)}, bf16[2304,768]{1,0:T(8,128)(2,1)}, f32[8,128]{1,0:T(8,128)S(1)}) custom-call(s32[16,16]{1,0:T(8,128)S(1)} %copy-done.2, s32[1]{0:T(128)} %bitcast.me_ref.refs_1_, s32[1]{0:T(128)S(6)} %copy.46.heads_ref.refs_2_, ...), custom_call_target="tpu_custom_call", output_to_operand_aliasing={{0}: (9, {}), {1}: (10, {})} | custom-call | flops 1 | bytes 1 | tf_op jit(solution)/shard_map/phase_w_whole/pallas_call | solution.py:316
  82.5 0.5 collective-permute-done.18.refs_0_
  83.0 0.1 split.12
  83.2 0.5 collective-permute-start.22
  83.7 1.5 %collective-permute-done.21.refs_6_ = bf16[144,2048]{1,0:T(8,128)(2,1)S(1)} collective-permute-done((bf16[144,2048]{1,0:T(8,128)(2,1)S(1)}, bf16[144,2048]{1,0:T(8,128)(2,1)S(1)}, u32[]{:S(2)}, u32[]{:S(2)}) %collective-permute-start.21) | collective-permute-done | bytes 589856 | tf_op jit(solution)/shard_map/ppermute | solution.py:448
  85.2 0.8 collective-permute-done.22.refs_8_
  86.0 7.5 %phase_w_whole.9 = (f32[768,4096]{1,0:T(8,128)S(1)}, bf16[2304,768]{1,0:T(8,128)(2,1)}, f32[8,128]{1,0:T(8,128)S(1)}) custom-call(s32[16,16]{1,0:T(8,128)S(1)} %copy-done.2, s32[1]{0:T(128)} %bitcast.me_ref.refs_1_, s32[1]{0:T(128)S(6)} %copy.46.heads_ref.refs_2_, ...), custom_call_target="tpu_custom_call", output_to_operand_aliasing={{0}: (9, {}), {1}: (10, {})} | custom-call | flops 1 | bytes 1 | tf_op jit(solution)/shard_map/phase_w_whole/pallas_call | solution.py:316
  93.5 2.1 %collective-permute-done.17.refs_0_ = bf16[144,4096]{1,0:T(8,128)(2,1)S(1)} collective-permute-done((bf16[144,4096]{1,0:T(8,128)(2,1)S(1)}, bf16[144,4096]{1,0:T(8,128)(2,1)S(1)}, u32[]{:S(2)}, u32[]{:S(2)}) %collective-permute-start.17) | collective-permute-done | bytes 1179680 | tf_op jit(solution)/shard_map/ppermute | solution.py:448
  95.6 0.1 split.13
  95.8 0.5 collective-permute-start.23
  96.3 3.0 %phase_w_None.2 = (f32[768,4096]{1,0:T(8,128)S(1)}, f32[8,128]{1,0:T(8,128)}) custom-call(s32[16,16]{1,0:T(8,128)S(1)} %copy-done.2, s32[1]{0:T(128)} %bitcast.me_ref.refs_1_, s32[1]{0:T(128)S(6)} %copy.46.heads_ref.refs_2_, bf16[768,144]{1,0:T(8,128)(2,1)S(1)} %get-tuple-element.88.refs_3_, ...), custom_call_target="tpu_custom_call", output_to_operand_aliasing={{0}: (6, {})} | custom-call | flops 1 | bytes 1 | tf_op jit(solution)/shard_map/phase_w_None/pallas_call | solution.py:316
  99.4 3.0 %phase_w_None.3 = (f32[768,4096]{1,0:T(8,128)S(1)}, f32[8,128]{1,0:T(8,128)S(1)}) custom-call(s32[16,16]{1,0:T(8,128)S(1)} %copy-done.2, s32[1]{0:T(128)} %bitcast.me_ref.refs_1_, s32[1]{0:T(128)S(6)} %copy.46.heads_ref.refs_2_, bf16[768,144]{1,0:T(8,128)(2,1)S(1)} %get-tuple-element.87.refs_3_, ...), custom_call_target="tpu_custom_call", output_to_operand_aliasing={{0}: (6, {})} | custom-call | flops 1 | bytes 1 | tf_op jit(solution)/shard_map/phase_w_None/pallas_call | solution.py:316
  102.4 3.1 %collective-permute-start.27 = (f32[8,128]{1,0:T(8,128)S(1)}, f32[8,128]{1,0:T(8,128)S(1)}, u32[]{:S(2)}, u32[]{:S(2)}) collective-permute-start(f32[8,128]{1,0:T(8,128)S(1)} %get-tuple-element.92), channel_id=1, source_target_pairs={{0,6},{1,7},{2,4},{3,5},{4,2},{5,3},{6,0},{7,1},{8,14},{9,15},{10,... | collective-permute-start | bytes 12296 | tf_op jit(solution)/shard_map/ppermute | solution.py:428
  105.5 0.4 collective-permute-start.26
  105.9 0.2 collective-permute-start.25
  106.1 2.7 %phase__first.1 = (f32[288,768]{1,0:T(8,128)S(1)}, f32[8,128]{1,0:T(8,128)S(1)}) custom-call(s32[16,16]{1,0:T(8,128)S(1)} %copy-done.2, s32[1]{0:T(128)} %bitcast.me_ref.refs_1_, s32[1]{0:T(128)S(6)} %copy.46.heads_ref.refs_2_, bf16[768,4096]{1,0:T(8,128)(2,1)S(1)} %bitcast.2, bf16[144,2048]{1,0:T(8,128)(2,1)S(1)} %get-tuple-element.83.refs_4_, ...), custom_call_target="tpu_custom_call" | custom-call | flops 1 | bytes 1 | tf_op jit(solution)/shard_map/phase__first/pallas_call | solution.py:316
  108.8 0.2 collective-permute-done.26
  109.1 0.4 collective-permute-done.25
  109.5 1.3 %collective-permute-start.30 = (f32[8,128]{1,0:T(8,128)S(1)}, f32[8,128]{1,0:T(8,128)S(1)}, u32[]{:S(2)}, u32[]{:S(2)}) collective-permute-start(f32[8,128]{1,0:T(8,128)S(1)} %after.11), channel_id=1, source_target_pairs={{0,9},{1,8},{2,11},{3,10},{4,13},{5,12},{6,15},{7,14},{8,1},{9,0},... | collective-permute-start | bytes 12296 | tf_op jit(solution)/shard_map/ppermute | solution.py:428
  110.9 1.3 %collective-permute-start.29 = (f32[8,128]{1,0:T(8,128)S(1)}, f32[8,128]{1,0:T(8,128)S(1)}, u32[]{:S(2)}, u32[]{:S(2)}) collective-permute-start(f32[8,128]{1,0:T(8,128)S(1)} %after.11), channel_id=1, source_target_pairs={{0,8},{1,9},{2,10},{3,11},{4,12},{5,13},{6,14},{7,15},{8,0},{9,1},... | collective-permute-start | bytes 12296 | tf_op jit(solution)/shard_map/ppermute | solution.py:428
  112.1 0.2 collective-permute-start.28
  112.3 2.7 %phase__last.1 = (bf16[2304,768]{1,0:T(8,128)(2,1)}, f32[8,128]{1,0:T(8,128)}) custom-call(s32[16,16]{1,0:T(8,128)S(1)} %copy-done.2, s32[1]{0:T(128)} %bitcast.me_ref.refs_1_, s32[1]{0:T(128)S(6)} %copy.46.heads_ref.refs_2_, bf16[768,4096]{1,0:T(8,128)(2,1)S(1)} %bitcast.2, ...), custom_call_target="tpu_custom_call", output_to_operand_aliasing={{0}: (7, {})} | custom-call | flops 1 | bytes 1 | tf_op jit(solution)/shard_map/phase__last/pallas_call | solution.py:316
  115.0 0.3 collective-permute-done.29
  115.4 3.0 %scale.1 = bf16[768,4096]{1,0:T(8,128)(2,1)} custom-call(f32[768,4096]{1,0:T(8,128)S(1)} %get-tuple-element.91.w_ref, f32[8,128]{1,0:T(8,128)S(1)} %add_add_fusion.squares_ref), custom_call_target="tpu_custom_call" | custom-call | flops 3145728 | bytes 6291456 | tf_op jit(solution)/shard_map/scale/pallas_call | solution.py:356
  (38 shorter events, 0.5 us)
Async XLA Ops:
  0.6 12.6 %copy-start.2 = (s32[16,16]{1,0:T(8,128)S(1)}, s32[16,16]{1,0:T(8,128)}, u32[]{:S(2)}) copy-start(s32[16,16]{1,0:T(8,128)} %constant.6.clone.table_ref.refs_0_) | copy-start | bytes 3076
  0.6 26.0 %collective-permute-start.1 = (bf16[144,4096]{1,0:T(8,128)(2,1)}, bf16[144,4096]{1,0:T(8,128)(2,1)S(1)}, u32[]{:S(2)}, u32[]{:S(2)}) collective-permute-start(bf16[144,4096]{1,0:T(8,128)(2,1)} %grad_ref.1), channel_id=1, source_target_pairs={{0,4},{1,3},{4,8},{5,1},{8,12},{9,5},{12,14},{13,9},{14,10},{15,13... | collective-permute-start | bytes 3538952 | tf_op jit(solution)/shard_map/ppermute | solution.py:448
  6.0 7.2 %collective-permute-start.2 = (bf16[144,2048]{1,0:T(8,128)(2,1)S(1)}, bf16[144,2048]{1,0:T(8,128)(2,1)S(1)}, u32[]{:S(2)}, u32[]{:S(2)}) collective-permute-start(bf16[144,2048]{1,0:T(8,128)(2,1)S(1)} %get-tuple-element.50.refs_5_), channel_id=1, source_target_pairs={{0,1},{1,0},{2,3},{3,2},{4,5},{5,4},{6,7},{7,6},{8,9},{9,8},{10,11... | collective-permute-start | bytes 1769480 | tf_op jit(solution)/shard_map/ppermute | solution.py:448
  6.1 7.2 %collective-permute-start.3 = (bf16[144,2048]{1,0:T(8,128)(2,1)S(1)}, bf16[144,2048]{1,0:T(8,128)(2,1)S(1)}, u32[]{:S(2)}, u32[]{:S(2)}) collective-permute-start(bf16[144,2048]{1,0:T(8,128)(2,1)S(1)} %get-tuple-element.51.refs_7_), channel_id=1, source_target_pairs={{0,1},{1,0},{2,3},{3,2},{4,5},{5,4},{6,7},{7,6},{8,9},{9,8},{10,11... | collective-permute-start | bytes 1769480 | tf_op jit(solution)/shard_map/ppermute | solution.py:448
  6.6 27.0 %collective-permute-start.7 = (bf16[144,4096]{1,0:T(8,128)(2,1)S(1)}, bf16[144,4096]{1,0:T(8,128)(2,1)S(1)}, u32[]{:S(2)}, u32[]{:S(2)}) collective-permute-start(bf16[144,4096]{1,0:T(8,128)(2,1)S(1)} %get-tuple-element.55), channel_id=1, source_target_pairs={{0,3},{1,4},{4,1},{5,8},{8,5},{9,12},{12,9},{13,14},{14,13},{15,10... | collective-permute-start | bytes 3538952 | tf_op jit(solution)/shard_map/ppermute | solution.py:448
  7.3 19.4 %collective-permute-start = (s32[8,128]{1,0:T(8,128)S(1)}, s32[8,128]{1,0:T(8,128)S(1)}, u32[]{:S(2)}, u32[]{:S(2)}) collective-permute-start(s32[8,128]{1,0:T(8,128)S(1)} %get-tuple-element.48._), channel_id=1, source_target_pairs={{0,4},{1,3},{4,8},{5,1},{8,12},{9,5},{12,14},{13,9},{14,10},{15,13... | collective-permute-start | bytes 12296 | tf_op jit(solution)/shard_map/ppermute | solution.py:448
  8.9 0.7 copy-start.1
  13.3 2.8 %copy-start = (bf16[768,4096]{1,0:T(8,128)(2,1)S(1)}, bf16[768,4096]{1,0:T(8,128)(2,1)}, u32[]{:S(2)}) copy-start(bf16[768,4096]{1,0:T(8,128)(2,1)} %refs_3_.3) | copy-start | bytes 18874372
  27.4 9.2 %collective-permute-start.5 = (bf16[144,2048]{1,0:T(8,128)(2,1)S(1)}, bf16[144,2048]{1,0:T(8,128)(2,1)S(1)}, u32[]{:S(2)}, u32[]{:S(2)}) collective-permute-start(bf16[144,2048]{1,0:T(8,128)(2,1)S(1)} %get-tuple-element.54.refs_5_), channel_id=1, source_target_pairs={{0,1},{1,0},{2,3},{3,2},{4,5},{5,4},{6,7},{7,6},{8,9},{9,8},{10,11... | collective-permute-start | bytes 1769480 | tf_op jit(solution)/shard_map/ppermute | solution.py:448
  27.5 23.7 %collective-permute-start.4 = (bf16[144,4096]{1,0:T(8,128)(2,1)S(1)}, bf16[144,4096]{1,0:T(8,128)(2,1)S(1)}, u32[]{:S(2)}, u32[]{:S(2)}) collective-permute-start(bf16[144,4096]{1,0:T(8,128)(2,1)S(1)} %arrived.2.x_ref), channel_id=1, source_target_pairs={{0,4},{1,3},{4,8},{5,1},{8,12},{9,5},{12,14},{13,9},{14,10},{15,13... | collective-permute-start | bytes 3538952 | tf_op jit(solution)/shard_map/ppermute | solution.py:448
  30.0 3.5 %collective-permute-start.6 = (s32[8,128]{1,0:T(8,128)S(1)}, s32[8,128]{1,0:T(8,128)S(1)}, u32[]{:S(2)}, u32[]{:S(2)}) collective-permute-start(s32[8,128]{1,0:T(8,128)S(1)} %get-tuple-element.48._), channel_id=1, source_target_pairs={{0,3},{1,4},{4,1},{5,8},{8,5},{9,12},{12,9},{13,14},{14,13},{15,10... | collective-permute-start | bytes 12296 | tf_op jit(solution)/shard_map/ppermute | solution.py:448
  34.3 23.4 %collective-permute-start.13 = (bf16[144,4096]{1,0:T(8,128)(2,1)S(1)}, bf16[144,4096]{1,0:T(8,128)(2,1)S(1)}, u32[]{:S(2)}, u32[]{:S(2)}) collective-permute-start(bf16[144,4096]{1,0:T(8,128)(2,1)S(1)} %arrived.3.x_ref), channel_id=1, source_target_pairs={{0,4},{1,3},{4,8},{5,1},{8,12},{9,5},{12,14},{13,9},{14,10},{15,13... | collective-permute-start | bytes 3538952 | tf_op jit(solution)/shard_map/ppermute | solution.py:448
  35.5 2.7 %collective-permute-start.9 = (bf16[144,2048]{1,0:T(8,128)(2,1)S(1)}, bf16[144,2048]{1,0:T(8,128)(2,1)S(1)}, u32[]{:S(2)}, u32[]{:S(2)}) collective-permute-start(bf16[144,2048]{1,0:T(8,128)(2,1)S(1)} %get-tuple-element.57.refs_9_), channel_id=1, source_target_pairs={{0,1},{1,0},{2,3},{3,2},{4,5},{5,4},{6,7},{7,6},{8,9},{9,8},{10,11... | collective-permute-start | bytes 1769480 | tf_op jit(solution)/shard_map/ppermute | solution.py:448
  36.6 2.5 %collective-permute-start.8 = (bf16[144,2048]{1,0:T(8,128)(2,1)S(1)}, bf16[144,2048]{1,0:T(8,128)(2,1)S(1)}, u32[]{:S(2)}, u32[]{:S(2)}) collective-permute-start(bf16[144,2048]{1,0:T(8,128)(2,1)S(1)} %get-tuple-element.56.refs_7_), channel_id=1, source_target_pairs={{0,1},{1,0},{2,3},{3,2},{4,5},{5,4},{6,7},{7,6},{8,9},{9,8},{10,11... | collective-permute-start | bytes 1769480 | tf_op jit(solution)/shard_map/ppermute | solution.py:448
  36.6 3.3 %collective-permute-start.10 = (bf16[144,2048]{1,0:T(8,128)(2,1)S(1)}, bf16[144,2048]{1,0:T(8,128)(2,1)S(1)}, u32[]{:S(2)}, u32[]{:S(2)}) collective-permute-start(bf16[144,2048]{1,0:T(8,128)(2,1)S(1)} %get-tuple-element.58.refs_11_), channel_id=1, source_target_pairs={{0,1},{1,0},{2,3},{3,2},{4,5},{5,4},{6,7},{7,6},{8,9},{9,8},{10,11... | collective-permute-start | bytes 1769480 | tf_op jit(solution)/shard_map/ppermute | solution.py:448
  51.1 20.9 %collective-permute-start.11 = (bf16[144,4096]{1,0:T(8,128)(2,1)S(1)}, bf16[144,4096]{1,0:T(8,128)(2,1)S(1)}, u32[]{:S(2)}, u32[]{:S(2)}) collective-permute-start(bf16[144,4096]{1,0:T(8,128)(2,1)S(1)} %after.6.x_ref), channel_id=1, source_target_pairs={{0,4},{1,3},{4,8},{5,1},{8,12},{9,5},{12,14},{13,9},{14,10},{15,13... | collective-permute-start | bytes 3538952 | tf_op jit(solution)/shard_map/ppermute | solution.py:448
  52.4 6.0 %collective-permute-start.12 = (bf16[144,2048]{1,0:T(8,128)(2,1)S(1)}, bf16[144,2048]{1,0:T(8,128)(2,1)S(1)}, u32[]{:S(2)}, u32[]{:S(2)}) collective-permute-start(bf16[144,2048]{1,0:T(8,128)(2,1)S(1)} %get-tuple-element.63.refs_5_), channel_id=1, source_target_pairs={{0,1},{1,0},{2,3},{3,2},{4,5},{5,4},{6,7},{7,6},{8,9},{9,8},{10,11... | collective-permute-start | bytes 1769480 | tf_op jit(solution)/shard_map/ppermute | solution.py:448
  53.1 6.5 %collective-permute-start.15 = (bf16[144,2048]{1,0:T(8,128)(2,1)S(1)}, bf16[144,2048]{1,0:T(8,128)(2,1)S(1)}, u32[]{:S(2)}, u32[]{:S(2)}) collective-permute-start(bf16[144,2048]{1,0:T(8,128)(2,1)S(1)} %get-tuple-element.65.refs_9_), channel_id=1, source_target_pairs={{0,1},{1,0},{2,3},{3,2},{4,5},{5,4},{6,7},{7,6},{8,9},{9,8},{10,11... | collective-permute-start | bytes 1769480 | tf_op jit(solution)/shard_map/ppermute | solution.py:448
  57.8 2.1 %collective-permute-start.14 = (bf16[144,2048]{1,0:T(8,128)(2,1)S(1)}, bf16[144,2048]{1,0:T(8,128)(2,1)S(1)}, u32[]{:S(2)}, u32[]{:S(2)}) collective-permute-start(bf16[144,2048]{1,0:T(8,128)(2,1)S(1)} %get-tuple-element.64.refs_7_), channel_id=1, source_target_pairs={{0,1},{1,0},{2,3},{3,2},{4,5},{5,4},{6,7},{7,6},{8,9},{9,8},{10,11... | collective-permute-start | bytes 1769480 | tf_op jit(solution)/shard_map/ppermute | solution.py:448
  57.9 2.8 %collective-permute-start.16 = (bf16[144,2048]{1,0:T(8,128)(2,1)S(1)}, bf16[144,2048]{1,0:T(8,128)(2,1)S(1)}, u32[]{:S(2)}, u32[]{:S(2)}) collective-permute-start(bf16[144,2048]{1,0:T(8,128)(2,1)S(1)} %get-tuple-element.66.refs_11_), channel_id=1, source_target_pairs={{0,1},{1,0},{2,3},{3,2},{4,5},{5,4},{6,7},{7,6},{8,9},{9,8},{10,11... | collective-permute-start | bytes 1769480 | tf_op jit(solution)/shard_map/ppermute | solution.py:448
  58.4 24.6 %collective-permute-start.18 = (bf16[144,4096]{1,0:T(8,128)(2,1)S(1)}, bf16[144,4096]{1,0:T(8,128)(2,1)S(1)}, u32[]{:S(2)}, u32[]{:S(2)}) collective-permute-start(bf16[144,4096]{1,0:T(8,128)(2,1)S(1)} %after.7.x_ref), channel_id=1, source_target_pairs={{0,4},{1,3},{4,8},{5,1},{8,12},{9,5},{12,14},{13,9},{14,10},{15,13... | collective-permute-start | bytes 3538952 | tf_op jit(solution)/shard_map/ppermute | solution.py:448
  72.1 2.1 %collective-permute-start.19 = (bf16[144,2048]{1,0:T(8,128)(2,1)S(1)}, bf16[144,2048]{1,0:T(8,128)(2,1)S(1)}, u32[]{:S(2)}, u32[]{:S(2)}) collective-permute-start(bf16[144,2048]{1,0:T(8,128)(2,1)S(1)} %get-tuple-element.72.refs_5_), channel_id=1, source_target_pairs={{0,1},{1,0},{2,3},{3,2},{4,5},{5,4},{6,7},{7,6},{8,9},{9,8},{10,11... | collective-permute-start | bytes 1769480 | tf_op jit(solution)/shard_map/ppermute | solution.py:448
  72.3 2.7 %collective-permute-start.20 = (bf16[144,2048]{1,0:T(8,128)(2,1)S(1)}, bf16[144,2048]{1,0:T(8,128)(2,1)S(1)}, u32[]{:S(2)}, u32[]{:S(2)}) collective-permute-start(bf16[144,2048]{1,0:T(8,128)(2,1)S(1)} %get-tuple-element.73.refs_7_), channel_id=1, source_target_pairs={{0,1},{1,0},{2,3},{3,2},{4,5},{5,4},{6,7},{7,6},{8,9},{9,8},{10,11... | collective-permute-start | bytes 1769480 | tf_op jit(solution)/shard_map/ppermute | solution.py:448
  72.7 22.9 %collective-permute-start.17 = (bf16[144,4096]{1,0:T(8,128)(2,1)S(1)}, bf16[144,4096]{1,0:T(8,128)(2,1)S(1)}, u32[]{:S(2)}, u32[]{:S(2)}) collective-permute-start(bf16[144,4096]{1,0:T(8,128)(2,1)S(1)} %after.8.x_ref), channel_id=1, source_target_pairs={{0,4},{1,3},{4,8},{5,1},{8,12},{9,5},{12,14},{13,9},{14,10},{15,13... | collective-permute-start | bytes 3538952 | tf_op jit(solution)/shard_map/ppermute | solution.py:448
  83.1 2.1 %collective-permute-start.21 = (bf16[144,2048]{1,0:T(8,128)(2,1)S(1)}, bf16[144,2048]{1,0:T(8,128)(2,1)S(1)}, u32[]{:S(2)}, u32[]{:S(2)}) collective-permute-start(bf16[144,2048]{1,0:T(8,128)(2,1)S(1)} %get-tuple-element.77.refs_5_), channel_id=1, source_target_pairs={{0,1},{1,0},{2,3},{3,2},{4,5},{5,4},{6,7},{7,6},{8,9},{9,8},{10,11... | collective-permute-start | bytes 1769480 | tf_op jit(solution)/shard_map/ppermute | solution.py:448
  83.2 2.8 %collective-permute-start.22 = (bf16[144,2048]{1,0:T(8,128)(2,1)S(1)}, bf16[144,2048]{1,0:T(8,128)(2,1)S(1)}, u32[]{:S(2)}, u32[]{:S(2)}) collective-permute-start(bf16[144,2048]{1,0:T(8,128)(2,1)S(1)} %get-tuple-element.78.refs_7_), channel_id=1, source_target_pairs={{0,1},{1,0},{2,3},{3,2},{4,5},{5,4},{6,7},{7,6},{8,9},{9,8},{10,11... | collective-permute-start | bytes 1769480 | tf_op jit(solution)/shard_map/ppermute | solution.py:448
  95.8 3.6 %collective-permute-start.24 = (bf16[144,2048]{1,0:T(8,128)(2,1)S(1)}, bf16[144,2048]{1,0:T(8,128)(2,1)S(1)}, u32[]{:S(2)}, u32[]{:S(2)}) collective-permute-start(bf16[144,2048]{1,0:T(8,128)(2,1)S(1)} %get-tuple-element.83.refs_4_), channel_id=1, source_target_pairs={{0,1},{1,0},{2,3},{3,2},{4,5},{5,4},{6,7},{7,6},{8,9},{9,8},{10,11... | collective-permute-start | bytes 1769480 | tf_op jit(solution)/shard_map/ppermute | solution.py:448
  95.8 3.5 %collective-permute-start.23 = (bf16[144,2048]{1,0:T(8,128)(2,1)S(1)}, bf16[144,2048]{1,0:T(8,128)(2,1)S(1)}, u32[]{:S(2)}, u32[]{:S(2)}) collective-permute-start(bf16[144,2048]{1,0:T(8,128)(2,1)S(1)} %get-tuple-element.82.refs_6_.refs_4_.refs_5_), channel_id=1, source_target_pairs={{0,1},{1,0},{2,3},{3,2},{4,5},{5,4},{6,7},{7,6},{8,9},{9,8},{10,11... | collective-permute-start | bytes 1769480 | tf_op jit(solution)/shard_map/ppermute | solution.py:448
  99.3 6.8 %slice-start = ((s8[6291456]{0:T(1024)(128)(4,1)}), s8[4194304]{0:T(1024)(128)(4,1)S(1)}, s32[]{:S(2)}) async-start(s8[6291456]{0:T(1024)(128)(4,1)} %bitcast.1), calls=%async_computation | async-start | bytes 8388608
  99.4 6.7 %slice-start.1 = ((s8[6291456]{0:T(1024)(128)(4,1)}), s8[2097152]{0:T(1024)(128)(4,1)S(1)}, s32[]{:S(2)}) async-start(s8[6291456]{0:T(1024)(128)(4,1)} %bitcast.1), calls=%async_computation.1 | async-start | bytes 4194304
  102.4 6.5 %collective-permute-start.27 = (f32[8,128]{1,0:T(8,128)S(1)}, f32[8,128]{1,0:T(8,128)S(1)}, u32[]{:S(2)}, u32[]{:S(2)}) collective-permute-start(f32[8,128]{1,0:T(8,128)S(1)} %get-tuple-element.92), channel_id=1, source_target_pairs={{0,6},{1,7},{2,4},{3,5},{4,2},{5,3},{6,0},{7,1},{8,14},{9,15},{10,... | collective-permute-start | bytes 12296 | tf_op jit(solution)/shard_map/ppermute | solution.py:428
  105.5 3.6 %collective-permute-start.26 = (f32[8,128]{1,0:T(8,128)S(1)}, f32[8,128]{1,0:T(8,128)S(1)}, u32[]{:S(2)}, u32[]{:S(2)}) collective-permute-start(f32[8,128]{1,0:T(8,128)S(1)} %get-tuple-element.92), channel_id=1, source_target_pairs={{0,4},{1,5},{2,6},{3,7},{4,0},{5,1},{6,2},{7,3},{8,12},{9,13},{10,... | collective-permute-start | bytes 12296 | tf_op jit(solution)/shard_map/ppermute | solution.py:428
  105.9 3.6 %collective-permute-start.25 = (f32[8,128]{1,0:T(8,128)S(1)}, f32[8,128]{1,0:T(8,128)S(1)}, u32[]{:S(2)}, u32[]{:S(2)}) collective-permute-start(f32[8,128]{1,0:T(8,128)S(1)} %get-tuple-element.92), channel_id=1, source_target_pairs={{0,2},{1,3},{2,0},{3,1},{4,6},{5,7},{6,4},{7,5},{8,10},{9,11},{10,... | collective-permute-start | bytes 12296 | tf_op jit(solution)/shard_map/ppermute | solution.py:428
  109.5 5.5 %collective-permute-start.30 = (f32[8,128]{1,0:T(8,128)S(1)}, f32[8,128]{1,0:T(8,128)S(1)}, u32[]{:S(2)}, u32[]{:S(2)}) collective-permute-start(f32[8,128]{1,0:T(8,128)S(1)} %after.11), channel_id=1, source_target_pairs={{0,9},{1,8},{2,11},{3,10},{4,13},{5,12},{6,15},{7,14},{8,1},{9,0},... | collective-permute-start | bytes 12296 | tf_op jit(solution)/shard_map/ppermute | solution.py:428
  110.9 4.5 %collective-permute-start.29 = (f32[8,128]{1,0:T(8,128)S(1)}, f32[8,128]{1,0:T(8,128)S(1)}, u32[]{:S(2)}, u32[]{:S(2)}) collective-permute-start(f32[8,128]{1,0:T(8,128)S(1)} %after.11), channel_id=1, source_target_pairs={{0,8},{1,9},{2,10},{3,11},{4,12},{5,13},{6,14},{7,15},{8,0},{9,1},... | collective-permute-start | bytes 12296 | tf_op jit(solution)/shard_map/ppermute | solution.py:428
  112.1 3.2 %collective-permute-start.28 = (f32[8,128]{1,0:T(8,128)S(1)}, f32[8,128]{1,0:T(8,128)S(1)}, u32[]{:S(2)}, u32[]{:S(2)}) collective-permute-start(f32[8,128]{1,0:T(8,128)S(1)} %after.11), channel_id=1, source_target_pairs={{0,1},{1,0},{2,3},{3,2},{4,5},{5,4},{6,7},{7,6},{8,9},{9,8},{10,11... | collective-permute-start | bytes 12296 | tf_op jit(solution)/shard_map/ppermute | solution.py:428

commit v18 on v14

--- a/solution.py
+++ b/solution.py
@@ -449,10 +449,11 @@
         where, seq_counts, out_grad, attn_out, [x for x in spans if x]
     )
     ats = [ats.pop(0) if x else None for x in spans]
-    y = send(own, ring.crossing())
+    others = swapped(near)
+    y = send(after(others[1], own)[0], ring.crossing())
     counts = send(count, ring.along()), send(count, ring.crossing())
     w, out, done = phase(
-        where, shapes, 0, grouped(near, swapped(near)), at=ats[0], weight=weight, attn="whole"
+        where, shapes, 0, grouped(near, others), at=ats[0], weight=weight, attn="whole"
     )
 
     for k in range(1, last):

time: 117 us -> 126 us (1.077)
  waiting for transfers between devices: 16.9 us -> 31.5 us
  local copies, waits for them, and re-layouts: 3.49 us -> 0.7 us
  starting transfers between devices: 28.8 us -> 26.7 us
    ppermute x25, waiting for transfers between devices: 16.1 us -> 30.7 us  [send(): return lax.ppermute(x, 'dp', pairs)]
    unnamed x8 -> x4, local copies, waits for them, and re-layouts: 3.49 us -> 0.7 us
    ppermute x25, starting transfers between devices: 22.3 us -> 20.2 us  [send(): return lax.ppermute(x, 'dp', pairs)]
  transfers between devices with their start and end apart: 31 -> 31, of which waited for: 16 -> 14; matrix products, arithmetic and copies ran while one was open for 0% -> 0% of each run, Pallas kernels for 51% -> 43%
where the time goes in v18:
time: 126 us
  Pallas kernels  65 us (52%)
  waiting for transfers between devices  31.5 us (25%)
  starting transfers between devices  26.7 us (21%)
  between operations  2.36 us (2%)
    pallas_call x9, Pallas kernels, phase(): pl.pallas_call(functools.partial(phase_kernel, spec), in_specs=specs, out...  55.8 us
    ppermute x25, waiting for transfers between devices, send(): return lax.ppermute(x, 'dp', pairs)  30.7 us
    ppermute x25, starting transfers between devices, send(): return lax.ppermute(x, 'dp', pairs)  20.2 us
    ppermute x6, starting transfers between devices, exchange(): lax.ppermute(x, 'dp', [(d, d ^ mask) for d in range(devices)])  6.5 us
    pallas_call x1, Pallas kernels, prepared(): pl.pallas_call(functools.partial(prep_kernel, spans, rows), in_specs=[sme...  4.23 us
    pallas_call x1, Pallas kernels, scaled(): pl.pallas_call(functools.partial(scale_kernel, parts), in_specs=[vmem, vm...  2.96 us
  transfers between devices with their start and end apart: 31, of which 14 were waited for; matrix products, arithmetic and copies ran while one was open for 0% of the time, Pallas kernels for 43%

profile of v18, /device:TPU:0, one launch (start us, length us, event | category | flops | bytes accessed | tf_op | source)
XLA Modules:
  0.0 126.3 jit_solution(1427603310721831639)
XLA Ops:
  1.9 0.7 copy-done.1
  2.6 4.2 %prep.1 = (bf16[144,4096]{1,0:T(8,128)(2,1)S(1)}, bf16[144,2048]{1,0:T(8,128)(2,1)S(1)}, bf16[144,2048]{1,0:T(8,128)(2,1)S(1)}, s32[8,128]{1,0:T(8,128)S(1)}, bf...) custom-call(s32[16,16]{1,0:T(8,128)S(1)} %copy-done.1, ...), custom_call_target="tpu_custom_call" | custom-call | flops 1 | bytes 1 | tf_op jit(solution)/shard_map/prep/pallas_call | solution.py:121
  6.9 0.5 collective-permute-start.3
  7.4 2.6 %collective-permute-start.1 = (bf16[144,4096]{1,0:T(8,128)(2,1)}, bf16[144,4096]{1,0:T(8,128)(2,1)S(1)}, u32[]{:S(2)}, u32[]{:S(2)}) collective-permute-start(bf16[144,4096]{1,0:T(8,128)(2,1)} %grad_ref.1), channel_id=1, source_target_pairs={{0,4},{1,3},{4,8},{5,1},{8,12},{9,5},{12,14},{13,9},{14,10},{15,13... | collective-permute-start | bytes 3538952 | tf_op jit(solution)/shard_map/ppermute | solution.py:436
  10.0 0.1 collective-permute-start.2
  10.1 1.5 %collective-permute-start.7 = (bf16[144,4096]{1,0:T(8,128)(2,1)S(1)}, bf16[144,4096]{1,0:T(8,128)(2,1)S(1)}, u32[]{:S(2)}, u32[]{:S(2)}) collective-permute-start(bf16[144,4096]{1,0:T(8,128)(2,1)S(1)} %after.7), channel_id=1, source_target_pairs={{0,3},{1,4},{4,1},{5,8},{8,5},{9,12},{12,9},{13,14},{14,13},{15,10... | collective-permute-start | bytes 3538952 | tf_op jit(solution)/shard_map/ppermute | solution.py:436
  11.6 0.5 collective-permute-start
  12.2 7.2 %phase_w_whole.5 = (f32[768,4096]{1,0:T(8,128)S(1)}, bf16[2304,768]{1,0:T(8,128)(2,1)}, f32[8,128]{1,0:T(8,128)S(1)}) custom-call(s32[16,16]{1,0:T(8,128)S(1)} %copy-done.1, s32[1]{0:T(128)} %bitcast.me_ref.refs_1_, s32[1]{0:T(128)S(6)} %copy.48.heads_ref.refs_2_, bf16[768,288]{1,0:T(8,128)(2,1)S(1)} %get-tuple-element.49.refs_3_, ...), custom_call_target="tpu_custom_call" | custom-call | flops 1 | bytes 1 | tf_op jit(solution)/shard_map/phase_w_whole/pallas_call | solution.py:304
  19.4 16.2 %collective-permute-done.count_ref = s32[8,128]{1,0:T(8,128)S(1)} collective-permute-done((s32[8,128]{1,0:T(8,128)S(1)}, s32[8,128]{1,0:T(8,128)S(1)}, u32[]{:S(2)}, u32[]{:S(2)}) %collective-permute-start) | collective-permute-done | bytes 4128 | tf_op jit(solution)/shard_map/ppermute | solution.py:436
  35.6 0.7 arrived.2.x_ref
  36.3 0.1 split.7
  36.4 0.1 collective-permute-start.5
  36.5 2.4 %collective-permute-start.4 = (bf16[144,4096]{1,0:T(8,128)(2,1)S(1)}, bf16[144,4096]{1,0:T(8,128)(2,1)S(1)}, u32[]{:S(2)}, u32[]{:S(2)}) collective-permute-start(bf16[144,4096]{1,0:T(8,128)(2,1)S(1)} %arrived.2.x_ref), channel_id=1, source_target_pairs={{0,4},{1,3},{4,8},{5,1},{8,12},{9,5},{12,14},{13,9},{14,10},{15,13... | collective-permute-start | bytes 3538952 | tf_op jit(solution)/shard_map/ppermute | solution.py:436
  38.9 1.3 %collective-permute-start.6 = (s32[8,128]{1,0:T(8,128)S(1)}, s32[8,128]{1,0:T(8,128)S(1)}, u32[]{:S(2)}, u32[]{:S(2)}) collective-permute-start(s32[8,128]{1,0:T(8,128)S(1)} %get-tuple-element.48), channel_id=1, source_target_pairs={{0,3},{1,4},{4,1},{5,8},{8,5},{9,12},{12,9},{13,14},{14,13},{15,10... | collective-permute-start | bytes 12296 | tf_op jit(solution)/shard_map/ppermute | solution.py:436
  40.2 0.4 collective-permute-start.9
  40.6 1.4 %collective-permute-done.6.count_ref = s32[8,128]{1,0:T(8,128)S(1)} collective-permute-done((s32[8,128]{1,0:T(8,128)S(1)}, s32[8,128]{1,0:T(8,128)S(1)}, u32[]{:S(2)}, u32[]{:S(2)}) %collective-permute-start.6) | collective-permute-done | bytes 4128 | tf_op jit(solution)/shard_map/ppermute | solution.py:436
  42.0 0.7 arrived.3.x_ref
  42.7 0.1 split.8
  42.8 1.5 %collective-permute-start.13 = (bf16[144,4096]{1,0:T(8,128)(2,1)S(1)}, bf16[144,4096]{1,0:T(8,128)(2,1)S(1)}, u32[]{:S(2)}, u32[]{:S(2)}) collective-permute-start(bf16[144,4096]{1,0:T(8,128)(2,1)S(1)} %arrived.3.x_ref), channel_id=1, source_target_pairs={{0,4},{1,3},{4,8},{5,1},{8,12},{9,5},{12,14},{13,9},{14,10},{15,13... | collective-permute-start | bytes 3538952 | tf_op jit(solution)/shard_map/ppermute | solution.py:436
  44.4 0.2 collective-permute-start.8
  44.6 0.3 collective-permute-start.10
  44.9 1.5 %collective-permute-done.8.refs_8_ = bf16[144,2048]{1,0:T(8,128)(2,1)S(1)} collective-permute-done((bf16[144,2048]{1,0:T(8,128)(2,1)S(1)}, bf16[144,2048]{1,0:T(8,128)(2,1)S(1)}, u32[]{:S(2)}, u32[]{:S(2)}) %collective-permute-start.8) | collective-permute-done | bytes 589856 | tf_op jit(solution)/shard_map/ppermute | solution.py:436
  46.4 0.8 collective-permute-done.10.refs_12_
  47.2 11.2 %phase_w_whole.6 = (f32[768,4096]{1,0:T(8,128)S(1)}, bf16[2304,768]{1,0:T(8,128)(2,1)}, f32[8,128]{1,0:T(8,128)S(1)}) custom-call(s32[16,16]{1,0:T(8,128)S(1)} %copy-done.1, s32[1]{0:T(128)} %bitcast.me_ref.refs_1_, s32[1]{0:T(128)S(6)} %copy.48.heads_ref.refs_2_, ...), custom_call_target="tpu_custom_call", output_to_operand_aliasing={{0}: (13, {}), {1}: (14, {})} | custom-call | flops 1 | bytes 1 | tf_op jit(solution)/shard_map/phase_w_whole/pallas_call | solution.py:304
  58.5 1.6 %collective-permute-start.11 = (bf16[144,4096]{1,0:T(8,128)(2,1)S(1)}, bf16[144,4096]{1,0:T(8,128)(2,1)S(1)}, u32[]{:S(2)}, u32[]{:S(2)}) collective-permute-start(bf16[144,4096]{1,0:T(8,128)(2,1)S(1)} %after.8.x_ref), channel_id=1, source_target_pairs={{0,4},{1,3},{4,8},{5,1},{8,12},{9,5},{12,14},{13,9},{14,10},{15,13... | collective-permute-start | bytes 3538952 | tf_op jit(solution)/shard_map/ppermute | solution.py:436
  60.1 0.1 split.9
  60.2 0.1 collective-permute-start.12
  60.3 0.5 collective-permute-start.15
  60.8 4.9 %collective-permute-done.13.refs_0_ = bf16[144,4096]{1,0:T(8,128)(2,1)S(1)} collective-permute-done((bf16[144,4096]{1,0:T(8,128)(2,1)S(1)}, bf16[144,4096]{1,0:T(8,128)(2,1)S(1)}, u32[]{:S(2)}, u32[]{:S(2)}) %collective-permute-start.13) | collective-permute-done | bytes 1179680 | tf_op jit(solution)/shard_map/ppermute | solution.py:436
  65.7 0.1 split.10
  65.9 0.5 collective-permute-start.16
  66.4 2.1 %collective-permute-start.18 = (bf16[144,4096]{1,0:T(8,128)(2,1)S(1)}, bf16[144,4096]{1,0:T(8,128)(2,1)S(1)}, u32[]{:S(2)}, u32[]{:S(2)}) collective-permute-start(bf16[144,4096]{1,0:T(8,128)(2,1)S(1)} %after.9.x_ref), channel_id=1, source_target_pairs={{0,4},{1,3},{4,8},{5,1},{8,12},{9,5},{12,14},{13,9},{14,10},{15,13... | collective-permute-start | bytes 3538952 | tf_op jit(solution)/shard_map/ppermute | solution.py:436
  68.5 0.3 collective-permute-done.16.refs_12_
  68.7 11.1 %phase_w_whole.7 = (f32[768,4096]{1,0:T(8,128)S(1)}, bf16[2304,768]{1,0:T(8,128)(2,1)}, f32[8,128]{1,0:T(8,128)S(1)}) custom-call(s32[16,16]{1,0:T(8,128)S(1)} %copy-done.1, s32[1]{0:T(128)} %bitcast.me_ref.refs_1_, s32[1]{0:T(128)S(6)} %copy.48.heads_ref.refs_2_, ...), custom_call_target="tpu_custom_call", output_to_operand_aliasing={{0}: (13, {}), {1}: (14, {})} | custom-call | flops 1 | bytes 1 | tf_op jit(solution)/shard_map/phase_w_whole/pallas_call | solution.py:304
  79.9 0.1 split.11
  80.0 0.2 collective-permute-start.19
  80.2 0.4 collective-permute-start.20
  80.5 2.1 %collective-permute-start.17 = (bf16[144,4096]{1,0:T(8,128)(2,1)S(1)}, bf16[144,4096]{1,0:T(8,128)(2,1)S(1)}, u32[]{:S(2)}, u32[]{:S(2)}) collective-permute-start(bf16[144,4096]{1,0:T(8,128)(2,1)S(1)} %after.10.x_ref), channel_id=1, source_target_pairs={{0,4},{1,3},{4,8},{5,1},{8,12},{9,5},{12,14},{13,9},{14,10},{15,13... | collective-permute-start | bytes 3538952 | tf_op jit(solution)/shard_map/ppermute | solution.py:436
  82.6 0.3 collective-permute-done.20.refs_8_
  82.9 7.4 %phase_w_whole.8 = (f32[768,4096]{1,0:T(8,128)S(1)}, bf16[2304,768]{1,0:T(8,128)(2,1)}, f32[8,128]{1,0:T(8,128)S(1)}) custom-call(s32[16,16]{1,0:T(8,128)S(1)} %copy-done.1, s32[1]{0:T(128)} %bitcast.me_ref.refs_1_, s32[1]{0:T(128)S(6)} %copy.48.heads_ref.refs_2_, ...), custom_call_target="tpu_custom_call", output_to_operand_aliasing={{0}: (9, {}), {1}: (10, {})} | custom-call | flops 1 | bytes 1 | tf_op jit(solution)/shard_map/phase_w_whole/pallas_call | solution.py:304
  90.3 0.7 collective-permute-done.18.refs_0_
  91.0 0.1 split.12
  91.1 0.1 collective-permute-start.21
  91.2 0.5 collective-permute-start.22
  91.7 1.5 %collective-permute-done.21.refs_6_ = bf16[144,2048]{1,0:T(8,128)(2,1)S(1)} collective-permute-done((bf16[144,2048]{1,0:T(8,128)(2,1)S(1)}, bf16[144,2048]{1,0:T(8,128)(2,1)S(1)}, u32[]{:S(2)}, u32[]{:S(2)}) %collective-permute-start.21) | collective-permute-done | bytes 589856 | tf_op jit(solution)/shard_map/ppermute | solution.py:436
  93.2 0.8 collective-permute-done.22.refs_8_
  94.0 7.4 %phase_w_whole.9 = (f32[768,4096]{1,0:T(8,128)S(1)}, bf16[2304,768]{1,0:T(8,128)(2,1)}, f32[8,128]{1,0:T(8,128)S(1)}) custom-call(s32[16,16]{1,0:T(8,128)S(1)} %copy-done.1, s32[1]{0:T(128)} %bitcast.me_ref.refs_1_, s32[1]{0:T(128)S(6)} %copy.48.heads_ref.refs_2_, ...), custom_call_target="tpu_custom_call", output_to_operand_aliasing={{0}: (9, {}), {1}: (10, {})} | custom-call | flops 1 | bytes 1 | tf_op jit(solution)/shard_map/phase_w_whole/pallas_call | solution.py:304
  101.4 2.2 %collective-permute-done.17.refs_0_ = bf16[144,4096]{1,0:T(8,128)(2,1)S(1)} collective-permute-done((bf16[144,4096]{1,0:T(8,128)(2,1)S(1)}, bf16[144,4096]{1,0:T(8,128)(2,1)S(1)}, u32[]{:S(2)}, u32[]{:S(2)}) %collective-permute-start.17) | collective-permute-done | bytes 1179680 | tf_op jit(solution)/shard_map/ppermute | solution.py:436
  103.6 0.1 split.13
  103.8 0.5 collective-permute-start.23
  104.3 3.0 %phase_w_None.2 = (f32[768,4096]{1,0:T(8,128)S(1)}, f32[8,128]{1,0:T(8,128)}) custom-call(s32[16,16]{1,0:T(8,128)S(1)} %copy-done.1, s32[1]{0:T(128)} %bitcast.me_ref.refs_1_, s32[1]{0:T(128)S(6)} %copy.48.heads_ref.refs_2_, bf16[768,144]{1,0:T(8,128)(2,1)S(1)} %get-tuple-element.88.refs_3_, ...), custom_call_target="tpu_custom_call", output_to_operand_aliasing={{0}: (6, {})} | custom-call | flops 1 | bytes 1 | tf_op jit(solution)/shard_map/phase_w_None/pallas_call | solution.py:304
  107.3 3.0 %phase_w_None.3 = (f32[768,4096]{1,0:T(8,128)S(1)}, f32[8,128]{1,0:T(8,128)S(1)}) custom-call(s32[16,16]{1,0:T(8,128)S(1)} %copy-done.1, s32[1]{0:T(128)} %bitcast.me_ref.refs_1_, s32[1]{0:T(128)S(6)} %copy.48.heads_ref.refs_2_, bf16[768,144]{1,0:T(8,128)(2,1)S(1)} %get-tuple-element.87.refs_3_, ...), custom_call_target="tpu_custom_call", output_to_operand_aliasing={{0}: (6, {})} | custom-call | flops 1 | bytes 1 | tf_op jit(solution)/shard_map/phase_w_None/pallas_call | solution.py:304
  110.3 3.1 %collective-permute-start.27 = (f32[8,128]{1,0:T(8,128)S(1)}, f32[8,128]{1,0:T(8,128)S(1)}, u32[]{:S(2)}, u32[]{:S(2)}) collective-permute-start(f32[8,128]{1,0:T(8,128)S(1)} %get-tuple-element.92), channel_id=1, source_target_pairs={{0,6},{1,7},{2,4},{3,5},{4,2},{5,3},{6,0},{7,1},{8,14},{9,15},{10,... | collective-permute-start | bytes 12296 | tf_op jit(solution)/shard_map/ppermute | solution.py:416
  113.4 0.5 collective-permute-start.26
  113.9 0.2 collective-permute-start.25
  114.1 2.7 %phase__first.1 = (f32[288,768]{1,0:T(8,128)S(1)}, f32[8,128]{1,0:T(8,128)S(1)}) custom-call(s32[16,16]{1,0:T(8,128)S(1)} %copy-done.1, s32[1]{0:T(128)} %bitcast.me_ref.refs_1_, s32[1]{0:T(128)S(6)} %copy.48.heads_ref.refs_2_, bf16[768,4096]{1,0:T(8,128)(2,1)S(1)} %copy-done, bf16[144,2048]{1,0:T(8,128)(2,1)S(1)} %get-tuple-element.83.refs_4_, ...), custom_call_target="tpu_custom_call" | custom-call | flops 1 | bytes 1 | tf_op jit(solution)/shard_map/phase__first/pallas_call | solution.py:304
  116.8 0.2 collective-permute-done.26
  117.0 0.5 collective-permute-done.25
  117.5 1.2 collective-permute-start.30
  118.6 1.5 %collective-permute-start.29 = (f32[8,128]{1,0:T(8,128)S(1)}, f32[8,128]{1,0:T(8,128)S(1)}, u32[]{:S(2)}, u32[]{:S(2)}) collective-permute-start(f32[8,128]{1,0:T(8,128)S(1)} %after.13), channel_id=1, source_target_pairs={{0,8},{1,9},{2,10},{3,11},{4,12},{5,13},{6,14},{7,15},{8,0},{9,1},... | collective-permute-start | bytes 12296 | tf_op jit(solution)/shard_map/ppermute | solution.py:416
  120.1 0.2 collective-permute-start.28
  120.3 2.7 %phase__last.1 = (bf16[2304,768]{1,0:T(8,128)(2,1)}, f32[8,128]{1,0:T(8,128)}) custom-call(s32[16,16]{1,0:T(8,128)S(1)} %copy-done.1, s32[1]{0:T(128)} %bitcast.me_ref.refs_1_, s32[1]{0:T(128)S(6)} %copy.48.heads_ref.refs_2_, bf16[768,4096]{1,0:T(8,128)(2,1)S(1)} %copy-done, ...), custom_call_target="tpu_custom_call", output_to_operand_aliasing={{0}: (7, {})} | custom-call | flops 1 | bytes 1 | tf_op jit(solution)/shard_map/phase__last/pallas_call | solution.py:304
  123.0 0.2 collective-permute-done.29
  123.2 3.0 %scale.1 = bf16[768,4096]{1,0:T(8,128)(2,1)} custom-call(f32[768,4096]{1,0:T(8,128)S(1)} %get-tuple-element.91.w_ref, f32[8,128]{1,0:T(8,128)S(1)} %add_add_fusion.squares_ref), custom_call_target="tpu_custom_call" | custom-call | flops 3145728 | bytes 6291456 | tf_op jit(solution)/shard_map/scale/pallas_call | solution.py:344
  (31 shorter events, 0.2 us)
Async XLA Ops:
  1.9 0.7 copy-start.1
  2.6 9.5 %copy-start = (bf16[768,4096]{1,0:T(8,128)(2,1)S(1)}, bf16[768,4096]{1,0:T(8,128)(2,1)}, u32[]{:S(2)}) copy-start(bf16[768,4096]{1,0:T(8,128)(2,1)} %refs_3_.3) | copy-start | bytes 18874372
  6.9 3.3 %collective-permute-start.3 = (bf16[144,2048]{1,0:T(8,128)(2,1)S(1)}, bf16[144,2048]{1,0:T(8,128)(2,1)S(1)}, u32[]{:S(2)}, u32[]{:S(2)}) collective-permute-start(bf16[144,2048]{1,0:T(8,128)(2,1)S(1)} %get-tuple-element.51.refs_7_), channel_id=1, source_target_pairs={{0,1},{1,0},{2,3},{3,2},{4,5},{5,4},{6,7},{7,6},{8,9},{9,8},{10,11... | collective-permute-start | bytes 1769480 | tf_op jit(solution)/shard_map/ppermute | solution.py:436
  7.4 28.2 %collective-permute-start.1 = (bf16[144,4096]{1,0:T(8,128)(2,1)}, bf16[144,4096]{1,0:T(8,128)(2,1)S(1)}, u32[]{:S(2)}, u32[]{:S(2)}) collective-permute-start(bf16[144,4096]{1,0:T(8,128)(2,1)} %grad_ref.1), channel_id=1, source_target_pairs={{0,4},{1,3},{4,8},{5,1},{8,12},{9,5},{12,14},{13,9},{14,10},{15,13... | collective-permute-start | bytes 3538952 | tf_op jit(solution)/shard_map/ppermute | solution.py:436
  10.0 2.1 %collective-permute-start.2 = (bf16[144,2048]{1,0:T(8,128)(2,1)S(1)}, bf16[144,2048]{1,0:T(8,128)(2,1)S(1)}, u32[]{:S(2)}, u32[]{:S(2)}) collective-permute-start(bf16[144,2048]{1,0:T(8,128)(2,1)S(1)} %get-tuple-element.50.refs_5_), channel_id=1, source_target_pairs={{0,1},{1,0},{2,3},{3,2},{4,5},{5,4},{6,7},{7,6},{8,9},{9,8},{10,11... | collective-permute-start | bytes 1769480 | tf_op jit(solution)/shard_map/ppermute | solution.py:436
  10.1 31.9 %collective-permute-start.7 = (bf16[144,4096]{1,0:T(8,128)(2,1)S(1)}, bf16[144,4096]{1,0:T(8,128)(2,1)S(1)}, u32[]{:S(2)}, u32[]{:S(2)}) collective-permute-start(bf16[144,4096]{1,0:T(8,128)(2,1)S(1)} %after.7), channel_id=1, source_target_pairs={{0,3},{1,4},{4,1},{5,8},{8,5},{9,12},{12,9},{13,14},{14,13},{15,10... | collective-permute-start | bytes 3538952 | tf_op jit(solution)/shard_map/ppermute | solution.py:436
  11.6 24.0 %collective-permute-start = (s32[8,128]{1,0:T(8,128)S(1)}, s32[8,128]{1,0:T(8,128)S(1)}, u32[]{:S(2)}, u32[]{:S(2)}) collective-permute-start(s32[8,128]{1,0:T(8,128)S(1)} %get-tuple-element.48), channel_id=1, source_target_pairs={{0,4},{1,3},{4,8},{5,1},{8,12},{9,5},{12,14},{13,9},{14,10},{15,13... | collective-permute-start | bytes 12296 | tf_op jit(solution)/shard_map/ppermute | solution.py:436
  36.4 8.1 %collective-permute-start.5 = (bf16[144,2048]{1,0:T(8,128)(2,1)S(1)}, bf16[144,2048]{1,0:T(8,128)(2,1)S(1)}, u32[]{:S(2)}, u32[]{:S(2)}) collective-permute-start(bf16[144,2048]{1,0:T(8,128)(2,1)S(1)} %get-tuple-element.54.refs_5_), channel_id=1, source_target_pairs={{0,1},{1,0},{2,3},{3,2},{4,5},{5,4},{6,7},{7,6},{8,9},{9,8},{10,11... | collective-permute-start | bytes 1769480 | tf_op jit(solution)/shard_map/ppermute | solution.py:436
  36.5 22.0 %collective-permute-start.4 = (bf16[144,4096]{1,0:T(8,128)(2,1)S(1)}, bf16[144,4096]{1,0:T(8,128)(2,1)S(1)}, u32[]{:S(2)}, u32[]{:S(2)}) collective-permute-start(bf16[144,4096]{1,0:T(8,128)(2,1)S(1)} %arrived.2.x_ref), channel_id=1, source_target_pairs={{0,4},{1,3},{4,8},{5,1},{8,12},{9,5},{12,14},{13,9},{14,10},{15,13... | collective-permute-start | bytes 3538952 | tf_op jit(solution)/shard_map/ppermute | solution.py:436
  38.9 3.1 %collective-permute-start.6 = (s32[8,128]{1,0:T(8,128)S(1)}, s32[8,128]{1,0:T(8,128)S(1)}, u32[]{:S(2)}, u32[]{:S(2)}) collective-permute-start(s32[8,128]{1,0:T(8,128)S(1)} %get-tuple-element.48), channel_id=1, source_target_pairs={{0,3},{1,4},{4,1},{5,8},{8,5},{9,12},{12,9},{13,14},{14,13},{15,10... | collective-permute-start | bytes 12296 | tf_op jit(solution)/shard_map/ppermute | solution.py:436
  40.2 4.7 %collective-permute-start.9 = (bf16[144,2048]{1,0:T(8,128)(2,1)S(1)}, bf16[144,2048]{1,0:T(8,128)(2,1)S(1)}, u32[]{:S(2)}, u32[]{:S(2)}) collective-permute-start(bf16[144,2048]{1,0:T(8,128)(2,1)S(1)} %get-tuple-element.57.refs_9_), channel_id=1, source_target_pairs={{0,1},{1,0},{2,3},{3,2},{4,5},{5,4},{6,7},{7,6},{8,9},{9,8},{10,11... | collective-permute-start | bytes 1769480 | tf_op jit(solution)/shard_map/ppermute | solution.py:436
  42.8 22.9 %collective-permute-start.13 = (bf16[144,4096]{1,0:T(8,128)(2,1)S(1)}, bf16[144,4096]{1,0:T(8,128)(2,1)S(1)}, u32[]{:S(2)}, u32[]{:S(2)}) collective-permute-start(bf16[144,4096]{1,0:T(8,128)(2,1)S(1)} %arrived.3.x_ref), channel_id=1, source_target_pairs={{0,4},{1,3},{4,8},{5,1},{8,12},{9,5},{12,14},{13,9},{14,10},{15,13... | collective-permute-start | bytes 3538952 | tf_op jit(solution)/shard_map/ppermute | solution.py:436
  44.4 2.0 %collective-permute-start.8 = (bf16[144,2048]{1,0:T(8,128)(2,1)S(1)}, bf16[144,2048]{1,0:T(8,128)(2,1)S(1)}, u32[]{:S(2)}, u32[]{:S(2)}) collective-permute-start(bf16[144,2048]{1,0:T(8,128)(2,1)S(1)} %get-tuple-element.56.refs_7_), channel_id=1, source_target_pairs={{0,1},{1,0},{2,3},{3,2},{4,5},{5,4},{6,7},{7,6},{8,9},{9,8},{10,11... | collective-permute-start | bytes 1769480 | tf_op jit(solution)/shard_map/ppermute | solution.py:436
  44.6 2.7 %collective-permute-start.10 = (bf16[144,2048]{1,0:T(8,128)(2,1)S(1)}, bf16[144,2048]{1,0:T(8,128)(2,1)S(1)}, u32[]{:S(2)}, u32[]{:S(2)}) collective-permute-start(bf16[144,2048]{1,0:T(8,128)(2,1)S(1)} %get-tuple-element.58.refs_11_), channel_id=1, source_target_pairs={{0,1},{1,0},{2,3},{3,2},{4,5},{5,4},{6,7},{7,6},{8,9},{9,8},{10,11... | collective-permute-start | bytes 1769480 | tf_op jit(solution)/shard_map/ppermute | solution.py:436
  58.5 21.4 %collective-permute-start.11 = (bf16[144,4096]{1,0:T(8,128)(2,1)S(1)}, bf16[144,4096]{1,0:T(8,128)(2,1)S(1)}, u32[]{:S(2)}, u32[]{:S(2)}) collective-permute-start(bf16[144,4096]{1,0:T(8,128)(2,1)S(1)} %after.8.x_ref), channel_id=1, source_target_pairs={{0,4},{1,3},{4,8},{5,1},{8,12},{9,5},{12,14},{13,9},{14,10},{15,13... | collective-permute-start | bytes 3538952 | tf_op jit(solution)/shard_map/ppermute | solution.py:436
  60.2 6.2 %collective-permute-start.12 = (bf16[144,2048]{1,0:T(8,128)(2,1)S(1)}, bf16[144,2048]{1,0:T(8,128)(2,1)S(1)}, u32[]{:S(2)}, u32[]{:S(2)}) collective-permute-start(bf16[144,2048]{1,0:T(8,128)(2,1)S(1)} %get-tuple-element.63.refs_5_), channel_id=1, source_target_pairs={{0,1},{1,0},{2,3},{3,2},{4,5},{5,4},{6,7},{7,6},{8,9},{9,8},{10,11... | collective-permute-start | bytes 1769480 | tf_op jit(solution)/shard_map/ppermute | solution.py:436
  60.3 8.2 %collective-permute-start.15 = (bf16[144,2048]{1,0:T(8,128)(2,1)S(1)}, bf16[144,2048]{1,0:T(8,128)(2,1)S(1)}, u32[]{:S(2)}, u32[]{:S(2)}) collective-permute-start(bf16[144,2048]{1,0:T(8,128)(2,1)S(1)} %get-tuple-element.65.refs_9_), channel_id=1, source_target_pairs={{0,1},{1,0},{2,3},{3,2},{4,5},{5,4},{6,7},{7,6},{8,9},{9,8},{10,11... | collective-permute-start | bytes 1769480 | tf_op jit(solution)/shard_map/ppermute | solution.py:436
  65.8 2.7 %collective-permute-start.14 = (bf16[144,2048]{1,0:T(8,128)(2,1)S(1)}, bf16[144,2048]{1,0:T(8,128)(2,1)S(1)}, u32[]{:S(2)}, u32[]{:S(2)}) collective-permute-start(bf16[144,2048]{1,0:T(8,128)(2,1)S(1)} %get-tuple-element.64.refs_7_), channel_id=1, source_target_pairs={{0,1},{1,0},{2,3},{3,2},{4,5},{5,4},{6,7},{7,6},{8,9},{9,8},{10,11... | collective-permute-start | bytes 1769480 | tf_op jit(solution)/shard_map/ppermute | solution.py:436
  65.9 2.8 %collective-permute-start.16 = (bf16[144,2048]{1,0:T(8,128)(2,1)S(1)}, bf16[144,2048]{1,0:T(8,128)(2,1)S(1)}, u32[]{:S(2)}, u32[]{:S(2)}) collective-permute-start(bf16[144,2048]{1,0:T(8,128)(2,1)S(1)} %get-tuple-element.66.refs_11_), channel_id=1, source_target_pairs={{0,1},{1,0},{2,3},{3,2},{4,5},{5,4},{6,7},{7,6},{8,9},{9,8},{10,11... | collective-permute-start | bytes 1769480 | tf_op jit(solution)/shard_map/ppermute | solution.py:436
  66.4 24.6 %collective-permute-start.18 = (bf16[144,4096]{1,0:T(8,128)(2,1)S(1)}, bf16[144,4096]{1,0:T(8,128)(2,1)S(1)}, u32[]{:S(2)}, u32[]{:S(2)}) collective-permute-start(bf16[144,4096]{1,0:T(8,128)(2,1)S(1)} %after.9.x_ref), channel_id=1, source_target_pairs={{0,4},{1,3},{4,8},{5,1},{8,12},{9,5},{12,14},{13,9},{14,10},{15,13... | collective-permute-start | bytes 3538952 | tf_op jit(solution)/shard_map/ppermute | solution.py:436
  80.0 2.7 %collective-permute-start.19 = (bf16[144,2048]{1,0:T(8,128)(2,1)S(1)}, bf16[144,2048]{1,0:T(8,128)(2,1)S(1)}, u32[]{:S(2)}, u32[]{:S(2)}) collective-permute-start(bf16[144,2048]{1,0:T(8,128)(2,1)S(1)} %get-tuple-element.72.refs_5_), channel_id=1, source_target_pairs={{0,1},{1,0},{2,3},{3,2},{4,5},{5,4},{6,7},{7,6},{8,9},{9,8},{10,11... | collective-permute-start | bytes 1769480 | tf_op jit(solution)/shard_map/ppermute | solution.py:436
  80.2 2.7 %collective-permute-start.20 = (bf16[144,2048]{1,0:T(8,128)(2,1)S(1)}, bf16[144,2048]{1,0:T(8,128)(2,1)S(1)}, u32[]{:S(2)}, u32[]{:S(2)}) collective-permute-start(bf16[144,2048]{1,0:T(8,128)(2,1)S(1)} %get-tuple-element.73.refs_7_), channel_id=1, source_target_pairs={{0,1},{1,0},{2,3},{3,2},{4,5},{5,4},{6,7},{7,6},{8,9},{9,8},{10,11... | collective-permute-start | bytes 1769480 | tf_op jit(solution)/shard_map/ppermute | solution.py:436
  80.5 23.1 %collective-permute-start.17 = (bf16[144,4096]{1,0:T(8,128)(2,1)S(1)}, bf16[144,4096]{1,0:T(8,128)(2,1)S(1)}, u32[]{:S(2)}, u32[]{:S(2)}) collective-permute-start(bf16[144,4096]{1,0:T(8,128)(2,1)S(1)} %after.10.x_ref), channel_id=1, source_target_pairs={{0,4},{1,3},{4,8},{5,1},{8,12},{9,5},{12,14},{13,9},{14,10},{15,13... | collective-permute-start | bytes 3538952 | tf_op jit(solution)/shard_map/ppermute | solution.py:436
  91.1 2.1 %collective-permute-start.21 = (bf16[144,2048]{1,0:T(8,128)(2,1)S(1)}, bf16[144,2048]{1,0:T(8,128)(2,1)S(1)}, u32[]{:S(2)}, u32[]{:S(2)}) collective-permute-start(bf16[144,2048]{1,0:T(8,128)(2,1)S(1)} %get-tuple-element.77.refs_5_), channel_id=1, source_target_pairs={{0,1},{1,0},{2,3},{3,2},{4,5},{5,4},{6,7},{7,6},{8,9},{9,8},{10,11... | collective-permute-start | bytes 1769480 | tf_op jit(solution)/shard_map/ppermute | solution.py:436
  91.2 2.8 %collective-permute-start.22 = (bf16[144,2048]{1,0:T(8,128)(2,1)S(1)}, bf16[144,2048]{1,0:T(8,128)(2,1)S(1)}, u32[]{:S(2)}, u32[]{:S(2)}) collective-permute-start(bf16[144,2048]{1,0:T(8,128)(2,1)S(1)} %get-tuple-element.78.refs_7_), channel_id=1, source_target_pairs={{0,1},{1,0},{2,3},{3,2},{4,5},{5,4},{6,7},{7,6},{8,9},{9,8},{10,11... | collective-permute-start | bytes 1769480 | tf_op jit(solution)/shard_map/ppermute | solution.py:436
  103.7 3.6 %collective-permute-start.24 = (bf16[144,2048]{1,0:T(8,128)(2,1)S(1)}, bf16[144,2048]{1,0:T(8,128)(2,1)S(1)}, u32[]{:S(2)}, u32[]{:S(2)}) collective-permute-start(bf16[144,2048]{1,0:T(8,128)(2,1)S(1)} %get-tuple-element.83.refs_4_), channel_id=1, source_target_pairs={{0,1},{1,0},{2,3},{3,2},{4,5},{5,4},{6,7},{7,6},{8,9},{9,8},{10,11... | collective-permute-start | bytes 1769480 | tf_op jit(solution)/shard_map/ppermute | solution.py:436
  103.8 3.5 %collective-permute-start.23 = (bf16[144,2048]{1,0:T(8,128)(2,1)S(1)}, bf16[144,2048]{1,0:T(8,128)(2,1)S(1)}, u32[]{:S(2)}, u32[]{:S(2)}) collective-permute-start(bf16[144,2048]{1,0:T(8,128)(2,1)S(1)} %get-tuple-element.82.refs_6_.refs_4_.refs_5_), channel_id=1, source_target_pairs={{0,1},{1,0},{2,3},{3,2},{4,5},{5,4},{6,7},{7,6},{8,9},{9,8},{10,11... | collective-permute-start | bytes 1769480 | tf_op jit(solution)/shard_map/ppermute | solution.py:436
  110.3 6.4 %collective-permute-start.27 = (f32[8,128]{1,0:T(8,128)S(1)}, f32[8,128]{1,0:T(8,128)S(1)}, u32[]{:S(2)}, u32[]{:S(2)}) collective-permute-start(f32[8,128]{1,0:T(8,128)S(1)} %get-tuple-element.92), channel_id=1, source_target_pairs={{0,6},{1,7},{2,4},{3,5},{4,2},{5,3},{6,0},{7,1},{8,14},{9,15},{10,... | collective-permute-start | bytes 12296 | tf_op jit(solution)/shard_map/ppermute | solution.py:416
  113.4 3.6 %collective-permute-start.26 = (f32[8,128]{1,0:T(8,128)S(1)}, f32[8,128]{1,0:T(8,128)S(1)}, u32[]{:S(2)}, u32[]{:S(2)}) collective-permute-start(f32[8,128]{1,0:T(8,128)S(1)} %get-tuple-element.92), channel_id=1, source_target_pairs={{0,4},{1,5},{2,6},{3,7},{4,0},{5,1},{6,2},{7,3},{8,12},{9,13},{10,... | collective-permute-start | bytes 12296 | tf_op jit(solution)/shard_map/ppermute | solution.py:416
  113.9 3.6 %collective-permute-start.25 = (f32[8,128]{1,0:T(8,128)S(1)}, f32[8,128]{1,0:T(8,128)S(1)}, u32[]{:S(2)}, u32[]{:S(2)}) collective-permute-start(f32[8,128]{1,0:T(8,128)S(1)} %get-tuple-element.92), channel_id=1, source_target_pairs={{0,2},{1,3},{2,0},{3,1},{4,6},{5,7},{6,4},{7,5},{8,10},{9,11},{10,... | collective-permute-start | bytes 12296 | tf_op jit(solution)/shard_map/ppermute | solution.py:416
  117.5 5.5 %collective-permute-start.30 = (f32[8,128]{1,0:T(8,128)S(1)}, f32[8,128]{1,0:T(8,128)S(1)}, u32[]{:S(2)}, u32[]{:S(2)}) collective-permute-start(f32[8,128]{1,0:T(8,128)S(1)} %after.13), channel_id=1, source_target_pairs={{0,9},{1,8},{2,11},{3,10},{4,13},{5,12},{6,15},{7,14},{8,1},{9,0},... | collective-permute-start | bytes 12296 | tf_op jit(solution)/shard_map/ppermute | solution.py:416
  118.6 4.5 %collective-permute-start.29 = (f32[8,128]{1,0:T(8,128)S(1)}, f32[8,128]{1,0:T(8,128)S(1)}, u32[]{:S(2)}, u32[]{:S(2)}) collective-permute-start(f32[8,128]{1,0:T(8,128)S(1)} %after.13), channel_id=1, source_target_pairs={{0,8},{1,9},{2,10},{3,11},{4,12},{5,13},{6,14},{7,15},{8,0},{9,1},... | collective-permute-start | bytes 12296 | tf_op jit(solution)/shard_map/ppermute | solution.py:416
  120.1 3.0 %collective-permute-start.28 = (f32[8,128]{1,0:T(8,128)S(1)}, f32[8,128]{1,0:T(8,128)S(1)}, u32[]{:S(2)}, u32[]{:S(2)}) collective-permute-start(f32[8,128]{1,0:T(8,128)S(1)} %after.13), channel_id=1, source_target_pairs={{0,1},{1,0},{2,3},{3,2},{4,5},{5,4},{6,7},{7,6},{8,9},{9,8},{10,11... | collective-permute-start | bytes 12296 | tf_op jit(solution)/shard_map/ppermute | solution.py:416
